TPU v7x, 32 devices: a whole 2x2x4 slice. The times are simulated.
32 devices in a mesh: groups: 2 (over y), space: 4 (over z), member: 4 (over x, core).
Axes of the slice: x: 2, y: 2, z: 4, core: 2. Of those that a mesh axis runs over, the one named last changes fastest.
Arguments:
- latent: bfloat16 [8, 8192, 256], P('member', ('groups', 'space')), parts along dimension 1, may hold values from -6 to 6
- neighbours: int32 [4, 12288], P(None, ('groups', 'space')), parts along dimension 1, may hold values from 0 to 1535
- weights: float32 [4, 12288], P(None, ('groups', 'space')), parts along dimension 1, may hold values from 0.1 to 1
- targets: bfloat16 [12288, 128], P(('groups', 'space')), parts along dimension 0, may hold values from -6 to 6
- counts: int32 [8], P('groups'), parts along dimension 0, may hold values from 1 to 1536, 2048 in all
- w_one: bfloat16 [256, 256], replicated, may hold values from -0.375 to 0.375
- b_one: float32 [256], replicated, may hold values from -3 to 3
- w_two: bfloat16 [256, 256], replicated, may hold values from -0.375 to 0.375
- b_two: float32 [256], replicated, may hold values from -3 to 3
- w_three: bfloat16 [256, 128], replicated, may hold values from -0.375 to 0.375
Outputs:
- region_score: float32 [8], P('groups'), parts along dimension 0
- latent_grad: bfloat16 [8, 8192, 256], P('member', ('groups', 'space')), parts along dimension 1
- w_one_grad: float32 [512, 256], P('groups'), parts along dimension 0
- b_one_grad: float32 [512], P('groups'), parts along dimension 0
- w_two_grad: float32 [512, 256], P('groups'), parts along dimension 0
- b_two_grad: float32 [512], P('groups'), parts along dimension 0
- w_three_grad: float32 [512, 128], P('groups'), parts along dimension 0
There are 2 independent parts, one for each index of `groups`. A program takes and returns all parts, laid end to end along the dimension named above; an argument that names none is the same for every part. Nothing has to cross between parts.
Inputs may be any that keep to these rules, and one draw needn't show every extreme that they name: The counts of one draw sum to 2048 and the largest equals 1536. `neighbours`: an entry below 256 names one of the last 256 nodes of the previous region, an entry of 1280 or more one of the first 256 nodes of the next region; the regions close into a loop.
All inputs are finite; a program needn't handle non-finite values.
Results may differ from a plain program's by a relative error of at most 0.018.
Values may be sent and summed in bfloat16 or wider, within the bound.
No kernel may reach another device: no remote copies, remote signals or barrier semaphores. Data moves between devices by JAX's collectives and lax.ppermute only.
A program may use at most 128 MiB of HBM per device.

v0:
```python
import jax
import jax.numpy as jnp
from jax import lax
from jax.experimental import pallas as pl
from jax.experimental.pallas import tpu as pltpu
from jax.sharding import PartitionSpec as P

K = 4
OBS_MEAN = 512
HALO = 256
EPSILON = 1e-05
BLOCK = 256
LANE = 128
CHUNK = 512
MIB = 1 << 20


def split(total, step):
    return [(start, min(step, total - start)) for start in range(0, total, step)]


def nt_dot(left, right):
    return lax.dot_general(
        left, right, (((1,), (1,)), ((), ())), preferred_element_type=jnp.float32
    )


def nn_dot(left, right):
    return jnp.dot(left, right, preferred_element_type=jnp.float32)


def kernel_call(body, out_shape, flops, moved, scratch=(), smem=0, operands=0):
    vmem = pl.BlockSpec(memory_space=pltpu.VMEM)
    specs = [pl.BlockSpec(memory_space=pltpu.SMEM)] * smem + [vmem] * (operands - smem)
    return pl.pallas_call(
        body,
        out_shape=out_shape,
        in_specs=specs,
        out_specs=jax.tree.map(lambda _: vmem, out_shape),
        scratch_shapes=list(scratch),
        compiler_params=pltpu.CompilerParams(vmem_limit_bytes=40 * MIB),
        cost_estimate=pl.CostEstimate(flops=flops, bytes_accessed=moved, transcendentals=0),
    )


def table_kernel(count_ref, nbr_ref, weight_ref, latent_ref, table_ref, part_ref):
    members, nodes, width = latent_ref.shape
    ext, slots = table_ref.shape
    live = lax.broadcasted_iota(jnp.int32, (1, slots), 1) < count_ref[0]
    nbr = [nbr_ref[k : k + 1, :] for k in range(K)]
    own = [jnp.where(live, weight_ref[k : k + 1, :], 0.0) for k in range(K)]
    joint = []
    for k in range(K):
        total = own[k]
        for j in range(K):
            if j != k:
                total = total + jnp.where(nbr[j] == nbr[k], own[j], 0.0)
        joint.append(total)
    groups = BLOCK // 16
    rows = (
        lax.broadcasted_iota(jnp.int32, (groups, 16, LANE), 0) * 16
        + lax.broadcasted_iota(jnp.int32, (groups, 16, LANE), 1)
    ).astype(jnp.float32).astype(jnp.bfloat16)
    for lo, size in split(slots, LANE):
        wide = [
            jnp.broadcast_to(joint[k][:, lo : lo + size], (16, size)).astype(jnp.bfloat16)
            for k in range(K)
        ]
        for b in range(ext // BLOCK):
            tile = jnp.zeros((groups, 16, size), jnp.bfloat16)
            for k in range(K):
                near = (nbr[k][:, lo : lo + size] - b * BLOCK).astype(jnp.float32)
                near = jnp.broadcast_to(near, (16, size)).astype(jnp.bfloat16)
                tile = jnp.where(rows[:, :, :size] == near[None], wide[k][None], tile)
            table_ref[b * BLOCK : (b + 1) * BLOCK, lo : lo + size] = tile.reshape(BLOCK, size)
    turned = jnp.concatenate([latent_ref[m].T for m in range(members)], axis=0)
    for lo, size in split(slots, CHUNK):
        part_ref[:, lo : lo + size] = nn_dot(
            turned, table_ref[HALO : HALO + nodes, lo : lo + size]
        )


def column(ref):
    height = ref.shape[1]
    return jnp.broadcast_to(ref[...], (LANE, height)).T


def forward_kernel(
    part_ref, table_ref, before_ref, after_ref, w_one_ref, b_one_ref, w_two_ref, b_two_ref, w_three_ref,
    mixed_ref, act_one_ref, slope_one_ref, act_two_ref, slope_two_ref, decoded_ref,
):
    members, _, width = before_ref.shape
    ext, slots = table_ref.shape
    ranks, _, _, share = decoded_ref.shape
    w_one, w_two, w_three = w_one_ref[...].T, w_two_ref[...].T, w_three_ref[...].T
    b_one, b_two = column(b_one_ref), column(b_two_ref)

    def layer(weight, bias, values, size):
        pre = nn_dot(weight, values) + jnp.concatenate([bias] * (size // LANE), axis=1)
        gate = 0.5 + 0.5 * jnp.tanh(0.5 * pre)
        act = pre * gate
        return act.astype(jnp.bfloat16), (gate + act * (1.0 - gate)).astype(jnp.bfloat16)

    for m in range(members):
        edges = jnp.concatenate([before_ref[m].T, after_ref[m].T], axis=1)
        for lo, size in split(slots, CHUNK):
            lanes = slice(lo, lo + size)
            rim = jnp.concatenate([table_ref[:HALO, lanes], table_ref[ext - HALO :, lanes]], axis=0)
            mixed = part_ref[m * width : (m + 1) * width, lanes] + nn_dot(edges, rim)
            mixed = mixed.astype(jnp.bfloat16)
            mixed_ref[m, :, lanes] = mixed
            act_one, slope_one = layer(w_one, b_one, mixed, size)
            act_one_ref[m, :, lanes] = act_one
            slope_one_ref[m, :, lanes] = slope_one
            act_two, slope_two = layer(w_two, b_two, act_one, size)
            act_two_ref[m, :, lanes] = act_two
            slope_two_ref[m, :, lanes] = slope_two
            decoded = nn_dot(w_three, act_two).astype(jnp.bfloat16)
            for q in range(ranks):
                first, last = max(lo, q * share), min(lo + size, (q + 1) * share)
                if first < last:
                    decoded_ref[q, m, :, first - q * share : last - q * share] = decoded[
                        :, first - lo : last - lo
                    ]


def score_kernel(where_ref, decoded_ref, target_ref, grad_ref, score_ref):
    ranks, members, channels, share = decoded_ref.shape
    count = ranks * members
    pairs = [(i, j) for i in range(count) for j in range(i + 1, count)]
    turned = target_ref[...].astype(jnp.float32).T
    total = jnp.zeros((1, LANE), jnp.float32)
    for lo, size in split(share, LANE):
        lanes = slice(lo, lo + size)

        def rows_of(c):
            values = [
                decoded_ref[i // members, i % members, c : c + 16, lanes].astype(jnp.float32)
                for i in range(count)
            ]
            return values, turned[c : c + 16, lanes]

        def fold(square):
            return square[:8] + square[8:]

        to_target = [jnp.zeros((8, size), jnp.float32)] * count
        apart = [jnp.zeros((8, size), jnp.float32)] * len(pairs)
        for c in range(0, channels, 16):
            values, goal = rows_of(c)
            for i in range(count):
                to_target[i] = to_target[i] + fold((values[i] - goal) ** 2)
            for p, (i, j) in enumerate(pairs):
                apart[p] = apart[p] + fold((values[i] - values[j]) ** 2)
        slot = where_ref[1] + lo + lax.broadcasted_iota(jnp.int32, (1, size), 1)
        live = (slot < where_ref[0]).astype(jnp.float32)
        score = jnp.zeros((1, size), jnp.float32)

        def inverse(square, scale):
            squared = jnp.sum(square, axis=0, keepdims=True) + EPSILON
            inv = lax.rsqrt(squared)
            return squared * inv * scale, jnp.broadcast_to(inv * (scale * live), (8, size))

        inv_target, inv_pair = [], []
        for square in to_target:
            dist, inv = inverse(square, 1.0)
            score = score + dist
            inv_target.append(inv)
        for square in apart:
            dist, inv = inverse(square, 1.0 / (count - 1))
            score = score - dist
            inv_pair.append(inv)
        score = score * live
        if size < LANE:
            score = jnp.concatenate([score, jnp.zeros((1, LANE - size), jnp.float32)], axis=1)
        total = total + score
        for c in range(0, channels, 16):
            values, goal = rows_of(c)
            halves = []
            for h in (0, 8):
                near = [v[h : h + 8] for v in values]
                grads = [(near[i] - goal[h : h + 8]) * inv_target[i] for i in range(count)]
                for p, (i, j) in enumerate(pairs):
                    term = (near[i] - near[j]) * inv_pair[p]
                    grads[i] = grads[i] - term
                    grads[j] = grads[j] + term
                halves.append(grads)
            for i in range(count):
                grad_ref[i // members, i % members, c : c + 16, lanes] = jnp.concatenate(
                    [halves[0][i], halves[1][i]], axis=0
                ).astype(jnp.bfloat16)
    score_ref[...] = total


def backward_kernel(
    region_ref, grad_ref, score_ref, mixed_ref, act_one_ref, slope_one_ref, act_two_ref, slope_two_ref,
    w_one_ref, w_two_ref, w_three_ref, sums_ref, d_mixed_ref, d_dec_ref, d_two_ref, d_one_ref,
):
    ranks, members, channels, share = grad_ref.shape
    _, width, slots = mixed_ref.shape
    hidden = act_one_ref.shape[1]
    for q in range(ranks):
        for m in range(members):
            d_dec_ref[m, :, q * share : (q + 1) * share] = grad_ref[q, m]
    w_one, w_two, w_three = w_one_ref[...], w_two_ref[...], w_three_ref[...]
    bias_one = jnp.zeros((hidden, LANE), jnp.float32)
    bias_two = jnp.zeros((hidden, LANE), jnp.float32)

    def lane_sum(values):
        return sum(values[:, lo : lo + LANE] for lo, _ in split(values.shape[1], LANE))

    for m in range(members):
        for lo, size in split(slots, CHUNK):
            lanes = slice(lo, lo + size)
            back = nn_dot(w_three, d_dec_ref[m, :, lanes]) * slope_two_ref[m, :, lanes].astype(jnp.float32)
            bias_two = bias_two + lane_sum(back)
            d_two = back.astype(jnp.bfloat16)
            d_two_ref[m, :, lanes] = d_two
            back = nn_dot(w_two, d_two) * slope_one_ref[m, :, lanes].astype(jnp.float32)
            bias_one = bias_one + lane_sum(back)
            d_one = back.astype(jnp.bfloat16)
            d_one_ref[m, :, lanes] = d_one
            d_mixed_ref[m * width : (m + 1) * width, lanes] = nn_dot(w_one, d_one).astype(jnp.bfloat16)

    def weight_sum(left_ref, right_ref):
        return sum(nt_dot(left_ref[m], right_ref[m]) for m in range(members))

    g_one = weight_sum(mixed_ref, d_one_ref)
    g_two = weight_sum(act_one_ref, d_two_ref)
    g_three = weight_sum(act_two_ref, d_dec_ref)
    kind = sums_ref.dtype
    sums_ref[:width] = g_one.astype(kind)
    sums_ref[width : width + hidden] = g_two.astype(kind)
    base, half = width + hidden, hidden // 2
    sums_ref[base : base + half, :channels] = g_three[:half].astype(kind)
    sums_ref[base : base + half, channels:] = g_three[half:].astype(kind)
    base = base + half
    rows_left = sums_ref.shape[0] - base
    region = lax.broadcasted_iota(jnp.int32, (1, hidden), 1) == region_ref[0]
    tally = jnp.where(region, jnp.sum(score_ref[...]), 0.0)
    high = tally.astype(jnp.bfloat16).astype(jnp.float32)
    extra = jnp.concatenate(
        [
            jnp.sum(bias_one.T, axis=0, keepdims=True),
            jnp.sum(bias_two.T, axis=0, keepdims=True),
            high,
            tally - high,
            jnp.zeros((12, hidden), jnp.float32),
        ],
        axis=0,
    )
    sums_ref[base : base + 16] = extra.astype(kind)
    if rows_left > 16:
        sums_ref[base + 16 :] = jnp.zeros((rows_left - 16, hidden), kind)


def rim_kernel(table_ref, d_mixed_ref, head_ref, tail_ref):
    members, _, width = head_ref.shape
    ext = table_ref.shape[0]
    for ref, start in ((head_ref, 0), (tail_ref, ext - HALO)):
        grads = nt_dot(table_ref[start : start + HALO, :], d_mixed_ref[...])
        for m in range(members):
            ref[m] = grads[:, m * width : (m + 1) * width].astype(jnp.bfloat16)


def own_kernel(table_ref, d_mixed_ref, own_ref):
    members, nodes, width = own_ref.shape
    for lo, size in split(nodes, BLOCK):
        grads = nt_dot(table_ref[HALO + lo : HALO + lo + size, :], d_mixed_ref[...])
        for m in range(members):
            own_ref[m, lo : lo + size] = grads[:, m * width : (m + 1) * width]


def shifted(shard, axis, by):
    length = lax.axis_size(axis)
    return lax.ppermute(shard, axis, [(i, (i + by) % length) for i in range(length)])


def per_device(latent, neighbours, weights, targets, counts, w_one, b_one, w_two, b_two, w_three):
    members, nodes, width = latent.shape
    slots, channels = targets.shape
    hidden = w_one.shape[1]
    ext = nodes + 2 * HALO
    region, regions = lax.axis_index("space"), lax.axis_size("space")
    rank, ranks = lax.axis_index("member"), lax.axis_size("member")
    share = slots // ranks
    bf16, f32 = jnp.bfloat16, jnp.float32
    shape = jax.ShapeDtypeStruct

    before = shifted(latent[:, nodes - HALO :], "space", 1)
    after = shifted(latent[:, :HALO], "space", -1)
    count = lax.dynamic_slice_in_dim(counts, region, 1)
    target = lax.dynamic_slice_in_dim(targets, rank * share, share)

    table, part = kernel_call(
        table_kernel,
        (shape((ext, slots), bf16), shape((members * width, slots), f32)),
        flops=2 * members * width * nodes * slots,
        moved=12 * MIB,
        smem=1,
        operands=4,
    )(count, neighbours, weights, latent)

    saved = shape((members, hidden, slots), bf16)
    mixed, act_one, slope_one, act_two, slope_two, decoded = kernel_call(
        forward_kernel,
        (shape((members, width, slots), bf16), saved, saved, saved, saved,
         shape((ranks, members, channels, share), bf16)),
        flops=2 * members * slots * (2 * HALO * width + width * hidden + hidden * hidden + hidden * channels),
        moved=16 * MIB,
        operands=9,
    )(part, table, before, after, w_one, b_one[None], w_two, b_two[None], w_three)

    everyone = lax.all_to_all(decoded, "member", 0, 0, tiled=True)
    place = jnp.concatenate([count, (rank * share)[None].astype(jnp.int32)])
    grads, score = kernel_call(
        score_kernel,
        (shape((ranks, members, channels, share), bf16), shape((1, LANE), f32)),
        flops=4 * MIB,
        moved=2 * MIB,
        smem=1,
        operands=3,
    )(place, everyone, target)
    d_decoded = lax.all_to_all(grads, "member", 0, 0, tiled=True)

    ways = regions * ranks
    used = width + hidden + hidden // 2 + 16
    rows = -(-used // (16 * ways)) * 16 * ways
    sums, d_mixed = kernel_call(
        backward_kernel,
        (shape((rows, hidden), bf16), shape((members * width, slots), bf16)),
        flops=4 * members * slots * (width * hidden + hidden * hidden + hidden * channels),
        moved=10 * MIB,
        scratch=(
            pltpu.VMEM((members, channels, slots), bf16),
            pltpu.VMEM((members, hidden, slots), bf16),
            pltpu.VMEM((members, hidden, slots), bf16),
        ),
        smem=1,
        operands=11,
    )(region[None].astype(jnp.int32), d_decoded, score, mixed, act_one, slope_one, act_two, slope_two,
      w_one, w_two, w_three)

    edge = shape((members, HALO, width), bf16)
    head, tail = kernel_call(
        rim_kernel, (edge, edge), flops=4 * members * HALO * width * slots, moved=3 * MIB, operands=2
    )(table, d_mixed)
    from_next = shifted(head, "space", -1)
    from_prev = shifted(tail, "space", 1)
    own = kernel_call(
        own_kernel,
        shape((members, nodes, width), f32),
        flops=2 * members * nodes * width * slots,
        moved=6 * MIB,
        operands=2,
    )(table, d_mixed)

    both = ("space", "member")
    pieces = lax.all_to_all(sums, both, 0, 0, tiled=True)
    piece = jnp.sum(pieces.reshape(ways, rows // ways, hidden).astype(f32), axis=0).astype(bf16)
    sums = lax.all_gather(piece, both, axis=0, tiled=True).astype(f32)

    latent_grad = jnp.concatenate(
        [own[:, :HALO] + from_prev.astype(f32), own[:, HALO : nodes - HALO],
         own[:, nodes - HALO :] + from_next.astype(f32)],
        axis=1,
    ).astype(bf16)
    g_one, g_two = sums[:width], sums[width : width + hidden]
    base, half = width + hidden, hidden // 2
    g_three = jnp.concatenate(
        [sums[base : base + half, :channels], sums[base : base + half, channels:]], axis=0
    )
    base = base + half
    tally = sums[base + 2, :regions] + sums[base + 3, :regions]
    region_score = tally / (OBS_MEAN * members * ranks)
    return (region_score, latent_grad, g_one, sums[base], g_two, sums[base + 1], g_three)


def solution(mesh):
    in_specs = (
        P("member", ("groups", "space"), None),
        P(None, ("groups", "space")),
        P(None, ("groups", "space")),
        P(("groups", "space"), None),
        P("groups"),
        P(),
        P(),
        P(),
        P(),
        P(),
    )
    out_specs = (
        P("groups"),
        P("member", ("groups", "space"), None),
        P("groups", None),
        P("groups"),
        P("groups", None),
        P("groups"),
        P("groups", None),
    )
    return jax.shard_map(
        per_device, mesh=mesh, in_specs=in_specs, out_specs=out_specs, check_vma=False
    )
```

profile of v0, /device:TPU:0, one launch (start us, length us, event | category | flops | bytes accessed | tf_op | source)
XLA Modules:
  0.0 125.6 jit_solution(894256660141272118)
XLA Ops:
  0.6 0.0 copy-start
  0.6 1.1 fusion.4
  1.8 3.1 %collective-permute-start = (bf16[2,256,256]{2,1,0:T(8,128)(2,1)S(1)}, bf16[2,256,256]{2,1,0:T(8,128)(2,1)S(1)}, u32[]{:S(2)}, u32[]{:S(2)}) collective-permute-start(bf16[2,256,256]{2,1,0:T(8,128)(2,1)S(1)} %get-tuple-element.38), channel_id=1, source_target_pairs={{0,4},{4,8},{8,12},{12,0},{1,5},{5,9},{9,13},{13,1},{2,6},{6,10},{... | collective-permute-start | bytes 786440 | tf_op jit(solution)/shard_map/ppermute | solution.py:275
  4.8 2.1 %collective-permute-start.1 = (bf16[2,256,256]{2,1,0:T(8,128)(2,1)S(1)}, bf16[2,256,256]{2,1,0:T(8,128)(2,1)S(1)}, u32[]{:S(2)}, u32[]{:S(2)}) collective-permute-start(bf16[2,256,256]{2,1,0:T(8,128)(2,1)S(1)} %get-tuple-element.37), channel_id=1, source_target_pairs={{0,12},{4,0},{8,4},{12,8},{1,13},{5,1},{9,5},{13,9},{2,14},{6,2},{... | collective-permute-start | bytes 786440 | tf_op jit(solution)/shard_map/ppermute | solution.py:275
  6.9 1.2 dynamic_slice.6.count_ref
  8.2 0.0 copy-start.18
  8.2 1.2 copy-done.18
  9.4 0.0 copy-start.21
  9.4 0.7 copy-done.21
  10.1 0.0 copy-start.22
  10.1 0.7 copy-done.22
  10.9 0.0 copy-start.11
  10.9 0.0 copy-start.20
  10.9 3.4 %shard_map.153 = (bf16[1536,1536]{1,0:T(8,128)(2,1)S(1)}, f32[512,1536]{1,0:T(8,128)S(1)}) custom-call(s32[1]{0:T(128)} %dynamic_slice.6.count_ref, s32[4,1536]{1,0:T(4,128)S(1)} %copy-done.21, f32[4,1536]{1,0:T(4,128)S(1)} %copy-done.22, bf16[2,1024,256]{2,1,0:T(8,128)(2,1)S(1)} %copy-done.18), custom_call_target="tpu_custom_call" | custom-call | flops 1610612736 | bytes 12582912 | tf_op jit(solution)/shard_map/pallas_call | solution.py:294
  14.3 0.0 copy-start.1
  14.3 2.1 %copy-done.1 = bf16[1536,1536]{1,0:T(8,128)(2,1)} copy-done((bf16[1536,1536]{1,0:T(8,128)(2,1)}, bf16[1536,1536]{1,0:T(8,128)(2,1)S(1)}, u32[]{:S(2)}) %copy-start.1) | copy-done | bytes 4718616
  16.5 0.0 collective-permute-done.before_ref
  16.5 1.8 %collective-permute-done.1.after_ref = bf16[2,256,256]{2,1,0:T(8,128)(2,1)S(1)} collective-permute-done((bf16[2,256,256]{2,1,0:T(8,128)(2,1)S(1)}, bf16[2,256,256]{2,1,0:T(8,128)(2,1)S(1)}, u32[]{:S(2)}, u32[]{:S(2)}) %collective-permute-start.1) | collective-permute-done | bytes 262176 | tf_op jit(solution)/shard_map/ppermute | solution.py:275
  18.2 0.0 copy-done.11
  18.2 0.0 copy-done.13
  18.2 0.0 copy-done.16
  18.2 0.0 copy-done.19
  18.3 0.0 copy-done.20
  18.3 9.1 %shard_map.154 = (bf16[2,256,1536]{2,1,0:T(8,128)(2,1)S(1)}, bf16[2,256,1536]{2,1,0:T(8,128)(2,1)S(1)}, bf16[2,256,1536]{2,1,0:T(8,128)(2,1)S(1)}, bf16[2,256,15...) custom-call(f32[512,1536]{1,0:T(8,128)S(1)} %get-tuple-element.21.part_ref, ...), custom_call_target="tpu_custom_call" | custom-call | flops 1811939328 | bytes 16777216 | tf_op jit(solution)/shard_map/pallas_call | solution.py:304
  27.3 1.2 copy-done.3
  28.5 1.2 copy-done.5
  29.7 1.2 copy-done.7
  30.9 1.1 copy-done.9
  32.1 3.5 %all-to-all-start = ((bf16[4,2,128,384]{3,2,1,0:T(8,128)(2,1)}), bf16[4,2,128,384]{3,2,1,0:T(8,128)(2,1)S(1)}, u32[]{:S(2)}, u32[]{:S(2)}) async-start(bf16[4,2,128,384]{3,2,1,0:T(8,128)(2,1)} %get-tuple-element.23), calls=%async_computation | async-start | bytes 1572864 | tf_op jit(solution)/shard_map/all_to_all | solution.py:313
  35.6 0.7 pad_add_fusion.where_ref
  36.3 0.0 copy-done
  36.3 10.9 %all-to-all-done.decoded_ref = bf16[4,2,128,384]{3,2,1,0:T(8,128)(2,1)S(1)} async-done(((bf16[4,2,128,384]{3,2,1,0:T(8,128)(2,1)}), bf16[4,2,128,384]{3,2,1,0:T(8,128)(2,1)S(1)}, u32[]{:S(2)}, u32[]{:S(2)}) %all-to-all-start) | async-done | bytes 786464 | tf_op jit(solution)/shard_map/all_to_all | solution.py:313
  47.2 2.5 %shard_map.155 = (bf16[4,2,128,384]{3,2,1,0:T(8,128)(2,1)S(1)}, f32[1,128]{1,0:T(1,128)S(1)}) custom-call(s32[2]{0:T(128)S(1)} %pad_add_fusion.where_ref, bf16[4,2,128,384]{3,2,1,0:T(8,128)(2,1)S(1)} %all-to-all-done.decoded_ref, bf16[384,128]{1,0:T(8,128)(2,1)S(1)} %constant_dynamic-slice_fusion.target_ref), custom_call_target="tpu_custom_call" | custom-call | flops 4194304 | bytes 2097152 | tf_op jit(solution)/shard_map/pallas_call | solution.py:315
  49.7 14.1 %all_to_all.19.grad_ref = bf16[4,2,128,384]{3,2,1,0:T(8,128)(2,1)S(1)} all-to-all(bf16[4,2,128,384]{3,2,1,0:T(8,128)(2,1)S(1)} %get-tuple-element.24), channel_id=1, replica_groups=mesh['groups'=2,'space'=4,'member'=4] {'member'}, dimensions={0} | all-to-all | bytes 1572864 | tf_op jit(solution)/shard_map/all_to_all | solution.py:323
  63.7 0.0 copy-done.4
  63.7 1.4 %copy-done.6 = bf16[2,256,1536]{2,1,0:T(8,128)(2,1)S(1)} copy-done((bf16[2,256,1536]{2,1,0:T(8,128)(2,1)S(1)}, bf16[2,256,1536]{2,1,0:T(8,128)(2,1)}, u32[]{:S(2)}) %copy-start.6) | copy-done | bytes 1572888
  65.1 1.4 %copy-done.8 = bf16[2,256,1536]{2,1,0:T(8,128)(2,1)S(1)} copy-done((bf16[2,256,1536]{2,1,0:T(8,128)(2,1)S(1)}, bf16[2,256,1536]{2,1,0:T(8,128)(2,1)}, u32[]{:S(2)}) %copy-start.8) | copy-done | bytes 1572888
  66.5 1.4 %copy-done.10 = bf16[2,256,1536]{2,1,0:T(8,128)(2,1)S(1)} copy-done((bf16[2,256,1536]{2,1,0:T(8,128)(2,1)S(1)}, bf16[2,256,1536]{2,1,0:T(8,128)(2,1)}, u32[]{:S(2)}) %copy-start.10) | copy-done | bytes 1572888
  67.9 0.9 copy-done.12
  68.9 0.9 copy-done.14
  69.8 0.8 copy-done.17
  70.6 4.2 %shard_map.156 = (bf16[768,256]{1,0:T(8,128)(2,1)S(1)}, bf16[512,1536]{1,0:T(8,128)(2,1)S(1)}) custom-call(s32[1]{0:T(128)} %bitcast.region_ref, bf16[4,2,128,384]{3,2,1,0:T(8,128)(2,1)S(1)} %all_to_all.19.grad_ref, f32[1,128]{1,0:T(1,128)S(1)} %get-tuple-element.25.score_ref, bf16[2,256,1536]{2,1,0:T(8,128)(2,1)S(1)} %get-tuple-element.26.mixed_ref, ...), custom_call_target="tpu_custom_call" | custom-call | flops 2013265920 | bytes 10485760 | tf_op jit(solution)/shard_map/pallas_call | solution.py:328
  74.8 0.0 copy-start.15
  74.8 0.8 copy-done.15
  75.6 3.7 %all-to-all-start.2 = ((bf16[16,48,256]{2,1,0:T(8,128)(2,1)}), bf16[16,48,256]{2,1,0:T(8,128)(2,1)S(1)}, u32[]{:S(2)}, u32[]{:S(2)}) async-start(bf16[16,48,256]{2,1,0:T(8,128)(2,1)} %bitcast.9), calls=%async_computation.2 | async-start | bytes 786432 | tf_op jit(solution)/shard_map/all_to_all | solution.py:358
  79.3 0.0 copy-start.2
  79.3 2.3 %copy-done.2 = bf16[1536,1536]{1,0:T(8,128)(2,1)S(1)} copy-done((bf16[1536,1536]{1,0:T(8,128)(2,1)S(1)}, bf16[1536,1536]{1,0:T(8,128)(2,1)}, u32[]{:S(2)}) %copy-start.2) | copy-done | bytes 4718616
  81.6 1.0 shard_map.158
  82.7 2.0 %collective-permute-start.2 = (bf16[2,256,256]{2,1,0:T(8,128)(2,1)S(1)}, bf16[2,256,256]{2,1,0:T(8,128)(2,1)S(1)}, u32[]{:S(2)}, u32[]{:S(2)}) collective-permute-start(bf16[2,256,256]{2,1,0:T(8,128)(2,1)S(1)} %get-tuple-element.33), channel_id=1, source_target_pairs={{0,4},{4,8},{8,12},{12,0},{1,5},{5,9},{9,13},{13,1},{2,6},{6,10},{... | collective-permute-start | bytes 786440 | tf_op jit(solution)/shard_map/ppermute | solution.py:275
  84.6 1.9 %collective-permute-start.3 = (bf16[2,256,256]{2,1,0:T(8,128)(2,1)S(1)}, bf16[2,256,256]{2,1,0:T(8,128)(2,1)S(1)}, u32[]{:S(2)}, u32[]{:S(2)}) collective-permute-start(bf16[2,256,256]{2,1,0:T(8,128)(2,1)S(1)} %get-tuple-element.34), channel_id=1, source_target_pairs={{0,12},{4,0},{8,4},{12,8},{1,13},{5,1},{9,5},{13,9},{2,14},{6,2},{... | collective-permute-start | bytes 786440 | tf_op jit(solution)/shard_map/ppermute | solution.py:275
  86.5 1.8 %shard_map.157 = f32[2,1024,256]{2,1,0:T(8,128)S(1)} custom-call(bf16[1536,1536]{1,0:T(8,128)(2,1)S(1)} %copy-done.2, bf16[512,1536]{1,0:T(8,128)(2,1)S(1)} %get-tuple-element.32.d_mixed_ref), custom_call_target="tpu_custom_call" | custom-call | flops 1610612736 | bytes 6291456 | tf_op jit(solution)/shard_map/pallas_call | solution.py:349
  88.4 0.1 slice.79
  88.4 8.3 %collective-permute-done.2 = bf16[2,256,256]{2,1,0:T(8,128)(2,1)S(1)} collective-permute-done((bf16[2,256,256]{2,1,0:T(8,128)(2,1)S(1)}, bf16[2,256,256]{2,1,0:T(8,128)(2,1)S(1)}, u32[]{:S(2)}, u32[]{:S(2)}) %collective-permute-start.2) | collective-permute-done | bytes 262176 | tf_op jit(solution)/shard_map/ppermute | solution.py:275
  96.7 3.7 %collective-permute-done.3 = bf16[2,256,256]{2,1,0:T(8,128)(2,1)S(1)} collective-permute-done((bf16[2,256,256]{2,1,0:T(8,128)(2,1)S(1)}, bf16[2,256,256]{2,1,0:T(8,128)(2,1)S(1)}, u32[]{:S(2)}, u32[]{:S(2)}) %collective-permute-start.3) | collective-permute-done | bytes 262176 | tf_op jit(solution)/shard_map/ppermute | solution.py:275
  100.4 0.1 fusion.1
  100.5 1.0 pad_maximum_fusion
  101.5 0.0 all-to-all-done.2
  101.5 0.1 reduce_sum.12
  101.6 21.3 %all_gather.3 = bf16[768,256]{1,0:T(8,128)(2,1)S(1)} all-gather(bf16[48,256]{1,0:T(8,128)(2,1)S(1)} %reduce_sum.12), channel_id=1, replica_groups=mesh['groups'=2,'space'=4,'member'=4] {'space','member'}, dimensions={0}, use_global_device_ids=true | all-gather | bytes 417792 | tf_op jit(solution)/shard_map/all_gather | solution.py:360
  122.9 0.1 convert_element_type.12
  123.0 0.8 fusion.7
  123.8 0.6 fusion.6
  124.4 0.5 fusion.3
  124.9 0.7 pad_maximum_fusion.1
  (16 shorter events, 0.0 us)
Async XLA Ops:
  0.6 35.7 %copy-start = (bf16[1536,128]{1,0:T(8,128)(2,1)S(1)}, bf16[1536,128]{1,0:T(8,128)(2,1)}, u32[]{:S(2)}) copy-start(bf16[1536,128]{1,0:T(8,128)(2,1)} %param.13) | copy-start | bytes 1179652
  1.8 14.7 %collective-permute-start = (bf16[2,256,256]{2,1,0:T(8,128)(2,1)S(1)}, bf16[2,256,256]{2,1,0:T(8,128)(2,1)S(1)}, u32[]{:S(2)}, u32[]{:S(2)}) collective-permute-start(bf16[2,256,256]{2,1,0:T(8,128)(2,1)S(1)} %get-tuple-element.38), channel_id=1, source_target_pairs={{0,4},{4,8},{8,12},{12,0},{1,5},{5,9},{9,13},{13,1},{2,6},{6,10},{... | collective-permute-start | bytes 786440 | tf_op jit(solution)/shard_map/ppermute | solution.py:275
  4.8 13.4 %collective-permute-start.1 = (bf16[2,256,256]{2,1,0:T(8,128)(2,1)S(1)}, bf16[2,256,256]{2,1,0:T(8,128)(2,1)S(1)}, u32[]{:S(2)}, u32[]{:S(2)}) collective-permute-start(bf16[2,256,256]{2,1,0:T(8,128)(2,1)S(1)} %get-tuple-element.37), channel_id=1, source_target_pairs={{0,12},{4,0},{8,4},{12,8},{1,13},{5,1},{9,5},{13,9},{2,14},{6,2},{... | collective-permute-start | bytes 786440 | tf_op jit(solution)/shard_map/ppermute | solution.py:275
  8.2 1.2 copy-start.18
  9.4 0.7 copy-start.21
  10.1 0.7 copy-start.22
  10.9 7.4 %copy-start.11 = (bf16[256,256]{1,0:T(8,128)(2,1)S(1)}, bf16[256,256]{1,0:T(8,128)(2,1)}, u32[]{:S(2)}) copy-start(bf16[256,256]{1,0:T(8,128)(2,1)} %w_one_ref.3) | copy-start | bytes 393220
  10.9 7.4 %copy-start.13 = (bf16[256,256]{1,0:T(8,128)(2,1)S(1)}, bf16[256,256]{1,0:T(8,128)(2,1)}, u32[]{:S(2)}) copy-start(bf16[256,256]{1,0:T(8,128)(2,1)} %w_two_ref.3) | copy-start | bytes 393220
  10.9 7.4 %copy-start.16 = (bf16[256,128]{1,0:T(8,128)(2,1)S(1)}, bf16[256,128]{1,0:T(8,128)(2,1)}, u32[]{:S(2)}) copy-start(bf16[256,128]{1,0:T(8,128)(2,1)} %w_three_ref.3) | copy-start | bytes 196612
  10.9 7.4 %copy-start.19 = (f32[256]{0:T(256)S(1)}, f32[256]{0:T(256)}, u32[]{:S(2)}) copy-start(f32[256]{0:T(256)} %param.16) | copy-start | bytes 3076
  10.9 7.4 %copy-start.20 = (f32[256]{0:T(256)S(1)}, f32[256]{0:T(256)}, u32[]{:S(2)}) copy-start(f32[256]{0:T(256)} %param.18) | copy-start | bytes 3076
  14.3 2.2 %copy-start.1 = (bf16[1536,1536]{1,0:T(8,128)(2,1)}, bf16[1536,1536]{1,0:T(8,128)(2,1)S(1)}, u32[]{:S(2)}) copy-start(bf16[1536,1536]{1,0:T(8,128)(2,1)S(1)} %get-tuple-element.22.table_ref) | copy-start | bytes 14155780
  27.3 1.2 copy-start.3
  28.5 1.2 copy-start.5
  29.7 1.2 copy-start.7
  30.9 1.1 copy-start.9
  32.1 15.1 %all-to-all-start = ((bf16[4,2,128,384]{3,2,1,0:T(8,128)(2,1)}), bf16[4,2,128,384]{3,2,1,0:T(8,128)(2,1)S(1)}, u32[]{:S(2)}, u32[]{:S(2)}) async-start(bf16[4,2,128,384]{3,2,1,0:T(8,128)(2,1)} %get-tuple-element.23), calls=%async_computation | async-start | bytes 1572864 | tf_op jit(solution)/shard_map/all_to_all | solution.py:313
  47.2 16.5 %copy-start.4 = (bf16[2,256,1536]{2,1,0:T(8,128)(2,1)S(1)}, bf16[2,256,1536]{2,1,0:T(8,128)(2,1)}, u32[]{:S(2)}) copy-start(bf16[2,256,1536]{2,1,0:T(8,128)(2,1)} %copy-done.3) | copy-start | bytes 4718596
  63.7 1.4 %copy-start.6 = (bf16[2,256,1536]{2,1,0:T(8,128)(2,1)S(1)}, bf16[2,256,1536]{2,1,0:T(8,128)(2,1)}, u32[]{:S(2)}) copy-start(bf16[2,256,1536]{2,1,0:T(8,128)(2,1)} %copy-done.5) | copy-start | bytes 4718596
  65.1 1.4 %copy-start.8 = (bf16[2,256,1536]{2,1,0:T(8,128)(2,1)S(1)}, bf16[2,256,1536]{2,1,0:T(8,128)(2,1)}, u32[]{:S(2)}) copy-start(bf16[2,256,1536]{2,1,0:T(8,128)(2,1)} %copy-done.7) | copy-start | bytes 4718596
  66.5 1.4 %copy-start.10 = (bf16[2,256,1536]{2,1,0:T(8,128)(2,1)S(1)}, bf16[2,256,1536]{2,1,0:T(8,128)(2,1)}, u32[]{:S(2)}) copy-start(bf16[2,256,1536]{2,1,0:T(8,128)(2,1)} %copy-done.9) | copy-start | bytes 4718596
  67.9 0.9 copy-start.12
  68.9 0.9 copy-start.14
  69.8 0.8 copy-start.17
  74.8 0.8 copy-start.15
  75.6 25.9 %all-to-all-start.2 = ((bf16[16,48,256]{2,1,0:T(8,128)(2,1)}), bf16[16,48,256]{2,1,0:T(8,128)(2,1)S(1)}, u32[]{:S(2)}, u32[]{:S(2)}) async-start(bf16[16,48,256]{2,1,0:T(8,128)(2,1)} %bitcast.9), calls=%async_computation.2 | async-start | bytes 786432 | tf_op jit(solution)/shard_map/all_to_all | solution.py:358
  79.3 2.3 %copy-start.2 = (bf16[1536,1536]{1,0:T(8,128)(2,1)S(1)}, bf16[1536,1536]{1,0:T(8,128)(2,1)}, u32[]{:S(2)}) copy-start(bf16[1536,1536]{1,0:T(8,128)(2,1)} %copy-done.1) | copy-start | bytes 14155780
  82.7 14.0 %collective-permute-start.2 = (bf16[2,256,256]{2,1,0:T(8,128)(2,1)S(1)}, bf16[2,256,256]{2,1,0:T(8,128)(2,1)S(1)}, u32[]{:S(2)}, u32[]{:S(2)}) collective-permute-start(bf16[2,256,256]{2,1,0:T(8,128)(2,1)S(1)} %get-tuple-element.33), channel_id=1, source_target_pairs={{0,4},{4,8},{8,12},{12,0},{1,5},{5,9},{9,13},{13,1},{2,6},{6,10},{... | collective-permute-start | bytes 786440 | tf_op jit(solution)/shard_map/ppermute | solution.py:275
  84.6 15.7 %collective-permute-start.3 = (bf16[2,256,256]{2,1,0:T(8,128)(2,1)S(1)}, bf16[2,256,256]{2,1,0:T(8,128)(2,1)S(1)}, u32[]{:S(2)}, u32[]{:S(2)}) collective-permute-start(bf16[2,256,256]{2,1,0:T(8,128)(2,1)S(1)} %get-tuple-element.34), channel_id=1, source_target_pairs={{0,12},{4,0},{8,4},{12,8},{1,13},{5,1},{9,5},{13,9},{2,14},{6,2},{... | collective-permute-start | bytes 786440 | tf_op jit(solution)/shard_map/ppermute | solution.py:275
where the time goes:
time: 126 us
  blocking collectives  35.4 us (28%)
  waiting for transfers between devices  24.6 us (20%)
  local copies, waits for them, and re-layouts  23.4 us (19%)
  Pallas kernels  22 us (17%)
  starting transfers between devices  16.2 us (13%)
  other arithmetic  3.18 us (3%)
    all_gather x1, blocking collectives, per_device(): sums = lax.all_gather(piece, both, axis=0, tiled=True).astype(f32)  21.3 us
    unnamed x46, local copies, waits for them, and re-layouts  19.6 us
    all_to_all x1, blocking collectives, per_device(): d_decoded = lax.all_to_all(grads, 'member', 0, 0, tiled=True)  14.1 us
    ppermute x4, waiting for transfers between devices, shifted(): lax.ppermute(shard, axis, [(i, (i + by) % length) for i in range(length)])  13.7 us
    all_to_all x1, waiting for transfers between devices, per_device(): everyone = lax.all_to_all(decoded, 'member', 0, 0, tiled=True)  10.9 us
    pallas_call x1, Pallas kernels, per_device(): kernel_call(forward_kernel, (shape((members, width, slots), bf16), saved,...  9.06 us
    ppermute x4, starting transfers between devices, shifted(): lax.ppermute(shard, axis, [(i, (i + by) % length) for i in range(length)])  9.04 us
    pallas_call x1, Pallas kernels, per_device(): kernel_call(backward_kernel, (shape((rows, hidden), bf16), shape((members...  4.22 us
  transfers between devices with their start and end apart: 6, of which 4 were waited for; matrix products, arithmetic and copies ran while one was open for 3% of the time, Pallas kernels for 5%

commit v1 on v0

v1 whole, which is shorter than its diff:
```python
import jax
import jax.numpy as jnp
from jax import lax
from jax.experimental import pallas as pl
from jax.experimental.pallas import tpu as pltpu
from jax.sharding import PartitionSpec as P

K = 4
OBS_MEAN = 512
HALO = 256
EPSILON = 1e-05
BLOCK = 256
LANE = 128
CHUNK = 512
MIB = 1 << 20


def split(total, step):
    return [(start, min(step, total - start)) for start in range(0, total, step)]


def nt_dot(left, right):
    return lax.dot_general(
        left, right, (((1,), (1,)), ((), ())), preferred_element_type=jnp.float32
    )


def nn_dot(left, right):
    return jnp.dot(left, right, preferred_element_type=jnp.float32)


def kernel_call(body, out_shape, flops, moved, scratch=(), smem=0, operands=0):
    vmem = pl.BlockSpec(memory_space=pltpu.VMEM)
    specs = [pl.BlockSpec(memory_space=pltpu.SMEM)] * smem + [vmem] * (operands - smem)
    return pl.pallas_call(
        body,
        out_shape=out_shape,
        in_specs=specs,
        out_specs=jax.tree.map(lambda _: vmem, out_shape),
        scratch_shapes=list(scratch),
        compiler_params=pltpu.CompilerParams(vmem_limit_bytes=40 * MIB),
        cost_estimate=pl.CostEstimate(flops=flops, bytes_accessed=moved, transcendentals=0),
    )


def table_kernel(count_ref, nbr_ref, weight_ref, latent_ref, table_ref, *part_refs):
    members, nodes, width = latent_ref.shape
    ext, slots = table_ref.shape
    live = lax.broadcasted_iota(jnp.int32, (1, slots), 1) < count_ref[0]
    nbr = [nbr_ref[k : k + 1, :] for k in range(K)]
    own = [jnp.where(live, weight_ref[k : k + 1, :], 0.0) for k in range(K)]
    joint = []
    for k in range(K):
        total = own[k]
        for j in range(K):
            if j != k:
                total = total + jnp.where(nbr[j] == nbr[k], own[j], 0.0)
        joint.append(total)
    groups = BLOCK // 16
    rows = (
        lax.broadcasted_iota(jnp.int32, (groups, 16, LANE), 0) * 16
        + lax.broadcasted_iota(jnp.int32, (groups, 16, LANE), 1)
    ).astype(jnp.float32).astype(jnp.bfloat16)
    for lo, size in split(slots, LANE):
        wide = [
            jnp.broadcast_to(joint[k][:, lo : lo + size], (16, size)).astype(jnp.bfloat16)
            for k in range(K)
        ]
        for b in range(ext // BLOCK):
            tile = jnp.zeros((groups, 16, size), jnp.bfloat16)
            for k in range(K):
                near = (nbr[k][:, lo : lo + size] - b * BLOCK).astype(jnp.float32)
                near = jnp.broadcast_to(near, (16, size)).astype(jnp.bfloat16)
                tile = jnp.where(rows[:, :, :size] == near[None], wide[k][None], tile)
            table_ref[b * BLOCK : (b + 1) * BLOCK, lo : lo + size] = tile.reshape(BLOCK, size)
    turned = jnp.concatenate([latent_ref[m].T for m in range(members)], axis=0)
    for lo, size in split(slots, CHUNK):
        part = nn_dot(turned, table_ref[HALO : HALO + nodes, lo : lo + size])
        for m in range(members):
            part_refs[m][:, lo : lo + size] = part[m * width : (m + 1) * width]


def column(ref):
    height = ref.shape[1]
    return jnp.broadcast_to(ref[...], (LANE, height)).T


def forward_kernel(
    rank_ref, part_ref, table_ref, before_ref, after_ref, w_one_ref, b_one_ref, w_two_ref, b_two_ref, w_three_ref,
    mixed_ref, act_one_ref, slope_one_ref, act_two_ref, slope_two_ref, *decoded_refs,
):
    *decoded_refs, stage_ref = decoded_refs
    ext, slots = table_ref.shape
    ranks, _, share = stage_ref.shape
    w_one, w_two, w_three = w_one_ref[...].T, w_two_ref[...].T, w_three_ref[...].T
    b_one, b_two = column(b_one_ref), column(b_two_ref)

    def layer(weight, bias, values, size):
        pre = nn_dot(weight, values) + jnp.concatenate([bias] * (size // LANE), axis=1)
        gate = 0.5 + 0.5 * jnp.tanh(0.5 * pre)
        act = pre * gate
        return act.astype(jnp.bfloat16), (gate + act * (1.0 - gate)).astype(jnp.bfloat16)

    edges = jnp.concatenate([before_ref[...].T, after_ref[...].T], axis=1)
    for lo, size in split(slots, CHUNK):
        lanes = slice(lo, lo + size)
        rim = jnp.concatenate([table_ref[:HALO, lanes], table_ref[ext - HALO :, lanes]], axis=0)
        mixed = (part_ref[:, lanes] + nn_dot(edges, rim)).astype(jnp.bfloat16)
        mixed_ref[:, lanes] = mixed
        act_one, slope_one_ref[:, lanes] = layer(w_one, b_one, mixed, size)
        act_one_ref[:, lanes] = act_one
        act_two, slope_two_ref[:, lanes] = layer(w_two, b_two, act_one, size)
        act_two_ref[:, lanes] = act_two
        decoded = nn_dot(w_three, act_two).astype(jnp.bfloat16)
        for q in range(ranks):
            first, last = max(lo, q * share), min(lo + size, (q + 1) * share)
            if first < last:
                stage_ref[q ^ rank_ref[0], :, first - q * share : last - q * share] = decoded[
                    :, first - lo : last - lo
                ]
    for i in range(ranks):
        decoded_refs[i][...] = stage_ref[i]


def score_kernel(where_ref, target_ref, *refs):
    count = (len(refs) - 1) // 2
    decoded_refs, grad_refs, score_ref = refs[:count], refs[count : 2 * count], refs[2 * count]
    channels, share = decoded_refs[0].shape
    pairs = [(i, j) for i in range(count) for j in range(i + 1, count)]
    turned = target_ref[...].astype(jnp.float32).T
    total = jnp.zeros((1, LANE), jnp.float32)
    for lo, size in split(share, LANE):
        lanes = slice(lo, lo + size)

        def rows_of(c):
            values = [ref[c : c + 16, lanes].astype(jnp.float32) for ref in decoded_refs]
            return values, turned[c : c + 16, lanes]

        def fold(square):
            return square[:8] + square[8:]

        to_target = [jnp.zeros((8, size), jnp.float32)] * count
        apart = [jnp.zeros((8, size), jnp.float32)] * len(pairs)
        for c in range(0, channels, 16):
            values, goal = rows_of(c)
            for i in range(count):
                to_target[i] = to_target[i] + fold((values[i] - goal) ** 2)
            for p, (i, j) in enumerate(pairs):
                apart[p] = apart[p] + fold((values[i] - values[j]) ** 2)
        slot = where_ref[1] + lo + lax.broadcasted_iota(jnp.int32, (1, size), 1)
        live = (slot < where_ref[0]).astype(jnp.float32)
        score = jnp.zeros((1, size), jnp.float32)

        def inverse(square, scale):
            squared = jnp.sum(square, axis=0, keepdims=True) + EPSILON
            inv = lax.rsqrt(squared)
            return squared * inv * scale, jnp.broadcast_to(inv * (scale * live), (8, size))

        inv_target, inv_pair = [], []
        for square in to_target:
            dist, inv = inverse(square, 1.0)
            score = score + dist
            inv_target.append(inv)
        for square in apart:
            dist, inv = inverse(square, 1.0 / (count - 1))
            score = score - dist
            inv_pair.append(inv)
        score = score * live
        if size < LANE:
            score = jnp.concatenate([score, jnp.zeros((1, LANE - size), jnp.float32)], axis=1)
        total = total + score
        for c in range(0, channels, 16):
            values, goal = rows_of(c)
            halves = []
            for h in (0, 8):
                near = [v[h : h + 8] for v in values]
                grads = [(near[i] - goal[h : h + 8]) * inv_target[i] for i in range(count)]
                for p, (i, j) in enumerate(pairs):
                    term = (near[i] - near[j]) * inv_pair[p]
                    grads[i] = grads[i] - term
                    grads[j] = grads[j] + term
                halves.append(grads)
            for i in range(count):
                grad_refs[i][c : c + 16, lanes] = jnp.concatenate(
                    [halves[0][i], halves[1][i]], axis=0
                ).astype(jnp.bfloat16)
    score_ref[...] = total


def backward_kernel(rank_ref, table_ref, slope_one_ref, slope_two_ref, w_one_ref, w_two_ref, w_three_ref, *refs):
    *refs, stage_ref = refs
    ranks, channels, share = stage_ref.shape
    grad_refs = refs[:ranks]
    d_dec_ref, d_two_ref, d_one_ref, d_mixed_ref, bias_one_ref, bias_two_ref, head_ref, tail_ref = refs[ranks:]
    ext, slots = table_ref.shape
    hidden = slope_one_ref.shape[0]
    for i in range(ranks):
        stage_ref[rank_ref[0] ^ i] = grad_refs[i][...]
    for q in range(ranks):
        d_dec_ref[:, q * share : (q + 1) * share] = stage_ref[q]
    w_one, w_two, w_three = w_one_ref[...], w_two_ref[...], w_three_ref[...]
    bias_one = jnp.zeros((hidden, LANE), jnp.float32)
    bias_two = jnp.zeros((hidden, LANE), jnp.float32)

    def lane_sum(values):
        return sum(values[:, lo : lo + LANE] for lo, _ in split(values.shape[1], LANE))

    for lo, size in split(slots, CHUNK):
        lanes = slice(lo, lo + size)
        back = nn_dot(w_three, d_dec_ref[:, lanes]) * slope_two_ref[:, lanes].astype(jnp.float32)
        bias_two = bias_two + lane_sum(back)
        d_two = back.astype(jnp.bfloat16)
        d_two_ref[:, lanes] = d_two
        back = nn_dot(w_two, d_two) * slope_one_ref[:, lanes].astype(jnp.float32)
        bias_one = bias_one + lane_sum(back)
        d_one = back.astype(jnp.bfloat16)
        d_one_ref[:, lanes] = d_one
        d_mixed_ref[:, lanes] = nn_dot(w_one, d_one).astype(jnp.bfloat16)
    bias_one_ref[...] = bias_one
    bias_two_ref[...] = bias_two
    head_ref[...] = nt_dot(table_ref[:HALO, :], d_mixed_ref[...]).astype(jnp.bfloat16)
    tail_ref[...] = nt_dot(table_ref[ext - HALO :, :], d_mixed_ref[...]).astype(jnp.bfloat16)


def sums_kernel(members, place_ref, score_ref, *refs):
    *refs, keep_ref, send_ref, stage_ref = refs
    saved = [refs[8 * m : 8 * (m + 1)] for m in range(members)]
    width, _ = saved[0][0].shape
    hidden, _ = saved[0][1].shape
    channels, _ = saved[0][5].shape
    rows = stage_ref.shape[0] * stage_ref.shape[1]

    def weight_sum(left, right):
        return sum(nt_dot(member[left][...], member[right][...]) for member in saved)

    def lane_total(at):
        return jnp.sum(sum(member[at][...] for member in saved).T, axis=0, keepdims=True)

    g_three = weight_sum(2, 5)
    half = hidden // 2
    region = lax.broadcasted_iota(jnp.int32, (1, hidden), 1) == place_ref[0]
    tally = jnp.where(region, jnp.sum(score_ref[...]), 0.0)
    high = tally.astype(jnp.bfloat16).astype(jnp.float32)
    used = width + hidden + half + 4
    parts = [
        weight_sum(0, 3),
        weight_sum(1, 4),
        jnp.concatenate([g_three[:half], g_three[half:]], axis=1),
        lane_total(6),
        lane_total(7),
        high,
        tally - high,
        jnp.zeros((rows - used, hidden), jnp.float32),
    ]
    stage_ref[...] = jnp.concatenate(parts, axis=0).astype(stage_ref.dtype).reshape(stage_ref.shape)
    keep_ref[...] = stage_ref[place_ref[1]]
    send_ref[...] = stage_ref[1 - place_ref[1]]


def pair_sum_kernel(one_ref, other_ref, sum_ref):
    sum_ref[...] = (one_ref[...].astype(jnp.float32) + other_ref[...].astype(jnp.float32)).astype(sum_ref.dtype)


def piece_kernel(pieces_ref, out_ref):
    ways = pieces_ref.shape[0]
    total = pieces_ref[0].astype(jnp.float32)
    for i in range(1, ways):
        total = total + pieces_ref[i].astype(jnp.float32)
    total = total.astype(out_ref.dtype)
    for i in range(ways):
        out_ref[i] = total


def unpack_kernel(place_ref, mine_ref, other_ref, one_ref, b_one_ref, two_ref, b_two_ref, three_ref, tally_ref, stage_ref):
    stage_ref[place_ref[1]] = mine_ref[...]
    stage_ref[1 - place_ref[1]] = other_ref[...]
    sums = stage_ref[...].reshape(-1, mine_ref.shape[1]).astype(jnp.float32)
    width, hidden = one_ref.shape
    half, channels = hidden // 2, three_ref.shape[1]
    one_ref[...] = sums[:width]
    two_ref[...] = sums[width : width + hidden]
    base = width + hidden
    three_ref[:half] = sums[base : base + half, :channels]
    three_ref[half:] = sums[base : base + half, channels:]
    base = base + half
    last = sums[base : base + 8]
    b_one_ref[...] = last[0:1]
    b_two_ref[...] = last[1:2]
    tally_ref[...] = last[2:3] + last[3:4]


def own_kernel(table_ref, *refs):
    *d_mixed_refs, own_ref = refs
    members, nodes, _ = own_ref.shape
    for m in range(members):
        own_ref[m] = nt_dot(table_ref[HALO : HALO + nodes, :], d_mixed_refs[m][...])


def finish_kernel(own_ref, *refs):
    *refs, out_ref = refs
    members, nodes, _ = own_ref.shape
    for m in range(members):
        from_prev, from_next = refs[m][...], refs[members + m][...]
        out_ref[m, :HALO] = (own_ref[m, :HALO] + from_prev.astype(jnp.float32)).astype(jnp.bfloat16)
        out_ref[m, HALO : nodes - HALO] = own_ref[m, HALO : nodes - HALO].astype(jnp.bfloat16)
        out_ref[m, nodes - HALO :] = (own_ref[m, nodes - HALO :] + from_next.astype(jnp.float32)).astype(jnp.bfloat16)


MEMBER = ("pair", "core")


def shifted(shard, axis, by):
    length = lax.axis_size(axis)
    return lax.ppermute(shard, axis, [(i, (i + by) % length) for i in range(length)])


def swapped(block, by):
    return lax.ppermute(block, MEMBER, [(i, i ^ by) for i in range(lax.axis_size(MEMBER))])


def per_device(latent, neighbours, weights, targets, counts, w_one, b_one, w_two, b_two, w_three):
    members, nodes, width = latent.shape
    slots, channels = targets.shape
    hidden = w_one.shape[1]
    ext = nodes + 2 * HALO
    region, regions = lax.axis_index("space"), lax.axis_size("space")
    rank, ranks = lax.axis_index(MEMBER), lax.axis_size(MEMBER)
    core = lax.axis_index("core")
    share = slots // ranks
    bf16, f32 = jnp.bfloat16, jnp.float32
    shape = jax.ShapeDtypeStruct
    each = range(members)

    before, after = [], []
    for m in each:
        before.append(shifted(latent[m, nodes - HALO :], "space", 1))
        after.append(shifted(latent[m, :HALO], "space", -1))
    count = lax.dynamic_slice_in_dim(counts, region, 1)
    target = lax.dynamic_slice_in_dim(targets, rank * share, share)
    rank_at = rank[None].astype(jnp.int32)
    place = jnp.stack([region, core]).astype(jnp.int32)

    table, *part = kernel_call(
        table_kernel,
        (shape((ext, slots), bf16),) + (shape((width, slots), f32),) * members,
        flops=2 * members * width * nodes * slots,
        moved=12 * MIB,
        smem=1,
        operands=4,
    )(count, neighbours, weights, latent)

    saved_shape = shape((hidden, slots), bf16)
    block = shape((channels, share), bf16)
    saved, sent = [], []
    for m in each:
        out = kernel_call(
            forward_kernel,
            (shape((width, slots), bf16),) + (saved_shape,) * 4 + (block,) * ranks,
            flops=2 * slots * (2 * HALO * width + width * hidden + hidden * hidden + hidden * channels),
            moved=8 * MIB,
            scratch=(pltpu.VMEM((ranks, channels, share), bf16),),
            smem=1,
            operands=10,
        )(rank_at, part[m], table, before[m], after[m], w_one, b_one[None], w_two, b_two[None], w_three)
        saved.append(out[:5])
        sent.append([out[5]] + [swapped(out[5 + i], i) for i in range(1, ranks)])

    everyone = [sent[m][i] for m in each for i in range(ranks)]
    slots_at = jnp.concatenate([count, (rank * share)[None].astype(jnp.int32)])
    *grads, score = kernel_call(
        score_kernel,
        (block,) * len(everyone) + (shape((1, LANE), f32),),
        flops=4 * MIB,
        moved=2 * MIB,
        smem=1,
        operands=2 + len(everyone),
    )(slots_at, target, *everyone)

    edge = shape((HALO, width), bf16)
    bias = shape((hidden, LANE), f32)
    back, from_next, from_prev = [], [], []
    for m in each:
        own_grads = grads[m * ranks : (m + 1) * ranks]
        own_grads = [own_grads[0]] + [swapped(own_grads[i], i) for i in range(1, ranks)]
        *out, head, tail = kernel_call(
            backward_kernel,
            (shape((channels, slots), bf16), saved_shape, saved_shape, shape((width, slots), bf16), bias, bias, edge, edge),
            flops=2 * slots * (2 * HALO * width + width * hidden + hidden * hidden + hidden * channels),
            moved=6 * MIB,
            scratch=(pltpu.VMEM((ranks, channels, share), bf16),),
            smem=1,
            operands=7 + ranks,
        )(rank_at, table, saved[m][2], saved[m][4], w_one, w_two, w_three, *own_grads)
        back.append(out)
        from_next.append(shifted(head, "space", -1))
        from_prev.append(shifted(tail, "space", 1))

    ways = regions * ranks // 2
    rows = -(-(width + hidden + hidden // 2 + 4) // (32 * ways)) * 32 * ways
    half = shape((rows // 2, hidden), bf16)
    operands = []
    for m in each:
        d_dec, d_two, d_one, _, bias_one, bias_two = back[m]
        mixed, act_one, _, act_two, _ = saved[m]
        operands += [mixed, act_one, act_two, d_one, d_two, d_dec, bias_one, bias_two]
    keep, send = kernel_call(
        lambda *refs: sums_kernel(members, *refs),
        (half, half),
        flops=2 * members * slots * (width * hidden + hidden * hidden + hidden * channels),
        moved=10 * MIB,
        scratch=(pltpu.VMEM((2, rows // 2, hidden), bf16),),
        smem=1,
        operands=2 + len(operands),
    )(place, score, *operands)
    swap = [(0, 1), (1, 0)]
    other = lax.ppermute(send, "core", swap)
    own = kernel_call(
        own_kernel,
        shape((members, nodes, width), f32),
        flops=2 * members * nodes * width * slots,
        moved=6 * MIB,
        operands=1 + members,
    )(table, *[out[3] for out in back])
    total = kernel_call(pair_sum_kernel, half, flops=MIB, moved=MIB, operands=2)(keep, other)
    total, own = lax.optimization_barrier((total, own))
    both = ("space", "pair")
    pieces = lax.all_to_all(total, both, 0, 0, tiled=True).reshape(ways, rows // 2 // ways, hidden)
    spread = kernel_call(piece_kernel, shape(pieces.shape, bf16), flops=MIB, moved=MIB, operands=1)(pieces)
    mine = lax.all_to_all(spread.reshape(rows // 2, hidden), both, 0, 0, tiled=True)
    other = lax.ppermute(mine, "core", swap)
    row = shape((1, hidden), f32)
    g_one, g_bone, g_two, g_btwo, g_three, tally = kernel_call(
        unpack_kernel,
        (shape((width, hidden), f32), row, shape((hidden, hidden), f32), row, shape((hidden, channels), f32), row),
        flops=MIB,
        moved=2 * MIB,
        scratch=(pltpu.VMEM((2, rows // 2, hidden), bf16),),
        smem=1,
        operands=3,
    )(place, mine, other)

    latent_grad = kernel_call(
        finish_kernel,
        shape((members, nodes, width), bf16),
        flops=MIB,
        moved=3 * MIB,
        operands=1 + 2 * members,
    )(own, *from_prev, *from_next)
    region_score = tally[0, :regions] / (OBS_MEAN * members * ranks)
    return (region_score, latent_grad, g_one, g_bone[0], g_two, g_btwo[0], g_three)


def solution(mesh):
    groups, space, member = mesh.devices.shape
    inner = jax.sharding.Mesh(
        mesh.devices.reshape(groups, space, member // 2, 2), ("groups", "space") + MEMBER
    )
    in_specs = (
        P(MEMBER, ("groups", "space"), None),
        P(None, ("groups", "space")),
        P(None, ("groups", "space")),
        P(("groups", "space"), None),
        P("groups"),
        P(),
        P(),
        P(),
        P(),
        P(),
    )
    out_specs = (
        P("groups"),
        P(MEMBER, ("groups", "space"), None),
        P("groups", None),
        P("groups"),
        P("groups", None),
        P("groups"),
        P("groups", None),
    )
    return jax.shard_map(
        per_device, mesh=inner, in_specs=in_specs, out_specs=out_specs, check_vma=False
    )
```

time: 126 us -> 93.8 us (0.74)
  local copies, waits for them, and re-layouts: 23.4 us -> 5.16 us
  blocking collectives: 35.4 us -> 21.7 us
  starting transfers between devices: 16.2 us -> 23.2 us
  waiting for transfers between devices: 24.6 us -> 18.6 us
  other arithmetic: 3.18 us -> 1.31 us
    all_gather x1 -> x0, blocking collectives: 21.3 us -> none  [per_device(): sums = lax.all_gather(piece, both, axis=0, tiled=True).astype(f32)]
    unnamed x46 -> x18, local copies, waits for them, and re-layouts: 19.6 us -> 2.73 us
    all_to_all x2 -> x0, waiting for transfers between devices: 10.9 us -> none  [the longest x1 10.9 us: per_device(): everyone = lax.all_to_all(decoded, 'member', 0, 0, tiled=True)]
    ppermute x0 -> x14, waiting for transfers between devices: none -> 9.44 us  [the longest x12 9.43 us: swapped(): lax.ppermute(block, MEMBER, [(i, i ^ by) for i in range(lax.axis_size(MEM...]
    ppermute x0 -> x14, starting transfers between devices: none -> 8.31 us  [the longest x12 7.91 us: swapped(): lax.ppermute(block, MEMBER, [(i, i ^ by) for i in range(lax.axis_size(MEM...]
    all_to_all x1 -> x2, blocking collectives: 14.1 us -> 21.7 us  [the longest x1 11 us: per_device(): lax.all_to_all(total, both, 0, 0, tiled=True)]
    all_to_all x2 -> x0, starting transfers between devices: 7.19 us -> none  [the longest x1 3.7 us: per_device(): pieces = lax.all_to_all(sums, both, 0, 0, tiled=True)]
    ppermute x4 -> x8, starting transfers between devices: 9.04 us -> 14.8 us  [shifted(): lax.ppermute(shard, axis, [(i, (i + by) % length) for i in range(length)])]
  transfers between devices with their start and end apart: 6 -> 22, of which waited for: 4 -> 10; matrix products, arithmetic and copies ran while one was open for 3% -> 2% of each run, Pallas kernels for 5% -> 16%
where the time goes in v1:
time: 93.8 us; the launch traced here: 93.4 us
  starting transfers between devices  23.2 us (25%)
  Pallas kernels  22.7 us (24%)
  blocking collectives  21.7 us (23%)
  waiting for transfers between devices  18.6 us (20%)
  local copies, waits for them, and re-layouts  5.16 us (6%)
  other arithmetic  1.31 us (1%)
    ppermute x8, starting transfers between devices, shifted(): lax.ppermute(shard, axis, [(i, (i + by) % length) for i in range(length)])  14.8 us
    all_to_all x1, blocking collectives, per_device(): lax.all_to_all(total, both, 0, 0, tiled=True)  11 us
    all_to_all x1, blocking collectives, per_device(): lax.all_to_all(spread.reshape(rows // 2, hidden), both, 0, 0, tiled=True)  10.7 us
    ppermute x12, waiting for transfers between devices, swapped(): lax.ppermute(block, MEMBER, [(i, i ^ by) for i in range(lax.axis_size(MEM...  9.43 us
    ppermute x8, waiting for transfers between devices, shifted(): lax.ppermute(shard, axis, [(i, (i + by) % length) for i in range(length)])  9.14 us
    ppermute x12, starting transfers between devices, swapped(): lax.ppermute(block, MEMBER, [(i, i ^ by) for i in range(lax.axis_size(MEM...  7.91 us
    pallas_call x2, Pallas kernels, per_device(): kernel_call(forward_kernel, (shape((width, slots), bf16),) + (saved_shape...  6.13 us
    pallas_call x2, Pallas kernels, per_device(): kernel_call(backward_kernel, (shape((channels, slots), bf16), saved_shape...  4.21 us
  transfers between devices with their start and end apart: 22, of which 10 were waited for; matrix products, arithmetic and copies ran while one was open for 2% of the time, Pallas kernels for 16%

profile of v1, /device:TPU:0, one launch (start us, length us, event | category | flops | bytes accessed | tf_op | source)
XLA Modules:
  0.0 93.4 jit_solution(8144011182814966263)
XLA Ops:
  0.6 0.0 copy-start
  0.6 1.2 %slice_bitcast_fusion = (bf16[256,256]{1,0:T(8,128)(2,1)S(1)}, bf16[256,256]{1,0:T(8,128)(2,1)S(1)}, bf16[256,256]{1,0:T(8,128)(2,1)S(1)}, bf16[256,256]{1,0:T(8,128)(2,1)S(1)}) fusion(bf16[2,1024,256]{2,1,0:T(8,128)(2,1)} %latent_ref.1), kind=kLoop, calls=%fused_computation | loop fusion | bytes 1048576 | tf_op jit(solution)/shard_map/squeeze | solution.py:337
  1.8 3.1 %collective-permute-start = (bf16[256,256]{1,0:T(8,128)(2,1)S(1)}, bf16[256,256]{1,0:T(8,128)(2,1)S(1)}, u32[]{:S(2)}, u32[]{:S(2)}) collective-permute-start(bf16[256,256]{1,0:T(8,128)(2,1)S(1)} %get-tuple-element.121), channel_id=1, source_target_pairs={{0,4},{4,8},{8,12},{12,0},{1,5},{5,9},{9,13},{13,1},{2,6},{6,10},{... | collective-permute-start | bytes 393224 | tf_op jit(solution)/shard_map/ppermute | solution.py:314
  4.9 2.1 %collective-permute-start.1 = (bf16[256,256]{1,0:T(8,128)(2,1)S(1)}, bf16[256,256]{1,0:T(8,128)(2,1)S(1)}, u32[]{:S(2)}, u32[]{:S(2)}) collective-permute-start(bf16[256,256]{1,0:T(8,128)(2,1)S(1)} %get-tuple-element.120), channel_id=1, source_target_pairs={{0,12},{4,0},{8,4},{12,8},{1,13},{5,1},{9,5},{13,9},{2,14},{6,2},{... | collective-permute-start | bytes 393224 | tf_op jit(solution)/shard_map/ppermute | solution.py:314
  7.0 0.0 collective-permute-start.5
  7.0 3.8 %collective-permute-start.6 = (bf16[256,256]{1,0:T(8,128)(2,1)S(1)}, bf16[256,256]{1,0:T(8,128)(2,1)S(1)}, u32[]{:S(2)}, u32[]{:S(2)}) collective-permute-start(bf16[256,256]{1,0:T(8,128)(2,1)S(1)} %get-tuple-element.119), channel_id=1, source_target_pairs={{0,12},{4,0},{8,4},{12,8},{1,13},{5,1},{9,5},{13,9},{2,14},{6,2},{... | collective-permute-start | bytes 393224 | tf_op jit(solution)/shard_map/ppermute | solution.py:314
  10.8 1.2 %dynamic_slice.6.count_ref = s32[1]{0:T(128)} dynamic-slice(s32[4]{0:T(128)} %param.14, s32[]{:T(128)S(6)} %select_n.6), dynamic_slice_sizes={1} | dynamic-slice | bytes 12 | tf_op jit(solution)/shard_map/dynamic_slice | solution.py:338
  12.1 1.2 %copy-done.4 = bf16[2,1024,256]{2,1,0:T(8,128)(2,1)S(1)} copy-done((bf16[2,1024,256]{2,1,0:T(8,128)(2,1)S(1)}, bf16[2,1024,256]{2,1,0:T(8,128)(2,1)}, u32[]{:S(2)}) %copy-start.4) | copy-done | bytes 1048600
  13.3 0.7 copy-done.7
  14.0 0.7 copy-done.8
  14.8 0.0 copy-start.6
  14.8 3.4 %shard_map.153 = (bf16[1536,1536]{1,0:T(8,128)(2,1)S(1)}, f32[256,1536]{1,0:T(8,128)S(1)}, f32[256,1536]{1,0:T(8,128)S(1)}) custom-call(s32[1]{0:T(128)} %dynamic_slice.6.count_ref, s32[4,1536]{1,0:T(4,128)S(1)} %copy-done.7, f32[4,1536]{1,0:T(4,128)S(1)} %copy-done.8, bf16[2,1024,256]{2,1,0:T(8,128)(2,1)S(1)} %copy-done.4), custom_call_target="tpu_custom_call" | custom-call | flops 1610612736 | bytes 12582912 | tf_op jit(solution)/shard_map/pallas_call | solution.py:343
  18.2 0.0 collective-permute-done.before_ref
  18.2 0.0 collective-permute-done.1.after_ref
  18.3 3.1 %shard_map.154 = (bf16[256,1536]{1,0:T(8,128)(2,1)S(1)}, bf16[256,1536]{1,0:T(8,128)(2,1)S(1)}, bf16[256,1536]{1,0:T(8,128)(2,1)S(1)}, bf16[256,1536]{1,0:T(8,12...) custom-call(s32[1]{0:T(128)} %bitcast.3.rank_ref, ...), custom_call_target="tpu_custom_call" | custom-call | flops 905969664 | bytes 8388608 | tf_op jit(solution)/shard_map/pallas_call | solution.py:356
  21.4 0.1 collective-permute-start.2
  21.5 1.7 %collective-permute-start.3 = (bf16[128,384]{1,0:T(8,128)(2,1)S(1)}, bf16[128,384]{1,0:T(8,128)(2,1)S(1)}, u32[]{:S(2)}, u32[]{:S(2)}) collective-permute-start(bf16[128,384]{1,0:T(8,128)(2,1)S(1)} %get-tuple-element.67), channel_id=1, source_target_pairs={{0,2},{1,3},{2,0},{3,1},{4,6},{5,7},{6,4},{7,5},{8,10},{9,11},{10,... | collective-permute-start | bytes 294920 | tf_op jit(solution)/shard_map/ppermute | solution.py:318
  23.2 0.2 collective-permute-start.4
  23.4 0.0 collective-permute-done.5.before_ref
  23.4 0.0 collective-permute-done.6.after_ref
  23.4 3.1 %shard_map.155 = (bf16[256,1536]{1,0:T(8,128)(2,1)S(1)}, bf16[256,1536]{1,0:T(8,128)(2,1)S(1)}, bf16[256,1536]{1,0:T(8,128)(2,1)S(1)}, bf16[256,1536]{1,0:T(8,12...) custom-call(s32[1]{0:T(128)} %bitcast.3.rank_ref, ...), custom_call_target="tpu_custom_call" | custom-call | flops 905969664 | bytes 8388608 | tf_op jit(solution)/shard_map/pallas_call | solution.py:356
  26.5 0.4 collective-permute-start.7
  26.8 1.6 %collective-permute-start.8 = (bf16[128,384]{1,0:T(8,128)(2,1)S(1)}, bf16[128,384]{1,0:T(8,128)(2,1)S(1)}, u32[]{:S(2)}, u32[]{:S(2)}) collective-permute-start(bf16[128,384]{1,0:T(8,128)(2,1)S(1)} %get-tuple-element.72), channel_id=1, source_target_pairs={{0,2},{1,3},{2,0},{3,1},{4,6},{5,7},{6,4},{7,5},{8,10},{9,11},{10,... | collective-permute-start | bytes 294920 | tf_op jit(solution)/shard_map/ppermute | solution.py:318
  28.5 0.0 collective-permute-done.2.refs_1_
  28.5 0.0 collective-permute-start.9
  28.5 0.7 pad_add_fusion.1.where_ref
  29.2 0.0 collective-permute-done.3.refs_2_
  29.2 0.0 collective-permute-done.4.refs_3_
  29.2 0.0 collective-permute-done.7.refs_5_
  29.2 2.7 %collective-permute-done.8.refs_6_ = bf16[128,384]{1,0:T(8,128)(2,1)S(1)} collective-permute-done((bf16[128,384]{1,0:T(8,128)(2,1)S(1)}, bf16[128,384]{1,0:T(8,128)(2,1)S(1)}, u32[]{:S(2)}, u32[]{:S(2)}) %collective-permute-start.8) | collective-permute-done | bytes 98336 | tf_op jit(solution)/shard_map/ppermute | solution.py:318
  32.0 1.6 %collective-permute-done.9.refs_7_ = bf16[128,384]{1,0:T(8,128)(2,1)S(1)} collective-permute-done((bf16[128,384]{1,0:T(8,128)(2,1)S(1)}, bf16[128,384]{1,0:T(8,128)(2,1)S(1)}, u32[]{:S(2)}, u32[]{:S(2)}) %collective-permute-start.9) | collective-permute-done | bytes 98336 | tf_op jit(solution)/shard_map/ppermute | solution.py:318
  33.6 2.5 %shard_map.156 = (bf16[128,384]{1,0:T(8,128)(2,1)S(1)}, bf16[128,384]{1,0:T(8,128)(2,1)S(1)}, bf16[128,384]{1,0:T(8,128)(2,1)S(1)}, bf16[128,384]{1,0:T(8,128)(2...) custom-call(s32[2]{0:T(128)S(1)} %pad_add_fusion.1.where_ref, ...), custom_call_target="tpu_custom_call" | custom-call | flops 4194304 | bytes 2097152 | tf_op jit(solution)/shard_map/pallas_call | solution.py:370
  36.1 0.2 collective-permute-start.10
  36.3 1.6 %collective-permute-start.11 = (bf16[128,384]{1,0:T(8,128)(2,1)S(1)}, bf16[128,384]{1,0:T(8,128)(2,1)S(1)}, u32[]{:S(2)}, u32[]{:S(2)}) collective-permute-start(bf16[128,384]{1,0:T(8,128)(2,1)S(1)} %get-tuple-element.82), channel_id=1, source_target_pairs={{0,2},{1,3},{2,0},{3,1},{4,6},{5,7},{6,4},{7,5},{8,10},{9,11},{10,... | collective-permute-start | bytes 294920 | tf_op jit(solution)/shard_map/ppermute | solution.py:318
  37.9 0.1 collective-permute-start.12
  38.0 0.4 collective-permute-start.13
  38.4 1.6 %collective-permute-start.14 = (bf16[128,384]{1,0:T(8,128)(2,1)S(1)}, bf16[128,384]{1,0:T(8,128)(2,1)S(1)}, u32[]{:S(2)}, u32[]{:S(2)}) collective-permute-start(bf16[128,384]{1,0:T(8,128)(2,1)S(1)} %get-tuple-element.96), channel_id=1, source_target_pairs={{0,2},{1,3},{2,0},{3,1},{4,6},{5,7},{6,4},{7,5},{8,10},{9,11},{10,... | collective-permute-start | bytes 294920 | tf_op jit(solution)/shard_map/ppermute | solution.py:318
  40.0 0.0 collective-permute-done.10.refs_1_
  40.0 0.1 pad_add_fusion.refs_0_.place_ref
  40.1 1.8 %collective-permute-done.11.refs_2_ = bf16[128,384]{1,0:T(8,128)(2,1)S(1)} collective-permute-done((bf16[128,384]{1,0:T(8,128)(2,1)S(1)}, bf16[128,384]{1,0:T(8,128)(2,1)S(1)}, u32[]{:S(2)}, u32[]{:S(2)}) %collective-permute-start.11) | collective-permute-done | bytes 98336 | tf_op jit(solution)/shard_map/ppermute | solution.py:318
  41.9 1.3 %collective-permute-done.12.refs_3_ = bf16[128,384]{1,0:T(8,128)(2,1)S(1)} collective-permute-done((bf16[128,384]{1,0:T(8,128)(2,1)S(1)}, bf16[128,384]{1,0:T(8,128)(2,1)S(1)}, u32[]{:S(2)}, u32[]{:S(2)}) %collective-permute-start.12) | collective-permute-done | bytes 98336 | tf_op jit(solution)/shard_map/ppermute | solution.py:318
  43.1 2.0 %shard_map.157 = (bf16[128,1536]{1,0:T(8,128)(2,1)S(1)}, bf16[256,1536]{1,0:T(8,128)(2,1)S(1)}, bf16[256,1536]{1,0:T(8,128)(2,1)S(1)}, bf16[256,1536]{1,0:T(8,12...) custom-call(s32[1]{0:T(128)} %bitcast.3.rank_ref, ...), custom_call_target="tpu_custom_call" | custom-call | flops 905969664 | bytes 6291456 | tf_op jit(solution)/shard_map/pallas_call | solution.py:385
  45.2 0.9 collective-permute-done.14.refs_2_
  46.1 1.1 %collective-permute-done.15.refs_3_ = bf16[128,384]{1,0:T(8,128)(2,1)S(1)} collective-permute-done((bf16[128,384]{1,0:T(8,128)(2,1)S(1)}, bf16[128,384]{1,0:T(8,128)(2,1)S(1)}, u32[]{:S(2)}, u32[]{:S(2)}) %collective-permute-start.15) | collective-permute-done | bytes 98336 | tf_op jit(solution)/shard_map/ppermute | solution.py:318
  47.2 2.2 %shard_map.158 = (bf16[128,1536]{1,0:T(8,128)(2,1)S(1)}, bf16[256,1536]{1,0:T(8,128)(2,1)S(1)}, bf16[256,1536]{1,0:T(8,128)(2,1)S(1)}, bf16[256,1536]{1,0:T(8,12...) custom-call(s32[1]{0:T(128)} %bitcast.3.rank_ref, ...), custom_call_target="tpu_custom_call" | custom-call | flops 905969664 | bytes 6291456 | tf_op jit(solution)/shard_map/pallas_call | solution.py:385
  49.4 2.0 %shard_map.159 = (bf16[384,256]{1,0:T(8,128)(2,1)S(1)}, bf16[384,256]{1,0:T(8,128)(2,1)S(1)}) custom-call(s32[2]{0:T(128)S(1)} %pad_add_fusion.refs_0_.place_ref, f32[1,128]{1,0:T(1,128)S(1)} %get-tuple-element.74.refs_1_, bf16[256,1536]{1,0:T(8,128)(2,1)S(1)} %get-tuple-element.75.refs_2_, bf16[256,1536]{1,0:T(8,128)(2,1)S(1)} %get-tuple-element.76.refs_3_, ...), custom_call_target="tpu_custom_call" | custom-call | flops 1006632960 | bytes 10485760 | tf_op jit(solution)/shard_map/pallas_call | solution.py:406
  51.3 0.4 collective-permute-start.16
  51.7 1.8 %shard_map.161.own_ref = f32[2,1024,256]{2,1,0:T(8,128)S(1)} custom-call(bf16[1536,1536]{1,0:T(8,128)(2,1)S(1)} %get-tuple-element.64.table_ref, bf16[256,1536]{1,0:T(8,128)(2,1)S(1)} %get-tuple-element.105.refs_0_, bf16[256,1536]{1,0:T(8,128)(2,1)S(1)} %get-tuple-element.106.refs_1_), custom_call_target="tpu_custom_call" | custom-call | flops 1610612736 | bytes 6291456 | tf_op jit(solution)/shard_map/pallas_call | solution.py:417
  53.6 0.0 collective-permute-done.16.other_ref
  53.6 11.0 %all_to_all.17.pieces_ref = bf16[8,48,256]{2,1,0:T(8,128)(2,1)S(1)} all-to-all(bf16[8,48,256]{2,1,0:T(8,128)(2,1)S(1)} %bitcast.22), channel_id=1, replica_groups=mesh['groups'=2,'space'=4,'pair'=2,'core'=2] {'space','pair'}, dimensions={0} | all-to-all | bytes 393216 | tf_op jit(solution)/shard_map/all_to_all | solution.py:427
  64.6 10.7 %all_to_all.18 = bf16[8,48,256]{2,1,0:T(8,128)(2,1)S(1)} all-to-all(bf16[8,48,256]{2,1,0:T(8,128)(2,1)S(1)} %shard_map.162), channel_id=1, replica_groups=mesh['groups'=2,'space'=4,'pair'=2,'core'=2] {'space','pair'}, dimensions={0} | all-to-all | bytes 393216 | tf_op jit(solution)/shard_map/all_to_all | solution.py:429
  75.3 0.0 collective-permute-start.17
  75.3 0.2 collective-permute-start.18
  75.6 1.0 %collective-permute-start.19 = (bf16[256,256]{1,0:T(8,128)(2,1)S(1)}, bf16[256,256]{1,0:T(8,128)(2,1)S(1)}, u32[]{:S(2)}, u32[]{:S(2)}) collective-permute-start(bf16[256,256]{1,0:T(8,128)(2,1)S(1)} %get-tuple-element.111), channel_id=1, source_target_pairs={{0,4},{4,8},{8,12},{12,0},{1,5},{5,9},{9,13},{13,1},{2,6},{6,10},{... | collective-permute-start | bytes 393224 | tf_op jit(solution)/shard_map/ppermute | solution.py:314
  76.6 2.8 %collective-permute-start.20 = (bf16[256,256]{1,0:T(8,128)(2,1)S(1)}, bf16[256,256]{1,0:T(8,128)(2,1)S(1)}, u32[]{:S(2)}, u32[]{:S(2)}) collective-permute-start(bf16[256,256]{1,0:T(8,128)(2,1)S(1)} %get-tuple-element.112), channel_id=1, source_target_pairs={{0,12},{4,0},{8,4},{12,8},{1,13},{5,1},{9,5},{13,9},{2,14},{6,2},{... | collective-permute-start | bytes 393224 | tf_op jit(solution)/shard_map/ppermute | solution.py:314
  79.4 1.8 %collective-permute-start.21 = (bf16[256,256]{1,0:T(8,128)(2,1)S(1)}, bf16[256,256]{1,0:T(8,128)(2,1)S(1)}, u32[]{:S(2)}, u32[]{:S(2)}) collective-permute-start(bf16[256,256]{1,0:T(8,128)(2,1)S(1)} %get-tuple-element.113), channel_id=1, source_target_pairs={{0,12},{4,0},{8,4},{12,8},{1,13},{5,1},{9,5},{13,9},{2,14},{6,2},{... | collective-permute-start | bytes 393224 | tf_op jit(solution)/shard_map/ppermute | solution.py:314
  81.2 2.4 %collective-permute-done.18.refs_0_ = bf16[256,256]{1,0:T(8,128)(2,1)S(1)} collective-permute-done((bf16[256,256]{1,0:T(8,128)(2,1)S(1)}, bf16[256,256]{1,0:T(8,128)(2,1)S(1)}, u32[]{:S(2)}, u32[]{:S(2)}) %collective-permute-start.18) | collective-permute-done | bytes 131104 | tf_op jit(solution)/shard_map/ppermute | solution.py:314
  83.6 2.7 %collective-permute-done.19.refs_1_ = bf16[256,256]{1,0:T(8,128)(2,1)S(1)} collective-permute-done((bf16[256,256]{1,0:T(8,128)(2,1)S(1)}, bf16[256,256]{1,0:T(8,128)(2,1)S(1)}, u32[]{:S(2)}, u32[]{:S(2)}) %collective-permute-start.19) | collective-permute-done | bytes 131104 | tf_op jit(solution)/shard_map/ppermute | solution.py:314
  86.3 2.2 %collective-permute-done.20.refs_2_ = bf16[256,256]{1,0:T(8,128)(2,1)S(1)} collective-permute-done((bf16[256,256]{1,0:T(8,128)(2,1)S(1)}, bf16[256,256]{1,0:T(8,128)(2,1)S(1)}, u32[]{:S(2)}, u32[]{:S(2)}) %collective-permute-start.20) | collective-permute-done | bytes 131104 | tf_op jit(solution)/shard_map/ppermute | solution.py:314
  88.5 1.8 %collective-permute-done.21.refs_3_ = bf16[256,256]{1,0:T(8,128)(2,1)S(1)} collective-permute-done((bf16[256,256]{1,0:T(8,128)(2,1)S(1)}, bf16[256,256]{1,0:T(8,128)(2,1)S(1)}, u32[]{:S(2)}, u32[]{:S(2)}) %collective-permute-start.21) | collective-permute-done | bytes 131104 | tf_op jit(solution)/shard_map/ppermute | solution.py:314
  90.3 1.1 %shard_map.164 = bf16[2,1024,256]{2,1,0:T(8,128)(2,1)} custom-call(f32[2,1024,256]{2,1,0:T(8,128)S(1)} %shard_map.161.own_ref, bf16[256,256]{1,0:T(8,128)(2,1)S(1)} %collective-permute-done.18.refs_0_, bf16[256,256]{1,0:T(8,128)(2,1)S(1)} %collective-permute-done.19.refs_1_, bf16[256,256]{1,0:T(8,128)(2,1)S(1)} %collective-permute-done.20.refs_2_, ...), custom_call_target="tpu_custom_call" | custom-call | flops 1048576 | bytes 3145728 | tf_op jit(solution)/shard_map/pallas_call | solution.py:442
  91.5 0.0 collective-permute-done.17.other_ref
  91.5 1.4 %shard_map.163 = (f32[256,256]{1,0:T(8,128)}, f32[1,256]{1,0:T(1,128)}, f32[256,256]{1,0:T(8,128)}, f32[1,256]{1,0:T(1,128)}, f32[256,128]{1,0:T(8,128)}, /*index=5*/f32[1,256]{1,0:T(1,128)S(1)}) custom-call(s32[2]{0:T(128)S(1)} %pad_add_fusion.refs_0_.place_ref, bf16[384,256]{1,0:T(8,128)(2,1)S(1)} %bitcast.21, ...), custom_call_target="tpu_custom_call" | custom-call | flops 1048576 | bytes 2097152 | tf_op jit(solution)/shard_map/pallas_call | solution.py:432
  92.9 0.5 multiply_bitcast_fusion
  (18 shorter events, 0.1 us)
Async XLA Ops:
  0.6 20.8 %copy-start = (bf16[1536,128]{1,0:T(8,128)(2,1)S(1)}, bf16[1536,128]{1,0:T(8,128)(2,1)}, u32[]{:S(2)}) copy-start(bf16[1536,128]{1,0:T(8,128)(2,1)} %param.13) | copy-start | bytes 1179652
  1.8 16.4 %collective-permute-start = (bf16[256,256]{1,0:T(8,128)(2,1)S(1)}, bf16[256,256]{1,0:T(8,128)(2,1)S(1)}, u32[]{:S(2)}, u32[]{:S(2)}) collective-permute-start(bf16[256,256]{1,0:T(8,128)(2,1)S(1)} %get-tuple-element.121), channel_id=1, source_target_pairs={{0,4},{4,8},{8,12},{12,0},{1,5},{5,9},{9,13},{13,1},{2,6},{6,10},{... | collective-permute-start | bytes 393224 | tf_op jit(solution)/shard_map/ppermute | solution.py:314
  4.9 13.3 %collective-permute-start.1 = (bf16[256,256]{1,0:T(8,128)(2,1)S(1)}, bf16[256,256]{1,0:T(8,128)(2,1)S(1)}, u32[]{:S(2)}, u32[]{:S(2)}) collective-permute-start(bf16[256,256]{1,0:T(8,128)(2,1)S(1)} %get-tuple-element.120), channel_id=1, source_target_pairs={{0,12},{4,0},{8,4},{12,8},{1,13},{5,1},{9,5},{13,9},{2,14},{6,2},{... | collective-permute-start | bytes 393224 | tf_op jit(solution)/shard_map/ppermute | solution.py:314
  7.0 16.4 %collective-permute-start.5 = (bf16[256,256]{1,0:T(8,128)(2,1)S(1)}, bf16[256,256]{1,0:T(8,128)(2,1)S(1)}, u32[]{:S(2)}, u32[]{:S(2)}) collective-permute-start(bf16[256,256]{1,0:T(8,128)(2,1)S(1)} %get-tuple-element.122), channel_id=1, source_target_pairs={{0,4},{4,8},{8,12},{12,0},{1,5},{5,9},{9,13},{13,1},{2,6},{6,10},{... | collective-permute-start | bytes 393224 | tf_op jit(solution)/shard_map/ppermute | solution.py:314
  7.0 16.4 %collective-permute-start.6 = (bf16[256,256]{1,0:T(8,128)(2,1)S(1)}, bf16[256,256]{1,0:T(8,128)(2,1)S(1)}, u32[]{:S(2)}, u32[]{:S(2)}) collective-permute-start(bf16[256,256]{1,0:T(8,128)(2,1)S(1)} %get-tuple-element.119), channel_id=1, source_target_pairs={{0,12},{4,0},{8,4},{12,8},{1,13},{5,1},{9,5},{13,9},{2,14},{6,2},{... | collective-permute-start | bytes 393224 | tf_op jit(solution)/shard_map/ppermute | solution.py:314
  12.1 1.2 %copy-start.4 = (bf16[2,1024,256]{2,1,0:T(8,128)(2,1)S(1)}, bf16[2,1024,256]{2,1,0:T(8,128)(2,1)}, u32[]{:S(2)}) copy-start(bf16[2,1024,256]{2,1,0:T(8,128)(2,1)} %latent_ref.1) | copy-start | bytes 3145732
  13.3 0.7 copy-start.7
  14.0 0.7 copy-start.8
  14.8 3.5 %copy-start.1 = (bf16[256,256]{1,0:T(8,128)(2,1)S(1)}, bf16[256,256]{1,0:T(8,128)(2,1)}, u32[]{:S(2)}) copy-start(bf16[256,256]{1,0:T(8,128)(2,1)} %w_one_ref.7) | copy-start | bytes 393220
  14.8 3.5 %copy-start.2 = (bf16[256,256]{1,0:T(8,128)(2,1)S(1)}, bf16[256,256]{1,0:T(8,128)(2,1)}, u32[]{:S(2)}) copy-start(bf16[256,256]{1,0:T(8,128)(2,1)} %w_two_ref.7) | copy-start | bytes 393220
  14.8 3.5 %copy-start.3 = (bf16[256,128]{1,0:T(8,128)(2,1)S(1)}, bf16[256,128]{1,0:T(8,128)(2,1)}, u32[]{:S(2)}) copy-start(bf16[256,128]{1,0:T(8,128)(2,1)} %w_three_ref.7) | copy-start | bytes 196612
  14.8 3.5 %copy-start.5 = (f32[256]{0:T(256)S(1)}, f32[256]{0:T(256)}, u32[]{:S(2)}) copy-start(f32[256]{0:T(256)} %param.16) | copy-start | bytes 3076
  14.8 3.5 %copy-start.6 = (f32[256]{0:T(256)S(1)}, f32[256]{0:T(256)}, u32[]{:S(2)}) copy-start(f32[256]{0:T(256)} %param.18) | copy-start | bytes 3076
  21.4 7.1 %collective-permute-start.2 = (bf16[128,384]{1,0:T(8,128)(2,1)S(1)}, bf16[128,384]{1,0:T(8,128)(2,1)S(1)}, u32[]{:S(2)}, u32[]{:S(2)}) collective-permute-start(bf16[128,384]{1,0:T(8,128)(2,1)S(1)} %get-tuple-element.66), channel_id=1, source_target_pairs={{0,1},{1,0},{2,3},{3,2},{4,5},{5,4},{6,7},{7,6},{8,9},{9,8},{10,11... | collective-permute-start | bytes 294920 | tf_op jit(solution)/shard_map/ppermute | solution.py:318
  21.5 7.7 %collective-permute-start.3 = (bf16[128,384]{1,0:T(8,128)(2,1)S(1)}, bf16[128,384]{1,0:T(8,128)(2,1)S(1)}, u32[]{:S(2)}, u32[]{:S(2)}) collective-permute-start(bf16[128,384]{1,0:T(8,128)(2,1)S(1)} %get-tuple-element.67), channel_id=1, source_target_pairs={{0,2},{1,3},{2,0},{3,1},{4,6},{5,7},{6,4},{7,5},{8,10},{9,11},{10,... | collective-permute-start | bytes 294920 | tf_op jit(solution)/shard_map/ppermute | solution.py:318
  23.2 6.0 %collective-permute-start.4 = (bf16[128,384]{1,0:T(8,128)(2,1)S(1)}, bf16[128,384]{1,0:T(8,128)(2,1)S(1)}, u32[]{:S(2)}, u32[]{:S(2)}) collective-permute-start(bf16[128,384]{1,0:T(8,128)(2,1)S(1)} %get-tuple-element.68), channel_id=1, source_target_pairs={{0,3},{1,2},{2,1},{3,0},{4,7},{5,6},{6,5},{7,4},{8,11},{9,10},{10,... | collective-permute-start | bytes 294920 | tf_op jit(solution)/shard_map/ppermute | solution.py:318
  26.5 2.8 %collective-permute-start.7 = (bf16[128,384]{1,0:T(8,128)(2,1)S(1)}, bf16[128,384]{1,0:T(8,128)(2,1)S(1)}, u32[]{:S(2)}, u32[]{:S(2)}) collective-permute-start(bf16[128,384]{1,0:T(8,128)(2,1)S(1)} %get-tuple-element.71), channel_id=1, source_target_pairs={{0,1},{1,0},{2,3},{3,2},{4,5},{5,4},{6,7},{7,6},{8,9},{9,8},{10,11... | collective-permute-start | bytes 294920 | tf_op jit(solution)/shard_map/ppermute | solution.py:318
  26.8 5.1 %collective-permute-start.8 = (bf16[128,384]{1,0:T(8,128)(2,1)S(1)}, bf16[128,384]{1,0:T(8,128)(2,1)S(1)}, u32[]{:S(2)}, u32[]{:S(2)}) collective-permute-start(bf16[128,384]{1,0:T(8,128)(2,1)S(1)} %get-tuple-element.72), channel_id=1, source_target_pairs={{0,2},{1,3},{2,0},{3,1},{4,6},{5,7},{6,4},{7,5},{8,10},{9,11},{10,... | collective-permute-start | bytes 294920 | tf_op jit(solution)/shard_map/ppermute | solution.py:318
  28.5 5.1 %collective-permute-start.9 = (bf16[128,384]{1,0:T(8,128)(2,1)S(1)}, bf16[128,384]{1,0:T(8,128)(2,1)S(1)}, u32[]{:S(2)}, u32[]{:S(2)}) collective-permute-start(bf16[128,384]{1,0:T(8,128)(2,1)S(1)} %get-tuple-element.73), channel_id=1, source_target_pairs={{0,3},{1,2},{2,1},{3,0},{4,7},{5,6},{6,5},{7,4},{8,11},{9,10},{10,... | collective-permute-start | bytes 294920 | tf_op jit(solution)/shard_map/ppermute | solution.py:318
  36.1 3.9 %collective-permute-start.10 = (bf16[128,384]{1,0:T(8,128)(2,1)S(1)}, bf16[128,384]{1,0:T(8,128)(2,1)S(1)}, u32[]{:S(2)}, u32[]{:S(2)}) collective-permute-start(bf16[128,384]{1,0:T(8,128)(2,1)S(1)} %get-tuple-element.81), channel_id=1, source_target_pairs={{0,1},{1,0},{2,3},{3,2},{4,5},{5,4},{6,7},{7,6},{8,9},{9,8},{10,11... | collective-permute-start | bytes 294920 | tf_op jit(solution)/shard_map/ppermute | solution.py:318
  36.3 5.6 %collective-permute-start.11 = (bf16[128,384]{1,0:T(8,128)(2,1)S(1)}, bf16[128,384]{1,0:T(8,128)(2,1)S(1)}, u32[]{:S(2)}, u32[]{:S(2)}) collective-permute-start(bf16[128,384]{1,0:T(8,128)(2,1)S(1)} %get-tuple-element.82), channel_id=1, source_target_pairs={{0,2},{1,3},{2,0},{3,1},{4,6},{5,7},{6,4},{7,5},{8,10},{9,11},{10,... | collective-permute-start | bytes 294920 | tf_op jit(solution)/shard_map/ppermute | solution.py:318
  37.9 5.3 %collective-permute-start.12 = (bf16[128,384]{1,0:T(8,128)(2,1)S(1)}, bf16[128,384]{1,0:T(8,128)(2,1)S(1)}, u32[]{:S(2)}, u32[]{:S(2)}) collective-permute-start(bf16[128,384]{1,0:T(8,128)(2,1)S(1)} %get-tuple-element.83), channel_id=1, source_target_pairs={{0,3},{1,2},{2,1},{3,0},{4,7},{5,6},{6,5},{7,4},{8,11},{9,10},{10,... | collective-permute-start | bytes 294920 | tf_op jit(solution)/shard_map/ppermute | solution.py:318
  38.0 7.2 %collective-permute-start.13 = (bf16[128,384]{1,0:T(8,128)(2,1)S(1)}, bf16[128,384]{1,0:T(8,128)(2,1)S(1)}, u32[]{:S(2)}, u32[]{:S(2)}) collective-permute-start(bf16[128,384]{1,0:T(8,128)(2,1)S(1)} %get-tuple-element.95), channel_id=1, source_target_pairs={{0,1},{1,0},{2,3},{3,2},{4,5},{5,4},{6,7},{7,6},{8,9},{9,8},{10,11... | collective-permute-start | bytes 294920 | tf_op jit(solution)/shard_map/ppermute | solution.py:318
  38.4 7.6 %collective-permute-start.14 = (bf16[128,384]{1,0:T(8,128)(2,1)S(1)}, bf16[128,384]{1,0:T(8,128)(2,1)S(1)}, u32[]{:S(2)}, u32[]{:S(2)}) collective-permute-start(bf16[128,384]{1,0:T(8,128)(2,1)S(1)} %get-tuple-element.96), channel_id=1, source_target_pairs={{0,2},{1,3},{2,0},{3,1},{4,6},{5,7},{6,4},{7,5},{8,10},{9,11},{10,... | collective-permute-start | bytes 294920 | tf_op jit(solution)/shard_map/ppermute | solution.py:318
  40.0 7.2 %collective-permute-start.15 = (bf16[128,384]{1,0:T(8,128)(2,1)S(1)}, bf16[128,384]{1,0:T(8,128)(2,1)S(1)}, u32[]{:S(2)}, u32[]{:S(2)}) collective-permute-start(bf16[128,384]{1,0:T(8,128)(2,1)S(1)} %get-tuple-element.97), channel_id=1, source_target_pairs={{0,3},{1,2},{2,1},{3,0},{4,7},{5,6},{6,5},{7,4},{8,11},{9,10},{10,... | collective-permute-start | bytes 294920 | tf_op jit(solution)/shard_map/ppermute | solution.py:318
  51.3 2.2 %collective-permute-start.16 = (bf16[384,256]{1,0:T(8,128)(2,1)S(1)}, bf16[384,256]{1,0:T(8,128)(2,1)S(1)}, u32[]{:S(2)}, u32[]{:S(2)}) collective-permute-start(bf16[384,256]{1,0:T(8,128)(2,1)S(1)} %get-tuple-element.104), channel_id=1, source_target_pairs={{0,1},{1,0},{2,3},{3,2},{4,5},{5,4},{6,7},{7,6},{8,9},{9,8},{10,11... | collective-permute-start | bytes 589832 | tf_op jit(solution)/shard_map/ppermute | solution.py:416
  75.3 16.1 %collective-permute-start.17 = (bf16[384,256]{1,0:T(8,128)(2,1)S(1)}, bf16[384,256]{1,0:T(8,128)(2,1)S(1)}, u32[]{:S(2)}, u32[]{:S(2)}) collective-permute-start(bf16[384,256]{1,0:T(8,128)(2,1)S(1)} %bitcast.20), channel_id=1, source_target_pairs={{0,1},{1,0},{2,3},{3,2},{4,5},{5,4},{6,7},{7,6},{8,9},{9,8},{10,11... | collective-permute-start | bytes 589832 | tf_op jit(solution)/shard_map/ppermute | solution.py:430
  75.3 8.2 %collective-permute-start.18 = (bf16[256,256]{1,0:T(8,128)(2,1)S(1)}, bf16[256,256]{1,0:T(8,128)(2,1)S(1)}, u32[]{:S(2)}, u32[]{:S(2)}) collective-permute-start(bf16[256,256]{1,0:T(8,128)(2,1)S(1)} %get-tuple-element.110), channel_id=1, source_target_pairs={{0,4},{4,8},{8,12},{12,0},{1,5},{5,9},{9,13},{13,1},{2,6},{6,10},{... | collective-permute-start | bytes 393224 | tf_op jit(solution)/shard_map/ppermute | solution.py:314
  75.6 10.7 %collective-permute-start.19 = (bf16[256,256]{1,0:T(8,128)(2,1)S(1)}, bf16[256,256]{1,0:T(8,128)(2,1)S(1)}, u32[]{:S(2)}, u32[]{:S(2)}) collective-permute-start(bf16[256,256]{1,0:T(8,128)(2,1)S(1)} %get-tuple-element.111), channel_id=1, source_target_pairs={{0,4},{4,8},{8,12},{12,0},{1,5},{5,9},{9,13},{13,1},{2,6},{6,10},{... | collective-permute-start | bytes 393224 | tf_op jit(solution)/shard_map/ppermute | solution.py:314
  76.6 12.0 %collective-permute-start.20 = (bf16[256,256]{1,0:T(8,128)(2,1)S(1)}, bf16[256,256]{1,0:T(8,128)(2,1)S(1)}, u32[]{:S(2)}, u32[]{:S(2)}) collective-permute-start(bf16[256,256]{1,0:T(8,128)(2,1)S(1)} %get-tuple-element.112), channel_id=1, source_target_pairs={{0,12},{4,0},{8,4},{12,8},{1,13},{5,1},{9,5},{13,9},{2,14},{6,2},{... | collective-permute-start | bytes 393224 | tf_op jit(solution)/shard_map/ppermute | solution.py:314
  79.4 10.9 %collective-permute-start.21 = (bf16[256,256]{1,0:T(8,128)(2,1)S(1)}, bf16[256,256]{1,0:T(8,128)(2,1)S(1)}, u32[]{:S(2)}, u32[]{:S(2)}) collective-permute-start(bf16[256,256]{1,0:T(8,128)(2,1)S(1)} %get-tuple-element.113), channel_id=1, source_target_pairs={{0,12},{4,0},{8,4},{12,8},{1,13},{5,1},{9,5},{13,9},{2,14},{6,2},{... | collective-permute-start | bytes 393224 | tf_op jit(solution)/shard_map/ppermute | solution.py:314

commit v2 on v1

--- a/solution.py
+++ b/solution.py
@@ -29,13 +29,13 @@
     return jnp.dot(left, right, preferred_element_type=jnp.float32)
 
 
-def kernel_call(body, out_shape, flops, moved, scratch=(), smem=0, operands=0):
+def kernel_call(body, out_shape, flops, moved, scratch=(), smem=0, hbm=0, operands=0):
     vmem = pl.BlockSpec(memory_space=pltpu.VMEM)
-    specs = [pl.BlockSpec(memory_space=pltpu.SMEM)] * smem + [vmem] * (operands - smem)
+    specs = [pl.BlockSpec(memory_space=pltpu.SMEM)] * smem + [pl.BlockSpec(memory_space=pltpu.HBM)] * hbm
     return pl.pallas_call(
         body,
         out_shape=out_shape,
-        in_specs=specs,
+        in_specs=specs + [vmem] * (operands - len(specs)),
         out_specs=jax.tree.map(lambda _: vmem, out_shape),
         scratch_shapes=list(scratch),
         compiler_params=pltpu.CompilerParams(vmem_limit_bytes=40 * MIB),
@@ -43,10 +43,21 @@
     )
 
 
-def table_kernel(count_ref, nbr_ref, weight_ref, latent_ref, table_ref, *part_refs):
+def table_kernel(region_ref, counts_ref, nbr_hbm, weight_hbm, latent_hbm, table_ref, *refs):
+    *part_refs, nbr_ref, weight_ref, latent_ref, sems = refs
     members, nodes, width = latent_ref.shape
     ext, slots = table_ref.shape
-    live = lax.broadcasted_iota(jnp.int32, (1, slots), 1) < count_ref[0]
+    fetches = [
+        pltpu.make_async_copy(source, to, sems.at[i])
+        for i, (source, to) in enumerate(
+            ((nbr_hbm, nbr_ref), (weight_hbm, weight_ref), (latent_hbm, latent_ref))
+        )
+    ]
+    for fetch in fetches:
+        fetch.start()
+    fetches[0].wait()
+    fetches[1].wait()
+    live = lax.broadcasted_iota(jnp.int32, (1, slots), 1) < counts_ref[region_ref[0]]
     nbr = [nbr_ref[k : k + 1, :] for k in range(K)]
     own = [jnp.where(live, weight_ref[k : k + 1, :], 0.0) for k in range(K)]
     joint = []
@@ -73,6 +84,7 @@
                 near = jnp.broadcast_to(near, (16, size)).astype(jnp.bfloat16)
                 tile = jnp.where(rows[:, :, :size] == near[None], wide[k][None], tile)
             table_ref[b * BLOCK : (b + 1) * BLOCK, lo : lo + size] = tile.reshape(BLOCK, size)
+    fetches[2].wait()
     turned = jnp.concatenate([latent_ref[m].T for m in range(members)], axis=0)
     for lo, size in split(slots, CHUNK):
         part = nn_dot(turned, table_ref[HALO : HALO + nodes, lo : lo + size])
@@ -122,7 +134,7 @@
         decoded_refs[i][...] = stage_ref[i]
 
 
-def score_kernel(where_ref, target_ref, *refs):
+def score_kernel(region_ref, rank_ref, counts_ref, target_ref, *refs):
     count = (len(refs) - 1) // 2
     decoded_refs, grad_refs, score_ref = refs[:count], refs[count : 2 * count], refs[2 * count]
     channels, share = decoded_refs[0].shape
@@ -147,8 +159,8 @@
                 to_target[i] = to_target[i] + fold((values[i] - goal) ** 2)
             for p, (i, j) in enumerate(pairs):
                 apart[p] = apart[p] + fold((values[i] - values[j]) ** 2)
-        slot = where_ref[1] + lo + lax.broadcasted_iota(jnp.int32, (1, size), 1)
-        live = (slot < where_ref[0]).astype(jnp.float32)
+        slot = rank_ref[0] * share + lo + lax.broadcasted_iota(jnp.int32, (1, size), 1)
+        live = (slot < counts_ref[region_ref[0]]).astype(jnp.float32)
         score = jnp.zeros((1, size), jnp.float32)
 
         def inverse(square, scale):
@@ -187,11 +199,9 @@
     score_ref[...] = total
 
 
-def backward_kernel(rank_ref, table_ref, slope_one_ref, slope_two_ref, w_one_ref, w_two_ref, w_three_ref, *refs):
-    *refs, stage_ref = refs
+def backward(rank_ref, table_ref, slope_one_ref, slope_two_ref, w_one_ref, w_two_ref, w_three_ref, grad_refs, out_refs, stage_ref):
+    d_dec_ref, d_two_ref, d_one_ref, d_mixed_ref, bias_one_ref, bias_two_ref, head_ref, tail_ref = out_refs
     ranks, channels, share = stage_ref.shape
-    grad_refs = refs[:ranks]
-    d_dec_ref, d_two_ref, d_one_ref, d_mixed_ref, bias_one_ref, bias_two_ref, head_ref, tail_ref = refs[ranks:]
     ext, slots = table_ref.shape
     hidden = slope_one_ref.shape[0]
     for i in range(ranks):
@@ -222,71 +232,88 @@
     tail_ref[...] = nt_dot(table_ref[ext - HALO :, :], d_mixed_ref[...]).astype(jnp.bfloat16)
 
 
-def sums_kernel(members, place_ref, score_ref, *refs):
-    *refs, keep_ref, send_ref, stage_ref = refs
-    saved = [refs[8 * m : 8 * (m + 1)] for m in range(members)]
-    width, _ = saved[0][0].shape
-    hidden, _ = saved[0][1].shape
-    channels, _ = saved[0][5].shape
-    rows = stage_ref.shape[0] * stage_ref.shape[1]
-
-    def weight_sum(left, right):
-        return sum(nt_dot(member[left][...], member[right][...]) for member in saved)
-
-    def lane_total(at):
-        return jnp.sum(sum(member[at][...] for member in saved).T, axis=0, keepdims=True)
-
-    g_three = weight_sum(2, 5)
+def backward_kernel(ranks, *refs):
+    backward(*refs[:7], refs[7 : 7 + ranks], refs[7 + ranks : -1], refs[-1])
+
+
+def weights_kernel(mixed_ref, act_one_ref, act_two_ref, d_one_ref, d_two_ref, d_dec_ref, one_ref, two_ref, three_ref):
+    one_ref[...] = nt_dot(mixed_ref[...], d_one_ref[...])
+    two_ref[...] = nt_dot(act_one_ref[...], d_two_ref[...])
+    three_ref[...] = nt_dot(act_two_ref[...], d_dec_ref[...])
+
+
+def last_backward_kernel(ranks, earlier, region_ref, *refs):
+    base, refs = refs[:7], refs[7:]
+    grad_refs, refs = refs[:ranks], refs[ranks:]
+    score_ref, mixed_ref, act_one_ref, act_two_ref = refs[:4]
+    before, refs = refs[4 : 4 + 5 * earlier], refs[4 + 5 * earlier :]
+    d_mixed_ref, head_ref, tail_ref = refs[:3]
+    piece_refs = refs[3 : 3 + ranks]
+    d_dec_ref, d_two_ref, d_one_ref, bias_one_ref, bias_two_ref, grad_stage_ref, stage_ref = refs[3 + ranks :]
+    results = (d_dec_ref, d_two_ref, d_one_ref, d_mixed_ref, bias_one_ref, bias_two_ref, head_ref, tail_ref)
+    backward(*base, grad_refs, results, grad_stage_ref)
+
+    def with_earlier(at, value):
+        return sum((before[5 * e + at][...] for e in range(earlier)), value)
+
+    def bias_row(at, ref):
+        return jnp.sum(with_earlier(at, ref[...]).T, axis=0, keepdims=True)
+
+    hidden = act_one_ref.shape[0]
     half = hidden // 2
-    region = lax.broadcasted_iota(jnp.int32, (1, hidden), 1) == place_ref[0]
+    g_one = with_earlier(0, nt_dot(mixed_ref[...], d_one_ref[...]))
+    g_two = with_earlier(1, nt_dot(act_one_ref[...], d_two_ref[...]))
+    g_three = with_earlier(2, nt_dot(act_two_ref[...], d_dec_ref[...]))
+    region = lax.broadcasted_iota(jnp.int32, (1, hidden), 1) == region_ref[0]
     tally = jnp.where(region, jnp.sum(score_ref[...]), 0.0)
     high = tally.astype(jnp.bfloat16).astype(jnp.float32)
-    used = width + hidden + half + 4
     parts = [
-        weight_sum(0, 3),
-        weight_sum(1, 4),
+        g_one,
+        g_two,
         jnp.concatenate([g_three[:half], g_three[half:]], axis=1),
-        lane_total(6),
-        lane_total(7),
+        bias_row(3, bias_one_ref),
+        bias_row(4, bias_two_ref),
         high,
         tally - high,
-        jnp.zeros((rows - used, hidden), jnp.float32),
     ]
+    used = sum(part.shape[0] for part in parts)
+    parts.append(jnp.zeros((ranks * stage_ref.shape[1] - used, hidden), jnp.float32))
     stage_ref[...] = jnp.concatenate(parts, axis=0).astype(stage_ref.dtype).reshape(stage_ref.shape)
-    keep_ref[...] = stage_ref[place_ref[1]]
-    send_ref[...] = stage_ref[1 - place_ref[1]]
-
-
-def pair_sum_kernel(one_ref, other_ref, sum_ref):
-    sum_ref[...] = (one_ref[...].astype(jnp.float32) + other_ref[...].astype(jnp.float32)).astype(sum_ref.dtype)
-
-
-def piece_kernel(pieces_ref, out_ref):
-    ways = pieces_ref.shape[0]
-    total = pieces_ref[0].astype(jnp.float32)
-    for i in range(1, ways):
-        total = total + pieces_ref[i].astype(jnp.float32)
-    total = total.astype(out_ref.dtype)
-    for i in range(ways):
-        out_ref[i] = total
-
-
-def unpack_kernel(place_ref, mine_ref, other_ref, one_ref, b_one_ref, two_ref, b_two_ref, three_ref, tally_ref, stage_ref):
-    stage_ref[place_ref[1]] = mine_ref[...]
-    stage_ref[1 - place_ref[1]] = other_ref[...]
-    sums = stage_ref[...].reshape(-1, mine_ref.shape[1]).astype(jnp.float32)
+    for i in range(ranks):
+        piece_refs[i][0] = stage_ref[base[0][0] ^ i]
+
+
+def halve_kernel(count, *refs):
+    for i in range(count):
+        total = refs[i][...].astype(jnp.float32) + refs[count + i][...].astype(jnp.float32)
+        refs[2 * count + i][...] = total.astype(refs[i].dtype)
+
+
+def region_sum_kernel(region_ref, *refs):
+    *refs, sum_ref, stage_ref = refs
+    for i, ref in enumerate(refs):
+        stage_ref[region_ref[0] ^ i] = ref[0]
+    sum_ref[0] = sum(stage_ref[i].astype(jnp.float32) for i in range(len(refs))).astype(sum_ref.dtype)
+
+
+def unpack_kernel(scale, rank_ref, *refs):
+    *refs, stage_ref = refs
+    ranks = stage_ref.shape[0]
+    one_ref, b_one_ref, two_ref, b_two_ref, three_ref, tally_ref = refs[ranks:]
+    for i in range(ranks):
+        stage_ref[rank_ref[0] ^ i] = refs[i][0]
     width, hidden = one_ref.shape
+    sums = stage_ref[...].reshape(-1, hidden).astype(jnp.float32)
     half, channels = hidden // 2, three_ref.shape[1]
     one_ref[...] = sums[:width]
     two_ref[...] = sums[width : width + hidden]
     base = width + hidden
     three_ref[:half] = sums[base : base + half, :channels]
     three_ref[half:] = sums[base : base + half, channels:]
-    base = base + half
-    last = sums[base : base + 8]
+    last = sums[base + half : base + half + 8]
     b_one_ref[...] = last[0:1]
     b_two_ref[...] = last[1:2]
-    tally_ref[...] = last[2:3] + last[3:4]
+    tally_ref[...] = (last[2:3] + last[3:4])[:, : tally_ref.shape[1]] * scale
 
 
 def own_kernel(table_ref, *refs):
@@ -306,16 +333,13 @@
         out_ref[m, nodes - HALO :] = (own_ref[m, nodes - HALO :] + from_next.astype(jnp.float32)).astype(jnp.bfloat16)
 
 
-MEMBER = ("pair", "core")
-
-
 def shifted(shard, axis, by):
     length = lax.axis_size(axis)
     return lax.ppermute(shard, axis, [(i, (i + by) % length) for i in range(length)])
 
 
-def swapped(block, by):
-    return lax.ppermute(block, MEMBER, [(i, i ^ by) for i in range(lax.axis_size(MEMBER))])
+def swapped(block, axis, by):
+    return lax.ppermute(block, axis, [(i, i ^ by) for i in range(lax.axis_size(axis))])
 
 
 def per_device(latent, neighbours, weights, targets, counts, w_one, b_one, w_two, b_two, w_three):
@@ -324,8 +348,7 @@
     hidden = w_one.shape[1]
     ext = nodes + 2 * HALO
     region, regions = lax.axis_index("space"), lax.axis_size("space")
-    rank, ranks = lax.axis_index(MEMBER), lax.axis_size(MEMBER)
-    core = lax.axis_index("core")
+    rank, ranks = lax.axis_index("member"), lax.axis_size("member")
     share = slots // ranks
     bf16, f32 = jnp.bfloat16, jnp.float32
     shape = jax.ShapeDtypeStruct
@@ -335,110 +358,136 @@
     for m in each:
         before.append(shifted(latent[m, nodes - HALO :], "space", 1))
         after.append(shifted(latent[m, :HALO], "space", -1))
-    count = lax.dynamic_slice_in_dim(counts, region, 1)
     target = lax.dynamic_slice_in_dim(targets, rank * share, share)
     rank_at = rank[None].astype(jnp.int32)
-    place = jnp.stack([region, core]).astype(jnp.int32)
+    region_at = region[None].astype(jnp.int32)
 
     table, *part = kernel_call(
         table_kernel,
         (shape((ext, slots), bf16),) + (shape((width, slots), f32),) * members,
         flops=2 * members * width * nodes * slots,
         moved=12 * MIB,
-        smem=1,
-        operands=4,
-    )(count, neighbours, weights, latent)
+        scratch=(
+            pltpu.VMEM(neighbours.shape, jnp.int32),
+            pltpu.VMEM(weights.shape, f32),
+            pltpu.VMEM(latent.shape, bf16),
+            pltpu.SemaphoreType.DMA((3,)),
+        ),
+        smem=2,
+        hbm=3,
+        operands=5,
+    )(region_at, counts, neighbours, weights, latent)
 
     saved_shape = shape((hidden, slots), bf16)
+    mixed_shape = shape((width, slots), bf16)
     block = shape((channels, share), bf16)
+    dense = width * hidden + hidden * hidden + hidden * channels
     saved, sent = [], []
     for m in each:
         out = kernel_call(
             forward_kernel,
-            (shape((width, slots), bf16),) + (saved_shape,) * 4 + (block,) * ranks,
-            flops=2 * slots * (2 * HALO * width + width * hidden + hidden * hidden + hidden * channels),
+            (mixed_shape,) + (saved_shape,) * 4 + (block,) * ranks,
+            flops=2 * slots * (2 * HALO * width + dense),
             moved=8 * MIB,
             scratch=(pltpu.VMEM((ranks, channels, share), bf16),),
             smem=1,
             operands=10,
         )(rank_at, part[m], table, before[m], after[m], w_one, b_one[None], w_two, b_two[None], w_three)
         saved.append(out[:5])
-        sent.append([out[5]] + [swapped(out[5 + i], i) for i in range(1, ranks)])
+        sent.append([out[5]] + [swapped(out[5 + i], "member", i) for i in range(1, ranks)])
 
     everyone = [sent[m][i] for m in each for i in range(ranks)]
-    slots_at = jnp.concatenate([count, (rank * share)[None].astype(jnp.int32)])
     *grads, score = kernel_call(
         score_kernel,
         (block,) * len(everyone) + (shape((1, LANE), f32),),
         flops=4 * MIB,
         moved=2 * MIB,
-        smem=1,
-        operands=2 + len(everyone),
-    )(slots_at, target, *everyone)
+        smem=3,
+        operands=4 + len(everyone),
+    )(region_at, rank_at, counts, target, *everyone)
 
     edge = shape((HALO, width), bf16)
     bias = shape((hidden, LANE), f32)
-    back, from_next, from_prev = [], [], []
+    stage = pltpu.VMEM((ranks, channels, share), bf16)
+    rows = -(-(width + hidden + hidden // 2 + 4) // (16 * ranks)) * 16
+    piece = shape((1, rows, hidden), bf16)
+    from_next, from_prev, d_mixed, carried = [], [], [], []
     for m in each:
-        own_grads = grads[m * ranks : (m + 1) * ranks]
-        own_grads = [own_grads[0]] + [swapped(own_grads[i], i) for i in range(1, ranks)]
-        *out, head, tail = kernel_call(
-            backward_kernel,
-            (shape((channels, slots), bf16), saved_shape, saved_shape, shape((width, slots), bf16), bias, bias, edge, edge),
-            flops=2 * slots * (2 * HALO * width + width * hidden + hidden * hidden + hidden * channels),
-            moved=6 * MIB,
-            scratch=(pltpu.VMEM((ranks, channels, share), bf16),),
-            smem=1,
-            operands=7 + ranks,
-        )(rank_at, table, saved[m][2], saved[m][4], w_one, w_two, w_three, *own_grads)
-        back.append(out)
+        mixed, act_one, slope_one, act_two, slope_two = saved[m]
+        given = grads[m * ranks : (m + 1) * ranks]
+        given = [given[0]] + [swapped(given[i], "member", i) for i in range(1, ranks)]
+        base = (rank_at, table, slope_one, slope_two, w_one, w_two, w_three, *given)
+        if m < members - 1:
+            d_dec, d_two, d_one, d_mix, bias_one, bias_two, head, tail = kernel_call(
+                lambda *refs: backward_kernel(ranks, *refs),
+                (shape((channels, slots), bf16), saved_shape, saved_shape, mixed_shape, bias, bias, edge, edge),
+                flops=2 * slots * (2 * HALO * width + dense),
+                moved=6 * MIB,
+                scratch=(stage,),
+                smem=1,
+                operands=len(base),
+            )(*base)
+            carried += kernel_call(
+                weights_kernel,
+                (shape((width, hidden), f32), shape((hidden, hidden), f32), shape((hidden, channels), f32)),
+                flops=2 * slots * dense,
+                moved=4 * MIB,
+                operands=6,
+            )(mixed, act_one, act_two, d_one, d_two, d_dec)
+            carried += [bias_one, bias_two]
+        else:
+            operands = (region_at, *base, score, mixed, act_one, act_two, *carried)
+            d_mix, head, tail, *pieces = kernel_call(
+                lambda *refs: last_backward_kernel(ranks, members - 1, *refs),
+                (mixed_shape, edge, edge) + (piece,) * ranks,
+                flops=2 * slots * (2 * HALO * width + 2 * dense),
+                moved=10 * MIB,
+                scratch=(
+                    pltpu.VMEM((channels, slots), bf16),
+                    pltpu.VMEM((hidden, slots), bf16),
+                    pltpu.VMEM((hidden, slots), bf16),
+                    pltpu.VMEM((hidden, LANE), f32),
+                    pltpu.VMEM((hidden, LANE), f32),
+                    stage,
+                    pltpu.VMEM((ranks, rows, hidden), bf16),
+                ),
+                smem=2,
+                operands=len(operands),
+            )(*operands)
+        d_mixed.append(d_mix)
         from_next.append(shifted(head, "space", -1))
         from_prev.append(shifted(tail, "space", 1))
 
-    ways = regions * ranks // 2
-    rows = -(-(width + hidden + hidden // 2 + 4) // (32 * ways)) * 32 * ways
-    half = shape((rows // 2, hidden), bf16)
-    operands = []
-    for m in each:
-        d_dec, d_two, d_one, _, bias_one, bias_two = back[m]
-        mixed, act_one, _, act_two, _ = saved[m]
-        operands += [mixed, act_one, act_two, d_one, d_two, d_dec, bias_one, bias_two]
-    keep, send = kernel_call(
-        lambda *refs: sums_kernel(members, *refs),
-        (half, half),
-        flops=2 * members * slots * (width * hidden + hidden * hidden + hidden * channels),
-        moved=10 * MIB,
-        scratch=(pltpu.VMEM((2, rows // 2, hidden), bf16),),
-        smem=1,
-        operands=2 + len(operands),
-    )(place, score, *operands)
-    swap = [(0, 1), (1, 0)]
-    other = lax.ppermute(send, "core", swap)
+    keep, send = pieces[::2], pieces[1::2]
+    bit, other = 1, [swapped(block, "member", 1) for block in send]
+    other, from_next[:-1], from_prev[:-1] = lax.optimization_barrier((other, from_next[:-1], from_prev[:-1]))
+    while len(keep) > 1:
+        both = kernel_call(
+            lambda *refs: halve_kernel(len(keep), *refs), (piece,) * len(keep), flops=MIB, moved=MIB, operands=2 * len(keep)
+        )(*keep, *other)
+        keep, send = both[::2], both[1::2]
+        bit = 2 * bit
+        other = [swapped(block, "member", bit) for block in send]
+    (quarter,) = kernel_call(
+        lambda *refs: halve_kernel(1, *refs), (piece,), flops=MIB, moved=MIB, operands=2
+    )(*keep, *other)
+    quarters = [quarter] + [swapped(quarter, "space", i) for i in range(1, regions)]
     own = kernel_call(
         own_kernel,
         shape((members, nodes, width), f32),
         flops=2 * members * nodes * width * slots,
         moved=6 * MIB,
         operands=1 + members,
-    )(table, *[out[3] for out in back])
-    total = kernel_call(pair_sum_kernel, half, flops=MIB, moved=MIB, operands=2)(keep, other)
-    total, own = lax.optimization_barrier((total, own))
-    both = ("space", "pair")
-    pieces = lax.all_to_all(total, both, 0, 0, tiled=True).reshape(ways, rows // 2 // ways, hidden)
-    spread = kernel_call(piece_kernel, shape(pieces.shape, bf16), flops=MIB, moved=MIB, operands=1)(pieces)
-    mine = lax.all_to_all(spread.reshape(rows // 2, hidden), both, 0, 0, tiled=True)
-    other = lax.ppermute(mine, "core", swap)
-    row = shape((1, hidden), f32)
-    g_one, g_bone, g_two, g_btwo, g_three, tally = kernel_call(
-        unpack_kernel,
-        (shape((width, hidden), f32), row, shape((hidden, hidden), f32), row, shape((hidden, channels), f32), row),
+    )(table, *d_mixed)
+    total = kernel_call(
+        region_sum_kernel,
+        piece,
         flops=MIB,
-        moved=2 * MIB,
-        scratch=(pltpu.VMEM((2, rows // 2, hidden), bf16),),
+        moved=MIB,
+        scratch=(pltpu.VMEM((regions, rows, hidden), bf16),),
         smem=1,
-        operands=3,
-    )(place, mine, other)
-
+        operands=1 + regions,
+    )(region_at, *quarters)
     latent_grad = kernel_call(
         finish_kernel,
         shape((members, nodes, width), bf16),
@@ -446,17 +495,29 @@
         moved=3 * MIB,
         operands=1 + 2 * members,
     )(own, *from_prev, *from_next)
-    region_score = tally[0, :regions] / (OBS_MEAN * members * ranks)
-    return (region_score, latent_grad, g_one, g_bone[0], g_two, g_btwo[0], g_three)
+    total, latent_grad = lax.optimization_barrier((total, latent_grad))
+    totals = {0: total}
+    while bit:
+        totals.update({i ^ bit: swapped(totals[i], "member", bit) for i in sorted(totals)})
+        bit = bit // 2
+    totals = [totals[i] for i in range(ranks)]
+    row = shape((1, hidden), f32)
+    g_one, g_bone, g_two, g_btwo, g_three, tally = kernel_call(
+        lambda *refs: unpack_kernel(1.0 / (OBS_MEAN * members * ranks), *refs),
+        (shape((width, hidden), f32), row, shape((hidden, hidden), f32), row, shape((hidden, channels), f32),
+         shape((1, regions), f32)),
+        flops=MIB,
+        moved=2 * MIB,
+        scratch=(pltpu.VMEM((ranks, rows, hidden), bf16),),
+        smem=1,
+        operands=1 + ranks,
+    )(rank_at, *totals)
+    return (tally[0], latent_grad, g_one, g_bone[0], g_two, g_btwo[0], g_three)
 
 
 def solution(mesh):
-    groups, space, member = mesh.devices.shape
-    inner = jax.sharding.Mesh(
-        mesh.devices.reshape(groups, space, member // 2, 2), ("groups", "space") + MEMBER
-    )
     in_specs = (
-        P(MEMBER, ("groups", "space"), None),
+        P("member", ("groups", "space"), None),
         P(None, ("groups", "space")),
         P(None, ("groups", "space")),
         P(("groups", "space"), None),
@@ -469,7 +530,7 @@
     )
     out_specs = (
         P("groups"),
-        P(MEMBER, ("groups", "space"), None),
+        P("member", ("groups", "space"), None),
         P("groups", None),
         P("groups"),
         P("groups", None),
@@ -477,5 +538,5 @@
         P("groups", None),
     )
     return jax.shard_map(
-        per_device, mesh=inner, in_specs=in_specs, out_specs=out_specs, check_vma=False
+        per_device, mesh=mesh, in_specs=in_specs, out_specs=out_specs, check_vma=False
     )

time: 93.8 us -> 101 us (1.077)
  blocking collectives: 21.7 us -> 0 us
  local copies, waits for them, and re-layouts: 5.16 us -> 25 us
  starting transfers between devices: 23.2 us -> 29.6 us
  waiting for transfers between devices: 18.6 us -> 21.6 us
  other arithmetic: 1.31 us -> 0.01 us
    all_to_all x2 -> x0, blocking collectives: 21.7 us -> none  [the longest x1 11 us: per_device(): lax.all_to_all(total, both, 0, 0, tiled=True)]
    unnamed x18 -> x66, local copies, waits for them, and re-layouts: 2.73 us -> 23.1 us
    ppermute x14 -> x21, waiting for transfers between devices: 9.44 us -> 20.3 us  [swapped(): lax.ppermute(block, axis, [(i, i ^ by) for i in range(lax.axis_size(axis))])]
    ppermute x8, waiting for transfers between devices: 9.14 us -> 1.32 us  [shifted(): lax.ppermute(shard, axis, [(i, (i + by) % length) for i in range(length)])]
    ppermute x14 -> x21, starting transfers between devices: 8.31 us -> 14.7 us  [swapped(): lax.ppermute(block, axis, [(i, i ^ by) for i in range(lax.axis_size(axis))])]
    dynamic_slice x1 -> x0, local copies, waits for them, and re-layouts: 1.24 us -> none  [per_device(): count = lax.dynamic_slice_in_dim(counts, region, 1)]
    pallas_call x8 -> x9, Pallas kernels: 13.8 us -> 13.2 us  [the longest x2 6.72 us: per_device(): kernel_call(forward_kernel, (mixed_shape,) + (saved_shape,) * 4 + (block,...]
  transfers between devices with their start and end apart: 22 -> 29, of which waited for: 10 -> 11; matrix products, arithmetic and copies ran while one was open for 2% -> 0% of each run, Pallas kernels for 16% -> 19%
where the time goes in v2:
time: 101 us; the launch traced here: 100 us
  starting transfers between devices  29.6 us (29%)
  local copies, waits for them, and re-layouts  25 us (25%)
  Pallas kernels  23 us (23%)
  waiting for transfers between devices  21.6 us (21%)
    unnamed x66, local copies, waits for them, and re-layouts  23.1 us
    ppermute x21, waiting for transfers between devices, swapped(): lax.ppermute(block, axis, [(i, i ^ by) for i in range(lax.axis_size(axis))])  20.3 us
    ppermute x8, starting transfers between devices, shifted(): lax.ppermute(shard, axis, [(i, (i + by) % length) for i in range(length)])  15 us
    ppermute x21, starting transfers between devices, swapped(): lax.ppermute(block, axis, [(i, i ^ by) for i in range(lax.axis_size(axis))])  14.7 us
    pallas_call x2, Pallas kernels, per_device(): kernel_call(forward_kernel, (mixed_shape,) + (saved_shape,) * 4 + (block,...  6.72 us
    pallas_call x1, Pallas kernels, per_device(): kernel_call(table_kernel, (shape((ext, slots), bf16),) + (shape((width, s...  4.37 us
    pallas_call x1, Pallas kernels, per_device(): kernel_call(lambda *refs: last_backward_kernel(ranks, members - 1, *refs)...  2.68 us
    pallas_call x1, Pallas kernels, per_device(): kernel_call(score_kernel, (block,) * len(everyone) + (shape((1, LANE), f3...  2.48 us
  transfers between devices with their start and end apart: 29, of which 11 were waited for; matrix products, arithmetic and copies ran while one was open for 0% of the time, Pallas kernels for 19%

profile of v2, /device:TPU:0, one launch (start us, length us, event | category | flops | bytes accessed | tf_op | source)
XLA Modules:
  0.0 100.2 jit_solution(10334712963056309567)
XLA Ops:
  0.6 1.9 %slice_bitcast_fusion = (bf16[256,256]{1,0:T(8,128)(2,1)}, bf16[256,256]{1,0:T(8,128)(2,1)S(1)}, bf16[256,256]{1,0:T(8,128)(2,1)S(1)}, bf16[256,256]{1,0:T(8,128)(2,1)}) fusion(bf16[2,1024,256]{2,1,0:T(8,128)(2,1)} %latent_hbm.1), kind=kLoop, calls=%fused_computation | loop fusion | bytes 1048576 | tf_op jit(solution)/shard_map/squeeze | solution.py:360
  2.5 5.0 %collective-permute-start.3 = (bf16[256,256]{1,0:T(8,128)(2,1)}, bf16[256,256]{1,0:T(8,128)(2,1)S(1)}, u32[]{:S(2)}, u32[]{:S(2)}) collective-permute-start(bf16[256,256]{1,0:T(8,128)(2,1)} %get-tuple-element.131), channel_id=1, source_target_pairs={{0,12},{4,0},{8,4},{12,8},{1,13},{5,1},{9,5},{13,9},{2,14},{6,2},{... | collective-permute-start | bytes 393224 | tf_op jit(solution)/shard_map/ppermute | solution.py:338
  7.6 0.4 collective-permute-start.1
  8.0 1.6 %collective-permute-start = (bf16[256,256]{1,0:T(8,128)(2,1)S(1)}, bf16[256,256]{1,0:T(8,128)(2,1)S(1)}, u32[]{:S(2)}, u32[]{:S(2)}) collective-permute-start(bf16[256,256]{1,0:T(8,128)(2,1)S(1)} %get-tuple-element.133), channel_id=1, source_target_pairs={{0,4},{4,8},{8,12},{12,0},{1,5},{5,9},{9,13},{13,1},{2,6},{6,10},{... | collective-permute-start | bytes 393224 | tf_op jit(solution)/shard_map/ppermute | solution.py:338
  9.6 1.2 %copy-done.18 = bf16[2,1024,256]{2,1,0:T(8,128)(2,1)S(1)} copy-done((bf16[2,1024,256]{2,1,0:T(8,128)(2,1)S(1)}, bf16[2,1024,256]{2,1,0:T(8,128)(2,1)}, u32[]{:S(2)}) %copy-start.18) | copy-done | bytes 1048600
  10.9 0.7 copy-done.25
  11.5 0.7 copy-done.29
  12.3 0.7 copy-done.30
  13.0 4.4 %shard_map.153 = (bf16[1536,1536]{1,0:T(8,128)(2,1)S(1)}, f32[256,1536]{1,0:T(8,128)S(1)}, f32[256,1536]{1,0:T(8,128)S(1)}) custom-call(s32[1]{0:T(128)} %bitcast.1.region_ref.refs_0_, s32[4]{0:T(128)S(1)} %copy-done.25, s32[4,1536]{1,0:T(4,128)S(1)} %copy-done.29, f32[4,1536]{1,0:T(4,128)S(1)} %copy-done.30, bf16[2,1024,256]{2,1,0:T(8,128)(2,1)S(1)} %copy-done.18), custom_call_target="tpu_custom_call" | custom-call | flops 1610612736 | bytes 12582912 | tf_op jit(solution)/shard_map/pallas_call | solution.py:365
  17.4 2.1 %copy-done.1 = bf16[1536,1536]{1,0:T(8,128)(2,1)} copy-done((bf16[1536,1536]{1,0:T(8,128)(2,1)}, bf16[1536,1536]{1,0:T(8,128)(2,1)S(1)}, u32[]{:S(2)}) %copy-start.1) | copy-done | bytes 4718616
  19.5 1.2 %copy-done.7 = f32[256,1536]{1,0:T(8,128)} copy-done((f32[256,1536]{1,0:T(8,128)}, f32[256,1536]{1,0:T(8,128)S(1)}, u32[]{:S(2)}) %copy-start.7) | copy-done | bytes 1572888
  20.7 0.7 copy-done.19
  21.4 2.3 %copy-done.2 = bf16[1536,1536]{1,0:T(8,128)(2,1)S(1)} copy-done((bf16[1536,1536]{1,0:T(8,128)(2,1)S(1)}, bf16[1536,1536]{1,0:T(8,128)(2,1)}, u32[]{:S(2)}) %copy-start.2) | copy-done | bytes 4718616
  23.7 1.4 %copy-done.8 = f32[256,1536]{1,0:T(8,128)S(1)} copy-done((f32[256,1536]{1,0:T(8,128)S(1)}, f32[256,1536]{1,0:T(8,128)}, u32[]{:S(2)}) %copy-start.8) | copy-done | bytes 1572888
  25.2 0.9 copy-done.20
  26.1 3.7 %shard_map.154 = (bf16[256,1536]{1,0:T(8,128)(2,1)S(1)}, bf16[256,1536]{1,0:T(8,128)(2,1)S(1)}, bf16[256,1536]{1,0:T(8,128)(2,1)S(1)}, bf16[256,1536]{1,0:T(8,12...) custom-call(s32[1]{0:T(128)} %bitcast.rank_ref.refs_0_.refs_1_, ...), custom_call_target="tpu_custom_call" | custom-call | flops 905969664 | bytes 8388608 | tf_op jit(solution)/shard_map/pallas_call | solution.py:387
  29.7 0.9 copy-done.10
  30.6 0.9 copy-done.12
  31.5 0.9 copy-done.14
  32.4 0.9 copy-done.16
  33.3 0.7 copy-done.21
  33.9 0.6 copy-done.27
  34.6 0.6 copy-done.28
  35.2 1.5 %collective-permute-start.8 = (bf16[128,384]{1,0:T(8,128)(2,1)}, bf16[128,384]{1,0:T(8,128)(2,1)S(1)}, u32[]{:S(2)}, u32[]{:S(2)}) collective-permute-start(bf16[128,384]{1,0:T(8,128)(2,1)} %copy-done.28), channel_id=1, source_target_pairs={{0,2},{1,3},{2,0},{3,1},{4,6},{5,7},{6,4},{7,5},{8,10},{9,11},{10,... | collective-permute-start | bytes 294920 | tf_op jit(solution)/shard_map/ppermute | solution.py:342
  36.7 0.4 collective-permute-start.9
  37.1 2.3 %copy-done.3 = bf16[1536,1536]{1,0:T(8,128)(2,1)S(1)} copy-done((bf16[1536,1536]{1,0:T(8,128)(2,1)S(1)}, bf16[1536,1536]{1,0:T(8,128)(2,1)}, u32[]{:S(2)}) %copy-start.3) | copy-done | bytes 4718616
  39.4 3.0 %shard_map.155 = (bf16[256,1536]{1,0:T(8,128)(2,1)S(1)}, bf16[256,1536]{1,0:T(8,128)(2,1)S(1)}, bf16[256,1536]{1,0:T(8,128)(2,1)S(1)}, bf16[256,1536]{1,0:T(8,12...) custom-call(s32[1]{0:T(128)} %bitcast.rank_ref.refs_0_.refs_1_, ...), custom_call_target="tpu_custom_call" | custom-call | flops 905969664 | bytes 8388608 | tf_op jit(solution)/shard_map/pallas_call | solution.py:387
  42.5 0.3 collective-permute-start.4
  42.8 1.5 %collective-permute-start.5 = (bf16[128,384]{1,0:T(8,128)(2,1)S(1)}, bf16[128,384]{1,0:T(8,128)(2,1)S(1)}, u32[]{:S(2)}, u32[]{:S(2)}) collective-permute-start(bf16[128,384]{1,0:T(8,128)(2,1)S(1)} %get-tuple-element.76), channel_id=1, source_target_pairs={{0,2},{1,3},{2,0},{3,1},{4,6},{5,7},{6,4},{7,5},{8,10},{9,11},{10,... | collective-permute-start | bytes 294920 | tf_op jit(solution)/shard_map/ppermute | solution.py:342
  44.5 3.8 %collective-permute-done.5.refs_2_ = bf16[128,384]{1,0:T(8,128)(2,1)S(1)} collective-permute-done((bf16[128,384]{1,0:T(8,128)(2,1)S(1)}, bf16[128,384]{1,0:T(8,128)(2,1)S(1)}, u32[]{:S(2)}, u32[]{:S(2)}) %collective-permute-start.5) | collective-permute-done | bytes 98336 | tf_op jit(solution)/shard_map/ppermute | solution.py:342
  48.2 1.2 %collective-permute-done.6.refs_3_ = bf16[128,384]{1,0:T(8,128)(2,1)S(1)} collective-permute-done((bf16[128,384]{1,0:T(8,128)(2,1)S(1)}, bf16[128,384]{1,0:T(8,128)(2,1)S(1)}, u32[]{:S(2)}, u32[]{:S(2)}) %collective-permute-start.6) | collective-permute-done | bytes 98336 | tf_op jit(solution)/shard_map/ppermute | solution.py:342
  49.4 2.5 %shard_map.156 = (bf16[128,384]{1,0:T(8,128)(2,1)S(1)}, bf16[128,384]{1,0:T(8,128)(2,1)S(1)}, bf16[128,384]{1,0:T(8,128)(2,1)S(1)}, bf16[128,384]{1,0:T(8,128)(2...) custom-call(s32[1]{0:T(128)} %bitcast.1.region_ref.refs_0_, ...), custom_call_target="tpu_custom_call" | custom-call | flops 4194304 | bytes 2097152 | tf_op jit(solution)/shard_map/pallas_call | solution.py:400
  51.9 0.3 collective-permute-start.13
  52.2 1.5 %collective-permute-start.14 = (bf16[128,384]{1,0:T(8,128)(2,1)S(1)}, bf16[128,384]{1,0:T(8,128)(2,1)S(1)}, u32[]{:S(2)}, u32[]{:S(2)}) collective-permute-start(bf16[128,384]{1,0:T(8,128)(2,1)S(1)} %get-tuple-element.97), channel_id=1, source_target_pairs={{0,2},{1,3},{2,0},{3,1},{4,6},{5,7},{6,4},{7,5},{8,10},{9,11},{10,... | collective-permute-start | bytes 294920 | tf_op jit(solution)/shard_map/ppermute | solution.py:342
  53.8 0.6 collective-permute-start.10
  54.4 1.5 %collective-permute-start.11 = (bf16[128,384]{1,0:T(8,128)(2,1)S(1)}, bf16[128,384]{1,0:T(8,128)(2,1)S(1)}, u32[]{:S(2)}, u32[]{:S(2)}) collective-permute-start(bf16[128,384]{1,0:T(8,128)(2,1)S(1)} %get-tuple-element.84), channel_id=1, source_target_pairs={{0,2},{1,3},{2,0},{3,1},{4,6},{5,7},{6,4},{7,5},{8,10},{9,11},{10,... | collective-permute-start | bytes 294920 | tf_op jit(solution)/shard_map/ppermute | solution.py:342
  55.9 1.8 %collective-permute-done.14.refs_9_ = bf16[128,384]{1,0:T(8,128)(2,1)S(1)} collective-permute-done((bf16[128,384]{1,0:T(8,128)(2,1)S(1)}, bf16[128,384]{1,0:T(8,128)(2,1)S(1)}, u32[]{:S(2)}, u32[]{:S(2)}) %collective-permute-start.14) | collective-permute-done | bytes 98336 | tf_op jit(solution)/shard_map/ppermute | solution.py:342
  57.6 1.4 %collective-permute-done.15.refs_10_ = bf16[128,384]{1,0:T(8,128)(2,1)S(1)} collective-permute-done((bf16[128,384]{1,0:T(8,128)(2,1)S(1)}, bf16[128,384]{1,0:T(8,128)(2,1)S(1)}, u32[]{:S(2)}, u32[]{:S(2)}) %collective-permute-start.15) | collective-permute-done | bytes 98336 | tf_op jit(solution)/shard_map/ppermute | solution.py:342
  59.0 2.3 %copy-done.4 = bf16[1536,1536]{1,0:T(8,128)(2,1)S(1)} copy-done((bf16[1536,1536]{1,0:T(8,128)(2,1)S(1)}, bf16[1536,1536]{1,0:T(8,128)(2,1)}, u32[]{:S(2)}) %copy-start.4) | copy-done | bytes 4718616
  61.3 2.0 %shard_map.157 = (bf16[128,1536]{1,0:T(8,128)(2,1)S(1)}, bf16[256,1536]{1,0:T(8,128)(2,1)S(1)}, bf16[256,1536]{1,0:T(8,128)(2,1)S(1)}, bf16[256,1536]{1,0:T(8,12...) custom-call(s32[1]{0:T(128)} %bitcast.rank_ref.refs_0_.refs_1_, ...), custom_call_target="tpu_custom_call" | custom-call | flops 905969664 | bytes 6291456 | tf_op jit(solution)/shard_map/pallas_call | solution.py:421
  63.4 4.0 %collective-permute-start.18 = (bf16[256,256]{1,0:T(8,128)(2,1)S(1)}, bf16[256,256]{1,0:T(8,128)(2,1)S(1)}, u32[]{:S(2)}, u32[]{:S(2)}) collective-permute-start(bf16[256,256]{1,0:T(8,128)(2,1)S(1)} %get-tuple-element.111), channel_id=1, source_target_pairs={{0,12},{4,0},{8,4},{12,8},{1,13},{5,1},{9,5},{13,9},{2,14},{6,2},{... | collective-permute-start | bytes 393224 | tf_op jit(solution)/shard_map/ppermute | solution.py:338
  67.4 0.8 shard_map.158
  68.3 0.3 copy-done.11
  68.5 0.2 copy-done.13
  69.0 0.2 copy-done.17
  69.2 2.7 %shard_map.159 = (bf16[256,1536]{1,0:T(8,128)(2,1)S(1)}, bf16[256,256]{1,0:T(8,128)(2,1)S(1)}, bf16[256,256]{1,0:T(8,128)(2,1)S(1)}, bf16[1,176,256]{2,1,0:T(8,1...) custom-call(s32[1]{0:T(128)} %bitcast.1.region_ref.refs_0_, ...), custom_call_target="tpu_custom_call" | custom-call | flops 1409286144 | bytes 10485760 | tf_op jit(solution)/shard_map/pallas_call | solution.py:440
  71.9 0.3 collective-permute-start.16
  72.3 0.2 collective-permute-start.17
  72.5 0.8 collective-permute-done.16.refs_2_
  73.3 0.3 collective-permute-done.17.refs_3_
  73.6 1.3 %collective-permute-done.19.refs_0_ = bf16[256,256]{1,0:T(8,128)(2,1)S(1)} collective-permute-done((bf16[256,256]{1,0:T(8,128)(2,1)S(1)}, bf16[256,256]{1,0:T(8,128)(2,1)S(1)}, u32[]{:S(2)}, u32[]{:S(2)}) %collective-permute-start.19) | collective-permute-done | bytes 131104 | tf_op jit(solution)/shard_map/ppermute | solution.py:338
  74.9 1.2 %collective-permute-start.20 = (bf16[1,176,256]{2,1,0:T(8,128)(2,1)S(1)}, bf16[1,176,256]{2,1,0:T(8,128)(2,1)S(1)}, u32[]{:S(2)}, u32[]{:S(2)}) collective-permute-start(bf16[1,176,256]{2,1,0:T(8,128)(2,1)S(1)} %get-tuple-element.116), channel_id=1, source_target_pairs={{0,2},{1,3},{2,0},{3,1},{4,6},{5,7},{6,4},{7,5},{8,10},{9,11},{10,... | collective-permute-start | bytes 270344 | tf_op jit(solution)/shard_map/ppermute | solution.py:342
  76.1 0.9 collective-permute-start.24
  76.9 3.0 %collective-permute-start.25 = (bf16[256,256]{1,0:T(8,128)(2,1)S(1)}, bf16[256,256]{1,0:T(8,128)(2,1)S(1)}, u32[]{:S(2)}, u32[]{:S(2)}) collective-permute-start(bf16[256,256]{1,0:T(8,128)(2,1)S(1)} %get-tuple-element.122), channel_id=1, source_target_pairs={{0,12},{4,0},{8,4},{12,8},{1,13},{5,1},{9,5},{13,9},{2,14},{6,2},{... | collective-permute-start | bytes 393224 | tf_op jit(solution)/shard_map/ppermute | solution.py:338
  79.9 2.4 %collective-permute-start.23 = (bf16[1,176,256]{2,1,0:T(8,128)(2,1)S(1)}, bf16[1,176,256]{2,1,0:T(8,128)(2,1)S(1)}, u32[]{:S(2)}, u32[]{:S(2)}) collective-permute-start(bf16[1,176,256]{2,1,0:T(8,128)(2,1)S(1)} %shard_map.161.refs_0_), channel_id=1, source_target_pairs={{0,12},{4,8},{8,4},{12,0},{1,13},{5,9},{9,5},{13,1},{2,14},{6,10},... | collective-permute-start | bytes 270344 | tf_op jit(solution)/shard_map/ppermute | solution.py:342
  82.4 2.0 %collective-permute-start.21 = (bf16[1,176,256]{2,1,0:T(8,128)(2,1)S(1)}, bf16[1,176,256]{2,1,0:T(8,128)(2,1)S(1)}, u32[]{:S(2)}, u32[]{:S(2)}) collective-permute-start(bf16[1,176,256]{2,1,0:T(8,128)(2,1)S(1)} %shard_map.161.refs_0_), channel_id=1, source_target_pairs={{0,4},{4,0},{8,12},{12,8},{1,5},{5,1},{9,13},{13,9},{2,6},{6,2},{1... | collective-permute-start | bytes 270344 | tf_op jit(solution)/shard_map/ppermute | solution.py:342
  84.4 1.8 %shard_map.163.own_ref = f32[2,1024,256]{2,1,0:T(8,128)S(1)} custom-call(bf16[1536,1536]{1,0:T(8,128)(2,1)S(1)} %bitcast.16, bf16[256,1536]{1,0:T(8,128)(2,1)S(1)} %get-tuple-element.117.refs_0_, bf16[256,1536]{1,0:T(8,128)(2,1)S(1)} %get-tuple-element.118.refs_1_), custom_call_target="tpu_custom_call" | custom-call | flops 1610612736 | bytes 6291456 | tf_op jit(solution)/shard_map/pallas_call | solution.py:475
  86.2 1.1 %shard_map.164 = bf16[2,1024,256]{2,1,0:T(8,128)(2,1)} custom-call(f32[2,1024,256]{2,1,0:T(8,128)S(1)} %shard_map.163.own_ref, bf16[256,256]{1,0:T(8,128)(2,1)S(1)} %collective-permute-done.19.refs_0_, bf16[256,256]{1,0:T(8,128)(2,1)S(1)} %collective-permute-done.24.refs_1_, bf16[256,256]{1,0:T(8,128)(2,1)S(1)} %collective-permute-done.18.refs_2_, ...), custom_call_target="tpu_custom_call" | custom-call | flops 1048576 | bytes 3145728 | tf_op jit(solution)/shard_map/pallas_call | solution.py:491
  87.3 1.7 %collective-permute-done.23.refs_3_ = bf16[1,176,256]{2,1,0:T(8,128)(2,1)S(1)} collective-permute-done((bf16[1,176,256]{2,1,0:T(8,128)(2,1)S(1)}, bf16[1,176,256]{2,1,0:T(8,128)(2,1)S(1)}, u32[]{:S(2)}, u32[]{:S(2)}) %collective-permute-start.23) | collective-permute-done | bytes 90144 | tf_op jit(solution)/shard_map/ppermute | solution.py:342
  89.1 4.3 %collective-permute-done.22.refs_2_ = bf16[1,176,256]{2,1,0:T(8,128)(2,1)S(1)} collective-permute-done((bf16[1,176,256]{2,1,0:T(8,128)(2,1)S(1)}, bf16[1,176,256]{2,1,0:T(8,128)(2,1)S(1)}, u32[]{:S(2)}, u32[]{:S(2)}) %collective-permute-start.22) | collective-permute-done | bytes 90144 | tf_op jit(solution)/shard_map/ppermute | solution.py:342
  93.4 0.7 collective-permute-start.27
  94.1 3.9 %collective-permute-done.27.refs_3_ = bf16[1,176,256]{2,1,0:T(8,128)(2,1)S(1)} collective-permute-done((bf16[1,176,256]{2,1,0:T(8,128)(2,1)S(1)}, bf16[1,176,256]{2,1,0:T(8,128)(2,1)S(1)}, u32[]{:S(2)}, u32[]{:S(2)}) %collective-permute-start.27) | collective-permute-done | bytes 90144 | tf_op jit(solution)/shard_map/ppermute | solution.py:342
  98.0 1.3 %collective-permute-done.28.refs_4_ = bf16[1,176,256]{2,1,0:T(8,128)(2,1)S(1)} collective-permute-done((bf16[1,176,256]{2,1,0:T(8,128)(2,1)S(1)}, bf16[1,176,256]{2,1,0:T(8,128)(2,1)S(1)}, u32[]{:S(2)}, u32[]{:S(2)}) %collective-permute-start.28) | collective-permute-done | bytes 90144 | tf_op jit(solution)/shard_map/ppermute | solution.py:342
  99.3 0.9 shard_map.165
  (76 shorter events, 0.8 us)
Async XLA Ops:
  0.6 43.8 %copy-start = (bf16[1536,128]{1,0:T(8,128)(2,1)S(1)}, bf16[1536,128]{1,0:T(8,128)(2,1)}, u32[]{:S(2)}) copy-start(bf16[1536,128]{1,0:T(8,128)(2,1)} %param.13) | copy-start | bytes 1179652
  2.5 34.6 %collective-permute-start.3 = (bf16[256,256]{1,0:T(8,128)(2,1)}, bf16[256,256]{1,0:T(8,128)(2,1)S(1)}, u32[]{:S(2)}, u32[]{:S(2)}) collective-permute-start(bf16[256,256]{1,0:T(8,128)(2,1)} %get-tuple-element.131), channel_id=1, source_target_pairs={{0,12},{4,0},{8,4},{12,8},{1,13},{5,1},{9,5},{13,9},{2,14},{6,2},{... | collective-permute-start | bytes 393224 | tf_op jit(solution)/shard_map/ppermute | solution.py:338
  7.6 13.1 %collective-permute-start.1 = (bf16[256,256]{1,0:T(8,128)(2,1)S(1)}, bf16[256,256]{1,0:T(8,128)(2,1)S(1)}, u32[]{:S(2)}, u32[]{:S(2)}) collective-permute-start(bf16[256,256]{1,0:T(8,128)(2,1)S(1)} %get-tuple-element.132), channel_id=1, source_target_pairs={{0,12},{4,0},{8,4},{12,8},{1,13},{5,1},{9,5},{13,9},{2,14},{6,2},{... | collective-permute-start | bytes 393224 | tf_op jit(solution)/shard_map/ppermute | solution.py:338
  8.0 12.7 %collective-permute-start = (bf16[256,256]{1,0:T(8,128)(2,1)S(1)}, bf16[256,256]{1,0:T(8,128)(2,1)S(1)}, u32[]{:S(2)}, u32[]{:S(2)}) collective-permute-start(bf16[256,256]{1,0:T(8,128)(2,1)S(1)} %get-tuple-element.133), channel_id=1, source_target_pairs={{0,4},{4,8},{8,12},{12,0},{1,5},{5,9},{9,13},{13,1},{2,6},{6,10},{... | collective-permute-start | bytes 393224 | tf_op jit(solution)/shard_map/ppermute | solution.py:338
  9.6 27.5 %collective-permute-start.2 = (bf16[256,256]{1,0:T(8,128)(2,1)}, bf16[256,256]{1,0:T(8,128)(2,1)S(1)}, u32[]{:S(2)}, u32[]{:S(2)}) collective-permute-start(bf16[256,256]{1,0:T(8,128)(2,1)} %get-tuple-element.134), channel_id=1, source_target_pairs={{0,4},{4,8},{8,12},{12,0},{1,5},{5,9},{9,13},{13,1},{2,6},{6,10},{... | collective-permute-start | bytes 393224 | tf_op jit(solution)/shard_map/ppermute | solution.py:338
  9.6 1.2 %copy-start.18 = (bf16[2,1024,256]{2,1,0:T(8,128)(2,1)S(1)}, bf16[2,1024,256]{2,1,0:T(8,128)(2,1)}, u32[]{:S(2)}) copy-start(bf16[2,1024,256]{2,1,0:T(8,128)(2,1)} %latent_hbm.1) | copy-start | bytes 3145732
  10.9 0.7 copy-start.25
  11.5 0.7 copy-start.29
  12.3 0.7 copy-start.30
  13.0 8.4 %copy-start.5 = (bf16[256,256]{1,0:T(8,128)(2,1)S(1)}, bf16[256,256]{1,0:T(8,128)(2,1)}, u32[]{:S(2)}) copy-start(bf16[256,256]{1,0:T(8,128)(2,1)} %refs_5_.3) | copy-start | bytes 393220
  13.0 8.4 %copy-start.6 = (bf16[256,256]{1,0:T(8,128)(2,1)S(1)}, bf16[256,256]{1,0:T(8,128)(2,1)}, u32[]{:S(2)}) copy-start(bf16[256,256]{1,0:T(8,128)(2,1)} %refs_6_.3) | copy-start | bytes 393220
  13.0 8.4 %copy-start.9 = (bf16[256,128]{1,0:T(8,128)(2,1)S(1)}, bf16[256,128]{1,0:T(8,128)(2,1)}, u32[]{:S(2)}) copy-start(bf16[256,128]{1,0:T(8,128)(2,1)} %refs_7_.1) | copy-start | bytes 196612
  13.0 8.4 %copy-start.23 = (f32[256]{0:T(256)S(1)}, f32[256]{0:T(256)}, u32[]{:S(2)}) copy-start(f32[256]{0:T(256)} %param.16) | copy-start | bytes 3076
  13.0 8.4 %copy-start.24 = (f32[256]{0:T(256)S(1)}, f32[256]{0:T(256)}, u32[]{:S(2)}) copy-start(f32[256]{0:T(256)} %param.18) | copy-start | bytes 3076
  17.4 2.2 %copy-start.1 = (bf16[1536,1536]{1,0:T(8,128)(2,1)}, bf16[1536,1536]{1,0:T(8,128)(2,1)S(1)}, u32[]{:S(2)}) copy-start(bf16[1536,1536]{1,0:T(8,128)(2,1)S(1)} %get-tuple-element.69.table_ref.refs_1_.refs_2_) | copy-start | bytes 14155780
  19.5 1.2 %copy-start.7 = (f32[256,1536]{1,0:T(8,128)}, f32[256,1536]{1,0:T(8,128)S(1)}, u32[]{:S(2)}) copy-start(f32[256,1536]{1,0:T(8,128)S(1)} %get-tuple-element.70.part_ref) | copy-start | bytes 4718596
  20.7 0.7 copy-start.19
  21.4 2.3 %copy-start.2 = (bf16[1536,1536]{1,0:T(8,128)(2,1)S(1)}, bf16[1536,1536]{1,0:T(8,128)(2,1)}, u32[]{:S(2)}) copy-start(bf16[1536,1536]{1,0:T(8,128)(2,1)} %copy-done.1) | copy-start | bytes 14155780
  23.7 1.4 %copy-start.8 = (f32[256,1536]{1,0:T(8,128)S(1)}, f32[256,1536]{1,0:T(8,128)}, u32[]{:S(2)}) copy-start(f32[256,1536]{1,0:T(8,128)} %copy-done.7) | copy-start | bytes 4718596
  25.2 0.9 copy-start.20
  29.7 0.9 copy-start.10
  30.6 0.9 copy-start.12
  31.5 0.9 copy-start.14
  32.4 0.9 copy-start.16
  33.3 0.7 copy-start.21
  33.9 0.7 copy-start.27
  34.6 0.6 copy-start.28
  35.2 9.1 %collective-permute-start.7 = (bf16[128,384]{1,0:T(8,128)(2,1)}, bf16[128,384]{1,0:T(8,128)(2,1)S(1)}, u32[]{:S(2)}, u32[]{:S(2)}) collective-permute-start(bf16[128,384]{1,0:T(8,128)(2,1)} %get-tuple-element.79), channel_id=1, source_target_pairs={{0,1},{1,0},{2,3},{3,2},{4,5},{5,4},{6,7},{7,6},{8,9},{9,8},{10,11... | collective-permute-start | bytes 294920 | tf_op jit(solution)/shard_map/ppermute | solution.py:342
  35.2 9.2 %collective-permute-start.8 = (bf16[128,384]{1,0:T(8,128)(2,1)}, bf16[128,384]{1,0:T(8,128)(2,1)S(1)}, u32[]{:S(2)}, u32[]{:S(2)}) collective-permute-start(bf16[128,384]{1,0:T(8,128)(2,1)} %copy-done.28), channel_id=1, source_target_pairs={{0,2},{1,3},{2,0},{3,1},{4,6},{5,7},{6,4},{7,5},{8,10},{9,11},{10,... | collective-permute-start | bytes 294920 | tf_op jit(solution)/shard_map/ppermute | solution.py:342
  36.7 7.7 %collective-permute-start.9 = (bf16[128,384]{1,0:T(8,128)(2,1)}, bf16[128,384]{1,0:T(8,128)(2,1)S(1)}, u32[]{:S(2)}, u32[]{:S(2)}) collective-permute-start(bf16[128,384]{1,0:T(8,128)(2,1)} %copy-done.27), channel_id=1, source_target_pairs={{0,3},{1,2},{2,1},{3,0},{4,7},{5,6},{6,5},{7,4},{8,11},{9,10},{10,... | collective-permute-start | bytes 294920 | tf_op jit(solution)/shard_map/ppermute | solution.py:342
  37.1 2.3 %copy-start.3 = (bf16[1536,1536]{1,0:T(8,128)(2,1)S(1)}, bf16[1536,1536]{1,0:T(8,128)(2,1)}, u32[]{:S(2)}) copy-start(bf16[1536,1536]{1,0:T(8,128)(2,1)} %copy-done.1) | copy-start | bytes 14155780
  39.4 10.0 %copy-start.22 = (bf16[128,384]{1,0:T(8,128)(2,1)S(1)}, bf16[128,384]{1,0:T(8,128)(2,1)}, u32[]{:S(2)}) copy-start(bf16[128,384]{1,0:T(8,128)(2,1)} %copy-done.21) | copy-start | bytes 294916
  39.4 10.0 %copy-start.26 = (s32[4]{0:T(128)S(1)}, s32[4]{0:T(128)}, u32[]{:S(2)}) copy-start(s32[4]{0:T(128)} %counts_ref.3) | copy-start | bytes 52
  39.4 28.8 %slice-start = ((s8[4718592]{0:T(1024)(128)(4,1)}), s8[4194304]{0:T(1024)(128)(4,1)S(1)}, s32[]{:S(2)}) async-start(s8[4718592]{0:T(1024)(128)(4,1)} %bitcast.15), calls=%async_computation | async-start | bytes 8388608
  42.5 2.0 %collective-permute-start.4 = (bf16[128,384]{1,0:T(8,128)(2,1)S(1)}, bf16[128,384]{1,0:T(8,128)(2,1)S(1)}, u32[]{:S(2)}, u32[]{:S(2)}) collective-permute-start(bf16[128,384]{1,0:T(8,128)(2,1)S(1)} %get-tuple-element.75), channel_id=1, source_target_pairs={{0,1},{1,0},{2,3},{3,2},{4,5},{5,4},{6,7},{7,6},{8,9},{9,8},{10,11... | collective-permute-start | bytes 294920 | tf_op jit(solution)/shard_map/ppermute | solution.py:342
  42.8 5.4 %collective-permute-start.5 = (bf16[128,384]{1,0:T(8,128)(2,1)S(1)}, bf16[128,384]{1,0:T(8,128)(2,1)S(1)}, u32[]{:S(2)}, u32[]{:S(2)}) collective-permute-start(bf16[128,384]{1,0:T(8,128)(2,1)S(1)} %get-tuple-element.76), channel_id=1, source_target_pairs={{0,2},{1,3},{2,0},{3,1},{4,6},{5,7},{6,4},{7,5},{8,10},{9,11},{10,... | collective-permute-start | bytes 294920 | tf_op jit(solution)/shard_map/ppermute | solution.py:342
  44.3 5.1 %collective-permute-start.6 = (bf16[128,384]{1,0:T(8,128)(2,1)S(1)}, bf16[128,384]{1,0:T(8,128)(2,1)S(1)}, u32[]{:S(2)}, u32[]{:S(2)}) collective-permute-start(bf16[128,384]{1,0:T(8,128)(2,1)S(1)} %get-tuple-element.77), channel_id=1, source_target_pairs={{0,3},{1,2},{2,1},{3,0},{4,7},{5,6},{6,5},{7,4},{8,11},{9,10},{10,... | collective-permute-start | bytes 294920 | tf_op jit(solution)/shard_map/ppermute | solution.py:342
  51.9 4.0 %collective-permute-start.13 = (bf16[128,384]{1,0:T(8,128)(2,1)S(1)}, bf16[128,384]{1,0:T(8,128)(2,1)S(1)}, u32[]{:S(2)}, u32[]{:S(2)}) collective-permute-start(bf16[128,384]{1,0:T(8,128)(2,1)S(1)} %get-tuple-element.96), channel_id=1, source_target_pairs={{0,1},{1,0},{2,3},{3,2},{4,5},{5,4},{6,7},{7,6},{8,9},{9,8},{10,11... | collective-permute-start | bytes 294920 | tf_op jit(solution)/shard_map/ppermute | solution.py:342
  52.2 5.4 %collective-permute-start.14 = (bf16[128,384]{1,0:T(8,128)(2,1)S(1)}, bf16[128,384]{1,0:T(8,128)(2,1)S(1)}, u32[]{:S(2)}, u32[]{:S(2)}) collective-permute-start(bf16[128,384]{1,0:T(8,128)(2,1)S(1)} %get-tuple-element.97), channel_id=1, source_target_pairs={{0,2},{1,3},{2,0},{3,1},{4,6},{5,7},{6,4},{7,5},{8,10},{9,11},{10,... | collective-permute-start | bytes 294920 | tf_op jit(solution)/shard_map/ppermute | solution.py:342
  53.7 5.3 %collective-permute-start.15 = (bf16[128,384]{1,0:T(8,128)(2,1)S(1)}, bf16[128,384]{1,0:T(8,128)(2,1)S(1)}, u32[]{:S(2)}, u32[]{:S(2)}) collective-permute-start(bf16[128,384]{1,0:T(8,128)(2,1)S(1)} %get-tuple-element.98), channel_id=1, source_target_pairs={{0,3},{1,2},{2,1},{3,0},{4,7},{5,6},{6,5},{7,4},{8,11},{9,10},{10,... | collective-permute-start | bytes 294920 | tf_op jit(solution)/shard_map/ppermute | solution.py:342
  53.8 14.4 %collective-permute-start.10 = (bf16[128,384]{1,0:T(8,128)(2,1)S(1)}, bf16[128,384]{1,0:T(8,128)(2,1)S(1)}, u32[]{:S(2)}, u32[]{:S(2)}) collective-permute-start(bf16[128,384]{1,0:T(8,128)(2,1)S(1)} %get-tuple-element.83), channel_id=1, source_target_pairs={{0,1},{1,0},{2,3},{3,2},{4,5},{5,4},{6,7},{7,6},{8,9},{9,8},{10,11... | collective-permute-start | bytes 294920 | tf_op jit(solution)/shard_map/ppermute | solution.py:342
  54.4 13.9 %collective-permute-start.11 = (bf16[128,384]{1,0:T(8,128)(2,1)S(1)}, bf16[128,384]{1,0:T(8,128)(2,1)S(1)}, u32[]{:S(2)}, u32[]{:S(2)}) collective-permute-start(bf16[128,384]{1,0:T(8,128)(2,1)S(1)} %get-tuple-element.84), channel_id=1, source_target_pairs={{0,2},{1,3},{2,0},{3,1},{4,6},{5,7},{6,4},{7,5},{8,10},{9,11},{10,... | collective-permute-start | bytes 294920 | tf_op jit(solution)/shard_map/ppermute | solution.py:342
  55.9 12.4 %collective-permute-start.12 = (bf16[128,384]{1,0:T(8,128)(2,1)S(1)}, bf16[128,384]{1,0:T(8,128)(2,1)S(1)}, u32[]{:S(2)}, u32[]{:S(2)}) collective-permute-start(bf16[128,384]{1,0:T(8,128)(2,1)S(1)} %get-tuple-element.85), channel_id=1, source_target_pairs={{0,3},{1,2},{2,1},{3,0},{4,7},{5,6},{6,5},{7,4},{8,11},{9,10},{10,... | collective-permute-start | bytes 294920 | tf_op jit(solution)/shard_map/ppermute | solution.py:342
  59.0 2.3 %copy-start.4 = (bf16[1536,1536]{1,0:T(8,128)(2,1)S(1)}, bf16[1536,1536]{1,0:T(8,128)(2,1)}, u32[]{:S(2)}) copy-start(bf16[1536,1536]{1,0:T(8,128)(2,1)} %copy-done.1) | copy-start | bytes 14155780
  61.3 6.9 %slice-start.1 = ((s8[4718592]{0:T(1024)(128)(4,1)}), s8[524288]{0:T(1024)(128)(4,1)S(1)}, s32[]{:S(2)}) async-start(s8[4718592]{0:T(1024)(128)(4,1)} %bitcast.15), calls=%async_computation.1 | async-start | bytes 1048576
  63.4 10.2 %collective-permute-start.18 = (bf16[256,256]{1,0:T(8,128)(2,1)S(1)}, bf16[256,256]{1,0:T(8,128)(2,1)S(1)}, u32[]{:S(2)}, u32[]{:S(2)}) collective-permute-start(bf16[256,256]{1,0:T(8,128)(2,1)S(1)} %get-tuple-element.111), channel_id=1, source_target_pairs={{0,12},{4,0},{8,4},{12,8},{1,13},{5,1},{9,5},{13,9},{2,14},{6,2},{... | collective-permute-start | bytes 393224 | tf_op jit(solution)/shard_map/ppermute | solution.py:338
  67.4 7.5 %collective-permute-start.19 = (bf16[256,256]{1,0:T(8,128)(2,1)S(1)}, bf16[256,256]{1,0:T(8,128)(2,1)S(1)}, u32[]{:S(2)}, u32[]{:S(2)}) collective-permute-start(bf16[256,256]{1,0:T(8,128)(2,1)S(1)} %get-tuple-element.112), channel_id=1, source_target_pairs={{0,4},{4,8},{8,12},{12,0},{1,5},{5,9},{9,13},{13,1},{2,6},{6,10},{... | collective-permute-start | bytes 393224 | tf_op jit(solution)/shard_map/ppermute | solution.py:338
  67.4 1.1 %copy-start.11 = (bf16[256,1536]{1,0:T(8,128)(2,1)S(1)}, bf16[256,1536]{1,0:T(8,128)(2,1)}, u32[]{:S(2)}) copy-start(bf16[256,1536]{1,0:T(8,128)(2,1)} %copy-done.10) | copy-start | bytes 2359300
  67.4 1.4 %copy-start.13 = (bf16[256,1536]{1,0:T(8,128)(2,1)S(1)}, bf16[256,1536]{1,0:T(8,128)(2,1)}, u32[]{:S(2)}) copy-start(bf16[256,1536]{1,0:T(8,128)(2,1)} %copy-done.12) | copy-start | bytes 2359300
  67.4 1.6 %copy-start.15 = (bf16[256,1536]{1,0:T(8,128)(2,1)S(1)}, bf16[256,1536]{1,0:T(8,128)(2,1)}, u32[]{:S(2)}) copy-start(bf16[256,1536]{1,0:T(8,128)(2,1)} %copy-done.14) | copy-start | bytes 2359300
  67.4 1.8 %copy-start.17 = (bf16[256,1536]{1,0:T(8,128)(2,1)S(1)}, bf16[256,1536]{1,0:T(8,128)(2,1)}, u32[]{:S(2)}) copy-start(bf16[256,1536]{1,0:T(8,128)(2,1)} %copy-done.16) | copy-start | bytes 2359300
  71.9 1.4 %collective-permute-start.16 = (bf16[1,176,256]{2,1,0:T(8,128)(2,1)S(1)}, bf16[1,176,256]{2,1,0:T(8,128)(2,1)S(1)}, u32[]{:S(2)}, u32[]{:S(2)}) collective-permute-start(bf16[1,176,256]{2,1,0:T(8,128)(2,1)S(1)} %get-tuple-element.109), channel_id=1, source_target_pairs={{0,1},{1,0},{2,3},{3,2},{4,5},{5,4},{6,7},{7,6},{8,9},{9,8},{10,11... | collective-permute-start | bytes 270344 | tf_op jit(solution)/shard_map/ppermute | solution.py:342
  72.3 1.3 %collective-permute-start.17 = (bf16[1,176,256]{2,1,0:T(8,128)(2,1)S(1)}, bf16[1,176,256]{2,1,0:T(8,128)(2,1)S(1)}, u32[]{:S(2)}, u32[]{:S(2)}) collective-permute-start(bf16[1,176,256]{2,1,0:T(8,128)(2,1)S(1)} %get-tuple-element.110), channel_id=1, source_target_pairs={{0,1},{1,0},{2,3},{3,2},{4,5},{5,4},{6,7},{7,6},{8,9},{9,8},{10,11... | collective-permute-start | bytes 270344 | tf_op jit(solution)/shard_map/ppermute | solution.py:342
  74.9 5.0 %collective-permute-start.20 = (bf16[1,176,256]{2,1,0:T(8,128)(2,1)S(1)}, bf16[1,176,256]{2,1,0:T(8,128)(2,1)S(1)}, u32[]{:S(2)}, u32[]{:S(2)}) collective-permute-start(bf16[1,176,256]{2,1,0:T(8,128)(2,1)S(1)} %get-tuple-element.116), channel_id=1, source_target_pairs={{0,2},{1,3},{2,0},{3,1},{4,6},{5,7},{6,4},{7,5},{8,10},{9,11},{10,... | collective-permute-start | bytes 270344 | tf_op jit(solution)/shard_map/ppermute | solution.py:342
  76.1 10.1 %collective-permute-start.24 = (bf16[256,256]{1,0:T(8,128)(2,1)S(1)}, bf16[256,256]{1,0:T(8,128)(2,1)S(1)}, u32[]{:S(2)}, u32[]{:S(2)}) collective-permute-start(bf16[256,256]{1,0:T(8,128)(2,1)S(1)} %get-tuple-element.120), channel_id=1, source_target_pairs={{0,4},{4,8},{8,12},{12,0},{1,5},{5,9},{9,13},{13,1},{2,6},{6,10},{... | collective-permute-start | bytes 393224 | tf_op jit(solution)/shard_map/ppermute | solution.py:338
  76.9 9.3 %collective-permute-start.25 = (bf16[256,256]{1,0:T(8,128)(2,1)S(1)}, bf16[256,256]{1,0:T(8,128)(2,1)S(1)}, u32[]{:S(2)}, u32[]{:S(2)}) collective-permute-start(bf16[256,256]{1,0:T(8,128)(2,1)S(1)} %get-tuple-element.122), channel_id=1, source_target_pairs={{0,12},{4,0},{8,4},{12,8},{1,13},{5,1},{9,5},{13,9},{2,14},{6,2},{... | collective-permute-start | bytes 393224 | tf_op jit(solution)/shard_map/ppermute | solution.py:338
  79.9 9.1 %collective-permute-start.23 = (bf16[1,176,256]{2,1,0:T(8,128)(2,1)S(1)}, bf16[1,176,256]{2,1,0:T(8,128)(2,1)S(1)}, u32[]{:S(2)}, u32[]{:S(2)}) collective-permute-start(bf16[1,176,256]{2,1,0:T(8,128)(2,1)S(1)} %shard_map.161.refs_0_), channel_id=1, source_target_pairs={{0,12},{4,8},{8,4},{12,0},{1,13},{5,9},{9,5},{13,1},{2,14},{6,10},... | collective-permute-start | bytes 270344 | tf_op jit(solution)/shard_map/ppermute | solution.py:342
  82.4 11.0 %collective-permute-start.22 = (bf16[1,176,256]{2,1,0:T(8,128)(2,1)S(1)}, bf16[1,176,256]{2,1,0:T(8,128)(2,1)S(1)}, u32[]{:S(2)}, u32[]{:S(2)}) collective-permute-start(bf16[1,176,256]{2,1,0:T(8,128)(2,1)S(1)} %shard_map.161.refs_0_), channel_id=1, source_target_pairs={{0,8},{4,12},{8,0},{12,4},{1,9},{5,13},{9,1},{13,5},{2,10},{6,14},... | collective-permute-start | bytes 270344 | tf_op jit(solution)/shard_map/ppermute | solution.py:342
  82.4 10.9 %collective-permute-start.21 = (bf16[1,176,256]{2,1,0:T(8,128)(2,1)S(1)}, bf16[1,176,256]{2,1,0:T(8,128)(2,1)S(1)}, u32[]{:S(2)}, u32[]{:S(2)}) collective-permute-start(bf16[1,176,256]{2,1,0:T(8,128)(2,1)S(1)} %shard_map.161.refs_0_), channel_id=1, source_target_pairs={{0,4},{4,0},{8,12},{12,8},{1,5},{5,1},{9,13},{13,9},{2,6},{6,2},{1... | collective-permute-start | bytes 270344 | tf_op jit(solution)/shard_map/ppermute | solution.py:342
  93.4 4.6 %collective-permute-start.27 = (bf16[1,176,256]{2,1,0:T(8,128)(2,1)S(1)}, bf16[1,176,256]{2,1,0:T(8,128)(2,1)S(1)}, u32[]{:S(2)}, u32[]{:S(2)}) collective-permute-start(bf16[1,176,256]{2,1,0:T(8,128)(2,1)S(1)} %shard_map.162.refs_1_), channel_id=1, source_target_pairs={{0,2},{1,3},{2,0},{3,1},{4,6},{5,7},{6,4},{7,5},{8,10},{9,11},{10,... | collective-permute-start | bytes 270344 | tf_op jit(solution)/shard_map/ppermute | solution.py:342
  94.1 3.9 %collective-permute-start.26 = (bf16[1,176,256]{2,1,0:T(8,128)(2,1)S(1)}, bf16[1,176,256]{2,1,0:T(8,128)(2,1)S(1)}, u32[]{:S(2)}, u32[]{:S(2)}) collective-permute-start(bf16[1,176,256]{2,1,0:T(8,128)(2,1)S(1)} %shard_map.162.refs_1_), channel_id=1, source_target_pairs={{0,1},{1,0},{2,3},{3,2},{4,5},{5,4},{6,7},{7,6},{8,9},{9,8},{10,11... | collective-permute-start | bytes 270344 | tf_op jit(solution)/shard_map/ppermute | solution.py:342
  98.0 1.3 %collective-permute-start.28 = (bf16[1,176,256]{2,1,0:T(8,128)(2,1)S(1)}, bf16[1,176,256]{2,1,0:T(8,128)(2,1)S(1)}, u32[]{:S(2)}, u32[]{:S(2)}) collective-permute-start(bf16[1,176,256]{2,1,0:T(8,128)(2,1)S(1)} %collective-permute-done.27.refs_3_), channel_id=1, source_target_pairs={{0,1},{1,0},{2,3},{3,2},{4,5},{5,4},{6,7},{7,6},{8,9},{9,8},{10,11... | collective-permute-start | bytes 270344 | tf_op jit(solution)/shard_map/ppermute | solution.py:342

commit v3 on v2

--- a/solution.py
+++ b/solution.py
@@ -29,9 +29,9 @@
     return jnp.dot(left, right, preferred_element_type=jnp.float32)
 
 
-def kernel_call(body, out_shape, flops, moved, scratch=(), smem=0, hbm=0, operands=0):
+def kernel_call(body, out_shape, flops, moved, scratch=(), smem=0, operands=0):
     vmem = pl.BlockSpec(memory_space=pltpu.VMEM)
-    specs = [pl.BlockSpec(memory_space=pltpu.SMEM)] * smem + [pl.BlockSpec(memory_space=pltpu.HBM)] * hbm
+    specs = [pl.BlockSpec(memory_space=pltpu.SMEM)] * smem
     return pl.pallas_call(
         body,
         out_shape=out_shape,
@@ -43,20 +43,17 @@
     )
 
 
-def table_kernel(region_ref, counts_ref, nbr_hbm, weight_hbm, latent_hbm, table_ref, *refs):
-    *part_refs, nbr_ref, weight_ref, latent_ref, sems = refs
+def rims_kernel(latent_ref, *refs):
+    members, nodes, _ = latent_ref.shape
+    for m in range(members):
+        refs[2 * m][...] = latent_ref[m, nodes - HALO :]
+        refs[2 * m + 1][...] = latent_ref[m, :HALO]
+    refs[-1][...] = latent_ref[...]
+
+
+def table_kernel(region_ref, rank_ref, counts_ref, nbr_ref, weight_ref, latent_ref, table_ref, *part_refs):
     members, nodes, width = latent_ref.shape
     ext, slots = table_ref.shape
-    fetches = [
-        pltpu.make_async_copy(source, to, sems.at[i])
-        for i, (source, to) in enumerate(
-            ((nbr_hbm, nbr_ref), (weight_hbm, weight_ref), (latent_hbm, latent_ref))
-        )
-    ]
-    for fetch in fetches:
-        fetch.start()
-    fetches[0].wait()
-    fetches[1].wait()
     live = lax.broadcasted_iota(jnp.int32, (1, slots), 1) < counts_ref[region_ref[0]]
     nbr = [nbr_ref[k : k + 1, :] for k in range(K)]
     own = [jnp.where(live, weight_ref[k : k + 1, :], 0.0) for k in range(K)]
@@ -84,7 +81,6 @@
                 near = jnp.broadcast_to(near, (16, size)).astype(jnp.bfloat16)
                 tile = jnp.where(rows[:, :, :size] == near[None], wide[k][None], tile)
             table_ref[b * BLOCK : (b + 1) * BLOCK, lo : lo + size] = tile.reshape(BLOCK, size)
-    fetches[2].wait()
     turned = jnp.concatenate([latent_ref[m].T for m in range(members)], axis=0)
     for lo, size in split(slots, CHUNK):
         part = nn_dot(turned, table_ref[HALO : HALO + nodes, lo : lo + size])
@@ -104,14 +100,14 @@
     *decoded_refs, stage_ref = decoded_refs
     ext, slots = table_ref.shape
     ranks, _, share = stage_ref.shape
-    w_one, w_two, w_three = w_one_ref[...].T, w_two_ref[...].T, w_three_ref[...].T
-    b_one, b_two = column(b_one_ref), column(b_two_ref)
+    w_one, w_two, w_three = w_one_ref[...].T * 0.5, w_two_ref[...].T * 0.5, w_three_ref[...].T
+    b_one, b_two = column(b_one_ref) * 0.5, column(b_two_ref) * 0.5
 
     def layer(weight, bias, values, size):
-        pre = nn_dot(weight, values) + jnp.concatenate([bias] * (size // LANE), axis=1)
-        gate = 0.5 + 0.5 * jnp.tanh(0.5 * pre)
-        act = pre * gate
-        return act.astype(jnp.bfloat16), (gate + act * (1.0 - gate)).astype(jnp.bfloat16)
+        half = nn_dot(weight, values) + jnp.concatenate([bias] * (size // LANE), axis=1)
+        gate = 1.0 + jnp.tanh(half)
+        act = half * gate
+        return act.astype(jnp.bfloat16), (gate + act * (2.0 - gate)).astype(jnp.bfloat16)
 
     edges = jnp.concatenate([before_ref[...].T, after_ref[...].T], axis=1)
     for lo, size in split(slots, CHUNK):
@@ -139,7 +135,8 @@
     decoded_refs, grad_refs, score_ref = refs[:count], refs[count : 2 * count], refs[2 * count]
     channels, share = decoded_refs[0].shape
     pairs = [(i, j) for i in range(count) for j in range(i + 1, count)]
-    turned = target_ref[...].astype(jnp.float32).T
+    first = pl.multiple_of(rank_ref[0] * share, 16)
+    turned = target_ref[pl.ds(first, share), :].astype(jnp.float32).T
     total = jnp.zeros((1, LANE), jnp.float32)
     for lo, size in split(share, LANE):
         lanes = slice(lo, lo + size)
@@ -159,7 +156,7 @@
                 to_target[i] = to_target[i] + fold((values[i] - goal) ** 2)
             for p, (i, j) in enumerate(pairs):
                 apart[p] = apart[p] + fold((values[i] - values[j]) ** 2)
-        slot = rank_ref[0] * share + lo + lax.broadcasted_iota(jnp.int32, (1, size), 1)
+        slot = first + lo + lax.broadcasted_iota(jnp.int32, (1, size), 1)
         live = (slot < counts_ref[region_ref[0]]).astype(jnp.float32)
         score = jnp.zeros((1, size), jnp.float32)
 
@@ -208,7 +205,7 @@
         stage_ref[rank_ref[0] ^ i] = grad_refs[i][...]
     for q in range(ranks):
         d_dec_ref[:, q * share : (q + 1) * share] = stage_ref[q]
-    w_one, w_two, w_three = w_one_ref[...], w_two_ref[...], w_three_ref[...]
+    w_one, w_two, w_three = w_one_ref[...], w_two_ref[...] * 0.5, w_three_ref[...] * 0.5
     bias_one = jnp.zeros((hidden, LANE), jnp.float32)
     bias_two = jnp.zeros((hidden, LANE), jnp.float32)
 
@@ -354,11 +351,12 @@
     shape = jax.ShapeDtypeStruct
     each = range(members)
 
-    before, after = [], []
-    for m in each:
-        before.append(shifted(latent[m, nodes - HALO :], "space", 1))
-        after.append(shifted(latent[m, :HALO], "space", -1))
-    target = lax.dynamic_slice_in_dim(targets, rank * share, share)
+    edge = shape((HALO, width), bf16)
+    *rims, latent = kernel_call(
+        rims_kernel, (edge,) * (2 * members) + (shape(latent.shape, bf16),), flops=MIB, moved=3 * MIB, operands=1
+    )(latent)
+    before = [shifted(rims[2 * m], "space", 1) for m in each]
+    after = [shifted(rims[2 * m + 1], "space", -1) for m in each]
     rank_at = rank[None].astype(jnp.int32)
     region_at = region[None].astype(jnp.int32)
 
@@ -367,16 +365,9 @@
         (shape((ext, slots), bf16),) + (shape((width, slots), f32),) * members,
         flops=2 * members * width * nodes * slots,
         moved=12 * MIB,
-        scratch=(
-            pltpu.VMEM(neighbours.shape, jnp.int32),
-            pltpu.VMEM(weights.shape, f32),
-            pltpu.VMEM(latent.shape, bf16),
-            pltpu.SemaphoreType.DMA((3,)),
-        ),
-        smem=2,
-        hbm=3,
-        operands=5,
-    )(region_at, counts, neighbours, weights, latent)
+        smem=3,
+        operands=6,
+    )(region_at, rank_at, counts, neighbours, weights, latent)
 
     saved_shape = shape((hidden, slots), bf16)
     mixed_shape = shape((width, slots), bf16)
@@ -404,9 +395,8 @@
         moved=2 * MIB,
         smem=3,
         operands=4 + len(everyone),
-    )(region_at, rank_at, counts, target, *everyone)
-
-    edge = shape((HALO, width), bf16)
+    )(region_at, rank_at, counts, targets, *everyone)
+
     bias = shape((hidden, LANE), f32)
     stage = pltpu.VMEM((ranks, channels, share), bf16)
     rows = -(-(width + hidden + hidden // 2 + 4) // (16 * ranks)) * 16

time: 101 us -> 76.6 us (0.76)
  local copies, waits for them, and re-layouts: 25 us -> 3.38 us
  Pallas kernels: 23 us -> 21.2 us
    unnamed x66 -> x22, local copies, waits for them, and re-layouts: 23.1 us -> 3.38 us
    squeeze x1 -> x0, local copies, waits for them, and re-layouts: 1.88 us -> none  [per_device(): after.append(shifted(latent[m, :HALO], 'space', -1))]
    pallas_call x1, Pallas kernels: 4.37 us -> 3.3 us  [per_device(): kernel_call(table_kernel, (shape((ext, slots), bf16),) + (shape((width, s...]
    ppermute x21, waiting for transfers between devices: 20.3 us -> 19.3 us  [swapped(): lax.ppermute(block, axis, [(i, i ^ by) for i in range(lax.axis_size(axis))])]
  transfers between devices with their start and end apart: 29 -> 29, of which waited for: 11 -> 12; matrix products, arithmetic and copies ran while one was open for 0% -> 0% of each run, Pallas kernels for 19% -> 23%
where the time goes in v3:
time: 76.6 us; the launch traced here: 76.3 us
  starting transfers between devices  29.7 us (39%)
  Pallas kernels  21.2 us (28%)
  waiting for transfers between devices  21.1 us (28%)
  local copies, waits for them, and re-layouts  3.38 us (4%)
  between operations  0.89 us (1%)
    ppermute x21, waiting for transfers between devices, swapped(): lax.ppermute(block, axis, [(i, i ^ by) for i in range(lax.axis_size(axis))])  19.3 us
    ppermute x8, starting transfers between devices, shifted(): lax.ppermute(shard, axis, [(i, (i + by) % length) for i in range(length)])  14.9 us
    ppermute x21, starting transfers between devices, swapped(): lax.ppermute(block, axis, [(i, i ^ by) for i in range(lax.axis_size(axis))])  14.8 us
    pallas_call x2, Pallas kernels, per_device(): kernel_call(forward_kernel, (mixed_shape,) + (saved_shape,) * 4 + (block,...  5.84 us
    unnamed x22, local copies, waits for them, and re-layouts  3.38 us
    pallas_call x1, Pallas kernels, per_device(): kernel_call(table_kernel, (shape((ext, slots), bf16),) + (shape((width, s...  3.3 us
    pallas_call x1, Pallas kernels, per_device(): kernel_call(lambda *refs: last_backward_kernel(ranks, members - 1, *refs)...  2.75 us
    pallas_call x1, Pallas kernels, per_device(): kernel_call(score_kernel, (block,) * len(everyone) + (shape((1, LANE), f3...  2.48 us
  transfers between devices with their start and end apart: 29, of which 12 were waited for; matrix products, arithmetic and copies ran while one was open for 0% of the time, Pallas kernels for 23%

profile of v3, /device:TPU:0, one launch (start us, length us, event | category | flops | bytes accessed | tf_op | source)
XLA Modules:
  0.0 76.3 jit_solution(11300493440986838020)
XLA Ops:
  0.6 1.2 %copy-done.3 = bf16[2,1024,256]{2,1,0:T(8,128)(2,1)S(1)} copy-done((bf16[2,1024,256]{2,1,0:T(8,128)(2,1)S(1)}, bf16[2,1024,256]{2,1,0:T(8,128)(2,1)}, u32[]{:S(2)}) %copy-start.3) | copy-done | bytes 1048600
  1.9 0.1 shard_map.153
  2.0 3.1 %collective-permute-start = (bf16[256,256]{1,0:T(8,128)(2,1)S(1)}, bf16[256,256]{1,0:T(8,128)(2,1)S(1)}, u32[]{:S(2)}, u32[]{:S(2)}) collective-permute-start(bf16[256,256]{1,0:T(8,128)(2,1)S(1)} %get-tuple-element.77), channel_id=1, source_target_pairs={{0,4},{4,8},{8,12},{12,0},{1,5},{5,9},{9,13},{13,1},{2,6},{6,10},{... | collective-permute-start | bytes 393224 | tf_op jit(solution)/shard_map/ppermute | solution.py:335
  5.0 2.1 %collective-permute-start.1 = (bf16[256,256]{1,0:T(8,128)(2,1)S(1)}, bf16[256,256]{1,0:T(8,128)(2,1)S(1)}, u32[]{:S(2)}, u32[]{:S(2)}) collective-permute-start(bf16[256,256]{1,0:T(8,128)(2,1)S(1)} %get-tuple-element.78), channel_id=1, source_target_pairs={{0,12},{4,0},{8,4},{12,8},{1,13},{5,1},{9,5},{13,9},{2,14},{6,2},{... | collective-permute-start | bytes 393224 | tf_op jit(solution)/shard_map/ppermute | solution.py:335
  7.1 3.8 %collective-permute-start.3 = (bf16[256,256]{1,0:T(8,128)(2,1)S(1)}, bf16[256,256]{1,0:T(8,128)(2,1)S(1)}, u32[]{:S(2)}, u32[]{:S(2)}) collective-permute-start(bf16[256,256]{1,0:T(8,128)(2,1)S(1)} %get-tuple-element.83), channel_id=1, source_target_pairs={{0,12},{4,0},{8,4},{12,8},{1,13},{5,1},{9,5},{13,9},{2,14},{6,2},{... | collective-permute-start | bytes 393224 | tf_op jit(solution)/shard_map/ppermute | solution.py:335
  11.0 0.7 copy-done.7
  11.6 0.7 copy-done.9
  12.4 0.7 copy-done.10
  13.1 0.0 copy-start.6
  13.1 3.3 %shard_map.154 = (bf16[1536,1536]{1,0:T(8,128)(2,1)S(1)}, f32[256,1536]{1,0:T(8,128)S(1)}, f32[256,1536]{1,0:T(8,128)S(1)}) custom-call(s32[1]{0:T(128)} %bitcast.1.region_ref.refs_0_, s32[1]{0:T(128)} %bitcast.rank_ref.refs_0_.refs_1_, s32[4]{0:T(128)S(1)} %copy-done.7, s32[4,1536]{1,0:T(4,128)S(1)} %copy-done.9, f32[4,1536]{1,0:T(4,128)S(1)} %copy-done.10, ...), custom_call_target="tpu_custom_call" | custom-call | flops 1610612736 | bytes 12582912 | tf_op jit(solution)/shard_map/pallas_call | solution.py:363
  16.4 0.0 collective-permute-done.before_ref
  16.5 2.9 %shard_map.155 = (bf16[256,1536]{1,0:T(8,128)(2,1)S(1)}, bf16[256,1536]{1,0:T(8,128)(2,1)S(1)}, bf16[256,1536]{1,0:T(8,128)(2,1)S(1)}, bf16[256,1536]{1,0:T(8,12...) custom-call(s32[1]{0:T(128)} %bitcast.rank_ref.refs_0_.refs_1_, ...), custom_call_target="tpu_custom_call" | custom-call | flops 905969664 | bytes 8388608 | tf_op jit(solution)/shard_map/pallas_call | solution.py:378
  19.4 0.1 collective-permute-start.7
  19.5 1.7 %collective-permute-start.8 = (bf16[128,384]{1,0:T(8,128)(2,1)S(1)}, bf16[128,384]{1,0:T(8,128)(2,1)S(1)}, u32[]{:S(2)}, u32[]{:S(2)}) collective-permute-start(bf16[128,384]{1,0:T(8,128)(2,1)S(1)} %get-tuple-element.90), channel_id=1, source_target_pairs={{0,2},{1,3},{2,0},{3,1},{4,6},{5,7},{6,4},{7,5},{8,10},{9,11},{10,... | collective-permute-start | bytes 294920 | tf_op jit(solution)/shard_map/ppermute | solution.py:339
  21.2 0.1 collective-permute-start.9
  21.4 0.0 copy-start.8
  21.4 2.9 %shard_map.156 = (bf16[256,1536]{1,0:T(8,128)(2,1)S(1)}, bf16[256,1536]{1,0:T(8,128)(2,1)S(1)}, bf16[256,1536]{1,0:T(8,128)(2,1)S(1)}, bf16[256,1536]{1,0:T(8,12...) custom-call(s32[1]{0:T(128)} %bitcast.rank_ref.refs_0_.refs_1_, ...), custom_call_target="tpu_custom_call" | custom-call | flops 905969664 | bytes 8388608 | tf_op jit(solution)/shard_map/pallas_call | solution.py:378
  24.3 0.4 collective-permute-start.4
  24.7 1.6 %collective-permute-start.5 = (bf16[128,384]{1,0:T(8,128)(2,1)S(1)}, bf16[128,384]{1,0:T(8,128)(2,1)S(1)}, u32[]{:S(2)}, u32[]{:S(2)}) collective-permute-start(bf16[128,384]{1,0:T(8,128)(2,1)S(1)} %get-tuple-element.86), channel_id=1, source_target_pairs={{0,2},{1,3},{2,0},{3,1},{4,6},{5,7},{6,4},{7,5},{8,10},{9,11},{10,... | collective-permute-start | bytes 294920 | tf_op jit(solution)/shard_map/ppermute | solution.py:339
  26.4 0.0 collective-permute-done.8.refs_6_
  26.4 0.0 collective-permute-done.9.refs_7_
  26.4 0.0 collective-permute-done.4.refs_1_
  26.4 3.4 %collective-permute-done.5.refs_2_ = bf16[128,384]{1,0:T(8,128)(2,1)S(1)} collective-permute-done((bf16[128,384]{1,0:T(8,128)(2,1)S(1)}, bf16[128,384]{1,0:T(8,128)(2,1)S(1)}, u32[]{:S(2)}, u32[]{:S(2)}) %collective-permute-start.5) | collective-permute-done | bytes 98336 | tf_op jit(solution)/shard_map/ppermute | solution.py:339
  29.8 1.7 %collective-permute-done.6.refs_3_ = bf16[128,384]{1,0:T(8,128)(2,1)S(1)} collective-permute-done((bf16[128,384]{1,0:T(8,128)(2,1)S(1)}, bf16[128,384]{1,0:T(8,128)(2,1)S(1)}, u32[]{:S(2)}, u32[]{:S(2)}) %collective-permute-start.6) | collective-permute-done | bytes 98336 | tf_op jit(solution)/shard_map/ppermute | solution.py:339
  31.5 2.5 %shard_map.157 = (bf16[128,384]{1,0:T(8,128)(2,1)S(1)}, bf16[128,384]{1,0:T(8,128)(2,1)S(1)}, bf16[128,384]{1,0:T(8,128)(2,1)S(1)}, bf16[128,384]{1,0:T(8,128)(2...) custom-call(s32[1]{0:T(128)} %bitcast.1.region_ref.refs_0_, ...), custom_call_target="tpu_custom_call" | custom-call | flops 4194304 | bytes 2097152 | tf_op jit(solution)/shard_map/pallas_call | solution.py:391
  34.0 0.2 collective-permute-start.13
  34.2 1.6 %collective-permute-start.14 = (bf16[128,384]{1,0:T(8,128)(2,1)S(1)}, bf16[128,384]{1,0:T(8,128)(2,1)S(1)}, u32[]{:S(2)}, u32[]{:S(2)}) collective-permute-start(bf16[128,384]{1,0:T(8,128)(2,1)S(1)} %get-tuple-element.107), channel_id=1, source_target_pairs={{0,2},{1,3},{2,0},{3,1},{4,6},{5,7},{6,4},{7,5},{8,10},{9,11},{10,... | collective-permute-start | bytes 294920 | tf_op jit(solution)/shard_map/ppermute | solution.py:339
  35.7 0.2 collective-permute-start.15
  35.9 0.4 collective-permute-start.10
  36.3 1.5 %collective-permute-start.11 = (bf16[128,384]{1,0:T(8,128)(2,1)S(1)}, bf16[128,384]{1,0:T(8,128)(2,1)S(1)}, u32[]{:S(2)}, u32[]{:S(2)}) collective-permute-start(bf16[128,384]{1,0:T(8,128)(2,1)S(1)} %get-tuple-element.94), channel_id=1, source_target_pairs={{0,2},{1,3},{2,0},{3,1},{4,6},{5,7},{6,4},{7,5},{8,10},{9,11},{10,... | collective-permute-start | bytes 294920 | tf_op jit(solution)/shard_map/ppermute | solution.py:339
  37.9 0.0 collective-permute-done.13.refs_8_
  37.9 0.0 collective-permute-start.12
  37.9 1.9 %collective-permute-done.14.refs_9_ = bf16[128,384]{1,0:T(8,128)(2,1)S(1)} collective-permute-done((bf16[128,384]{1,0:T(8,128)(2,1)S(1)}, bf16[128,384]{1,0:T(8,128)(2,1)S(1)}, u32[]{:S(2)}, u32[]{:S(2)}) %collective-permute-start.14) | collective-permute-done | bytes 98336 | tf_op jit(solution)/shard_map/ppermute | solution.py:339
  39.8 1.2 %collective-permute-done.15.refs_10_ = bf16[128,384]{1,0:T(8,128)(2,1)S(1)} collective-permute-done((bf16[128,384]{1,0:T(8,128)(2,1)S(1)}, bf16[128,384]{1,0:T(8,128)(2,1)S(1)}, u32[]{:S(2)}, u32[]{:S(2)}) %collective-permute-start.15) | collective-permute-done | bytes 98336 | tf_op jit(solution)/shard_map/ppermute | solution.py:339
  41.0 2.0 %shard_map.158 = (bf16[128,1536]{1,0:T(8,128)(2,1)S(1)}, bf16[256,1536]{1,0:T(8,128)(2,1)S(1)}, bf16[256,1536]{1,0:T(8,128)(2,1)S(1)}, bf16[256,1536]{1,0:T(8,12...) custom-call(s32[1]{0:T(128)} %bitcast.rank_ref.refs_0_.refs_1_, ...), custom_call_target="tpu_custom_call" | custom-call | flops 905969664 | bytes 6291456 | tf_op jit(solution)/shard_map/pallas_call | solution.py:411
  43.0 0.1 collective-permute-start.18
  43.1 2.0 %collective-permute-start.19 = (bf16[256,256]{1,0:T(8,128)(2,1)S(1)}, bf16[256,256]{1,0:T(8,128)(2,1)S(1)}, u32[]{:S(2)}, u32[]{:S(2)}) collective-permute-start(bf16[256,256]{1,0:T(8,128)(2,1)S(1)} %get-tuple-element.122), channel_id=1, source_target_pairs={{0,4},{4,8},{8,12},{12,0},{1,5},{5,9},{9,13},{13,1},{2,6},{6,10},{... | collective-permute-start | bytes 393224 | tf_op jit(solution)/shard_map/ppermute | solution.py:335
  45.1 0.8 %shard_map.159 = (f32[256,256]{1,0:T(8,128)S(1)}, f32[256,256]{1,0:T(8,128)S(1)}, f32[256,128]{1,0:T(8,128)S(1)}) custom-call(bf16[256,1536]{1,0:T(8,128)(2,1)S(1)} %get-tuple-element.100.mixed_ref, bf16[256,1536]{1,0:T(8,128)(2,1)S(1)} %get-tuple-element.101.act_one_ref, bf16[256,1536]{1,0:T(8,128)(2,1)S(1)} %get-tuple-element.102.act_two_ref, ...), custom_call_target="tpu_custom_call" | custom-call | flops 503316480 | bytes 4194304 | tf_op jit(solution)/shard_map/pallas_call | solution.py:420
  45.9 0.0 collective-permute-done.10.refs_9_
  45.9 2.7 %shard_map.160 = (bf16[256,1536]{1,0:T(8,128)(2,1)S(1)}, bf16[256,256]{1,0:T(8,128)(2,1)S(1)}, bf16[256,256]{1,0:T(8,128)(2,1)S(1)}, bf16[1,176,256]{2,1,0:T(8,1...) custom-call(s32[1]{0:T(128)} %bitcast.1.region_ref.refs_0_, ...), custom_call_target="tpu_custom_call" | custom-call | flops 1409286144 | bytes 10485760 | tf_op jit(solution)/shard_map/pallas_call | solution.py:430
  48.7 0.2 collective-permute-start.16
  48.9 0.3 collective-permute-start.17
  49.3 0.8 %collective-permute-done.16.refs_2_ = bf16[1,176,256]{2,1,0:T(8,128)(2,1)S(1)} collective-permute-done((bf16[1,176,256]{2,1,0:T(8,128)(2,1)S(1)}, bf16[1,176,256]{2,1,0:T(8,128)(2,1)S(1)}, u32[]{:S(2)}, u32[]{:S(2)}) %collective-permute-start.16) | collective-permute-done | bytes 90144 | tf_op jit(solution)/shard_map/ppermute | solution.py:339
  50.1 0.2 collective-permute-done.17.refs_3_
  50.2 1.8 %collective-permute-done.18.refs_2_ = bf16[256,256]{1,0:T(8,128)(2,1)S(1)} collective-permute-done((bf16[256,256]{1,0:T(8,128)(2,1)S(1)}, bf16[256,256]{1,0:T(8,128)(2,1)S(1)}, u32[]{:S(2)}, u32[]{:S(2)}) %collective-permute-start.18) | collective-permute-done | bytes 131104 | tf_op jit(solution)/shard_map/ppermute | solution.py:335
  52.1 0.5 collective-permute-start.20
  52.6 0.0 collective-permute-start.24
  52.6 3.8 %collective-permute-start.25 = (bf16[256,256]{1,0:T(8,128)(2,1)S(1)}, bf16[256,256]{1,0:T(8,128)(2,1)S(1)}, u32[]{:S(2)}, u32[]{:S(2)}) collective-permute-start(bf16[256,256]{1,0:T(8,128)(2,1)S(1)} %get-tuple-element.132), channel_id=1, source_target_pairs={{0,12},{4,0},{8,4},{12,8},{1,13},{5,1},{9,5},{13,9},{2,14},{6,2},{... | collective-permute-start | bytes 393224 | tf_op jit(solution)/shard_map/ppermute | solution.py:335
  56.4 0.2 collective-permute-done.20.refs_1_
  56.7 0.7 collective-permute-start.23
  57.4 1.1 %collective-permute-start.22 = (bf16[1,176,256]{2,1,0:T(8,128)(2,1)S(1)}, bf16[1,176,256]{2,1,0:T(8,128)(2,1)S(1)}, u32[]{:S(2)}, u32[]{:S(2)}) collective-permute-start(bf16[1,176,256]{2,1,0:T(8,128)(2,1)S(1)} %shard_map.162.refs_0_), channel_id=1, source_target_pairs={{0,8},{4,12},{8,0},{12,4},{1,9},{5,13},{9,1},{13,5},{2,10},{6,14},... | collective-permute-start | bytes 270344 | tf_op jit(solution)/shard_map/ppermute | solution.py:339
  58.6 2.6 %collective-permute-start.21 = (bf16[1,176,256]{2,1,0:T(8,128)(2,1)S(1)}, bf16[1,176,256]{2,1,0:T(8,128)(2,1)S(1)}, u32[]{:S(2)}, u32[]{:S(2)}) collective-permute-start(bf16[1,176,256]{2,1,0:T(8,128)(2,1)S(1)} %shard_map.162.refs_0_), channel_id=1, source_target_pairs={{0,4},{4,0},{8,12},{12,8},{1,5},{5,1},{9,13},{13,9},{2,6},{6,2},{1... | collective-permute-start | bytes 270344 | tf_op jit(solution)/shard_map/ppermute | solution.py:339
  61.1 1.8 %shard_map.164.own_ref = f32[2,1024,256]{2,1,0:T(8,128)S(1)} custom-call(bf16[1536,1536]{1,0:T(8,128)(2,1)S(1)} %get-tuple-element.75.table_ref.refs_1_.refs_2_, bf16[256,1536]{1,0:T(8,128)(2,1)S(1)} %get-tuple-element.127.refs_0_, bf16[256,1536]{1,0:T(8,128)(2,1)S(1)} %get-tuple-element.128.refs_1_), custom_call_target="tpu_custom_call" | custom-call | flops 1610612736 | bytes 6291456 | tf_op jit(solution)/shard_map/pallas_call | solution.py:465
  63.0 0.0 collective-permute-done.25.refs_3_
  63.0 1.1 %shard_map.165 = bf16[2,1024,256]{2,1,0:T(8,128)(2,1)} custom-call(f32[2,1024,256]{2,1,0:T(8,128)S(1)} %shard_map.164.own_ref, bf16[256,256]{1,0:T(8,128)(2,1)S(1)} %collective-permute-done.19.refs_0_, bf16[256,256]{1,0:T(8,128)(2,1)S(1)} %collective-permute-done.24.refs_1_, bf16[256,256]{1,0:T(8,128)(2,1)S(1)} %collective-permute-done.18.refs_2_, ...), custom_call_target="tpu_custom_call" | custom-call | flops 1048576 | bytes 3145728 | tf_op jit(solution)/shard_map/pallas_call | solution.py:481
  64.1 1.5 %collective-permute-done.23.refs_3_ = bf16[1,176,256]{2,1,0:T(8,128)(2,1)S(1)} collective-permute-done((bf16[1,176,256]{2,1,0:T(8,128)(2,1)S(1)}, bf16[1,176,256]{2,1,0:T(8,128)(2,1)S(1)}, u32[]{:S(2)}, u32[]{:S(2)}) %collective-permute-start.23) | collective-permute-done | bytes 90144 | tf_op jit(solution)/shard_map/ppermute | solution.py:339
  65.6 3.8 %collective-permute-done.22.refs_2_ = bf16[1,176,256]{2,1,0:T(8,128)(2,1)S(1)} collective-permute-done((bf16[1,176,256]{2,1,0:T(8,128)(2,1)S(1)}, bf16[1,176,256]{2,1,0:T(8,128)(2,1)S(1)}, u32[]{:S(2)}, u32[]{:S(2)}) %collective-permute-start.22) | collective-permute-done | bytes 90144 | tf_op jit(solution)/shard_map/ppermute | solution.py:339
  69.4 0.1 shard_map.163.refs_1_
  69.5 1.4 %collective-permute-start.27 = (bf16[1,176,256]{2,1,0:T(8,128)(2,1)S(1)}, bf16[1,176,256]{2,1,0:T(8,128)(2,1)S(1)}, u32[]{:S(2)}, u32[]{:S(2)}) collective-permute-start(bf16[1,176,256]{2,1,0:T(8,128)(2,1)S(1)} %shard_map.163.refs_1_), channel_id=1, source_target_pairs={{0,2},{1,3},{2,0},{3,1},{4,6},{5,7},{6,4},{7,5},{8,10},{9,11},{10,... | collective-permute-start | bytes 270344 | tf_op jit(solution)/shard_map/ppermute | solution.py:339
  70.9 3.2 %collective-permute-done.27.refs_3_ = bf16[1,176,256]{2,1,0:T(8,128)(2,1)S(1)} collective-permute-done((bf16[1,176,256]{2,1,0:T(8,128)(2,1)S(1)}, bf16[1,176,256]{2,1,0:T(8,128)(2,1)S(1)}, u32[]{:S(2)}, u32[]{:S(2)}) %collective-permute-start.27) | collective-permute-done | bytes 90144 | tf_op jit(solution)/shard_map/ppermute | solution.py:339
  74.1 0.0 collective-permute-start.28
  74.1 0.0 collective-permute-done.26.refs_2_
  74.1 1.3 %collective-permute-done.28.refs_4_ = bf16[1,176,256]{2,1,0:T(8,128)(2,1)S(1)} collective-permute-done((bf16[1,176,256]{2,1,0:T(8,128)(2,1)S(1)}, bf16[1,176,256]{2,1,0:T(8,128)(2,1)S(1)}, u32[]{:S(2)}, u32[]{:S(2)}) %collective-permute-start.28) | collective-permute-done | bytes 90144 | tf_op jit(solution)/shard_map/ppermute | solution.py:339
  75.4 0.9 %shard_map.166 = (f32[256,256]{1,0:T(8,128)}, f32[1,256]{1,0:T(1,128)}, f32[256,256]{1,0:T(8,128)}, f32[1,256]{1,0:T(1,128)}, f32[256,128]{1,0:T(8,128)}, /*index=5*/f32[1,4]{1,0:T(1,128)}) custom-call(s32[1]{0:T(128)} %bitcast.rank_ref.refs_0_.refs_1_, bf16[1,176,256]{2,1,0:T(8,128)(2,1)S(1)} %shard_map.163.refs_1_, ...), custom_call_target="tpu_custom_call" | custom-call | flops 1048576 | bytes 2097152 | tf_op jit(solution)/shard_map/pallas_call | solution.py:495
  (30 shorter events, 0.1 us)
Async XLA Ops:
  0.6 1.2 %copy-start.3 = (bf16[2,1024,256]{2,1,0:T(8,128)(2,1)S(1)}, bf16[2,1024,256]{2,1,0:T(8,128)(2,1)}, u32[]{:S(2)}) copy-start(bf16[2,1024,256]{2,1,0:T(8,128)(2,1)} %latent_ref.1) | copy-start | bytes 3145732
  2.0 14.5 %collective-permute-start = (bf16[256,256]{1,0:T(8,128)(2,1)S(1)}, bf16[256,256]{1,0:T(8,128)(2,1)S(1)}, u32[]{:S(2)}, u32[]{:S(2)}) collective-permute-start(bf16[256,256]{1,0:T(8,128)(2,1)S(1)} %get-tuple-element.77), channel_id=1, source_target_pairs={{0,4},{4,8},{8,12},{12,0},{1,5},{5,9},{9,13},{13,1},{2,6},{6,10},{... | collective-permute-start | bytes 393224 | tf_op jit(solution)/shard_map/ppermute | solution.py:335
  5.0 11.4 %collective-permute-start.1 = (bf16[256,256]{1,0:T(8,128)(2,1)S(1)}, bf16[256,256]{1,0:T(8,128)(2,1)S(1)}, u32[]{:S(2)}, u32[]{:S(2)}) collective-permute-start(bf16[256,256]{1,0:T(8,128)(2,1)S(1)} %get-tuple-element.78), channel_id=1, source_target_pairs={{0,12},{4,0},{8,4},{12,8},{1,13},{5,1},{9,5},{13,9},{2,14},{6,2},{... | collective-permute-start | bytes 393224 | tf_op jit(solution)/shard_map/ppermute | solution.py:335
  7.1 14.2 %collective-permute-start.2 = (bf16[256,256]{1,0:T(8,128)(2,1)S(1)}, bf16[256,256]{1,0:T(8,128)(2,1)S(1)}, u32[]{:S(2)}, u32[]{:S(2)}) collective-permute-start(bf16[256,256]{1,0:T(8,128)(2,1)S(1)} %get-tuple-element.82), channel_id=1, source_target_pairs={{0,4},{4,8},{8,12},{12,0},{1,5},{5,9},{9,13},{13,1},{2,6},{6,10},{... | collective-permute-start | bytes 393224 | tf_op jit(solution)/shard_map/ppermute | solution.py:335
  7.1 14.2 %collective-permute-start.3 = (bf16[256,256]{1,0:T(8,128)(2,1)S(1)}, bf16[256,256]{1,0:T(8,128)(2,1)S(1)}, u32[]{:S(2)}, u32[]{:S(2)}) collective-permute-start(bf16[256,256]{1,0:T(8,128)(2,1)S(1)} %get-tuple-element.83), channel_id=1, source_target_pairs={{0,12},{4,0},{8,4},{12,8},{1,13},{5,1},{9,5},{13,9},{2,14},{6,2},{... | collective-permute-start | bytes 393224 | tf_op jit(solution)/shard_map/ppermute | solution.py:335
  11.0 0.7 copy-start.7
  11.6 0.7 copy-start.9
  12.3 0.7 copy-start.10
  13.1 3.4 %copy-start = (bf16[256,256]{1,0:T(8,128)(2,1)S(1)}, bf16[256,256]{1,0:T(8,128)(2,1)}, u32[]{:S(2)}) copy-start(bf16[256,256]{1,0:T(8,128)(2,1)} %refs_5_.3) | copy-start | bytes 393220
  13.1 3.4 %copy-start.1 = (bf16[256,256]{1,0:T(8,128)(2,1)S(1)}, bf16[256,256]{1,0:T(8,128)(2,1)}, u32[]{:S(2)}) copy-start(bf16[256,256]{1,0:T(8,128)(2,1)} %refs_6_.3) | copy-start | bytes 393220
  13.1 3.4 %copy-start.2 = (bf16[256,128]{1,0:T(8,128)(2,1)S(1)}, bf16[256,128]{1,0:T(8,128)(2,1)}, u32[]{:S(2)}) copy-start(bf16[256,128]{1,0:T(8,128)(2,1)} %refs_7_.1) | copy-start | bytes 196612
  13.1 3.4 %copy-start.5 = (f32[256]{0:T(256)S(1)}, f32[256]{0:T(256)}, u32[]{:S(2)}) copy-start(f32[256]{0:T(256)} %param.16) | copy-start | bytes 3076
  13.1 3.4 %copy-start.6 = (f32[256]{0:T(256)S(1)}, f32[256]{0:T(256)}, u32[]{:S(2)}) copy-start(f32[256]{0:T(256)} %param.18) | copy-start | bytes 3076
  19.4 7.0 %collective-permute-start.7 = (bf16[128,384]{1,0:T(8,128)(2,1)S(1)}, bf16[128,384]{1,0:T(8,128)(2,1)S(1)}, u32[]{:S(2)}, u32[]{:S(2)}) collective-permute-start(bf16[128,384]{1,0:T(8,128)(2,1)S(1)} %get-tuple-element.89), channel_id=1, source_target_pairs={{0,1},{1,0},{2,3},{3,2},{4,5},{5,4},{6,7},{7,6},{8,9},{9,8},{10,11... | collective-permute-start | bytes 294920 | tf_op jit(solution)/shard_map/ppermute | solution.py:339
  19.5 6.9 %collective-permute-start.8 = (bf16[128,384]{1,0:T(8,128)(2,1)S(1)}, bf16[128,384]{1,0:T(8,128)(2,1)S(1)}, u32[]{:S(2)}, u32[]{:S(2)}) collective-permute-start(bf16[128,384]{1,0:T(8,128)(2,1)S(1)} %get-tuple-element.90), channel_id=1, source_target_pairs={{0,2},{1,3},{2,0},{3,1},{4,6},{5,7},{6,4},{7,5},{8,10},{9,11},{10,... | collective-permute-start | bytes 294920 | tf_op jit(solution)/shard_map/ppermute | solution.py:339
  21.2 5.2 %collective-permute-start.9 = (bf16[128,384]{1,0:T(8,128)(2,1)S(1)}, bf16[128,384]{1,0:T(8,128)(2,1)S(1)}, u32[]{:S(2)}, u32[]{:S(2)}) collective-permute-start(bf16[128,384]{1,0:T(8,128)(2,1)S(1)} %get-tuple-element.91), channel_id=1, source_target_pairs={{0,3},{1,2},{2,1},{3,0},{4,7},{5,6},{6,5},{7,4},{8,11},{9,10},{10,... | collective-permute-start | bytes 294920 | tf_op jit(solution)/shard_map/ppermute | solution.py:339
  21.4 10.1 %copy-start.4 = (bf16[1536,128]{1,0:T(8,128)(2,1)S(1)}, bf16[1536,128]{1,0:T(8,128)(2,1)}, u32[]{:S(2)}) copy-start(bf16[1536,128]{1,0:T(8,128)(2,1)} %target_ref.1) | copy-start | bytes 1179652
  21.4 10.1 %copy-start.8 = (s32[4]{0:T(128)S(1)}, s32[4]{0:T(128)}, u32[]{:S(2)}) copy-start(s32[4]{0:T(128)} %counts_ref.3) | copy-start | bytes 52
  24.3 2.1 %collective-permute-start.4 = (bf16[128,384]{1,0:T(8,128)(2,1)S(1)}, bf16[128,384]{1,0:T(8,128)(2,1)S(1)}, u32[]{:S(2)}, u32[]{:S(2)}) collective-permute-start(bf16[128,384]{1,0:T(8,128)(2,1)S(1)} %get-tuple-element.85), channel_id=1, source_target_pairs={{0,1},{1,0},{2,3},{3,2},{4,5},{5,4},{6,7},{7,6},{8,9},{9,8},{10,11... | collective-permute-start | bytes 294920 | tf_op jit(solution)/shard_map/ppermute | solution.py:339
  24.7 5.1 %collective-permute-start.5 = (bf16[128,384]{1,0:T(8,128)(2,1)S(1)}, bf16[128,384]{1,0:T(8,128)(2,1)S(1)}, u32[]{:S(2)}, u32[]{:S(2)}) collective-permute-start(bf16[128,384]{1,0:T(8,128)(2,1)S(1)} %get-tuple-element.86), channel_id=1, source_target_pairs={{0,2},{1,3},{2,0},{3,1},{4,6},{5,7},{6,4},{7,5},{8,10},{9,11},{10,... | collective-permute-start | bytes 294920 | tf_op jit(solution)/shard_map/ppermute | solution.py:339
  26.4 5.1 %collective-permute-start.6 = (bf16[128,384]{1,0:T(8,128)(2,1)S(1)}, bf16[128,384]{1,0:T(8,128)(2,1)S(1)}, u32[]{:S(2)}, u32[]{:S(2)}) collective-permute-start(bf16[128,384]{1,0:T(8,128)(2,1)S(1)} %get-tuple-element.87), channel_id=1, source_target_pairs={{0,3},{1,2},{2,1},{3,0},{4,7},{5,6},{6,5},{7,4},{8,11},{9,10},{10,... | collective-permute-start | bytes 294920 | tf_op jit(solution)/shard_map/ppermute | solution.py:339
  34.0 3.9 %collective-permute-start.13 = (bf16[128,384]{1,0:T(8,128)(2,1)S(1)}, bf16[128,384]{1,0:T(8,128)(2,1)S(1)}, u32[]{:S(2)}, u32[]{:S(2)}) collective-permute-start(bf16[128,384]{1,0:T(8,128)(2,1)S(1)} %get-tuple-element.106), channel_id=1, source_target_pairs={{0,1},{1,0},{2,3},{3,2},{4,5},{5,4},{6,7},{7,6},{8,9},{9,8},{10,11... | collective-permute-start | bytes 294920 | tf_op jit(solution)/shard_map/ppermute | solution.py:339
  34.2 5.6 %collective-permute-start.14 = (bf16[128,384]{1,0:T(8,128)(2,1)S(1)}, bf16[128,384]{1,0:T(8,128)(2,1)S(1)}, u32[]{:S(2)}, u32[]{:S(2)}) collective-permute-start(bf16[128,384]{1,0:T(8,128)(2,1)S(1)} %get-tuple-element.107), channel_id=1, source_target_pairs={{0,2},{1,3},{2,0},{3,1},{4,6},{5,7},{6,4},{7,5},{8,10},{9,11},{10,... | collective-permute-start | bytes 294920 | tf_op jit(solution)/shard_map/ppermute | solution.py:339
  35.7 5.3 %collective-permute-start.15 = (bf16[128,384]{1,0:T(8,128)(2,1)S(1)}, bf16[128,384]{1,0:T(8,128)(2,1)S(1)}, u32[]{:S(2)}, u32[]{:S(2)}) collective-permute-start(bf16[128,384]{1,0:T(8,128)(2,1)S(1)} %get-tuple-element.108), channel_id=1, source_target_pairs={{0,3},{1,2},{2,1},{3,0},{4,7},{5,6},{6,5},{7,4},{8,11},{9,10},{10,... | collective-permute-start | bytes 294920 | tf_op jit(solution)/shard_map/ppermute | solution.py:339
  35.9 10.0 %collective-permute-start.10 = (bf16[128,384]{1,0:T(8,128)(2,1)S(1)}, bf16[128,384]{1,0:T(8,128)(2,1)S(1)}, u32[]{:S(2)}, u32[]{:S(2)}) collective-permute-start(bf16[128,384]{1,0:T(8,128)(2,1)S(1)} %get-tuple-element.93), channel_id=1, source_target_pairs={{0,1},{1,0},{2,3},{3,2},{4,5},{5,4},{6,7},{7,6},{8,9},{9,8},{10,11... | collective-permute-start | bytes 294920 | tf_op jit(solution)/shard_map/ppermute | solution.py:339
  36.3 9.6 %collective-permute-start.11 = (bf16[128,384]{1,0:T(8,128)(2,1)S(1)}, bf16[128,384]{1,0:T(8,128)(2,1)S(1)}, u32[]{:S(2)}, u32[]{:S(2)}) collective-permute-start(bf16[128,384]{1,0:T(8,128)(2,1)S(1)} %get-tuple-element.94), channel_id=1, source_target_pairs={{0,2},{1,3},{2,0},{3,1},{4,6},{5,7},{6,4},{7,5},{8,10},{9,11},{10,... | collective-permute-start | bytes 294920 | tf_op jit(solution)/shard_map/ppermute | solution.py:339
  37.9 8.1 %collective-permute-start.12 = (bf16[128,384]{1,0:T(8,128)(2,1)S(1)}, bf16[128,384]{1,0:T(8,128)(2,1)S(1)}, u32[]{:S(2)}, u32[]{:S(2)}) collective-permute-start(bf16[128,384]{1,0:T(8,128)(2,1)S(1)} %get-tuple-element.95), channel_id=1, source_target_pairs={{0,3},{1,2},{2,1},{3,0},{4,7},{5,6},{6,5},{7,4},{8,11},{9,10},{10,... | collective-permute-start | bytes 294920 | tf_op jit(solution)/shard_map/ppermute | solution.py:339
  43.0 9.0 %collective-permute-start.18 = (bf16[256,256]{1,0:T(8,128)(2,1)S(1)}, bf16[256,256]{1,0:T(8,128)(2,1)S(1)}, u32[]{:S(2)}, u32[]{:S(2)}) collective-permute-start(bf16[256,256]{1,0:T(8,128)(2,1)S(1)} %get-tuple-element.121), channel_id=1, source_target_pairs={{0,12},{4,0},{8,4},{12,8},{1,13},{5,1},{9,5},{13,9},{2,14},{6,2},{... | collective-permute-start | bytes 393224 | tf_op jit(solution)/shard_map/ppermute | solution.py:335
  43.1 8.9 %collective-permute-start.19 = (bf16[256,256]{1,0:T(8,128)(2,1)S(1)}, bf16[256,256]{1,0:T(8,128)(2,1)S(1)}, u32[]{:S(2)}, u32[]{:S(2)}) collective-permute-start(bf16[256,256]{1,0:T(8,128)(2,1)S(1)} %get-tuple-element.122), channel_id=1, source_target_pairs={{0,4},{4,8},{8,12},{12,0},{1,5},{5,9},{9,13},{13,1},{2,6},{6,10},{... | collective-permute-start | bytes 393224 | tf_op jit(solution)/shard_map/ppermute | solution.py:335
  48.7 1.4 %collective-permute-start.16 = (bf16[1,176,256]{2,1,0:T(8,128)(2,1)S(1)}, bf16[1,176,256]{2,1,0:T(8,128)(2,1)S(1)}, u32[]{:S(2)}, u32[]{:S(2)}) collective-permute-start(bf16[1,176,256]{2,1,0:T(8,128)(2,1)S(1)} %get-tuple-element.119), channel_id=1, source_target_pairs={{0,1},{1,0},{2,3},{3,2},{4,5},{5,4},{6,7},{7,6},{8,9},{9,8},{10,11... | collective-permute-start | bytes 270344 | tf_op jit(solution)/shard_map/ppermute | solution.py:339
  48.9 1.3 %collective-permute-start.17 = (bf16[1,176,256]{2,1,0:T(8,128)(2,1)S(1)}, bf16[1,176,256]{2,1,0:T(8,128)(2,1)S(1)}, u32[]{:S(2)}, u32[]{:S(2)}) collective-permute-start(bf16[1,176,256]{2,1,0:T(8,128)(2,1)S(1)} %get-tuple-element.120), channel_id=1, source_target_pairs={{0,1},{1,0},{2,3},{3,2},{4,5},{5,4},{6,7},{7,6},{8,9},{9,8},{10,11... | collective-permute-start | bytes 270344 | tf_op jit(solution)/shard_map/ppermute | solution.py:339
  52.1 4.6 %collective-permute-start.20 = (bf16[1,176,256]{2,1,0:T(8,128)(2,1)S(1)}, bf16[1,176,256]{2,1,0:T(8,128)(2,1)S(1)}, u32[]{:S(2)}, u32[]{:S(2)}) collective-permute-start(bf16[1,176,256]{2,1,0:T(8,128)(2,1)S(1)} %get-tuple-element.126), channel_id=1, source_target_pairs={{0,2},{1,3},{2,0},{3,1},{4,6},{5,7},{6,4},{7,5},{8,10},{9,11},{10,... | collective-permute-start | bytes 270344 | tf_op jit(solution)/shard_map/ppermute | solution.py:339
  52.6 10.4 %collective-permute-start.24 = (bf16[256,256]{1,0:T(8,128)(2,1)S(1)}, bf16[256,256]{1,0:T(8,128)(2,1)S(1)}, u32[]{:S(2)}, u32[]{:S(2)}) collective-permute-start(bf16[256,256]{1,0:T(8,128)(2,1)S(1)} %get-tuple-element.130), channel_id=1, source_target_pairs={{0,4},{4,8},{8,12},{12,0},{1,5},{5,9},{9,13},{13,1},{2,6},{6,10},{... | collective-permute-start | bytes 393224 | tf_op jit(solution)/shard_map/ppermute | solution.py:335
  52.6 10.4 %collective-permute-start.25 = (bf16[256,256]{1,0:T(8,128)(2,1)S(1)}, bf16[256,256]{1,0:T(8,128)(2,1)S(1)}, u32[]{:S(2)}, u32[]{:S(2)}) collective-permute-start(bf16[256,256]{1,0:T(8,128)(2,1)S(1)} %get-tuple-element.132), channel_id=1, source_target_pairs={{0,12},{4,0},{8,4},{12,8},{1,13},{5,1},{9,5},{13,9},{2,14},{6,2},{... | collective-permute-start | bytes 393224 | tf_op jit(solution)/shard_map/ppermute | solution.py:335
  56.7 8.9 %collective-permute-start.23 = (bf16[1,176,256]{2,1,0:T(8,128)(2,1)S(1)}, bf16[1,176,256]{2,1,0:T(8,128)(2,1)S(1)}, u32[]{:S(2)}, u32[]{:S(2)}) collective-permute-start(bf16[1,176,256]{2,1,0:T(8,128)(2,1)S(1)} %shard_map.162.refs_0_), channel_id=1, source_target_pairs={{0,12},{4,8},{8,4},{12,0},{1,13},{5,9},{9,5},{13,1},{2,14},{6,10},... | collective-permute-start | bytes 270344 | tf_op jit(solution)/shard_map/ppermute | solution.py:339
  57.4 12.0 %collective-permute-start.22 = (bf16[1,176,256]{2,1,0:T(8,128)(2,1)S(1)}, bf16[1,176,256]{2,1,0:T(8,128)(2,1)S(1)}, u32[]{:S(2)}, u32[]{:S(2)}) collective-permute-start(bf16[1,176,256]{2,1,0:T(8,128)(2,1)S(1)} %shard_map.162.refs_0_), channel_id=1, source_target_pairs={{0,8},{4,12},{8,0},{12,4},{1,9},{5,13},{9,1},{13,5},{2,10},{6,14},... | collective-permute-start | bytes 270344 | tf_op jit(solution)/shard_map/ppermute | solution.py:339
  58.6 10.9 %collective-permute-start.21 = (bf16[1,176,256]{2,1,0:T(8,128)(2,1)S(1)}, bf16[1,176,256]{2,1,0:T(8,128)(2,1)S(1)}, u32[]{:S(2)}, u32[]{:S(2)}) collective-permute-start(bf16[1,176,256]{2,1,0:T(8,128)(2,1)S(1)} %shard_map.162.refs_0_), channel_id=1, source_target_pairs={{0,4},{4,0},{8,12},{12,8},{1,5},{5,1},{9,13},{13,9},{2,6},{6,2},{1... | collective-permute-start | bytes 270344 | tf_op jit(solution)/shard_map/ppermute | solution.py:339
  69.5 4.6 %collective-permute-start.27 = (bf16[1,176,256]{2,1,0:T(8,128)(2,1)S(1)}, bf16[1,176,256]{2,1,0:T(8,128)(2,1)S(1)}, u32[]{:S(2)}, u32[]{:S(2)}) collective-permute-start(bf16[1,176,256]{2,1,0:T(8,128)(2,1)S(1)} %shard_map.163.refs_1_), channel_id=1, source_target_pairs={{0,2},{1,3},{2,0},{3,1},{4,6},{5,7},{6,4},{7,5},{8,10},{9,11},{10,... | collective-permute-start | bytes 270344 | tf_op jit(solution)/shard_map/ppermute | solution.py:339
  70.9 3.2 %collective-permute-start.26 = (bf16[1,176,256]{2,1,0:T(8,128)(2,1)S(1)}, bf16[1,176,256]{2,1,0:T(8,128)(2,1)S(1)}, u32[]{:S(2)}, u32[]{:S(2)}) collective-permute-start(bf16[1,176,256]{2,1,0:T(8,128)(2,1)S(1)} %shard_map.163.refs_1_), channel_id=1, source_target_pairs={{0,1},{1,0},{2,3},{3,2},{4,5},{5,4},{6,7},{7,6},{8,9},{9,8},{10,11... | collective-permute-start | bytes 270344 | tf_op jit(solution)/shard_map/ppermute | solution.py:339
  74.1 1.3 %collective-permute-start.28 = (bf16[1,176,256]{2,1,0:T(8,128)(2,1)S(1)}, bf16[1,176,256]{2,1,0:T(8,128)(2,1)S(1)}, u32[]{:S(2)}, u32[]{:S(2)}) collective-permute-start(bf16[1,176,256]{2,1,0:T(8,128)(2,1)S(1)} %collective-permute-done.27.refs_3_), channel_id=1, source_target_pairs={{0,1},{1,0},{2,3},{3,2},{4,5},{5,4},{6,7},{7,6},{8,9},{9,8},{10,11... | collective-permute-start | bytes 270344 | tf_op jit(solution)/shard_map/ppermute | solution.py:339

commit v4 on v3

v4 whole, which is shorter than its diff:
```python
import jax
import jax.numpy as jnp
from jax import lax
from jax.experimental import pallas as pl
from jax.experimental.pallas import tpu as pltpu
from jax.sharding import PartitionSpec as P

K = 4
OBS_MEAN = 512
HALO = 256
EPSILON = 1e-05
BLOCK = 256
LANE = 128
CHUNK = 512
MIB = 1 << 20


def split(total, step):
    return [(start, min(step, total - start)) for start in range(0, total, step)]


def nt_dot(left, right):
    return lax.dot_general(
        left, right, (((1,), (1,)), ((), ())), preferred_element_type=jnp.float32
    )


def nn_dot(left, right):
    return jnp.dot(left, right, preferred_element_type=jnp.float32)


def kernel_call(body, out_shape, flops, moved, scratch=(), smem=0, operands=0):
    vmem = pl.BlockSpec(memory_space=pltpu.VMEM)
    specs = [pl.BlockSpec(memory_space=pltpu.SMEM)] * smem
    return pl.pallas_call(
        body,
        out_shape=out_shape,
        in_specs=specs + [vmem] * (operands - len(specs)),
        out_specs=jax.tree.map(lambda _: vmem, out_shape),
        scratch_shapes=list(scratch),
        compiler_params=pltpu.CompilerParams(vmem_limit_bytes=40 * MIB),
        cost_estimate=pl.CostEstimate(flops=flops, bytes_accessed=moved, transcendentals=0),
    )


def rims_kernel(latent_ref, *refs):
    members, nodes, _ = latent_ref.shape
    for m in range(members):
        refs[2 * m][...] = latent_ref[m, nodes - HALO :]
        refs[2 * m + 1][...] = latent_ref[m, :HALO]
    refs[-1][...] = latent_ref[...]


def table_kernel(region_ref, rank_ref, counts_ref, nbr_ref, weight_ref, latent_ref, table_ref, *part_refs):
    members, nodes, width = latent_ref.shape
    ext, slots = table_ref.shape
    live = lax.broadcasted_iota(jnp.int32, (1, slots), 1) < counts_ref[region_ref[0]]
    nbr = [nbr_ref[k : k + 1, :] for k in range(K)]
    own = [jnp.where(live, weight_ref[k : k + 1, :], 0.0) for k in range(K)]
    joint = []
    for k in range(K):
        total = own[k]
        for j in range(K):
            if j != k:
                total = total + jnp.where(nbr[j] == nbr[k], own[j], 0.0)
        joint.append(total)
    groups = BLOCK // 16
    rows = (
        lax.broadcasted_iota(jnp.int32, (groups, 16, LANE), 0) * 16
        + lax.broadcasted_iota(jnp.int32, (groups, 16, LANE), 1)
    ).astype(jnp.float32).astype(jnp.bfloat16)
    for lo, size in split(slots, LANE):
        wide = [
            jnp.broadcast_to(joint[k][:, lo : lo + size], (16, size)).astype(jnp.bfloat16)
            for k in range(K)
        ]
        for b in range(ext // BLOCK):
            tile = jnp.zeros((groups, 16, size), jnp.bfloat16)
            for k in range(K):
                near = (nbr[k][:, lo : lo + size] - b * BLOCK).astype(jnp.float32)
                near = jnp.broadcast_to(near, (16, size)).astype(jnp.bfloat16)
                tile = jnp.where(rows[:, :, :size] == near[None], wide[k][None], tile)
            table_ref[b * BLOCK : (b + 1) * BLOCK, lo : lo + size] = tile.reshape(BLOCK, size)
    turned = jnp.concatenate([latent_ref[m].T for m in range(members)], axis=0)
    for lo, size in split(slots, CHUNK):
        part = nn_dot(turned, table_ref[HALO : HALO + nodes, lo : lo + size])
        for m in range(members):
            part_refs[m][:, lo : lo + size] = part[m * width : (m + 1) * width]


def column(ref):
    height = ref.shape[1]
    return jnp.broadcast_to(ref[...], (LANE, height)).T


def forward_kernel(
    part_ref, table_ref, before_ref, after_ref, w_one_ref, b_one_ref, w_two_ref, b_two_ref, w_three_ref,
    mixed_ref, act_one_ref, slope_one_ref, act_two_ref, slope_two_ref, decoded_ref,
):
    ext, slots = table_ref.shape
    w_one, w_two, w_three = w_one_ref[...].T * 0.5, w_two_ref[...].T * 0.5, w_three_ref[...].T
    b_one, b_two = column(b_one_ref) * 0.5, column(b_two_ref) * 0.5

    def layer(weight, bias, values, size):
        half = nn_dot(weight, values) + jnp.concatenate([bias] * (size // LANE), axis=1)
        gate = 1.0 + jnp.tanh(half)
        act = half * gate
        return act.astype(jnp.bfloat16), (gate + act * (2.0 - gate)).astype(jnp.bfloat16)

    edges = jnp.concatenate([before_ref[...].T, after_ref[...].T], axis=1)
    for lo, size in split(slots, CHUNK):
        lanes = slice(lo, lo + size)
        rim = jnp.concatenate([table_ref[:HALO, lanes], table_ref[ext - HALO :, lanes]], axis=0)
        mixed = (part_ref[:, lanes] + nn_dot(edges, rim)).astype(jnp.bfloat16)
        mixed_ref[:, lanes] = mixed
        act_one, slope_one_ref[:, lanes] = layer(w_one, b_one, mixed, size)
        act_one_ref[:, lanes] = act_one
        act_two, slope_two_ref[:, lanes] = layer(w_two, b_two, act_one, size)
        act_two_ref[:, lanes] = act_two
        decoded_ref[:, lanes] = nn_dot(w_three, act_two).astype(jnp.bfloat16)


def score_kernel(mine, others, count, first, last, region_ref, counts_ref, *refs):
    own_refs, refs = refs[:mine], refs[mine:]
    other_refs, refs = refs[:others], refs[others:]
    if first:
        target_ref, refs = refs[0], refs[1:]
        old_refs, old_score = None, 0.0
    else:
        old_refs, old_score, refs = refs[:mine], refs[mine][...], refs[mine + 1 :]
    grad_refs, score_ref = refs[:mine], refs[mine]
    channels, slots = own_refs[0].shape
    inner = [(i, j) for i in range(mine) for j in range(i + 1, mine)] if first else []
    outer = [(i, mine + j) for i in range(mine) for j in range(others)]
    pairs = inner + outer
    shares = [1.0 / (count - 1)] * len(inner) + [0.5 / (count - 1)] * len(outer)
    live_count = counts_ref[region_ref[0]]

    def one_tile(at, total):
        start = pl.multiple_of(at * LANE, LANE)
        lanes = pl.ds(start, LANE)
        if first:
            turned = target_ref[lanes, :].astype(jnp.float32).T

        def rows_of(c):
            return [ref[c : c + 16, lanes].astype(jnp.float32) for ref in (*own_refs, *other_refs)]

        def fold(square):
            return square[:8] + square[8:]

        to_target = [jnp.zeros((8, LANE), jnp.float32)] * (mine if first else 0)
        apart = [jnp.zeros((8, LANE), jnp.float32)] * len(pairs)
        for c in range(0, channels, 16):
            values = rows_of(c)
            for i in range(len(to_target)):
                to_target[i] = to_target[i] + fold((values[i] - turned[c : c + 16]) ** 2)
            for p, (i, j) in enumerate(pairs):
                apart[p] = apart[p] + fold((values[i] - values[j]) ** 2)
        live = start + lax.broadcasted_iota(jnp.int32, (1, LANE), 1) < live_count
        score = jnp.zeros((1, LANE), jnp.float32)

        def inverse(square):
            squared = jnp.sum(square, axis=0, keepdims=True) + EPSILON
            inv = lax.rsqrt(squared)
            return squared * inv, inv

        inv_target, inv_pair = [], []
        for square in to_target:
            dist, inv = inverse(square)
            score = score + dist
            inv_target.append(jnp.broadcast_to(inv, (8, LANE)))
        for square, share in zip(apart, shares):
            dist, inv = inverse(square)
            score = score - dist * share
            inv_pair.append(jnp.broadcast_to(inv * (1.0 / (count - 1)), (8, LANE)))
        for c in range(0, channels, 16):
            values = rows_of(c)
            halves = []
            for h in (0, 8):
                near = [v[h : h + 8] for v in values]
                rows = slice(c + h, c + h + 8)
                if first:
                    grads = [(near[i] - turned[rows]) * inv_target[i] for i in range(mine)]
                else:
                    grads = [old_refs[i][rows, lanes] for i in range(mine)]
                for p, (i, j) in enumerate(pairs):
                    term = (near[i] - near[j]) * inv_pair[p]
                    grads[i] = grads[i] - term
                    if j < mine:
                        grads[j] = grads[j] + term
                halves.append(grads)
            for i in range(mine):
                grad = jnp.concatenate([halves[0][i], halves[1][i]], axis=0)
                if last:
                    grad = jnp.where(live, grad, 0.0)
                grad_refs[i][c : c + 16, lanes] = grad.astype(grad_refs[i].dtype)
        return total + jnp.where(live, score, 0.0)

    score_ref[...] = old_score + lax.fori_loop(0, slots // LANE, one_tile, jnp.zeros((1, LANE), jnp.float32))


def backward_kernel(members, ranks, region_ref, rank_ref, w_two_ref, w_three_ref, score_ref, *refs):
    saved = [refs[6 * m : 6 * (m + 1)] for m in range(members)]
    refs = refs[6 * members :]
    d_one_refs, refs = refs[:members], refs[members:]
    piece_refs, (d_two_ref, stage_ref) = refs[:ranks], refs[ranks:]
    w_two, w_three = w_two_ref[...] * 0.5, w_three_ref[...] * 0.5
    width, slots = saved[0][0].shape
    hidden = saved[0][1].shape[0]
    bias_one = jnp.zeros((hidden, LANE), jnp.float32)
    bias_two = jnp.zeros((hidden, LANE), jnp.float32)

    def lane_sum(values):
        return sum(values[:, lo : lo + LANE] for lo, _ in split(values.shape[1], LANE))

    g_one, g_two, g_three = 0.0, 0.0, 0.0
    for m in range(members):
        mixed_ref, act_one_ref, slope_one_ref, act_two_ref, slope_two_ref, d_dec_ref = saved[m]
        for lo, size in split(slots, CHUNK):
            lanes = slice(lo, lo + size)
            back = nn_dot(w_three, d_dec_ref[:, lanes]) * slope_two_ref[:, lanes].astype(jnp.float32)
            bias_two = bias_two + lane_sum(back)
            d_two = back.astype(jnp.bfloat16)
            d_two_ref[m, :, lanes] = d_two
            back = nn_dot(w_two, d_two) * slope_one_ref[:, lanes].astype(jnp.float32)
            bias_one = bias_one + lane_sum(back)
            d_one_refs[m][:, lanes] = back.astype(jnp.bfloat16)
        g_three = g_three + nt_dot(act_two_ref[...], d_dec_ref[...])
        g_two = g_two + nt_dot(act_one_ref[...], d_two_ref[m])
        g_one = g_one + nt_dot(mixed_ref[...], d_one_refs[m][...])
    half = hidden // 2
    region = lax.broadcasted_iota(jnp.int32, (1, hidden), 1) == region_ref[0]
    tally = jnp.where(region, jnp.sum(score_ref[...]), 0.0)
    high = tally.astype(jnp.bfloat16).astype(jnp.float32)
    parts = [
        g_one,
        g_two,
        jnp.concatenate([g_three[:half], g_three[half:]], axis=1),
        jnp.sum(bias_one.T, axis=0, keepdims=True),
        jnp.sum(bias_two.T, axis=0, keepdims=True),
        high,
        tally - high,
    ]
    used = sum(part.shape[0] for part in parts)
    parts.append(jnp.zeros((ranks * stage_ref.shape[1] - used, hidden), jnp.float32))
    stage_ref[...] = jnp.concatenate(parts, axis=0).astype(stage_ref.dtype).reshape(stage_ref.shape)
    for i in range(ranks):
        piece_refs[i][...] = stage_ref[rank_ref[0] ^ i]


def edges_kernel(members, table_ref, w_one_ref, *refs):
    d_one_refs, refs = refs[:members], refs[members:]
    d_mixed_refs, (head_ref, tail_ref) = refs[:members], refs[members:]
    ext = table_ref.shape[0]
    for m in range(members):
        d_mixed = nn_dot(w_one_ref[...], d_one_refs[m][...]).astype(jnp.bfloat16)
        d_mixed_refs[m][...] = d_mixed
        head_ref[m] = nt_dot(table_ref[:HALO, :], d_mixed).astype(jnp.bfloat16)
        tail_ref[m] = nt_dot(table_ref[ext - HALO :, :], d_mixed).astype(jnp.bfloat16)


def sum_kernel(count, *refs):
    for i in range(count):
        total = refs[i][...].astype(jnp.float32) + refs[count + i][...].astype(jnp.float32)
        refs[2 * count + i][...] = total.astype(refs[i].dtype)


def unpack_kernel(scale, rank_ref, *refs):
    *refs, stage_ref = refs
    ranks = stage_ref.shape[0]
    one_ref, b_one_ref, two_ref, b_two_ref, three_ref, tally_ref = refs[ranks:]
    for i in range(ranks):
        stage_ref[rank_ref[0] ^ i] = refs[i][...]
    width, hidden = one_ref.shape
    sums = stage_ref[...].reshape(-1, hidden).astype(jnp.float32)
    half, channels = hidden // 2, three_ref.shape[1]
    one_ref[...] = sums[:width]
    two_ref[...] = sums[width : width + hidden]
    base = width + hidden
    three_ref[:half] = sums[base : base + half, :channels]
    three_ref[half:] = sums[base : base + half, channels:]
    last = sums[base + half : base + half + 8]
    b_one_ref[...] = last[0:1]
    b_two_ref[...] = last[1:2]
    tally_ref[...] = (last[2:3] + last[3:4])[:, : tally_ref.shape[1]] * scale


def own_kernel(table_ref, *refs):
    *d_mixed_refs, own_ref = refs
    members, nodes, _ = own_ref.shape
    for m in range(members):
        own_ref[m] = nt_dot(table_ref[HALO : HALO + nodes, :], d_mixed_refs[m][...])


def finish_kernel(own_ref, from_prev_ref, from_next_ref, out_ref):
    nodes = own_ref.shape[1]
    from_prev, from_next = from_prev_ref[...].astype(jnp.float32), from_next_ref[...].astype(jnp.float32)
    out_ref[:, :HALO] = (own_ref[:, :HALO] + from_prev).astype(jnp.bfloat16)
    out_ref[:, HALO : nodes - HALO] = own_ref[:, HALO : nodes - HALO].astype(jnp.bfloat16)
    out_ref[:, nodes - HALO :] = (own_ref[:, nodes - HALO :] + from_next).astype(jnp.bfloat16)


def shifted(shard, axis, by):
    length = lax.axis_size(axis)
    return lax.ppermute(shard, axis, [(i, (i + by) % length) for i in range(length)])


def swapped(block, axis, by):
    return lax.ppermute(block, axis, [(i, i ^ by) for i in range(lax.axis_size(axis))])


def per_device(latent, neighbours, weights, targets, counts, w_one, b_one, w_two, b_two, w_three):
    members, nodes, width = latent.shape
    slots, channels = targets.shape
    hidden = w_one.shape[1]
    ext = nodes + 2 * HALO
    region, regions = lax.axis_index("space"), lax.axis_size("space")
    rank, ranks = lax.axis_index("member"), lax.axis_size("member")
    share = slots // ranks
    bf16, f32 = jnp.bfloat16, jnp.float32
    shape = jax.ShapeDtypeStruct
    each = range(members)

    edge = shape((HALO, width), bf16)
    *rims, latent = kernel_call(
        rims_kernel, (edge,) * (2 * members) + (shape(latent.shape, bf16),), flops=MIB, moved=3 * MIB, operands=1
    )(latent)
    before = [shifted(rims[2 * m], "space", 1) for m in each]
    after = [shifted(rims[2 * m + 1], "space", -1) for m in each]
    rank_at = rank[None].astype(jnp.int32)
    region_at = region[None].astype(jnp.int32)

    table, *part = kernel_call(
        table_kernel,
        (shape((ext, slots), bf16),) + (shape((width, slots), f32),) * members,
        flops=2 * members * width * nodes * slots,
        moved=12 * MIB,
        smem=3,
        operands=6,
    )(region_at, rank_at, counts, neighbours, weights, latent)

    saved_shape = shape((hidden, slots), bf16)
    mixed_shape = shape((width, slots), bf16)
    decoded_shape = shape((channels, slots), bf16)
    dense = width * hidden + hidden * hidden + hidden * channels
    saved, known = [], []
    for m in each:
        *kept, decoded = kernel_call(
            forward_kernel,
            (mixed_shape,) + (saved_shape,) * 4 + (decoded_shape,),
            flops=2 * slots * (2 * HALO * width + dense),
            moved=8 * MIB,
            operands=9,
        )(part[m], table, before[m], after[m], w_one, b_one[None], w_two, b_two[None], w_three)
        saved.append(kept)
        known.append({0: decoded})
        bit = 2
        while bit < ranks:
            known[m].update({i ^ bit: swapped(known[m][i], "member", bit) for i in sorted(known[m])})
            bit = 2 * bit
        known[m][1] = swapped(decoded, "member", 1)

    def scored(others, carried, first=False, last=False):
        operands = (region_at, counts, *[known[m][0] for m in each], *others, *carried)
        return kernel_call(
            lambda *refs: score_kernel(members, len(others), members * ranks, first, last, *refs),
            (shape((channels, slots), bf16 if last else f32),) * members + (shape((1, LANE), f32),),
            flops=4 * MIB,
            moved=2 * MIB,
            smem=2,
            operands=len(operands),
        )(*operands)

    near = [{i: block for i, block in known[m].items() if i > 1} for m in each]
    beside = [known[m][1] for m in each]
    near[:-1], beside = lax.optimization_barrier((near[:-1], beside))
    carried = scored(beside, [targets], first=True)
    near[-1], carried = lax.optimization_barrier((near[-1], carried))
    others = [block for blocks in near for block in blocks.values()]
    others += [swapped(block, "member", 1) for block in others]
    carried = scored(others, carried, last=True)
    *d_decoded, score = carried

    rows = -(-(width + hidden + hidden // 2 + 4) // (16 * ranks)) * 16
    piece = shape((rows, hidden), bf16)
    operands = [region_at, rank_at, w_two, w_three, score]
    for m in each:
        operands += [*saved[m], d_decoded[m]]
    out = kernel_call(
        lambda *refs: backward_kernel(members, ranks, *refs),
        (saved_shape,) * members + (piece,) * ranks,
        flops=4 * members * slots * dense,
        moved=10 * MIB,
        scratch=(pltpu.VMEM((members, hidden, slots), bf16), pltpu.VMEM((ranks, rows, hidden), bf16)),
        smem=2,
        operands=len(operands),
    )(*operands)
    d_one, pieces = out[:members], out[members:]

    def summed(ones, others):
        return kernel_call(
            lambda *refs: sum_kernel(len(ones), *refs), (piece,) * len(ones), flops=MIB, moved=MIB, operands=2 * len(ones)
        )(*ones, *others)

    both = shape((members, HALO, width), bf16)
    *d_mixed, head, tail = kernel_call(
        lambda *refs: edges_kernel(members, *refs),
        (mixed_shape,) * members + (both, both),
        flops=2 * members * slots * width * (hidden + 2 * HALO),
        moved=6 * MIB,
        operands=2 + members,
    )(table, w_one, *d_one)
    bit = 1
    while bit < ranks:
        received = [swapped(sent, "member", bit) for sent in pieces[1::2]]
        if bit == 1:
            received, head, tail = lax.optimization_barrier((received, head, tail))
        pieces = summed(pieces[::2], received)
        bit = 2 * bit
    from_next = shifted(head, "space", -1)
    from_prev = shifted(tail, "space", 1)
    own = kernel_call(
        own_kernel,
        shape((members, nodes, width), f32),
        flops=2 * members * nodes * width * slots,
        moved=6 * MIB,
        operands=1 + members,
    )(table, *d_mixed)
    (total,) = pieces
    step = 1
    while step < regions:
        (total,) = summed([total], [swapped(total, "space", step)])
        step = 2 * step
    latent_grad = kernel_call(
        finish_kernel,
        shape((members, nodes, width), bf16),
        flops=MIB,
        moved=3 * MIB,
        operands=3,
    )(own, from_prev, from_next)
    total, latent_grad = lax.optimization_barrier((total, latent_grad))
    totals = {0: total}
    while bit > 1:
        bit = bit // 2
        totals.update({i ^ bit: swapped(totals[i], "member", bit) for i in sorted(totals)})
    totals = [totals[i] for i in range(ranks)]
    row = shape((1, hidden), f32)
    g_one, g_bone, g_two, g_btwo, g_three, tally = kernel_call(
        lambda *refs: unpack_kernel(1.0 / (OBS_MEAN * members * ranks), *refs),
        (shape((width, hidden), f32), row, shape((hidden, hidden), f32), row, shape((hidden, channels), f32),
         shape((1, regions), f32)),
        flops=MIB,
        moved=2 * MIB,
        scratch=(pltpu.VMEM((ranks, rows, hidden), bf16),),
        smem=1,
        operands=1 + ranks,
    )(rank_at, *totals)
    return (tally[0], latent_grad, g_one, g_bone[0], g_two, g_btwo[0], g_three)


def solution(mesh):
    in_specs = (
        P("member", ("groups", "space"), None),
        P(None, ("groups", "space")),
        P(None, ("groups", "space")),
        P(("groups", "space"), None),
        P("groups"),
        P(),
        P(),
        P(),
        P(),
        P(),
    )
    out_specs = (
        P("groups"),
        P("member", ("groups", "space"), None),
        P("groups", None),
        P("groups"),
        P("groups", None),
        P("groups"),
        P("groups", None),
    )
    return jax.shard_map(
        per_device, mesh=mesh, in_specs=in_specs, out_specs=out_specs, check_vma=False
    )
```

time: 76.6 us -> 79.4 us (1.037)
  waiting for transfers between devices: 21.1 us -> 32.1 us
  starting transfers between devices: 29.7 us -> 20.5 us
  Pallas kernels: 21.2 us -> 22.2 us
    ppermute x21 -> x14, waiting for transfers between devices: 19.3 us -> 32.1 us  [swapped(): lax.ppermute(block, axis, [(i, i ^ by) for i in range(lax.axis_size(axis))])]
    ppermute x21 -> x14, starting transfers between devices: 14.8 us -> 7.71 us  [swapped(): lax.ppermute(block, axis, [(i, i ^ by) for i in range(lax.axis_size(axis))])]
    ppermute x8 -> x6, starting transfers between devices: 14.9 us -> 12.8 us  [shifted(): lax.ppermute(shard, axis, [(i, (i + by) % length) for i in range(length)])]
    ppermute x8 -> x6, waiting for transfers between devices: 1.8 us -> 0.02 us  [shifted(): lax.ppermute(shard, axis, [(i, (i + by) % length) for i in range(length)])]
    pallas_call x9 -> x10, Pallas kernels: 14 us -> 15 us  [the longest x2 5.74 us: per_device(): kernel_call(forward_kernel, (mixed_shape,) + (saved_shape,) * 4 + (decode...]
  transfers between devices with their start and end apart: 29 -> 20, of which waited for: 12 -> 7; matrix products, arithmetic and copies ran while one was open for 0% -> 0% of each run, Pallas kernels for 23% -> 20%
where the time goes in v4:
time: 79.4 us; the launch traced here: 79.1 us
  waiting for transfers between devices  32.1 us (40%)
  Pallas kernels  22.2 us (28%)
  starting transfers between devices  20.5 us (26%)
  local copies, waits for them, and re-layouts  3.38 us (4%)
  between operations  0.88 us (1%)
    ppermute x14, waiting for transfers between devices, swapped(): lax.ppermute(block, axis, [(i, i ^ by) for i in range(lax.axis_size(axis))])  32.1 us
    ppermute x6, starting transfers between devices, shifted(): lax.ppermute(shard, axis, [(i, (i + by) % length) for i in range(length)])  12.8 us
    ppermute x14, starting transfers between devices, swapped(): lax.ppermute(block, axis, [(i, i ^ by) for i in range(lax.axis_size(axis))])  7.71 us
    pallas_call x2, Pallas kernels, per_device(): kernel_call(forward_kernel, (mixed_shape,) + (saved_shape,) * 4 + (decode...  5.74 us
    pallas_call x2, Pallas kernels, scored(): kernel_call(lambda *refs: score_kernel(members, len(others), members * ra...  4.96 us
    unnamed x22, local copies, waits for them, and re-layouts  3.38 us
    pallas_call x1, Pallas kernels, per_device(): kernel_call(table_kernel, (shape((ext, slots), bf16),) + (shape((width, s...  3.29 us
    pallas_call x1, Pallas kernels, per_device(): kernel_call(lambda *refs: backward_kernel(members, ranks, *refs), (saved_...  2.84 us
  transfers between devices with their start and end apart: 20, of which 7 were waited for; matrix products, arithmetic and copies ran while one was open for 0% of the time, Pallas kernels for 20%

profile of v4, /device:TPU:0, one launch (start us, length us, event | category | flops | bytes accessed | tf_op | source)
XLA Modules:
  0.0 79.1 jit_solution(11803121763563133698)
XLA Ops:
  0.6 0.0 copy-start.2
  0.6 1.2 %copy-done.2 = bf16[2,1024,256]{2,1,0:T(8,128)(2,1)S(1)} copy-done((bf16[2,1024,256]{2,1,0:T(8,128)(2,1)S(1)}, bf16[2,1024,256]{2,1,0:T(8,128)(2,1)}, u32[]{:S(2)}) %copy-start.2) | copy-done | bytes 1048600
  1.9 0.1 shard_map.153
  2.0 3.1 %collective-permute-start = (bf16[256,256]{1,0:T(8,128)(2,1)S(1)}, bf16[256,256]{1,0:T(8,128)(2,1)S(1)}, u32[]{:S(2)}, u32[]{:S(2)}) collective-permute-start(bf16[256,256]{1,0:T(8,128)(2,1)S(1)} %get-tuple-element.67), channel_id=1, source_target_pairs={{0,4},{4,8},{8,12},{12,0},{1,5},{5,9},{9,13},{13,1},{2,6},{6,10},{... | collective-permute-start | bytes 393224 | tf_op jit(solution)/shard_map/ppermute | solution.py:305
  5.0 2.1 %collective-permute-start.1 = (bf16[256,256]{1,0:T(8,128)(2,1)S(1)}, bf16[256,256]{1,0:T(8,128)(2,1)S(1)}, u32[]{:S(2)}, u32[]{:S(2)}) collective-permute-start(bf16[256,256]{1,0:T(8,128)(2,1)S(1)} %get-tuple-element.68), channel_id=1, source_target_pairs={{0,12},{4,0},{8,4},{12,8},{1,13},{5,1},{9,5},{13,9},{2,14},{6,2},{... | collective-permute-start | bytes 393224 | tf_op jit(solution)/shard_map/ppermute | solution.py:305
  7.1 0.0 collective-permute-start.2
  7.1 3.8 %collective-permute-start.3 = (bf16[256,256]{1,0:T(8,128)(2,1)S(1)}, bf16[256,256]{1,0:T(8,128)(2,1)S(1)}, u32[]{:S(2)}, u32[]{:S(2)}) collective-permute-start(bf16[256,256]{1,0:T(8,128)(2,1)S(1)} %get-tuple-element.72), channel_id=1, source_target_pairs={{0,12},{4,0},{8,4},{12,8},{1,13},{5,1},{9,5},{13,9},{2,14},{6,2},{... | collective-permute-start | bytes 393224 | tf_op jit(solution)/shard_map/ppermute | solution.py:305
  11.0 0.7 copy-done.7
  11.6 0.7 copy-done.9
  12.4 0.7 copy-done.10
  13.1 0.0 copy-start.6
  13.1 3.3 %shard_map.154 = (bf16[1536,1536]{1,0:T(8,128)(2,1)S(1)}, f32[256,1536]{1,0:T(8,128)S(1)}, f32[256,1536]{1,0:T(8,128)S(1)}) custom-call(s32[1]{0:T(128)} %bitcast.1.region_ref.refs_0_, s32[1]{0:T(128)} %bitcast.rank_ref.refs_1_.refs_0_, s32[4]{0:T(128)S(1)} %copy-done.7, s32[4,1536]{1,0:T(4,128)S(1)} %copy-done.9, f32[4,1536]{1,0:T(4,128)S(1)} %copy-done.10, ...), custom_call_target="tpu_custom_call" | custom-call | flops 1610612736 | bytes 12582912 | tf_op jit(solution)/shard_map/pallas_call | solution.py:333
  16.4 0.0 collective-permute-done.before_ref
  16.4 0.0 collective-permute-done.1.after_ref
  16.4 0.0 copy-done
  16.4 0.0 copy-done.1
  16.4 0.0 copy-done.3
  16.5 0.0 copy-done.5
  16.5 0.0 copy-done.6
  16.5 2.9 %shard_map.155 = (bf16[256,1536]{1,0:T(8,128)(2,1)S(1)}, bf16[256,1536]{1,0:T(8,128)(2,1)S(1)}, bf16[256,1536]{1,0:T(8,128)(2,1)S(1)}, bf16[256,1536]{1,0:T(8,12...) custom-call(f32[256,1536]{1,0:T(8,128)S(1)} %get-tuple-element.65.part_ref, ...), custom_call_target="tpu_custom_call" | custom-call | flops 905969664 | bytes 8388608 | tf_op jit(solution)/shard_map/pallas_call | solution.py:348
  19.4 0.1 collective-permute-start.5
  19.4 1.7 %collective-permute-start.4 = (bf16[128,1536]{1,0:T(8,128)(2,1)S(1)}, bf16[128,1536]{1,0:T(8,128)(2,1)S(1)}, u32[]{:S(2)}, u32[]{:S(2)}) collective-permute-start(bf16[128,1536]{1,0:T(8,128)(2,1)S(1)} %get-tuple-element.69.refs_2_), channel_id=1, source_target_pairs={{0,2},{1,3},{2,0},{3,1},{4,6},{5,7},{6,4},{7,5},{8,10},{9,11},{10,... | collective-permute-start | bytes 1179656 | tf_op jit(solution)/shard_map/ppermute | solution.py:309
  21.1 0.0 collective-permute-done.2.before_ref
  21.1 0.0 collective-permute-done.3.after_ref
  21.2 0.0 copy-start.8
  21.2 2.9 %shard_map.156 = (bf16[256,1536]{1,0:T(8,128)(2,1)S(1)}, bf16[256,1536]{1,0:T(8,128)(2,1)S(1)}, bf16[256,1536]{1,0:T(8,128)(2,1)S(1)}, bf16[256,1536]{1,0:T(8,12...) custom-call(f32[256,1536]{1,0:T(8,128)S(1)} %get-tuple-element.70.part_ref, ...), custom_call_target="tpu_custom_call" | custom-call | flops 905969664 | bytes 8388608 | tf_op jit(solution)/shard_map/pallas_call | solution.py:348
  24.0 0.2 collective-permute-start.6
  24.3 0.4 collective-permute-start.7
  24.7 0.0 collective-permute-done.5.refs_4_
  24.7 6.8 %collective-permute-done.4.refs_4_ = bf16[128,1536]{1,0:T(8,128)(2,1)S(1)} collective-permute-done((bf16[128,1536]{1,0:T(8,128)(2,1)S(1)}, bf16[128,1536]{1,0:T(8,128)(2,1)S(1)}, u32[]{:S(2)}, u32[]{:S(2)}) %collective-permute-start.4) | collective-permute-done | bytes 393248 | tf_op jit(solution)/shard_map/ppermute | solution.py:309
  31.4 0.0 collective-permute-done.6.refs_5_
  31.4 0.0 collective-permute-start.8
  31.4 0.0 copy-done.4
  31.4 2.4 %shard_map.157 = (f32[128,1536]{1,0:T(8,128)S(1)}, f32[128,1536]{1,0:T(8,128)S(1)}, f32[1,128]{1,0:T(1,128)S(1)}) custom-call(s32[1]{0:T(128)} %bitcast.1.region_ref.refs_0_, s32[4]{0:T(128)S(1)} %copy-done.8, bf16[128,1536]{1,0:T(8,128)(2,1)S(1)} %get-tuple-element.69.refs_2_, bf16[128,1536]{1,0:T(8,128)(2,1)S(1)} %get-tuple-element.73.refs_3_, ...), custom_call_target="tpu_custom_call" | custom-call | flops 4194304 | bytes 2097152 | tf_op jit(solution)/shard_map/pallas_call | solution.py:365
  33.9 5.5 %collective-permute-done.7.refs_5_ = bf16[128,1536]{1,0:T(8,128)(2,1)S(1)} collective-permute-done((bf16[128,1536]{1,0:T(8,128)(2,1)S(1)}, bf16[128,1536]{1,0:T(8,128)(2,1)S(1)}, u32[]{:S(2)}, u32[]{:S(2)}) %collective-permute-start.7) | collective-permute-done | bytes 393248 | tf_op jit(solution)/shard_map/ppermute | solution.py:309
  39.4 0.0 collective-permute-start.9
  39.4 0.0 collective-permute-done.8.refs_6_
  39.4 1.7 %collective-permute-done.9.refs_7_ = bf16[128,1536]{1,0:T(8,128)(2,1)S(1)} collective-permute-done((bf16[128,1536]{1,0:T(8,128)(2,1)S(1)}, bf16[128,1536]{1,0:T(8,128)(2,1)S(1)}, u32[]{:S(2)}, u32[]{:S(2)}) %collective-permute-start.9) | collective-permute-done | bytes 393248 | tf_op jit(solution)/shard_map/ppermute | solution.py:309
  41.1 2.5 %shard_map.158 = (bf16[128,1536]{1,0:T(8,128)(2,1)S(1)}, bf16[128,1536]{1,0:T(8,128)(2,1)S(1)}, f32[1,128]{1,0:T(1,128)S(1)}) custom-call(s32[1]{0:T(128)} %bitcast.1.region_ref.refs_0_, s32[4]{0:T(128)S(1)} %copy-done.8, bf16[128,1536]{1,0:T(8,128)(2,1)S(1)} %get-tuple-element.69.refs_2_, bf16[128,1536]{1,0:T(8,128)(2,1)S(1)} %get-tuple-element.73.refs_3_, ...), custom_call_target="tpu_custom_call" | custom-call | flops 4194304 | bytes 2097152 | tf_op jit(solution)/shard_map/pallas_call | solution.py:365
  43.7 2.8 %shard_map.159 = (bf16[256,1536]{1,0:T(8,128)(2,1)S(1)}, bf16[256,1536]{1,0:T(8,128)(2,1)S(1)}, bf16[176,256]{1,0:T(8,128)(2,1)S(1)}, bf16[176,256]{1,0:T(8,128)...) custom-call(s32[1]{0:T(128)} %bitcast.1.region_ref.refs_0_, s32[1]{0:T(128)} %bitcast.rank_ref.refs_1_.refs_0_, ...), custom_call_target="tpu_custom_call" | custom-call | flops 2013265920 | bytes 10485760 | tf_op jit(solution)/shard_map/pallas_call | solution.py:389
  46.5 0.2 collective-permute-start.10
  46.7 0.4 collective-permute-start.11
  47.1 1.4 %shard_map.160 = (bf16[256,1536]{1,0:T(8,128)(2,1)S(1)}, bf16[256,1536]{1,0:T(8,128)(2,1)S(1)}, bf16[2,256,256]{2,1,0:T(8,128)(2,1)S(1)}, bf16[2,256,256]{2,1,0:T(8,128)(2,1)S(1)}) custom-call(bf16[1536,1536]{1,0:T(8,128)(2,1)S(1)} %get-tuple-element.66.table_ref.refs_0_, bf16[256,256]{1,0:T(8,128)(2,1)S(1)} %copy-done.1, ...), custom_call_target="tpu_custom_call" | custom-call | flops 1207959552 | bytes 6291456 | tf_op jit(solution)/shard_map/pallas_call | solution.py:406
  48.5 0.0 collective-permute-done.10.refs_2_
  48.5 0.0 collective-permute-done.11.refs_3_
  48.5 1.7 %collective-permute-start.12 = (bf16[176,256]{1,0:T(8,128)(2,1)S(1)}, bf16[176,256]{1,0:T(8,128)(2,1)S(1)}, u32[]{:S(2)}, u32[]{:S(2)}) collective-permute-start(bf16[176,256]{1,0:T(8,128)(2,1)S(1)} %get-tuple-element.108), channel_id=1, source_target_pairs={{0,2},{1,3},{2,0},{3,1},{4,6},{5,7},{6,4},{7,5},{8,10},{9,11},{10,... | collective-permute-start | bytes 270344 | tf_op jit(solution)/shard_map/ppermute | solution.py:309
  50.2 0.0 collective-permute-start.15
  50.3 3.8 %collective-permute-start.16 = (bf16[2,256,256]{2,1,0:T(8,128)(2,1)S(1)}, bf16[2,256,256]{2,1,0:T(8,128)(2,1)S(1)}, u32[]{:S(2)}, u32[]{:S(2)}) collective-permute-start(bf16[2,256,256]{2,1,0:T(8,128)(2,1)S(1)} %get-tuple-element.112), channel_id=1, source_target_pairs={{0,12},{4,0},{8,4},{12,8},{1,13},{5,1},{9,5},{13,9},{2,14},{6,2},{... | collective-permute-start | bytes 786440 | tf_op jit(solution)/shard_map/ppermute | solution.py:305
  54.1 0.0 collective-permute-done.12.refs_1_
  54.1 0.1 collective-permute-start.13
  54.2 11.7 %collective-permute-done.13.refs_1_ = bf16[176,256]{1,0:T(8,128)(2,1)S(1)} collective-permute-done((bf16[176,256]{1,0:T(8,128)(2,1)S(1)}, bf16[176,256]{1,0:T(8,128)(2,1)S(1)}, u32[]{:S(2)}, u32[]{:S(2)}) %collective-permute-start.13) | collective-permute-done | bytes 90144 | tf_op jit(solution)/shard_map/ppermute | solution.py:309
  65.9 2.5 %collective-permute-start.14 = (bf16[176,256]{1,0:T(8,128)(2,1)S(1)}, bf16[176,256]{1,0:T(8,128)(2,1)S(1)}, u32[]{:S(2)}, u32[]{:S(2)}) collective-permute-start(bf16[176,256]{1,0:T(8,128)(2,1)S(1)} %shard_map.163.refs_0_), channel_id=1, source_target_pairs={{0,8},{4,12},{8,0},{12,4},{1,9},{5,13},{9,1},{13,5},{2,10},{6,14},... | collective-permute-start | bytes 270344 | tf_op jit(solution)/shard_map/ppermute | solution.py:309
  68.4 1.8 %shard_map.165.own_ref = f32[2,1024,256]{2,1,0:T(8,128)S(1)} custom-call(bf16[1536,1536]{1,0:T(8,128)(2,1)S(1)} %get-tuple-element.66.table_ref.refs_0_, bf16[256,1536]{1,0:T(8,128)(2,1)S(1)} %get-tuple-element.109.refs_0_, bf16[256,1536]{1,0:T(8,128)(2,1)S(1)} %get-tuple-element.110.refs_1_), custom_call_target="tpu_custom_call" | custom-call | flops 1610612736 | bytes 6291456 | tf_op jit(solution)/shard_map/pallas_call | solution.py:422
  70.2 0.0 collective-permute-done.15.from_prev_ref
  70.2 0.0 collective-permute-done.16.from_next_ref
  70.2 1.1 %shard_map.166 = bf16[2,1024,256]{2,1,0:T(8,128)(2,1)} custom-call(f32[2,1024,256]{2,1,0:T(8,128)S(1)} %shard_map.165.own_ref, bf16[2,256,256]{2,1,0:T(8,128)(2,1)S(1)} %collective-permute-done.15.from_prev_ref, bf16[2,256,256]{2,1,0:T(8,128)(2,1)S(1)} %collective-permute-done.16.from_next_ref), custom_call_target="tpu_custom_call" | custom-call | flops 1048576 | bytes 3145728 | tf_op jit(solution)/shard_map/pallas_call | solution.py:434
  71.3 1.0 %collective-permute-done.14.refs_1_ = bf16[176,256]{1,0:T(8,128)(2,1)S(1)} collective-permute-done((bf16[176,256]{1,0:T(8,128)(2,1)S(1)}, bf16[176,256]{1,0:T(8,128)(2,1)S(1)}, u32[]{:S(2)}, u32[]{:S(2)}) %collective-permute-start.14) | collective-permute-done | bytes 90144 | tf_op jit(solution)/shard_map/ppermute | solution.py:309
  72.3 0.5 collective-permute-start.18
  72.8 0.0 collective-permute-start.17
  72.8 4.1 %collective-permute-done.18.refs_3_ = bf16[176,256]{1,0:T(8,128)(2,1)S(1)} collective-permute-done((bf16[176,256]{1,0:T(8,128)(2,1)S(1)}, bf16[176,256]{1,0:T(8,128)(2,1)S(1)}, u32[]{:S(2)}, u32[]{:S(2)}) %collective-permute-start.18) | collective-permute-done | bytes 90144 | tf_op jit(solution)/shard_map/ppermute | solution.py:309
  76.9 0.0 collective-permute-start.19
  76.9 0.0 collective-permute-done.17.refs_2_
  76.9 1.3 %collective-permute-done.19.refs_4_ = bf16[176,256]{1,0:T(8,128)(2,1)S(1)} collective-permute-done((bf16[176,256]{1,0:T(8,128)(2,1)S(1)}, bf16[176,256]{1,0:T(8,128)(2,1)S(1)}, u32[]{:S(2)}, u32[]{:S(2)}) %collective-permute-start.19) | collective-permute-done | bytes 90144 | tf_op jit(solution)/shard_map/ppermute | solution.py:309
  78.2 0.9 %shard_map.167 = (f32[256,256]{1,0:T(8,128)}, f32[1,256]{1,0:T(1,128)}, f32[256,256]{1,0:T(8,128)}, f32[1,256]{1,0:T(1,128)}, f32[256,128]{1,0:T(8,128)}, /*index=5*/f32[1,4]{1,0:T(1,128)}) custom-call(s32[1]{0:T(128)} %bitcast.rank_ref.refs_1_.refs_0_, bf16[176,256]{1,0:T(8,128)(2,1)S(1)} %shard_map.164.refs_1_, ...), custom_call_target="tpu_custom_call" | custom-call | flops 1048576 | bytes 2097152 | tf_op jit(solution)/shard_map/pallas_call | solution.py:448
  (13 shorter events, 0.1 us)
Async XLA Ops:
  0.6 1.2 %copy-start.2 = (bf16[2,1024,256]{2,1,0:T(8,128)(2,1)S(1)}, bf16[2,1024,256]{2,1,0:T(8,128)(2,1)}, u32[]{:S(2)}) copy-start(bf16[2,1024,256]{2,1,0:T(8,128)(2,1)} %latent_ref.1) | copy-start | bytes 3145732
  2.0 14.4 %collective-permute-start = (bf16[256,256]{1,0:T(8,128)(2,1)S(1)}, bf16[256,256]{1,0:T(8,128)(2,1)S(1)}, u32[]{:S(2)}, u32[]{:S(2)}) collective-permute-start(bf16[256,256]{1,0:T(8,128)(2,1)S(1)} %get-tuple-element.67), channel_id=1, source_target_pairs={{0,4},{4,8},{8,12},{12,0},{1,5},{5,9},{9,13},{13,1},{2,6},{6,10},{... | collective-permute-start | bytes 393224 | tf_op jit(solution)/shard_map/ppermute | solution.py:305
  5.0 11.4 %collective-permute-start.1 = (bf16[256,256]{1,0:T(8,128)(2,1)S(1)}, bf16[256,256]{1,0:T(8,128)(2,1)S(1)}, u32[]{:S(2)}, u32[]{:S(2)}) collective-permute-start(bf16[256,256]{1,0:T(8,128)(2,1)S(1)} %get-tuple-element.68), channel_id=1, source_target_pairs={{0,12},{4,0},{8,4},{12,8},{1,13},{5,1},{9,5},{13,9},{2,14},{6,2},{... | collective-permute-start | bytes 393224 | tf_op jit(solution)/shard_map/ppermute | solution.py:305
  7.1 14.0 %collective-permute-start.2 = (bf16[256,256]{1,0:T(8,128)(2,1)S(1)}, bf16[256,256]{1,0:T(8,128)(2,1)S(1)}, u32[]{:S(2)}, u32[]{:S(2)}) collective-permute-start(bf16[256,256]{1,0:T(8,128)(2,1)S(1)} %get-tuple-element.71), channel_id=1, source_target_pairs={{0,4},{4,8},{8,12},{12,0},{1,5},{5,9},{9,13},{13,1},{2,6},{6,10},{... | collective-permute-start | bytes 393224 | tf_op jit(solution)/shard_map/ppermute | solution.py:305
  7.1 14.0 %collective-permute-start.3 = (bf16[256,256]{1,0:T(8,128)(2,1)S(1)}, bf16[256,256]{1,0:T(8,128)(2,1)S(1)}, u32[]{:S(2)}, u32[]{:S(2)}) collective-permute-start(bf16[256,256]{1,0:T(8,128)(2,1)S(1)} %get-tuple-element.72), channel_id=1, source_target_pairs={{0,12},{4,0},{8,4},{12,8},{1,13},{5,1},{9,5},{13,9},{2,14},{6,2},{... | collective-permute-start | bytes 393224 | tf_op jit(solution)/shard_map/ppermute | solution.py:305
  11.0 0.7 copy-start.7
  11.6 0.7 copy-start.9
  12.3 0.7 copy-start.10
  13.1 3.3 %copy-start = (bf16[256,256]{1,0:T(8,128)(2,1)S(1)}, bf16[256,256]{1,0:T(8,128)(2,1)}, u32[]{:S(2)}) copy-start(bf16[256,256]{1,0:T(8,128)(2,1)} %refs_2_.1) | copy-start | bytes 393220
  13.1 3.4 %copy-start.1 = (bf16[256,256]{1,0:T(8,128)(2,1)S(1)}, bf16[256,256]{1,0:T(8,128)(2,1)}, u32[]{:S(2)}) copy-start(bf16[256,256]{1,0:T(8,128)(2,1)} %refs_1_.5) | copy-start | bytes 393220
  13.1 3.4 %copy-start.3 = (bf16[256,128]{1,0:T(8,128)(2,1)S(1)}, bf16[256,128]{1,0:T(8,128)(2,1)}, u32[]{:S(2)}) copy-start(bf16[256,128]{1,0:T(8,128)(2,1)} %refs_3_.1) | copy-start | bytes 196612
  13.1 3.4 %copy-start.5 = (f32[256]{0:T(256)S(1)}, f32[256]{0:T(256)}, u32[]{:S(2)}) copy-start(f32[256]{0:T(256)} %param.16) | copy-start | bytes 3076
  13.1 3.4 %copy-start.6 = (f32[256]{0:T(256)S(1)}, f32[256]{0:T(256)}, u32[]{:S(2)}) copy-start(f32[256]{0:T(256)} %param.18) | copy-start | bytes 3076
  19.4 5.3 %collective-permute-start.5 = (bf16[128,1536]{1,0:T(8,128)(2,1)S(1)}, bf16[128,1536]{1,0:T(8,128)(2,1)S(1)}, u32[]{:S(2)}, u32[]{:S(2)}) collective-permute-start(bf16[128,1536]{1,0:T(8,128)(2,1)S(1)} %get-tuple-element.69.refs_2_), channel_id=1, source_target_pairs={{0,1},{1,0},{2,3},{3,2},{4,5},{5,4},{6,7},{7,6},{8,9},{9,8},{10,11... | collective-permute-start | bytes 1179656 | tf_op jit(solution)/shard_map/ppermute | solution.py:309
  19.4 12.0 %collective-permute-start.4 = (bf16[128,1536]{1,0:T(8,128)(2,1)S(1)}, bf16[128,1536]{1,0:T(8,128)(2,1)S(1)}, u32[]{:S(2)}, u32[]{:S(2)}) collective-permute-start(bf16[128,1536]{1,0:T(8,128)(2,1)S(1)} %get-tuple-element.69.refs_2_), channel_id=1, source_target_pairs={{0,2},{1,3},{2,0},{3,1},{4,6},{5,7},{6,4},{7,5},{8,10},{9,11},{10,... | collective-permute-start | bytes 1179656 | tf_op jit(solution)/shard_map/ppermute | solution.py:309
  21.1 10.3 %copy-start.4 = (bf16[1536,128]{1,0:T(8,128)(2,1)S(1)}, bf16[1536,128]{1,0:T(8,128)(2,1)}, u32[]{:S(2)}) copy-start(bf16[1536,128]{1,0:T(8,128)(2,1)} %refs_6_.1) | copy-start | bytes 1179652
  21.2 10.3 %copy-start.8 = (s32[4]{0:T(128)S(1)}, s32[4]{0:T(128)}, u32[]{:S(2)}) copy-start(s32[4]{0:T(128)} %refs_1_.4) | copy-start | bytes 52
  24.0 7.4 %collective-permute-start.6 = (bf16[128,1536]{1,0:T(8,128)(2,1)S(1)}, bf16[128,1536]{1,0:T(8,128)(2,1)S(1)}, u32[]{:S(2)}, u32[]{:S(2)}) collective-permute-start(bf16[128,1536]{1,0:T(8,128)(2,1)S(1)} %get-tuple-element.73.refs_3_), channel_id=1, source_target_pairs={{0,1},{1,0},{2,3},{3,2},{4,5},{5,4},{6,7},{7,6},{8,9},{9,8},{10,11... | collective-permute-start | bytes 1179656 | tf_op jit(solution)/shard_map/ppermute | solution.py:309
  24.3 15.1 %collective-permute-start.7 = (bf16[128,1536]{1,0:T(8,128)(2,1)S(1)}, bf16[128,1536]{1,0:T(8,128)(2,1)S(1)}, u32[]{:S(2)}, u32[]{:S(2)}) collective-permute-start(bf16[128,1536]{1,0:T(8,128)(2,1)S(1)} %get-tuple-element.73.refs_3_), channel_id=1, source_target_pairs={{0,2},{1,3},{2,0},{3,1},{4,6},{5,7},{6,4},{7,5},{8,10},{9,11},{10,... | collective-permute-start | bytes 1179656 | tf_op jit(solution)/shard_map/ppermute | solution.py:309
  31.4 8.0 %collective-permute-start.8 = (bf16[128,1536]{1,0:T(8,128)(2,1)S(1)}, bf16[128,1536]{1,0:T(8,128)(2,1)S(1)}, u32[]{:S(2)}, u32[]{:S(2)}) collective-permute-start(bf16[128,1536]{1,0:T(8,128)(2,1)S(1)} %collective-permute-done.4.refs_4_), channel_id=1, source_target_pairs={{0,1},{1,0},{2,3},{3,2},{4,5},{5,4},{6,7},{7,6},{8,9},{9,8},{10,11... | collective-permute-start | bytes 1179656 | tf_op jit(solution)/shard_map/ppermute | solution.py:309
  39.4 1.7 %collective-permute-start.9 = (bf16[128,1536]{1,0:T(8,128)(2,1)S(1)}, bf16[128,1536]{1,0:T(8,128)(2,1)S(1)}, u32[]{:S(2)}, u32[]{:S(2)}) collective-permute-start(bf16[128,1536]{1,0:T(8,128)(2,1)S(1)} %collective-permute-done.7.refs_5_), channel_id=1, source_target_pairs={{0,1},{1,0},{2,3},{3,2},{4,5},{5,4},{6,7},{7,6},{8,9},{9,8},{10,11... | collective-permute-start | bytes 1179656 | tf_op jit(solution)/shard_map/ppermute | solution.py:309
  46.5 2.0 %collective-permute-start.10 = (bf16[176,256]{1,0:T(8,128)(2,1)S(1)}, bf16[176,256]{1,0:T(8,128)(2,1)S(1)}, u32[]{:S(2)}, u32[]{:S(2)}) collective-permute-start(bf16[176,256]{1,0:T(8,128)(2,1)S(1)} %get-tuple-element.99), channel_id=1, source_target_pairs={{0,1},{1,0},{2,3},{3,2},{4,5},{5,4},{6,7},{7,6},{8,9},{9,8},{10,11... | collective-permute-start | bytes 270344 | tf_op jit(solution)/shard_map/ppermute | solution.py:309
  46.7 1.8 %collective-permute-start.11 = (bf16[176,256]{1,0:T(8,128)(2,1)S(1)}, bf16[176,256]{1,0:T(8,128)(2,1)S(1)}, u32[]{:S(2)}, u32[]{:S(2)}) collective-permute-start(bf16[176,256]{1,0:T(8,128)(2,1)S(1)} %get-tuple-element.100), channel_id=1, source_target_pairs={{0,1},{1,0},{2,3},{3,2},{4,5},{5,4},{6,7},{7,6},{8,9},{9,8},{10,11... | collective-permute-start | bytes 270344 | tf_op jit(solution)/shard_map/ppermute | solution.py:309
  48.5 5.5 %collective-permute-start.12 = (bf16[176,256]{1,0:T(8,128)(2,1)S(1)}, bf16[176,256]{1,0:T(8,128)(2,1)S(1)}, u32[]{:S(2)}, u32[]{:S(2)}) collective-permute-start(bf16[176,256]{1,0:T(8,128)(2,1)S(1)} %get-tuple-element.108), channel_id=1, source_target_pairs={{0,2},{1,3},{2,0},{3,1},{4,6},{5,7},{6,4},{7,5},{8,10},{9,11},{10,... | collective-permute-start | bytes 270344 | tf_op jit(solution)/shard_map/ppermute | solution.py:309
  50.2 19.9 %collective-permute-start.15 = (bf16[2,256,256]{2,1,0:T(8,128)(2,1)S(1)}, bf16[2,256,256]{2,1,0:T(8,128)(2,1)S(1)}, u32[]{:S(2)}, u32[]{:S(2)}) collective-permute-start(bf16[2,256,256]{2,1,0:T(8,128)(2,1)S(1)} %get-tuple-element.111), channel_id=1, source_target_pairs={{0,4},{4,8},{8,12},{12,0},{1,5},{5,9},{9,13},{13,1},{2,6},{6,10},{... | collective-permute-start | bytes 786440 | tf_op jit(solution)/shard_map/ppermute | solution.py:305
  50.3 19.9 %collective-permute-start.16 = (bf16[2,256,256]{2,1,0:T(8,128)(2,1)S(1)}, bf16[2,256,256]{2,1,0:T(8,128)(2,1)S(1)}, u32[]{:S(2)}, u32[]{:S(2)}) collective-permute-start(bf16[2,256,256]{2,1,0:T(8,128)(2,1)S(1)} %get-tuple-element.112), channel_id=1, source_target_pairs={{0,12},{4,0},{8,4},{12,8},{1,13},{5,1},{9,5},{13,9},{2,14},{6,2},{... | collective-permute-start | bytes 786440 | tf_op jit(solution)/shard_map/ppermute | solution.py:305
  54.1 11.8 %collective-permute-start.13 = (bf16[176,256]{1,0:T(8,128)(2,1)S(1)}, bf16[176,256]{1,0:T(8,128)(2,1)S(1)}, u32[]{:S(2)}, u32[]{:S(2)}) collective-permute-start(bf16[176,256]{1,0:T(8,128)(2,1)S(1)} %shard_map.162.refs_0_), channel_id=1, source_target_pairs={{0,4},{4,0},{8,12},{12,8},{1,5},{5,1},{9,13},{13,9},{2,6},{6,2},{1... | collective-permute-start | bytes 270344 | tf_op jit(solution)/shard_map/ppermute | solution.py:309
  65.9 6.4 %collective-permute-start.14 = (bf16[176,256]{1,0:T(8,128)(2,1)S(1)}, bf16[176,256]{1,0:T(8,128)(2,1)S(1)}, u32[]{:S(2)}, u32[]{:S(2)}) collective-permute-start(bf16[176,256]{1,0:T(8,128)(2,1)S(1)} %shard_map.163.refs_0_), channel_id=1, source_target_pairs={{0,8},{4,12},{8,0},{12,4},{1,9},{5,13},{9,1},{13,5},{2,10},{6,14},... | collective-permute-start | bytes 270344 | tf_op jit(solution)/shard_map/ppermute | solution.py:309
  72.3 4.6 %collective-permute-start.18 = (bf16[176,256]{1,0:T(8,128)(2,1)S(1)}, bf16[176,256]{1,0:T(8,128)(2,1)S(1)}, u32[]{:S(2)}, u32[]{:S(2)}) collective-permute-start(bf16[176,256]{1,0:T(8,128)(2,1)S(1)} %shard_map.164.refs_1_), channel_id=1, source_target_pairs={{0,2},{1,3},{2,0},{3,1},{4,6},{5,7},{6,4},{7,5},{8,10},{9,11},{10,... | collective-permute-start | bytes 270344 | tf_op jit(solution)/shard_map/ppermute | solution.py:309
  72.8 4.1 %collective-permute-start.17 = (bf16[176,256]{1,0:T(8,128)(2,1)S(1)}, bf16[176,256]{1,0:T(8,128)(2,1)S(1)}, u32[]{:S(2)}, u32[]{:S(2)}) collective-permute-start(bf16[176,256]{1,0:T(8,128)(2,1)S(1)} %shard_map.164.refs_1_), channel_id=1, source_target_pairs={{0,1},{1,0},{2,3},{3,2},{4,5},{5,4},{6,7},{7,6},{8,9},{9,8},{10,11... | collective-permute-start | bytes 270344 | tf_op jit(solution)/shard_map/ppermute | solution.py:309
  76.9 1.3 %collective-permute-start.19 = (bf16[176,256]{1,0:T(8,128)(2,1)S(1)}, bf16[176,256]{1,0:T(8,128)(2,1)S(1)}, u32[]{:S(2)}, u32[]{:S(2)}) collective-permute-start(bf16[176,256]{1,0:T(8,128)(2,1)S(1)} %collective-permute-done.18.refs_3_), channel_id=1, source_target_pairs={{0,1},{1,0},{2,3},{3,2},{4,5},{5,4},{6,7},{7,6},{8,9},{9,8},{10,11... | collective-permute-start | bytes 270344 | tf_op jit(solution)/shard_map/ppermute | solution.py:309

commit v5 on v4

--- a/solution.py
+++ b/solution.py
@@ -51,8 +51,8 @@
     refs[-1][...] = latent_ref[...]
 
 
-def table_kernel(region_ref, rank_ref, counts_ref, nbr_ref, weight_ref, latent_ref, table_ref, *part_refs):
-    members, nodes, width = latent_ref.shape
+def table_kernel(region_ref, rank_ref, counts_ref, nbr_ref, weight_ref, latent_ref, table_ref, part_ref):
+    nodes = latent_ref.shape[1]
     ext, slots = table_ref.shape
     live = lax.broadcasted_iota(jnp.int32, (1, slots), 1) < counts_ref[region_ref[0]]
     nbr = [nbr_ref[k : k + 1, :] for k in range(K)]
@@ -81,11 +81,9 @@
                 near = jnp.broadcast_to(near, (16, size)).astype(jnp.bfloat16)
                 tile = jnp.where(rows[:, :, :size] == near[None], wide[k][None], tile)
             table_ref[b * BLOCK : (b + 1) * BLOCK, lo : lo + size] = tile.reshape(BLOCK, size)
-    turned = jnp.concatenate([latent_ref[m].T for m in range(members)], axis=0)
+    turned = latent_ref[0].T
     for lo, size in split(slots, CHUNK):
-        part = nn_dot(turned, table_ref[HALO : HALO + nodes, lo : lo + size])
-        for m in range(members):
-            part_refs[m][:, lo : lo + size] = part[m * width : (m + 1) * width]
+        part_ref[:, lo : lo + size] = nn_dot(turned, table_ref[HALO : HALO + nodes, lo : lo + size])
 
 
 def column(ref):
@@ -94,7 +92,7 @@
 
 
 def forward_kernel(
-    part_ref, table_ref, before_ref, after_ref, w_one_ref, b_one_ref, w_two_ref, b_two_ref, w_three_ref,
+    member, own_ref, table_ref, before_ref, after_ref, w_one_ref, b_one_ref, w_two_ref, b_two_ref, w_three_ref,
     mixed_ref, act_one_ref, slope_one_ref, act_two_ref, slope_two_ref, decoded_ref,
 ):
     ext, slots = table_ref.shape
@@ -107,11 +105,18 @@
         act = half * gate
         return act.astype(jnp.bfloat16), (gate + act * (2.0 - gate)).astype(jnp.bfloat16)
 
-    edges = jnp.concatenate([before_ref[...].T, after_ref[...].T], axis=1)
+    if member:
+        nodes = jnp.concatenate([before_ref[...].T, own_ref[member].T, after_ref[...].T], axis=1)
+    else:
+        nodes = jnp.concatenate([before_ref[...].T, after_ref[...].T], axis=1)
     for lo, size in split(slots, CHUNK):
         lanes = slice(lo, lo + size)
-        rim = jnp.concatenate([table_ref[:HALO, lanes], table_ref[ext - HALO :, lanes]], axis=0)
-        mixed = (part_ref[:, lanes] + nn_dot(edges, rim)).astype(jnp.bfloat16)
+        if member:
+            mixed = nn_dot(nodes, table_ref[:, lanes])
+        else:
+            rims = jnp.concatenate([table_ref[:HALO, lanes], table_ref[ext - HALO :, lanes]], axis=0)
+            mixed = own_ref[:, lanes] + nn_dot(nodes, rims)
+        mixed = mixed.astype(jnp.bfloat16)
         mixed_ref[:, lanes] = mixed
         act_one, slope_one_ref[:, lanes] = layer(w_one, b_one, mixed, size)
         act_one_ref[:, lanes] = act_one
@@ -330,10 +335,10 @@
     rank_at = rank[None].astype(jnp.int32)
     region_at = region[None].astype(jnp.int32)
 
-    table, *part = kernel_call(
+    table, part = kernel_call(
         table_kernel,
-        (shape((ext, slots), bf16),) + (shape((width, slots), f32),) * members,
-        flops=2 * members * width * nodes * slots,
+        (shape((ext, slots), bf16), shape((width, slots), f32)),
+        flops=2 * width * nodes * slots,
         moved=12 * MIB,
         smem=3,
         operands=6,
@@ -346,12 +351,12 @@
     saved, known = [], []
     for m in each:
         *kept, decoded = kernel_call(
-            forward_kernel,
+            lambda *refs: forward_kernel(m, *refs),
             (mixed_shape,) + (saved_shape,) * 4 + (decoded_shape,),
-            flops=2 * slots * (2 * HALO * width + dense),
+            flops=2 * slots * ((ext if m else 2 * HALO) * width + dense),
             moved=8 * MIB,
             operands=9,
-        )(part[m], table, before[m], after[m], w_one, b_one[None], w_two, b_two[None], w_three)
+        )(latent if m else part, table, before[m], after[m], w_one, b_one[None], w_two, b_two[None], w_three)
         saved.append(kept)
         known.append({0: decoded})
         bit = 2
@@ -372,12 +377,11 @@
         )(*operands)
 
     near = [{i: block for i, block in known[m].items() if i > 1} for m in each]
-    beside = [known[m][1] for m in each]
-    near[:-1], beside = lax.optimization_barrier((near[:-1], beside))
-    carried = scored(beside, [targets], first=True)
+    early = [known[m][1] for m in each] + [block for blocks in near[:-1] for block in blocks.values()]
+    carried = scored(early, [targets], first=True)
     near[-1], carried = lax.optimization_barrier((near[-1], carried))
-    others = [block for blocks in near for block in blocks.values()]
-    others += [swapped(block, "member", 1) for block in others]
+    others = [*near[-1].values()]
+    others += [swapped(block, "member", 1) for blocks in near for block in blocks.values()]
     carried = scored(others, carried, last=True)
     *d_decoded, score = carried
 
@@ -417,8 +421,6 @@
             received, head, tail = lax.optimization_barrier((received, head, tail))
         pieces = summed(pieces[::2], received)
         bit = 2 * bit
-    from_next = shifted(head, "space", -1)
-    from_prev = shifted(tail, "space", 1)
     own = kernel_call(
         own_kernel,
         shape((members, nodes, width), f32),
@@ -431,6 +433,10 @@
     while step < regions:
         (total,) = summed([total], [swapped(total, "space", step)])
         step = 2 * step
+        if step == regions // 2:
+            total, head, tail = lax.optimization_barrier((total, head, tail))
+            from_next = shifted(head, "space", -1)
+            from_prev = shifted(tail, "space", 1)
     latent_grad = kernel_call(
         finish_kernel,
         shape((members, nodes, width), bf16),
@@ -438,12 +444,12 @@
         moved=3 * MIB,
         operands=3,
     )(own, from_prev, from_next)
-    total, latent_grad = lax.optimization_barrier((total, latent_grad))
     totals = {0: total}
     while bit > 1:
         bit = bit // 2
         totals.update({i ^ bit: swapped(totals[i], "member", bit) for i in sorted(totals)})
     totals = [totals[i] for i in range(ranks)]
+    totals, latent_grad = lax.optimization_barrier((totals, latent_grad))
     row = shape((1, hidden), f32)
     g_one, g_bone, g_two, g_btwo, g_three, tally = kernel_call(
         lambda *refs: unpack_kernel(1.0 / (OBS_MEAN * members * ranks), *refs),

time: 79.4 us -> 76.1 us (0.958)
  waiting for transfers between devices: 32.1 us -> 29.1 us
    ppermute x14, waiting for transfers between devices: 32.1 us -> 29 us  [swapped(): lax.ppermute(block, axis, [(i, i ^ by) for i in range(lax.axis_size(axis))])]
  transfers between devices with their start and end apart: 20 -> 20, of which waited for: 7 -> 8; matrix products, arithmetic and copies ran while one was open for 0% -> 0% of each run, Pallas kernels for 20% -> 22%
where the time goes in v5:
time: 76.1 us; the launch traced here: 75.7 us
  waiting for transfers between devices  29.1 us (38%)
  Pallas kernels  22.5 us (30%)
  starting transfers between devices  19.9 us (26%)
  local copies, waits for them, and re-layouts  3.42 us (4%)
  between operations  0.89 us (1%)
    ppermute x14, waiting for transfers between devices, swapped(): lax.ppermute(block, axis, [(i, i ^ by) for i in range(lax.axis_size(axis))])  29 us
    ppermute x6, starting transfers between devices, shifted(): lax.ppermute(shard, axis, [(i, (i + by) % length) for i in range(length)])  12.9 us
    ppermute x14, starting transfers between devices, swapped(): lax.ppermute(block, axis, [(i, i ^ by) for i in range(lax.axis_size(axis))])  7 us
    pallas_call x2, Pallas kernels, per_device(): kernel_call(lambda *refs: forward_kernel(m, *refs), (mixed_shape,) + (sav...  6.56 us
    pallas_call x2, Pallas kernels, scored(): kernel_call(lambda *refs: score_kernel(members, len(others), members * ra...  4.58 us
    unnamed x22, local copies, waits for them, and re-layouts  3.42 us
    pallas_call x1, Pallas kernels, per_device(): kernel_call(table_kernel, (shape((ext, slots), bf16), shape((width, slots...  3.11 us
    pallas_call x1, Pallas kernels, per_device(): kernel_call(lambda *refs: backward_kernel(members, ranks, *refs), (saved_...  2.84 us
  transfers between devices with their start and end apart: 20, of which 8 were waited for; matrix products, arithmetic and copies ran while one was open for 0% of the time, Pallas kernels for 22%

profile of v5, /device:TPU:0, one launch (start us, length us, event | category | flops | bytes accessed | tf_op | source)
XLA Modules:
  0.0 75.7 jit_solution(9949225003196464164)
XLA Ops:
  0.6 0.0 copy-start
  0.6 0.0 copy-start.1
  0.7 0.0 copy-start.2
  0.7 1.3 %copy-done.2 = bf16[2,1024,256]{2,1,0:T(8,128)(2,1)S(1)} copy-done((bf16[2,1024,256]{2,1,0:T(8,128)(2,1)S(1)}, bf16[2,1024,256]{2,1,0:T(8,128)(2,1)}, u32[]{:S(2)}) %copy-start.2) | copy-done | bytes 1048600
  1.9 0.1 shard_map.153
  2.0 3.1 %collective-permute-start = (bf16[256,256]{1,0:T(8,128)(2,1)S(1)}, bf16[256,256]{1,0:T(8,128)(2,1)S(1)}, u32[]{:S(2)}, u32[]{:S(2)}) collective-permute-start(bf16[256,256]{1,0:T(8,128)(2,1)S(1)} %get-tuple-element.69), channel_id=1, source_target_pairs={{0,4},{4,8},{8,12},{12,0},{1,5},{5,9},{9,13},{13,1},{2,6},{6,10},{... | collective-permute-start | bytes 393224 | tf_op jit(solution)/shard_map/ppermute | solution.py:310
  5.1 2.1 %collective-permute-start.1 = (bf16[256,256]{1,0:T(8,128)(2,1)S(1)}, bf16[256,256]{1,0:T(8,128)(2,1)S(1)}, u32[]{:S(2)}, u32[]{:S(2)}) collective-permute-start(bf16[256,256]{1,0:T(8,128)(2,1)S(1)} %get-tuple-element.70), channel_id=1, source_target_pairs={{0,12},{4,0},{8,4},{12,8},{1,13},{5,1},{9,5},{13,9},{2,14},{6,2},{... | collective-permute-start | bytes 393224 | tf_op jit(solution)/shard_map/ppermute | solution.py:310
  7.2 0.0 collective-permute-start.2
  7.2 3.8 %collective-permute-start.3 = (bf16[256,256]{1,0:T(8,128)(2,1)S(1)}, bf16[256,256]{1,0:T(8,128)(2,1)S(1)}, u32[]{:S(2)}, u32[]{:S(2)}) collective-permute-start(bf16[256,256]{1,0:T(8,128)(2,1)S(1)} %get-tuple-element.73), channel_id=1, source_target_pairs={{0,12},{4,0},{8,4},{12,8},{1,13},{5,1},{9,5},{13,9},{2,14},{6,2},{... | collective-permute-start | bytes 393224 | tf_op jit(solution)/shard_map/ppermute | solution.py:310
  11.0 0.7 copy-done.7
  11.7 0.7 copy-done.9
  12.4 0.7 copy-done.10
  13.2 3.1 %shard_map.154 = (bf16[1536,1536]{1,0:T(8,128)(2,1)S(1)}, f32[256,1536]{1,0:T(8,128)S(1)}) custom-call(s32[1]{0:T(128)} %bitcast.1.region_ref.refs_0_, s32[1]{0:T(128)} %bitcast.rank_ref.refs_1_.refs_0_, s32[4]{0:T(128)S(1)} %copy-done.7, s32[4,1536]{1,0:T(4,128)S(1)} %copy-done.9, f32[4,1536]{1,0:T(4,128)S(1)} %copy-done.10, ...), custom_call_target="tpu_custom_call" | custom-call | flops 805306368 | bytes 12582912 | tf_op jit(solution)/shard_map/pallas_call | solution.py:338
  16.3 0.0 collective-permute-done.refs_2_
  16.3 0.0 collective-permute-done.1.refs_3_
  16.3 0.0 copy-done
  16.3 0.0 copy-done.1
  16.3 0.0 copy-done.3
  16.3 0.0 copy-done.5
  16.4 2.9 %shard_map.155 = (bf16[256,1536]{1,0:T(8,128)(2,1)S(1)}, bf16[256,1536]{1,0:T(8,128)(2,1)S(1)}, bf16[256,1536]{1,0:T(8,128)(2,1)S(1)}, bf16[256,1536]{1,0:T(8,12...) custom-call(f32[256,1536]{1,0:T(8,128)S(1)} %get-tuple-element.67.refs_0_, ...), custom_call_target="tpu_custom_call" | custom-call | flops 905969664 | bytes 8388608 | tf_op jit(solution)/shard_map/pallas_call | solution.py:353
  19.2 0.0 copy-start.4
  19.2 0.0 copy-start.8
  19.3 1.7 %collective-permute-start.7 = (bf16[128,1536]{1,0:T(8,128)(2,1)S(1)}, bf16[128,1536]{1,0:T(8,128)(2,1)S(1)}, u32[]{:S(2)}, u32[]{:S(2)}) collective-permute-start(bf16[128,1536]{1,0:T(8,128)(2,1)S(1)} %get-tuple-element.71.refs_2_), channel_id=1, source_target_pairs={{0,2},{1,3},{2,0},{3,1},{4,6},{5,7},{6,4},{7,5},{8,10},{9,11},{10,... | collective-permute-start | bytes 1179656 | tf_op jit(solution)/shard_map/ppermute | solution.py:314
  21.0 0.0 collective-permute-start.5
  21.0 0.0 collective-permute-done.2.refs_2_
  21.0 0.0 collective-permute-done.3.refs_3_
  21.0 3.7 %shard_map.156 = (bf16[256,1536]{1,0:T(8,128)(2,1)S(1)}, bf16[256,1536]{1,0:T(8,128)(2,1)S(1)}, bf16[256,1536]{1,0:T(8,128)(2,1)S(1)}, bf16[256,1536]{1,0:T(8,12...) custom-call(bf16[2,1024,256]{2,1,0:T(8,128)(2,1)S(1)} %get-tuple-element.66.latent_ref.refs_0_, ...), custom_call_target="tpu_custom_call" | custom-call | flops 1711276032 | bytes 8388608 | tf_op jit(solution)/shard_map/pallas_call | solution.py:353
  24.7 0.6 collective-permute-start.6
  25.2 0.4 collective-permute-start.4
  25.6 5.1 %collective-permute-done.7.refs_6_ = bf16[128,1536]{1,0:T(8,128)(2,1)S(1)} collective-permute-done((bf16[128,1536]{1,0:T(8,128)(2,1)S(1)}, bf16[128,1536]{1,0:T(8,128)(2,1)S(1)}, u32[]{:S(2)}, u32[]{:S(2)}) %collective-permute-start.7) | collective-permute-done | bytes 393248 | tf_op jit(solution)/shard_map/ppermute | solution.py:314
  30.7 0.0 collective-permute-done.5.refs_4_
  30.7 0.0 collective-permute-done.6.refs_5_
  30.7 2.5 %shard_map.157 = (f32[128,1536]{1,0:T(8,128)S(1)}, f32[128,1536]{1,0:T(8,128)S(1)}, f32[1,128]{1,0:T(1,128)S(1)}) custom-call(s32[1]{0:T(128)} %bitcast.1.region_ref.refs_0_, s32[4]{0:T(128)S(1)} %copy-done.8, bf16[128,1536]{1,0:T(8,128)(2,1)S(1)} %get-tuple-element.71.refs_2_, bf16[128,1536]{1,0:T(8,128)(2,1)S(1)} %get-tuple-element.74.refs_3_, ...), custom_call_target="tpu_custom_call" | custom-call | flops 4194304 | bytes 2097152 | tf_op jit(solution)/shard_map/pallas_call | solution.py:370
  33.2 4.5 %collective-permute-done.4.refs_4_ = bf16[128,1536]{1,0:T(8,128)(2,1)S(1)} collective-permute-done((bf16[128,1536]{1,0:T(8,128)(2,1)S(1)}, bf16[128,1536]{1,0:T(8,128)(2,1)S(1)}, u32[]{:S(2)}, u32[]{:S(2)}) %collective-permute-start.4) | collective-permute-done | bytes 393248 | tf_op jit(solution)/shard_map/ppermute | solution.py:314
  37.8 0.0 collective-permute-start.8
  37.8 0.5 collective-permute-start.9
  38.3 1.2 %collective-permute-done.8.refs_5_ = bf16[128,1536]{1,0:T(8,128)(2,1)S(1)} collective-permute-done((bf16[128,1536]{1,0:T(8,128)(2,1)S(1)}, bf16[128,1536]{1,0:T(8,128)(2,1)S(1)}, u32[]{:S(2)}, u32[]{:S(2)}) %collective-permute-start.8) | collective-permute-done | bytes 393248 | tf_op jit(solution)/shard_map/ppermute | solution.py:314
  39.5 0.6 collective-permute-done.9.refs_6_
  40.0 2.1 %shard_map.158 = (bf16[128,1536]{1,0:T(8,128)(2,1)S(1)}, bf16[128,1536]{1,0:T(8,128)(2,1)S(1)}, f32[1,128]{1,0:T(1,128)S(1)}) custom-call(s32[1]{0:T(128)} %bitcast.1.region_ref.refs_0_, s32[4]{0:T(128)S(1)} %copy-done.8, bf16[128,1536]{1,0:T(8,128)(2,1)S(1)} %get-tuple-element.71.refs_2_, bf16[128,1536]{1,0:T(8,128)(2,1)S(1)} %get-tuple-element.74.refs_3_, ...), custom_call_target="tpu_custom_call" | custom-call | flops 4194304 | bytes 2097152 | tf_op jit(solution)/shard_map/pallas_call | solution.py:370
  42.1 2.8 %shard_map.159 = (bf16[256,1536]{1,0:T(8,128)(2,1)S(1)}, bf16[256,1536]{1,0:T(8,128)(2,1)S(1)}, bf16[176,256]{1,0:T(8,128)(2,1)S(1)}, bf16[176,256]{1,0:T(8,128)...) custom-call(s32[1]{0:T(128)} %bitcast.1.region_ref.refs_0_, s32[1]{0:T(128)} %bitcast.rank_ref.refs_1_.refs_0_, ...), custom_call_target="tpu_custom_call" | custom-call | flops 2013265920 | bytes 10485760 | tf_op jit(solution)/shard_map/pallas_call | solution.py:393
  45.0 0.2 collective-permute-start.10
  45.2 0.4 collective-permute-start.11
  45.5 1.4 %shard_map.160 = (bf16[256,1536]{1,0:T(8,128)(2,1)S(1)}, bf16[256,1536]{1,0:T(8,128)(2,1)S(1)}, bf16[2,256,256]{2,1,0:T(8,128)(2,1)S(1)}, bf16[2,256,256]{2,1,0:T(8,128)(2,1)S(1)}) custom-call(bf16[1536,1536]{1,0:T(8,128)(2,1)S(1)} %get-tuple-element.68.refs_1_.refs_0_.table_ref, bf16[256,256]{1,0:T(8,128)(2,1)S(1)} %copy-done.1, ...), custom_call_target="tpu_custom_call" | custom-call | flops 1207959552 | bytes 6291456 | tf_op jit(solution)/shard_map/pallas_call | solution.py:410
  46.9 0.0 collective-permute-done.10.refs_2_
  46.9 0.0 collective-permute-done.11.refs_3_
  47.0 1.6 %collective-permute-start.12 = (bf16[176,256]{1,0:T(8,128)(2,1)S(1)}, bf16[176,256]{1,0:T(8,128)(2,1)S(1)}, u32[]{:S(2)}, u32[]{:S(2)}) collective-permute-start(bf16[176,256]{1,0:T(8,128)(2,1)S(1)} %get-tuple-element.106), channel_id=1, source_target_pairs={{0,2},{1,3},{2,0},{3,1},{4,6},{5,7},{6,4},{7,5},{8,10},{9,11},{10,... | collective-permute-start | bytes 270344 | tf_op jit(solution)/shard_map/ppermute | solution.py:314
  48.6 3.2 %collective-permute-done.12.refs_1_ = bf16[176,256]{1,0:T(8,128)(2,1)S(1)} collective-permute-done((bf16[176,256]{1,0:T(8,128)(2,1)S(1)}, bf16[176,256]{1,0:T(8,128)(2,1)S(1)}, u32[]{:S(2)}, u32[]{:S(2)}) %collective-permute-start.12) | collective-permute-done | bytes 90144 | tf_op jit(solution)/shard_map/ppermute | solution.py:314
  51.8 0.1 collective-permute-start.13
  51.8 4.5 %collective-permute-done.13.refs_1_ = bf16[176,256]{1,0:T(8,128)(2,1)S(1)} collective-permute-done((bf16[176,256]{1,0:T(8,128)(2,1)S(1)}, bf16[176,256]{1,0:T(8,128)(2,1)S(1)}, u32[]{:S(2)}, u32[]{:S(2)}) %collective-permute-start.13) | collective-permute-done | bytes 90144 | tf_op jit(solution)/shard_map/ppermute | solution.py:314
  56.4 0.1 collective-permute-start.14
  56.5 0.8 %collective-permute-start.18 = (bf16[2,256,256]{2,1,0:T(8,128)(2,1)S(1)}, bf16[2,256,256]{2,1,0:T(8,128)(2,1)S(1)}, u32[]{:S(2)}, u32[]{:S(2)}) collective-permute-start(bf16[2,256,256]{2,1,0:T(8,128)(2,1)S(1)} %get-tuple-element.112), channel_id=1, source_target_pairs={{0,4},{4,8},{8,12},{12,0},{1,5},{5,9},{9,13},{13,1},{2,6},{6,10},{... | collective-permute-start | bytes 786440 | tf_op jit(solution)/shard_map/ppermute | solution.py:310
  57.3 3.0 %collective-permute-start.19 = (bf16[2,256,256]{2,1,0:T(8,128)(2,1)S(1)}, bf16[2,256,256]{2,1,0:T(8,128)(2,1)S(1)}, u32[]{:S(2)}, u32[]{:S(2)}) collective-permute-start(bf16[2,256,256]{2,1,0:T(8,128)(2,1)S(1)} %get-tuple-element.113), channel_id=1, source_target_pairs={{0,12},{4,0},{8,4},{12,8},{1,13},{5,1},{9,5},{13,9},{2,14},{6,2},{... | collective-permute-start | bytes 786440 | tf_op jit(solution)/shard_map/ppermute | solution.py:310
  60.3 6.9 %collective-permute-done.14.refs_1_ = bf16[176,256]{1,0:T(8,128)(2,1)S(1)} collective-permute-done((bf16[176,256]{1,0:T(8,128)(2,1)S(1)}, bf16[176,256]{1,0:T(8,128)(2,1)S(1)}, u32[]{:S(2)}, u32[]{:S(2)}) %collective-permute-start.14) | collective-permute-done | bytes 90144 | tf_op jit(solution)/shard_map/ppermute | solution.py:314
  67.3 1.6 %collective-permute-start.16 = (bf16[176,256]{1,0:T(8,128)(2,1)S(1)}, bf16[176,256]{1,0:T(8,128)(2,1)S(1)}, u32[]{:S(2)}, u32[]{:S(2)}) collective-permute-start(bf16[176,256]{1,0:T(8,128)(2,1)S(1)} %shard_map.164.refs_1_), channel_id=1, source_target_pairs={{0,2},{1,3},{2,0},{3,1},{4,6},{5,7},{6,4},{7,5},{8,10},{9,11},{10,... | collective-permute-start | bytes 270344 | tf_op jit(solution)/shard_map/ppermute | solution.py:314
  68.9 0.0 collective-permute-start.15
  68.9 3.0 %collective-permute-done.16.refs_3_ = bf16[176,256]{1,0:T(8,128)(2,1)S(1)} collective-permute-done((bf16[176,256]{1,0:T(8,128)(2,1)S(1)}, bf16[176,256]{1,0:T(8,128)(2,1)S(1)}, u32[]{:S(2)}, u32[]{:S(2)}) %collective-permute-start.16) | collective-permute-done | bytes 90144 | tf_op jit(solution)/shard_map/ppermute | solution.py:314
  71.9 0.0 collective-permute-start.17
  71.9 1.8 %shard_map.165.own_ref = f32[2,1024,256]{2,1,0:T(8,128)S(1)} custom-call(bf16[1536,1536]{1,0:T(8,128)(2,1)S(1)} %get-tuple-element.68.refs_1_.refs_0_.table_ref, bf16[256,1536]{1,0:T(8,128)(2,1)S(1)} %get-tuple-element.110.refs_0_, bf16[256,1536]{1,0:T(8,128)(2,1)S(1)} %get-tuple-element.111.refs_1_), custom_call_target="tpu_custom_call" | custom-call | flops 1610612736 | bytes 6291456 | tf_op jit(solution)/shard_map/pallas_call | solution.py:424
  73.7 0.0 collective-permute-done.18.from_prev_ref
  73.7 0.0 collective-permute-done.19.from_next_ref
  73.7 1.1 %shard_map.166 = bf16[2,1024,256]{2,1,0:T(8,128)(2,1)} custom-call(f32[2,1024,256]{2,1,0:T(8,128)S(1)} %shard_map.165.own_ref, bf16[2,256,256]{2,1,0:T(8,128)(2,1)S(1)} %collective-permute-done.18.from_prev_ref, bf16[2,256,256]{2,1,0:T(8,128)(2,1)S(1)} %collective-permute-done.19.from_next_ref), custom_call_target="tpu_custom_call" | custom-call | flops 1048576 | bytes 3145728 | tf_op jit(solution)/shard_map/pallas_call | solution.py:440
  74.8 0.0 collective-permute-done.15.refs_2_
  74.9 0.0 collective-permute-done.17.refs_4_
  74.9 0.9 %shard_map.167 = (f32[256,256]{1,0:T(8,128)}, f32[1,256]{1,0:T(1,128)}, f32[256,256]{1,0:T(8,128)}, f32[1,256]{1,0:T(1,128)}, f32[256,128]{1,0:T(8,128)}, /*index=5*/f32[1,4]{1,0:T(1,128)}) custom-call(s32[1]{0:T(128)} %bitcast.rank_ref.refs_1_.refs_0_, bf16[176,256]{1,0:T(8,128)(2,1)S(1)} %shard_map.164.refs_1_, ...), custom_call_target="tpu_custom_call" | custom-call | flops 1048576 | bytes 2097152 | tf_op jit(solution)/shard_map/pallas_call | solution.py:454
  (13 shorter events, 0.1 us)
Async XLA Ops:
  0.6 15.7 %copy-start = (bf16[256,256]{1,0:T(8,128)(2,1)S(1)}, bf16[256,256]{1,0:T(8,128)(2,1)}, u32[]{:S(2)}) copy-start(bf16[256,256]{1,0:T(8,128)(2,1)} %refs_2_.1) | copy-start | bytes 393220
  0.6 15.7 %copy-start.1 = (bf16[256,256]{1,0:T(8,128)(2,1)S(1)}, bf16[256,256]{1,0:T(8,128)(2,1)}, u32[]{:S(2)}) copy-start(bf16[256,256]{1,0:T(8,128)(2,1)} %refs_1_.5) | copy-start | bytes 393220
  0.7 1.3 %copy-start.2 = (bf16[2,1024,256]{2,1,0:T(8,128)(2,1)S(1)}, bf16[2,1024,256]{2,1,0:T(8,128)(2,1)}, u32[]{:S(2)}) copy-start(bf16[2,1024,256]{2,1,0:T(8,128)(2,1)} %latent_ref.1) | copy-start | bytes 3145732
  1.9 14.4 %copy-start.3 = (bf16[256,128]{1,0:T(8,128)(2,1)S(1)}, bf16[256,128]{1,0:T(8,128)(2,1)}, u32[]{:S(2)}) copy-start(bf16[256,128]{1,0:T(8,128)(2,1)} %refs_3_.1) | copy-start | bytes 196612
  1.9 14.4 %copy-start.5 = (f32[256]{0:T(256)S(1)}, f32[256]{0:T(256)}, u32[]{:S(2)}) copy-start(f32[256]{0:T(256)} %param.16) | copy-start | bytes 3076
  1.9 14.4 %copy-start.6 = (f32[256]{0:T(256)S(1)}, f32[256]{0:T(256)}, u32[]{:S(2)}) copy-start(f32[256]{0:T(256)} %param.18) | copy-start | bytes 3076
  2.0 14.2 %collective-permute-start = (bf16[256,256]{1,0:T(8,128)(2,1)S(1)}, bf16[256,256]{1,0:T(8,128)(2,1)S(1)}, u32[]{:S(2)}, u32[]{:S(2)}) collective-permute-start(bf16[256,256]{1,0:T(8,128)(2,1)S(1)} %get-tuple-element.69), channel_id=1, source_target_pairs={{0,4},{4,8},{8,12},{12,0},{1,5},{5,9},{9,13},{13,1},{2,6},{6,10},{... | collective-permute-start | bytes 393224 | tf_op jit(solution)/shard_map/ppermute | solution.py:310
  5.1 11.2 %collective-permute-start.1 = (bf16[256,256]{1,0:T(8,128)(2,1)S(1)}, bf16[256,256]{1,0:T(8,128)(2,1)S(1)}, u32[]{:S(2)}, u32[]{:S(2)}) collective-permute-start(bf16[256,256]{1,0:T(8,128)(2,1)S(1)} %get-tuple-element.70), channel_id=1, source_target_pairs={{0,12},{4,0},{8,4},{12,8},{1,13},{5,1},{9,5},{13,9},{2,14},{6,2},{... | collective-permute-start | bytes 393224 | tf_op jit(solution)/shard_map/ppermute | solution.py:310
  7.2 13.8 %collective-permute-start.2 = (bf16[256,256]{1,0:T(8,128)(2,1)S(1)}, bf16[256,256]{1,0:T(8,128)(2,1)S(1)}, u32[]{:S(2)}, u32[]{:S(2)}) collective-permute-start(bf16[256,256]{1,0:T(8,128)(2,1)S(1)} %get-tuple-element.72), channel_id=1, source_target_pairs={{0,4},{4,8},{8,12},{12,0},{1,5},{5,9},{9,13},{13,1},{2,6},{6,10},{... | collective-permute-start | bytes 393224 | tf_op jit(solution)/shard_map/ppermute | solution.py:310
  7.2 13.8 %collective-permute-start.3 = (bf16[256,256]{1,0:T(8,128)(2,1)S(1)}, bf16[256,256]{1,0:T(8,128)(2,1)S(1)}, u32[]{:S(2)}, u32[]{:S(2)}) collective-permute-start(bf16[256,256]{1,0:T(8,128)(2,1)S(1)} %get-tuple-element.73), channel_id=1, source_target_pairs={{0,12},{4,0},{8,4},{12,8},{1,13},{5,1},{9,5},{13,9},{2,14},{6,2},{... | collective-permute-start | bytes 393224 | tf_op jit(solution)/shard_map/ppermute | solution.py:310
  11.0 0.7 copy-start.7
  11.7 0.7 copy-start.9
  12.4 0.7 copy-start.10
  19.2 11.5 %copy-start.4 = (bf16[1536,128]{1,0:T(8,128)(2,1)S(1)}, bf16[1536,128]{1,0:T(8,128)(2,1)}, u32[]{:S(2)}) copy-start(bf16[1536,128]{1,0:T(8,128)(2,1)} %refs_7_.1) | copy-start | bytes 1179652
  19.2 11.5 %copy-start.8 = (s32[4]{0:T(128)S(1)}, s32[4]{0:T(128)}, u32[]{:S(2)}) copy-start(s32[4]{0:T(128)} %refs_1_.4) | copy-start | bytes 52
  19.3 11.4 %collective-permute-start.7 = (bf16[128,1536]{1,0:T(8,128)(2,1)S(1)}, bf16[128,1536]{1,0:T(8,128)(2,1)S(1)}, u32[]{:S(2)}, u32[]{:S(2)}) collective-permute-start(bf16[128,1536]{1,0:T(8,128)(2,1)S(1)} %get-tuple-element.71.refs_2_), channel_id=1, source_target_pairs={{0,2},{1,3},{2,0},{3,1},{4,6},{5,7},{6,4},{7,5},{8,10},{9,11},{10,... | collective-permute-start | bytes 1179656 | tf_op jit(solution)/shard_map/ppermute | solution.py:314
  21.0 9.7 %collective-permute-start.5 = (bf16[128,1536]{1,0:T(8,128)(2,1)S(1)}, bf16[128,1536]{1,0:T(8,128)(2,1)S(1)}, u32[]{:S(2)}, u32[]{:S(2)}) collective-permute-start(bf16[128,1536]{1,0:T(8,128)(2,1)S(1)} %get-tuple-element.71.refs_2_), channel_id=1, source_target_pairs={{0,1},{1,0},{2,3},{3,2},{4,5},{5,4},{6,7},{7,6},{8,9},{9,8},{10,11... | collective-permute-start | bytes 1179656 | tf_op jit(solution)/shard_map/ppermute | solution.py:314
  24.7 6.0 %collective-permute-start.6 = (bf16[128,1536]{1,0:T(8,128)(2,1)S(1)}, bf16[128,1536]{1,0:T(8,128)(2,1)S(1)}, u32[]{:S(2)}, u32[]{:S(2)}) collective-permute-start(bf16[128,1536]{1,0:T(8,128)(2,1)S(1)} %get-tuple-element.74.refs_3_), channel_id=1, source_target_pairs={{0,1},{1,0},{2,3},{3,2},{4,5},{5,4},{6,7},{7,6},{8,9},{9,8},{10,11... | collective-permute-start | bytes 1179656 | tf_op jit(solution)/shard_map/ppermute | solution.py:314
  25.2 12.5 %collective-permute-start.4 = (bf16[128,1536]{1,0:T(8,128)(2,1)S(1)}, bf16[128,1536]{1,0:T(8,128)(2,1)S(1)}, u32[]{:S(2)}, u32[]{:S(2)}) collective-permute-start(bf16[128,1536]{1,0:T(8,128)(2,1)S(1)} %get-tuple-element.74.refs_3_), channel_id=1, source_target_pairs={{0,2},{1,3},{2,0},{3,1},{4,6},{5,7},{6,4},{7,5},{8,10},{9,11},{10,... | collective-permute-start | bytes 1179656 | tf_op jit(solution)/shard_map/ppermute | solution.py:314
  37.8 1.7 %collective-permute-start.8 = (bf16[128,1536]{1,0:T(8,128)(2,1)S(1)}, bf16[128,1536]{1,0:T(8,128)(2,1)S(1)}, u32[]{:S(2)}, u32[]{:S(2)}) collective-permute-start(bf16[128,1536]{1,0:T(8,128)(2,1)S(1)} %collective-permute-done.7.refs_6_), channel_id=1, source_target_pairs={{0,1},{1,0},{2,3},{3,2},{4,5},{5,4},{6,7},{7,6},{8,9},{9,8},{10,11... | collective-permute-start | bytes 1179656 | tf_op jit(solution)/shard_map/ppermute | solution.py:314
  37.8 2.3 %collective-permute-start.9 = (bf16[128,1536]{1,0:T(8,128)(2,1)S(1)}, bf16[128,1536]{1,0:T(8,128)(2,1)S(1)}, u32[]{:S(2)}, u32[]{:S(2)}) collective-permute-start(bf16[128,1536]{1,0:T(8,128)(2,1)S(1)} %collective-permute-done.4.refs_4_), channel_id=1, source_target_pairs={{0,1},{1,0},{2,3},{3,2},{4,5},{5,4},{6,7},{7,6},{8,9},{9,8},{10,11... | collective-permute-start | bytes 1179656 | tf_op jit(solution)/shard_map/ppermute | solution.py:314
  45.0 2.0 %collective-permute-start.10 = (bf16[176,256]{1,0:T(8,128)(2,1)S(1)}, bf16[176,256]{1,0:T(8,128)(2,1)S(1)}, u32[]{:S(2)}, u32[]{:S(2)}) collective-permute-start(bf16[176,256]{1,0:T(8,128)(2,1)S(1)} %get-tuple-element.97), channel_id=1, source_target_pairs={{0,1},{1,0},{2,3},{3,2},{4,5},{5,4},{6,7},{7,6},{8,9},{9,8},{10,11... | collective-permute-start | bytes 270344 | tf_op jit(solution)/shard_map/ppermute | solution.py:314
  45.2 1.8 %collective-permute-start.11 = (bf16[176,256]{1,0:T(8,128)(2,1)S(1)}, bf16[176,256]{1,0:T(8,128)(2,1)S(1)}, u32[]{:S(2)}, u32[]{:S(2)}) collective-permute-start(bf16[176,256]{1,0:T(8,128)(2,1)S(1)} %get-tuple-element.98), channel_id=1, source_target_pairs={{0,1},{1,0},{2,3},{3,2},{4,5},{5,4},{6,7},{7,6},{8,9},{9,8},{10,11... | collective-permute-start | bytes 270344 | tf_op jit(solution)/shard_map/ppermute | solution.py:314
  47.0 4.7 %collective-permute-start.12 = (bf16[176,256]{1,0:T(8,128)(2,1)S(1)}, bf16[176,256]{1,0:T(8,128)(2,1)S(1)}, u32[]{:S(2)}, u32[]{:S(2)}) collective-permute-start(bf16[176,256]{1,0:T(8,128)(2,1)S(1)} %get-tuple-element.106), channel_id=1, source_target_pairs={{0,2},{1,3},{2,0},{3,1},{4,6},{5,7},{6,4},{7,5},{8,10},{9,11},{10,... | collective-permute-start | bytes 270344 | tf_op jit(solution)/shard_map/ppermute | solution.py:314
  51.8 4.6 %collective-permute-start.13 = (bf16[176,256]{1,0:T(8,128)(2,1)S(1)}, bf16[176,256]{1,0:T(8,128)(2,1)S(1)}, u32[]{:S(2)}, u32[]{:S(2)}) collective-permute-start(bf16[176,256]{1,0:T(8,128)(2,1)S(1)} %shard_map.162.refs_0_), channel_id=1, source_target_pairs={{0,4},{4,0},{8,12},{12,8},{1,5},{5,1},{9,13},{13,9},{2,6},{6,2},{1... | collective-permute-start | bytes 270344 | tf_op jit(solution)/shard_map/ppermute | solution.py:314
  56.4 10.9 %collective-permute-start.14 = (bf16[176,256]{1,0:T(8,128)(2,1)S(1)}, bf16[176,256]{1,0:T(8,128)(2,1)S(1)}, u32[]{:S(2)}, u32[]{:S(2)}) collective-permute-start(bf16[176,256]{1,0:T(8,128)(2,1)S(1)} %shard_map.163.refs_0_), channel_id=1, source_target_pairs={{0,8},{4,12},{8,0},{12,4},{1,9},{5,13},{9,1},{13,5},{2,10},{6,14},... | collective-permute-start | bytes 270344 | tf_op jit(solution)/shard_map/ppermute | solution.py:314
  56.5 17.3 %collective-permute-start.18 = (bf16[2,256,256]{2,1,0:T(8,128)(2,1)S(1)}, bf16[2,256,256]{2,1,0:T(8,128)(2,1)S(1)}, u32[]{:S(2)}, u32[]{:S(2)}) collective-permute-start(bf16[2,256,256]{2,1,0:T(8,128)(2,1)S(1)} %get-tuple-element.112), channel_id=1, source_target_pairs={{0,4},{4,8},{8,12},{12,0},{1,5},{5,9},{9,13},{13,1},{2,6},{6,10},{... | collective-permute-start | bytes 786440 | tf_op jit(solution)/shard_map/ppermute | solution.py:310
  57.3 16.5 %collective-permute-start.19 = (bf16[2,256,256]{2,1,0:T(8,128)(2,1)S(1)}, bf16[2,256,256]{2,1,0:T(8,128)(2,1)S(1)}, u32[]{:S(2)}, u32[]{:S(2)}) collective-permute-start(bf16[2,256,256]{2,1,0:T(8,128)(2,1)S(1)} %get-tuple-element.113), channel_id=1, source_target_pairs={{0,12},{4,0},{8,4},{12,8},{1,13},{5,1},{9,5},{13,9},{2,14},{6,2},{... | collective-permute-start | bytes 786440 | tf_op jit(solution)/shard_map/ppermute | solution.py:310
  67.3 4.6 %collective-permute-start.16 = (bf16[176,256]{1,0:T(8,128)(2,1)S(1)}, bf16[176,256]{1,0:T(8,128)(2,1)S(1)}, u32[]{:S(2)}, u32[]{:S(2)}) collective-permute-start(bf16[176,256]{1,0:T(8,128)(2,1)S(1)} %shard_map.164.refs_1_), channel_id=1, source_target_pairs={{0,2},{1,3},{2,0},{3,1},{4,6},{5,7},{6,4},{7,5},{8,10},{9,11},{10,... | collective-permute-start | bytes 270344 | tf_op jit(solution)/shard_map/ppermute | solution.py:314
  68.9 6.0 %collective-permute-start.15 = (bf16[176,256]{1,0:T(8,128)(2,1)S(1)}, bf16[176,256]{1,0:T(8,128)(2,1)S(1)}, u32[]{:S(2)}, u32[]{:S(2)}) collective-permute-start(bf16[176,256]{1,0:T(8,128)(2,1)S(1)} %shard_map.164.refs_1_), channel_id=1, source_target_pairs={{0,1},{1,0},{2,3},{3,2},{4,5},{5,4},{6,7},{7,6},{8,9},{9,8},{10,11... | collective-permute-start | bytes 270344 | tf_op jit(solution)/shard_map/ppermute | solution.py:314
  71.9 3.0 %collective-permute-start.17 = (bf16[176,256]{1,0:T(8,128)(2,1)S(1)}, bf16[176,256]{1,0:T(8,128)(2,1)S(1)}, u32[]{:S(2)}, u32[]{:S(2)}) collective-permute-start(bf16[176,256]{1,0:T(8,128)(2,1)S(1)} %collective-permute-done.16.refs_3_), channel_id=1, source_target_pairs={{0,1},{1,0},{2,3},{3,2},{4,5},{5,4},{6,7},{7,6},{8,9},{9,8},{10,11... | collective-permute-start | bytes 270344 | tf_op jit(solution)/shard_map/ppermute | solution.py:314

commit v6 on v5

--- a/solution.py
+++ b/solution.py
@@ -255,13 +255,13 @@
 
 def edges_kernel(members, table_ref, w_one_ref, *refs):
     d_one_refs, refs = refs[:members], refs[members:]
-    d_mixed_refs, (head_ref, tail_ref) = refs[:members], refs[members:]
     ext = table_ref.shape[0]
     for m in range(members):
+        d_mixed_ref, head_ref, tail_ref = refs[3 * m : 3 * (m + 1)]
         d_mixed = nn_dot(w_one_ref[...], d_one_refs[m][...]).astype(jnp.bfloat16)
-        d_mixed_refs[m][...] = d_mixed
-        head_ref[m] = nt_dot(table_ref[:HALO, :], d_mixed).astype(jnp.bfloat16)
-        tail_ref[m] = nt_dot(table_ref[ext - HALO :, :], d_mixed).astype(jnp.bfloat16)
+        d_mixed_ref[...] = d_mixed
+        head_ref[...] = nt_dot(table_ref[:HALO, :], d_mixed).astype(jnp.bfloat16)
+        tail_ref[...] = nt_dot(table_ref[ext - HALO :, :], d_mixed).astype(jnp.bfloat16)
 
 
 def sum_kernel(count, *refs):
@@ -297,12 +297,14 @@
         own_ref[m] = nt_dot(table_ref[HALO : HALO + nodes, :], d_mixed_refs[m][...])
 
 
-def finish_kernel(own_ref, from_prev_ref, from_next_ref, out_ref):
-    nodes = own_ref.shape[1]
-    from_prev, from_next = from_prev_ref[...].astype(jnp.float32), from_next_ref[...].astype(jnp.float32)
-    out_ref[:, :HALO] = (own_ref[:, :HALO] + from_prev).astype(jnp.bfloat16)
-    out_ref[:, HALO : nodes - HALO] = own_ref[:, HALO : nodes - HALO].astype(jnp.bfloat16)
-    out_ref[:, nodes - HALO :] = (own_ref[:, nodes - HALO :] + from_next).astype(jnp.bfloat16)
+def finish_kernel(own_ref, *refs):
+    *refs, out_ref = refs
+    members, nodes, _ = own_ref.shape
+    for m in range(members):
+        from_next, from_prev = refs[2 * m][...].astype(jnp.float32), refs[2 * m + 1][...].astype(jnp.float32)
+        out_ref[m, :HALO] = (own_ref[m, :HALO] + from_prev).astype(jnp.bfloat16)
+        out_ref[m, HALO : nodes - HALO] = own_ref[m, HALO : nodes - HALO].astype(jnp.bfloat16)
+        out_ref[m, nodes - HALO :] = (own_ref[m, nodes - HALO :] + from_next).astype(jnp.bfloat16)
 
 
 def shifted(shard, axis, by):
@@ -406,19 +408,23 @@
             lambda *refs: sum_kernel(len(ones), *refs), (piece,) * len(ones), flops=MIB, moved=MIB, operands=2 * len(ones)
         )(*ones, *others)
 
-    both = shape((members, HALO, width), bf16)
-    *d_mixed, head, tail = kernel_call(
+    out = kernel_call(
         lambda *refs: edges_kernel(members, *refs),
-        (mixed_shape,) * members + (both, both),
+        (mixed_shape, edge, edge) * members,
         flops=2 * members * slots * width * (hidden + 2 * HALO),
         moved=6 * MIB,
         operands=2 + members,
     )(table, w_one, *d_one)
+    d_mixed, heads, tails = out[::3], out[1::3], out[2::3]
+
+    def returned(m):
+        return [shifted(heads[m], "space", -1), shifted(tails[m], "space", 1)]
+
     bit = 1
     while bit < ranks:
         received = [swapped(sent, "member", bit) for sent in pieces[1::2]]
         if bit == 1:
-            received, head, tail = lax.optimization_barrier((received, head, tail))
+            received, heads, tails = lax.optimization_barrier((received, heads, tails))
         pieces = summed(pieces[::2], received)
         bit = 2 * bit
     own = kernel_call(
@@ -428,28 +434,29 @@
         moved=6 * MIB,
         operands=1 + members,
     )(table, *d_mixed)
+    edges = [block for m in each[:-1] for block in returned(m)]
     (total,) = pieces
     step = 1
     while step < regions:
         (total,) = summed([total], [swapped(total, "space", step)])
         step = 2 * step
         if step == regions // 2:
-            total, head, tail = lax.optimization_barrier((total, head, tail))
-            from_next = shifted(head, "space", -1)
-            from_prev = shifted(tail, "space", 1)
+            total, edges, own, heads, tails = lax.optimization_barrier((total, edges, own, heads, tails))
+            edges = [*edges, *returned(members - 1)]
     latent_grad = kernel_call(
         finish_kernel,
         shape((members, nodes, width), bf16),
         flops=MIB,
         moved=3 * MIB,
-        operands=3,
-    )(own, from_prev, from_next)
+        operands=1 + 2 * members,
+    )(own, *edges)
     totals = {0: total}
     while bit > 1:
         bit = bit // 2
+        if bit == 1:
+            totals[ranks // 2], latent_grad = lax.optimization_barrier((totals[ranks // 2], latent_grad))
         totals.update({i ^ bit: swapped(totals[i], "member", bit) for i in sorted(totals)})
     totals = [totals[i] for i in range(ranks)]
-    totals, latent_grad = lax.optimization_barrier((totals, latent_grad))
     row = shape((1, hidden), f32)
     g_one, g_bone, g_two, g_btwo, g_three, tally = kernel_call(
         lambda *refs: unpack_kernel(1.0 / (OBS_MEAN * members * ranks), *refs),

time: 76.1 us -> 73.7 us (0.968)
  waiting for transfers between devices: 29.1 us -> 27.1 us
    ppermute x14, waiting for transfers between devices: 29 us -> 24.7 us  [swapped(): lax.ppermute(block, axis, [(i, i ^ by) for i in range(lax.axis_size(axis))])]
    ppermute x6 -> x8, waiting for transfers between devices: 0.02 us -> 2.33 us  [shifted(): lax.ppermute(shard, axis, [(i, (i + by) % length) for i in range(length)])]
    ppermute x14, starting transfers between devices: 7 us -> 5.84 us  [swapped(): lax.ppermute(block, axis, [(i, i ^ by) for i in range(lax.axis_size(axis))])]
    ppermute x6 -> x8, starting transfers between devices: 12.9 us -> 13.7 us  [shifted(): lax.ppermute(shard, axis, [(i, (i + by) % length) for i in range(length)])]
  transfers between devices with their start and end apart: 20 -> 22, of which waited for: 8 -> 10; matrix products, arithmetic and copies ran while one was open for 0% -> 0% of each run, Pallas kernels for 22% -> 23%
where the time goes in v6:
time: 73.7 us; the launch traced here: 73.4 us
  waiting for transfers between devices  27.1 us (37%)
  Pallas kernels  22.5 us (31%)
  starting transfers between devices  19.5 us (26%)
  local copies, waits for them, and re-layouts  3.42 us (5%)
  between operations  0.89 us (1%)
    ppermute x14, waiting for transfers between devices, swapped(): lax.ppermute(block, axis, [(i, i ^ by) for i in range(lax.axis_size(axis))])  24.7 us
    ppermute x8, starting transfers between devices, shifted(): lax.ppermute(shard, axis, [(i, (i + by) % length) for i in range(length)])  13.7 us
    pallas_call x2, Pallas kernels, per_device(): kernel_call(lambda *refs: forward_kernel(m, *refs), (mixed_shape,) + (sav...  6.56 us
    ppermute x14, starting transfers between devices, swapped(): lax.ppermute(block, axis, [(i, i ^ by) for i in range(lax.axis_size(axis))])  5.84 us
    pallas_call x2, Pallas kernels, scored(): kernel_call(lambda *refs: score_kernel(members, len(others), members * ra...  4.58 us
    unnamed x22, local copies, waits for them, and re-layouts  3.42 us
    pallas_call x1, Pallas kernels, per_device(): kernel_call(table_kernel, (shape((ext, slots), bf16), shape((width, slots...  3.11 us
    pallas_call x1, Pallas kernels, per_device(): kernel_call(lambda *refs: backward_kernel(members, ranks, *refs), (saved_...  2.84 us
  transfers between devices with their start and end apart: 22, of which 10 were waited for; matrix products, arithmetic and copies ran while one was open for 0% of the time, Pallas kernels for 23%

profile of v6, /device:TPU:0, one launch (start us, length us, event | category | flops | bytes accessed | tf_op | source)
XLA Modules:
  0.0 73.4 jit_solution(5668285258720645030)
XLA Ops:
  0.7 1.3 %copy-done.2 = bf16[2,1024,256]{2,1,0:T(8,128)(2,1)S(1)} copy-done((bf16[2,1024,256]{2,1,0:T(8,128)(2,1)S(1)}, bf16[2,1024,256]{2,1,0:T(8,128)(2,1)}, u32[]{:S(2)}) %copy-start.2) | copy-done | bytes 1048600
  1.9 0.1 shard_map.153
  2.0 3.1 %collective-permute-start = (bf16[256,256]{1,0:T(8,128)(2,1)S(1)}, bf16[256,256]{1,0:T(8,128)(2,1)S(1)}, u32[]{:S(2)}, u32[]{:S(2)}) collective-permute-start(bf16[256,256]{1,0:T(8,128)(2,1)S(1)} %get-tuple-element.73), channel_id=1, source_target_pairs={{0,4},{4,8},{8,12},{12,0},{1,5},{5,9},{9,13},{13,1},{2,6},{6,10},{... | collective-permute-start | bytes 393224 | tf_op jit(solution)/shard_map/ppermute | solution.py:312
  5.1 2.1 %collective-permute-start.1 = (bf16[256,256]{1,0:T(8,128)(2,1)S(1)}, bf16[256,256]{1,0:T(8,128)(2,1)S(1)}, u32[]{:S(2)}, u32[]{:S(2)}) collective-permute-start(bf16[256,256]{1,0:T(8,128)(2,1)S(1)} %get-tuple-element.74), channel_id=1, source_target_pairs={{0,12},{4,0},{8,4},{12,8},{1,13},{5,1},{9,5},{13,9},{2,14},{6,2},{... | collective-permute-start | bytes 393224 | tf_op jit(solution)/shard_map/ppermute | solution.py:312
  7.2 0.0 collective-permute-start.2
  7.2 3.8 %collective-permute-start.3 = (bf16[256,256]{1,0:T(8,128)(2,1)S(1)}, bf16[256,256]{1,0:T(8,128)(2,1)S(1)}, u32[]{:S(2)}, u32[]{:S(2)}) collective-permute-start(bf16[256,256]{1,0:T(8,128)(2,1)S(1)} %get-tuple-element.77), channel_id=1, source_target_pairs={{0,12},{4,0},{8,4},{12,8},{1,13},{5,1},{9,5},{13,9},{2,14},{6,2},{... | collective-permute-start | bytes 393224 | tf_op jit(solution)/shard_map/ppermute | solution.py:312
  11.0 0.7 copy-done.7
  11.7 0.7 %copy-done.9 = s32[4,1536]{1,0:T(4,128)S(1)} copy-done((s32[4,1536]{1,0:T(4,128)S(1)}, s32[4,1536]{1,0:T(4,128)}, u32[]{:S(2)}) %copy-start.9) | copy-done | bytes 24600
  12.4 0.7 %copy-done.10 = f32[4,1536]{1,0:T(4,128)S(1)} copy-done((f32[4,1536]{1,0:T(4,128)S(1)}, f32[4,1536]{1,0:T(4,128)}, u32[]{:S(2)}) %copy-start.10) | copy-done | bytes 24600
  13.2 3.1 %shard_map.154 = (bf16[1536,1536]{1,0:T(8,128)(2,1)S(1)}, f32[256,1536]{1,0:T(8,128)S(1)}) custom-call(s32[1]{0:T(128)} %bitcast.1.region_ref.refs_0_, s32[1]{0:T(128)} %bitcast.rank_ref.refs_1_.refs_0_, s32[4]{0:T(128)S(1)} %copy-done.7, s32[4,1536]{1,0:T(4,128)S(1)} %copy-done.9, f32[4,1536]{1,0:T(4,128)S(1)} %copy-done.10, ...), custom_call_target="tpu_custom_call" | custom-call | flops 805306368 | bytes 12582912 | tf_op jit(solution)/shard_map/pallas_call | solution.py:340
  16.3 0.0 collective-permute-done.refs_2_
  16.3 0.0 collective-permute-done.1.refs_3_
  16.3 0.0 copy-done
  16.3 0.0 copy-done.1
  16.3 0.0 copy-done.3
  16.4 2.9 %shard_map.155 = (bf16[256,1536]{1,0:T(8,128)(2,1)S(1)}, bf16[256,1536]{1,0:T(8,128)(2,1)S(1)}, bf16[256,1536]{1,0:T(8,128)(2,1)S(1)}, bf16[256,1536]{1,0:T(8,12...) custom-call(f32[256,1536]{1,0:T(8,128)S(1)} %get-tuple-element.71.refs_0_, ...), custom_call_target="tpu_custom_call" | custom-call | flops 905969664 | bytes 8388608 | tf_op jit(solution)/shard_map/pallas_call | solution.py:355
  19.2 0.0 copy-start.4
  19.2 0.0 copy-start.8
  19.3 1.7 %collective-permute-start.7 = (bf16[128,1536]{1,0:T(8,128)(2,1)S(1)}, bf16[128,1536]{1,0:T(8,128)(2,1)S(1)}, u32[]{:S(2)}, u32[]{:S(2)}) collective-permute-start(bf16[128,1536]{1,0:T(8,128)(2,1)S(1)} %get-tuple-element.75.refs_2_), channel_id=1, source_target_pairs={{0,2},{1,3},{2,0},{3,1},{4,6},{5,7},{6,4},{7,5},{8,10},{9,11},{10,... | collective-permute-start | bytes 1179656 | tf_op jit(solution)/shard_map/ppermute | solution.py:316
  21.0 0.0 collective-permute-start.5
  21.0 0.0 collective-permute-done.2.refs_2_
  21.0 0.0 collective-permute-done.3.refs_3_
  21.0 3.7 %shard_map.156 = (bf16[256,1536]{1,0:T(8,128)(2,1)S(1)}, bf16[256,1536]{1,0:T(8,128)(2,1)S(1)}, bf16[256,1536]{1,0:T(8,128)(2,1)S(1)}, bf16[256,1536]{1,0:T(8,12...) custom-call(bf16[2,1024,256]{2,1,0:T(8,128)(2,1)S(1)} %get-tuple-element.70.latent_ref.refs_0_, ...), custom_call_target="tpu_custom_call" | custom-call | flops 1711276032 | bytes 8388608 | tf_op jit(solution)/shard_map/pallas_call | solution.py:355
  24.7 0.6 collective-permute-start.6
  25.2 0.4 collective-permute-start.4
  25.6 5.1 %collective-permute-done.7.refs_6_ = bf16[128,1536]{1,0:T(8,128)(2,1)S(1)} collective-permute-done((bf16[128,1536]{1,0:T(8,128)(2,1)S(1)}, bf16[128,1536]{1,0:T(8,128)(2,1)S(1)}, u32[]{:S(2)}, u32[]{:S(2)}) %collective-permute-start.7) | collective-permute-done | bytes 393248 | tf_op jit(solution)/shard_map/ppermute | solution.py:316
  30.7 0.0 collective-permute-done.5.refs_4_
  30.7 0.0 collective-permute-done.6.refs_5_
  30.7 2.5 %shard_map.157 = (f32[128,1536]{1,0:T(8,128)S(1)}, f32[128,1536]{1,0:T(8,128)S(1)}, f32[1,128]{1,0:T(1,128)S(1)}) custom-call(s32[1]{0:T(128)} %bitcast.1.region_ref.refs_0_, s32[4]{0:T(128)S(1)} %copy-done.8, bf16[128,1536]{1,0:T(8,128)(2,1)S(1)} %get-tuple-element.75.refs_2_, bf16[128,1536]{1,0:T(8,128)(2,1)S(1)} %get-tuple-element.78.refs_3_, ...), custom_call_target="tpu_custom_call" | custom-call | flops 4194304 | bytes 2097152 | tf_op jit(solution)/shard_map/pallas_call | solution.py:372
  33.2 4.5 %collective-permute-done.4.refs_4_ = bf16[128,1536]{1,0:T(8,128)(2,1)S(1)} collective-permute-done((bf16[128,1536]{1,0:T(8,128)(2,1)S(1)}, bf16[128,1536]{1,0:T(8,128)(2,1)S(1)}, u32[]{:S(2)}, u32[]{:S(2)}) %collective-permute-start.4) | collective-permute-done | bytes 393248 | tf_op jit(solution)/shard_map/ppermute | solution.py:316
  37.8 0.0 collective-permute-start.8
  37.8 0.5 collective-permute-start.9
  38.3 1.2 %collective-permute-done.8.refs_5_ = bf16[128,1536]{1,0:T(8,128)(2,1)S(1)} collective-permute-done((bf16[128,1536]{1,0:T(8,128)(2,1)S(1)}, bf16[128,1536]{1,0:T(8,128)(2,1)S(1)}, u32[]{:S(2)}, u32[]{:S(2)}) %collective-permute-start.8) | collective-permute-done | bytes 393248 | tf_op jit(solution)/shard_map/ppermute | solution.py:316
  39.5 0.6 collective-permute-done.9.refs_6_
  40.0 2.1 %shard_map.158 = (bf16[128,1536]{1,0:T(8,128)(2,1)S(1)}, bf16[128,1536]{1,0:T(8,128)(2,1)S(1)}, f32[1,128]{1,0:T(1,128)S(1)}) custom-call(s32[1]{0:T(128)} %bitcast.1.region_ref.refs_0_, s32[4]{0:T(128)S(1)} %copy-done.8, bf16[128,1536]{1,0:T(8,128)(2,1)S(1)} %get-tuple-element.75.refs_2_, bf16[128,1536]{1,0:T(8,128)(2,1)S(1)} %get-tuple-element.78.refs_3_, ...), custom_call_target="tpu_custom_call" | custom-call | flops 4194304 | bytes 2097152 | tf_op jit(solution)/shard_map/pallas_call | solution.py:372
  42.1 2.8 %shard_map.159 = (bf16[256,1536]{1,0:T(8,128)(2,1)S(1)}, bf16[256,1536]{1,0:T(8,128)(2,1)S(1)}, bf16[176,256]{1,0:T(8,128)(2,1)S(1)}, bf16[176,256]{1,0:T(8,128)...) custom-call(s32[1]{0:T(128)} %bitcast.1.region_ref.refs_0_, s32[1]{0:T(128)} %bitcast.rank_ref.refs_1_.refs_0_, ...), custom_call_target="tpu_custom_call" | custom-call | flops 2013265920 | bytes 10485760 | tf_op jit(solution)/shard_map/pallas_call | solution.py:395
  45.0 0.2 collective-permute-start.10
  45.2 0.4 collective-permute-start.11
  45.5 1.4 %shard_map.160 = (bf16[256,1536]{1,0:T(8,128)(2,1)S(1)}, bf16[256,256]{1,0:T(8,128)(2,1)S(1)}, bf16[256,256]{1,0:T(8,128)(2,1)S(1)}, bf16[256,1536]{1,0:T(8,128)...) custom-call(bf16[1536,1536]{1,0:T(8,128)(2,1)S(1)} %get-tuple-element.72.refs_1_.refs_0_.table_ref, ...), custom_call_target="tpu_custom_call" | custom-call | flops 1207959552 | bytes 6291456 | tf_op jit(solution)/shard_map/pallas_call | solution.py:411
  46.9 0.0 collective-permute-done.10.refs_2_
  46.9 0.0 collective-permute-done.11.refs_3_
  47.0 1.6 %collective-permute-start.12 = (bf16[176,256]{1,0:T(8,128)(2,1)S(1)}, bf16[176,256]{1,0:T(8,128)(2,1)S(1)}, u32[]{:S(2)}, u32[]{:S(2)}) collective-permute-start(bf16[176,256]{1,0:T(8,128)(2,1)S(1)} %get-tuple-element.112), channel_id=1, source_target_pairs={{0,2},{1,3},{2,0},{3,1},{4,6},{5,7},{6,4},{7,5},{8,10},{9,11},{10,... | collective-permute-start | bytes 270344 | tf_op jit(solution)/shard_map/ppermute | solution.py:316
  48.6 0.3 collective-permute-start.14
  48.8 1.7 %collective-permute-start.15 = (bf16[256,256]{1,0:T(8,128)(2,1)S(1)}, bf16[256,256]{1,0:T(8,128)(2,1)S(1)}, u32[]{:S(2)}, u32[]{:S(2)}) collective-permute-start(bf16[256,256]{1,0:T(8,128)(2,1)S(1)} %get-tuple-element.114), channel_id=1, source_target_pairs={{0,4},{4,8},{8,12},{12,0},{1,5},{5,9},{9,13},{13,1},{2,6},{6,10},{... | collective-permute-start | bytes 393224 | tf_op jit(solution)/shard_map/ppermute | solution.py:312
  50.6 1.1 %collective-permute-done.12.refs_1_ = bf16[176,256]{1,0:T(8,128)(2,1)S(1)} collective-permute-done((bf16[176,256]{1,0:T(8,128)(2,1)S(1)}, bf16[176,256]{1,0:T(8,128)(2,1)S(1)}, u32[]{:S(2)}, u32[]{:S(2)}) %collective-permute-start.12) | collective-permute-done | bytes 90144 | tf_op jit(solution)/shard_map/ppermute | solution.py:316
  51.8 0.1 collective-permute-start.13
  51.8 1.8 %shard_map.164.own_ref = f32[2,1024,256]{2,1,0:T(8,128)S(1)} custom-call(bf16[1536,1536]{1,0:T(8,128)(2,1)S(1)} %get-tuple-element.72.refs_1_.refs_0_.table_ref, bf16[256,1536]{1,0:T(8,128)(2,1)S(1)} %get-tuple-element.115.refs_0_, bf16[256,1536]{1,0:T(8,128)(2,1)S(1)} %get-tuple-element.116.refs_1_), custom_call_target="tpu_custom_call" | custom-call | flops 1610612736 | bytes 6291456 | tf_op jit(solution)/shard_map/pallas_call | solution.py:430
  53.6 4.9 %collective-permute-done.13.refs_1_ = bf16[176,256]{1,0:T(8,128)(2,1)S(1)} collective-permute-done((bf16[176,256]{1,0:T(8,128)(2,1)S(1)}, bf16[176,256]{1,0:T(8,128)(2,1)S(1)}, u32[]{:S(2)}, u32[]{:S(2)}) %collective-permute-start.13) | collective-permute-done | bytes 90144 | tf_op jit(solution)/shard_map/ppermute | solution.py:316
  58.6 0.0 collective-permute-done.14.refs_0_
  58.6 0.0 collective-permute-done.15.refs_1_
  58.6 0.1 collective-permute-start.16
  58.7 2.6 %collective-permute-start.19 = (bf16[256,256]{1,0:T(8,128)(2,1)S(1)}, bf16[256,256]{1,0:T(8,128)(2,1)S(1)}, u32[]{:S(2)}, u32[]{:S(2)}) collective-permute-start(bf16[256,256]{1,0:T(8,128)(2,1)S(1)} %get-tuple-element.123), channel_id=1, source_target_pairs={{0,12},{4,0},{8,4},{12,8},{1,13},{5,1},{9,5},{13,9},{2,14},{6,2},{... | collective-permute-start | bytes 393224 | tf_op jit(solution)/shard_map/ppermute | solution.py:312
  61.3 0.0 collective-permute-start.20
  61.3 5.3 %collective-permute-done.16.refs_1_ = bf16[176,256]{1,0:T(8,128)(2,1)S(1)} collective-permute-done((bf16[176,256]{1,0:T(8,128)(2,1)S(1)}, bf16[176,256]{1,0:T(8,128)(2,1)S(1)}, u32[]{:S(2)}, u32[]{:S(2)}) %collective-permute-start.16) | collective-permute-done | bytes 90144 | tf_op jit(solution)/shard_map/ppermute | solution.py:316
  66.6 0.4 collective-permute-start.18
  67.0 0.0 collective-permute-start.17
  67.0 0.0 collective-permute-done.19.refs_2_
  67.0 2.3 %collective-permute-done.20.refs_3_ = bf16[256,256]{1,0:T(8,128)(2,1)S(1)} collective-permute-done((bf16[256,256]{1,0:T(8,128)(2,1)S(1)}, bf16[256,256]{1,0:T(8,128)(2,1)S(1)}, u32[]{:S(2)}, u32[]{:S(2)}) %collective-permute-start.20) | collective-permute-done | bytes 131104 | tf_op jit(solution)/shard_map/ppermute | solution.py:312
  69.3 1.1 %shard_map.166 = bf16[2,1024,256]{2,1,0:T(8,128)(2,1)} custom-call(f32[2,1024,256]{2,1,0:T(8,128)S(1)} %shard_map.164.own_ref, bf16[256,256]{1,0:T(8,128)(2,1)S(1)} %collective-permute-done.14.refs_0_, bf16[256,256]{1,0:T(8,128)(2,1)S(1)} %collective-permute-done.15.refs_1_, bf16[256,256]{1,0:T(8,128)(2,1)S(1)} %collective-permute-done.19.refs_2_, ...), custom_call_target="tpu_custom_call" | custom-call | flops 1048576 | bytes 3145728 | tf_op jit(solution)/shard_map/pallas_call | solution.py:446
  70.5 0.8 %collective-permute-done.18.refs_3_ = bf16[176,256]{1,0:T(8,128)(2,1)S(1)} collective-permute-done((bf16[176,256]{1,0:T(8,128)(2,1)S(1)}, bf16[176,256]{1,0:T(8,128)(2,1)S(1)}, u32[]{:S(2)}, u32[]{:S(2)}) %collective-permute-start.18) | collective-permute-done | bytes 90144 | tf_op jit(solution)/shard_map/ppermute | solution.py:316
  71.2 0.0 collective-permute-start.21
  71.2 0.0 collective-permute-done.17.refs_2_
  71.2 1.3 %collective-permute-done.21.refs_4_ = bf16[176,256]{1,0:T(8,128)(2,1)S(1)} collective-permute-done((bf16[176,256]{1,0:T(8,128)(2,1)S(1)}, bf16[176,256]{1,0:T(8,128)(2,1)S(1)}, u32[]{:S(2)}, u32[]{:S(2)}) %collective-permute-start.21) | collective-permute-done | bytes 90144 | tf_op jit(solution)/shard_map/ppermute | solution.py:316
  72.5 0.9 %shard_map.167 = (f32[256,256]{1,0:T(8,128)}, f32[1,256]{1,0:T(1,128)}, f32[256,256]{1,0:T(8,128)}, f32[1,256]{1,0:T(1,128)}, f32[256,128]{1,0:T(8,128)}, /*index=5*/f32[1,4]{1,0:T(1,128)}) custom-call(s32[1]{0:T(128)} %bitcast.rank_ref.refs_1_.refs_0_, bf16[176,256]{1,0:T(8,128)(2,1)S(1)} %shard_map.165.refs_1_, ...), custom_call_target="tpu_custom_call" | custom-call | flops 1048576 | bytes 2097152 | tf_op jit(solution)/shard_map/pallas_call | solution.py:461
  (17 shorter events, 0.1 us)
Async XLA Ops:
  0.6 15.7 %copy-start = (bf16[256,256]{1,0:T(8,128)(2,1)S(1)}, bf16[256,256]{1,0:T(8,128)(2,1)}, u32[]{:S(2)}) copy-start(bf16[256,256]{1,0:T(8,128)(2,1)} %refs_2_.1) | copy-start | bytes 393220
  0.6 15.7 %copy-start.1 = (bf16[256,256]{1,0:T(8,128)(2,1)S(1)}, bf16[256,256]{1,0:T(8,128)(2,1)}, u32[]{:S(2)}) copy-start(bf16[256,256]{1,0:T(8,128)(2,1)} %refs_1_.5) | copy-start | bytes 393220
  0.7 1.3 %copy-start.2 = (bf16[2,1024,256]{2,1,0:T(8,128)(2,1)S(1)}, bf16[2,1024,256]{2,1,0:T(8,128)(2,1)}, u32[]{:S(2)}) copy-start(bf16[2,1024,256]{2,1,0:T(8,128)(2,1)} %latent_ref.1) | copy-start | bytes 3145732
  1.9 14.4 %copy-start.3 = (bf16[256,128]{1,0:T(8,128)(2,1)S(1)}, bf16[256,128]{1,0:T(8,128)(2,1)}, u32[]{:S(2)}) copy-start(bf16[256,128]{1,0:T(8,128)(2,1)} %refs_3_.1) | copy-start | bytes 196612
  1.9 14.4 %copy-start.5 = (f32[256]{0:T(256)S(1)}, f32[256]{0:T(256)}, u32[]{:S(2)}) copy-start(f32[256]{0:T(256)} %param.16) | copy-start | bytes 3076
  1.9 14.4 %copy-start.6 = (f32[256]{0:T(256)S(1)}, f32[256]{0:T(256)}, u32[]{:S(2)}) copy-start(f32[256]{0:T(256)} %param.18) | copy-start | bytes 3076
  2.0 14.2 %collective-permute-start = (bf16[256,256]{1,0:T(8,128)(2,1)S(1)}, bf16[256,256]{1,0:T(8,128)(2,1)S(1)}, u32[]{:S(2)}, u32[]{:S(2)}) collective-permute-start(bf16[256,256]{1,0:T(8,128)(2,1)S(1)} %get-tuple-element.73), channel_id=1, source_target_pairs={{0,4},{4,8},{8,12},{12,0},{1,5},{5,9},{9,13},{13,1},{2,6},{6,10},{... | collective-permute-start | bytes 393224 | tf_op jit(solution)/shard_map/ppermute | solution.py:312
  5.1 11.2 %collective-permute-start.1 = (bf16[256,256]{1,0:T(8,128)(2,1)S(1)}, bf16[256,256]{1,0:T(8,128)(2,1)S(1)}, u32[]{:S(2)}, u32[]{:S(2)}) collective-permute-start(bf16[256,256]{1,0:T(8,128)(2,1)S(1)} %get-tuple-element.74), channel_id=1, source_target_pairs={{0,12},{4,0},{8,4},{12,8},{1,13},{5,1},{9,5},{13,9},{2,14},{6,2},{... | collective-permute-start | bytes 393224 | tf_op jit(solution)/shard_map/ppermute | solution.py:312
  7.2 13.8 %collective-permute-start.2 = (bf16[256,256]{1,0:T(8,128)(2,1)S(1)}, bf16[256,256]{1,0:T(8,128)(2,1)S(1)}, u32[]{:S(2)}, u32[]{:S(2)}) collective-permute-start(bf16[256,256]{1,0:T(8,128)(2,1)S(1)} %get-tuple-element.76), channel_id=1, source_target_pairs={{0,4},{4,8},{8,12},{12,0},{1,5},{5,9},{9,13},{13,1},{2,6},{6,10},{... | collective-permute-start | bytes 393224 | tf_op jit(solution)/shard_map/ppermute | solution.py:312
  7.2 13.8 %collective-permute-start.3 = (bf16[256,256]{1,0:T(8,128)(2,1)S(1)}, bf16[256,256]{1,0:T(8,128)(2,1)S(1)}, u32[]{:S(2)}, u32[]{:S(2)}) collective-permute-start(bf16[256,256]{1,0:T(8,128)(2,1)S(1)} %get-tuple-element.77), channel_id=1, source_target_pairs={{0,12},{4,0},{8,4},{12,8},{1,13},{5,1},{9,5},{13,9},{2,14},{6,2},{... | collective-permute-start | bytes 393224 | tf_op jit(solution)/shard_map/ppermute | solution.py:312
  11.0 0.7 copy-start.7
  11.7 0.7 %copy-start.9 = (s32[4,1536]{1,0:T(4,128)S(1)}, s32[4,1536]{1,0:T(4,128)}, u32[]{:S(2)}) copy-start(s32[4,1536]{1,0:T(4,128)} %nbr_ref.1) | copy-start | bytes 73732
  12.4 0.7 %copy-start.10 = (f32[4,1536]{1,0:T(4,128)S(1)}, f32[4,1536]{1,0:T(4,128)}, u32[]{:S(2)}) copy-start(f32[4,1536]{1,0:T(4,128)} %weight_ref.1) | copy-start | bytes 73732
  19.2 11.5 %copy-start.4 = (bf16[1536,128]{1,0:T(8,128)(2,1)S(1)}, bf16[1536,128]{1,0:T(8,128)(2,1)}, u32[]{:S(2)}) copy-start(bf16[1536,128]{1,0:T(8,128)(2,1)} %refs_7_.1) | copy-start | bytes 1179652
  19.2 11.5 %copy-start.8 = (s32[4]{0:T(128)S(1)}, s32[4]{0:T(128)}, u32[]{:S(2)}) copy-start(s32[4]{0:T(128)} %refs_1_.4) | copy-start | bytes 52
  19.3 11.4 %collective-permute-start.7 = (bf16[128,1536]{1,0:T(8,128)(2,1)S(1)}, bf16[128,1536]{1,0:T(8,128)(2,1)S(1)}, u32[]{:S(2)}, u32[]{:S(2)}) collective-permute-start(bf16[128,1536]{1,0:T(8,128)(2,1)S(1)} %get-tuple-element.75.refs_2_), channel_id=1, source_target_pairs={{0,2},{1,3},{2,0},{3,1},{4,6},{5,7},{6,4},{7,5},{8,10},{9,11},{10,... | collective-permute-start | bytes 1179656 | tf_op jit(solution)/shard_map/ppermute | solution.py:316
  21.0 9.7 %collective-permute-start.5 = (bf16[128,1536]{1,0:T(8,128)(2,1)S(1)}, bf16[128,1536]{1,0:T(8,128)(2,1)S(1)}, u32[]{:S(2)}, u32[]{:S(2)}) collective-permute-start(bf16[128,1536]{1,0:T(8,128)(2,1)S(1)} %get-tuple-element.75.refs_2_), channel_id=1, source_target_pairs={{0,1},{1,0},{2,3},{3,2},{4,5},{5,4},{6,7},{7,6},{8,9},{9,8},{10,11... | collective-permute-start | bytes 1179656 | tf_op jit(solution)/shard_map/ppermute | solution.py:316
  24.7 6.0 %collective-permute-start.6 = (bf16[128,1536]{1,0:T(8,128)(2,1)S(1)}, bf16[128,1536]{1,0:T(8,128)(2,1)S(1)}, u32[]{:S(2)}, u32[]{:S(2)}) collective-permute-start(bf16[128,1536]{1,0:T(8,128)(2,1)S(1)} %get-tuple-element.78.refs_3_), channel_id=1, source_target_pairs={{0,1},{1,0},{2,3},{3,2},{4,5},{5,4},{6,7},{7,6},{8,9},{9,8},{10,11... | collective-permute-start | bytes 1179656 | tf_op jit(solution)/shard_map/ppermute | solution.py:316
  25.2 12.5 %collective-permute-start.4 = (bf16[128,1536]{1,0:T(8,128)(2,1)S(1)}, bf16[128,1536]{1,0:T(8,128)(2,1)S(1)}, u32[]{:S(2)}, u32[]{:S(2)}) collective-permute-start(bf16[128,1536]{1,0:T(8,128)(2,1)S(1)} %get-tuple-element.78.refs_3_), channel_id=1, source_target_pairs={{0,2},{1,3},{2,0},{3,1},{4,6},{5,7},{6,4},{7,5},{8,10},{9,11},{10,... | collective-permute-start | bytes 1179656 | tf_op jit(solution)/shard_map/ppermute | solution.py:316
  37.8 1.7 %collective-permute-start.8 = (bf16[128,1536]{1,0:T(8,128)(2,1)S(1)}, bf16[128,1536]{1,0:T(8,128)(2,1)S(1)}, u32[]{:S(2)}, u32[]{:S(2)}) collective-permute-start(bf16[128,1536]{1,0:T(8,128)(2,1)S(1)} %collective-permute-done.7.refs_6_), channel_id=1, source_target_pairs={{0,1},{1,0},{2,3},{3,2},{4,5},{5,4},{6,7},{7,6},{8,9},{9,8},{10,11... | collective-permute-start | bytes 1179656 | tf_op jit(solution)/shard_map/ppermute | solution.py:316
  37.8 2.3 %collective-permute-start.9 = (bf16[128,1536]{1,0:T(8,128)(2,1)S(1)}, bf16[128,1536]{1,0:T(8,128)(2,1)S(1)}, u32[]{:S(2)}, u32[]{:S(2)}) collective-permute-start(bf16[128,1536]{1,0:T(8,128)(2,1)S(1)} %collective-permute-done.4.refs_4_), channel_id=1, source_target_pairs={{0,1},{1,0},{2,3},{3,2},{4,5},{5,4},{6,7},{7,6},{8,9},{9,8},{10,11... | collective-permute-start | bytes 1179656 | tf_op jit(solution)/shard_map/ppermute | solution.py:316
  45.0 2.0 %collective-permute-start.10 = (bf16[176,256]{1,0:T(8,128)(2,1)S(1)}, bf16[176,256]{1,0:T(8,128)(2,1)S(1)}, u32[]{:S(2)}, u32[]{:S(2)}) collective-permute-start(bf16[176,256]{1,0:T(8,128)(2,1)S(1)} %get-tuple-element.101), channel_id=1, source_target_pairs={{0,1},{1,0},{2,3},{3,2},{4,5},{5,4},{6,7},{7,6},{8,9},{9,8},{10,11... | collective-permute-start | bytes 270344 | tf_op jit(solution)/shard_map/ppermute | solution.py:316
  45.2 1.8 %collective-permute-start.11 = (bf16[176,256]{1,0:T(8,128)(2,1)S(1)}, bf16[176,256]{1,0:T(8,128)(2,1)S(1)}, u32[]{:S(2)}, u32[]{:S(2)}) collective-permute-start(bf16[176,256]{1,0:T(8,128)(2,1)S(1)} %get-tuple-element.102), channel_id=1, source_target_pairs={{0,1},{1,0},{2,3},{3,2},{4,5},{5,4},{6,7},{7,6},{8,9},{9,8},{10,11... | collective-permute-start | bytes 270344 | tf_op jit(solution)/shard_map/ppermute | solution.py:316
  47.0 4.7 %collective-permute-start.12 = (bf16[176,256]{1,0:T(8,128)(2,1)S(1)}, bf16[176,256]{1,0:T(8,128)(2,1)S(1)}, u32[]{:S(2)}, u32[]{:S(2)}) collective-permute-start(bf16[176,256]{1,0:T(8,128)(2,1)S(1)} %get-tuple-element.112), channel_id=1, source_target_pairs={{0,2},{1,3},{2,0},{3,1},{4,6},{5,7},{6,4},{7,5},{8,10},{9,11},{10,... | collective-permute-start | bytes 270344 | tf_op jit(solution)/shard_map/ppermute | solution.py:316
  48.6 10.0 %collective-permute-start.14 = (bf16[256,256]{1,0:T(8,128)(2,1)S(1)}, bf16[256,256]{1,0:T(8,128)(2,1)S(1)}, u32[]{:S(2)}, u32[]{:S(2)}) collective-permute-start(bf16[256,256]{1,0:T(8,128)(2,1)S(1)} %get-tuple-element.113), channel_id=1, source_target_pairs={{0,12},{4,0},{8,4},{12,8},{1,13},{5,1},{9,5},{13,9},{2,14},{6,2},{... | collective-permute-start | bytes 393224 | tf_op jit(solution)/shard_map/ppermute | solution.py:312
  48.8 9.8 %collective-permute-start.15 = (bf16[256,256]{1,0:T(8,128)(2,1)S(1)}, bf16[256,256]{1,0:T(8,128)(2,1)S(1)}, u32[]{:S(2)}, u32[]{:S(2)}) collective-permute-start(bf16[256,256]{1,0:T(8,128)(2,1)S(1)} %get-tuple-element.114), channel_id=1, source_target_pairs={{0,4},{4,8},{8,12},{12,0},{1,5},{5,9},{9,13},{13,1},{2,6},{6,10},{... | collective-permute-start | bytes 393224 | tf_op jit(solution)/shard_map/ppermute | solution.py:312
  51.8 6.8 %collective-permute-start.13 = (bf16[176,256]{1,0:T(8,128)(2,1)S(1)}, bf16[176,256]{1,0:T(8,128)(2,1)S(1)}, u32[]{:S(2)}, u32[]{:S(2)}) collective-permute-start(bf16[176,256]{1,0:T(8,128)(2,1)S(1)} %shard_map.162.refs_0_), channel_id=1, source_target_pairs={{0,4},{4,0},{8,12},{12,8},{1,5},{5,1},{9,13},{13,9},{2,6},{6,2},{1... | collective-permute-start | bytes 270344 | tf_op jit(solution)/shard_map/ppermute | solution.py:316
  58.6 8.0 %collective-permute-start.16 = (bf16[176,256]{1,0:T(8,128)(2,1)S(1)}, bf16[176,256]{1,0:T(8,128)(2,1)S(1)}, u32[]{:S(2)}, u32[]{:S(2)}) collective-permute-start(bf16[176,256]{1,0:T(8,128)(2,1)S(1)} %shard_map.163.refs_0_), channel_id=1, source_target_pairs={{0,8},{4,12},{8,0},{12,4},{1,9},{5,13},{9,1},{13,5},{2,10},{6,14},... | collective-permute-start | bytes 270344 | tf_op jit(solution)/shard_map/ppermute | solution.py:316
  58.7 8.4 %collective-permute-start.19 = (bf16[256,256]{1,0:T(8,128)(2,1)S(1)}, bf16[256,256]{1,0:T(8,128)(2,1)S(1)}, u32[]{:S(2)}, u32[]{:S(2)}) collective-permute-start(bf16[256,256]{1,0:T(8,128)(2,1)S(1)} %get-tuple-element.123), channel_id=1, source_target_pairs={{0,12},{4,0},{8,4},{12,8},{1,13},{5,1},{9,5},{13,9},{2,14},{6,2},{... | collective-permute-start | bytes 393224 | tf_op jit(solution)/shard_map/ppermute | solution.py:312
  61.3 8.0 %collective-permute-start.20 = (bf16[256,256]{1,0:T(8,128)(2,1)S(1)}, bf16[256,256]{1,0:T(8,128)(2,1)S(1)}, u32[]{:S(2)}, u32[]{:S(2)}) collective-permute-start(bf16[256,256]{1,0:T(8,128)(2,1)S(1)} %get-tuple-element.124), channel_id=1, source_target_pairs={{0,4},{4,8},{8,12},{12,0},{1,5},{5,9},{9,13},{13,1},{2,6},{6,10},{... | collective-permute-start | bytes 393224 | tf_op jit(solution)/shard_map/ppermute | solution.py:312
  66.6 4.6 %collective-permute-start.18 = (bf16[176,256]{1,0:T(8,128)(2,1)S(1)}, bf16[176,256]{1,0:T(8,128)(2,1)S(1)}, u32[]{:S(2)}, u32[]{:S(2)}) collective-permute-start(bf16[176,256]{1,0:T(8,128)(2,1)S(1)} %shard_map.165.refs_1_), channel_id=1, source_target_pairs={{0,2},{1,3},{2,0},{3,1},{4,6},{5,7},{6,4},{7,5},{8,10},{9,11},{10,... | collective-permute-start | bytes 270344 | tf_op jit(solution)/shard_map/ppermute | solution.py:316
  67.0 4.2 %collective-permute-start.17 = (bf16[176,256]{1,0:T(8,128)(2,1)S(1)}, bf16[176,256]{1,0:T(8,128)(2,1)S(1)}, u32[]{:S(2)}, u32[]{:S(2)}) collective-permute-start(bf16[176,256]{1,0:T(8,128)(2,1)S(1)} %shard_map.165.refs_1_), channel_id=1, source_target_pairs={{0,1},{1,0},{2,3},{3,2},{4,5},{5,4},{6,7},{7,6},{8,9},{9,8},{10,11... | collective-permute-start | bytes 270344 | tf_op jit(solution)/shard_map/ppermute | solution.py:316
  71.2 1.3 %collective-permute-start.21 = (bf16[176,256]{1,0:T(8,128)(2,1)S(1)}, bf16[176,256]{1,0:T(8,128)(2,1)S(1)}, u32[]{:S(2)}, u32[]{:S(2)}) collective-permute-start(bf16[176,256]{1,0:T(8,128)(2,1)S(1)} %collective-permute-done.18.refs_3_), channel_id=1, source_target_pairs={{0,1},{1,0},{2,3},{3,2},{4,5},{5,4},{6,7},{7,6},{8,9},{9,8},{10,11... | collective-permute-start | bytes 270344 | tf_op jit(solution)/shard_map/ppermute | solution.py:316

commit v7 on v6

--- a/solution.py
+++ b/solution.py
@@ -38,7 +38,7 @@
         in_specs=specs + [vmem] * (operands - len(specs)),
         out_specs=jax.tree.map(lambda _: vmem, out_shape),
         scratch_shapes=list(scratch),
-        compiler_params=pltpu.CompilerParams(vmem_limit_bytes=40 * MIB),
+        compiler_params=pltpu.CompilerParams(vmem_limit_bytes=24 * MIB),
         cost_estimate=pl.CostEstimate(flops=flops, bytes_accessed=moved, transcendentals=0),
     )
 
@@ -69,21 +69,20 @@
         lax.broadcasted_iota(jnp.int32, (groups, 16, LANE), 0) * 16
         + lax.broadcasted_iota(jnp.int32, (groups, 16, LANE), 1)
     ).astype(jnp.float32).astype(jnp.bfloat16)
-    for lo, size in split(slots, LANE):
-        wide = [
-            jnp.broadcast_to(joint[k][:, lo : lo + size], (16, size)).astype(jnp.bfloat16)
-            for k in range(K)
-        ]
-        for b in range(ext // BLOCK):
-            tile = jnp.zeros((groups, 16, size), jnp.bfloat16)
-            for k in range(K):
-                near = (nbr[k][:, lo : lo + size] - b * BLOCK).astype(jnp.float32)
-                near = jnp.broadcast_to(near, (16, size)).astype(jnp.bfloat16)
-                tile = jnp.where(rows[:, :, :size] == near[None], wide[k][None], tile)
-            table_ref[b * BLOCK : (b + 1) * BLOCK, lo : lo + size] = tile.reshape(BLOCK, size)
     turned = latent_ref[0].T
-    for lo, size in split(slots, CHUNK):
-        part_ref[:, lo : lo + size] = nn_dot(turned, table_ref[HALO : HALO + nodes, lo : lo + size])
+    for start, length in split(slots, CHUNK):
+        for lo, size in split(length, LANE):
+            lanes = slice(start + lo, start + lo + size)
+            wide = [jnp.broadcast_to(joint[k][:, lanes], (16, size)).astype(jnp.bfloat16) for k in range(K)]
+            for b in range(ext // BLOCK):
+                tile = jnp.zeros((groups, 16, size), jnp.bfloat16)
+                for k in range(K):
+                    near = (nbr[k][:, lanes] - b * BLOCK).astype(jnp.float32)
+                    near = jnp.broadcast_to(near, (16, size)).astype(jnp.bfloat16)
+                    tile = jnp.where(rows[:, :, :size] == near[None], wide[k][None], tile)
+                table_ref[b * BLOCK : (b + 1) * BLOCK, lanes] = tile.reshape(BLOCK, size)
+        lanes = slice(start, start + length)
+        part_ref[:, lanes] = nn_dot(turned, table_ref[HALO : HALO + nodes, lanes])
 
 
 def column(ref):
@@ -204,36 +203,56 @@
     score_ref[...] = old_score + lax.fori_loop(0, slots // LANE, one_tile, jnp.zeros((1, LANE), jnp.float32))
 
 
-def backward_kernel(members, ranks, region_ref, rank_ref, w_two_ref, w_three_ref, score_ref, *refs):
-    saved = [refs[6 * m : 6 * (m + 1)] for m in range(members)]
-    refs = refs[6 * members :]
-    d_one_refs, refs = refs[:members], refs[members:]
-    piece_refs, (d_two_ref, stage_ref) = refs[:ranks], refs[ranks:]
-    w_two, w_three = w_two_ref[...] * 0.5, w_three_ref[...] * 0.5
-    width, slots = saved[0][0].shape
-    hidden = saved[0][1].shape[0]
+def rims_back(table_ref, w_one, d_one, refs):
+    d_mixed_ref, head_ref, tail_ref = refs
+    ext = table_ref.shape[0]
+    d_mixed = nn_dot(w_one, d_one).astype(jnp.bfloat16)
+    d_mixed_ref[...] = d_mixed
+    head_ref[...] = nt_dot(table_ref[:HALO, :], d_mixed).astype(jnp.bfloat16)
+    tail_ref[...] = nt_dot(table_ref[ext - HALO :, :], d_mixed).astype(jnp.bfloat16)
+
+
+def backward_kernel(members, table_ref, w_one_ref, w_two_ref, w_three_ref, *refs):
+    saved = [refs[3 * m : 3 * (m + 1)] for m in range(members)]
+    refs = refs[3 * members :]
+    d_one_refs, d_two_refs, refs = refs[:members], refs[members : 2 * members], refs[2 * members :]
+    bias_one_ref, bias_two_ref, *rim_refs = refs
+    w_one, w_two, w_three = w_one_ref[...], w_two_ref[...] * 0.5, w_three_ref[...] * 0.5
+    hidden, slots = saved[0][0].shape
     bias_one = jnp.zeros((hidden, LANE), jnp.float32)
     bias_two = jnp.zeros((hidden, LANE), jnp.float32)
 
     def lane_sum(values):
         return sum(values[:, lo : lo + LANE] for lo, _ in split(values.shape[1], LANE))
 
-    g_one, g_two, g_three = 0.0, 0.0, 0.0
     for m in range(members):
-        mixed_ref, act_one_ref, slope_one_ref, act_two_ref, slope_two_ref, d_dec_ref = saved[m]
+        slope_one_ref, slope_two_ref, d_dec_ref = saved[m]
         for lo, size in split(slots, CHUNK):
             lanes = slice(lo, lo + size)
             back = nn_dot(w_three, d_dec_ref[:, lanes]) * slope_two_ref[:, lanes].astype(jnp.float32)
             bias_two = bias_two + lane_sum(back)
             d_two = back.astype(jnp.bfloat16)
-            d_two_ref[m, :, lanes] = d_two
+            d_two_refs[m][:, lanes] = d_two
             back = nn_dot(w_two, d_two) * slope_one_ref[:, lanes].astype(jnp.float32)
             bias_one = bias_one + lane_sum(back)
             d_one_refs[m][:, lanes] = back.astype(jnp.bfloat16)
+        if m < members - 1:
+            rims_back(table_ref, w_one, d_one_refs[m][...], rim_refs[3 * m : 3 * (m + 1)])
+    bias_one_ref[...] = bias_one
+    bias_two_ref[...] = bias_two
+
+
+def sums_kernel(members, ranks, region_ref, rank_ref, table_ref, w_one_ref, score_ref, bias_one_ref, bias_two_ref, *refs):
+    saved = [refs[6 * m : 6 * (m + 1)] for m in range(members)]
+    refs = refs[6 * members :]
+    rim_refs, piece_refs, stage_ref = refs[:3], refs[3 : 3 + ranks], refs[3 + ranks]
+    hidden = bias_one_ref.shape[0]
+    half = hidden // 2
+    g_one, g_two, g_three = 0.0, 0.0, 0.0
+    for mixed_ref, act_one_ref, act_two_ref, d_one_ref, d_two_ref, d_dec_ref in saved:
+        g_one = g_one + nt_dot(mixed_ref[...], d_one_ref[...])
+        g_two = g_two + nt_dot(act_one_ref[...], d_two_ref[...])
         g_three = g_three + nt_dot(act_two_ref[...], d_dec_ref[...])
-        g_two = g_two + nt_dot(act_one_ref[...], d_two_ref[m])
-        g_one = g_one + nt_dot(mixed_ref[...], d_one_refs[m][...])
-    half = hidden // 2
     region = lax.broadcasted_iota(jnp.int32, (1, hidden), 1) == region_ref[0]
     tally = jnp.where(region, jnp.sum(score_ref[...]), 0.0)
     high = tally.astype(jnp.bfloat16).astype(jnp.float32)
@@ -241,8 +260,8 @@
         g_one,
         g_two,
         jnp.concatenate([g_three[:half], g_three[half:]], axis=1),
-        jnp.sum(bias_one.T, axis=0, keepdims=True),
-        jnp.sum(bias_two.T, axis=0, keepdims=True),
+        jnp.sum(bias_one_ref[...].T, axis=0, keepdims=True),
+        jnp.sum(bias_two_ref[...].T, axis=0, keepdims=True),
         high,
         tally - high,
     ]
@@ -251,23 +270,12 @@
     stage_ref[...] = jnp.concatenate(parts, axis=0).astype(stage_ref.dtype).reshape(stage_ref.shape)
     for i in range(ranks):
         piece_refs[i][...] = stage_ref[rank_ref[0] ^ i]
-
-
-def edges_kernel(members, table_ref, w_one_ref, *refs):
-    d_one_refs, refs = refs[:members], refs[members:]
-    ext = table_ref.shape[0]
-    for m in range(members):
-        d_mixed_ref, head_ref, tail_ref = refs[3 * m : 3 * (m + 1)]
-        d_mixed = nn_dot(w_one_ref[...], d_one_refs[m][...]).astype(jnp.bfloat16)
-        d_mixed_ref[...] = d_mixed
-        head_ref[...] = nt_dot(table_ref[:HALO, :], d_mixed).astype(jnp.bfloat16)
-        tail_ref[...] = nt_dot(table_ref[ext - HALO :, :], d_mixed).astype(jnp.bfloat16)
-
-
-def sum_kernel(count, *refs):
-    for i in range(count):
-        total = refs[i][...].astype(jnp.float32) + refs[count + i][...].astype(jnp.float32)
-        refs[2 * count + i][...] = total.astype(refs[i].dtype)
+    rims_back(table_ref, w_one_ref[...], saved[-1][3][...], rim_refs)
+
+
+def sum_kernel(*refs):
+    *refs, sum_ref = refs
+    sum_ref[...] = sum(ref[...].astype(jnp.float32) for ref in refs).astype(sum_ref.dtype)
 
 
 def unpack_kernel(scale, rank_ref, *refs):
@@ -330,7 +338,7 @@
 
     edge = shape((HALO, width), bf16)
     *rims, latent = kernel_call(
-        rims_kernel, (edge,) * (2 * members) + (shape(latent.shape, bf16),), flops=MIB, moved=3 * MIB, operands=1
+        rims_kernel, (edge,) * (2 * members) + (shape(latent.shape, bf16),), flops=4 << 30, moved=3 * MIB, operands=1
     )(latent)
     before = [shifted(rims[2 * m], "space", 1) for m in each]
     after = [shifted(rims[2 * m + 1], "space", -1) for m in each]
@@ -389,44 +397,48 @@
 
     rows = -(-(width + hidden + hidden // 2 + 4) // (16 * ranks)) * 16
     piece = shape((rows, hidden), bf16)
-    operands = [region_at, rank_at, w_two, w_three, score]
+    bias = shape((hidden, LANE), f32)
+    one_rims = (mixed_shape, edge, edge)
+    operands = [table, w_one, w_two, w_three]
     for m in each:
-        operands += [*saved[m], d_decoded[m]]
+        operands += [saved[m][2], saved[m][4], d_decoded[m]]
     out = kernel_call(
-        lambda *refs: backward_kernel(members, ranks, *refs),
-        (saved_shape,) * members + (piece,) * ranks,
-        flops=4 * members * slots * dense,
+        lambda *refs: backward_kernel(members, *refs),
+        (saved_shape,) * (2 * members) + (bias, bias) + one_rims * (members - 1),
+        flops=2 * members * slots * dense,
         moved=10 * MIB,
-        scratch=(pltpu.VMEM((members, hidden, slots), bf16), pltpu.VMEM((ranks, rows, hidden), bf16)),
+        operands=len(operands),
+    )(*operands)
+    d_one, d_two, (bias_one, bias_two), rims = (
+        out[:members], out[members : 2 * members], out[2 * members : 2 * members + 2], out[2 * members + 2 :]
+    )
+
+    def returned(head, tail):
+        return [shifted(head, "space", -1), shifted(tail, "space", 1)]
+
+    edges = [block for m in each[:-1] for block in returned(*rims[3 * m + 1 : 3 * m + 3])]
+    operands = [region_at, rank_at, table, w_one, score, bias_one, bias_two]
+    for m in each:
+        mixed, act_one, _, act_two, _ = saved[m]
+        operands += [mixed, act_one, act_two, d_one[m], d_two[m], d_decoded[m]]
+    d_mixed, head, tail, *pieces = kernel_call(
+        lambda *refs: sums_kernel(members, ranks, *refs),
+        one_rims + (piece,) * ranks,
+        flops=2 * members * slots * dense,
+        moved=10 * MIB,
+        scratch=(pltpu.VMEM((ranks, rows, hidden), bf16),),
         smem=2,
         operands=len(operands),
     )(*operands)
-    d_one, pieces = out[:members], out[members:]
-
-    def summed(ones, others):
-        return kernel_call(
-            lambda *refs: sum_kernel(len(ones), *refs), (piece,) * len(ones), flops=MIB, moved=MIB, operands=2 * len(ones)
-        )(*ones, *others)
-
-    out = kernel_call(
-        lambda *refs: edges_kernel(members, *refs),
-        (mixed_shape, edge, edge) * members,
-        flops=2 * members * slots * width * (hidden + 2 * HALO),
-        moved=6 * MIB,
-        operands=2 + members,
-    )(table, w_one, *d_one)
-    d_mixed, heads, tails = out[::3], out[1::3], out[2::3]
-
-    def returned(m):
-        return [shifted(heads[m], "space", -1), shifted(tails[m], "space", 1)]
-
-    bit = 1
-    while bit < ranks:
-        received = [swapped(sent, "member", bit) for sent in pieces[1::2]]
-        if bit == 1:
-            received, heads, tails = lax.optimization_barrier((received, heads, tails))
-        pieces = summed(pieces[::2], received)
-        bit = 2 * bit
+    d_mixed = [*rims[::3], d_mixed]
+
+    def summed(*blocks):
+        return kernel_call(sum_kernel, piece, flops=MIB, moved=MIB, operands=len(blocks))(*blocks)
+
+    pieces = [pieces[0]] + [swapped(pieces[i], "member", i) for i in range(1, ranks)]
+    pieces, edges = lax.optimization_barrier((pieces, edges))
+    total = summed(*pieces)
+    edges = [*edges, *returned(head, tail)]
     own = kernel_call(
         own_kernel,
         shape((members, nodes, width), f32),
@@ -434,15 +446,19 @@
         moved=6 * MIB,
         operands=1 + members,
     )(table, *d_mixed)
-    edges = [block for m in each[:-1] for block in returned(m)]
-    (total,) = pieces
     step = 1
     while step < regions:
-        (total,) = summed([total], [swapped(total, "space", step)])
+        total = summed(total, swapped(total, "space", step))
         step = 2 * step
         if step == regions // 2:
-            total, edges, own, heads, tails = lax.optimization_barrier((total, edges, own, heads, tails))
-            edges = [*edges, *returned(members - 1)]
+            total, own = lax.optimization_barrier((total, own))
+    totals = {0: total}
+    bit = 2
+    while bit < ranks:
+        totals.update({i ^ bit: swapped(totals[i], "member", bit) for i in sorted(totals)})
+        bit = 2 * bit
+    beside = swapped(total, "member", 1)
+    beside, edges = lax.optimization_barrier((beside, edges))
     latent_grad = kernel_call(
         finish_kernel,
         shape((members, nodes, width), bf16),
@@ -450,12 +466,11 @@
         moved=3 * MIB,
         operands=1 + 2 * members,
     )(own, *edges)
-    totals = {0: total}
-    while bit > 1:
-        bit = bit // 2
-        if bit == 1:
-            totals[ranks // 2], latent_grad = lax.optimization_barrier((totals[ranks // 2], latent_grad))
-        totals.update({i ^ bit: swapped(totals[i], "member", bit) for i in sorted(totals)})
+    across = {i: block for i, block in totals.items() if i}
+    across, latent_grad = lax.optimization_barrier((across, latent_grad))
+    totals.update({i ^ 1: swapped(block, "member", 1) for i, block in across.items()})
+    totals.update(across)
+    totals[1] = beside
     totals = [totals[i] for i in range(ranks)]
     row = shape((1, hidden), f32)
     g_one, g_bone, g_two, g_btwo, g_three, tally = kernel_call(

time: 73.7 us -> 74 us (level)
  starting transfers between devices: 19.5 us -> 23.8 us
  local copies, waits for them, and re-layouts: 3.42 us -> 1.27 us
  waiting for transfers between devices: 27.1 us -> 25.2 us
    ppermute x14, starting transfers between devices: 5.84 us -> 10.5 us  [swapped(): lax.ppermute(block, axis, [(i, i ^ by) for i in range(lax.axis_size(axis))])]
    unnamed x22 -> x20, local copies, waits for them, and re-layouts: 3.42 us -> 1.27 us
    ppermute x14, waiting for transfers between devices: 24.7 us -> 23.3 us  [swapped(): lax.ppermute(block, axis, [(i, i ^ by) for i in range(lax.axis_size(axis))])]
    pallas_call x6 -> x5, Pallas kernels: 4.34 us -> 4.56 us  [the longest x1 2.38 us: per_device(): kernel_call(lambda *refs: backward_kernel(members, *refs), (saved_shape,)...]
  transfers between devices with their start and end apart: 22 -> 22, of which waited for: 10 -> 12; matrix products, arithmetic and copies ran while one was open for 0% -> 0% of each run, Pallas kernels for 23% -> 23%
where the time goes in v7:
time: 74 us; the launch traced here: 73.9 us
  waiting for transfers between devices  25.2 us (34%)
  starting transfers between devices  23.8 us (32%)
  Pallas kernels  22.8 us (31%)
  local copies, waits for them, and re-layouts  1.27 us (2%)
  between operations  0.84 us (1%)
    ppermute x14, waiting for transfers between devices, swapped(): lax.ppermute(block, axis, [(i, i ^ by) for i in range(lax.axis_size(axis))])  23.3 us
    ppermute x8, starting transfers between devices, shifted(): lax.ppermute(shard, axis, [(i, (i + by) % length) for i in range(length)])  13.3 us
    ppermute x14, starting transfers between devices, swapped(): lax.ppermute(block, axis, [(i, i ^ by) for i in range(lax.axis_size(axis))])  10.5 us
    pallas_call x2, Pallas kernels, per_device(): kernel_call(lambda *refs: forward_kernel(m, *refs), (mixed_shape,) + (sav...  6.57 us
    pallas_call x2, Pallas kernels, scored(): kernel_call(lambda *refs: score_kernel(members, len(others), members * ra...  4.58 us
    pallas_call x1, Pallas kernels, per_device(): kernel_call(table_kernel, (shape((ext, slots), bf16), shape((width, slots...  3.13 us
    pallas_call x1, Pallas kernels, per_device(): kernel_call(lambda *refs: backward_kernel(members, *refs), (saved_shape,)...  2.38 us
    pallas_call x1, Pallas kernels, per_device(): kernel_call(lambda *refs: sums_kernel(members, ranks, *refs), one_rims +...  2.08 us
  transfers between devices with their start and end apart: 22, of which 12 were waited for; matrix products, arithmetic and copies ran while one was open for 0% of the time, Pallas kernels for 23%

profile of v7, /device:TPU:0, one launch (start us, length us, event | category | flops | bytes accessed | tf_op | source)
XLA Modules:
  0.0 73.9 jit_solution(15473863107276297819)
XLA Ops:
  0.6 0.0 copy-start.6
  0.7 1.2 %copy-done.7 = bf16[2,1024,256]{2,1,0:T(8,128)(2,1)S(1)} copy-done((bf16[2,1024,256]{2,1,0:T(8,128)(2,1)S(1)}, bf16[2,1024,256]{2,1,0:T(8,128)(2,1)}, u32[]{:S(2)}) %copy-start.7) | copy-done | bytes 1048600
  1.9 0.1 shard_map.153
  2.0 0.0 copy-start
  2.0 0.0 copy-start.1
  2.0 0.0 copy-start.2
  2.0 0.0 copy-start.4
  2.0 0.0 copy-start.5
  2.0 3.1 %collective-permute-start = (bf16[256,256]{1,0:T(8,128)(2,1)S(1)}, bf16[256,256]{1,0:T(8,128)(2,1)S(1)}, u32[]{:S(2)}, u32[]{:S(2)}) collective-permute-start(bf16[256,256]{1,0:T(8,128)(2,1)S(1)} %get-tuple-element.76), channel_id=1, source_target_pairs={{0,4},{4,8},{8,12},{12,0},{1,5},{5,9},{9,13},{13,1},{2,6},{6,10},{... | collective-permute-start | bytes 393224 | tf_op jit(solution)/shard_map/ppermute | solution.py:320
  5.1 2.1 %collective-permute-start.1 = (bf16[256,256]{1,0:T(8,128)(2,1)S(1)}, bf16[256,256]{1,0:T(8,128)(2,1)S(1)}, u32[]{:S(2)}, u32[]{:S(2)}) collective-permute-start(bf16[256,256]{1,0:T(8,128)(2,1)S(1)} %get-tuple-element.77), channel_id=1, source_target_pairs={{0,12},{4,0},{8,4},{12,8},{1,13},{5,1},{9,5},{13,9},{2,14},{6,2},{... | collective-permute-start | bytes 393224 | tf_op jit(solution)/shard_map/ppermute | solution.py:320
  7.2 0.0 collective-permute-start.2
  7.2 3.8 %collective-permute-start.3 = (bf16[256,256]{1,0:T(8,128)(2,1)S(1)}, bf16[256,256]{1,0:T(8,128)(2,1)S(1)}, u32[]{:S(2)}, u32[]{:S(2)}) collective-permute-start(bf16[256,256]{1,0:T(8,128)(2,1)S(1)} %get-tuple-element.80), channel_id=1, source_target_pairs={{0,12},{4,0},{8,4},{12,8},{1,13},{5,1},{9,5},{13,9},{2,14},{6,2},{... | collective-permute-start | bytes 393224 | tf_op jit(solution)/shard_map/ppermute | solution.py:320
  11.0 3.1 %shard_map.154 = (bf16[1536,1536]{1,0:T(8,128)(2,1)S(1)}, f32[256,1536]{1,0:T(8,128)S(1)}) custom-call(s32[1]{0:T(128)} %bitcast.1.region_ref.refs_0_, s32[1]{0:T(128)} %bitcast.rank_ref.refs_1_.refs_0_, s32[4]{0:T(128)S(1)} %copy-done.6, s32[4,1536]{1,0:T(4,128)S(1)} %copy-done.8, f32[4,1536]{1,0:T(4,128)S(1)} %copy-done.9, ...), custom_call_target="tpu_custom_call" | custom-call | flops 805306368 | bytes 12582912 | tf_op jit(solution)/shard_map/pallas_call | solution.py:348
  14.2 0.0 collective-permute-done.refs_2_
  14.2 0.6 collective-permute-done.1.refs_3_
  14.9 2.9 %shard_map.155 = (bf16[256,1536]{1,0:T(8,128)(2,1)S(1)}, bf16[256,1536]{1,0:T(8,128)(2,1)S(1)}, bf16[256,1536]{1,0:T(8,128)(2,1)S(1)}, bf16[256,1536]{1,0:T(8,12...) custom-call(f32[256,1536]{1,0:T(8,128)S(1)} %get-tuple-element.75.refs_0_, ...), custom_call_target="tpu_custom_call" | custom-call | flops 905969664 | bytes 8388608 | tf_op jit(solution)/shard_map/pallas_call | solution.py:363
  17.7 0.0 copy-start.3
  17.8 1.8 %collective-permute-start.7 = (bf16[128,1536]{1,0:T(8,128)(2,1)S(1)}, bf16[128,1536]{1,0:T(8,128)(2,1)S(1)}, u32[]{:S(2)}, u32[]{:S(2)}) collective-permute-start(bf16[128,1536]{1,0:T(8,128)(2,1)S(1)} %get-tuple-element.78.refs_2_), channel_id=1, source_target_pairs={{0,2},{1,3},{2,0},{3,1},{4,6},{5,7},{6,4},{7,5},{8,10},{9,11},{10,... | collective-permute-start | bytes 1179656 | tf_op jit(solution)/shard_map/ppermute | solution.py:324
  19.6 0.0 collective-permute-start.5
  19.6 0.0 collective-permute-done.2.refs_2_
  19.6 0.0 collective-permute-done.3.refs_3_
  19.6 3.7 %shard_map.156 = (bf16[256,1536]{1,0:T(8,128)(2,1)S(1)}, bf16[256,1536]{1,0:T(8,128)(2,1)S(1)}, bf16[256,1536]{1,0:T(8,128)(2,1)S(1)}, bf16[256,1536]{1,0:T(8,12...) custom-call(bf16[2,1024,256]{2,1,0:T(8,128)(2,1)S(1)} %get-tuple-element.73.latent_ref.refs_0_, ...), custom_call_target="tpu_custom_call" | custom-call | flops 1711276032 | bytes 8388608 | tf_op jit(solution)/shard_map/pallas_call | solution.py:363
  23.3 0.6 collective-permute-start.6
  23.9 0.2 collective-permute-start.4
  24.1 3.9 %collective-permute-done.7.refs_6_ = bf16[128,1536]{1,0:T(8,128)(2,1)S(1)} collective-permute-done((bf16[128,1536]{1,0:T(8,128)(2,1)S(1)}, bf16[128,1536]{1,0:T(8,128)(2,1)S(1)}, u32[]{:S(2)}, u32[]{:S(2)}) %collective-permute-start.7) | collective-permute-done | bytes 393248 | tf_op jit(solution)/shard_map/ppermute | solution.py:324
  28.0 0.0 collective-permute-done.5.refs_4_
  28.0 0.0 collective-permute-done.6.refs_5_
  28.0 2.5 %shard_map.157 = (f32[128,1536]{1,0:T(8,128)S(1)}, f32[128,1536]{1,0:T(8,128)S(1)}, f32[1,128]{1,0:T(1,128)S(1)}) custom-call(s32[1]{0:T(128)} %bitcast.1.region_ref.refs_0_, s32[4]{0:T(128)S(1)} %copy-done.6, bf16[128,1536]{1,0:T(8,128)(2,1)S(1)} %get-tuple-element.78.refs_2_, bf16[128,1536]{1,0:T(8,128)(2,1)S(1)} %get-tuple-element.81.refs_3_, ...), custom_call_target="tpu_custom_call" | custom-call | flops 4194304 | bytes 2097152 | tf_op jit(solution)/shard_map/pallas_call | solution.py:380
  30.6 5.1 %collective-permute-done.4.refs_4_ = bf16[128,1536]{1,0:T(8,128)(2,1)S(1)} collective-permute-done((bf16[128,1536]{1,0:T(8,128)(2,1)S(1)}, bf16[128,1536]{1,0:T(8,128)(2,1)S(1)}, u32[]{:S(2)}, u32[]{:S(2)}) %collective-permute-start.4) | collective-permute-done | bytes 393248 | tf_op jit(solution)/shard_map/ppermute | solution.py:324
  35.7 0.0 collective-permute-start.8
  35.7 0.5 collective-permute-start.9
  36.2 1.2 %collective-permute-done.8.refs_5_ = bf16[128,1536]{1,0:T(8,128)(2,1)S(1)} collective-permute-done((bf16[128,1536]{1,0:T(8,128)(2,1)S(1)}, bf16[128,1536]{1,0:T(8,128)(2,1)S(1)}, u32[]{:S(2)}, u32[]{:S(2)}) %collective-permute-start.8) | collective-permute-done | bytes 393248 | tf_op jit(solution)/shard_map/ppermute | solution.py:324
  37.4 0.6 collective-permute-done.9.refs_6_
  37.9 2.1 %shard_map.158 = (bf16[128,1536]{1,0:T(8,128)(2,1)S(1)}, bf16[128,1536]{1,0:T(8,128)(2,1)S(1)}, f32[1,128]{1,0:T(1,128)S(1)}) custom-call(s32[1]{0:T(128)} %bitcast.1.region_ref.refs_0_, s32[4]{0:T(128)S(1)} %copy-done.6, bf16[128,1536]{1,0:T(8,128)(2,1)S(1)} %get-tuple-element.78.refs_2_, bf16[128,1536]{1,0:T(8,128)(2,1)S(1)} %get-tuple-element.81.refs_3_, ...), custom_call_target="tpu_custom_call" | custom-call | flops 4194304 | bytes 2097152 | tf_op jit(solution)/shard_map/pallas_call | solution.py:380
  40.0 2.4 %shard_map.159 = (bf16[256,1536]{1,0:T(8,128)(2,1)S(1)}, bf16[256,1536]{1,0:T(8,128)(2,1)S(1)}, bf16[256,1536]{1,0:T(8,128)(2,1)S(1)}, bf16[256,1536]{1,0:T(8,12...) custom-call(bf16[1536,1536]{1,0:T(8,128)(2,1)S(1)} %get-tuple-elemen, ...), custom_call_target="tpu_custom_call" | custom-call | flops 1006632960 | bytes 10485760 | tf_op jit(solution)/shard_map/pallas_call | solution.py:405
  42.4 1.2 %collective-permute-start.13 = (bf16[256,256]{1,0:T(8,128)(2,1)S(1)}, bf16[256,256]{1,0:T(8,128)(2,1)S(1)}, u32[]{:S(2)}, u32[]{:S(2)}) collective-permute-start(bf16[256,256]{1,0:T(8,128)(2,1)S(1)} %get-tuple-element.112), channel_id=1, source_target_pairs={{0,12},{4,0},{8,4},{12,8},{1,13},{5,1},{9,5},{13,9},{2,14},{6,2},{... | collective-permute-start | bytes 393224 | tf_op jit(solution)/shard_map/ppermute | solution.py:320
  43.6 0.9 %collective-permute-start.14 = (bf16[256,256]{1,0:T(8,128)(2,1)S(1)}, bf16[256,256]{1,0:T(8,128)(2,1)S(1)}, u32[]{:S(2)}, u32[]{:S(2)}) collective-permute-start(bf16[256,256]{1,0:T(8,128)(2,1)S(1)} %get-tuple-element.113), channel_id=1, source_target_pairs={{0,4},{4,8},{8,12},{12,0},{1,5},{5,9},{9,13},{13,1},{2,6},{6,10},{... | collective-permute-start | bytes 393224 | tf_op jit(solution)/shard_map/ppermute | solution.py:320
  44.5 2.1 %shard_map.160 = (bf16[256,1536]{1,0:T(8,128)(2,1)S(1)}, bf16[256,256]{1,0:T(8,128)(2,1)S(1)}, bf16[256,256]{1,0:T(8,128)(2,1)S(1)}, bf16[176,256]{1,0:T(8,128)(...) custom-call(s32[1]{0:T(128)} %bitcast.1.region_ref.refs_0_, ...), custom_call_target="tpu_custom_call" | custom-call | flops 1006632960 | bytes 10485760 | tf_op jit(solution)/shard_map/pallas_call | solution.py:424
  46.6 0.1 collective-permute-start.10
  46.6 1.6 %collective-permute-start.11 = (bf16[176,256]{1,0:T(8,128)(2,1)S(1)}, bf16[176,256]{1,0:T(8,128)(2,1)S(1)}, u32[]{:S(2)}, u32[]{:S(2)}) collective-permute-start(bf16[176,256]{1,0:T(8,128)(2,1)S(1)} %get-tuple-element.110), channel_id=1, source_target_pairs={{0,2},{1,3},{2,0},{3,1},{4,6},{5,7},{6,4},{7,5},{8,10},{9,11},{10,... | collective-permute-start | bytes 270344 | tf_op jit(solution)/shard_map/ppermute | solution.py:324
  48.2 0.3 collective-permute-start.12
  48.5 0.0 collective-permute-done.10.refs_1_
  48.5 3.6 %collective-permute-done.11.refs_2_ = bf16[176,256]{1,0:T(8,128)(2,1)S(1)} collective-permute-done((bf16[176,256]{1,0:T(8,128)(2,1)S(1)}, bf16[176,256]{1,0:T(8,128)(2,1)S(1)}, u32[]{:S(2)}, u32[]{:S(2)}) %collective-permute-start.11) | collective-permute-done | bytes 90144 | tf_op jit(solution)/shard_map/ppermute | solution.py:324
  52.1 1.0 %collective-permute-done.12.refs_3_ = bf16[176,256]{1,0:T(8,128)(2,1)S(1)} collective-permute-done((bf16[176,256]{1,0:T(8,128)(2,1)S(1)}, bf16[176,256]{1,0:T(8,128)(2,1)S(1)}, u32[]{:S(2)}, u32[]{:S(2)}) %collective-permute-start.12) | collective-permute-done | bytes 90144 | tf_op jit(solution)/shard_map/ppermute | solution.py:324
  53.2 0.0 collective-permute-done.13.refs_0_
  53.2 0.0 collective-permute-done.14.refs_1_
  53.2 0.1 shard_map.161.refs_0_
  53.2 1.8 %collective-permute-start.15 = (bf16[176,256]{1,0:T(8,128)(2,1)S(1)}, bf16[176,256]{1,0:T(8,128)(2,1)S(1)}, u32[]{:S(2)}, u32[]{:S(2)}) collective-permute-start(bf16[176,256]{1,0:T(8,128)(2,1)S(1)} %shard_map.161.refs_0_), channel_id=1, source_target_pairs={{0,4},{4,0},{8,12},{12,8},{1,5},{5,1},{9,13},{13,9},{2,6},{6,2},{1... | collective-permute-start | bytes 270344 | tf_op jit(solution)/shard_map/ppermute | solution.py:324
  55.1 1.8 %shard_map.163.own_ref = f32[2,1024,256]{2,1,0:T(8,128)S(1)} custom-call(bf16[1536,1536]{1,0:T(8,128)(2,1)S(1)} %get-tuple-element.74.refs_1_.refs_0_.refs_2_.table_ref, bf16[256,1536]{1,0:T(8,128)(2,1)S(1)} %get-tuple-element.118.refs_0_, bf16[256,1536]{1,0:T(8,128)(2,1)S(1)} %get-tuple-element.119.refs_1_), custom_call_target="tpu_custom_call" | custom-call | flops 1610612736 | bytes 6291456 | tf_op jit(solution)/shard_map/pallas_call | solution.py:442
  56.9 1.2 %collective-permute-done.15.refs_1_ = bf16[176,256]{1,0:T(8,128)(2,1)S(1)} collective-permute-done((bf16[176,256]{1,0:T(8,128)(2,1)S(1)}, bf16[176,256]{1,0:T(8,128)(2,1)S(1)}, u32[]{:S(2)}, u32[]{:S(2)}) %collective-permute-start.15) | collective-permute-done | bytes 90144 | tf_op jit(solution)/shard_map/ppermute | solution.py:324
  58.1 1.8 %collective-permute-start.16 = (bf16[176,256]{1,0:T(8,128)(2,1)S(1)}, bf16[176,256]{1,0:T(8,128)(2,1)S(1)}, u32[]{:S(2)}, u32[]{:S(2)}) collective-permute-start(bf16[176,256]{1,0:T(8,128)(2,1)S(1)} %shard_map.162.refs_0_), channel_id=1, source_target_pairs={{0,8},{4,12},{8,0},{12,4},{1,9},{5,13},{9,1},{13,5},{2,10},{6,14},... | collective-permute-start | bytes 270344 | tf_op jit(solution)/shard_map/ppermute | solution.py:324
  59.9 2.2 %collective-permute-start.18 = (bf16[256,256]{1,0:T(8,128)(2,1)S(1)}, bf16[256,256]{1,0:T(8,128)(2,1)S(1)}, u32[]{:S(2)}, u32[]{:S(2)}) collective-permute-start(bf16[256,256]{1,0:T(8,128)(2,1)S(1)} %get-tuple-element.123), channel_id=1, source_target_pairs={{0,12},{4,0},{8,4},{12,8},{1,13},{5,1},{9,5},{13,9},{2,14},{6,2},{... | collective-permute-start | bytes 393224 | tf_op jit(solution)/shard_map/ppermute | solution.py:320
  62.2 0.0 collective-permute-start.19
  62.2 4.4 %collective-permute-done.16.refs_1_ = bf16[176,256]{1,0:T(8,128)(2,1)S(1)} collective-permute-done((bf16[176,256]{1,0:T(8,128)(2,1)S(1)}, bf16[176,256]{1,0:T(8,128)(2,1)S(1)}, u32[]{:S(2)}, u32[]{:S(2)}) %collective-permute-start.16) | collective-permute-done | bytes 90144 | tf_op jit(solution)/shard_map/ppermute | solution.py:324
  66.6 0.1 collective-permute-start.17
  66.7 1.7 %collective-permute-start.20 = (bf16[176,256]{1,0:T(8,128)(2,1)S(1)}, bf16[176,256]{1,0:T(8,128)(2,1)S(1)}, u32[]{:S(2)}, u32[]{:S(2)}) collective-permute-start(bf16[176,256]{1,0:T(8,128)(2,1)S(1)} %shard_map.164.refs_1_), channel_id=1, source_target_pairs={{0,2},{1,3},{2,0},{3,1},{4,6},{5,7},{6,4},{7,5},{8,10},{9,11},{10,... | collective-permute-start | bytes 270344 | tf_op jit(solution)/shard_map/ppermute | solution.py:324
  68.4 0.0 collective-permute-done.18.refs_2_
  68.4 1.2 %collective-permute-done.19.refs_3_ = bf16[256,256]{1,0:T(8,128)(2,1)S(1)} collective-permute-done((bf16[256,256]{1,0:T(8,128)(2,1)S(1)}, bf16[256,256]{1,0:T(8,128)(2,1)S(1)}, u32[]{:S(2)}, u32[]{:S(2)}) %collective-permute-start.19) | collective-permute-done | bytes 131104 | tf_op jit(solution)/shard_map/ppermute | solution.py:320
  69.6 0.0 collective-permute-done.17.refs_2_
  69.6 1.1 %shard_map.165 = bf16[2,1024,256]{2,1,0:T(8,128)(2,1)} custom-call(f32[2,1024,256]{2,1,0:T(8,128)S(1)} %shard_map.163.own_ref, bf16[256,256]{1,0:T(8,128)(2,1)S(1)} %collective-permute-done.13.refs_0_, bf16[256,256]{1,0:T(8,128)(2,1)S(1)} %collective-permute-done.14.refs_1_, bf16[256,256]{1,0:T(8,128)(2,1)S(1)} %collective-permute-done.18.refs_2_, ...), custom_call_target="tpu_custom_call" | custom-call | flops 1048576 | bytes 3145728 | tf_op jit(solution)/shard_map/pallas_call | solution.py:462
  70.7 1.0 %collective-permute-done.20.refs_3_ = bf16[176,256]{1,0:T(8,128)(2,1)S(1)} collective-permute-done((bf16[176,256]{1,0:T(8,128)(2,1)S(1)}, bf16[176,256]{1,0:T(8,128)(2,1)S(1)}, u32[]{:S(2)}, u32[]{:S(2)}) %collective-permute-start.20) | collective-permute-done | bytes 90144 | tf_op jit(solution)/shard_map/ppermute | solution.py:324
  71.7 0.0 collective-permute-start.21
  71.7 1.3 %collective-permute-done.21.refs_4_ = bf16[176,256]{1,0:T(8,128)(2,1)S(1)} collective-permute-done((bf16[176,256]{1,0:T(8,128)(2,1)S(1)}, bf16[176,256]{1,0:T(8,128)(2,1)S(1)}, u32[]{:S(2)}, u32[]{:S(2)}) %collective-permute-start.21) | collective-permute-done | bytes 90144 | tf_op jit(solution)/shard_map/ppermute | solution.py:324
  73.0 0.9 %shard_map.166 = (f32[256,256]{1,0:T(8,128)}, f32[1,256]{1,0:T(1,128)}, f32[256,256]{1,0:T(8,128)}, f32[1,256]{1,0:T(1,128)}, f32[256,128]{1,0:T(8,128)}, /*index=5*/f32[1,4]{1,0:T(1,128)}) custom-call(s32[1]{0:T(128)} %bitcast.rank_ref.refs_1_.refs_0_, bf16[176,256]{1,0:T(8,128)(2,1)S(1)} %shard_map.164.refs_1_, ...), custom_call_target="tpu_custom_call" | custom-call | flops 1048576 | bytes 2097152 | tf_op jit(solution)/shard_map/pallas_call | solution.py:476
  (14 shorter events, 0.1 us)
Async XLA Ops:
  0.6 10.4 %copy-start.6 = (s32[4]{0:T(128)S(1)}, s32[4]{0:T(128)}, u32[]{:S(2)}) copy-start(s32[4]{0:T(128)} %refs_1_.4) | copy-start | bytes 52
  0.6 1.2 %copy-start.7 = (bf16[2,1024,256]{2,1,0:T(8,128)(2,1)S(1)}, bf16[2,1024,256]{2,1,0:T(8,128)(2,1)}, u32[]{:S(2)}) copy-start(bf16[2,1024,256]{2,1,0:T(8,128)(2,1)} %latent_ref.1) | copy-start | bytes 3145732
  1.9 9.2 %copy-start.8 = (s32[4,1536]{1,0:T(4,128)S(1)}, s32[4,1536]{1,0:T(4,128)}, u32[]{:S(2)}) copy-start(s32[4,1536]{1,0:T(4,128)} %nbr_ref.1) | copy-start | bytes 73732
  1.9 9.2 %copy-start.9 = (f32[4,1536]{1,0:T(4,128)S(1)}, f32[4,1536]{1,0:T(4,128)}, u32[]{:S(2)}) copy-start(f32[4,1536]{1,0:T(4,128)} %weight_ref.1) | copy-start | bytes 73732
  2.0 12.8 %copy-start = (bf16[256,256]{1,0:T(8,128)(2,1)S(1)}, bf16[256,256]{1,0:T(8,128)(2,1)}, u32[]{:S(2)}) copy-start(bf16[256,256]{1,0:T(8,128)(2,1)} %refs_3_.3) | copy-start | bytes 393220
  2.0 12.8 %copy-start.1 = (bf16[256,256]{1,0:T(8,128)(2,1)S(1)}, bf16[256,256]{1,0:T(8,128)(2,1)}, u32[]{:S(2)}) copy-start(bf16[256,256]{1,0:T(8,128)(2,1)} %refs_2_.1) | copy-start | bytes 393220
  2.0 12.8 %copy-start.2 = (bf16[256,128]{1,0:T(8,128)(2,1)S(1)}, bf16[256,128]{1,0:T(8,128)(2,1)}, u32[]{:S(2)}) copy-start(bf16[256,128]{1,0:T(8,128)(2,1)} %refs_3_.2) | copy-start | bytes 196612
  2.0 12.8 %copy-start.4 = (f32[256]{0:T(256)S(1)}, f32[256]{0:T(256)}, u32[]{:S(2)}) copy-start(f32[256]{0:T(256)} %param.16) | copy-start | bytes 3076
  2.0 12.8 %copy-start.5 = (f32[256]{0:T(256)S(1)}, f32[256]{0:T(256)}, u32[]{:S(2)}) copy-start(f32[256]{0:T(256)} %param.18) | copy-start | bytes 3076
  2.0 12.1 %collective-permute-start = (bf16[256,256]{1,0:T(8,128)(2,1)S(1)}, bf16[256,256]{1,0:T(8,128)(2,1)S(1)}, u32[]{:S(2)}, u32[]{:S(2)}) collective-permute-start(bf16[256,256]{1,0:T(8,128)(2,1)S(1)} %get-tuple-element.76), channel_id=1, source_target_pairs={{0,4},{4,8},{8,12},{12,0},{1,5},{5,9},{9,13},{13,1},{2,6},{6,10},{... | collective-permute-start | bytes 393224 | tf_op jit(solution)/shard_map/ppermute | solution.py:320
  5.1 9.7 %collective-permute-start.1 = (bf16[256,256]{1,0:T(8,128)(2,1)S(1)}, bf16[256,256]{1,0:T(8,128)(2,1)S(1)}, u32[]{:S(2)}, u32[]{:S(2)}) collective-permute-start(bf16[256,256]{1,0:T(8,128)(2,1)S(1)} %get-tuple-element.77), channel_id=1, source_target_pairs={{0,12},{4,0},{8,4},{12,8},{1,13},{5,1},{9,5},{13,9},{2,14},{6,2},{... | collective-permute-start | bytes 393224 | tf_op jit(solution)/shard_map/ppermute | solution.py:320
  7.2 12.4 %collective-permute-start.2 = (bf16[256,256]{1,0:T(8,128)(2,1)S(1)}, bf16[256,256]{1,0:T(8,128)(2,1)S(1)}, u32[]{:S(2)}, u32[]{:S(2)}) collective-permute-start(bf16[256,256]{1,0:T(8,128)(2,1)S(1)} %get-tuple-element.79), channel_id=1, source_target_pairs={{0,4},{4,8},{8,12},{12,0},{1,5},{5,9},{9,13},{13,1},{2,6},{6,10},{... | collective-permute-start | bytes 393224 | tf_op jit(solution)/shard_map/ppermute | solution.py:320
  7.2 12.4 %collective-permute-start.3 = (bf16[256,256]{1,0:T(8,128)(2,1)S(1)}, bf16[256,256]{1,0:T(8,128)(2,1)S(1)}, u32[]{:S(2)}, u32[]{:S(2)}) collective-permute-start(bf16[256,256]{1,0:T(8,128)(2,1)S(1)} %get-tuple-element.80), channel_id=1, source_target_pairs={{0,12},{4,0},{8,4},{12,8},{1,13},{5,1},{9,5},{13,9},{2,14},{6,2},{... | collective-permute-start | bytes 393224 | tf_op jit(solution)/shard_map/ppermute | solution.py:320
  17.7 10.3 %copy-start.3 = (bf16[1536,128]{1,0:T(8,128)(2,1)S(1)}, bf16[1536,128]{1,0:T(8,128)(2,1)}, u32[]{:S(2)}) copy-start(bf16[1536,128]{1,0:T(8,128)(2,1)} %refs_7_.1) | copy-start | bytes 1179652
  17.8 10.3 %collective-permute-start.7 = (bf16[128,1536]{1,0:T(8,128)(2,1)S(1)}, bf16[128,1536]{1,0:T(8,128)(2,1)S(1)}, u32[]{:S(2)}, u32[]{:S(2)}) collective-permute-start(bf16[128,1536]{1,0:T(8,128)(2,1)S(1)} %get-tuple-element.78.refs_2_), channel_id=1, source_target_pairs={{0,2},{1,3},{2,0},{3,1},{4,6},{5,7},{6,4},{7,5},{8,10},{9,11},{10,... | collective-permute-start | bytes 1179656 | tf_op jit(solution)/shard_map/ppermute | solution.py:324
  19.6 8.4 %collective-permute-start.5 = (bf16[128,1536]{1,0:T(8,128)(2,1)S(1)}, bf16[128,1536]{1,0:T(8,128)(2,1)S(1)}, u32[]{:S(2)}, u32[]{:S(2)}) collective-permute-start(bf16[128,1536]{1,0:T(8,128)(2,1)S(1)} %get-tuple-element.78.refs_2_), channel_id=1, source_target_pairs={{0,1},{1,0},{2,3},{3,2},{4,5},{5,4},{6,7},{7,6},{8,9},{9,8},{10,11... | collective-permute-start | bytes 1179656 | tf_op jit(solution)/shard_map/ppermute | solution.py:324
  23.3 4.7 %collective-permute-start.6 = (bf16[128,1536]{1,0:T(8,128)(2,1)S(1)}, bf16[128,1536]{1,0:T(8,128)(2,1)S(1)}, u32[]{:S(2)}, u32[]{:S(2)}) collective-permute-start(bf16[128,1536]{1,0:T(8,128)(2,1)S(1)} %get-tuple-element.81.refs_3_), channel_id=1, source_target_pairs={{0,1},{1,0},{2,3},{3,2},{4,5},{5,4},{6,7},{7,6},{8,9},{9,8},{10,11... | collective-permute-start | bytes 1179656 | tf_op jit(solution)/shard_map/ppermute | solution.py:324
  23.9 11.8 %collective-permute-start.4 = (bf16[128,1536]{1,0:T(8,128)(2,1)S(1)}, bf16[128,1536]{1,0:T(8,128)(2,1)S(1)}, u32[]{:S(2)}, u32[]{:S(2)}) collective-permute-start(bf16[128,1536]{1,0:T(8,128)(2,1)S(1)} %get-tuple-element.81.refs_3_), channel_id=1, source_target_pairs={{0,2},{1,3},{2,0},{3,1},{4,6},{5,7},{6,4},{7,5},{8,10},{9,11},{10,... | collective-permute-start | bytes 1179656 | tf_op jit(solution)/shard_map/ppermute | solution.py:324
  35.7 1.7 %collective-permute-start.8 = (bf16[128,1536]{1,0:T(8,128)(2,1)S(1)}, bf16[128,1536]{1,0:T(8,128)(2,1)S(1)}, u32[]{:S(2)}, u32[]{:S(2)}) collective-permute-start(bf16[128,1536]{1,0:T(8,128)(2,1)S(1)} %collective-permute-done.7.refs_6_), channel_id=1, source_target_pairs={{0,1},{1,0},{2,3},{3,2},{4,5},{5,4},{6,7},{7,6},{8,9},{9,8},{10,11... | collective-permute-start | bytes 1179656 | tf_op jit(solution)/shard_map/ppermute | solution.py:324
  35.7 2.3 %collective-permute-start.9 = (bf16[128,1536]{1,0:T(8,128)(2,1)S(1)}, bf16[128,1536]{1,0:T(8,128)(2,1)S(1)}, u32[]{:S(2)}, u32[]{:S(2)}) collective-permute-start(bf16[128,1536]{1,0:T(8,128)(2,1)S(1)} %collective-permute-done.4.refs_4_), channel_id=1, source_target_pairs={{0,1},{1,0},{2,3},{3,2},{4,5},{5,4},{6,7},{7,6},{8,9},{9,8},{10,11... | collective-permute-start | bytes 1179656 | tf_op jit(solution)/shard_map/ppermute | solution.py:324
  42.4 10.8 %collective-permute-start.13 = (bf16[256,256]{1,0:T(8,128)(2,1)S(1)}, bf16[256,256]{1,0:T(8,128)(2,1)S(1)}, u32[]{:S(2)}, u32[]{:S(2)}) collective-permute-start(bf16[256,256]{1,0:T(8,128)(2,1)S(1)} %get-tuple-element.112), channel_id=1, source_target_pairs={{0,12},{4,0},{8,4},{12,8},{1,13},{5,1},{9,5},{13,9},{2,14},{6,2},{... | collective-permute-start | bytes 393224 | tf_op jit(solution)/shard_map/ppermute | solution.py:320
  43.6 9.6 %collective-permute-start.14 = (bf16[256,256]{1,0:T(8,128)(2,1)S(1)}, bf16[256,256]{1,0:T(8,128)(2,1)S(1)}, u32[]{:S(2)}, u32[]{:S(2)}) collective-permute-start(bf16[256,256]{1,0:T(8,128)(2,1)S(1)} %get-tuple-element.113), channel_id=1, source_target_pairs={{0,4},{4,8},{8,12},{12,0},{1,5},{5,9},{9,13},{13,1},{2,6},{6,10},{... | collective-permute-start | bytes 393224 | tf_op jit(solution)/shard_map/ppermute | solution.py:320
  46.6 1.9 %collective-permute-start.10 = (bf16[176,256]{1,0:T(8,128)(2,1)S(1)}, bf16[176,256]{1,0:T(8,128)(2,1)S(1)}, u32[]{:S(2)}, u32[]{:S(2)}) collective-permute-start(bf16[176,256]{1,0:T(8,128)(2,1)S(1)} %get-tuple-element.109), channel_id=1, source_target_pairs={{0,1},{1,0},{2,3},{3,2},{4,5},{5,4},{6,7},{7,6},{8,9},{9,8},{10,11... | collective-permute-start | bytes 270344 | tf_op jit(solution)/shard_map/ppermute | solution.py:324
  46.6 5.5 %collective-permute-start.11 = (bf16[176,256]{1,0:T(8,128)(2,1)S(1)}, bf16[176,256]{1,0:T(8,128)(2,1)S(1)}, u32[]{:S(2)}, u32[]{:S(2)}) collective-permute-start(bf16[176,256]{1,0:T(8,128)(2,1)S(1)} %get-tuple-element.110), channel_id=1, source_target_pairs={{0,2},{1,3},{2,0},{3,1},{4,6},{5,7},{6,4},{7,5},{8,10},{9,11},{10,... | collective-permute-start | bytes 270344 | tf_op jit(solution)/shard_map/ppermute | solution.py:324
  48.2 4.9 %collective-permute-start.12 = (bf16[176,256]{1,0:T(8,128)(2,1)S(1)}, bf16[176,256]{1,0:T(8,128)(2,1)S(1)}, u32[]{:S(2)}, u32[]{:S(2)}) collective-permute-start(bf16[176,256]{1,0:T(8,128)(2,1)S(1)} %get-tuple-element.111), channel_id=1, source_target_pairs={{0,3},{1,2},{2,1},{3,0},{4,7},{5,6},{6,5},{7,4},{8,11},{9,10},{10,... | collective-permute-start | bytes 270344 | tf_op jit(solution)/shard_map/ppermute | solution.py:324
  53.2 4.9 %collective-permute-start.15 = (bf16[176,256]{1,0:T(8,128)(2,1)S(1)}, bf16[176,256]{1,0:T(8,128)(2,1)S(1)}, u32[]{:S(2)}, u32[]{:S(2)}) collective-permute-start(bf16[176,256]{1,0:T(8,128)(2,1)S(1)} %shard_map.161.refs_0_), channel_id=1, source_target_pairs={{0,4},{4,0},{8,12},{12,8},{1,5},{5,1},{9,13},{13,9},{2,6},{6,2},{1... | collective-permute-start | bytes 270344 | tf_op jit(solution)/shard_map/ppermute | solution.py:324
  58.1 8.5 %collective-permute-start.16 = (bf16[176,256]{1,0:T(8,128)(2,1)S(1)}, bf16[176,256]{1,0:T(8,128)(2,1)S(1)}, u32[]{:S(2)}, u32[]{:S(2)}) collective-permute-start(bf16[176,256]{1,0:T(8,128)(2,1)S(1)} %shard_map.162.refs_0_), channel_id=1, source_target_pairs={{0,8},{4,12},{8,0},{12,4},{1,9},{5,13},{9,1},{13,5},{2,10},{6,14},... | collective-permute-start | bytes 270344 | tf_op jit(solution)/shard_map/ppermute | solution.py:324
  59.9 8.5 %collective-permute-start.18 = (bf16[256,256]{1,0:T(8,128)(2,1)S(1)}, bf16[256,256]{1,0:T(8,128)(2,1)S(1)}, u32[]{:S(2)}, u32[]{:S(2)}) collective-permute-start(bf16[256,256]{1,0:T(8,128)(2,1)S(1)} %get-tuple-element.123), channel_id=1, source_target_pairs={{0,12},{4,0},{8,4},{12,8},{1,13},{5,1},{9,5},{13,9},{2,14},{6,2},{... | collective-permute-start | bytes 393224 | tf_op jit(solution)/shard_map/ppermute | solution.py:320
  62.2 7.5 %collective-permute-start.19 = (bf16[256,256]{1,0:T(8,128)(2,1)S(1)}, bf16[256,256]{1,0:T(8,128)(2,1)S(1)}, u32[]{:S(2)}, u32[]{:S(2)}) collective-permute-start(bf16[256,256]{1,0:T(8,128)(2,1)S(1)} %get-tuple-element.124), channel_id=1, source_target_pairs={{0,4},{4,8},{8,12},{12,0},{1,5},{5,9},{9,13},{13,1},{2,6},{6,10},{... | collective-permute-start | bytes 393224 | tf_op jit(solution)/shard_map/ppermute | solution.py:320
  66.6 3.0 %collective-permute-start.17 = (bf16[176,256]{1,0:T(8,128)(2,1)S(1)}, bf16[176,256]{1,0:T(8,128)(2,1)S(1)}, u32[]{:S(2)}, u32[]{:S(2)}) collective-permute-start(bf16[176,256]{1,0:T(8,128)(2,1)S(1)} %shard_map.164.refs_1_), channel_id=1, source_target_pairs={{0,1},{1,0},{2,3},{3,2},{4,5},{5,4},{6,7},{7,6},{8,9},{9,8},{10,11... | collective-permute-start | bytes 270344 | tf_op jit(solution)/shard_map/ppermute | solution.py:324
  66.7 5.0 %collective-permute-start.20 = (bf16[176,256]{1,0:T(8,128)(2,1)S(1)}, bf16[176,256]{1,0:T(8,128)(2,1)S(1)}, u32[]{:S(2)}, u32[]{:S(2)}) collective-permute-start(bf16[176,256]{1,0:T(8,128)(2,1)S(1)} %shard_map.164.refs_1_), channel_id=1, source_target_pairs={{0,2},{1,3},{2,0},{3,1},{4,6},{5,7},{6,4},{7,5},{8,10},{9,11},{10,... | collective-permute-start | bytes 270344 | tf_op jit(solution)/shard_map/ppermute | solution.py:324
  71.7 1.3 %collective-permute-start.21 = (bf16[176,256]{1,0:T(8,128)(2,1)S(1)}, bf16[176,256]{1,0:T(8,128)(2,1)S(1)}, u32[]{:S(2)}, u32[]{:S(2)}) collective-permute-start(bf16[176,256]{1,0:T(8,128)(2,1)S(1)} %collective-permute-done.20.refs_3_), channel_id=1, source_target_pairs={{0,1},{1,0},{2,3},{3,2},{4,5},{5,4},{6,7},{7,6},{8,9},{9,8},{10,11... | collective-permute-start | bytes 270344 | tf_op jit(solution)/shard_map/ppermute | solution.py:324

commit v8 on v7

--- a/solution.py
+++ b/solution.py
@@ -203,22 +203,14 @@
     score_ref[...] = old_score + lax.fori_loop(0, slots // LANE, one_tile, jnp.zeros((1, LANE), jnp.float32))
 
 
-def rims_back(table_ref, w_one, d_one, refs):
-    d_mixed_ref, head_ref, tail_ref = refs
-    ext = table_ref.shape[0]
-    d_mixed = nn_dot(w_one, d_one).astype(jnp.bfloat16)
-    d_mixed_ref[...] = d_mixed
-    head_ref[...] = nt_dot(table_ref[:HALO, :], d_mixed).astype(jnp.bfloat16)
-    tail_ref[...] = nt_dot(table_ref[ext - HALO :, :], d_mixed).astype(jnp.bfloat16)
-
-
 def backward_kernel(members, table_ref, w_one_ref, w_two_ref, w_three_ref, *refs):
     saved = [refs[3 * m : 3 * (m + 1)] for m in range(members)]
     refs = refs[3 * members :]
-    d_one_refs, d_two_refs, refs = refs[:members], refs[members : 2 * members], refs[2 * members :]
-    bias_one_ref, bias_two_ref, *rim_refs = refs
+    d_one_refs, d_two_refs, d_mixed_refs = (refs[i * members : (i + 1) * members] for i in range(3))
+    bias_one_ref, bias_two_ref, head_ref, tail_ref = refs[3 * members :]
     w_one, w_two, w_three = w_one_ref[...], w_two_ref[...] * 0.5, w_three_ref[...] * 0.5
     hidden, slots = saved[0][0].shape
+    ext = table_ref.shape[0]
     bias_one = jnp.zeros((hidden, LANE), jnp.float32)
     bias_two = jnp.zeros((hidden, LANE), jnp.float32)
 
@@ -235,17 +227,18 @@
             d_two_refs[m][:, lanes] = d_two
             back = nn_dot(w_two, d_two) * slope_one_ref[:, lanes].astype(jnp.float32)
             bias_one = bias_one + lane_sum(back)
-            d_one_refs[m][:, lanes] = back.astype(jnp.bfloat16)
-        if m < members - 1:
-            rims_back(table_ref, w_one, d_one_refs[m][...], rim_refs[3 * m : 3 * (m + 1)])
+            d_one = back.astype(jnp.bfloat16)
+            d_one_refs[m][:, lanes] = d_one
+            d_mixed_refs[m][:, lanes] = nn_dot(w_one, d_one).astype(jnp.bfloat16)
+        head_ref[m] = nt_dot(table_ref[:HALO, :], d_mixed_refs[m][...]).astype(jnp.bfloat16)
+        tail_ref[m] = nt_dot(table_ref[ext - HALO :, :], d_mixed_refs[m][...]).astype(jnp.bfloat16)
     bias_one_ref[...] = bias_one
     bias_two_ref[...] = bias_two
 
 
-def sums_kernel(members, ranks, region_ref, rank_ref, table_ref, w_one_ref, score_ref, bias_one_ref, bias_two_ref, *refs):
+def sums_kernel(members, ranks, region_ref, rank_ref, score_ref, bias_one_ref, bias_two_ref, *refs):
     saved = [refs[6 * m : 6 * (m + 1)] for m in range(members)]
-    refs = refs[6 * members :]
-    rim_refs, piece_refs, stage_ref = refs[:3], refs[3 : 3 + ranks], refs[3 + ranks]
+    *piece_refs, stage_ref = refs[6 * members :]
     hidden = bias_one_ref.shape[0]
     half = hidden // 2
     g_one, g_two, g_three = 0.0, 0.0, 0.0
@@ -270,12 +263,13 @@
     stage_ref[...] = jnp.concatenate(parts, axis=0).astype(stage_ref.dtype).reshape(stage_ref.shape)
     for i in range(ranks):
         piece_refs[i][...] = stage_ref[rank_ref[0] ^ i]
-    rims_back(table_ref, w_one_ref[...], saved[-1][3][...], rim_refs)
 
 
 def sum_kernel(*refs):
-    *refs, sum_ref = refs
-    sum_ref[...] = sum(ref[...].astype(jnp.float32) for ref in refs).astype(sum_ref.dtype)
+    count = len(refs) // 3
+    for i in range(count):
+        total = refs[i][...].astype(jnp.float32) + refs[count + i][...].astype(jnp.float32)
+        refs[2 * count + i][...] = total.astype(refs[i].dtype)
 
 
 def unpack_kernel(scale, rank_ref, *refs):
@@ -305,14 +299,12 @@
         own_ref[m] = nt_dot(table_ref[HALO : HALO + nodes, :], d_mixed_refs[m][...])
 
 
-def finish_kernel(own_ref, *refs):
-    *refs, out_ref = refs
-    members, nodes, _ = own_ref.shape
-    for m in range(members):
-        from_next, from_prev = refs[2 * m][...].astype(jnp.float32), refs[2 * m + 1][...].astype(jnp.float32)
-        out_ref[m, :HALO] = (own_ref[m, :HALO] + from_prev).astype(jnp.bfloat16)
-        out_ref[m, HALO : nodes - HALO] = own_ref[m, HALO : nodes - HALO].astype(jnp.bfloat16)
-        out_ref[m, nodes - HALO :] = (own_ref[m, nodes - HALO :] + from_next).astype(jnp.bfloat16)
+def finish_kernel(own_ref, from_next_ref, from_prev_ref, out_ref):
+    nodes = own_ref.shape[1]
+    from_next, from_prev = from_next_ref[...].astype(jnp.float32), from_prev_ref[...].astype(jnp.float32)
+    out_ref[:, :HALO] = (own_ref[:, :HALO] + from_prev).astype(jnp.bfloat16)
+    out_ref[:, HALO : nodes - HALO] = own_ref[:, HALO : nodes - HALO].astype(jnp.bfloat16)
+    out_ref[:, nodes - HALO :] = (own_ref[:, nodes - HALO :] + from_next).astype(jnp.bfloat16)
 
 
 def shifted(shard, axis, by):
@@ -398,47 +390,48 @@
     rows = -(-(width + hidden + hidden // 2 + 4) // (16 * ranks)) * 16
     piece = shape((rows, hidden), bf16)
     bias = shape((hidden, LANE), f32)
-    one_rims = (mixed_shape, edge, edge)
+    rims = shape((members, HALO, width), bf16)
     operands = [table, w_one, w_two, w_three]
     for m in each:
         operands += [saved[m][2], saved[m][4], d_decoded[m]]
     out = kernel_call(
         lambda *refs: backward_kernel(members, *refs),
-        (saved_shape,) * (2 * members) + (bias, bias) + one_rims * (members - 1),
-        flops=2 * members * slots * dense,
+        (saved_shape,) * (2 * members) + (mixed_shape,) * members + (bias, bias, rims, rims),
+        flops=2 * members * slots * (dense + 2 * HALO * width),
         moved=10 * MIB,
         operands=len(operands),
     )(*operands)
-    d_one, d_two, (bias_one, bias_two), rims = (
-        out[:members], out[members : 2 * members], out[2 * members : 2 * members + 2], out[2 * members + 2 :]
-    )
-
-    def returned(head, tail):
-        return [shifted(head, "space", -1), shifted(tail, "space", 1)]
-
-    edges = [block for m in each[:-1] for block in returned(*rims[3 * m + 1 : 3 * m + 3])]
-    operands = [region_at, rank_at, table, w_one, score, bias_one, bias_two]
+    d_one, d_two, d_mixed = (out[i * members : (i + 1) * members] for i in range(3))
+    bias_one, bias_two, head, tail = out[3 * members :]
+    from_next = shifted(head, "space", -1)
+    operands = [region_at, rank_at, score, bias_one, bias_two]
     for m in each:
         mixed, act_one, _, act_two, _ = saved[m]
         operands += [mixed, act_one, act_two, d_one[m], d_two[m], d_decoded[m]]
-    d_mixed, head, tail, *pieces = kernel_call(
+    pieces = kernel_call(
         lambda *refs: sums_kernel(members, ranks, *refs),
-        one_rims + (piece,) * ranks,
+        (piece,) * ranks,
         flops=2 * members * slots * dense,
         moved=10 * MIB,
         scratch=(pltpu.VMEM((ranks, rows, hidden), bf16),),
         smem=2,
         operands=len(operands),
     )(*operands)
-    d_mixed = [*rims[::3], d_mixed]
-
-    def summed(*blocks):
-        return kernel_call(sum_kernel, piece, flops=MIB, moved=MIB, operands=len(blocks))(*blocks)
-
-    pieces = [pieces[0]] + [swapped(pieces[i], "member", i) for i in range(1, ranks)]
-    pieces, edges = lax.optimization_barrier((pieces, edges))
-    total = summed(*pieces)
-    edges = [*edges, *returned(head, tail)]
+
+    def summed(ones, others):
+        return kernel_call(
+            sum_kernel, (piece,) * len(ones), flops=MIB, moved=MIB, operands=2 * len(ones)
+        )(*ones, *others)
+
+    bit = 1
+    while bit < ranks:
+        received = [swapped(sent, "member", bit) for sent in pieces[1::2]]
+        if bit == ranks // 2:
+            received, from_next = lax.optimization_barrier((received, from_next))
+        pieces = summed(pieces[::2], received)
+        bit = 2 * bit
+    (total,) = pieces
+    from_prev = shifted(tail, "space", 1)
     own = kernel_call(
         own_kernel,
         shape((members, nodes, width), f32),
@@ -448,7 +441,7 @@
     )(table, *d_mixed)
     step = 1
     while step < regions:
-        total = summed(total, swapped(total, "space", step))
+        (total,) = summed([total], [swapped(total, "space", step)])
         step = 2 * step
         if step == regions // 2:
             total, own = lax.optimization_barrier((total, own))
@@ -458,14 +451,14 @@
         totals.update({i ^ bit: swapped(totals[i], "member", bit) for i in sorted(totals)})
         bit = 2 * bit
     beside = swapped(total, "member", 1)
-    beside, edges = lax.optimization_barrier((beside, edges))
+    beside, from_prev = lax.optimization_barrier((beside, from_prev))
     latent_grad = kernel_call(
         finish_kernel,
         shape((members, nodes, width), bf16),
         flops=MIB,
         moved=3 * MIB,
-        operands=1 + 2 * members,
-    )(own, *edges)
+        operands=3,
+    )(own, from_next, from_prev)
     across = {i: block for i, block in totals.items() if i}
     across, latent_grad = lax.optimization_barrier((across, latent_grad))
     totals.update({i ^ 1: swapped(block, "member", 1) for i, block in across.items()})

time: 74 us -> 75.5 us (1.020)
  waiting for transfers between devices: 25.2 us -> 31 us
  starting transfers between devices: 23.8 us -> 18.7 us
  Pallas kernels: 22.8 us -> 23.6 us
    ppermute x14, waiting for transfers between devices: 23.3 us -> 30.3 us  [swapped(): lax.ppermute(block, axis, [(i, i ^ by) for i in range(lax.axis_size(axis))])]
    ppermute x14, starting transfers between devices: 10.5 us -> 7.58 us  [swapped(): lax.ppermute(block, axis, [(i, i ^ by) for i in range(lax.axis_size(axis))])]
    ppermute x8 -> x6, starting transfers between devices: 13.3 us -> 11.1 us  [shifted(): lax.ppermute(shard, axis, [(i, (i + by) % length) for i in range(length)])]
    pallas_call x1, Pallas kernels: 2.38 us -> 3.77 us  [per_device(): kernel_call(lambda *refs: backward_kernel(members, *refs), (saved_shape,)...]
    ppermute x8 -> x6, waiting for transfers between devices: 1.87 us -> 0.66 us  [shifted(): lax.ppermute(shard, axis, [(i, (i + by) % length) for i in range(length)])]
    pallas_call x4 -> x5, Pallas kernels: 2.18 us -> 1.58 us  [the longest x1 1.46 us: per_device(): kernel_call(lambda *refs: sums_kernel(members, ranks, *refs), (piece,) *...]
  transfers between devices with their start and end apart: 22 -> 20, of which waited for: 12 -> 13; matrix products, arithmetic and copies ran while one was open for 0% -> 0% of each run, Pallas kernels for 23% -> 22%
where the time goes in v8:
time: 75.5 us; the launch traced here: 75.3 us
  waiting for transfers between devices  31 us (41%)
  Pallas kernels  23.6 us (31%)
  starting transfers between devices  18.7 us (25%)
  local copies, waits for them, and re-layouts  1.27 us (2%)
  between operations  0.84 us (1%)
    ppermute x14, waiting for transfers between devices, swapped(): lax.ppermute(block, axis, [(i, i ^ by) for i in range(lax.axis_size(axis))])  30.3 us
    ppermute x6, starting transfers between devices, shifted(): lax.ppermute(shard, axis, [(i, (i + by) % length) for i in range(length)])  11.1 us
    ppermute x14, starting transfers between devices, swapped(): lax.ppermute(block, axis, [(i, i ^ by) for i in range(lax.axis_size(axis))])  7.58 us
    pallas_call x2, Pallas kernels, per_device(): kernel_call(lambda *refs: forward_kernel(m, *refs), (mixed_shape,) + (sav...  6.56 us
    pallas_call x2, Pallas kernels, scored(): kernel_call(lambda *refs: score_kernel(members, len(others), members * ra...  4.58 us
    pallas_call x1, Pallas kernels, per_device(): kernel_call(lambda *refs: backward_kernel(members, *refs), (saved_shape,)...  3.77 us
    pallas_call x1, Pallas kernels, per_device(): kernel_call(table_kernel, (shape((ext, slots), bf16), shape((width, slots...  3.12 us
    pallas_call x1, Pallas kernels, per_device(): kernel_call(own_kernel, shape((members, nodes, width), f32), flops=2 * me...  1.81 us
  transfers between devices with their start and end apart: 20, of which 13 were waited for; matrix products, arithmetic and copies ran while one was open for 0% of the time, Pallas kernels for 22%

profile of v8, /device:TPU:0, one launch (start us, length us, event | category | flops | bytes accessed | tf_op | source)
XLA Modules:
  0.0 75.3 jit_solution(524677111439901571)
XLA Ops:
  0.6 0.0 copy-start.6
  0.6 0.0 copy-start.7
  0.7 1.2 %copy-done.7 = bf16[2,1024,256]{2,1,0:T(8,128)(2,1)S(1)} copy-done((bf16[2,1024,256]{2,1,0:T(8,128)(2,1)S(1)}, bf16[2,1024,256]{2,1,0:T(8,128)(2,1)}, u32[]{:S(2)}) %copy-start.7) | copy-done | bytes 1048600
  1.9 0.1 shard_map.153
  2.0 0.0 copy-start
  2.0 0.0 copy-start.1
  2.0 0.0 copy-start.2
  2.0 0.0 copy-start.4
  2.0 0.0 copy-start.5
  2.0 3.1 %collective-permute-start = (bf16[256,256]{1,0:T(8,128)(2,1)S(1)}, bf16[256,256]{1,0:T(8,128)(2,1)S(1)}, u32[]{:S(2)}, u32[]{:S(2)}) collective-permute-start(bf16[256,256]{1,0:T(8,128)(2,1)S(1)} %get-tuple-element.69), channel_id=1, source_target_pairs={{0,4},{4,8},{8,12},{12,0},{1,5},{5,9},{9,13},{13,1},{2,6},{6,10},{... | collective-permute-start | bytes 393224 | tf_op jit(solution)/shard_map/ppermute | solution.py:312
  5.1 2.1 %collective-permute-start.1 = (bf16[256,256]{1,0:T(8,128)(2,1)S(1)}, bf16[256,256]{1,0:T(8,128)(2,1)S(1)}, u32[]{:S(2)}, u32[]{:S(2)}) collective-permute-start(bf16[256,256]{1,0:T(8,128)(2,1)S(1)} %get-tuple-element.70), channel_id=1, source_target_pairs={{0,12},{4,0},{8,4},{12,8},{1,13},{5,1},{9,5},{13,9},{2,14},{6,2},{... | collective-permute-start | bytes 393224 | tf_op jit(solution)/shard_map/ppermute | solution.py:312
  7.2 0.0 collective-permute-start.2
  7.2 3.8 %collective-permute-start.3 = (bf16[256,256]{1,0:T(8,128)(2,1)S(1)}, bf16[256,256]{1,0:T(8,128)(2,1)S(1)}, u32[]{:S(2)}, u32[]{:S(2)}) collective-permute-start(bf16[256,256]{1,0:T(8,128)(2,1)S(1)} %get-tuple-element.73), channel_id=1, source_target_pairs={{0,12},{4,0},{8,4},{12,8},{1,13},{5,1},{9,5},{13,9},{2,14},{6,2},{... | collective-permute-start | bytes 393224 | tf_op jit(solution)/shard_map/ppermute | solution.py:312
  11.0 0.0 copy-done.6
  11.0 0.0 copy-done.8
  11.0 0.0 copy-done.9
  11.0 3.1 %shard_map.154 = (bf16[1536,1536]{1,0:T(8,128)(2,1)S(1)}, f32[256,1536]{1,0:T(8,128)S(1)}) custom-call(s32[1]{0:T(128)} %bitcast.1.region_ref.refs_0_, s32[1]{0:T(128)} %bitcast.rank_ref.refs_1_.refs_0_, s32[4]{0:T(128)S(1)} %copy-done.6, s32[4,1536]{1,0:T(4,128)S(1)} %copy-done.8, f32[4,1536]{1,0:T(4,128)S(1)} %copy-done.9, ...), custom_call_target="tpu_custom_call" | custom-call | flops 805306368 | bytes 12582912 | tf_op jit(solution)/shard_map/pallas_call | solution.py:340
  14.2 0.0 collective-permute-done.refs_2_
  14.2 0.6 collective-permute-done.1.refs_3_
  14.8 0.0 copy-done.1
  14.9 2.9 %shard_map.155 = (bf16[256,1536]{1,0:T(8,128)(2,1)S(1)}, bf16[256,1536]{1,0:T(8,128)(2,1)S(1)}, bf16[256,1536]{1,0:T(8,128)(2,1)S(1)}, bf16[256,1536]{1,0:T(8,12...) custom-call(f32[256,1536]{1,0:T(8,128)S(1)} %get-tuple-element.67.refs_0_, ...), custom_call_target="tpu_custom_call" | custom-call | flops 905969664 | bytes 8388608 | tf_op jit(solution)/shard_map/pallas_call | solution.py:355
  17.7 0.0 copy-start.3
  17.8 1.8 %collective-permute-start.7 = (bf16[128,1536]{1,0:T(8,128)(2,1)S(1)}, bf16[128,1536]{1,0:T(8,128)(2,1)S(1)}, u32[]{:S(2)}, u32[]{:S(2)}) collective-permute-start(bf16[128,1536]{1,0:T(8,128)(2,1)S(1)} %get-tuple-element.71.refs_2_), channel_id=1, source_target_pairs={{0,2},{1,3},{2,0},{3,1},{4,6},{5,7},{6,4},{7,5},{8,10},{9,11},{10,... | collective-permute-start | bytes 1179656 | tf_op jit(solution)/shard_map/ppermute | solution.py:316
  19.6 0.0 collective-permute-start.5
  19.6 0.0 collective-permute-done.2.refs_2_
  19.6 0.0 collective-permute-done.3.refs_3_
  19.6 3.7 %shard_map.156 = (bf16[256,1536]{1,0:T(8,128)(2,1)S(1)}, bf16[256,1536]{1,0:T(8,128)(2,1)S(1)}, bf16[256,1536]{1,0:T(8,128)(2,1)S(1)}, bf16[256,1536]{1,0:T(8,12...) custom-call(bf16[2,1024,256]{2,1,0:T(8,128)(2,1)S(1)} %get-tuple-element.66.latent_ref.refs_0_, ...), custom_call_target="tpu_custom_call" | custom-call | flops 1711276032 | bytes 8388608 | tf_op jit(solution)/shard_map/pallas_call | solution.py:355
  23.3 0.6 collective-permute-start.6
  23.9 0.2 collective-permute-start.4
  24.1 3.9 %collective-permute-done.7.refs_6_ = bf16[128,1536]{1,0:T(8,128)(2,1)S(1)} collective-permute-done((bf16[128,1536]{1,0:T(8,128)(2,1)S(1)}, bf16[128,1536]{1,0:T(8,128)(2,1)S(1)}, u32[]{:S(2)}, u32[]{:S(2)}) %collective-permute-start.7) | collective-permute-done | bytes 393248 | tf_op jit(solution)/shard_map/ppermute | solution.py:316
  28.0 0.0 collective-permute-done.5.refs_4_
  28.0 0.0 collective-permute-done.6.refs_5_
  28.0 2.5 %shard_map.157 = (f32[128,1536]{1,0:T(8,128)S(1)}, f32[128,1536]{1,0:T(8,128)S(1)}, f32[1,128]{1,0:T(1,128)S(1)}) custom-call(s32[1]{0:T(128)} %bitcast.1.region_ref.refs_0_, s32[4]{0:T(128)S(1)} %copy-done.6, bf16[128,1536]{1,0:T(8,128)(2,1)S(1)} %get-tuple-element.71.refs_2_, bf16[128,1536]{1,0:T(8,128)(2,1)S(1)} %get-tuple-element.74.refs_3_, ...), custom_call_target="tpu_custom_call" | custom-call | flops 4194304 | bytes 2097152 | tf_op jit(solution)/shard_map/pallas_call | solution.py:372
  30.5 5.1 %collective-permute-done.4.refs_4_ = bf16[128,1536]{1,0:T(8,128)(2,1)S(1)} collective-permute-done((bf16[128,1536]{1,0:T(8,128)(2,1)S(1)}, bf16[128,1536]{1,0:T(8,128)(2,1)S(1)}, u32[]{:S(2)}, u32[]{:S(2)}) %collective-permute-start.4) | collective-permute-done | bytes 393248 | tf_op jit(solution)/shard_map/ppermute | solution.py:316
  35.6 0.0 collective-permute-start.8
  35.6 0.5 collective-permute-start.9
  36.1 1.2 %collective-permute-done.8.refs_5_ = bf16[128,1536]{1,0:T(8,128)(2,1)S(1)} collective-permute-done((bf16[128,1536]{1,0:T(8,128)(2,1)S(1)}, bf16[128,1536]{1,0:T(8,128)(2,1)S(1)}, u32[]{:S(2)}, u32[]{:S(2)}) %collective-permute-start.8) | collective-permute-done | bytes 393248 | tf_op jit(solution)/shard_map/ppermute | solution.py:316
  37.4 0.6 collective-permute-done.9.refs_6_
  37.9 2.1 %shard_map.158 = (bf16[128,1536]{1,0:T(8,128)(2,1)S(1)}, bf16[128,1536]{1,0:T(8,128)(2,1)S(1)}, f32[1,128]{1,0:T(1,128)S(1)}) custom-call(s32[1]{0:T(128)} %bitcast.1.region_ref.refs_0_, s32[4]{0:T(128)S(1)} %copy-done.6, bf16[128,1536]{1,0:T(8,128)(2,1)S(1)} %get-tuple-element.71.refs_2_, bf16[128,1536]{1,0:T(8,128)(2,1)S(1)} %get-tuple-element.74.refs_3_, ...), custom_call_target="tpu_custom_call" | custom-call | flops 4194304 | bytes 2097152 | tf_op jit(solution)/shard_map/pallas_call | solution.py:372
  40.0 3.8 %shard_map.159 = (bf16[256,1536]{1,0:T(8,128)(2,1)S(1)}, bf16[256,1536]{1,0:T(8,128)(2,1)S(1)}, bf16[256,1536]{1,0:T(8,128)(2,1)S(1)}, bf16[256,1536]{1,0:T(8,12...) custom-call(bf16[1536,1536]{1,0:T(8,128)(2,1)S(1)} %get-tuple-elemen, ...), custom_call_target="tpu_custom_call" | custom-call | flops 1811939328 | bytes 10485760 | tf_op jit(solution)/shard_map/pallas_call | solution.py:397
  43.8 1.2 %collective-permute-start.13 = (bf16[2,256,256]{2,1,0:T(8,128)(2,1)S(1)}, bf16[2,256,256]{2,1,0:T(8,128)(2,1)S(1)}, u32[]{:S(2)}, u32[]{:S(2)}) collective-permute-start(bf16[2,256,256]{2,1,0:T(8,128)(2,1)S(1)} %get-tuple-element.107), channel_id=1, source_target_pairs={{0,12},{4,0},{8,4},{12,8},{1,13},{5,1},{9,5},{13,9},{2,14},{6,2},{... | collective-permute-start | bytes 786440 | tf_op jit(solution)/shard_map/ppermute | solution.py:312
  45.0 1.5 %shard_map.160 = (bf16[176,256]{1,0:T(8,128)(2,1)S(1)}, bf16[176,256]{1,0:T(8,128)(2,1)S(1)}, bf16[176,256]{1,0:T(8,128)(2,1)S(1)}, bf16[176,256]{1,0:T(8,128)(2,1)S(1)}) custom-call(s32[1]{0:T(128)} %bitcast.1.region_ref.refs_0_, s32[1]{0:T(128)} %bitcast.rank_ref.refs_1_.refs_0_, f32[1,128]{1,0:T(1,128)S(1)} %get-tuple-element.82.refs_2_, ...), custom_call_target="tpu_custom_call" | custom-call | flops 1006632960 | bytes 10485760 | tf_op jit(solution)/shard_map/pallas_call | solution.py:411
  46.4 0.1 collective-permute-start.10
  46.5 0.5 collective-permute-start.11
  47.0 0.8 %collective-permute-done.10.refs_2_ = bf16[176,256]{1,0:T(8,128)(2,1)S(1)} collective-permute-done((bf16[176,256]{1,0:T(8,128)(2,1)S(1)}, bf16[176,256]{1,0:T(8,128)(2,1)S(1)}, u32[]{:S(2)}, u32[]{:S(2)}) %collective-permute-start.10) | collective-permute-done | bytes 90144 | tf_op jit(solution)/shard_map/ppermute | solution.py:316
  47.8 0.2 collective-permute-done.11.refs_3_
  48.0 1.6 %collective-permute-start.12 = (bf16[176,256]{1,0:T(8,128)(2,1)S(1)}, bf16[176,256]{1,0:T(8,128)(2,1)S(1)}, u32[]{:S(2)}, u32[]{:S(2)}) collective-permute-start(bf16[176,256]{1,0:T(8,128)(2,1)S(1)} %get-tuple-element.106), channel_id=1, source_target_pairs={{0,2},{1,3},{2,0},{3,1},{4,6},{5,7},{6,4},{7,5},{8,10},{9,11},{10,... | collective-permute-start | bytes 270344 | tf_op jit(solution)/shard_map/ppermute | solution.py:316
  49.6 0.9 %collective-permute-start.17 = (bf16[2,256,256]{2,1,0:T(8,128)(2,1)S(1)}, bf16[2,256,256]{2,1,0:T(8,128)(2,1)S(1)}, u32[]{:S(2)}, u32[]{:S(2)}) collective-permute-start(bf16[2,256,256]{2,1,0:T(8,128)(2,1)S(1)} %get-tuple-element.112), channel_id=1, source_target_pairs={{0,4},{4,8},{8,12},{12,0},{1,5},{5,9},{9,13},{13,1},{2,6},{6,10},{... | collective-permute-start | bytes 786440 | tf_op jit(solution)/shard_map/ppermute | solution.py:312
  50.4 2.5 %collective-permute-done.12.refs_1_ = bf16[176,256]{1,0:T(8,128)(2,1)S(1)} collective-permute-done((bf16[176,256]{1,0:T(8,128)(2,1)S(1)}, bf16[176,256]{1,0:T(8,128)(2,1)S(1)}, u32[]{:S(2)}, u32[]{:S(2)}) %collective-permute-start.12) | collective-permute-done | bytes 90144 | tf_op jit(solution)/shard_map/ppermute | solution.py:316
  52.9 0.0 collective-permute-done.13.from_next_ref
  53.0 0.9 %collective-permute-start.14 = (bf16[176,256]{1,0:T(8,128)(2,1)S(1)}, bf16[176,256]{1,0:T(8,128)(2,1)S(1)}, u32[]{:S(2)}, u32[]{:S(2)}) collective-permute-start(bf16[176,256]{1,0:T(8,128)(2,1)S(1)} %shard_map.162.refs_0_), channel_id=1, source_target_pairs={{0,4},{4,0},{8,12},{12,8},{1,5},{5,1},{9,13},{13,9},{2,6},{6,2},{1... | collective-permute-start | bytes 270344 | tf_op jit(solution)/shard_map/ppermute | solution.py:316
  53.9 1.8 %shard_map.164.own_ref = f32[2,1024,256]{2,1,0:T(8,128)S(1)} custom-call(bf16[1536,1536]{1,0:T(8,128)(2,1)S(1)} %get-tuple-element.68.refs_1_.refs_0_.table_ref, bf16[256,1536]{1,0:T(8,128)(2,1)S(1)} %get-tuple-element.109.refs_0_, bf16[256,1536]{1,0:T(8,128)(2,1)S(1)} %get-tuple-element.110.refs_1_), custom_call_target="tpu_custom_call" | custom-call | flops 1610612736 | bytes 6291456 | tf_op jit(solution)/shard_map/pallas_call | solution.py:435
  55.7 5.8 %collective-permute-done.14.refs_1_ = bf16[176,256]{1,0:T(8,128)(2,1)S(1)} collective-permute-done((bf16[176,256]{1,0:T(8,128)(2,1)S(1)}, bf16[176,256]{1,0:T(8,128)(2,1)S(1)}, u32[]{:S(2)}, u32[]{:S(2)}) %collective-permute-start.14) | collective-permute-done | bytes 90144 | tf_op jit(solution)/shard_map/ppermute | solution.py:316
  61.6 0.6 collective-permute-start.15
  62.2 5.8 %collective-permute-done.15.refs_1_ = bf16[176,256]{1,0:T(8,128)(2,1)S(1)} collective-permute-done((bf16[176,256]{1,0:T(8,128)(2,1)S(1)}, bf16[176,256]{1,0:T(8,128)(2,1)S(1)}, u32[]{:S(2)}, u32[]{:S(2)}) %collective-permute-start.15) | collective-permute-done | bytes 90144 | tf_op jit(solution)/shard_map/ppermute | solution.py:316
  68.0 0.1 collective-permute-start.16
  68.1 0.6 collective-permute-start.18
  68.7 0.0 collective-permute-done.17.from_prev_ref
  68.8 0.6 collective-permute-done.16.refs_2_
  69.4 1.1 %shard_map.166 = bf16[2,1024,256]{2,1,0:T(8,128)(2,1)} custom-call(f32[2,1024,256]{2,1,0:T(8,128)S(1)} %shard_map.164.own_ref, bf16[2,256,256]{2,1,0:T(8,128)(2,1)S(1)} %collective-permute-done.13.from_next_ref, bf16[2,256,256]{2,1,0:T(8,128)(2,1)S(1)} %collective-permute-done.17.from_prev_ref), custom_call_target="tpu_custom_call" | custom-call | flops 1048576 | bytes 3145728 | tf_op jit(solution)/shard_map/pallas_call | solution.py:455
  70.5 2.6 %collective-permute-done.18.refs_3_ = bf16[176,256]{1,0:T(8,128)(2,1)S(1)} collective-permute-done((bf16[176,256]{1,0:T(8,128)(2,1)S(1)}, bf16[176,256]{1,0:T(8,128)(2,1)S(1)}, u32[]{:S(2)}, u32[]{:S(2)}) %collective-permute-start.18) | collective-permute-done | bytes 90144 | tf_op jit(solution)/shard_map/ppermute | solution.py:316
  73.2 0.0 collective-permute-start.19
  73.2 1.3 %collective-permute-done.19.refs_4_ = bf16[176,256]{1,0:T(8,128)(2,1)S(1)} collective-permute-done((bf16[176,256]{1,0:T(8,128)(2,1)S(1)}, bf16[176,256]{1,0:T(8,128)(2,1)S(1)}, u32[]{:S(2)}, u32[]{:S(2)}) %collective-permute-start.19) | collective-permute-done | bytes 90144 | tf_op jit(solution)/shard_map/ppermute | solution.py:316
  74.4 0.9 %shard_map.167 = (f32[256,256]{1,0:T(8,128)}, f32[1,256]{1,0:T(1,128)}, f32[256,256]{1,0:T(8,128)}, f32[1,256]{1,0:T(1,128)}, f32[256,128]{1,0:T(8,128)}, /*index=5*/f32[1,4]{1,0:T(1,128)}) custom-call(s32[1]{0:T(128)} %bitcast.rank_ref.refs_1_.refs_0_, bf16[176,256]{1,0:T(8,128)(2,1)S(1)} %shard_map.165.refs_1_, ...), custom_call_target="tpu_custom_call" | custom-call | flops 1048576 | bytes 2097152 | tf_op jit(solution)/shard_map/pallas_call | solution.py:469
  (11 shorter events, 0.1 us)
Async XLA Ops:
  0.6 10.4 %copy-start.6 = (s32[4]{0:T(128)S(1)}, s32[4]{0:T(128)}, u32[]{:S(2)}) copy-start(s32[4]{0:T(128)} %refs_1_.4) | copy-start | bytes 52
  0.6 1.2 %copy-start.7 = (bf16[2,1024,256]{2,1,0:T(8,128)(2,1)S(1)}, bf16[2,1024,256]{2,1,0:T(8,128)(2,1)}, u32[]{:S(2)}) copy-start(bf16[2,1024,256]{2,1,0:T(8,128)(2,1)} %latent_ref.1) | copy-start | bytes 3145732
  1.9 9.2 %copy-start.8 = (s32[4,1536]{1,0:T(4,128)S(1)}, s32[4,1536]{1,0:T(4,128)}, u32[]{:S(2)}) copy-start(s32[4,1536]{1,0:T(4,128)} %nbr_ref.1) | copy-start | bytes 73732
  1.9 9.2 %copy-start.9 = (f32[4,1536]{1,0:T(4,128)S(1)}, f32[4,1536]{1,0:T(4,128)}, u32[]{:S(2)}) copy-start(f32[4,1536]{1,0:T(4,128)} %weight_ref.1) | copy-start | bytes 73732
  2.0 12.8 %copy-start = (bf16[256,256]{1,0:T(8,128)(2,1)S(1)}, bf16[256,256]{1,0:T(8,128)(2,1)}, u32[]{:S(2)}) copy-start(bf16[256,256]{1,0:T(8,128)(2,1)} %refs_1_.5) | copy-start | bytes 393220
  2.0 12.8 %copy-start.1 = (bf16[256,256]{1,0:T(8,128)(2,1)S(1)}, bf16[256,256]{1,0:T(8,128)(2,1)}, u32[]{:S(2)}) copy-start(bf16[256,256]{1,0:T(8,128)(2,1)} %refs_2_.1) | copy-start | bytes 393220
  2.0 12.8 %copy-start.2 = (bf16[256,128]{1,0:T(8,128)(2,1)S(1)}, bf16[256,128]{1,0:T(8,128)(2,1)}, u32[]{:S(2)}) copy-start(bf16[256,128]{1,0:T(8,128)(2,1)} %refs_3_.1) | copy-start | bytes 196612
  2.0 12.8 %copy-start.4 = (f32[256]{0:T(256)S(1)}, f32[256]{0:T(256)}, u32[]{:S(2)}) copy-start(f32[256]{0:T(256)} %param.16) | copy-start | bytes 3076
  2.0 12.8 %copy-start.5 = (f32[256]{0:T(256)S(1)}, f32[256]{0:T(256)}, u32[]{:S(2)}) copy-start(f32[256]{0:T(256)} %param.18) | copy-start | bytes 3076
  2.0 12.1 %collective-permute-start = (bf16[256,256]{1,0:T(8,128)(2,1)S(1)}, bf16[256,256]{1,0:T(8,128)(2,1)S(1)}, u32[]{:S(2)}, u32[]{:S(2)}) collective-permute-start(bf16[256,256]{1,0:T(8,128)(2,1)S(1)} %get-tuple-element.69), channel_id=1, source_target_pairs={{0,4},{4,8},{8,12},{12,0},{1,5},{5,9},{9,13},{13,1},{2,6},{6,10},{... | collective-permute-start | bytes 393224 | tf_op jit(solution)/shard_map/ppermute | solution.py:312
  5.1 9.7 %collective-permute-start.1 = (bf16[256,256]{1,0:T(8,128)(2,1)S(1)}, bf16[256,256]{1,0:T(8,128)(2,1)S(1)}, u32[]{:S(2)}, u32[]{:S(2)}) collective-permute-start(bf16[256,256]{1,0:T(8,128)(2,1)S(1)} %get-tuple-element.70), channel_id=1, source_target_pairs={{0,12},{4,0},{8,4},{12,8},{1,13},{5,1},{9,5},{13,9},{2,14},{6,2},{... | collective-permute-start | bytes 393224 | tf_op jit(solution)/shard_map/ppermute | solution.py:312
  7.2 12.4 %collective-permute-start.2 = (bf16[256,256]{1,0:T(8,128)(2,1)S(1)}, bf16[256,256]{1,0:T(8,128)(2,1)S(1)}, u32[]{:S(2)}, u32[]{:S(2)}) collective-permute-start(bf16[256,256]{1,0:T(8,128)(2,1)S(1)} %get-tuple-element.72), channel_id=1, source_target_pairs={{0,4},{4,8},{8,12},{12,0},{1,5},{5,9},{9,13},{13,1},{2,6},{6,10},{... | collective-permute-start | bytes 393224 | tf_op jit(solution)/shard_map/ppermute | solution.py:312
  7.2 12.4 %collective-permute-start.3 = (bf16[256,256]{1,0:T(8,128)(2,1)S(1)}, bf16[256,256]{1,0:T(8,128)(2,1)S(1)}, u32[]{:S(2)}, u32[]{:S(2)}) collective-permute-start(bf16[256,256]{1,0:T(8,128)(2,1)S(1)} %get-tuple-element.73), channel_id=1, source_target_pairs={{0,12},{4,0},{8,4},{12,8},{1,13},{5,1},{9,5},{13,9},{2,14},{6,2},{... | collective-permute-start | bytes 393224 | tf_op jit(solution)/shard_map/ppermute | solution.py:312
  17.7 10.3 %copy-start.3 = (bf16[1536,128]{1,0:T(8,128)(2,1)S(1)}, bf16[1536,128]{1,0:T(8,128)(2,1)}, u32[]{:S(2)}) copy-start(bf16[1536,128]{1,0:T(8,128)(2,1)} %refs_7_.1) | copy-start | bytes 1179652
  17.8 10.2 %collective-permute-start.7 = (bf16[128,1536]{1,0:T(8,128)(2,1)S(1)}, bf16[128,1536]{1,0:T(8,128)(2,1)S(1)}, u32[]{:S(2)}, u32[]{:S(2)}) collective-permute-start(bf16[128,1536]{1,0:T(8,128)(2,1)S(1)} %get-tuple-element.71.refs_2_), channel_id=1, source_target_pairs={{0,2},{1,3},{2,0},{3,1},{4,6},{5,7},{6,4},{7,5},{8,10},{9,11},{10,... | collective-permute-start | bytes 1179656 | tf_op jit(solution)/shard_map/ppermute | solution.py:316
  19.6 8.4 %collective-permute-start.5 = (bf16[128,1536]{1,0:T(8,128)(2,1)S(1)}, bf16[128,1536]{1,0:T(8,128)(2,1)S(1)}, u32[]{:S(2)}, u32[]{:S(2)}) collective-permute-start(bf16[128,1536]{1,0:T(8,128)(2,1)S(1)} %get-tuple-element.71.refs_2_), channel_id=1, source_target_pairs={{0,1},{1,0},{2,3},{3,2},{4,5},{5,4},{6,7},{7,6},{8,9},{9,8},{10,11... | collective-permute-start | bytes 1179656 | tf_op jit(solution)/shard_map/ppermute | solution.py:316
  23.3 4.7 %collective-permute-start.6 = (bf16[128,1536]{1,0:T(8,128)(2,1)S(1)}, bf16[128,1536]{1,0:T(8,128)(2,1)S(1)}, u32[]{:S(2)}, u32[]{:S(2)}) collective-permute-start(bf16[128,1536]{1,0:T(8,128)(2,1)S(1)} %get-tuple-element.74.refs_3_), channel_id=1, source_target_pairs={{0,1},{1,0},{2,3},{3,2},{4,5},{5,4},{6,7},{7,6},{8,9},{9,8},{10,11... | collective-permute-start | bytes 1179656 | tf_op jit(solution)/shard_map/ppermute | solution.py:316
  23.9 11.8 %collective-permute-start.4 = (bf16[128,1536]{1,0:T(8,128)(2,1)S(1)}, bf16[128,1536]{1,0:T(8,128)(2,1)S(1)}, u32[]{:S(2)}, u32[]{:S(2)}) collective-permute-start(bf16[128,1536]{1,0:T(8,128)(2,1)S(1)} %get-tuple-element.74.refs_3_), channel_id=1, source_target_pairs={{0,2},{1,3},{2,0},{3,1},{4,6},{5,7},{6,4},{7,5},{8,10},{9,11},{10,... | collective-permute-start | bytes 1179656 | tf_op jit(solution)/shard_map/ppermute | solution.py:316
  35.6 1.7 %collective-permute-start.8 = (bf16[128,1536]{1,0:T(8,128)(2,1)S(1)}, bf16[128,1536]{1,0:T(8,128)(2,1)S(1)}, u32[]{:S(2)}, u32[]{:S(2)}) collective-permute-start(bf16[128,1536]{1,0:T(8,128)(2,1)S(1)} %collective-permute-done.7.refs_6_), channel_id=1, source_target_pairs={{0,1},{1,0},{2,3},{3,2},{4,5},{5,4},{6,7},{7,6},{8,9},{9,8},{10,11... | collective-permute-start | bytes 1179656 | tf_op jit(solution)/shard_map/ppermute | solution.py:316
  35.6 2.3 %collective-permute-start.9 = (bf16[128,1536]{1,0:T(8,128)(2,1)S(1)}, bf16[128,1536]{1,0:T(8,128)(2,1)S(1)}, u32[]{:S(2)}, u32[]{:S(2)}) collective-permute-start(bf16[128,1536]{1,0:T(8,128)(2,1)S(1)} %collective-permute-done.4.refs_4_), channel_id=1, source_target_pairs={{0,1},{1,0},{2,3},{3,2},{4,5},{5,4},{6,7},{7,6},{8,9},{9,8},{10,11... | collective-permute-start | bytes 1179656 | tf_op jit(solution)/shard_map/ppermute | solution.py:316
  43.8 9.2 %collective-permute-start.13 = (bf16[2,256,256]{2,1,0:T(8,128)(2,1)S(1)}, bf16[2,256,256]{2,1,0:T(8,128)(2,1)S(1)}, u32[]{:S(2)}, u32[]{:S(2)}) collective-permute-start(bf16[2,256,256]{2,1,0:T(8,128)(2,1)S(1)} %get-tuple-element.107), channel_id=1, source_target_pairs={{0,12},{4,0},{8,4},{12,8},{1,13},{5,1},{9,5},{13,9},{2,14},{6,2},{... | collective-permute-start | bytes 786440 | tf_op jit(solution)/shard_map/ppermute | solution.py:312
  46.4 1.4 %collective-permute-start.10 = (bf16[176,256]{1,0:T(8,128)(2,1)S(1)}, bf16[176,256]{1,0:T(8,128)(2,1)S(1)}, u32[]{:S(2)}, u32[]{:S(2)}) collective-permute-start(bf16[176,256]{1,0:T(8,128)(2,1)S(1)} %get-tuple-element.103), channel_id=1, source_target_pairs={{0,1},{1,0},{2,3},{3,2},{4,5},{5,4},{6,7},{7,6},{8,9},{9,8},{10,11... | collective-permute-start | bytes 270344 | tf_op jit(solution)/shard_map/ppermute | solution.py:316
  46.5 1.4 %collective-permute-start.11 = (bf16[176,256]{1,0:T(8,128)(2,1)S(1)}, bf16[176,256]{1,0:T(8,128)(2,1)S(1)}, u32[]{:S(2)}, u32[]{:S(2)}) collective-permute-start(bf16[176,256]{1,0:T(8,128)(2,1)S(1)} %get-tuple-element.104), channel_id=1, source_target_pairs={{0,1},{1,0},{2,3},{3,2},{4,5},{5,4},{6,7},{7,6},{8,9},{9,8},{10,11... | collective-permute-start | bytes 270344 | tf_op jit(solution)/shard_map/ppermute | solution.py:316
  48.0 4.9 %collective-permute-start.12 = (bf16[176,256]{1,0:T(8,128)(2,1)S(1)}, bf16[176,256]{1,0:T(8,128)(2,1)S(1)}, u32[]{:S(2)}, u32[]{:S(2)}) collective-permute-start(bf16[176,256]{1,0:T(8,128)(2,1)S(1)} %get-tuple-element.106), channel_id=1, source_target_pairs={{0,2},{1,3},{2,0},{3,1},{4,6},{5,7},{6,4},{7,5},{8,10},{9,11},{10,... | collective-permute-start | bytes 270344 | tf_op jit(solution)/shard_map/ppermute | solution.py:316
  49.6 19.2 %collective-permute-start.17 = (bf16[2,256,256]{2,1,0:T(8,128)(2,1)S(1)}, bf16[2,256,256]{2,1,0:T(8,128)(2,1)S(1)}, u32[]{:S(2)}, u32[]{:S(2)}) collective-permute-start(bf16[2,256,256]{2,1,0:T(8,128)(2,1)S(1)} %get-tuple-element.112), channel_id=1, source_target_pairs={{0,4},{4,8},{8,12},{12,0},{1,5},{5,9},{9,13},{13,1},{2,6},{6,10},{... | collective-permute-start | bytes 786440 | tf_op jit(solution)/shard_map/ppermute | solution.py:312
  53.0 8.6 %collective-permute-start.14 = (bf16[176,256]{1,0:T(8,128)(2,1)S(1)}, bf16[176,256]{1,0:T(8,128)(2,1)S(1)}, u32[]{:S(2)}, u32[]{:S(2)}) collective-permute-start(bf16[176,256]{1,0:T(8,128)(2,1)S(1)} %shard_map.162.refs_0_), channel_id=1, source_target_pairs={{0,4},{4,0},{8,12},{12,8},{1,5},{5,1},{9,13},{13,9},{2,6},{6,2},{1... | collective-permute-start | bytes 270344 | tf_op jit(solution)/shard_map/ppermute | solution.py:316
  61.6 6.4 %collective-permute-start.15 = (bf16[176,256]{1,0:T(8,128)(2,1)S(1)}, bf16[176,256]{1,0:T(8,128)(2,1)S(1)}, u32[]{:S(2)}, u32[]{:S(2)}) collective-permute-start(bf16[176,256]{1,0:T(8,128)(2,1)S(1)} %shard_map.163.refs_0_), channel_id=1, source_target_pairs={{0,8},{4,12},{8,0},{12,4},{1,9},{5,13},{9,1},{13,5},{2,10},{6,14},... | collective-permute-start | bytes 270344 | tf_op jit(solution)/shard_map/ppermute | solution.py:316
  68.0 1.4 %collective-permute-start.16 = (bf16[176,256]{1,0:T(8,128)(2,1)S(1)}, bf16[176,256]{1,0:T(8,128)(2,1)S(1)}, u32[]{:S(2)}, u32[]{:S(2)}) collective-permute-start(bf16[176,256]{1,0:T(8,128)(2,1)S(1)} %shard_map.165.refs_1_), channel_id=1, source_target_pairs={{0,1},{1,0},{2,3},{3,2},{4,5},{5,4},{6,7},{7,6},{8,9},{9,8},{10,11... | collective-permute-start | bytes 270344 | tf_op jit(solution)/shard_map/ppermute | solution.py:316
  68.1 5.0 %collective-permute-start.18 = (bf16[176,256]{1,0:T(8,128)(2,1)S(1)}, bf16[176,256]{1,0:T(8,128)(2,1)S(1)}, u32[]{:S(2)}, u32[]{:S(2)}) collective-permute-start(bf16[176,256]{1,0:T(8,128)(2,1)S(1)} %shard_map.165.refs_1_), channel_id=1, source_target_pairs={{0,2},{1,3},{2,0},{3,1},{4,6},{5,7},{6,4},{7,5},{8,10},{9,11},{10,... | collective-permute-start | bytes 270344 | tf_op jit(solution)/shard_map/ppermute | solution.py:316
  73.2 1.3 %collective-permute-start.19 = (bf16[176,256]{1,0:T(8,128)(2,1)S(1)}, bf16[176,256]{1,0:T(8,128)(2,1)S(1)}, u32[]{:S(2)}, u32[]{:S(2)}) collective-permute-start(bf16[176,256]{1,0:T(8,128)(2,1)S(1)} %collective-permute-done.18.refs_3_), channel_id=1, source_target_pairs={{0,1},{1,0},{2,3},{3,2},{4,5},{5,4},{6,7},{7,6},{8,9},{9,8},{10,11... | collective-permute-start | bytes 270344 | tf_op jit(solution)/shard_map/ppermute | solution.py:316

commit v9 on v6

--- a/solution.py
+++ b/solution.py
@@ -38,21 +38,26 @@
         in_specs=specs + [vmem] * (operands - len(specs)),
         out_specs=jax.tree.map(lambda _: vmem, out_shape),
         scratch_shapes=list(scratch),
-        compiler_params=pltpu.CompilerParams(vmem_limit_bytes=40 * MIB),
+        compiler_params=pltpu.CompilerParams(vmem_limit_bytes=24 * MIB),
         cost_estimate=pl.CostEstimate(flops=flops, bytes_accessed=moved, transcendentals=0),
     )
 
 
-def rims_kernel(latent_ref, *refs):
+def cut_rims(latent_ref, member, last_ref, first_ref):
+    nodes = latent_ref.shape[1]
+    last_ref[...] = latent_ref[member, nodes - HALO :]
+    first_ref[...] = latent_ref[member, :HALO]
+
+
+def rims_kernel(latent_ref, last_ref, first_ref, copy_ref):
+    cut_rims(latent_ref, 0, last_ref, first_ref)
+    copy_ref[...] = latent_ref[...]
+
+
+def table_kernel(region_ref, rank_ref, counts_ref, nbr_ref, weight_ref, latent_ref, table_ref, part_ref, *rim_refs):
     members, nodes, _ = latent_ref.shape
-    for m in range(members):
-        refs[2 * m][...] = latent_ref[m, nodes - HALO :]
-        refs[2 * m + 1][...] = latent_ref[m, :HALO]
-    refs[-1][...] = latent_ref[...]
-
-
-def table_kernel(region_ref, rank_ref, counts_ref, nbr_ref, weight_ref, latent_ref, table_ref, part_ref):
-    nodes = latent_ref.shape[1]
+    for m in range(1, members):
+        cut_rims(latent_ref, m, *rim_refs[2 * m - 2 : 2 * m])
     ext, slots = table_ref.shape
     live = lax.broadcasted_iota(jnp.int32, (1, slots), 1) < counts_ref[region_ref[0]]
     nbr = [nbr_ref[k : k + 1, :] for k in range(K)]
@@ -69,21 +74,20 @@
         lax.broadcasted_iota(jnp.int32, (groups, 16, LANE), 0) * 16
         + lax.broadcasted_iota(jnp.int32, (groups, 16, LANE), 1)
     ).astype(jnp.float32).astype(jnp.bfloat16)
-    for lo, size in split(slots, LANE):
-        wide = [
-            jnp.broadcast_to(joint[k][:, lo : lo + size], (16, size)).astype(jnp.bfloat16)
-            for k in range(K)
-        ]
-        for b in range(ext // BLOCK):
-            tile = jnp.zeros((groups, 16, size), jnp.bfloat16)
-            for k in range(K):
-                near = (nbr[k][:, lo : lo + size] - b * BLOCK).astype(jnp.float32)
-                near = jnp.broadcast_to(near, (16, size)).astype(jnp.bfloat16)
-                tile = jnp.where(rows[:, :, :size] == near[None], wide[k][None], tile)
-            table_ref[b * BLOCK : (b + 1) * BLOCK, lo : lo + size] = tile.reshape(BLOCK, size)
     turned = latent_ref[0].T
-    for lo, size in split(slots, CHUNK):
-        part_ref[:, lo : lo + size] = nn_dot(turned, table_ref[HALO : HALO + nodes, lo : lo + size])
+    for start, length in split(slots, CHUNK):
+        for lo, size in split(length, LANE):
+            lanes = slice(start + lo, start + lo + size)
+            wide = [jnp.broadcast_to(joint[k][:, lanes], (16, size)).astype(jnp.bfloat16) for k in range(K)]
+            for b in range(ext // BLOCK):
+                tile = jnp.zeros((groups, 16, size), jnp.bfloat16)
+                for k in range(K):
+                    near = (nbr[k][:, lanes] - b * BLOCK).astype(jnp.float32)
+                    near = jnp.broadcast_to(near, (16, size)).astype(jnp.bfloat16)
+                    tile = jnp.where(rows[:, :, :size] == near[None], wide[k][None], tile)
+                table_ref[b * BLOCK : (b + 1) * BLOCK, lanes] = tile.reshape(BLOCK, size)
+        lanes = slice(start, start + length)
+        part_ref[:, lanes] = nn_dot(turned, table_ref[HALO : HALO + nodes, lanes])
 
 
 def column(ref):
@@ -207,18 +211,16 @@
 def backward_kernel(members, ranks, region_ref, rank_ref, w_two_ref, w_three_ref, score_ref, *refs):
     saved = [refs[6 * m : 6 * (m + 1)] for m in range(members)]
     refs = refs[6 * members :]
-    d_one_refs, refs = refs[:members], refs[members:]
-    piece_refs, (d_two_ref, stage_ref) = refs[:ranks], refs[ranks:]
+    d_one_refs, piece_refs, (d_two_ref, stage_ref) = refs[:members], refs[members:-2], refs[-2:]
     w_two, w_three = w_two_ref[...] * 0.5, w_three_ref[...] * 0.5
-    width, slots = saved[0][0].shape
-    hidden = saved[0][1].shape[0]
+    hidden, slots = saved[0][1].shape
     bias_one = jnp.zeros((hidden, LANE), jnp.float32)
     bias_two = jnp.zeros((hidden, LANE), jnp.float32)
+    g_one, g_two, g_three = 0.0, 0.0, 0.0
 
     def lane_sum(values):
         return sum(values[:, lo : lo + LANE] for lo, _ in split(values.shape[1], LANE))
 
-    g_one, g_two, g_three = 0.0, 0.0, 0.0
     for m in range(members):
         mixed_ref, act_one_ref, slope_one_ref, act_two_ref, slope_two_ref, d_dec_ref = saved[m]
         for lo, size in split(slots, CHUNK):
@@ -256,12 +258,14 @@
 def edges_kernel(members, table_ref, w_one_ref, *refs):
     d_one_refs, refs = refs[:members], refs[members:]
     ext = table_ref.shape[0]
+    rows = jnp.concatenate([table_ref[:HALO, :], table_ref[ext - HALO :, :]], axis=0)
     for m in range(members):
         d_mixed_ref, head_ref, tail_ref = refs[3 * m : 3 * (m + 1)]
         d_mixed = nn_dot(w_one_ref[...], d_one_refs[m][...]).astype(jnp.bfloat16)
         d_mixed_ref[...] = d_mixed
-        head_ref[...] = nt_dot(table_ref[:HALO, :], d_mixed).astype(jnp.bfloat16)
-        tail_ref[...] = nt_dot(table_ref[ext - HALO :, :], d_mixed).astype(jnp.bfloat16)
+        grads = nt_dot(rows, d_mixed).astype(jnp.bfloat16)
+        head_ref[...] = grads[:HALO]
+        tail_ref[...] = grads[HALO:]
 
 
 def sum_kernel(count, *refs):
@@ -329,30 +333,31 @@
     each = range(members)
 
     edge = shape((HALO, width), bf16)
-    *rims, latent = kernel_call(
-        rims_kernel, (edge,) * (2 * members) + (shape(latent.shape, bf16),), flops=MIB, moved=3 * MIB, operands=1
+    last, first, latent = kernel_call(
+        rims_kernel, (edge, edge, shape(latent.shape, bf16)), flops=4 << 30, moved=3 * MIB, operands=1
     )(latent)
-    before = [shifted(rims[2 * m], "space", 1) for m in each]
-    after = [shifted(rims[2 * m + 1], "space", -1) for m in each]
+    before, after = [shifted(last, "space", 1)], [shifted(first, "space", -1)]
     rank_at = rank[None].astype(jnp.int32)
     region_at = region[None].astype(jnp.int32)
 
-    table, part = kernel_call(
+    table, part, *rims = kernel_call(
         table_kernel,
-        (shape((ext, slots), bf16), shape((width, slots), f32)),
+        (shape((ext, slots), bf16), shape((width, slots), f32)) + (edge,) * (2 * members - 2),
         flops=2 * width * nodes * slots,
         moved=12 * MIB,
         smem=3,
         operands=6,
     )(region_at, rank_at, counts, neighbours, weights, latent)
+    before += [shifted(block, "space", 1) for block in rims[::2]]
+    after += [shifted(block, "space", -1) for block in rims[1::2]]
 
     saved_shape = shape((hidden, slots), bf16)
     mixed_shape = shape((width, slots), bf16)
     decoded_shape = shape((channels, slots), bf16)
     dense = width * hidden + hidden * hidden + hidden * channels
-    saved, known = [], []
+    saved, decoded, beside, across = [], [], [], []
     for m in each:
-        *kept, decoded = kernel_call(
+        *kept, block = kernel_call(
             lambda *refs: forward_kernel(m, *refs),
             (mixed_shape,) + (saved_shape,) * 4 + (decoded_shape,),
             flops=2 * slots * ((ext if m else 2 * HALO) * width + dense),
@@ -360,15 +365,16 @@
             operands=9,
         )(latent if m else part, table, before[m], after[m], w_one, b_one[None], w_two, b_two[None], w_three)
         saved.append(kept)
-        known.append({0: decoded})
-        bit = 2
+        decoded.append(block)
+        blocks, bit = {0: block}, 2
         while bit < ranks:
-            known[m].update({i ^ bit: swapped(known[m][i], "member", bit) for i in sorted(known[m])})
+            blocks.update({i ^ bit: swapped(blocks[i], "member", bit) for i in sorted(blocks)})
             bit = 2 * bit
-        known[m][1] = swapped(decoded, "member", 1)
+        across.append([blocks[i] for i in sorted(blocks) if i])
+        beside.append(swapped(block, "member", 1))
 
     def scored(others, carried, first=False, last=False):
-        operands = (region_at, counts, *[known[m][0] for m in each], *others, *carried)
+        operands = (region_at, counts, *decoded, *others, *carried)
         return kernel_call(
             lambda *refs: score_kernel(members, len(others), members * ranks, first, last, *refs),
             (shape((channels, slots), bf16 if last else f32),) * members + (shape((1, LANE), f32),),
@@ -378,20 +384,16 @@
             operands=len(operands),
         )(*operands)
 
-    near = [{i: block for i, block in known[m].items() if i > 1} for m in each]
-    early = [known[m][1] for m in each] + [block for blocks in near[:-1] for block in blocks.values()]
-    carried = scored(early, [targets], first=True)
-    near[-1], carried = lax.optimization_barrier((near[-1], carried))
-    others = [*near[-1].values()]
-    others += [swapped(block, "member", 1) for blocks in near for block in blocks.values()]
-    carried = scored(others, carried, last=True)
-    *d_decoded, score = carried
+    carried = scored(beside + [block for blocks in across[:-1] for block in blocks], [targets], first=True)
+    across[-1], carried = lax.optimization_barrier((across[-1], carried))
+    others = [*across[-1]] + [swapped(block, "member", 1) for blocks in across for block in blocks]
+    *grads, score = scored(others, carried, last=True)
 
     rows = -(-(width + hidden + hidden // 2 + 4) // (16 * ranks)) * 16
     piece = shape((rows, hidden), bf16)
     operands = [region_at, rank_at, w_two, w_three, score]
     for m in each:
-        operands += [*saved[m], d_decoded[m]]
+        operands += [*saved[m], grads[m]]
     out = kernel_call(
         lambda *refs: backward_kernel(members, ranks, *refs),
         (saved_shape,) * members + (piece,) * ranks,
@@ -443,6 +445,13 @@
         if step == regions // 2:
             total, edges, own, heads, tails = lax.optimization_barrier((total, edges, own, heads, tails))
             edges = [*edges, *returned(members - 1)]
+    totals = {0: total}
+    bit = 2
+    while bit < ranks:
+        totals.update({i ^ bit: swapped(totals[i], "member", bit) for i in sorted(totals)})
+        bit = 2 * bit
+    totals[1] = swapped(total, "member", 1)
+    totals[1], edges = lax.optimization_barrier((totals[1], edges))
     latent_grad = kernel_call(
         finish_kernel,
         shape((members, nodes, width), bf16),
@@ -450,12 +459,10 @@
         moved=3 * MIB,
         operands=1 + 2 * members,
     )(own, *edges)
-    totals = {0: total}
-    while bit > 1:
-        bit = bit // 2
-        if bit == 1:
-            totals[ranks // 2], latent_grad = lax.optimization_barrier((totals[ranks // 2], latent_grad))
-        totals.update({i ^ bit: swapped(totals[i], "member", bit) for i in sorted(totals)})
+    far = {i: block for i, block in totals.items() if i > 1}
+    far, latent_grad = lax.optimization_barrier((far, latent_grad))
+    totals.update(far)
+    totals.update({i ^ 1: swapped(block, "member", 1) for i, block in far.items()})
     totals = [totals[i] for i in range(ranks)]
     row = shape((1, hidden), f32)
     g_one, g_bone, g_two, g_btwo, g_three, tally = kernel_call(

time: 73.7 us -> 71.5 us (0.970)
  starting transfers between devices: 19.5 us -> 22.9 us
  waiting for transfers between devices: 27.1 us -> 23.8 us
  local copies, waits for them, and re-layouts: 3.42 us -> 1.27 us
    ppermute x14, waiting for transfers between devices: 24.7 us -> 21.4 us  [swapped(): lax.ppermute(block, axis, [(i, i ^ by) for i in range(lax.axis_size(axis))])]
    ppermute x14, starting transfers between devices: 5.84 us -> 8.72 us  [swapped(): lax.ppermute(block, axis, [(i, i ^ by) for i in range(lax.axis_size(axis))])]
    unnamed x22 -> x20, local copies, waits for them, and re-layouts: 3.42 us -> 1.27 us
  transfers between devices with their start and end apart: 22 -> 22, of which waited for: 10 -> 9; matrix products, arithmetic and copies ran while one was open for 0% -> 0% of each run, Pallas kernels for 23% -> 23%
where the time goes in v9:
time: 71.5 us; the launch traced here: 71.3 us
  waiting for transfers between devices  23.8 us (33%)
  starting transfers between devices  22.9 us (32%)
  Pallas kernels  22.5 us (31%)
  local copies, waits for them, and re-layouts  1.27 us (2%)
  between operations  0.88 us (1%)
    ppermute x14, waiting for transfers between devices, swapped(): lax.ppermute(block, axis, [(i, i ^ by) for i in range(lax.axis_size(axis))])  21.4 us
    ppermute x8, starting transfers between devices, shifted(): lax.ppermute(shard, axis, [(i, (i + by) % length) for i in range(length)])  14.2 us
    ppermute x14, starting transfers between devices, swapped(): lax.ppermute(block, axis, [(i, i ^ by) for i in range(lax.axis_size(axis))])  8.72 us
    pallas_call x2, Pallas kernels, per_device(): kernel_call(lambda *refs: forward_kernel(m, *refs), (mixed_shape,) + (sav...  6.56 us
    pallas_call x2, Pallas kernels, scored(): kernel_call(lambda *refs: score_kernel(members, len(others), members * ra...  4.58 us
    pallas_call x1, Pallas kernels, per_device(): kernel_call(table_kernel, (shape((ext, slots), bf16), shape((width, slots...  3.11 us
    pallas_call x1, Pallas kernels, per_device(): kernel_call(lambda *refs: backward_kernel(members, ranks, *refs), (saved_...  2.85 us
    ppermute x8, waiting for transfers between devices, shifted(): lax.ppermute(shard, axis, [(i, (i + by) % length) for i in range(length)])  2.36 us
  transfers between devices with their start and end apart: 22, of which 9 were waited for; matrix products, arithmetic and copies ran while one was open for 0% of the time, Pallas kernels for 23%

profile of v9, /device:TPU:0, one launch (start us, length us, event | category | flops | bytes accessed | tf_op | source)
XLA Modules:
  0.0 71.3 jit_solution(5506543008257857002)
XLA Ops:
  0.6 0.0 copy-start.6
  0.7 1.2 %copy-done.7 = bf16[2,1024,256]{2,1,0:T(8,128)(2,1)S(1)} copy-done((bf16[2,1024,256]{2,1,0:T(8,128)(2,1)S(1)}, bf16[2,1024,256]{2,1,0:T(8,128)(2,1)}, u32[]{:S(2)}) %copy-start.7) | copy-done | bytes 1048600
  1.9 0.1 shard_map.153
  2.0 0.0 copy-start
  2.0 0.0 copy-start.1
  2.0 0.0 copy-start.2
  2.0 0.0 copy-start.4
  2.0 0.0 copy-start.5
  2.0 3.1 %collective-permute-start = (bf16[256,256]{1,0:T(8,128)(2,1)S(1)}, bf16[256,256]{1,0:T(8,128)(2,1)S(1)}, u32[]{:S(2)}, u32[]{:S(2)}) collective-permute-start(bf16[256,256]{1,0:T(8,128)(2,1)S(1)} %get-tuple-element.78), channel_id=1, source_target_pairs={{0,4},{4,8},{8,12},{12,0},{1,5},{5,9},{9,13},{13,1},{2,6},{6,10},{... | collective-permute-start | bytes 393224 | tf_op jit(solution)/shard_map/ppermute | solution.py:316
  5.1 2.1 %collective-permute-start.1 = (bf16[256,256]{1,0:T(8,128)(2,1)S(1)}, bf16[256,256]{1,0:T(8,128)(2,1)S(1)}, u32[]{:S(2)}, u32[]{:S(2)}) collective-permute-start(bf16[256,256]{1,0:T(8,128)(2,1)S(1)} %get-tuple-element.79), channel_id=1, source_target_pairs={{0,12},{4,0},{8,4},{12,8},{1,13},{5,1},{9,5},{13,9},{2,14},{6,2},{... | collective-permute-start | bytes 393224 | tf_op jit(solution)/shard_map/ppermute | solution.py:316
  7.2 0.0 copy-done.9
  7.2 3.1 %shard_map.154 = (bf16[1536,1536]{1,0:T(8,128)(2,1)S(1)}, f32[256,1536]{1,0:T(8,128)S(1)}, bf16[256,256]{1,0:T(8,128)(2,1)S(1)}, bf16[256,256]{1,0:T(8,128)(2,1)S(1)}) custom-call(s32[1]{0:T(128)} %bitcast.1.region_ref.refs_0_, s32[1]{0:T(128)} %bitcast.rank_ref.refs_1_.refs_0_, s32[4]{0:T(128)S(1)} %copy-done.6, s32[4,1536]{1,0:T(4,128)S(1)} %copy-done.8, ...), custom_call_target="tpu_custom_call" | custom-call | flops 805306368 | bytes 12582912 | tf_op jit(solution)/shard_map/pallas_call | solution.py:343
  10.3 0.1 collective-permute-start.2
  10.4 3.8 %collective-permute-start.3 = (bf16[256,256]{1,0:T(8,128)(2,1)S(1)}, bf16[256,256]{1,0:T(8,128)(2,1)S(1)}, u32[]{:S(2)}, u32[]{:S(2)}) collective-permute-start(bf16[256,256]{1,0:T(8,128)(2,1)S(1)} %get-tuple-element.82), channel_id=1, source_target_pairs={{0,12},{4,0},{8,4},{12,8},{1,13},{5,1},{9,5},{13,9},{2,14},{6,2},{... | collective-permute-start | bytes 393224 | tf_op jit(solution)/shard_map/ppermute | solution.py:316
  14.2 0.0 collective-permute-done.refs_2_
  14.2 0.0 collective-permute-done.1.refs_3_
  14.3 2.9 %shard_map.155 = (bf16[256,1536]{1,0:T(8,128)(2,1)S(1)}, bf16[256,1536]{1,0:T(8,128)(2,1)S(1)}, bf16[256,1536]{1,0:T(8,128)(2,1)S(1)}, bf16[256,1536]{1,0:T(8,12...) custom-call(f32[256,1536]{1,0:T(8,128)S(1)} %get-tuple-element.76.refs_0_, ...), custom_call_target="tpu_custom_call" | custom-call | flops 905969664 | bytes 8388608 | tf_op jit(solution)/shard_map/pallas_call | solution.py:360
  17.1 0.0 copy-start.3
  17.1 1.7 %collective-permute-start.7 = (bf16[128,1536]{1,0:T(8,128)(2,1)S(1)}, bf16[128,1536]{1,0:T(8,128)(2,1)S(1)}, u32[]{:S(2)}, u32[]{:S(2)}) collective-permute-start(bf16[128,1536]{1,0:T(8,128)(2,1)S(1)} %get-tuple-element.80.refs_2_), channel_id=1, source_target_pairs={{0,2},{1,3},{2,0},{3,1},{4,6},{5,7},{6,4},{7,5},{8,10},{9,11},{10,... | collective-permute-start | bytes 1179656 | tf_op jit(solution)/shard_map/ppermute | solution.py:320
  18.9 0.0 collective-permute-start.5
  18.9 0.0 collective-permute-done.2.refs_2_
  18.9 0.0 collective-permute-done.3.refs_3_
  18.9 3.7 %shard_map.156 = (bf16[256,1536]{1,0:T(8,128)(2,1)S(1)}, bf16[256,1536]{1,0:T(8,128)(2,1)S(1)}, bf16[256,1536]{1,0:T(8,128)(2,1)S(1)}, bf16[256,1536]{1,0:T(8,12...) custom-call(bf16[2,1024,256]{2,1,0:T(8,128)(2,1)S(1)} %get-tuple-element.75.latent_ref.refs_0_, ...), custom_call_target="tpu_custom_call" | custom-call | flops 1711276032 | bytes 8388608 | tf_op jit(solution)/shard_map/pallas_call | solution.py:360
  22.6 0.6 collective-permute-start.6
  23.1 0.8 %collective-permute-start.4 = (bf16[128,1536]{1,0:T(8,128)(2,1)S(1)}, bf16[128,1536]{1,0:T(8,128)(2,1)S(1)}, u32[]{:S(2)}, u32[]{:S(2)}) collective-permute-start(bf16[128,1536]{1,0:T(8,128)(2,1)S(1)} %get-tuple-element.83.refs_3_), channel_id=1, source_target_pairs={{0,2},{1,3},{2,0},{3,1},{4,6},{5,7},{6,4},{7,5},{8,10},{9,11},{10,... | collective-permute-start | bytes 1179656 | tf_op jit(solution)/shard_map/ppermute | solution.py:320
  23.9 4.6 %collective-permute-done.7.refs_6_ = bf16[128,1536]{1,0:T(8,128)(2,1)S(1)} collective-permute-done((bf16[128,1536]{1,0:T(8,128)(2,1)S(1)}, bf16[128,1536]{1,0:T(8,128)(2,1)S(1)}, u32[]{:S(2)}, u32[]{:S(2)}) %collective-permute-start.7) | collective-permute-done | bytes 393248 | tf_op jit(solution)/shard_map/ppermute | solution.py:320
  28.6 0.0 collective-permute-done.5.refs_4_
  28.6 0.0 collective-permute-done.6.refs_5_
  28.6 2.5 %shard_map.157 = (f32[128,1536]{1,0:T(8,128)S(1)}, f32[128,1536]{1,0:T(8,128)S(1)}, f32[1,128]{1,0:T(1,128)S(1)}) custom-call(s32[1]{0:T(128)} %bitcast.1.region_ref.refs_0_, s32[4]{0:T(128)S(1)} %copy-done.6, bf16[128,1536]{1,0:T(8,128)(2,1)S(1)} %get-tuple-element.80.refs_2_, bf16[128,1536]{1,0:T(8,128)(2,1)S(1)} %get-tuple-element.83.refs_3_, ...), custom_call_target="tpu_custom_call" | custom-call | flops 4194304 | bytes 2097152 | tf_op jit(solution)/shard_map/pallas_call | solution.py:378
  31.1 4.5 %collective-permute-done.4.refs_4_ = bf16[128,1536]{1,0:T(8,128)(2,1)S(1)} collective-permute-done((bf16[128,1536]{1,0:T(8,128)(2,1)S(1)}, bf16[128,1536]{1,0:T(8,128)(2,1)S(1)}, u32[]{:S(2)}, u32[]{:S(2)}) %collective-permute-start.4) | collective-permute-done | bytes 393248 | tf_op jit(solution)/shard_map/ppermute | solution.py:320
  35.7 0.0 collective-permute-start.8
  35.7 0.5 collective-permute-start.9
  36.2 1.2 %collective-permute-done.8.refs_5_ = bf16[128,1536]{1,0:T(8,128)(2,1)S(1)} collective-permute-done((bf16[128,1536]{1,0:T(8,128)(2,1)S(1)}, bf16[128,1536]{1,0:T(8,128)(2,1)S(1)}, u32[]{:S(2)}, u32[]{:S(2)}) %collective-permute-start.8) | collective-permute-done | bytes 393248 | tf_op jit(solution)/shard_map/ppermute | solution.py:320
  37.4 0.6 collective-permute-done.9.refs_6_
  37.9 2.1 %shard_map.158 = (bf16[128,1536]{1,0:T(8,128)(2,1)S(1)}, bf16[128,1536]{1,0:T(8,128)(2,1)S(1)}, f32[1,128]{1,0:T(1,128)S(1)}) custom-call(s32[1]{0:T(128)} %bitcast.1.region_ref.refs_0_, s32[4]{0:T(128)S(1)} %copy-done.6, bf16[128,1536]{1,0:T(8,128)(2,1)S(1)} %get-tuple-element.80.refs_2_, bf16[128,1536]{1,0:T(8,128)(2,1)S(1)} %get-tuple-element.83.refs_3_, ...), custom_call_target="tpu_custom_call" | custom-call | flops 4194304 | bytes 2097152 | tf_op jit(solution)/shard_map/pallas_call | solution.py:378
  40.0 2.9 %shard_map.159 = (bf16[256,1536]{1,0:T(8,128)(2,1)S(1)}, bf16[256,1536]{1,0:T(8,128)(2,1)S(1)}, bf16[176,256]{1,0:T(8,128)(2,1)S(1)}, bf16[176,256]{1,0:T(8,128)...) custom-call(s32[1]{0:T(128)} %bitcast.1.region_ref.refs_0_, s32[1]{0:T(128)} %bitcast.rank_ref.refs_1_.refs_0_, ...), custom_call_target="tpu_custom_call" | custom-call | flops 2013265920 | bytes 10485760 | tf_op jit(solution)/shard_map/pallas_call | solution.py:397
  42.9 0.2 collective-permute-start.10
  43.1 0.4 collective-permute-start.11
  43.4 1.4 %shard_map.160 = (bf16[256,1536]{1,0:T(8,128)(2,1)S(1)}, bf16[256,256]{1,0:T(8,128)(2,1)S(1)}, bf16[256,256]{1,0:T(8,128)(2,1)S(1)}, bf16[256,1536]{1,0:T(8,128)...) custom-call(bf16[1536,1536]{1,0:T(8,128)(2,1)S(1)} %get-tuple-element.77.refs_1_.refs_0_.table_ref, ...), custom_call_target="tpu_custom_call" | custom-call | flops 1207959552 | bytes 6291456 | tf_op jit(solution)/shard_map/pallas_call | solution.py:413
  44.8 0.0 collective-permute-done.10.refs_2_
  44.9 0.0 collective-permute-done.11.refs_3_
  44.9 1.6 %collective-permute-start.12 = (bf16[176,256]{1,0:T(8,128)(2,1)S(1)}, bf16[176,256]{1,0:T(8,128)(2,1)S(1)}, u32[]{:S(2)}, u32[]{:S(2)}) collective-permute-start(bf16[176,256]{1,0:T(8,128)(2,1)S(1)} %get-tuple-element.117), channel_id=1, source_target_pairs={{0,2},{1,3},{2,0},{3,1},{4,6},{5,7},{6,4},{7,5},{8,10},{9,11},{10,... | collective-permute-start | bytes 270344 | tf_op jit(solution)/shard_map/ppermute | solution.py:320
  46.5 1.1 %collective-permute-start.14 = (bf16[256,256]{1,0:T(8,128)(2,1)S(1)}, bf16[256,256]{1,0:T(8,128)(2,1)S(1)}, u32[]{:S(2)}, u32[]{:S(2)}) collective-permute-start(bf16[256,256]{1,0:T(8,128)(2,1)S(1)} %get-tuple-element.118), channel_id=1, source_target_pairs={{0,12},{4,0},{8,4},{12,8},{1,13},{5,1},{9,5},{13,9},{2,14},{6,2},{... | collective-permute-start | bytes 393224 | tf_op jit(solution)/shard_map/ppermute | solution.py:316
  47.6 0.9 %collective-permute-start.15 = (bf16[256,256]{1,0:T(8,128)(2,1)S(1)}, bf16[256,256]{1,0:T(8,128)(2,1)S(1)}, u32[]{:S(2)}, u32[]{:S(2)}) collective-permute-start(bf16[256,256]{1,0:T(8,128)(2,1)S(1)} %get-tuple-element.119), channel_id=1, source_target_pairs={{0,4},{4,8},{8,12},{12,0},{1,5},{5,9},{9,13},{13,1},{2,6},{6,10},{... | collective-permute-start | bytes 393224 | tf_op jit(solution)/shard_map/ppermute | solution.py:316
  48.5 1.1 %collective-permute-done.12.refs_1_ = bf16[176,256]{1,0:T(8,128)(2,1)S(1)} collective-permute-done((bf16[176,256]{1,0:T(8,128)(2,1)S(1)}, bf16[176,256]{1,0:T(8,128)(2,1)S(1)}, u32[]{:S(2)}, u32[]{:S(2)}) %collective-permute-start.12) | collective-permute-done | bytes 90144 | tf_op jit(solution)/shard_map/ppermute | solution.py:320
  49.7 0.9 %collective-permute-start.13 = (bf16[176,256]{1,0:T(8,128)(2,1)S(1)}, bf16[176,256]{1,0:T(8,128)(2,1)S(1)}, u32[]{:S(2)}, u32[]{:S(2)}) collective-permute-start(bf16[176,256]{1,0:T(8,128)(2,1)S(1)} %shard_map.162.refs_0_), channel_id=1, source_target_pairs={{0,4},{4,0},{8,12},{12,8},{1,5},{5,1},{9,13},{13,9},{2,6},{6,2},{1... | collective-permute-start | bytes 270344 | tf_op jit(solution)/shard_map/ppermute | solution.py:320
  50.5 1.8 %shard_map.164.own_ref = f32[2,1024,256]{2,1,0:T(8,128)S(1)} custom-call(bf16[1536,1536]{1,0:T(8,128)(2,1)S(1)} %get-tuple-element.77.refs_1_.refs_0_.table_ref, bf16[256,1536]{1,0:T(8,128)(2,1)S(1)} %get-tuple-element.120.refs_0_, bf16[256,1536]{1,0:T(8,128)(2,1)S(1)} %get-tuple-element.121.refs_1_), custom_call_target="tpu_custom_call" | custom-call | flops 1610612736 | bytes 6291456 | tf_op jit(solution)/shard_map/pallas_call | solution.py:432
  52.3 4.1 %collective-permute-done.13.refs_1_ = bf16[176,256]{1,0:T(8,128)(2,1)S(1)} collective-permute-done((bf16[176,256]{1,0:T(8,128)(2,1)S(1)}, bf16[176,256]{1,0:T(8,128)(2,1)S(1)}, u32[]{:S(2)}, u32[]{:S(2)}) %collective-permute-start.13) | collective-permute-done | bytes 90144 | tf_op jit(solution)/shard_map/ppermute | solution.py:320
  56.5 0.0 collective-permute-done.14.refs_0_
  56.5 0.0 collective-permute-done.15.refs_1_
  56.5 0.5 collective-permute-start.16
  57.0 3.1 %collective-permute-start.18 = (bf16[256,256]{1,0:T(8,128)(2,1)S(1)}, bf16[256,256]{1,0:T(8,128)(2,1)S(1)}, u32[]{:S(2)}, u32[]{:S(2)}) collective-permute-start(bf16[256,256]{1,0:T(8,128)(2,1)S(1)} %get-tuple-element.127), channel_id=1, source_target_pairs={{0,12},{4,0},{8,4},{12,8},{1,13},{5,1},{9,5},{13,9},{2,14},{6,2},{... | collective-permute-start | bytes 393224 | tf_op jit(solution)/shard_map/ppermute | solution.py:316
  60.1 0.0 collective-permute-start.19
  60.1 3.9 %collective-permute-done.16.refs_1_ = bf16[176,256]{1,0:T(8,128)(2,1)S(1)} collective-permute-done((bf16[176,256]{1,0:T(8,128)(2,1)S(1)}, bf16[176,256]{1,0:T(8,128)(2,1)S(1)}, u32[]{:S(2)}, u32[]{:S(2)}) %collective-permute-start.16) | collective-permute-done | bytes 90144 | tf_op jit(solution)/shard_map/ppermute | solution.py:320
  64.0 0.1 collective-permute-start.17
  64.1 1.6 %collective-permute-start.20 = (bf16[176,256]{1,0:T(8,128)(2,1)S(1)}, bf16[176,256]{1,0:T(8,128)(2,1)S(1)}, u32[]{:S(2)}, u32[]{:S(2)}) collective-permute-start(bf16[176,256]{1,0:T(8,128)(2,1)S(1)} %shard_map.165.refs_1_), channel_id=1, source_target_pairs={{0,2},{1,3},{2,0},{3,1},{4,6},{5,7},{6,4},{7,5},{8,10},{9,11},{10,... | collective-permute-start | bytes 270344 | tf_op jit(solution)/shard_map/ppermute | solution.py:320
  65.7 0.0 collective-permute-done.18.refs_2_
  65.7 2.3 %collective-permute-done.19.refs_3_ = bf16[256,256]{1,0:T(8,128)(2,1)S(1)} collective-permute-done((bf16[256,256]{1,0:T(8,128)(2,1)S(1)}, bf16[256,256]{1,0:T(8,128)(2,1)S(1)}, u32[]{:S(2)}, u32[]{:S(2)}) %collective-permute-start.19) | collective-permute-done | bytes 131104 | tf_op jit(solution)/shard_map/ppermute | solution.py:316
  68.0 0.0 collective-permute-done.17.refs_2_
  68.0 1.1 %shard_map.166 = bf16[2,1024,256]{2,1,0:T(8,128)(2,1)} custom-call(f32[2,1024,256]{2,1,0:T(8,128)S(1)} %shard_map.164.own_ref, bf16[256,256]{1,0:T(8,128)(2,1)S(1)} %collective-permute-done.14.refs_0_, bf16[256,256]{1,0:T(8,128)(2,1)S(1)} %collective-permute-done.15.refs_1_, bf16[256,256]{1,0:T(8,128)(2,1)S(1)} %collective-permute-done.18.refs_2_, ...), custom_call_target="tpu_custom_call" | custom-call | flops 1048576 | bytes 3145728 | tf_op jit(solution)/shard_map/pallas_call | solution.py:455
  69.2 0.0 collective-permute-done.20.refs_3_
  69.2 0.0 collective-permute-start.21
  69.2 1.3 %collective-permute-done.21.refs_4_ = bf16[176,256]{1,0:T(8,128)(2,1)S(1)} collective-permute-done((bf16[176,256]{1,0:T(8,128)(2,1)S(1)}, bf16[176,256]{1,0:T(8,128)(2,1)S(1)}, u32[]{:S(2)}, u32[]{:S(2)}) %collective-permute-start.21) | collective-permute-done | bytes 90144 | tf_op jit(solution)/shard_map/ppermute | solution.py:320
  70.4 0.9 %shard_map.167 = (f32[256,256]{1,0:T(8,128)}, f32[1,256]{1,0:T(1,128)}, f32[256,256]{1,0:T(8,128)}, f32[1,256]{1,0:T(1,128)}, f32[256,128]{1,0:T(8,128)}, /*index=5*/f32[1,4]{1,0:T(1,128)}) custom-call(s32[1]{0:T(128)} %bitcast.rank_ref.refs_1_.refs_0_, bf16[176,256]{1,0:T(8,128)(2,1)S(1)} %shard_map.165.refs_1_, ...), custom_call_target="tpu_custom_call" | custom-call | flops 1048576 | bytes 2097152 | tf_op jit(solution)/shard_map/pallas_call | solution.py:468
  (15 shorter events, 0.1 us)
Async XLA Ops:
  0.6 6.6 %copy-start.6 = (s32[4]{0:T(128)S(1)}, s32[4]{0:T(128)}, u32[]{:S(2)}) copy-start(s32[4]{0:T(128)} %refs_1_.4) | copy-start | bytes 52
  0.6 1.2 %copy-start.7 = (bf16[2,1024,256]{2,1,0:T(8,128)(2,1)S(1)}, bf16[2,1024,256]{2,1,0:T(8,128)(2,1)}, u32[]{:S(2)}) copy-start(bf16[2,1024,256]{2,1,0:T(8,128)(2,1)} %latent_ref.1) | copy-start | bytes 3145732
  1.9 5.3 %copy-start.8 = (s32[4,1536]{1,0:T(4,128)S(1)}, s32[4,1536]{1,0:T(4,128)}, u32[]{:S(2)}) copy-start(s32[4,1536]{1,0:T(4,128)} %nbr_ref.1) | copy-start | bytes 73732
  1.9 5.3 %copy-start.9 = (f32[4,1536]{1,0:T(4,128)S(1)}, f32[4,1536]{1,0:T(4,128)}, u32[]{:S(2)}) copy-start(f32[4,1536]{1,0:T(4,128)} %weight_ref.1) | copy-start | bytes 73732
  2.0 12.2 %copy-start = (bf16[256,256]{1,0:T(8,128)(2,1)S(1)}, bf16[256,256]{1,0:T(8,128)(2,1)}, u32[]{:S(2)}) copy-start(bf16[256,256]{1,0:T(8,128)(2,1)} %refs_2_.1) | copy-start | bytes 393220
  2.0 12.2 %copy-start.1 = (bf16[256,256]{1,0:T(8,128)(2,1)S(1)}, bf16[256,256]{1,0:T(8,128)(2,1)}, u32[]{:S(2)}) copy-start(bf16[256,256]{1,0:T(8,128)(2,1)} %refs_1_.5) | copy-start | bytes 393220
  2.0 12.2 %copy-start.2 = (bf16[256,128]{1,0:T(8,128)(2,1)S(1)}, bf16[256,128]{1,0:T(8,128)(2,1)}, u32[]{:S(2)}) copy-start(bf16[256,128]{1,0:T(8,128)(2,1)} %refs_3_.1) | copy-start | bytes 196612
  2.0 12.2 %copy-start.4 = (f32[256]{0:T(256)S(1)}, f32[256]{0:T(256)}, u32[]{:S(2)}) copy-start(f32[256]{0:T(256)} %param.16) | copy-start | bytes 3076
  2.0 12.2 %copy-start.5 = (f32[256]{0:T(256)S(1)}, f32[256]{0:T(256)}, u32[]{:S(2)}) copy-start(f32[256]{0:T(256)} %param.18) | copy-start | bytes 3076
  2.0 12.2 %collective-permute-start = (bf16[256,256]{1,0:T(8,128)(2,1)S(1)}, bf16[256,256]{1,0:T(8,128)(2,1)S(1)}, u32[]{:S(2)}, u32[]{:S(2)}) collective-permute-start(bf16[256,256]{1,0:T(8,128)(2,1)S(1)} %get-tuple-element.78), channel_id=1, source_target_pairs={{0,4},{4,8},{8,12},{12,0},{1,5},{5,9},{9,13},{13,1},{2,6},{6,10},{... | collective-permute-start | bytes 393224 | tf_op jit(solution)/shard_map/ppermute | solution.py:316
  5.1 9.1 %collective-permute-start.1 = (bf16[256,256]{1,0:T(8,128)(2,1)S(1)}, bf16[256,256]{1,0:T(8,128)(2,1)S(1)}, u32[]{:S(2)}, u32[]{:S(2)}) collective-permute-start(bf16[256,256]{1,0:T(8,128)(2,1)S(1)} %get-tuple-element.79), channel_id=1, source_target_pairs={{0,12},{4,0},{8,4},{12,8},{1,13},{5,1},{9,5},{13,9},{2,14},{6,2},{... | collective-permute-start | bytes 393224 | tf_op jit(solution)/shard_map/ppermute | solution.py:316
  10.3 8.5 %collective-permute-start.2 = (bf16[256,256]{1,0:T(8,128)(2,1)S(1)}, bf16[256,256]{1,0:T(8,128)(2,1)S(1)}, u32[]{:S(2)}, u32[]{:S(2)}) collective-permute-start(bf16[256,256]{1,0:T(8,128)(2,1)S(1)} %get-tuple-element.81), channel_id=1, source_target_pairs={{0,4},{4,8},{8,12},{12,0},{1,5},{5,9},{9,13},{13,1},{2,6},{6,10},{... | collective-permute-start | bytes 393224 | tf_op jit(solution)/shard_map/ppermute | solution.py:316
  10.4 8.5 %collective-permute-start.3 = (bf16[256,256]{1,0:T(8,128)(2,1)S(1)}, bf16[256,256]{1,0:T(8,128)(2,1)S(1)}, u32[]{:S(2)}, u32[]{:S(2)}) collective-permute-start(bf16[256,256]{1,0:T(8,128)(2,1)S(1)} %get-tuple-element.82), channel_id=1, source_target_pairs={{0,12},{4,0},{8,4},{12,8},{1,13},{5,1},{9,5},{13,9},{2,14},{6,2},{... | collective-permute-start | bytes 393224 | tf_op jit(solution)/shard_map/ppermute | solution.py:316
  17.1 11.5 %copy-start.3 = (bf16[1536,128]{1,0:T(8,128)(2,1)S(1)}, bf16[1536,128]{1,0:T(8,128)(2,1)}, u32[]{:S(2)}) copy-start(bf16[1536,128]{1,0:T(8,128)(2,1)} %refs_7_.1) | copy-start | bytes 1179652
  17.1 11.4 %collective-permute-start.7 = (bf16[128,1536]{1,0:T(8,128)(2,1)S(1)}, bf16[128,1536]{1,0:T(8,128)(2,1)S(1)}, u32[]{:S(2)}, u32[]{:S(2)}) collective-permute-start(bf16[128,1536]{1,0:T(8,128)(2,1)S(1)} %get-tuple-element.80.refs_2_), channel_id=1, source_target_pairs={{0,2},{1,3},{2,0},{3,1},{4,6},{5,7},{6,4},{7,5},{8,10},{9,11},{10,... | collective-permute-start | bytes 1179656 | tf_op jit(solution)/shard_map/ppermute | solution.py:320
  18.9 9.7 %collective-permute-start.5 = (bf16[128,1536]{1,0:T(8,128)(2,1)S(1)}, bf16[128,1536]{1,0:T(8,128)(2,1)S(1)}, u32[]{:S(2)}, u32[]{:S(2)}) collective-permute-start(bf16[128,1536]{1,0:T(8,128)(2,1)S(1)} %get-tuple-element.80.refs_2_), channel_id=1, source_target_pairs={{0,1},{1,0},{2,3},{3,2},{4,5},{5,4},{6,7},{7,6},{8,9},{9,8},{10,11... | collective-permute-start | bytes 1179656 | tf_op jit(solution)/shard_map/ppermute | solution.py:320
  22.6 6.0 %collective-permute-start.6 = (bf16[128,1536]{1,0:T(8,128)(2,1)S(1)}, bf16[128,1536]{1,0:T(8,128)(2,1)S(1)}, u32[]{:S(2)}, u32[]{:S(2)}) collective-permute-start(bf16[128,1536]{1,0:T(8,128)(2,1)S(1)} %get-tuple-element.83.refs_3_), channel_id=1, source_target_pairs={{0,1},{1,0},{2,3},{3,2},{4,5},{5,4},{6,7},{7,6},{8,9},{9,8},{10,11... | collective-permute-start | bytes 1179656 | tf_op jit(solution)/shard_map/ppermute | solution.py:320
  23.1 12.5 %collective-permute-start.4 = (bf16[128,1536]{1,0:T(8,128)(2,1)S(1)}, bf16[128,1536]{1,0:T(8,128)(2,1)S(1)}, u32[]{:S(2)}, u32[]{:S(2)}) collective-permute-start(bf16[128,1536]{1,0:T(8,128)(2,1)S(1)} %get-tuple-element.83.refs_3_), channel_id=1, source_target_pairs={{0,2},{1,3},{2,0},{3,1},{4,6},{5,7},{6,4},{7,5},{8,10},{9,11},{10,... | collective-permute-start | bytes 1179656 | tf_op jit(solution)/shard_map/ppermute | solution.py:320
  35.7 1.7 %collective-permute-start.8 = (bf16[128,1536]{1,0:T(8,128)(2,1)S(1)}, bf16[128,1536]{1,0:T(8,128)(2,1)S(1)}, u32[]{:S(2)}, u32[]{:S(2)}) collective-permute-start(bf16[128,1536]{1,0:T(8,128)(2,1)S(1)} %collective-permute-done.7.refs_6_), channel_id=1, source_target_pairs={{0,1},{1,0},{2,3},{3,2},{4,5},{5,4},{6,7},{7,6},{8,9},{9,8},{10,11... | collective-permute-start | bytes 1179656 | tf_op jit(solution)/shard_map/ppermute | solution.py:320
  35.7 2.3 %collective-permute-start.9 = (bf16[128,1536]{1,0:T(8,128)(2,1)S(1)}, bf16[128,1536]{1,0:T(8,128)(2,1)S(1)}, u32[]{:S(2)}, u32[]{:S(2)}) collective-permute-start(bf16[128,1536]{1,0:T(8,128)(2,1)S(1)} %collective-permute-done.4.refs_4_), channel_id=1, source_target_pairs={{0,1},{1,0},{2,3},{3,2},{4,5},{5,4},{6,7},{7,6},{8,9},{9,8},{10,11... | collective-permute-start | bytes 1179656 | tf_op jit(solution)/shard_map/ppermute | solution.py:320
  42.9 2.0 %collective-permute-start.10 = (bf16[176,256]{1,0:T(8,128)(2,1)S(1)}, bf16[176,256]{1,0:T(8,128)(2,1)S(1)}, u32[]{:S(2)}, u32[]{:S(2)}) collective-permute-start(bf16[176,256]{1,0:T(8,128)(2,1)S(1)} %get-tuple-element.106), channel_id=1, source_target_pairs={{0,1},{1,0},{2,3},{3,2},{4,5},{5,4},{6,7},{7,6},{8,9},{9,8},{10,11... | collective-permute-start | bytes 270344 | tf_op jit(solution)/shard_map/ppermute | solution.py:320
  43.1 1.8 %collective-permute-start.11 = (bf16[176,256]{1,0:T(8,128)(2,1)S(1)}, bf16[176,256]{1,0:T(8,128)(2,1)S(1)}, u32[]{:S(2)}, u32[]{:S(2)}) collective-permute-start(bf16[176,256]{1,0:T(8,128)(2,1)S(1)} %get-tuple-element.107), channel_id=1, source_target_pairs={{0,1},{1,0},{2,3},{3,2},{4,5},{5,4},{6,7},{7,6},{8,9},{9,8},{10,11... | collective-permute-start | bytes 270344 | tf_op jit(solution)/shard_map/ppermute | solution.py:320
  44.9 4.7 %collective-permute-start.12 = (bf16[176,256]{1,0:T(8,128)(2,1)S(1)}, bf16[176,256]{1,0:T(8,128)(2,1)S(1)}, u32[]{:S(2)}, u32[]{:S(2)}) collective-permute-start(bf16[176,256]{1,0:T(8,128)(2,1)S(1)} %get-tuple-element.117), channel_id=1, source_target_pairs={{0,2},{1,3},{2,0},{3,1},{4,6},{5,7},{6,4},{7,5},{8,10},{9,11},{10,... | collective-permute-start | bytes 270344 | tf_op jit(solution)/shard_map/ppermute | solution.py:320
  46.5 10.0 %collective-permute-start.14 = (bf16[256,256]{1,0:T(8,128)(2,1)S(1)}, bf16[256,256]{1,0:T(8,128)(2,1)S(1)}, u32[]{:S(2)}, u32[]{:S(2)}) collective-permute-start(bf16[256,256]{1,0:T(8,128)(2,1)S(1)} %get-tuple-element.118), channel_id=1, source_target_pairs={{0,12},{4,0},{8,4},{12,8},{1,13},{5,1},{9,5},{13,9},{2,14},{6,2},{... | collective-permute-start | bytes 393224 | tf_op jit(solution)/shard_map/ppermute | solution.py:316
  47.6 8.9 %collective-permute-start.15 = (bf16[256,256]{1,0:T(8,128)(2,1)S(1)}, bf16[256,256]{1,0:T(8,128)(2,1)S(1)}, u32[]{:S(2)}, u32[]{:S(2)}) collective-permute-start(bf16[256,256]{1,0:T(8,128)(2,1)S(1)} %get-tuple-element.119), channel_id=1, source_target_pairs={{0,4},{4,8},{8,12},{12,0},{1,5},{5,9},{9,13},{13,1},{2,6},{6,10},{... | collective-permute-start | bytes 393224 | tf_op jit(solution)/shard_map/ppermute | solution.py:316
  49.7 6.8 %collective-permute-start.13 = (bf16[176,256]{1,0:T(8,128)(2,1)S(1)}, bf16[176,256]{1,0:T(8,128)(2,1)S(1)}, u32[]{:S(2)}, u32[]{:S(2)}) collective-permute-start(bf16[176,256]{1,0:T(8,128)(2,1)S(1)} %shard_map.162.refs_0_), channel_id=1, source_target_pairs={{0,4},{4,0},{8,12},{12,8},{1,5},{5,1},{9,13},{13,9},{2,6},{6,2},{1... | collective-permute-start | bytes 270344 | tf_op jit(solution)/shard_map/ppermute | solution.py:320
  56.5 7.5 %collective-permute-start.16 = (bf16[176,256]{1,0:T(8,128)(2,1)S(1)}, bf16[176,256]{1,0:T(8,128)(2,1)S(1)}, u32[]{:S(2)}, u32[]{:S(2)}) collective-permute-start(bf16[176,256]{1,0:T(8,128)(2,1)S(1)} %shard_map.163.refs_0_), channel_id=1, source_target_pairs={{0,8},{4,12},{8,0},{12,4},{1,9},{5,13},{9,1},{13,5},{2,10},{6,14},... | collective-permute-start | bytes 270344 | tf_op jit(solution)/shard_map/ppermute | solution.py:320
  57.0 8.7 %collective-permute-start.18 = (bf16[256,256]{1,0:T(8,128)(2,1)S(1)}, bf16[256,256]{1,0:T(8,128)(2,1)S(1)}, u32[]{:S(2)}, u32[]{:S(2)}) collective-permute-start(bf16[256,256]{1,0:T(8,128)(2,1)S(1)} %get-tuple-element.127), channel_id=1, source_target_pairs={{0,12},{4,0},{8,4},{12,8},{1,13},{5,1},{9,5},{13,9},{2,14},{6,2},{... | collective-permute-start | bytes 393224 | tf_op jit(solution)/shard_map/ppermute | solution.py:316
  60.1 7.9 %collective-permute-start.19 = (bf16[256,256]{1,0:T(8,128)(2,1)S(1)}, bf16[256,256]{1,0:T(8,128)(2,1)S(1)}, u32[]{:S(2)}, u32[]{:S(2)}) collective-permute-start(bf16[256,256]{1,0:T(8,128)(2,1)S(1)} %get-tuple-element.128), channel_id=1, source_target_pairs={{0,4},{4,8},{8,12},{12,0},{1,5},{5,9},{9,13},{13,1},{2,6},{6,10},{... | collective-permute-start | bytes 393224 | tf_op jit(solution)/shard_map/ppermute | solution.py:316
  64.0 4.0 %collective-permute-start.17 = (bf16[176,256]{1,0:T(8,128)(2,1)S(1)}, bf16[176,256]{1,0:T(8,128)(2,1)S(1)}, u32[]{:S(2)}, u32[]{:S(2)}) collective-permute-start(bf16[176,256]{1,0:T(8,128)(2,1)S(1)} %shard_map.165.refs_1_), channel_id=1, source_target_pairs={{0,1},{1,0},{2,3},{3,2},{4,5},{5,4},{6,7},{7,6},{8,9},{9,8},{10,11... | collective-permute-start | bytes 270344 | tf_op jit(solution)/shard_map/ppermute | solution.py:320
  64.1 5.1 %collective-permute-start.20 = (bf16[176,256]{1,0:T(8,128)(2,1)S(1)}, bf16[176,256]{1,0:T(8,128)(2,1)S(1)}, u32[]{:S(2)}, u32[]{:S(2)}) collective-permute-start(bf16[176,256]{1,0:T(8,128)(2,1)S(1)} %shard_map.165.refs_1_), channel_id=1, source_target_pairs={{0,2},{1,3},{2,0},{3,1},{4,6},{5,7},{6,4},{7,5},{8,10},{9,11},{10,... | collective-permute-start | bytes 270344 | tf_op jit(solution)/shard_map/ppermute | solution.py:320
  69.2 1.3 %collective-permute-start.21 = (bf16[176,256]{1,0:T(8,128)(2,1)S(1)}, bf16[176,256]{1,0:T(8,128)(2,1)S(1)}, u32[]{:S(2)}, u32[]{:S(2)}) collective-permute-start(bf16[176,256]{1,0:T(8,128)(2,1)S(1)} %collective-permute-done.20.refs_3_), channel_id=1, source_target_pairs={{0,1},{1,0},{2,3},{3,2},{4,5},{5,4},{6,7},{7,6},{8,9},{9,8},{10,11... | collective-permute-start | bytes 270344 | tf_op jit(solution)/shard_map/ppermute | solution.py:320

commit v10 on v9

--- a/solution.py
+++ b/solution.py
@@ -256,16 +256,15 @@
 
 
 def edges_kernel(members, table_ref, w_one_ref, *refs):
-    d_one_refs, refs = refs[:members], refs[members:]
+    d_one_refs, d_mixed_refs, (head_ref, tail_ref) = refs[:members], refs[members : 2 * members], refs[2 * members :]
     ext = table_ref.shape[0]
     rows = jnp.concatenate([table_ref[:HALO, :], table_ref[ext - HALO :, :]], axis=0)
     for m in range(members):
-        d_mixed_ref, head_ref, tail_ref = refs[3 * m : 3 * (m + 1)]
         d_mixed = nn_dot(w_one_ref[...], d_one_refs[m][...]).astype(jnp.bfloat16)
-        d_mixed_ref[...] = d_mixed
+        d_mixed_refs[m][...] = d_mixed
         grads = nt_dot(rows, d_mixed).astype(jnp.bfloat16)
-        head_ref[...] = grads[:HALO]
-        tail_ref[...] = grads[HALO:]
+        head_ref[m] = grads[:HALO]
+        tail_ref[m] = grads[HALO:]
 
 
 def sum_kernel(count, *refs):
@@ -301,14 +300,12 @@
         own_ref[m] = nt_dot(table_ref[HALO : HALO + nodes, :], d_mixed_refs[m][...])
 
 
-def finish_kernel(own_ref, *refs):
-    *refs, out_ref = refs
-    members, nodes, _ = own_ref.shape
-    for m in range(members):
-        from_next, from_prev = refs[2 * m][...].astype(jnp.float32), refs[2 * m + 1][...].astype(jnp.float32)
-        out_ref[m, :HALO] = (own_ref[m, :HALO] + from_prev).astype(jnp.bfloat16)
-        out_ref[m, HALO : nodes - HALO] = own_ref[m, HALO : nodes - HALO].astype(jnp.bfloat16)
-        out_ref[m, nodes - HALO :] = (own_ref[m, nodes - HALO :] + from_next).astype(jnp.bfloat16)
+def finish_kernel(own_ref, from_next_ref, from_prev_ref, out_ref):
+    nodes = own_ref.shape[1]
+    from_next, from_prev = from_next_ref[...].astype(jnp.float32), from_prev_ref[...].astype(jnp.float32)
+    out_ref[:, :HALO] = (own_ref[:, :HALO] + from_prev).astype(jnp.bfloat16)
+    out_ref[:, HALO : nodes - HALO] = own_ref[:, HALO : nodes - HALO].astype(jnp.bfloat16)
+    out_ref[:, nodes - HALO :] = (own_ref[:, nodes - HALO :] + from_next).astype(jnp.bfloat16)
 
 
 def shifted(shard, axis, by):
@@ -410,23 +407,20 @@
             lambda *refs: sum_kernel(len(ones), *refs), (piece,) * len(ones), flops=MIB, moved=MIB, operands=2 * len(ones)
         )(*ones, *others)
 
-    out = kernel_call(
+    rims = shape((members, HALO, width), bf16)
+    *d_mixed, head, tail = kernel_call(
         lambda *refs: edges_kernel(members, *refs),
-        (mixed_shape, edge, edge) * members,
+        (mixed_shape,) * members + (rims, rims),
         flops=2 * members * slots * width * (hidden + 2 * HALO),
         moved=6 * MIB,
         operands=2 + members,
     )(table, w_one, *d_one)
-    d_mixed, heads, tails = out[::3], out[1::3], out[2::3]
-
-    def returned(m):
-        return [shifted(heads[m], "space", -1), shifted(tails[m], "space", 1)]
 
     bit = 1
     while bit < ranks:
         received = [swapped(sent, "member", bit) for sent in pieces[1::2]]
         if bit == 1:
-            received, heads, tails = lax.optimization_barrier((received, heads, tails))
+            received, head, tail = lax.optimization_barrier((received, head, tail))
         pieces = summed(pieces[::2], received)
         bit = 2 * bit
     own = kernel_call(
@@ -436,34 +430,30 @@
         moved=6 * MIB,
         operands=1 + members,
     )(table, *d_mixed)
-    edges = [block for m in each[:-1] for block in returned(m)]
+    from_next = shifted(head, "space", -1)
     (total,) = pieces
     step = 1
     while step < regions:
         (total,) = summed([total], [swapped(total, "space", step)])
         step = 2 * step
         if step == regions // 2:
-            total, edges, own, heads, tails = lax.optimization_barrier((total, edges, own, heads, tails))
-            edges = [*edges, *returned(members - 1)]
+            total, from_next, own, tail = lax.optimization_barrier((total, from_next, own, tail))
+            from_prev = shifted(tail, "space", 1)
     totals = {0: total}
     bit = 2
     while bit < ranks:
         totals.update({i ^ bit: swapped(totals[i], "member", bit) for i in sorted(totals)})
         bit = 2 * bit
-    totals[1] = swapped(total, "member", 1)
-    totals[1], edges = lax.optimization_barrier((totals[1], edges))
+    totals.update({i ^ 1: swapped(block, "member", 1) for i, block in totals.items()})
     latent_grad = kernel_call(
         finish_kernel,
         shape((members, nodes, width), bf16),
         flops=MIB,
         moved=3 * MIB,
-        operands=1 + 2 * members,
-    )(own, *edges)
-    far = {i: block for i, block in totals.items() if i > 1}
-    far, latent_grad = lax.optimization_barrier((far, latent_grad))
-    totals.update(far)
-    totals.update({i ^ 1: swapped(block, "member", 1) for i, block in far.items()})
+        operands=3,
+    )(own, from_next, from_prev)
     totals = [totals[i] for i in range(ranks)]
+    totals, latent_grad = lax.optimization_barrier((totals, latent_grad))
     row = shape((1, hidden), f32)
     g_one, g_bone, g_two, g_btwo, g_three, tally = kernel_call(
         lambda *refs: unpack_kernel(1.0 / (OBS_MEAN * members * ranks), *refs),

time: 71.5 us -> 74.5 us (1.042)
  waiting for transfers between devices: 23.8 us -> 27.8 us
  starting transfers between devices: 22.9 us -> 21.9 us
    ppermute x14, waiting for transfers between devices: 21.4 us -> 27.8 us  [swapped(): lax.ppermute(block, axis, [(i, i ^ by) for i in range(lax.axis_size(axis))])]
    ppermute x8 -> x6, waiting for transfers between devices: 2.36 us -> 0.02 us  [shifted(): lax.ppermute(shard, axis, [(i, (i + by) % length) for i in range(length)])]
    ppermute x8 -> x6, starting transfers between devices: 14.2 us -> 12.4 us  [shifted(): lax.ppermute(shard, axis, [(i, (i + by) % length) for i in range(length)])]
    ppermute x14, starting transfers between devices: 8.72 us -> 9.48 us  [swapped(): lax.ppermute(block, axis, [(i, i ^ by) for i in range(lax.axis_size(axis))])]
  transfers between devices with their start and end apart: 22 -> 20, of which waited for: 9 -> 9; matrix products, arithmetic and copies ran while one was open for 0% -> 0% of each run, Pallas kernels for 23% -> 22%
where the time goes in v10:
time: 74.5 us; the launch traced here: 74.4 us
  waiting for transfers between devices  27.8 us (37%)
  Pallas kernels  22.5 us (30%)
  starting transfers between devices  21.9 us (29%)
  local copies, waits for them, and re-layouts  1.27 us (2%)
  between operations  0.86 us (1%)
    ppermute x14, waiting for transfers between devices, swapped(): lax.ppermute(block, axis, [(i, i ^ by) for i in range(lax.axis_size(axis))])  27.8 us
    ppermute x6, starting transfers between devices, shifted(): lax.ppermute(shard, axis, [(i, (i + by) % length) for i in range(length)])  12.4 us
    ppermute x14, starting transfers between devices, swapped(): lax.ppermute(block, axis, [(i, i ^ by) for i in range(lax.axis_size(axis))])  9.48 us
    pallas_call x2, Pallas kernels, per_device(): kernel_call(lambda *refs: forward_kernel(m, *refs), (mixed_shape,) + (sav...  6.56 us
    pallas_call x2, Pallas kernels, scored(): kernel_call(lambda *refs: score_kernel(members, len(others), members * ra...  4.58 us
    pallas_call x1, Pallas kernels, per_device(): kernel_call(table_kernel, (shape((ext, slots), bf16), shape((width, slots...  3.11 us
    pallas_call x1, Pallas kernels, per_device(): kernel_call(lambda *refs: backward_kernel(members, ranks, *refs), (saved_...  2.85 us
    pallas_call x1, Pallas kernels, per_device(): kernel_call(own_kernel, shape((members, nodes, width), f32), flops=2 * me...  1.81 us
  transfers between devices with their start and end apart: 20, of which 9 were waited for; matrix products, arithmetic and copies ran while one was open for 0% of the time, Pallas kernels for 22%

profile of v10, /device:TPU:0, one launch (start us, length us, event | category | flops | bytes accessed | tf_op | source)
XLA Modules:
  0.0 74.4 jit_solution(8287715414902650177)
XLA Ops:
  0.6 0.0 copy-start.6
  0.6 0.0 copy-start.7
  0.7 1.2 %copy-done.7 = bf16[2,1024,256]{2,1,0:T(8,128)(2,1)S(1)} copy-done((bf16[2,1024,256]{2,1,0:T(8,128)(2,1)S(1)}, bf16[2,1024,256]{2,1,0:T(8,128)(2,1)}, u32[]{:S(2)}) %copy-start.7) | copy-done | bytes 1048600
  1.9 0.1 shard_map.153
  2.0 0.0 copy-start
  2.0 0.0 copy-start.1
  2.0 0.0 copy-start.2
  2.0 0.0 copy-start.4
  2.0 0.0 copy-start.5
  2.0 3.1 %collective-permute-start = (bf16[256,256]{1,0:T(8,128)(2,1)S(1)}, bf16[256,256]{1,0:T(8,128)(2,1)S(1)}, u32[]{:S(2)}, u32[]{:S(2)}) collective-permute-start(bf16[256,256]{1,0:T(8,128)(2,1)S(1)} %get-tuple-element.70), channel_id=1, source_target_pairs={{0,4},{4,8},{8,12},{12,0},{1,5},{5,9},{9,13},{13,1},{2,6},{6,10},{... | collective-permute-start | bytes 393224 | tf_op jit(solution)/shard_map/ppermute | solution.py:313
  5.1 2.1 %collective-permute-start.1 = (bf16[256,256]{1,0:T(8,128)(2,1)S(1)}, bf16[256,256]{1,0:T(8,128)(2,1)S(1)}, u32[]{:S(2)}, u32[]{:S(2)}) collective-permute-start(bf16[256,256]{1,0:T(8,128)(2,1)S(1)} %get-tuple-element.71), channel_id=1, source_target_pairs={{0,12},{4,0},{8,4},{12,8},{1,13},{5,1},{9,5},{13,9},{2,14},{6,2},{... | collective-permute-start | bytes 393224 | tf_op jit(solution)/shard_map/ppermute | solution.py:313
  7.2 0.0 copy-done.6
  7.2 0.0 copy-done.8
  7.2 0.0 copy-done.9
  7.2 3.1 %shard_map.154 = (bf16[1536,1536]{1,0:T(8,128)(2,1)S(1)}, f32[256,1536]{1,0:T(8,128)S(1)}, bf16[256,256]{1,0:T(8,128)(2,1)S(1)}, bf16[256,256]{1,0:T(8,128)(2,1)S(1)}) custom-call(s32[1]{0:T(128)} %bitcast.1.region_ref.refs_0_, s32[1]{0:T(128)} %bitcast.rank_ref.refs_1_.refs_0_, s32[4]{0:T(128)S(1)} %copy-done.6, s32[4,1536]{1,0:T(4,128)S(1)} %copy-done.8, ...), custom_call_target="tpu_custom_call" | custom-call | flops 805306368 | bytes 12582912 | tf_op jit(solution)/shard_map/pallas_call | solution.py:340
  10.3 0.1 collective-permute-start.2
  10.4 3.8 %collective-permute-start.3 = (bf16[256,256]{1,0:T(8,128)(2,1)S(1)}, bf16[256,256]{1,0:T(8,128)(2,1)S(1)}, u32[]{:S(2)}, u32[]{:S(2)}) collective-permute-start(bf16[256,256]{1,0:T(8,128)(2,1)S(1)} %get-tuple-element.74), channel_id=1, source_target_pairs={{0,12},{4,0},{8,4},{12,8},{1,13},{5,1},{9,5},{13,9},{2,14},{6,2},{... | collective-permute-start | bytes 393224 | tf_op jit(solution)/shard_map/ppermute | solution.py:313
  14.2 0.0 collective-permute-done.refs_2_
  14.2 0.0 collective-permute-done.1.refs_3_
  14.2 0.0 copy-done
  14.3 2.9 %shard_map.155 = (bf16[256,1536]{1,0:T(8,128)(2,1)S(1)}, bf16[256,1536]{1,0:T(8,128)(2,1)S(1)}, bf16[256,1536]{1,0:T(8,128)(2,1)S(1)}, bf16[256,1536]{1,0:T(8,12...) custom-call(f32[256,1536]{1,0:T(8,128)S(1)} %get-tuple-element.68.refs_0_, ...), custom_call_target="tpu_custom_call" | custom-call | flops 905969664 | bytes 8388608 | tf_op jit(solution)/shard_map/pallas_call | solution.py:357
  17.1 0.0 copy-start.3
  17.1 1.7 %collective-permute-start.7 = (bf16[128,1536]{1,0:T(8,128)(2,1)S(1)}, bf16[128,1536]{1,0:T(8,128)(2,1)S(1)}, u32[]{:S(2)}, u32[]{:S(2)}) collective-permute-start(bf16[128,1536]{1,0:T(8,128)(2,1)S(1)} %get-tuple-element.72.refs_2_), channel_id=1, source_target_pairs={{0,2},{1,3},{2,0},{3,1},{4,6},{5,7},{6,4},{7,5},{8,10},{9,11},{10,... | collective-permute-start | bytes 1179656 | tf_op jit(solution)/shard_map/ppermute | solution.py:317
  18.9 0.0 collective-permute-start.5
  18.9 0.0 collective-permute-done.2.refs_2_
  18.9 0.0 collective-permute-done.3.refs_3_
  18.9 3.7 %shard_map.156 = (bf16[256,1536]{1,0:T(8,128)(2,1)S(1)}, bf16[256,1536]{1,0:T(8,128)(2,1)S(1)}, bf16[256,1536]{1,0:T(8,128)(2,1)S(1)}, bf16[256,1536]{1,0:T(8,12...) custom-call(bf16[2,1024,256]{2,1,0:T(8,128)(2,1)S(1)} %get-tuple-element.67.latent_ref.refs_0_, ...), custom_call_target="tpu_custom_call" | custom-call | flops 1711276032 | bytes 8388608 | tf_op jit(solution)/shard_map/pallas_call | solution.py:357
  22.6 0.6 collective-permute-start.6
  23.1 0.8 %collective-permute-start.4 = (bf16[128,1536]{1,0:T(8,128)(2,1)S(1)}, bf16[128,1536]{1,0:T(8,128)(2,1)S(1)}, u32[]{:S(2)}, u32[]{:S(2)}) collective-permute-start(bf16[128,1536]{1,0:T(8,128)(2,1)S(1)} %get-tuple-element.75.refs_3_), channel_id=1, source_target_pairs={{0,2},{1,3},{2,0},{3,1},{4,6},{5,7},{6,4},{7,5},{8,10},{9,11},{10,... | collective-permute-start | bytes 1179656 | tf_op jit(solution)/shard_map/ppermute | solution.py:317
  23.9 4.6 %collective-permute-done.7.refs_6_ = bf16[128,1536]{1,0:T(8,128)(2,1)S(1)} collective-permute-done((bf16[128,1536]{1,0:T(8,128)(2,1)S(1)}, bf16[128,1536]{1,0:T(8,128)(2,1)S(1)}, u32[]{:S(2)}, u32[]{:S(2)}) %collective-permute-start.7) | collective-permute-done | bytes 393248 | tf_op jit(solution)/shard_map/ppermute | solution.py:317
  28.6 0.0 collective-permute-done.5.refs_4_
  28.6 0.0 collective-permute-done.6.refs_5_
  28.6 2.5 %shard_map.157 = (f32[128,1536]{1,0:T(8,128)S(1)}, f32[128,1536]{1,0:T(8,128)S(1)}, f32[1,128]{1,0:T(1,128)S(1)}) custom-call(s32[1]{0:T(128)} %bitcast.1.region_ref.refs_0_, s32[4]{0:T(128)S(1)} %copy-done.6, bf16[128,1536]{1,0:T(8,128)(2,1)S(1)} %get-tuple-element.72.refs_2_, bf16[128,1536]{1,0:T(8,128)(2,1)S(1)} %get-tuple-element.75.refs_3_, ...), custom_call_target="tpu_custom_call" | custom-call | flops 4194304 | bytes 2097152 | tf_op jit(solution)/shard_map/pallas_call | solution.py:375
  31.1 4.5 %collective-permute-done.4.refs_4_ = bf16[128,1536]{1,0:T(8,128)(2,1)S(1)} collective-permute-done((bf16[128,1536]{1,0:T(8,128)(2,1)S(1)}, bf16[128,1536]{1,0:T(8,128)(2,1)S(1)}, u32[]{:S(2)}, u32[]{:S(2)}) %collective-permute-start.4) | collective-permute-done | bytes 393248 | tf_op jit(solution)/shard_map/ppermute | solution.py:317
  35.7 0.0 collective-permute-start.8
  35.7 0.5 collective-permute-start.9
  36.2 1.2 %collective-permute-done.8.refs_5_ = bf16[128,1536]{1,0:T(8,128)(2,1)S(1)} collective-permute-done((bf16[128,1536]{1,0:T(8,128)(2,1)S(1)}, bf16[128,1536]{1,0:T(8,128)(2,1)S(1)}, u32[]{:S(2)}, u32[]{:S(2)}) %collective-permute-start.8) | collective-permute-done | bytes 393248 | tf_op jit(solution)/shard_map/ppermute | solution.py:317
  37.4 0.6 collective-permute-done.9.refs_6_
  37.9 2.1 %shard_map.158 = (bf16[128,1536]{1,0:T(8,128)(2,1)S(1)}, bf16[128,1536]{1,0:T(8,128)(2,1)S(1)}, f32[1,128]{1,0:T(1,128)S(1)}) custom-call(s32[1]{0:T(128)} %bitcast.1.region_ref.refs_0_, s32[4]{0:T(128)S(1)} %copy-done.6, bf16[128,1536]{1,0:T(8,128)(2,1)S(1)} %get-tuple-element.72.refs_2_, bf16[128,1536]{1,0:T(8,128)(2,1)S(1)} %get-tuple-element.75.refs_3_, ...), custom_call_target="tpu_custom_call" | custom-call | flops 4194304 | bytes 2097152 | tf_op jit(solution)/shard_map/pallas_call | solution.py:375
  40.0 2.9 %shard_map.159 = (bf16[256,1536]{1,0:T(8,128)(2,1)S(1)}, bf16[256,1536]{1,0:T(8,128)(2,1)S(1)}, bf16[176,256]{1,0:T(8,128)(2,1)S(1)}, bf16[176,256]{1,0:T(8,128)...) custom-call(s32[1]{0:T(128)} %bitcast.1.region_ref.refs_0_, s32[1]{0:T(128)} %bitcast.rank_ref.refs_1_.refs_0_, ...), custom_call_target="tpu_custom_call" | custom-call | flops 2013265920 | bytes 10485760 | tf_op jit(solution)/shard_map/pallas_call | solution.py:394
  42.9 0.2 collective-permute-start.10
  43.1 0.4 collective-permute-start.11
  43.4 1.4 %shard_map.160 = (bf16[256,1536]{1,0:T(8,128)(2,1)S(1)}, bf16[256,1536]{1,0:T(8,128)(2,1)S(1)}, bf16[2,256,256]{2,1,0:T(8,128)(2,1)S(1)}, bf16[2,256,256]{2,1,0:T(8,128)(2,1)S(1)}) custom-call(bf16[1536,1536]{1,0:T(8,128)(2,1)S(1)} %get-tuple-element.69.refs_1_.refs_0_.table_ref, bf16[256,256]{1,0:T(8,128)(2,1)S(1)} %copy-done.1, ...), custom_call_target="tpu_custom_call" | custom-call | flops 1207959552 | bytes 6291456 | tf_op jit(solution)/shard_map/pallas_call | solution.py:411
  44.8 0.0 collective-permute-done.10.refs_2_
  44.9 0.0 collective-permute-done.11.refs_3_
  44.9 1.2 %collective-permute-start.14 = (bf16[2,256,256]{2,1,0:T(8,128)(2,1)S(1)}, bf16[2,256,256]{2,1,0:T(8,128)(2,1)S(1)}, u32[]{:S(2)}, u32[]{:S(2)}) collective-permute-start(bf16[2,256,256]{2,1,0:T(8,128)(2,1)S(1)} %get-tuple-element.108), channel_id=1, source_target_pairs={{0,12},{4,0},{8,4},{12,8},{1,13},{5,1},{9,5},{13,9},{2,14},{6,2},{... | collective-permute-start | bytes 786440 | tf_op jit(solution)/shard_map/ppermute | solution.py:313
  46.1 1.6 %collective-permute-start.12 = (bf16[176,256]{1,0:T(8,128)(2,1)S(1)}, bf16[176,256]{1,0:T(8,128)(2,1)S(1)}, u32[]{:S(2)}, u32[]{:S(2)}) collective-permute-start(bf16[176,256]{1,0:T(8,128)(2,1)S(1)} %get-tuple-element.107), channel_id=1, source_target_pairs={{0,2},{1,3},{2,0},{3,1},{4,6},{5,7},{6,4},{7,5},{8,10},{9,11},{10,... | collective-permute-start | bytes 270344 | tf_op jit(solution)/shard_map/ppermute | solution.py:317
  47.6 3.0 %collective-permute-done.12.refs_1_ = bf16[176,256]{1,0:T(8,128)(2,1)S(1)} collective-permute-done((bf16[176,256]{1,0:T(8,128)(2,1)S(1)}, bf16[176,256]{1,0:T(8,128)(2,1)S(1)}, u32[]{:S(2)}, u32[]{:S(2)}) %collective-permute-start.12) | collective-permute-done | bytes 90144 | tf_op jit(solution)/shard_map/ppermute | solution.py:317
  50.7 1.0 %collective-permute-start.13 = (bf16[176,256]{1,0:T(8,128)(2,1)S(1)}, bf16[176,256]{1,0:T(8,128)(2,1)S(1)}, u32[]{:S(2)}, u32[]{:S(2)}) collective-permute-start(bf16[176,256]{1,0:T(8,128)(2,1)S(1)} %shard_map.162.refs_0_), channel_id=1, source_target_pairs={{0,4},{4,0},{8,12},{12,8},{1,5},{5,1},{9,13},{13,9},{2,6},{6,2},{1... | collective-permute-start | bytes 270344 | tf_op jit(solution)/shard_map/ppermute | solution.py:317
  51.7 1.8 %shard_map.164.own_ref = f32[2,1024,256]{2,1,0:T(8,128)S(1)} custom-call(bf16[1536,1536]{1,0:T(8,128)(2,1)S(1)} %get-tuple-element.69.refs_1_.refs_0_.table_ref, bf16[256,1536]{1,0:T(8,128)(2,1)S(1)} %get-tuple-element.109.refs_0_, bf16[256,1536]{1,0:T(8,128)(2,1)S(1)} %get-tuple-element.110.refs_1_), custom_call_target="tpu_custom_call" | custom-call | flops 1610612736 | bytes 6291456 | tf_op jit(solution)/shard_map/pallas_call | solution.py:426
  53.5 1.8 %collective-permute-done.13.refs_1_ = bf16[176,256]{1,0:T(8,128)(2,1)S(1)} collective-permute-done((bf16[176,256]{1,0:T(8,128)(2,1)S(1)}, bf16[176,256]{1,0:T(8,128)(2,1)S(1)}, u32[]{:S(2)}, u32[]{:S(2)}) %collective-permute-start.13) | collective-permute-done | bytes 90144 | tf_op jit(solution)/shard_map/ppermute | solution.py:317
  55.3 0.0 collective-permute-done.14.from_next_ref
  55.3 1.2 %collective-permute-start.15 = (bf16[176,256]{1,0:T(8,128)(2,1)S(1)}, bf16[176,256]{1,0:T(8,128)(2,1)S(1)}, u32[]{:S(2)}, u32[]{:S(2)}) collective-permute-start(bf16[176,256]{1,0:T(8,128)(2,1)S(1)} %shard_map.163.refs_0_), channel_id=1, source_target_pairs={{0,8},{4,12},{8,0},{12,4},{1,9},{5,13},{9,1},{13,5},{2,10},{6,14},... | collective-permute-start | bytes 270344 | tf_op jit(solution)/shard_map/ppermute | solution.py:317
  56.5 2.2 %collective-permute-start.19 = (bf16[2,256,256]{2,1,0:T(8,128)(2,1)S(1)}, bf16[2,256,256]{2,1,0:T(8,128)(2,1)S(1)}, u32[]{:S(2)}, u32[]{:S(2)}) collective-permute-start(bf16[2,256,256]{2,1,0:T(8,128)(2,1)S(1)} %get-tuple-element.115), channel_id=1, source_target_pairs={{0,4},{4,8},{8,12},{12,0},{1,5},{5,9},{9,13},{13,1},{2,6},{6,10},{... | collective-permute-start | bytes 786440 | tf_op jit(solution)/shard_map/ppermute | solution.py:313
  58.8 8.8 %collective-permute-done.15.refs_1_ = bf16[176,256]{1,0:T(8,128)(2,1)S(1)} collective-permute-done((bf16[176,256]{1,0:T(8,128)(2,1)S(1)}, bf16[176,256]{1,0:T(8,128)(2,1)S(1)}, u32[]{:S(2)}, u32[]{:S(2)}) %collective-permute-start.15) | collective-permute-done | bytes 90144 | tf_op jit(solution)/shard_map/ppermute | solution.py:317
  67.6 1.6 %collective-permute-start.17 = (bf16[176,256]{1,0:T(8,128)(2,1)S(1)}, bf16[176,256]{1,0:T(8,128)(2,1)S(1)}, u32[]{:S(2)}, u32[]{:S(2)}) collective-permute-start(bf16[176,256]{1,0:T(8,128)(2,1)S(1)} %shard_map.165.refs_1_), channel_id=1, source_target_pairs={{0,2},{1,3},{2,0},{3,1},{4,6},{5,7},{6,4},{7,5},{8,10},{9,11},{10,... | collective-permute-start | bytes 270344 | tf_op jit(solution)/shard_map/ppermute | solution.py:317
  69.2 0.0 collective-permute-start.16
  69.2 3.0 %collective-permute-done.17.refs_3_ = bf16[176,256]{1,0:T(8,128)(2,1)S(1)} collective-permute-done((bf16[176,256]{1,0:T(8,128)(2,1)S(1)}, bf16[176,256]{1,0:T(8,128)(2,1)S(1)}, u32[]{:S(2)}, u32[]{:S(2)}) %collective-permute-start.17) | collective-permute-done | bytes 90144 | tf_op jit(solution)/shard_map/ppermute | solution.py:317
  72.2 0.0 collective-permute-start.18
  72.2 0.0 collective-permute-done.19.from_prev_ref
  72.2 1.1 %shard_map.166 = bf16[2,1024,256]{2,1,0:T(8,128)(2,1)} custom-call(f32[2,1024,256]{2,1,0:T(8,128)S(1)} %shard_map.164.own_ref, bf16[2,256,256]{2,1,0:T(8,128)(2,1)S(1)} %collective-permute-done.14.from_next_ref, bf16[2,256,256]{2,1,0:T(8,128)(2,1)S(1)} %collective-permute-done.19.from_prev_ref), custom_call_target="tpu_custom_call" | custom-call | flops 1048576 | bytes 3145728 | tf_op jit(solution)/shard_map/pallas_call | solution.py:448
  73.3 0.0 collective-permute-done.16.refs_2_
  73.3 0.2 collective-permute-done.18.refs_4_
  73.5 0.9 %shard_map.167 = (f32[256,256]{1,0:T(8,128)}, f32[1,256]{1,0:T(1,128)}, f32[256,256]{1,0:T(8,128)}, f32[1,256]{1,0:T(1,128)}, f32[256,128]{1,0:T(8,128)}, /*index=5*/f32[1,4]{1,0:T(1,128)}) custom-call(s32[1]{0:T(128)} %bitcast.rank_ref.refs_1_.refs_0_, bf16[176,256]{1,0:T(8,128)(2,1)S(1)} %shard_map.165.refs_1_, ...), custom_call_target="tpu_custom_call" | custom-call | flops 1048576 | bytes 2097152 | tf_op jit(solution)/shard_map/pallas_call | solution.py:458
  (11 shorter events, 0.1 us)
Async XLA Ops:
  0.6 6.6 %copy-start.6 = (s32[4]{0:T(128)S(1)}, s32[4]{0:T(128)}, u32[]{:S(2)}) copy-start(s32[4]{0:T(128)} %refs_1_.4) | copy-start | bytes 52
  0.6 1.2 %copy-start.7 = (bf16[2,1024,256]{2,1,0:T(8,128)(2,1)S(1)}, bf16[2,1024,256]{2,1,0:T(8,128)(2,1)}, u32[]{:S(2)}) copy-start(bf16[2,1024,256]{2,1,0:T(8,128)(2,1)} %latent_ref.1) | copy-start | bytes 3145732
  1.9 5.3 %copy-start.8 = (s32[4,1536]{1,0:T(4,128)S(1)}, s32[4,1536]{1,0:T(4,128)}, u32[]{:S(2)}) copy-start(s32[4,1536]{1,0:T(4,128)} %nbr_ref.1) | copy-start | bytes 73732
  1.9 5.3 %copy-start.9 = (f32[4,1536]{1,0:T(4,128)S(1)}, f32[4,1536]{1,0:T(4,128)}, u32[]{:S(2)}) copy-start(f32[4,1536]{1,0:T(4,128)} %weight_ref.1) | copy-start | bytes 73732
  2.0 12.2 %copy-start = (bf16[256,256]{1,0:T(8,128)(2,1)S(1)}, bf16[256,256]{1,0:T(8,128)(2,1)}, u32[]{:S(2)}) copy-start(bf16[256,256]{1,0:T(8,128)(2,1)} %refs_2_.1) | copy-start | bytes 393220
  2.0 12.2 %copy-start.1 = (bf16[256,256]{1,0:T(8,128)(2,1)S(1)}, bf16[256,256]{1,0:T(8,128)(2,1)}, u32[]{:S(2)}) copy-start(bf16[256,256]{1,0:T(8,128)(2,1)} %refs_1_.5) | copy-start | bytes 393220
  2.0 12.2 %copy-start.2 = (bf16[256,128]{1,0:T(8,128)(2,1)S(1)}, bf16[256,128]{1,0:T(8,128)(2,1)}, u32[]{:S(2)}) copy-start(bf16[256,128]{1,0:T(8,128)(2,1)} %refs_3_.1) | copy-start | bytes 196612
  2.0 12.2 %copy-start.4 = (f32[256]{0:T(256)S(1)}, f32[256]{0:T(256)}, u32[]{:S(2)}) copy-start(f32[256]{0:T(256)} %param.16) | copy-start | bytes 3076
  2.0 12.2 %copy-start.5 = (f32[256]{0:T(256)S(1)}, f32[256]{0:T(256)}, u32[]{:S(2)}) copy-start(f32[256]{0:T(256)} %param.18) | copy-start | bytes 3076
  2.0 12.2 %collective-permute-start = (bf16[256,256]{1,0:T(8,128)(2,1)S(1)}, bf16[256,256]{1,0:T(8,128)(2,1)S(1)}, u32[]{:S(2)}, u32[]{:S(2)}) collective-permute-start(bf16[256,256]{1,0:T(8,128)(2,1)S(1)} %get-tuple-element.70), channel_id=1, source_target_pairs={{0,4},{4,8},{8,12},{12,0},{1,5},{5,9},{9,13},{13,1},{2,6},{6,10},{... | collective-permute-start | bytes 393224 | tf_op jit(solution)/shard_map/ppermute | solution.py:313
  5.1 9.1 %collective-permute-start.1 = (bf16[256,256]{1,0:T(8,128)(2,1)S(1)}, bf16[256,256]{1,0:T(8,128)(2,1)S(1)}, u32[]{:S(2)}, u32[]{:S(2)}) collective-permute-start(bf16[256,256]{1,0:T(8,128)(2,1)S(1)} %get-tuple-element.71), channel_id=1, source_target_pairs={{0,12},{4,0},{8,4},{12,8},{1,13},{5,1},{9,5},{13,9},{2,14},{6,2},{... | collective-permute-start | bytes 393224 | tf_op jit(solution)/shard_map/ppermute | solution.py:313
  10.3 8.5 %collective-permute-start.2 = (bf16[256,256]{1,0:T(8,128)(2,1)S(1)}, bf16[256,256]{1,0:T(8,128)(2,1)S(1)}, u32[]{:S(2)}, u32[]{:S(2)}) collective-permute-start(bf16[256,256]{1,0:T(8,128)(2,1)S(1)} %get-tuple-element.73), channel_id=1, source_target_pairs={{0,4},{4,8},{8,12},{12,0},{1,5},{5,9},{9,13},{13,1},{2,6},{6,10},{... | collective-permute-start | bytes 393224 | tf_op jit(solution)/shard_map/ppermute | solution.py:313
  10.4 8.5 %collective-permute-start.3 = (bf16[256,256]{1,0:T(8,128)(2,1)S(1)}, bf16[256,256]{1,0:T(8,128)(2,1)S(1)}, u32[]{:S(2)}, u32[]{:S(2)}) collective-permute-start(bf16[256,256]{1,0:T(8,128)(2,1)S(1)} %get-tuple-element.74), channel_id=1, source_target_pairs={{0,12},{4,0},{8,4},{12,8},{1,13},{5,1},{9,5},{13,9},{2,14},{6,2},{... | collective-permute-start | bytes 393224 | tf_op jit(solution)/shard_map/ppermute | solution.py:313
  17.1 11.5 %copy-start.3 = (bf16[1536,128]{1,0:T(8,128)(2,1)S(1)}, bf16[1536,128]{1,0:T(8,128)(2,1)}, u32[]{:S(2)}) copy-start(bf16[1536,128]{1,0:T(8,128)(2,1)} %refs_7_.1) | copy-start | bytes 1179652
  17.1 11.4 %collective-permute-start.7 = (bf16[128,1536]{1,0:T(8,128)(2,1)S(1)}, bf16[128,1536]{1,0:T(8,128)(2,1)S(1)}, u32[]{:S(2)}, u32[]{:S(2)}) collective-permute-start(bf16[128,1536]{1,0:T(8,128)(2,1)S(1)} %get-tuple-element.72.refs_2_), channel_id=1, source_target_pairs={{0,2},{1,3},{2,0},{3,1},{4,6},{5,7},{6,4},{7,5},{8,10},{9,11},{10,... | collective-permute-start | bytes 1179656 | tf_op jit(solution)/shard_map/ppermute | solution.py:317
  18.9 9.7 %collective-permute-start.5 = (bf16[128,1536]{1,0:T(8,128)(2,1)S(1)}, bf16[128,1536]{1,0:T(8,128)(2,1)S(1)}, u32[]{:S(2)}, u32[]{:S(2)}) collective-permute-start(bf16[128,1536]{1,0:T(8,128)(2,1)S(1)} %get-tuple-element.72.refs_2_), channel_id=1, source_target_pairs={{0,1},{1,0},{2,3},{3,2},{4,5},{5,4},{6,7},{7,6},{8,9},{9,8},{10,11... | collective-permute-start | bytes 1179656 | tf_op jit(solution)/shard_map/ppermute | solution.py:317
  22.6 6.0 %collective-permute-start.6 = (bf16[128,1536]{1,0:T(8,128)(2,1)S(1)}, bf16[128,1536]{1,0:T(8,128)(2,1)S(1)}, u32[]{:S(2)}, u32[]{:S(2)}) collective-permute-start(bf16[128,1536]{1,0:T(8,128)(2,1)S(1)} %get-tuple-element.75.refs_3_), channel_id=1, source_target_pairs={{0,1},{1,0},{2,3},{3,2},{4,5},{5,4},{6,7},{7,6},{8,9},{9,8},{10,11... | collective-permute-start | bytes 1179656 | tf_op jit(solution)/shard_map/ppermute | solution.py:317
  23.1 12.5 %collective-permute-start.4 = (bf16[128,1536]{1,0:T(8,128)(2,1)S(1)}, bf16[128,1536]{1,0:T(8,128)(2,1)S(1)}, u32[]{:S(2)}, u32[]{:S(2)}) collective-permute-start(bf16[128,1536]{1,0:T(8,128)(2,1)S(1)} %get-tuple-element.75.refs_3_), channel_id=1, source_target_pairs={{0,2},{1,3},{2,0},{3,1},{4,6},{5,7},{6,4},{7,5},{8,10},{9,11},{10,... | collective-permute-start | bytes 1179656 | tf_op jit(solution)/shard_map/ppermute | solution.py:317
  35.7 1.7 %collective-permute-start.8 = (bf16[128,1536]{1,0:T(8,128)(2,1)S(1)}, bf16[128,1536]{1,0:T(8,128)(2,1)S(1)}, u32[]{:S(2)}, u32[]{:S(2)}) collective-permute-start(bf16[128,1536]{1,0:T(8,128)(2,1)S(1)} %collective-permute-done.7.refs_6_), channel_id=1, source_target_pairs={{0,1},{1,0},{2,3},{3,2},{4,5},{5,4},{6,7},{7,6},{8,9},{9,8},{10,11... | collective-permute-start | bytes 1179656 | tf_op jit(solution)/shard_map/ppermute | solution.py:317
  35.7 2.3 %collective-permute-start.9 = (bf16[128,1536]{1,0:T(8,128)(2,1)S(1)}, bf16[128,1536]{1,0:T(8,128)(2,1)S(1)}, u32[]{:S(2)}, u32[]{:S(2)}) collective-permute-start(bf16[128,1536]{1,0:T(8,128)(2,1)S(1)} %collective-permute-done.4.refs_4_), channel_id=1, source_target_pairs={{0,1},{1,0},{2,3},{3,2},{4,5},{5,4},{6,7},{7,6},{8,9},{9,8},{10,11... | collective-permute-start | bytes 1179656 | tf_op jit(solution)/shard_map/ppermute | solution.py:317
  42.9 2.0 %collective-permute-start.10 = (bf16[176,256]{1,0:T(8,128)(2,1)S(1)}, bf16[176,256]{1,0:T(8,128)(2,1)S(1)}, u32[]{:S(2)}, u32[]{:S(2)}) collective-permute-start(bf16[176,256]{1,0:T(8,128)(2,1)S(1)} %get-tuple-element.98), channel_id=1, source_target_pairs={{0,1},{1,0},{2,3},{3,2},{4,5},{5,4},{6,7},{7,6},{8,9},{9,8},{10,11... | collective-permute-start | bytes 270344 | tf_op jit(solution)/shard_map/ppermute | solution.py:317
  43.1 1.8 %collective-permute-start.11 = (bf16[176,256]{1,0:T(8,128)(2,1)S(1)}, bf16[176,256]{1,0:T(8,128)(2,1)S(1)}, u32[]{:S(2)}, u32[]{:S(2)}) collective-permute-start(bf16[176,256]{1,0:T(8,128)(2,1)S(1)} %get-tuple-element.99), channel_id=1, source_target_pairs={{0,1},{1,0},{2,3},{3,2},{4,5},{5,4},{6,7},{7,6},{8,9},{9,8},{10,11... | collective-permute-start | bytes 270344 | tf_op jit(solution)/shard_map/ppermute | solution.py:317
  44.9 10.5 %collective-permute-start.14 = (bf16[2,256,256]{2,1,0:T(8,128)(2,1)S(1)}, bf16[2,256,256]{2,1,0:T(8,128)(2,1)S(1)}, u32[]{:S(2)}, u32[]{:S(2)}) collective-permute-start(bf16[2,256,256]{2,1,0:T(8,128)(2,1)S(1)} %get-tuple-element.108), channel_id=1, source_target_pairs={{0,12},{4,0},{8,4},{12,8},{1,13},{5,1},{9,5},{13,9},{2,14},{6,2},{... | collective-permute-start | bytes 786440 | tf_op jit(solution)/shard_map/ppermute | solution.py:313
  46.1 4.6 %collective-permute-start.12 = (bf16[176,256]{1,0:T(8,128)(2,1)S(1)}, bf16[176,256]{1,0:T(8,128)(2,1)S(1)}, u32[]{:S(2)}, u32[]{:S(2)}) collective-permute-start(bf16[176,256]{1,0:T(8,128)(2,1)S(1)} %get-tuple-element.107), channel_id=1, source_target_pairs={{0,2},{1,3},{2,0},{3,1},{4,6},{5,7},{6,4},{7,5},{8,10},{9,11},{10,... | collective-permute-start | bytes 270344 | tf_op jit(solution)/shard_map/ppermute | solution.py:317
  50.7 4.6 %collective-permute-start.13 = (bf16[176,256]{1,0:T(8,128)(2,1)S(1)}, bf16[176,256]{1,0:T(8,128)(2,1)S(1)}, u32[]{:S(2)}, u32[]{:S(2)}) collective-permute-start(bf16[176,256]{1,0:T(8,128)(2,1)S(1)} %shard_map.162.refs_0_), channel_id=1, source_target_pairs={{0,4},{4,0},{8,12},{12,8},{1,5},{5,1},{9,13},{13,9},{2,6},{6,2},{1... | collective-permute-start | bytes 270344 | tf_op jit(solution)/shard_map/ppermute | solution.py:317
  55.3 12.3 %collective-permute-start.15 = (bf16[176,256]{1,0:T(8,128)(2,1)S(1)}, bf16[176,256]{1,0:T(8,128)(2,1)S(1)}, u32[]{:S(2)}, u32[]{:S(2)}) collective-permute-start(bf16[176,256]{1,0:T(8,128)(2,1)S(1)} %shard_map.163.refs_0_), channel_id=1, source_target_pairs={{0,8},{4,12},{8,0},{12,4},{1,9},{5,13},{9,1},{13,5},{2,10},{6,14},... | collective-permute-start | bytes 270344 | tf_op jit(solution)/shard_map/ppermute | solution.py:317
  56.5 15.7 %collective-permute-start.19 = (bf16[2,256,256]{2,1,0:T(8,128)(2,1)S(1)}, bf16[2,256,256]{2,1,0:T(8,128)(2,1)S(1)}, u32[]{:S(2)}, u32[]{:S(2)}) collective-permute-start(bf16[2,256,256]{2,1,0:T(8,128)(2,1)S(1)} %get-tuple-element.115), channel_id=1, source_target_pairs={{0,4},{4,8},{8,12},{12,0},{1,5},{5,9},{9,13},{13,1},{2,6},{6,10},{... | collective-permute-start | bytes 786440 | tf_op jit(solution)/shard_map/ppermute | solution.py:313
  67.6 4.6 %collective-permute-start.17 = (bf16[176,256]{1,0:T(8,128)(2,1)S(1)}, bf16[176,256]{1,0:T(8,128)(2,1)S(1)}, u32[]{:S(2)}, u32[]{:S(2)}) collective-permute-start(bf16[176,256]{1,0:T(8,128)(2,1)S(1)} %shard_map.165.refs_1_), channel_id=1, source_target_pairs={{0,2},{1,3},{2,0},{3,1},{4,6},{5,7},{6,4},{7,5},{8,10},{9,11},{10,... | collective-permute-start | bytes 270344 | tf_op jit(solution)/shard_map/ppermute | solution.py:317
  69.2 4.2 %collective-permute-start.16 = (bf16[176,256]{1,0:T(8,128)(2,1)S(1)}, bf16[176,256]{1,0:T(8,128)(2,1)S(1)}, u32[]{:S(2)}, u32[]{:S(2)}) collective-permute-start(bf16[176,256]{1,0:T(8,128)(2,1)S(1)} %shard_map.165.refs_1_), channel_id=1, source_target_pairs={{0,1},{1,0},{2,3},{3,2},{4,5},{5,4},{6,7},{7,6},{8,9},{9,8},{10,11... | collective-permute-start | bytes 270344 | tf_op jit(solution)/shard_map/ppermute | solution.py:317
  72.2 1.3 %collective-permute-start.18 = (bf16[176,256]{1,0:T(8,128)(2,1)S(1)}, bf16[176,256]{1,0:T(8,128)(2,1)S(1)}, u32[]{:S(2)}, u32[]{:S(2)}) collective-permute-start(bf16[176,256]{1,0:T(8,128)(2,1)S(1)} %collective-permute-done.17.refs_3_), channel_id=1, source_target_pairs={{0,1},{1,0},{2,3},{3,2},{4,5},{5,4},{6,7},{7,6},{8,9},{9,8},{10,11... | collective-permute-start | bytes 270344 | tf_op jit(solution)/shard_map/ppermute | solution.py:317

commit v11 on v10

--- a/solution.py
+++ b/solution.py
@@ -256,7 +256,7 @@
 
 
 def edges_kernel(members, table_ref, w_one_ref, *refs):
-    d_one_refs, d_mixed_refs, (head_ref, tail_ref) = refs[:members], refs[members : 2 * members], refs[2 * members :]
+    d_one_refs, d_mixed_refs, (head_ref, *tail_refs) = refs[:members], refs[members : 2 * members], refs[2 * members :]
     ext = table_ref.shape[0]
     rows = jnp.concatenate([table_ref[:HALO, :], table_ref[ext - HALO :, :]], axis=0)
     for m in range(members):
@@ -264,7 +264,7 @@
         d_mixed_refs[m][...] = d_mixed
         grads = nt_dot(rows, d_mixed).astype(jnp.bfloat16)
         head_ref[m] = grads[:HALO]
-        tail_ref[m] = grads[HALO:]
+        tail_refs[m][...] = grads[HALO:]
 
 
 def sum_kernel(count, *refs):
@@ -300,12 +300,14 @@
         own_ref[m] = nt_dot(table_ref[HALO : HALO + nodes, :], d_mixed_refs[m][...])
 
 
-def finish_kernel(own_ref, from_next_ref, from_prev_ref, out_ref):
-    nodes = own_ref.shape[1]
-    from_next, from_prev = from_next_ref[...].astype(jnp.float32), from_prev_ref[...].astype(jnp.float32)
-    out_ref[:, :HALO] = (own_ref[:, :HALO] + from_prev).astype(jnp.bfloat16)
-    out_ref[:, HALO : nodes - HALO] = own_ref[:, HALO : nodes - HALO].astype(jnp.bfloat16)
-    out_ref[:, nodes - HALO :] = (own_ref[:, nodes - HALO :] + from_next).astype(jnp.bfloat16)
+def finish_kernel(own_ref, from_next_ref, *refs):
+    *from_prev_refs, out_ref = refs
+    members, nodes, _ = own_ref.shape
+    for m in range(members):
+        from_next, from_prev = from_next_ref[m].astype(jnp.float32), from_prev_refs[m][...].astype(jnp.float32)
+        out_ref[m, :HALO] = (own_ref[m, :HALO] + from_prev).astype(jnp.bfloat16)
+        out_ref[m, HALO : nodes - HALO] = own_ref[m, HALO : nodes - HALO].astype(jnp.bfloat16)
+        out_ref[m, nodes - HALO :] = (own_ref[m, nodes - HALO :] + from_next).astype(jnp.bfloat16)
 
 
 def shifted(shard, axis, by):
@@ -408,19 +410,20 @@
         )(*ones, *others)
 
     rims = shape((members, HALO, width), bf16)
-    *d_mixed, head, tail = kernel_call(
+    out = kernel_call(
         lambda *refs: edges_kernel(members, *refs),
-        (mixed_shape,) * members + (rims, rims),
+        (mixed_shape,) * members + (rims,) + (edge,) * members,
         flops=2 * members * slots * width * (hidden + 2 * HALO),
         moved=6 * MIB,
         operands=2 + members,
     )(table, w_one, *d_one)
+    d_mixed, head, tails = out[:members], out[members], out[members + 1 :]
 
     bit = 1
     while bit < ranks:
         received = [swapped(sent, "member", bit) for sent in pieces[1::2]]
         if bit == 1:
-            received, head, tail = lax.optimization_barrier((received, head, tail))
+            received, head, tails = lax.optimization_barrier((received, head, tails))
         pieces = summed(pieces[::2], received)
         bit = 2 * bit
     own = kernel_call(
@@ -431,14 +434,16 @@
         operands=1 + members,
     )(table, *d_mixed)
     from_next = shifted(head, "space", -1)
+    from_prev = [shifted(tail, "space", 1) for tail in tails[:-1]]
     (total,) = pieces
     step = 1
     while step < regions:
+        if 2 * step == regions:
+            total, from_next, from_prev, own = lax.optimization_barrier((total, from_next, from_prev, own))
         (total,) = summed([total], [swapped(total, "space", step)])
         step = 2 * step
-        if step == regions // 2:
-            total, from_next, own, tail = lax.optimization_barrier((total, from_next, own, tail))
-            from_prev = shifted(tail, "space", 1)
+    total, last_tail = lax.optimization_barrier((total, tails[-1]))
+    from_prev = [*from_prev, shifted(last_tail, "space", 1)]
     totals = {0: total}
     bit = 2
     while bit < ranks:
@@ -450,8 +455,8 @@
         shape((members, nodes, width), bf16),
         flops=MIB,
         moved=3 * MIB,
-        operands=3,
-    )(own, from_next, from_prev)
+        operands=2 + members,
+    )(own, from_next, *from_prev)
     totals = [totals[i] for i in range(ranks)]
     totals, latent_grad = lax.optimization_barrier((totals, latent_grad))
     row = shape((1, hidden), f32)

time: 74.5 us -> 75.3 us (1.011)
  waiting for transfers between devices: 27.8 us -> 30 us
  starting transfers between devices: 21.9 us -> 20.4 us
    ppermute x6 -> x7, waiting for transfers between devices: 0.02 us -> 3.73 us  [shifted(): lax.ppermute(shard, axis, [(i, (i + by) % length) for i in range(length)])]
    ppermute x14, waiting for transfers between devices: 27.8 us -> 26.3 us  [swapped(): lax.ppermute(block, axis, [(i, i ^ by) for i in range(lax.axis_size(axis))])]
    ppermute x6 -> x7, starting transfers between devices: 12.4 us -> 11.1 us  [shifted(): lax.ppermute(shard, axis, [(i, (i + by) % length) for i in range(length)])]
  transfers between devices with their start and end apart: 20 -> 21, of which waited for: 9 -> 9; matrix products, arithmetic and copies ran while one was open for 0% -> 0% of each run, Pallas kernels for 22% -> 22%
where the time goes in v11:
time: 75.3 us; the launch traced here: 75.1 us
  waiting for transfers between devices  30 us (40%)
  Pallas kernels  22.5 us (30%)
  starting transfers between devices  20.4 us (27%)
  local copies, waits for them, and re-layouts  1.27 us (2%)
  between operations  0.87 us (1%)
    ppermute x14, waiting for transfers between devices, swapped(): lax.ppermute(block, axis, [(i, i ^ by) for i in range(lax.axis_size(axis))])  26.3 us
    ppermute x7, starting transfers between devices, shifted(): lax.ppermute(shard, axis, [(i, (i + by) % length) for i in range(length)])  11.1 us
    ppermute x14, starting transfers between devices, swapped(): lax.ppermute(block, axis, [(i, i ^ by) for i in range(lax.axis_size(axis))])  9.32 us
    pallas_call x2, Pallas kernels, per_device(): kernel_call(lambda *refs: forward_kernel(m, *refs), (mixed_shape,) + (sav...  6.56 us
    pallas_call x2, Pallas kernels, scored(): kernel_call(lambda *refs: score_kernel(members, len(others), members * ra...  4.58 us
    ppermute x7, waiting for transfers between devices, shifted(): lax.ppermute(shard, axis, [(i, (i + by) % length) for i in range(length)])  3.73 us
    pallas_call x1, Pallas kernels, per_device(): kernel_call(table_kernel, (shape((ext, slots), bf16), shape((width, slots...  3.11 us
    pallas_call x1, Pallas kernels, per_device(): kernel_call(lambda *refs: backward_kernel(members, ranks, *refs), (saved_...  2.85 us
  transfers between devices with their start and end apart: 21, of which 9 were waited for; matrix products, arithmetic and copies ran while one was open for 0% of the time, Pallas kernels for 22%

profile of v11, /device:TPU:0, one launch (start us, length us, event | category | flops | bytes accessed | tf_op | source)
XLA Modules:
  0.0 75.1 jit_solution(15125114838492820709)
XLA Ops:
  0.6 0.0 copy-start.6
  0.6 0.0 copy-start.7
  0.7 1.2 %copy-done.7 = bf16[2,1024,256]{2,1,0:T(8,128)(2,1)S(1)} copy-done((bf16[2,1024,256]{2,1,0:T(8,128)(2,1)S(1)}, bf16[2,1024,256]{2,1,0:T(8,128)(2,1)}, u32[]{:S(2)}) %copy-start.7) | copy-done | bytes 1048600
  1.9 0.1 shard_map.153
  2.0 0.0 copy-start
  2.0 0.0 copy-start.1
  2.0 0.0 copy-start.2
  2.0 0.0 copy-start.4
  2.0 0.0 copy-start.5
  2.0 3.1 %collective-permute-start = (bf16[256,256]{1,0:T(8,128)(2,1)S(1)}, bf16[256,256]{1,0:T(8,128)(2,1)S(1)}, u32[]{:S(2)}, u32[]{:S(2)}) collective-permute-start(bf16[256,256]{1,0:T(8,128)(2,1)S(1)} %get-tuple-element.74), channel_id=1, source_target_pairs={{0,4},{4,8},{8,12},{12,0},{1,5},{5,9},{9,13},{13,1},{2,6},{6,10},{... | collective-permute-start | bytes 393224 | tf_op jit(solution)/shard_map/ppermute | solution.py:315
  5.1 2.1 %collective-permute-start.1 = (bf16[256,256]{1,0:T(8,128)(2,1)S(1)}, bf16[256,256]{1,0:T(8,128)(2,1)S(1)}, u32[]{:S(2)}, u32[]{:S(2)}) collective-permute-start(bf16[256,256]{1,0:T(8,128)(2,1)S(1)} %get-tuple-element.75), channel_id=1, source_target_pairs={{0,12},{4,0},{8,4},{12,8},{1,13},{5,1},{9,5},{13,9},{2,14},{6,2},{... | collective-permute-start | bytes 393224 | tf_op jit(solution)/shard_map/ppermute | solution.py:315
  7.2 0.0 copy-done.6
  7.2 3.1 %shard_map.154 = (bf16[1536,1536]{1,0:T(8,128)(2,1)S(1)}, f32[256,1536]{1,0:T(8,128)S(1)}, bf16[256,256]{1,0:T(8,128)(2,1)S(1)}, bf16[256,256]{1,0:T(8,128)(2,1)S(1)}) custom-call(s32[1]{0:T(128)} %bitcast.1.region_ref.refs_0_, s32[1]{0:T(128)} %bitcast.rank_ref.refs_1_.refs_0_, s32[4]{0:T(128)S(1)} %copy-done.6, s32[4,1536]{1,0:T(4,128)S(1)} %copy-done.8, ...), custom_call_target="tpu_custom_call" | custom-call | flops 805306368 | bytes 12582912 | tf_op jit(solution)/shard_map/pallas_call | solution.py:342
  10.3 0.1 collective-permute-start.2
  10.4 3.8 %collective-permute-start.3 = (bf16[256,256]{1,0:T(8,128)(2,1)S(1)}, bf16[256,256]{1,0:T(8,128)(2,1)S(1)}, u32[]{:S(2)}, u32[]{:S(2)}) collective-permute-start(bf16[256,256]{1,0:T(8,128)(2,1)S(1)} %get-tuple-element.78), channel_id=1, source_target_pairs={{0,12},{4,0},{8,4},{12,8},{1,13},{5,1},{9,5},{13,9},{2,14},{6,2},{... | collective-permute-start | bytes 393224 | tf_op jit(solution)/shard_map/ppermute | solution.py:315
  14.2 0.0 collective-permute-done.refs_2_
  14.2 0.0 collective-permute-done.1.refs_3_
  14.2 0.0 copy-done
  14.3 2.9 %shard_map.155 = (bf16[256,1536]{1,0:T(8,128)(2,1)S(1)}, bf16[256,1536]{1,0:T(8,128)(2,1)S(1)}, bf16[256,1536]{1,0:T(8,128)(2,1)S(1)}, bf16[256,1536]{1,0:T(8,12...) custom-call(f32[256,1536]{1,0:T(8,128)S(1)} %get-tuple-element.72.refs_0_, ...), custom_call_target="tpu_custom_call" | custom-call | flops 905969664 | bytes 8388608 | tf_op jit(solution)/shard_map/pallas_call | solution.py:359
  17.1 0.0 copy-start.3
  17.1 1.7 %collective-permute-start.7 = (bf16[128,1536]{1,0:T(8,128)(2,1)S(1)}, bf16[128,1536]{1,0:T(8,128)(2,1)S(1)}, u32[]{:S(2)}, u32[]{:S(2)}) collective-permute-start(bf16[128,1536]{1,0:T(8,128)(2,1)S(1)} %get-tuple-element.76.refs_2_), channel_id=1, source_target_pairs={{0,2},{1,3},{2,0},{3,1},{4,6},{5,7},{6,4},{7,5},{8,10},{9,11},{10,... | collective-permute-start | bytes 1179656 | tf_op jit(solution)/shard_map/ppermute | solution.py:319
  18.9 0.0 collective-permute-start.5
  18.9 0.0 collective-permute-done.2.refs_2_
  18.9 0.0 collective-permute-done.3.refs_3_
  18.9 3.7 %shard_map.156 = (bf16[256,1536]{1,0:T(8,128)(2,1)S(1)}, bf16[256,1536]{1,0:T(8,128)(2,1)S(1)}, bf16[256,1536]{1,0:T(8,128)(2,1)S(1)}, bf16[256,1536]{1,0:T(8,12...) custom-call(bf16[2,1024,256]{2,1,0:T(8,128)(2,1)S(1)} %get-tuple-element.71.latent_ref.refs_0_, ...), custom_call_target="tpu_custom_call" | custom-call | flops 1711276032 | bytes 8388608 | tf_op jit(solution)/shard_map/pallas_call | solution.py:359
  22.6 0.6 collective-permute-start.6
  23.1 0.8 %collective-permute-start.4 = (bf16[128,1536]{1,0:T(8,128)(2,1)S(1)}, bf16[128,1536]{1,0:T(8,128)(2,1)S(1)}, u32[]{:S(2)}, u32[]{:S(2)}) collective-permute-start(bf16[128,1536]{1,0:T(8,128)(2,1)S(1)} %get-tuple-element.79.refs_3_), channel_id=1, source_target_pairs={{0,2},{1,3},{2,0},{3,1},{4,6},{5,7},{6,4},{7,5},{8,10},{9,11},{10,... | collective-permute-start | bytes 1179656 | tf_op jit(solution)/shard_map/ppermute | solution.py:319
  23.9 4.6 %collective-permute-done.7.refs_6_ = bf16[128,1536]{1,0:T(8,128)(2,1)S(1)} collective-permute-done((bf16[128,1536]{1,0:T(8,128)(2,1)S(1)}, bf16[128,1536]{1,0:T(8,128)(2,1)S(1)}, u32[]{:S(2)}, u32[]{:S(2)}) %collective-permute-start.7) | collective-permute-done | bytes 393248 | tf_op jit(solution)/shard_map/ppermute | solution.py:319
  28.6 0.0 collective-permute-done.5.refs_4_
  28.6 0.0 collective-permute-done.6.refs_5_
  28.6 2.5 %shard_map.157 = (f32[128,1536]{1,0:T(8,128)S(1)}, f32[128,1536]{1,0:T(8,128)S(1)}, f32[1,128]{1,0:T(1,128)S(1)}) custom-call(s32[1]{0:T(128)} %bitcast.1.region_ref.refs_0_, s32[4]{0:T(128)S(1)} %copy-done.6, bf16[128,1536]{1,0:T(8,128)(2,1)S(1)} %get-tuple-element.76.refs_2_, bf16[128,1536]{1,0:T(8,128)(2,1)S(1)} %get-tuple-element.79.refs_3_, ...), custom_call_target="tpu_custom_call" | custom-call | flops 4194304 | bytes 2097152 | tf_op jit(solution)/shard_map/pallas_call | solution.py:377
  31.1 4.5 %collective-permute-done.4.refs_4_ = bf16[128,1536]{1,0:T(8,128)(2,1)S(1)} collective-permute-done((bf16[128,1536]{1,0:T(8,128)(2,1)S(1)}, bf16[128,1536]{1,0:T(8,128)(2,1)S(1)}, u32[]{:S(2)}, u32[]{:S(2)}) %collective-permute-start.4) | collective-permute-done | bytes 393248 | tf_op jit(solution)/shard_map/ppermute | solution.py:319
  35.7 0.0 collective-permute-start.8
  35.7 0.5 collective-permute-start.9
  36.2 1.2 %collective-permute-done.8.refs_5_ = bf16[128,1536]{1,0:T(8,128)(2,1)S(1)} collective-permute-done((bf16[128,1536]{1,0:T(8,128)(2,1)S(1)}, bf16[128,1536]{1,0:T(8,128)(2,1)S(1)}, u32[]{:S(2)}, u32[]{:S(2)}) %collective-permute-start.8) | collective-permute-done | bytes 393248 | tf_op jit(solution)/shard_map/ppermute | solution.py:319
  37.4 0.6 collective-permute-done.9.refs_6_
  37.9 2.1 %shard_map.158 = (bf16[128,1536]{1,0:T(8,128)(2,1)S(1)}, bf16[128,1536]{1,0:T(8,128)(2,1)S(1)}, f32[1,128]{1,0:T(1,128)S(1)}) custom-call(s32[1]{0:T(128)} %bitcast.1.region_ref.refs_0_, s32[4]{0:T(128)S(1)} %copy-done.6, bf16[128,1536]{1,0:T(8,128)(2,1)S(1)} %get-tuple-element.76.refs_2_, bf16[128,1536]{1,0:T(8,128)(2,1)S(1)} %get-tuple-element.79.refs_3_, ...), custom_call_target="tpu_custom_call" | custom-call | flops 4194304 | bytes 2097152 | tf_op jit(solution)/shard_map/pallas_call | solution.py:377
  40.0 2.9 %shard_map.159 = (bf16[256,1536]{1,0:T(8,128)(2,1)S(1)}, bf16[256,1536]{1,0:T(8,128)(2,1)S(1)}, bf16[176,256]{1,0:T(8,128)(2,1)S(1)}, bf16[176,256]{1,0:T(8,128)...) custom-call(s32[1]{0:T(128)} %bitcast.1.region_ref.refs_0_, s32[1]{0:T(128)} %bitcast.rank_ref.refs_1_.refs_0_, ...), custom_call_target="tpu_custom_call" | custom-call | flops 2013265920 | bytes 10485760 | tf_op jit(solution)/shard_map/pallas_call | solution.py:396
  42.9 0.2 collective-permute-start.10
  43.1 0.4 collective-permute-start.11
  43.4 1.4 %shard_map.160 = (bf16[256,1536]{1,0:T(8,128)(2,1)S(1)}, bf16[256,1536]{1,0:T(8,128)(2,1)S(1)}, bf16[2,256,256]{2,1,0:T(8,128)(2,1)S(1)}, bf16[256,256]{1,0:T(8,128)(2,1)S(1)}, bf16[256,256]{1,0:T(8,128)(2,1)S(1)}) custom-call(bf16[1536,1536]{1,0:T(8,128)(2,1)S(1)} %get-tuple-element.73.refs_1_.refs_0_.table_ref, bf16[256,256]{1,0:T(8,128)(2,1)S(1)} %copy-done.1, ...), custom_call_target="tpu_custom_call" | custom-call | flops 1207959552 | bytes 6291456 | tf_op jit(solution)/shard_map/pallas_call | solution.py:413
  44.8 0.0 collective-permute-done.10.refs_2_
  44.9 0.0 collective-permute-done.11.refs_3_
  44.9 1.2 %collective-permute-start.14 = (bf16[2,256,256]{2,1,0:T(8,128)(2,1)S(1)}, bf16[2,256,256]{2,1,0:T(8,128)(2,1)S(1)}, u32[]{:S(2)}, u32[]{:S(2)}) collective-permute-start(bf16[2,256,256]{2,1,0:T(8,128)(2,1)S(1)} %get-tuple-element.113), channel_id=1, source_target_pairs={{0,12},{4,0},{8,4},{12,8},{1,13},{5,1},{9,5},{13,9},{2,14},{6,2},{... | collective-permute-start | bytes 786440 | tf_op jit(solution)/shard_map/ppermute | solution.py:315
  46.1 1.6 %collective-permute-start.12 = (bf16[176,256]{1,0:T(8,128)(2,1)S(1)}, bf16[176,256]{1,0:T(8,128)(2,1)S(1)}, u32[]{:S(2)}, u32[]{:S(2)}) collective-permute-start(bf16[176,256]{1,0:T(8,128)(2,1)S(1)} %get-tuple-element.112), channel_id=1, source_target_pairs={{0,2},{1,3},{2,0},{3,1},{4,6},{5,7},{6,4},{7,5},{8,10},{9,11},{10,... | collective-permute-start | bytes 270344 | tf_op jit(solution)/shard_map/ppermute | solution.py:319
  47.6 0.9 %collective-permute-start.15 = (bf16[256,256]{1,0:T(8,128)(2,1)S(1)}, bf16[256,256]{1,0:T(8,128)(2,1)S(1)}, u32[]{:S(2)}, u32[]{:S(2)}) collective-permute-start(bf16[256,256]{1,0:T(8,128)(2,1)S(1)} %get-tuple-element.114), channel_id=1, source_target_pairs={{0,4},{4,8},{8,12},{12,0},{1,5},{5,9},{9,13},{13,1},{2,6},{6,10},{... | collective-permute-start | bytes 393224 | tf_op jit(solution)/shard_map/ppermute | solution.py:315
  48.5 2.1 %collective-permute-done.12.refs_1_ = bf16[176,256]{1,0:T(8,128)(2,1)S(1)} collective-permute-done((bf16[176,256]{1,0:T(8,128)(2,1)S(1)}, bf16[176,256]{1,0:T(8,128)(2,1)S(1)}, u32[]{:S(2)}, u32[]{:S(2)}) %collective-permute-start.12) | collective-permute-done | bytes 90144 | tf_op jit(solution)/shard_map/ppermute | solution.py:319
  50.7 1.0 %collective-permute-start.13 = (bf16[176,256]{1,0:T(8,128)(2,1)S(1)}, bf16[176,256]{1,0:T(8,128)(2,1)S(1)}, u32[]{:S(2)}, u32[]{:S(2)}) collective-permute-start(bf16[176,256]{1,0:T(8,128)(2,1)S(1)} %shard_map.162.refs_0_), channel_id=1, source_target_pairs={{0,4},{4,0},{8,12},{12,8},{1,5},{5,1},{9,13},{13,9},{2,6},{6,2},{1... | collective-permute-start | bytes 270344 | tf_op jit(solution)/shard_map/ppermute | solution.py:319
  51.7 1.8 %shard_map.164.own_ref = f32[2,1024,256]{2,1,0:T(8,128)S(1)} custom-call(bf16[1536,1536]{1,0:T(8,128)(2,1)S(1)} %get-tuple-element.73.refs_1_.refs_0_.table_ref, bf16[256,1536]{1,0:T(8,128)(2,1)S(1)} %get-tuple-element.115.refs_0_, bf16[256,1536]{1,0:T(8,128)(2,1)S(1)} %get-tuple-element.116.refs_1_), custom_call_target="tpu_custom_call" | custom-call | flops 1610612736 | bytes 6291456 | tf_op jit(solution)/shard_map/pallas_call | solution.py:429
  53.5 4.5 %collective-permute-done.13.refs_1_ = bf16[176,256]{1,0:T(8,128)(2,1)S(1)} collective-permute-done((bf16[176,256]{1,0:T(8,128)(2,1)S(1)}, bf16[176,256]{1,0:T(8,128)(2,1)S(1)}, u32[]{:S(2)}, u32[]{:S(2)}) %collective-permute-start.13) | collective-permute-done | bytes 90144 | tf_op jit(solution)/shard_map/ppermute | solution.py:319
  58.0 0.0 collective-permute-done.15.refs_0_
  58.0 0.0 collective-permute-done.14.from_next_ref
  58.1 1.0 %collective-permute-start.16 = (bf16[176,256]{1,0:T(8,128)(2,1)S(1)}, bf16[176,256]{1,0:T(8,128)(2,1)S(1)}, u32[]{:S(2)}, u32[]{:S(2)}) collective-permute-start(bf16[176,256]{1,0:T(8,128)(2,1)S(1)} %shard_map.163.refs_0_), channel_id=1, source_target_pairs={{0,8},{4,12},{8,0},{12,4},{1,9},{5,13},{9,1},{13,5},{2,10},{6,14},... | collective-permute-start | bytes 270344 | tf_op jit(solution)/shard_map/ppermute | solution.py:319
  59.1 5.7 %collective-permute-done.16.refs_1_ = bf16[176,256]{1,0:T(8,128)(2,1)S(1)} collective-permute-done((bf16[176,256]{1,0:T(8,128)(2,1)S(1)}, bf16[176,256]{1,0:T(8,128)(2,1)S(1)}, u32[]{:S(2)}, u32[]{:S(2)}) %collective-permute-start.16) | collective-permute-done | bytes 90144 | tf_op jit(solution)/shard_map/ppermute | solution.py:319
  64.8 1.6 %collective-permute-start.18 = (bf16[176,256]{1,0:T(8,128)(2,1)S(1)}, bf16[176,256]{1,0:T(8,128)(2,1)S(1)}, u32[]{:S(2)}, u32[]{:S(2)}) collective-permute-start(bf16[176,256]{1,0:T(8,128)(2,1)S(1)} %shard_map.165.refs_1_), channel_id=1, source_target_pairs={{0,2},{1,3},{2,0},{3,1},{4,6},{5,7},{6,4},{7,5},{8,10},{9,11},{10,... | collective-permute-start | bytes 270344 | tf_op jit(solution)/shard_map/ppermute | solution.py:319
  66.4 0.0 collective-permute-start.20
  66.4 0.0 collective-permute-start.17
  66.4 3.0 %collective-permute-done.18.refs_3_ = bf16[176,256]{1,0:T(8,128)(2,1)S(1)} collective-permute-done((bf16[176,256]{1,0:T(8,128)(2,1)S(1)}, bf16[176,256]{1,0:T(8,128)(2,1)S(1)}, u32[]{:S(2)}, u32[]{:S(2)}) %collective-permute-start.18) | collective-permute-done | bytes 90144 | tf_op jit(solution)/shard_map/ppermute | solution.py:319
  69.4 0.0 collective-permute-start.19
  69.4 3.7 %collective-permute-done.20.refs_1_ = bf16[256,256]{1,0:T(8,128)(2,1)S(1)} collective-permute-done((bf16[256,256]{1,0:T(8,128)(2,1)S(1)}, bf16[256,256]{1,0:T(8,128)(2,1)S(1)}, u32[]{:S(2)}, u32[]{:S(2)}) %collective-permute-start.20) | collective-permute-done | bytes 131104 | tf_op jit(solution)/shard_map/ppermute | solution.py:315
  73.1 1.1 %shard_map.166 = bf16[2,1024,256]{2,1,0:T(8,128)(2,1)} custom-call(f32[2,1024,256]{2,1,0:T(8,128)S(1)} %shard_map.164.own_ref, bf16[2,256,256]{2,1,0:T(8,128)(2,1)S(1)} %collective-permute-done.14.from_next_ref, bf16[256,256]{1,0:T(8,128)(2,1)S(1)} %collective-permute-done.15.refs_0_, bf16[256,256]{1,0:T(8,128)(2,1)S(1)} %collective-permute-done.20.refs_1_), custom_call_target="tpu_custom_call" | custom-call | flops 1048576 | bytes 3145728 | tf_op jit(solution)/shard_map/pallas_call | solution.py:453
  74.2 0.0 collective-permute-done.17.refs_2_
  74.2 0.0 collective-permute-done.19.refs_4_
  74.2 0.9 %shard_map.167 = (f32[256,256]{1,0:T(8,128)}, f32[1,256]{1,0:T(1,128)}, f32[256,256]{1,0:T(8,128)}, f32[1,256]{1,0:T(1,128)}, f32[256,128]{1,0:T(8,128)}, /*index=5*/f32[1,4]{1,0:T(1,128)}) custom-call(s32[1]{0:T(128)} %bitcast.rank_ref.refs_1_.refs_0_, bf16[176,256]{1,0:T(8,128)(2,1)S(1)} %shard_map.165.refs_1_, ...), custom_call_target="tpu_custom_call" | custom-call | flops 1048576 | bytes 2097152 | tf_op jit(solution)/shard_map/pallas_call | solution.py:463
  (13 shorter events, 0.1 us)
Async XLA Ops:
  0.6 6.6 %copy-start.6 = (s32[4]{0:T(128)S(1)}, s32[4]{0:T(128)}, u32[]{:S(2)}) copy-start(s32[4]{0:T(128)} %refs_1_.4) | copy-start | bytes 52
  0.6 1.2 %copy-start.7 = (bf16[2,1024,256]{2,1,0:T(8,128)(2,1)S(1)}, bf16[2,1024,256]{2,1,0:T(8,128)(2,1)}, u32[]{:S(2)}) copy-start(bf16[2,1024,256]{2,1,0:T(8,128)(2,1)} %latent_ref.1) | copy-start | bytes 3145732
  1.9 5.3 %copy-start.8 = (s32[4,1536]{1,0:T(4,128)S(1)}, s32[4,1536]{1,0:T(4,128)}, u32[]{:S(2)}) copy-start(s32[4,1536]{1,0:T(4,128)} %nbr_ref.1) | copy-start | bytes 73732
  1.9 5.3 %copy-start.9 = (f32[4,1536]{1,0:T(4,128)S(1)}, f32[4,1536]{1,0:T(4,128)}, u32[]{:S(2)}) copy-start(f32[4,1536]{1,0:T(4,128)} %weight_ref.1) | copy-start | bytes 73732
  2.0 12.2 %copy-start = (bf16[256,256]{1,0:T(8,128)(2,1)S(1)}, bf16[256,256]{1,0:T(8,128)(2,1)}, u32[]{:S(2)}) copy-start(bf16[256,256]{1,0:T(8,128)(2,1)} %refs_2_.1) | copy-start | bytes 393220
  2.0 12.2 %copy-start.1 = (bf16[256,256]{1,0:T(8,128)(2,1)S(1)}, bf16[256,256]{1,0:T(8,128)(2,1)}, u32[]{:S(2)}) copy-start(bf16[256,256]{1,0:T(8,128)(2,1)} %refs_1_.5) | copy-start | bytes 393220
  2.0 12.2 %copy-start.2 = (bf16[256,128]{1,0:T(8,128)(2,1)S(1)}, bf16[256,128]{1,0:T(8,128)(2,1)}, u32[]{:S(2)}) copy-start(bf16[256,128]{1,0:T(8,128)(2,1)} %refs_3_.1) | copy-start | bytes 196612
  2.0 12.2 %copy-start.4 = (f32[256]{0:T(256)S(1)}, f32[256]{0:T(256)}, u32[]{:S(2)}) copy-start(f32[256]{0:T(256)} %param.16) | copy-start | bytes 3076
  2.0 12.2 %copy-start.5 = (f32[256]{0:T(256)S(1)}, f32[256]{0:T(256)}, u32[]{:S(2)}) copy-start(f32[256]{0:T(256)} %param.18) | copy-start | bytes 3076
  2.0 12.2 %collective-permute-start = (bf16[256,256]{1,0:T(8,128)(2,1)S(1)}, bf16[256,256]{1,0:T(8,128)(2,1)S(1)}, u32[]{:S(2)}, u32[]{:S(2)}) collective-permute-start(bf16[256,256]{1,0:T(8,128)(2,1)S(1)} %get-tuple-element.74), channel_id=1, source_target_pairs={{0,4},{4,8},{8,12},{12,0},{1,5},{5,9},{9,13},{13,1},{2,6},{6,10},{... | collective-permute-start | bytes 393224 | tf_op jit(solution)/shard_map/ppermute | solution.py:315
  5.1 9.1 %collective-permute-start.1 = (bf16[256,256]{1,0:T(8,128)(2,1)S(1)}, bf16[256,256]{1,0:T(8,128)(2,1)S(1)}, u32[]{:S(2)}, u32[]{:S(2)}) collective-permute-start(bf16[256,256]{1,0:T(8,128)(2,1)S(1)} %get-tuple-element.75), channel_id=1, source_target_pairs={{0,12},{4,0},{8,4},{12,8},{1,13},{5,1},{9,5},{13,9},{2,14},{6,2},{... | collective-permute-start | bytes 393224 | tf_op jit(solution)/shard_map/ppermute | solution.py:315
  10.3 8.5 %collective-permute-start.2 = (bf16[256,256]{1,0:T(8,128)(2,1)S(1)}, bf16[256,256]{1,0:T(8,128)(2,1)S(1)}, u32[]{:S(2)}, u32[]{:S(2)}) collective-permute-start(bf16[256,256]{1,0:T(8,128)(2,1)S(1)} %get-tuple-element.77), channel_id=1, source_target_pairs={{0,4},{4,8},{8,12},{12,0},{1,5},{5,9},{9,13},{13,1},{2,6},{6,10},{... | collective-permute-start | bytes 393224 | tf_op jit(solution)/shard_map/ppermute | solution.py:315
  10.4 8.5 %collective-permute-start.3 = (bf16[256,256]{1,0:T(8,128)(2,1)S(1)}, bf16[256,256]{1,0:T(8,128)(2,1)S(1)}, u32[]{:S(2)}, u32[]{:S(2)}) collective-permute-start(bf16[256,256]{1,0:T(8,128)(2,1)S(1)} %get-tuple-element.78), channel_id=1, source_target_pairs={{0,12},{4,0},{8,4},{12,8},{1,13},{5,1},{9,5},{13,9},{2,14},{6,2},{... | collective-permute-start | bytes 393224 | tf_op jit(solution)/shard_map/ppermute | solution.py:315
  17.1 11.5 %copy-start.3 = (bf16[1536,128]{1,0:T(8,128)(2,1)S(1)}, bf16[1536,128]{1,0:T(8,128)(2,1)}, u32[]{:S(2)}) copy-start(bf16[1536,128]{1,0:T(8,128)(2,1)} %refs_7_.1) | copy-start | bytes 1179652
  17.1 11.4 %collective-permute-start.7 = (bf16[128,1536]{1,0:T(8,128)(2,1)S(1)}, bf16[128,1536]{1,0:T(8,128)(2,1)S(1)}, u32[]{:S(2)}, u32[]{:S(2)}) collective-permute-start(bf16[128,1536]{1,0:T(8,128)(2,1)S(1)} %get-tuple-element.76.refs_2_), channel_id=1, source_target_pairs={{0,2},{1,3},{2,0},{3,1},{4,6},{5,7},{6,4},{7,5},{8,10},{9,11},{10,... | collective-permute-start | bytes 1179656 | tf_op jit(solution)/shard_map/ppermute | solution.py:319
  18.9 9.7 %collective-permute-start.5 = (bf16[128,1536]{1,0:T(8,128)(2,1)S(1)}, bf16[128,1536]{1,0:T(8,128)(2,1)S(1)}, u32[]{:S(2)}, u32[]{:S(2)}) collective-permute-start(bf16[128,1536]{1,0:T(8,128)(2,1)S(1)} %get-tuple-element.76.refs_2_), channel_id=1, source_target_pairs={{0,1},{1,0},{2,3},{3,2},{4,5},{5,4},{6,7},{7,6},{8,9},{9,8},{10,11... | collective-permute-start | bytes 1179656 | tf_op jit(solution)/shard_map/ppermute | solution.py:319
  22.6 6.0 %collective-permute-start.6 = (bf16[128,1536]{1,0:T(8,128)(2,1)S(1)}, bf16[128,1536]{1,0:T(8,128)(2,1)S(1)}, u32[]{:S(2)}, u32[]{:S(2)}) collective-permute-start(bf16[128,1536]{1,0:T(8,128)(2,1)S(1)} %get-tuple-element.79.refs_3_), channel_id=1, source_target_pairs={{0,1},{1,0},{2,3},{3,2},{4,5},{5,4},{6,7},{7,6},{8,9},{9,8},{10,11... | collective-permute-start | bytes 1179656 | tf_op jit(solution)/shard_map/ppermute | solution.py:319
  23.1 12.5 %collective-permute-start.4 = (bf16[128,1536]{1,0:T(8,128)(2,1)S(1)}, bf16[128,1536]{1,0:T(8,128)(2,1)S(1)}, u32[]{:S(2)}, u32[]{:S(2)}) collective-permute-start(bf16[128,1536]{1,0:T(8,128)(2,1)S(1)} %get-tuple-element.79.refs_3_), channel_id=1, source_target_pairs={{0,2},{1,3},{2,0},{3,1},{4,6},{5,7},{6,4},{7,5},{8,10},{9,11},{10,... | collective-permute-start | bytes 1179656 | tf_op jit(solution)/shard_map/ppermute | solution.py:319
  35.7 1.7 %collective-permute-start.8 = (bf16[128,1536]{1,0:T(8,128)(2,1)S(1)}, bf16[128,1536]{1,0:T(8,128)(2,1)S(1)}, u32[]{:S(2)}, u32[]{:S(2)}) collective-permute-start(bf16[128,1536]{1,0:T(8,128)(2,1)S(1)} %collective-permute-done.7.refs_6_), channel_id=1, source_target_pairs={{0,1},{1,0},{2,3},{3,2},{4,5},{5,4},{6,7},{7,6},{8,9},{9,8},{10,11... | collective-permute-start | bytes 1179656 | tf_op jit(solution)/shard_map/ppermute | solution.py:319
  35.7 2.3 %collective-permute-start.9 = (bf16[128,1536]{1,0:T(8,128)(2,1)S(1)}, bf16[128,1536]{1,0:T(8,128)(2,1)S(1)}, u32[]{:S(2)}, u32[]{:S(2)}) collective-permute-start(bf16[128,1536]{1,0:T(8,128)(2,1)S(1)} %collective-permute-done.4.refs_4_), channel_id=1, source_target_pairs={{0,1},{1,0},{2,3},{3,2},{4,5},{5,4},{6,7},{7,6},{8,9},{9,8},{10,11... | collective-permute-start | bytes 1179656 | tf_op jit(solution)/shard_map/ppermute | solution.py:319
  42.9 2.0 %collective-permute-start.10 = (bf16[176,256]{1,0:T(8,128)(2,1)S(1)}, bf16[176,256]{1,0:T(8,128)(2,1)S(1)}, u32[]{:S(2)}, u32[]{:S(2)}) collective-permute-start(bf16[176,256]{1,0:T(8,128)(2,1)S(1)} %get-tuple-element.102), channel_id=1, source_target_pairs={{0,1},{1,0},{2,3},{3,2},{4,5},{5,4},{6,7},{7,6},{8,9},{9,8},{10,11... | collective-permute-start | bytes 270344 | tf_op jit(solution)/shard_map/ppermute | solution.py:319
  43.1 1.8 %collective-permute-start.11 = (bf16[176,256]{1,0:T(8,128)(2,1)S(1)}, bf16[176,256]{1,0:T(8,128)(2,1)S(1)}, u32[]{:S(2)}, u32[]{:S(2)}) collective-permute-start(bf16[176,256]{1,0:T(8,128)(2,1)S(1)} %get-tuple-element.103), channel_id=1, source_target_pairs={{0,1},{1,0},{2,3},{3,2},{4,5},{5,4},{6,7},{7,6},{8,9},{9,8},{10,11... | collective-permute-start | bytes 270344 | tf_op jit(solution)/shard_map/ppermute | solution.py:319
  44.9 13.2 %collective-permute-start.14 = (bf16[2,256,256]{2,1,0:T(8,128)(2,1)S(1)}, bf16[2,256,256]{2,1,0:T(8,128)(2,1)S(1)}, u32[]{:S(2)}, u32[]{:S(2)}) collective-permute-start(bf16[2,256,256]{2,1,0:T(8,128)(2,1)S(1)} %get-tuple-element.113), channel_id=1, source_target_pairs={{0,12},{4,0},{8,4},{12,8},{1,13},{5,1},{9,5},{13,9},{2,14},{6,2},{... | collective-permute-start | bytes 786440 | tf_op jit(solution)/shard_map/ppermute | solution.py:315
  46.1 4.6 %collective-permute-start.12 = (bf16[176,256]{1,0:T(8,128)(2,1)S(1)}, bf16[176,256]{1,0:T(8,128)(2,1)S(1)}, u32[]{:S(2)}, u32[]{:S(2)}) collective-permute-start(bf16[176,256]{1,0:T(8,128)(2,1)S(1)} %get-tuple-element.112), channel_id=1, source_target_pairs={{0,2},{1,3},{2,0},{3,1},{4,6},{5,7},{6,4},{7,5},{8,10},{9,11},{10,... | collective-permute-start | bytes 270344 | tf_op jit(solution)/shard_map/ppermute | solution.py:319
  47.6 10.4 %collective-permute-start.15 = (bf16[256,256]{1,0:T(8,128)(2,1)S(1)}, bf16[256,256]{1,0:T(8,128)(2,1)S(1)}, u32[]{:S(2)}, u32[]{:S(2)}) collective-permute-start(bf16[256,256]{1,0:T(8,128)(2,1)S(1)} %get-tuple-element.114), channel_id=1, source_target_pairs={{0,4},{4,8},{8,12},{12,0},{1,5},{5,9},{9,13},{13,1},{2,6},{6,10},{... | collective-permute-start | bytes 393224 | tf_op jit(solution)/shard_map/ppermute | solution.py:315
  50.7 7.3 %collective-permute-start.13 = (bf16[176,256]{1,0:T(8,128)(2,1)S(1)}, bf16[176,256]{1,0:T(8,128)(2,1)S(1)}, u32[]{:S(2)}, u32[]{:S(2)}) collective-permute-start(bf16[176,256]{1,0:T(8,128)(2,1)S(1)} %shard_map.162.refs_0_), channel_id=1, source_target_pairs={{0,4},{4,0},{8,12},{12,8},{1,5},{5,1},{9,13},{13,9},{2,6},{6,2},{1... | collective-permute-start | bytes 270344 | tf_op jit(solution)/shard_map/ppermute | solution.py:319
  58.1 6.7 %collective-permute-start.16 = (bf16[176,256]{1,0:T(8,128)(2,1)S(1)}, bf16[176,256]{1,0:T(8,128)(2,1)S(1)}, u32[]{:S(2)}, u32[]{:S(2)}) collective-permute-start(bf16[176,256]{1,0:T(8,128)(2,1)S(1)} %shard_map.163.refs_0_), channel_id=1, source_target_pairs={{0,8},{4,12},{8,0},{12,4},{1,9},{5,13},{9,1},{13,5},{2,10},{6,14},... | collective-permute-start | bytes 270344 | tf_op jit(solution)/shard_map/ppermute | solution.py:319
  64.8 4.6 %collective-permute-start.18 = (bf16[176,256]{1,0:T(8,128)(2,1)S(1)}, bf16[176,256]{1,0:T(8,128)(2,1)S(1)}, u32[]{:S(2)}, u32[]{:S(2)}) collective-permute-start(bf16[176,256]{1,0:T(8,128)(2,1)S(1)} %shard_map.165.refs_1_), channel_id=1, source_target_pairs={{0,2},{1,3},{2,0},{3,1},{4,6},{5,7},{6,4},{7,5},{8,10},{9,11},{10,... | collective-permute-start | bytes 270344 | tf_op jit(solution)/shard_map/ppermute | solution.py:319
  66.4 6.8 %collective-permute-start.20 = (bf16[256,256]{1,0:T(8,128)(2,1)S(1)}, bf16[256,256]{1,0:T(8,128)(2,1)S(1)}, u32[]{:S(2)}, u32[]{:S(2)}) collective-permute-start(bf16[256,256]{1,0:T(8,128)(2,1)S(1)} %get-tuple-element.123), channel_id=1, source_target_pairs={{0,4},{4,8},{8,12},{12,0},{1,5},{5,9},{9,13},{13,1},{2,6},{6,10},{... | collective-permute-start | bytes 393224 | tf_op jit(solution)/shard_map/ppermute | solution.py:315
  66.4 7.9 %collective-permute-start.17 = (bf16[176,256]{1,0:T(8,128)(2,1)S(1)}, bf16[176,256]{1,0:T(8,128)(2,1)S(1)}, u32[]{:S(2)}, u32[]{:S(2)}) collective-permute-start(bf16[176,256]{1,0:T(8,128)(2,1)S(1)} %shard_map.165.refs_1_), channel_id=1, source_target_pairs={{0,1},{1,0},{2,3},{3,2},{4,5},{5,4},{6,7},{7,6},{8,9},{9,8},{10,11... | collective-permute-start | bytes 270344 | tf_op jit(solution)/shard_map/ppermute | solution.py:319
  69.4 4.8 %collective-permute-start.19 = (bf16[176,256]{1,0:T(8,128)(2,1)S(1)}, bf16[176,256]{1,0:T(8,128)(2,1)S(1)}, u32[]{:S(2)}, u32[]{:S(2)}) collective-permute-start(bf16[176,256]{1,0:T(8,128)(2,1)S(1)} %collective-permute-done.18.refs_3_), channel_id=1, source_target_pairs={{0,1},{1,0},{2,3},{3,2},{4,5},{5,4},{6,7},{7,6},{8,9},{9,8},{10,11... | collective-permute-start | bytes 270344 | tf_op jit(solution)/shard_map/ppermute | solution.py:319

commit v12 on v10

--- a/solution.py
+++ b/solution.py
@@ -43,21 +43,26 @@
     )
 
 
-def cut_rims(latent_ref, member, last_ref, first_ref):
-    nodes = latent_ref.shape[1]
-    last_ref[...] = latent_ref[member, nodes - HALO :]
-    first_ref[...] = latent_ref[member, :HALO]
-
-
-def rims_kernel(latent_ref, last_ref, first_ref, copy_ref):
-    cut_rims(latent_ref, 0, last_ref, first_ref)
+def rim_starts(region_ref, length):
+    odd = lax.rem(region_ref[0], 2)
+    far = length - HALO
+    return [pl.ds(pl.multiple_of(start, HALO), HALO) for start in ((1 - odd) * far, odd * far)]
+
+
+def cut_rims(region_ref, latent_ref, member, *rim_refs):
+    for ref, rows in zip(rim_refs, rim_starts(region_ref, latent_ref.shape[1])):
+        ref[...] = latent_ref[member, rows]
+
+
+def rims_kernel(region_ref, latent_ref, one_ref, other_ref, copy_ref):
+    cut_rims(region_ref, latent_ref, 0, one_ref, other_ref)
     copy_ref[...] = latent_ref[...]
 
 
 def table_kernel(region_ref, rank_ref, counts_ref, nbr_ref, weight_ref, latent_ref, table_ref, part_ref, *rim_refs):
     members, nodes, _ = latent_ref.shape
     for m in range(1, members):
-        cut_rims(latent_ref, m, *rim_refs[2 * m - 2 : 2 * m])
+        cut_rims(region_ref, latent_ref, m, *rim_refs[2 * m - 2 : 2 * m])
     ext, slots = table_ref.shape
     live = lax.broadcasted_iota(jnp.int32, (1, slots), 1) < counts_ref[region_ref[0]]
     nbr = [nbr_ref[k : k + 1, :] for k in range(K)]
@@ -96,7 +101,7 @@
 
 
 def forward_kernel(
-    member, own_ref, table_ref, before_ref, after_ref, w_one_ref, b_one_ref, w_two_ref, b_two_ref, w_three_ref,
+    member, region_ref, own_ref, table_ref, one_ref, other_ref, w_one_ref, b_one_ref, w_two_ref, b_two_ref, w_three_ref,
     mixed_ref, act_one_ref, slope_one_ref, act_two_ref, slope_two_ref, decoded_ref,
 ):
     ext, slots = table_ref.shape
@@ -109,17 +114,13 @@
         act = half * gate
         return act.astype(jnp.bfloat16), (gate + act * (2.0 - gate)).astype(jnp.bfloat16)
 
-    if member:
-        nodes = jnp.concatenate([before_ref[...].T, own_ref[member].T, after_ref[...].T], axis=1)
-    else:
-        nodes = jnp.concatenate([before_ref[...].T, after_ref[...].T], axis=1)
+    edges = jnp.concatenate([one_ref[...].T, other_ref[...].T], axis=1)
+    own = own_ref[member].T if member else None
     for lo, size in split(slots, CHUNK):
         lanes = slice(lo, lo + size)
-        if member:
-            mixed = nn_dot(nodes, table_ref[:, lanes])
-        else:
-            rims = jnp.concatenate([table_ref[:HALO, lanes], table_ref[ext - HALO :, lanes]], axis=0)
-            mixed = own_ref[:, lanes] + nn_dot(nodes, rims)
+        rims = jnp.concatenate([table_ref[rows, lanes] for rows in rim_starts(region_ref, ext)], axis=0)
+        share = nn_dot(own, table_ref[HALO : ext - HALO, lanes]) if member else own_ref[:, lanes]
+        mixed = share + nn_dot(edges, rims)
         mixed = mixed.astype(jnp.bfloat16)
         mixed_ref[:, lanes] = mixed
         act_one, slope_one_ref[:, lanes] = layer(w_one, b_one, mixed, size)
@@ -255,16 +256,17 @@
         piece_refs[i][...] = stage_ref[rank_ref[0] ^ i]
 
 
-def edges_kernel(members, table_ref, w_one_ref, *refs):
-    d_one_refs, d_mixed_refs, (head_ref, tail_ref) = refs[:members], refs[members : 2 * members], refs[2 * members :]
+def edges_kernel(members, region_ref, table_ref, w_one_ref, *refs):
+    d_one_refs, refs = refs[:members], refs[members:]
     ext = table_ref.shape[0]
-    rows = jnp.concatenate([table_ref[:HALO, :], table_ref[ext - HALO :, :]], axis=0)
+    rows = jnp.concatenate([table_ref[rows, :] for rows in rim_starts(region_ref, ext)], axis=0)
     for m in range(members):
+        d_mixed_ref, one_ref, other_ref = refs[3 * m : 3 * (m + 1)]
         d_mixed = nn_dot(w_one_ref[...], d_one_refs[m][...]).astype(jnp.bfloat16)
-        d_mixed_refs[m][...] = d_mixed
+        d_mixed_ref[...] = d_mixed
         grads = nt_dot(rows, d_mixed).astype(jnp.bfloat16)
-        head_ref[m] = grads[:HALO]
-        tail_ref[m] = grads[HALO:]
+        one_ref[...] = grads[:HALO]
+        other_ref[...] = grads[HALO:]
 
 
 def sum_kernel(count, *refs):
@@ -300,17 +302,20 @@
         own_ref[m] = nt_dot(table_ref[HALO : HALO + nodes, :], d_mixed_refs[m][...])
 
 
-def finish_kernel(own_ref, from_next_ref, from_prev_ref, out_ref):
-    nodes = own_ref.shape[1]
-    from_next, from_prev = from_next_ref[...].astype(jnp.float32), from_prev_ref[...].astype(jnp.float32)
-    out_ref[:, :HALO] = (own_ref[:, :HALO] + from_prev).astype(jnp.bfloat16)
+def finish_kernel(region_ref, own_ref, *refs):
+    *refs, out_ref = refs
+    members, nodes, _ = own_ref.shape
     out_ref[:, HALO : nodes - HALO] = own_ref[:, HALO : nodes - HALO].astype(jnp.bfloat16)
-    out_ref[:, nodes - HALO :] = (own_ref[:, nodes - HALO :] + from_next).astype(jnp.bfloat16)
-
-
-def shifted(shard, axis, by):
-    length = lax.axis_size(axis)
-    return lax.ppermute(shard, axis, [(i, (i + by) % length) for i in range(length)])
+    for m in range(members):
+        for ref, rows in zip(refs[2 * m : 2 * (m + 1)], rim_starts(region_ref, nodes)):
+            out_ref[m, rows] = (own_ref[m, rows] + ref[...].astype(jnp.float32)).astype(jnp.bfloat16)
+
+
+def exchanged(blocks):
+    size = lax.axis_size("space")
+    one = [(i, i ^ 1) for i in range(size)]
+    other = [(i, (i + 1) % size if i % 2 else (i - 1) % size) for i in range(size)]
+    return [lax.ppermute(block, "space", pairs) for block, pairs in zip(blocks, (one, other))]
 
 
 def swapped(block, axis, by):
@@ -330,12 +335,12 @@
     each = range(members)
 
     edge = shape((HALO, width), bf16)
-    last, first, latent = kernel_call(
-        rims_kernel, (edge, edge, shape(latent.shape, bf16)), flops=4 << 30, moved=3 * MIB, operands=1
-    )(latent)
-    before, after = [shifted(last, "space", 1)], [shifted(first, "space", -1)]
+    region_at = region[None].astype(jnp.int32)
+    *rims, latent = kernel_call(
+        rims_kernel, (edge, edge, shape(latent.shape, bf16)), flops=4 << 30, moved=3 * MIB, smem=1, operands=2
+    )(region_at, latent)
+    halo = [exchanged(rims)]
     rank_at = rank[None].astype(jnp.int32)
-    region_at = region[None].astype(jnp.int32)
 
     table, part, *rims = kernel_call(
         table_kernel,
@@ -345,8 +350,7 @@
         smem=3,
         operands=6,
     )(region_at, rank_at, counts, neighbours, weights, latent)
-    before += [shifted(block, "space", 1) for block in rims[::2]]
-    after += [shifted(block, "space", -1) for block in rims[1::2]]
+    halo += [exchanged(rims[2 * m : 2 * m + 2]) for m in range(members - 1)]
 
     saved_shape = shape((hidden, slots), bf16)
     mixed_shape = shape((width, slots), bf16)
@@ -359,8 +363,9 @@
             (mixed_shape,) + (saved_shape,) * 4 + (decoded_shape,),
             flops=2 * slots * ((ext if m else 2 * HALO) * width + dense),
             moved=8 * MIB,
-            operands=9,
-        )(latent if m else part, table, before[m], after[m], w_one, b_one[None], w_two, b_two[None], w_three)
+            smem=1,
+            operands=10,
+        )(region_at, latent if m else part, table, *halo[m], w_one, b_one[None], w_two, b_two[None], w_three)
         saved.append(kept)
         decoded.append(block)
         blocks, bit = {0: block}, 2
@@ -407,20 +412,21 @@
             lambda *refs: sum_kernel(len(ones), *refs), (piece,) * len(ones), flops=MIB, moved=MIB, operands=2 * len(ones)
         )(*ones, *others)
 
-    rims = shape((members, HALO, width), bf16)
-    *d_mixed, head, tail = kernel_call(
+    out = kernel_call(
         lambda *refs: edges_kernel(members, *refs),
-        (mixed_shape,) * members + (rims, rims),
+        (mixed_shape, edge, edge) * members,
         flops=2 * members * slots * width * (hidden + 2 * HALO),
         moved=6 * MIB,
-        operands=2 + members,
-    )(table, w_one, *d_one)
+        smem=1,
+        operands=3 + members,
+    )(region_at, table, w_one, *d_one)
+    d_mixed, rims = out[::3], [out[3 * m + 1 : 3 * m + 3] for m in each]
 
     bit = 1
     while bit < ranks:
         received = [swapped(sent, "member", bit) for sent in pieces[1::2]]
         if bit == 1:
-            received, head, tail = lax.optimization_barrier((received, head, tail))
+            received, rims = lax.optimization_barrier((received, rims))
         pieces = summed(pieces[::2], received)
         bit = 2 * bit
     own = kernel_call(
@@ -430,28 +436,32 @@
         moved=6 * MIB,
         operands=1 + members,
     )(table, *d_mixed)
-    from_next = shifted(head, "space", -1)
+    edges = [block for m in each[:-1] for block in exchanged(rims[m])]
     (total,) = pieces
     step = 1
     while step < regions:
         (total,) = summed([total], [swapped(total, "space", step)])
         step = 2 * step
         if step == regions // 2:
-            total, from_next, own, tail = lax.optimization_barrier((total, from_next, own, tail))
-            from_prev = shifted(tail, "space", 1)
+            total, edges, own, rims = lax.optimization_barrier((total, edges, own, rims))
+            edges = [*edges, *exchanged(rims[-1])]
     totals = {0: total}
     bit = 2
     while bit < ranks:
         totals.update({i ^ bit: swapped(totals[i], "member", bit) for i in sorted(totals)})
         bit = 2 * bit
+    far = {i: block for i, block in totals.items() if i}
+    far, edges = lax.optimization_barrier((far, edges))
+    totals.update(far)
     totals.update({i ^ 1: swapped(block, "member", 1) for i, block in totals.items()})
     latent_grad = kernel_call(
         finish_kernel,
         shape((members, nodes, width), bf16),
         flops=MIB,
         moved=3 * MIB,
-        operands=3,
-    )(own, from_next, from_prev)
+        smem=1,
+        operands=2 + 2 * members,
+    )(region_at, own, *edges)
     totals = [totals[i] for i in range(ranks)]
     totals, latent_grad = lax.optimization_barrier((totals, latent_grad))
     row = shape((1, hidden), f32)

time: 74.5 us -> 72.4 us (0.972)
  waiting for transfers between devices: 27.8 us -> 23.3 us
  starting transfers between devices: 21.9 us -> 24.2 us
    ppermute x14, waiting for transfers between devices: 27.8 us -> 20.1 us  [swapped(): lax.ppermute(block, axis, [(i, i ^ by) for i in range(lax.axis_size(axis))])]
    ppermute x6 -> x8, waiting for transfers between devices: 0.02 us -> 3.16 us  [exchanged(): lax.ppermute(block, 'space', pairs)]
    ppermute x6 -> x8, starting transfers between devices: 12.4 us -> 13.6 us  [exchanged(): lax.ppermute(block, 'space', pairs)]
    ppermute x14, starting transfers between devices: 9.48 us -> 10.6 us  [swapped(): lax.ppermute(block, axis, [(i, i ^ by) for i in range(lax.axis_size(axis))])]
  transfers between devices with their start and end apart: 20 -> 22, of which waited for: 9 -> 11; matrix products, arithmetic and copies ran while one was open for 0% -> 0% of each run, Pallas kernels for 22% -> 23%
where the time goes in v12:
time: 72.4 us; the launch traced here: 72.3 us
  starting transfers between devices  24.2 us (33%)
  waiting for transfers between devices  23.3 us (32%)
  Pallas kernels  22.7 us (31%)
  local copies, waits for them, and re-layouts  1.27 us (2%)
  between operations  0.85 us (1%)
    ppermute x14, waiting for transfers between devices, swapped(): lax.ppermute(block, axis, [(i, i ^ by) for i in range(lax.axis_size(axis))])  20.1 us
    ppermute x8, starting transfers between devices, exchanged(): lax.ppermute(block, 'space', pairs)  13.6 us
    ppermute x14, starting transfers between devices, swapped(): lax.ppermute(block, axis, [(i, i ^ by) for i in range(lax.axis_size(axis))])  10.6 us
    pallas_call x2, Pallas kernels, per_device(): kernel_call(lambda *refs: forward_kernel(m, *refs), (mixed_shape,) + (sav...  6.57 us
    pallas_call x2, Pallas kernels, scored(): kernel_call(lambda *refs: score_kernel(members, len(others), members * ra...  4.77 us
    ppermute x8, waiting for transfers between devices, exchanged(): lax.ppermute(block, 'space', pairs)  3.16 us
    pallas_call x1, Pallas kernels, per_device(): kernel_call(table_kernel, (shape((ext, slots), bf16), shape((width, slots...  3.13 us
    pallas_call x1, Pallas kernels, per_device(): kernel_call(lambda *refs: backward_kernel(members, ranks, *refs), (saved_...  2.84 us
  transfers between devices with their start and end apart: 22, of which 11 were waited for; matrix products, arithmetic and copies ran while one was open for 0% of the time, Pallas kernels for 23%

profile of v12, /device:TPU:0, one launch (start us, length us, event | category | flops | bytes accessed | tf_op | source)
XLA Modules:
  0.0 72.3 jit_solution(12820505723584389961)
XLA Ops:
  0.6 1.2 %copy-done.7 = bf16[2,1024,256]{2,1,0:T(8,128)(2,1)S(1)} copy-done((bf16[2,1024,256]{2,1,0:T(8,128)(2,1)S(1)}, bf16[2,1024,256]{2,1,0:T(8,128)(2,1)}, u32[]{:S(2)}) %copy-start.7) | copy-done | bytes 1048600
  1.9 0.1 shard_map.153
  2.0 0.0 copy-start
  2.0 0.0 copy-start.1
  2.0 0.0 copy-start.2
  2.0 0.0 copy-start.4
  2.0 0.0 copy-start.5
  2.0 3.1 %collective-permute-start = (bf16[256,256]{1,0:T(8,128)(2,1)S(1)}, bf16[256,256]{1,0:T(8,128)(2,1)S(1)}, u32[]{:S(2)}, u32[]{:S(2)}) collective-permute-start(bf16[256,256]{1,0:T(8,128)(2,1)S(1)} %get-tuple-element.81), channel_id=1, source_target_pairs={{0,4},{4,0},{8,12},{12,8},{1,5},{5,1},{9,13},{13,9},{2,6},{6,2},{1... | collective-permute-start | bytes 393224 | tf_op jit(solution)/shard_map/ppermute | solution.py:318
  5.1 2.5 %collective-permute-start.1 = (bf16[256,256]{1,0:T(8,128)(2,1)S(1)}, bf16[256,256]{1,0:T(8,128)(2,1)S(1)}, u32[]{:S(2)}, u32[]{:S(2)}) collective-permute-start(bf16[256,256]{1,0:T(8,128)(2,1)S(1)} %get-tuple-element.82), channel_id=1, source_target_pairs={{0,12},{4,8},{8,4},{12,0},{1,13},{5,9},{9,5},{13,1},{2,14},{6,10},... | collective-permute-start | bytes 393224 | tf_op jit(solution)/shard_map/ppermute | solution.py:318
  7.6 0.0 copy-done.6
  7.6 0.0 copy-done.9
  7.6 3.1 %shard_map.154 = (bf16[1536,1536]{1,0:T(8,128)(2,1)S(1)}, f32[256,1536]{1,0:T(8,128)S(1)}, bf16[256,256]{1,0:T(8,128)(2,1)S(1)}, bf16[256,256]{1,0:T(8,128)(2,1)S(1)}) custom-call(s32[1]{0:T(128)} %bitcast.1.region_ref.refs_0_, s32[1]{0:T(128)} %bitcast.rank_ref.refs_1_.refs_0_, s32[4]{0:T(128)S(1)} %copy-done.6, s32[4,1536]{1,0:T(4,128)S(1)} %copy-done.8, ...), custom_call_target="tpu_custom_call" | custom-call | flops 805306368 | bytes 12582912 | tf_op jit(solution)/shard_map/pallas_call | solution.py:345
  10.7 0.7 %collective-permute-start.2 = (bf16[256,256]{1,0:T(8,128)(2,1)S(1)}, bf16[256,256]{1,0:T(8,128)(2,1)S(1)}, u32[]{:S(2)}, u32[]{:S(2)}) collective-permute-start(bf16[256,256]{1,0:T(8,128)(2,1)S(1)} %get-tuple-element.84), channel_id=1, source_target_pairs={{0,4},{4,0},{8,12},{12,8},{1,5},{5,1},{9,13},{13,9},{2,6},{6,2},{1... | collective-permute-start | bytes 393224 | tf_op jit(solution)/shard_map/ppermute | solution.py:318
  11.5 0.9 %collective-permute-start.3 = (bf16[256,256]{1,0:T(8,128)(2,1)S(1)}, bf16[256,256]{1,0:T(8,128)(2,1)S(1)}, u32[]{:S(2)}, u32[]{:S(2)}) collective-permute-start(bf16[256,256]{1,0:T(8,128)(2,1)S(1)} %get-tuple-element.85), channel_id=1, source_target_pairs={{0,12},{4,8},{8,4},{12,0},{1,13},{5,9},{9,5},{13,1},{2,14},{6,10},... | collective-permute-start | bytes 393224 | tf_op jit(solution)/shard_map/ppermute | solution.py:318
  12.4 0.0 collective-permute-done.refs_3_
  12.4 2.2 %collective-permute-done.1.refs_4_ = bf16[256,256]{1,0:T(8,128)(2,1)S(1)} collective-permute-done((bf16[256,256]{1,0:T(8,128)(2,1)S(1)}, bf16[256,256]{1,0:T(8,128)(2,1)S(1)}, u32[]{:S(2)}, u32[]{:S(2)}) %collective-permute-start.1) | collective-permute-done | bytes 131104 | tf_op jit(solution)/shard_map/ppermute | solution.py:318
  14.7 2.9 %shard_map.155 = (bf16[256,1536]{1,0:T(8,128)(2,1)S(1)}, bf16[256,1536]{1,0:T(8,128)(2,1)S(1)}, bf16[256,1536]{1,0:T(8,128)(2,1)S(1)}, bf16[256,1536]{1,0:T(8,12...) custom-call(s32[1]{0:T(128)} %bitcast.1.region_ref.refs_0_, ...), custom_call_target="tpu_custom_call" | custom-call | flops 905969664 | bytes 8388608 | tf_op jit(solution)/shard_map/pallas_call | solution.py:361
  17.5 0.0 copy-start.3
  17.6 1.5 %collective-permute-start.7 = (bf16[128,1536]{1,0:T(8,128)(2,1)S(1)}, bf16[128,1536]{1,0:T(8,128)(2,1)S(1)}, u32[]{:S(2)}, u32[]{:S(2)}) collective-permute-start(bf16[128,1536]{1,0:T(8,128)(2,1)S(1)} %get-tuple-element.83.refs_2_), channel_id=1, source_target_pairs={{0,2},{1,3},{2,0},{3,1},{4,6},{5,7},{6,4},{7,5},{8,10},{9,11},{10,... | collective-permute-start | bytes 1179656 | tf_op jit(solution)/shard_map/ppermute | solution.py:322
  19.1 0.0 collective-permute-start.5
  19.1 0.0 collective-permute-done.2.refs_3_
  19.1 0.2 collective-permute-done.3.refs_4_
  19.3 3.7 %shard_map.156 = (bf16[256,1536]{1,0:T(8,128)(2,1)S(1)}, bf16[256,1536]{1,0:T(8,128)(2,1)S(1)}, bf16[256,1536]{1,0:T(8,128)(2,1)S(1)}, bf16[256,1536]{1,0:T(8,12...) custom-call(s32[1]{0:T(128)} %bitcast.1.region_ref.refs_0_, ...), custom_call_target="tpu_custom_call" | custom-call | flops 1711276032 | bytes 8388608 | tf_op jit(solution)/shard_map/pallas_call | solution.py:361
  23.0 0.4 collective-permute-start.6
  23.4 1.3 %collective-permute-start.4 = (bf16[128,1536]{1,0:T(8,128)(2,1)S(1)}, bf16[128,1536]{1,0:T(8,128)(2,1)S(1)}, u32[]{:S(2)}, u32[]{:S(2)}) collective-permute-start(bf16[128,1536]{1,0:T(8,128)(2,1)S(1)} %get-tuple-element.86.refs_3_), channel_id=1, source_target_pairs={{0,2},{1,3},{2,0},{3,1},{4,6},{5,7},{6,4},{7,5},{8,10},{9,11},{10,... | collective-permute-start | bytes 1179656 | tf_op jit(solution)/shard_map/ppermute | solution.py:322
  24.7 2.2 %collective-permute-done.7.refs_6_ = bf16[128,1536]{1,0:T(8,128)(2,1)S(1)} collective-permute-done((bf16[128,1536]{1,0:T(8,128)(2,1)S(1)}, bf16[128,1536]{1,0:T(8,128)(2,1)S(1)}, u32[]{:S(2)}, u32[]{:S(2)}) %collective-permute-start.7) | collective-permute-done | bytes 393248 | tf_op jit(solution)/shard_map/ppermute | solution.py:322
  26.9 0.0 collective-permute-done.5.refs_4_
  26.9 0.0 collective-permute-done.6.refs_5_
  26.9 2.7 %shard_map.157 = (f32[128,1536]{1,0:T(8,128)S(1)}, f32[128,1536]{1,0:T(8,128)S(1)}, f32[1,128]{1,0:T(1,128)S(1)}) custom-call(s32[1]{0:T(128)} %bitcast.1.region_ref.refs_0_, s32[4]{0:T(128)S(1)} %copy-done.6, bf16[128,1536]{1,0:T(8,128)(2,1)S(1)} %get-tuple-element.83.refs_2_, bf16[128,1536]{1,0:T(8,128)(2,1)S(1)} %get-tuple-element.86.refs_3_, ...), custom_call_target="tpu_custom_call" | custom-call | flops 4194304 | bytes 2097152 | tf_op jit(solution)/shard_map/pallas_call | solution.py:380
  29.6 5.4 %collective-permute-done.4.refs_4_ = bf16[128,1536]{1,0:T(8,128)(2,1)S(1)} collective-permute-done((bf16[128,1536]{1,0:T(8,128)(2,1)S(1)}, bf16[128,1536]{1,0:T(8,128)(2,1)S(1)}, u32[]{:S(2)}, u32[]{:S(2)}) %collective-permute-start.4) | collective-permute-done | bytes 393248 | tf_op jit(solution)/shard_map/ppermute | solution.py:322
  35.0 0.0 collective-permute-start.8
  35.0 0.5 collective-permute-start.9
  35.5 1.2 %collective-permute-done.8.refs_5_ = bf16[128,1536]{1,0:T(8,128)(2,1)S(1)} collective-permute-done((bf16[128,1536]{1,0:T(8,128)(2,1)S(1)}, bf16[128,1536]{1,0:T(8,128)(2,1)S(1)}, u32[]{:S(2)}, u32[]{:S(2)}) %collective-permute-start.8) | collective-permute-done | bytes 393248 | tf_op jit(solution)/shard_map/ppermute | solution.py:322
  36.7 0.6 collective-permute-done.9.refs_6_
  37.3 2.1 %shard_map.158 = (bf16[128,1536]{1,0:T(8,128)(2,1)S(1)}, bf16[128,1536]{1,0:T(8,128)(2,1)S(1)}, f32[1,128]{1,0:T(1,128)S(1)}) custom-call(s32[1]{0:T(128)} %bitcast.1.region_ref.refs_0_, s32[4]{0:T(128)S(1)} %copy-done.6, bf16[128,1536]{1,0:T(8,128)(2,1)S(1)} %get-tuple-element.83.refs_2_, bf16[128,1536]{1,0:T(8,128)(2,1)S(1)} %get-tuple-element.86.refs_3_, ...), custom_call_target="tpu_custom_call" | custom-call | flops 4194304 | bytes 2097152 | tf_op jit(solution)/shard_map/pallas_call | solution.py:380
  39.4 2.8 %shard_map.159 = (bf16[256,1536]{1,0:T(8,128)(2,1)S(1)}, bf16[256,1536]{1,0:T(8,128)(2,1)S(1)}, bf16[176,256]{1,0:T(8,128)(2,1)S(1)}, bf16[176,256]{1,0:T(8,128)...) custom-call(s32[1]{0:T(128)} %bitcast.1.region_ref.refs_0_, s32[1]{0:T(128)} %bitcast.rank_ref.refs_1_.refs_0_, ...), custom_call_target="tpu_custom_call" | custom-call | flops 2013265920 | bytes 10485760 | tf_op jit(solution)/shard_map/pallas_call | solution.py:399
  42.2 0.2 collective-permute-start.10
  42.4 0.4 collective-permute-start.11
  42.8 1.4 %shard_map.160 = (bf16[256,1536]{1,0:T(8,128)(2,1)S(1)}, bf16[256,256]{1,0:T(8,128)(2,1)S(1)}, bf16[256,256]{1,0:T(8,128)(2,1)S(1)}, bf16[256,1536]{1,0:T(8,128)...) custom-call(s32[1]{0:T(128)} %bitcast.1.region_ref.refs_0_, ...), custom_call_target="tpu_custom_call" | custom-call | flops 1207959552 | bytes 6291456 | tf_op jit(solution)/shard_map/pallas_call | solution.py:415
  44.2 0.0 collective-permute-done.10.refs_2_
  44.2 0.0 collective-permute-done.11.refs_3_
  44.3 1.6 %collective-permute-start.12 = (bf16[176,256]{1,0:T(8,128)(2,1)S(1)}, bf16[176,256]{1,0:T(8,128)(2,1)S(1)}, u32[]{:S(2)}, u32[]{:S(2)}) collective-permute-start(bf16[176,256]{1,0:T(8,128)(2,1)S(1)} %get-tuple-element.120), channel_id=1, source_target_pairs={{0,2},{1,3},{2,0},{3,1},{4,6},{5,7},{6,4},{7,5},{8,10},{9,11},{10,... | collective-permute-start | bytes 270344 | tf_op jit(solution)/shard_map/ppermute | solution.py:322
  45.8 0.7 collective-permute-start.14
  46.5 2.9 %collective-permute-start.15 = (bf16[256,256]{1,0:T(8,128)(2,1)S(1)}, bf16[256,256]{1,0:T(8,128)(2,1)S(1)}, u32[]{:S(2)}, u32[]{:S(2)}) collective-permute-start(bf16[256,256]{1,0:T(8,128)(2,1)S(1)} %get-tuple-element.122), channel_id=1, source_target_pairs={{0,12},{4,8},{8,4},{12,0},{1,13},{5,9},{9,5},{13,1},{2,14},{6,10},... | collective-permute-start | bytes 393224 | tf_op jit(solution)/shard_map/ppermute | solution.py:318
  49.4 0.0 collective-permute-done.12.refs_1_
  49.4 0.4 collective-permute-start.13
  49.8 1.8 %shard_map.164.own_ref = f32[2,1024,256]{2,1,0:T(8,128)S(1)} custom-call(bf16[1536,1536]{1,0:T(8,128)(2,1)S(1)} %get-tuple-element.80.refs_2_.refs_1_.table_ref, bf16[256,1536]{1,0:T(8,128)(2,1)S(1)} %get-tuple-element.123.refs_0_, bf16[256,1536]{1,0:T(8,128)(2,1)S(1)} %get-tuple-element.124.refs_1_), custom_call_target="tpu_custom_call" | custom-call | flops 1610612736 | bytes 6291456 | tf_op jit(solution)/shard_map/pallas_call | solution.py:432
  51.6 4.0 %collective-permute-done.13.refs_1_ = bf16[176,256]{1,0:T(8,128)(2,1)S(1)} collective-permute-done((bf16[176,256]{1,0:T(8,128)(2,1)S(1)}, bf16[176,256]{1,0:T(8,128)(2,1)S(1)}, u32[]{:S(2)}, u32[]{:S(2)}) %collective-permute-start.13) | collective-permute-done | bytes 90144 | tf_op jit(solution)/shard_map/ppermute | solution.py:322
  55.7 0.0 collective-permute-done.14.refs_0_
  55.7 0.7 collective-permute-done.15.refs_1_
  56.4 1.6 %collective-permute-start.16 = (bf16[176,256]{1,0:T(8,128)(2,1)S(1)}, bf16[176,256]{1,0:T(8,128)(2,1)S(1)}, u32[]{:S(2)}, u32[]{:S(2)}) collective-permute-start(bf16[176,256]{1,0:T(8,128)(2,1)S(1)} %shard_map.163.refs_0_), channel_id=1, source_target_pairs={{0,8},{4,12},{8,0},{12,4},{1,9},{5,13},{9,1},{13,5},{2,10},{6,14},... | collective-permute-start | bytes 270344 | tf_op jit(solution)/shard_map/ppermute | solution.py:322
  58.1 0.8 %collective-permute-start.19 = (bf16[256,256]{1,0:T(8,128)(2,1)S(1)}, bf16[256,256]{1,0:T(8,128)(2,1)S(1)}, u32[]{:S(2)}, u32[]{:S(2)}) collective-permute-start(bf16[256,256]{1,0:T(8,128)(2,1)S(1)} %get-tuple-element.130), channel_id=1, source_target_pairs={{0,4},{4,0},{8,12},{12,8},{1,5},{5,1},{9,13},{13,9},{2,6},{6,2},{1... | collective-permute-start | bytes 393224 | tf_op jit(solution)/shard_map/ppermute | solution.py:318
  58.9 1.9 %collective-permute-start.20 = (bf16[256,256]{1,0:T(8,128)(2,1)S(1)}, bf16[256,256]{1,0:T(8,128)(2,1)S(1)}, u32[]{:S(2)}, u32[]{:S(2)}) collective-permute-start(bf16[256,256]{1,0:T(8,128)(2,1)S(1)} %get-tuple-element.131), channel_id=1, source_target_pairs={{0,12},{4,8},{8,4},{12,0},{1,13},{5,9},{9,5},{13,1},{2,14},{6,10},... | collective-permute-start | bytes 393224 | tf_op jit(solution)/shard_map/ppermute | solution.py:318
  60.8 4.0 %collective-permute-done.16.refs_1_ = bf16[176,256]{1,0:T(8,128)(2,1)S(1)} collective-permute-done((bf16[176,256]{1,0:T(8,128)(2,1)S(1)}, bf16[176,256]{1,0:T(8,128)(2,1)S(1)}, u32[]{:S(2)}, u32[]{:S(2)}) %collective-permute-start.16) | collective-permute-done | bytes 90144 | tf_op jit(solution)/shard_map/ppermute | solution.py:322
  64.8 2.8 %collective-permute-start.18 = (bf16[176,256]{1,0:T(8,128)(2,1)S(1)}, bf16[176,256]{1,0:T(8,128)(2,1)S(1)}, u32[]{:S(2)}, u32[]{:S(2)}) collective-permute-start(bf16[176,256]{1,0:T(8,128)(2,1)S(1)} %shard_map.165.refs_1_), channel_id=1, source_target_pairs={{0,2},{1,3},{2,0},{3,1},{4,6},{5,7},{6,4},{7,5},{8,10},{9,11},{10,... | collective-permute-start | bytes 270344 | tf_op jit(solution)/shard_map/ppermute | solution.py:322
  67.6 0.0 collective-permute-start.17
  67.6 0.0 collective-permute-done.19.refs_2_
  67.6 0.0 collective-permute-done.20.refs_3_
  67.6 2.5 %collective-permute-done.18.refs_3_ = bf16[176,256]{1,0:T(8,128)(2,1)S(1)} collective-permute-done((bf16[176,256]{1,0:T(8,128)(2,1)S(1)}, bf16[176,256]{1,0:T(8,128)(2,1)S(1)}, u32[]{:S(2)}, u32[]{:S(2)}) %collective-permute-start.18) | collective-permute-done | bytes 90144 | tf_op jit(solution)/shard_map/ppermute | solution.py:322
  70.1 0.0 collective-permute-start.21
  70.1 1.1 %shard_map.166 = bf16[2,1024,256]{2,1,0:T(8,128)(2,1)} custom-call(s32[1]{0:T(128)} %bitcast.1.region_ref.refs_0_, f32[2,1024,256]{2,1,0:T(8,128)S(1)} %shard_map.164.own_ref, bf16[256,256]{1,0:T(8,128)(2,1)S(1)} %collective-permute-done.14.refs_0_, bf16[256,256]{1,0:T(8,128)(2,1)S(1)} %collective-permute-done.15.refs_1_, ...), custom_call_target="tpu_custom_call" | custom-call | flops 1048576 | bytes 3145728 | tf_op jit(solution)/shard_map/pallas_call | solution.py:457
  71.2 0.0 collective-permute-done.17.refs_2_
  71.2 0.2 collective-permute-done.21.refs_4_
  71.4 0.9 %shard_map.167 = (f32[256,256]{1,0:T(8,128)}, f32[1,256]{1,0:T(1,128)}, f32[256,256]{1,0:T(8,128)}, f32[1,256]{1,0:T(1,128)}, f32[256,128]{1,0:T(8,128)}, /*index=5*/f32[1,4]{1,0:T(1,128)}) custom-call(s32[1]{0:T(128)} %bitcast.rank_ref.refs_1_.refs_0_, bf16[176,256]{1,0:T(8,128)(2,1)S(1)} %shard_map.165.refs_1_, ...), custom_call_target="tpu_custom_call" | custom-call | flops 1048576 | bytes 2097152 | tf_op jit(solution)/shard_map/pallas_call | solution.py:468
  (15 shorter events, 0.1 us)
Async XLA Ops:
  0.6 1.2 %copy-start.7 = (bf16[2,1024,256]{2,1,0:T(8,128)(2,1)S(1)}, bf16[2,1024,256]{2,1,0:T(8,128)(2,1)}, u32[]{:S(2)}) copy-start(bf16[2,1024,256]{2,1,0:T(8,128)(2,1)} %latent_ref.1) | copy-start | bytes 3145732
  1.9 5.7 %copy-start.6 = (s32[4]{0:T(128)S(1)}, s32[4]{0:T(128)}, u32[]{:S(2)}) copy-start(s32[4]{0:T(128)} %refs_1_.3) | copy-start | bytes 52
  1.9 5.7 %copy-start.8 = (s32[4,1536]{1,0:T(4,128)S(1)}, s32[4,1536]{1,0:T(4,128)}, u32[]{:S(2)}) copy-start(s32[4,1536]{1,0:T(4,128)} %nbr_ref.1) | copy-start | bytes 73732
  1.9 5.7 %copy-start.9 = (f32[4,1536]{1,0:T(4,128)S(1)}, f32[4,1536]{1,0:T(4,128)}, u32[]{:S(2)}) copy-start(f32[4,1536]{1,0:T(4,128)} %weight_ref.1) | copy-start | bytes 73732
  2.0 12.7 %copy-start = (bf16[256,256]{1,0:T(8,128)(2,1)S(1)}, bf16[256,256]{1,0:T(8,128)(2,1)}, u32[]{:S(2)}) copy-start(bf16[256,256]{1,0:T(8,128)(2,1)} %refs_2_.2) | copy-start | bytes 393220
  2.0 12.7 %copy-start.1 = (bf16[256,256]{1,0:T(8,128)(2,1)S(1)}, bf16[256,256]{1,0:T(8,128)(2,1)}, u32[]{:S(2)}) copy-start(bf16[256,256]{1,0:T(8,128)(2,1)} %refs_2_.3) | copy-start | bytes 393220
  2.0 12.7 %copy-start.2 = (bf16[256,128]{1,0:T(8,128)(2,1)S(1)}, bf16[256,128]{1,0:T(8,128)(2,1)}, u32[]{:S(2)}) copy-start(bf16[256,128]{1,0:T(8,128)(2,1)} %refs_3_.1) | copy-start | bytes 196612
  2.0 12.6 %copy-start.4 = (f32[256]{0:T(256)S(1)}, f32[256]{0:T(256)}, u32[]{:S(2)}) copy-start(f32[256]{0:T(256)} %param.16) | copy-start | bytes 3076
  2.0 12.6 %copy-start.5 = (f32[256]{0:T(256)S(1)}, f32[256]{0:T(256)}, u32[]{:S(2)}) copy-start(f32[256]{0:T(256)} %param.18) | copy-start | bytes 3076
  2.0 10.4 %collective-permute-start = (bf16[256,256]{1,0:T(8,128)(2,1)S(1)}, bf16[256,256]{1,0:T(8,128)(2,1)S(1)}, u32[]{:S(2)}, u32[]{:S(2)}) collective-permute-start(bf16[256,256]{1,0:T(8,128)(2,1)S(1)} %get-tuple-element.81), channel_id=1, source_target_pairs={{0,4},{4,0},{8,12},{12,8},{1,5},{5,1},{9,13},{13,9},{2,6},{6,2},{1... | collective-permute-start | bytes 393224 | tf_op jit(solution)/shard_map/ppermute | solution.py:318
  5.1 9.5 %collective-permute-start.1 = (bf16[256,256]{1,0:T(8,128)(2,1)S(1)}, bf16[256,256]{1,0:T(8,128)(2,1)S(1)}, u32[]{:S(2)}, u32[]{:S(2)}) collective-permute-start(bf16[256,256]{1,0:T(8,128)(2,1)S(1)} %get-tuple-element.82), channel_id=1, source_target_pairs={{0,12},{4,8},{8,4},{12,0},{1,13},{5,9},{9,5},{13,1},{2,14},{6,10},... | collective-permute-start | bytes 393224 | tf_op jit(solution)/shard_map/ppermute | solution.py:318
  10.7 8.4 %collective-permute-start.2 = (bf16[256,256]{1,0:T(8,128)(2,1)S(1)}, bf16[256,256]{1,0:T(8,128)(2,1)S(1)}, u32[]{:S(2)}, u32[]{:S(2)}) collective-permute-start(bf16[256,256]{1,0:T(8,128)(2,1)S(1)} %get-tuple-element.84), channel_id=1, source_target_pairs={{0,4},{4,0},{8,12},{12,8},{1,5},{5,1},{9,13},{13,9},{2,6},{6,2},{1... | collective-permute-start | bytes 393224 | tf_op jit(solution)/shard_map/ppermute | solution.py:318
  11.5 7.8 %collective-permute-start.3 = (bf16[256,256]{1,0:T(8,128)(2,1)S(1)}, bf16[256,256]{1,0:T(8,128)(2,1)S(1)}, u32[]{:S(2)}, u32[]{:S(2)}) collective-permute-start(bf16[256,256]{1,0:T(8,128)(2,1)S(1)} %get-tuple-element.85), channel_id=1, source_target_pairs={{0,12},{4,8},{8,4},{12,0},{1,13},{5,9},{9,5},{13,1},{2,14},{6,10},... | collective-permute-start | bytes 393224 | tf_op jit(solution)/shard_map/ppermute | solution.py:318
  17.5 9.4 %copy-start.3 = (bf16[1536,128]{1,0:T(8,128)(2,1)S(1)}, bf16[1536,128]{1,0:T(8,128)(2,1)}, u32[]{:S(2)}) copy-start(bf16[1536,128]{1,0:T(8,128)(2,1)} %refs_7_.5) | copy-start | bytes 1179652
  17.6 9.3 %collective-permute-start.7 = (bf16[128,1536]{1,0:T(8,128)(2,1)S(1)}, bf16[128,1536]{1,0:T(8,128)(2,1)S(1)}, u32[]{:S(2)}, u32[]{:S(2)}) collective-permute-start(bf16[128,1536]{1,0:T(8,128)(2,1)S(1)} %get-tuple-element.83.refs_2_), channel_id=1, source_target_pairs={{0,2},{1,3},{2,0},{3,1},{4,6},{5,7},{6,4},{7,5},{8,10},{9,11},{10,... | collective-permute-start | bytes 1179656 | tf_op jit(solution)/shard_map/ppermute | solution.py:322
  19.1 7.8 %collective-permute-start.5 = (bf16[128,1536]{1,0:T(8,128)(2,1)S(1)}, bf16[128,1536]{1,0:T(8,128)(2,1)S(1)}, u32[]{:S(2)}, u32[]{:S(2)}) collective-permute-start(bf16[128,1536]{1,0:T(8,128)(2,1)S(1)} %get-tuple-element.83.refs_2_), channel_id=1, source_target_pairs={{0,1},{1,0},{2,3},{3,2},{4,5},{5,4},{6,7},{7,6},{8,9},{9,8},{10,11... | collective-permute-start | bytes 1179656 | tf_op jit(solution)/shard_map/ppermute | solution.py:322
  23.0 3.9 %collective-permute-start.6 = (bf16[128,1536]{1,0:T(8,128)(2,1)S(1)}, bf16[128,1536]{1,0:T(8,128)(2,1)S(1)}, u32[]{:S(2)}, u32[]{:S(2)}) collective-permute-start(bf16[128,1536]{1,0:T(8,128)(2,1)S(1)} %get-tuple-element.86.refs_3_), channel_id=1, source_target_pairs={{0,1},{1,0},{2,3},{3,2},{4,5},{5,4},{6,7},{7,6},{8,9},{9,8},{10,11... | collective-permute-start | bytes 1179656 | tf_op jit(solution)/shard_map/ppermute | solution.py:322
  23.4 11.6 %collective-permute-start.4 = (bf16[128,1536]{1,0:T(8,128)(2,1)S(1)}, bf16[128,1536]{1,0:T(8,128)(2,1)S(1)}, u32[]{:S(2)}, u32[]{:S(2)}) collective-permute-start(bf16[128,1536]{1,0:T(8,128)(2,1)S(1)} %get-tuple-element.86.refs_3_), channel_id=1, source_target_pairs={{0,2},{1,3},{2,0},{3,1},{4,6},{5,7},{6,4},{7,5},{8,10},{9,11},{10,... | collective-permute-start | bytes 1179656 | tf_op jit(solution)/shard_map/ppermute | solution.py:322
  35.0 1.7 %collective-permute-start.8 = (bf16[128,1536]{1,0:T(8,128)(2,1)S(1)}, bf16[128,1536]{1,0:T(8,128)(2,1)S(1)}, u32[]{:S(2)}, u32[]{:S(2)}) collective-permute-start(bf16[128,1536]{1,0:T(8,128)(2,1)S(1)} %collective-permute-done.7.refs_6_), channel_id=1, source_target_pairs={{0,1},{1,0},{2,3},{3,2},{4,5},{5,4},{6,7},{7,6},{8,9},{9,8},{10,11... | collective-permute-start | bytes 1179656 | tf_op jit(solution)/shard_map/ppermute | solution.py:322
  35.0 2.3 %collective-permute-start.9 = (bf16[128,1536]{1,0:T(8,128)(2,1)S(1)}, bf16[128,1536]{1,0:T(8,128)(2,1)S(1)}, u32[]{:S(2)}, u32[]{:S(2)}) collective-permute-start(bf16[128,1536]{1,0:T(8,128)(2,1)S(1)} %collective-permute-done.4.refs_4_), channel_id=1, source_target_pairs={{0,1},{1,0},{2,3},{3,2},{4,5},{5,4},{6,7},{7,6},{8,9},{9,8},{10,11... | collective-permute-start | bytes 1179656 | tf_op jit(solution)/shard_map/ppermute | solution.py:322
  42.2 2.0 %collective-permute-start.10 = (bf16[176,256]{1,0:T(8,128)(2,1)S(1)}, bf16[176,256]{1,0:T(8,128)(2,1)S(1)}, u32[]{:S(2)}, u32[]{:S(2)}) collective-permute-start(bf16[176,256]{1,0:T(8,128)(2,1)S(1)} %get-tuple-element.109), channel_id=1, source_target_pairs={{0,1},{1,0},{2,3},{3,2},{4,5},{5,4},{6,7},{7,6},{8,9},{9,8},{10,11... | collective-permute-start | bytes 270344 | tf_op jit(solution)/shard_map/ppermute | solution.py:322
  42.4 1.8 %collective-permute-start.11 = (bf16[176,256]{1,0:T(8,128)(2,1)S(1)}, bf16[176,256]{1,0:T(8,128)(2,1)S(1)}, u32[]{:S(2)}, u32[]{:S(2)}) collective-permute-start(bf16[176,256]{1,0:T(8,128)(2,1)S(1)} %get-tuple-element.110), channel_id=1, source_target_pairs={{0,1},{1,0},{2,3},{3,2},{4,5},{5,4},{6,7},{7,6},{8,9},{9,8},{10,11... | collective-permute-start | bytes 270344 | tf_op jit(solution)/shard_map/ppermute | solution.py:322
  44.3 5.1 %collective-permute-start.12 = (bf16[176,256]{1,0:T(8,128)(2,1)S(1)}, bf16[176,256]{1,0:T(8,128)(2,1)S(1)}, u32[]{:S(2)}, u32[]{:S(2)}) collective-permute-start(bf16[176,256]{1,0:T(8,128)(2,1)S(1)} %get-tuple-element.120), channel_id=1, source_target_pairs={{0,2},{1,3},{2,0},{3,1},{4,6},{5,7},{6,4},{7,5},{8,10},{9,11},{10,... | collective-permute-start | bytes 270344 | tf_op jit(solution)/shard_map/ppermute | solution.py:322
  45.8 9.9 %collective-permute-start.14 = (bf16[256,256]{1,0:T(8,128)(2,1)S(1)}, bf16[256,256]{1,0:T(8,128)(2,1)S(1)}, u32[]{:S(2)}, u32[]{:S(2)}) collective-permute-start(bf16[256,256]{1,0:T(8,128)(2,1)S(1)} %get-tuple-element.121), channel_id=1, source_target_pairs={{0,4},{4,0},{8,12},{12,8},{1,5},{5,1},{9,13},{13,9},{2,6},{6,2},{1... | collective-permute-start | bytes 393224 | tf_op jit(solution)/shard_map/ppermute | solution.py:318
  46.5 9.9 %collective-permute-start.15 = (bf16[256,256]{1,0:T(8,128)(2,1)S(1)}, bf16[256,256]{1,0:T(8,128)(2,1)S(1)}, u32[]{:S(2)}, u32[]{:S(2)}) collective-permute-start(bf16[256,256]{1,0:T(8,128)(2,1)S(1)} %get-tuple-element.122), channel_id=1, source_target_pairs={{0,12},{4,8},{8,4},{12,0},{1,13},{5,9},{9,5},{13,1},{2,14},{6,10},... | collective-permute-start | bytes 393224 | tf_op jit(solution)/shard_map/ppermute | solution.py:318
  49.4 6.2 %collective-permute-start.13 = (bf16[176,256]{1,0:T(8,128)(2,1)S(1)}, bf16[176,256]{1,0:T(8,128)(2,1)S(1)}, u32[]{:S(2)}, u32[]{:S(2)}) collective-permute-start(bf16[176,256]{1,0:T(8,128)(2,1)S(1)} %shard_map.162.refs_0_), channel_id=1, source_target_pairs={{0,4},{4,0},{8,12},{12,8},{1,5},{5,1},{9,13},{13,9},{2,6},{6,2},{1... | collective-permute-start | bytes 270344 | tf_op jit(solution)/shard_map/ppermute | solution.py:322
  56.4 8.4 %collective-permute-start.16 = (bf16[176,256]{1,0:T(8,128)(2,1)S(1)}, bf16[176,256]{1,0:T(8,128)(2,1)S(1)}, u32[]{:S(2)}, u32[]{:S(2)}) collective-permute-start(bf16[176,256]{1,0:T(8,128)(2,1)S(1)} %shard_map.163.refs_0_), channel_id=1, source_target_pairs={{0,8},{4,12},{8,0},{12,4},{1,9},{5,13},{9,1},{13,5},{2,10},{6,14},... | collective-permute-start | bytes 270344 | tf_op jit(solution)/shard_map/ppermute | solution.py:322
  58.1 9.6 %collective-permute-start.19 = (bf16[256,256]{1,0:T(8,128)(2,1)S(1)}, bf16[256,256]{1,0:T(8,128)(2,1)S(1)}, u32[]{:S(2)}, u32[]{:S(2)}) collective-permute-start(bf16[256,256]{1,0:T(8,128)(2,1)S(1)} %get-tuple-element.130), channel_id=1, source_target_pairs={{0,4},{4,0},{8,12},{12,8},{1,5},{5,1},{9,13},{13,9},{2,6},{6,2},{1... | collective-permute-start | bytes 393224 | tf_op jit(solution)/shard_map/ppermute | solution.py:318
  58.9 8.7 %collective-permute-start.20 = (bf16[256,256]{1,0:T(8,128)(2,1)S(1)}, bf16[256,256]{1,0:T(8,128)(2,1)S(1)}, u32[]{:S(2)}, u32[]{:S(2)}) collective-permute-start(bf16[256,256]{1,0:T(8,128)(2,1)S(1)} %get-tuple-element.131), channel_id=1, source_target_pairs={{0,12},{4,8},{8,4},{12,0},{1,13},{5,9},{9,5},{13,1},{2,14},{6,10},... | collective-permute-start | bytes 393224 | tf_op jit(solution)/shard_map/ppermute | solution.py:318
  64.8 5.3 %collective-permute-start.18 = (bf16[176,256]{1,0:T(8,128)(2,1)S(1)}, bf16[176,256]{1,0:T(8,128)(2,1)S(1)}, u32[]{:S(2)}, u32[]{:S(2)}) collective-permute-start(bf16[176,256]{1,0:T(8,128)(2,1)S(1)} %shard_map.165.refs_1_), channel_id=1, source_target_pairs={{0,2},{1,3},{2,0},{3,1},{4,6},{5,7},{6,4},{7,5},{8,10},{9,11},{10,... | collective-permute-start | bytes 270344 | tf_op jit(solution)/shard_map/ppermute | solution.py:322
  67.6 3.6 %collective-permute-start.17 = (bf16[176,256]{1,0:T(8,128)(2,1)S(1)}, bf16[176,256]{1,0:T(8,128)(2,1)S(1)}, u32[]{:S(2)}, u32[]{:S(2)}) collective-permute-start(bf16[176,256]{1,0:T(8,128)(2,1)S(1)} %shard_map.165.refs_1_), channel_id=1, source_target_pairs={{0,1},{1,0},{2,3},{3,2},{4,5},{5,4},{6,7},{7,6},{8,9},{9,8},{10,11... | collective-permute-start | bytes 270344 | tf_op jit(solution)/shard_map/ppermute | solution.py:322
  70.1 1.3 %collective-permute-start.21 = (bf16[176,256]{1,0:T(8,128)(2,1)S(1)}, bf16[176,256]{1,0:T(8,128)(2,1)S(1)}, u32[]{:S(2)}, u32[]{:S(2)}) collective-permute-start(bf16[176,256]{1,0:T(8,128)(2,1)S(1)} %collective-permute-done.18.refs_3_), channel_id=1, source_target_pairs={{0,1},{1,0},{2,3},{3,2},{4,5},{5,4},{6,7},{7,6},{8,9},{9,8},{10,11... | collective-permute-start | bytes 270344 | tf_op jit(solution)/shard_map/ppermute | solution.py:322

commit v13 on v12

--- a/solution.py
+++ b/solution.py
@@ -257,16 +257,15 @@
 
 
 def edges_kernel(members, region_ref, table_ref, w_one_ref, *refs):
-    d_one_refs, refs = refs[:members], refs[members:]
+    d_one_refs, d_mixed_refs, (one_ref, other_ref) = refs[:members], refs[members : 2 * members], refs[2 * members :]
     ext = table_ref.shape[0]
     rows = jnp.concatenate([table_ref[rows, :] for rows in rim_starts(region_ref, ext)], axis=0)
     for m in range(members):
-        d_mixed_ref, one_ref, other_ref = refs[3 * m : 3 * (m + 1)]
         d_mixed = nn_dot(w_one_ref[...], d_one_refs[m][...]).astype(jnp.bfloat16)
-        d_mixed_ref[...] = d_mixed
+        d_mixed_refs[m][...] = d_mixed
         grads = nt_dot(rows, d_mixed).astype(jnp.bfloat16)
-        one_ref[...] = grads[:HALO]
-        other_ref[...] = grads[HALO:]
+        one_ref[m] = grads[:HALO]
+        other_ref[m] = grads[HALO:]
 
 
 def sum_kernel(count, *refs):
@@ -302,20 +301,17 @@
         own_ref[m] = nt_dot(table_ref[HALO : HALO + nodes, :], d_mixed_refs[m][...])
 
 
-def finish_kernel(region_ref, own_ref, *refs):
-    *refs, out_ref = refs
-    members, nodes, _ = own_ref.shape
+def finish_kernel(region_ref, own_ref, one_ref, other_ref, out_ref):
+    nodes = own_ref.shape[1]
     out_ref[:, HALO : nodes - HALO] = own_ref[:, HALO : nodes - HALO].astype(jnp.bfloat16)
-    for m in range(members):
-        for ref, rows in zip(refs[2 * m : 2 * (m + 1)], rim_starts(region_ref, nodes)):
-            out_ref[m, rows] = (own_ref[m, rows] + ref[...].astype(jnp.float32)).astype(jnp.bfloat16)
-
-
-def exchanged(blocks):
+    for ref, rows in zip((one_ref, other_ref), rim_starts(region_ref, nodes)):
+        out_ref[:, rows] = (own_ref[:, rows] + ref[...].astype(jnp.float32)).astype(jnp.bfloat16)
+
+
+def exchanged(block, second):
     size = lax.axis_size("space")
-    one = [(i, i ^ 1) for i in range(size)]
-    other = [(i, (i + 1) % size if i % 2 else (i - 1) % size) for i in range(size)]
-    return [lax.ppermute(block, "space", pairs) for block, pairs in zip(blocks, (one, other))]
+    pairs = [(i, (i + 1) % size if i % 2 else (i - 1) % size) if second else (i, i ^ 1) for i in range(size)]
+    return lax.ppermute(block, "space", pairs)
 
 
 def swapped(block, axis, by):
@@ -339,7 +335,7 @@
     *rims, latent = kernel_call(
         rims_kernel, (edge, edge, shape(latent.shape, bf16)), flops=4 << 30, moved=3 * MIB, smem=1, operands=2
     )(region_at, latent)
-    halo = [exchanged(rims)]
+    halo = [[exchanged(rims[0], False), exchanged(rims[1], True)]]
     rank_at = rank[None].astype(jnp.int32)
 
     table, part, *rims = kernel_call(
@@ -350,7 +346,7 @@
         smem=3,
         operands=6,
     )(region_at, rank_at, counts, neighbours, weights, latent)
-    halo += [exchanged(rims[2 * m : 2 * m + 2]) for m in range(members - 1)]
+    halo += [[exchanged(rims[2 * m], False), exchanged(rims[2 * m + 1], True)] for m in range(members - 1)]
 
     saved_shape = shape((hidden, slots), bf16)
     mixed_shape = shape((width, slots), bf16)
@@ -414,13 +410,13 @@
 
     out = kernel_call(
         lambda *refs: edges_kernel(members, *refs),
-        (mixed_shape, edge, edge) * members,
+        (mixed_shape,) * members + (shape((members, HALO, width), bf16),) * 2,
         flops=2 * members * slots * width * (hidden + 2 * HALO),
         moved=6 * MIB,
         smem=1,
         operands=3 + members,
     )(region_at, table, w_one, *d_one)
-    d_mixed, rims = out[::3], [out[3 * m + 1 : 3 * m + 3] for m in each]
+    d_mixed, rims = out[:members], out[members:]
 
     bit = 1
     while bit < ranks:
@@ -436,23 +432,20 @@
         moved=6 * MIB,
         operands=1 + members,
     )(table, *d_mixed)
-    edges = [block for m in each[:-1] for block in exchanged(rims[m])]
+    other = exchanged(rims[1], True)
     (total,) = pieces
     step = 1
     while step < regions:
         (total,) = summed([total], [swapped(total, "space", step)])
         step = 2 * step
-        if step == regions // 2:
-            total, edges, own, rims = lax.optimization_barrier((total, edges, own, rims))
-            edges = [*edges, *exchanged(rims[-1])]
+        if 2 * step == regions:
+            total, other, own, rims = lax.optimization_barrier((total, other, own, rims))
+            one = exchanged(rims[0], False)
     totals = {0: total}
     bit = 2
     while bit < ranks:
         totals.update({i ^ bit: swapped(totals[i], "member", bit) for i in sorted(totals)})
         bit = 2 * bit
-    far = {i: block for i, block in totals.items() if i}
-    far, edges = lax.optimization_barrier((far, edges))
-    totals.update(far)
     totals.update({i ^ 1: swapped(block, "member", 1) for i, block in totals.items()})
     latent_grad = kernel_call(
         finish_kernel,
@@ -460,8 +453,8 @@
         flops=MIB,
         moved=3 * MIB,
         smem=1,
-        operands=2 + 2 * members,
-    )(region_at, own, *edges)
+        operands=4,
+    )(region_at, own, one, other)
     totals = [totals[i] for i in range(ranks)]
     totals, latent_grad = lax.optimization_barrier((totals, latent_grad))
     row = shape((1, hidden), f32)

time: 72.4 us -> 72.4 us (level)
  starting transfers between devices: 24.2 us -> 21.2 us
  waiting for transfers between devices: 23.3 us -> 26.2 us
    ppermute x8 -> x6, starting transfers between devices: 13.6 us -> 8.98 us  [exchanged(): return lax.ppermute(block, 'space', pairs)]
    ppermute x14, waiting for transfers between devices: 20.1 us -> 23.7 us  [swapped(): lax.ppermute(block, axis, [(i, i ^ by) for i in range(lax.axis_size(axis))])]
    ppermute x14, starting transfers between devices: 10.6 us -> 12.2 us  [swapped(): lax.ppermute(block, axis, [(i, i ^ by) for i in range(lax.axis_size(axis))])]
    ppermute x8 -> x6, waiting for transfers between devices: 3.16 us -> 2.46 us  [exchanged(): return lax.ppermute(block, 'space', pairs)]
  transfers between devices with their start and end apart: 22 -> 20, of which waited for: 11 -> 11; matrix products, arithmetic and copies ran while one was open for 0% -> 0% of each run, Pallas kernels for 23% -> 23%
where the time goes in v13:
time: 72.4 us; the launch traced here: 72.2 us
  waiting for transfers between devices  26.2 us (36%)
  Pallas kernels  22.8 us (31%)
  starting transfers between devices  21.2 us (29%)
  local copies, waits for them, and re-layouts  1.27 us (2%)
  between operations  0.84 us (1%)
    ppermute x14, waiting for transfers between devices, swapped(): lax.ppermute(block, axis, [(i, i ^ by) for i in range(lax.axis_size(axis))])  23.7 us
    ppermute x14, starting transfers between devices, swapped(): lax.ppermute(block, axis, [(i, i ^ by) for i in range(lax.axis_size(axis))])  12.2 us
    ppermute x6, starting transfers between devices, exchanged(): return lax.ppermute(block, 'space', pairs)  8.98 us
    pallas_call x2, Pallas kernels, per_device(): kernel_call(lambda *refs: forward_kernel(m, *refs), (mixed_shape,) + (sav...  6.57 us
    pallas_call x2, Pallas kernels, scored(): kernel_call(lambda *refs: score_kernel(members, len(others), members * ra...  4.77 us
    pallas_call x1, Pallas kernels, per_device(): kernel_call(table_kernel, (shape((ext, slots), bf16), shape((width, slots...  3.13 us
    pallas_call x1, Pallas kernels, per_device(): kernel_call(lambda *refs: backward_kernel(members, ranks, *refs), (saved_...  2.84 us
    ppermute x6, waiting for transfers between devices, exchanged(): return lax.ppermute(block, 'space', pairs)  2.46 us
  transfers between devices with their start and end apart: 20, of which 11 were waited for; matrix products, arithmetic and copies ran while one was open for 0% of the time, Pallas kernels for 23%

profile of v13, /device:TPU:0, one launch (start us, length us, event | category | flops | bytes accessed | tf_op | source)
XLA Modules:
  0.0 72.2 jit_solution(2537506234873498616)
XLA Ops:
  0.6 0.0 copy-start.7
  0.6 1.2 %copy-done.7 = bf16[2,1024,256]{2,1,0:T(8,128)(2,1)S(1)} copy-done((bf16[2,1024,256]{2,1,0:T(8,128)(2,1)S(1)}, bf16[2,1024,256]{2,1,0:T(8,128)(2,1)}, u32[]{:S(2)}) %copy-start.7) | copy-done | bytes 1048600
  1.9 0.1 shard_map.153
  2.0 0.0 copy-start
  2.0 0.0 copy-start.1
  2.0 0.0 copy-start.2
  2.0 0.0 copy-start.4
  2.0 0.0 copy-start.5
  2.0 3.1 %collective-permute-start = (bf16[256,256]{1,0:T(8,128)(2,1)S(1)}, bf16[256,256]{1,0:T(8,128)(2,1)S(1)}, u32[]{:S(2)}, u32[]{:S(2)}) collective-permute-start(bf16[256,256]{1,0:T(8,128)(2,1)S(1)} %get-tuple-element.70), channel_id=1, source_target_pairs={{0,4},{4,0},{8,12},{12,8},{1,5},{5,1},{9,13},{13,9},{2,6},{6,2},{1... | collective-permute-start | bytes 393224 | tf_op jit(solution)/shard_map/ppermute | solution.py:314
  5.1 2.5 %collective-permute-start.1 = (bf16[256,256]{1,0:T(8,128)(2,1)S(1)}, bf16[256,256]{1,0:T(8,128)(2,1)S(1)}, u32[]{:S(2)}, u32[]{:S(2)}) collective-permute-start(bf16[256,256]{1,0:T(8,128)(2,1)S(1)} %get-tuple-element.71), channel_id=1, source_target_pairs={{0,12},{4,8},{8,4},{12,0},{1,13},{5,9},{9,5},{13,1},{2,14},{6,10},... | collective-permute-start | bytes 393224 | tf_op jit(solution)/shard_map/ppermute | solution.py:314
  7.6 0.0 copy-done.8
  7.6 3.1 %shard_map.154 = (bf16[1536,1536]{1,0:T(8,128)(2,1)S(1)}, f32[256,1536]{1,0:T(8,128)S(1)}, bf16[256,256]{1,0:T(8,128)(2,1)S(1)}, bf16[256,256]{1,0:T(8,128)(2,1)S(1)}) custom-call(s32[1]{0:T(128)} %bitcast.1.region_ref.refs_0_, s32[1]{0:T(128)} %bitcast.rank_ref.refs_1_.refs_0_, s32[4]{0:T(128)S(1)} %copy-done.6, s32[4,1536]{1,0:T(4,128)S(1)} %copy-done.8, ...), custom_call_target="tpu_custom_call" | custom-call | flops 805306368 | bytes 12582912 | tf_op jit(solution)/shard_map/pallas_call | solution.py:341
  10.7 0.7 %collective-permute-start.2 = (bf16[256,256]{1,0:T(8,128)(2,1)S(1)}, bf16[256,256]{1,0:T(8,128)(2,1)S(1)}, u32[]{:S(2)}, u32[]{:S(2)}) collective-permute-start(bf16[256,256]{1,0:T(8,128)(2,1)S(1)} %get-tuple-element.73), channel_id=1, source_target_pairs={{0,4},{4,0},{8,12},{12,8},{1,5},{5,1},{9,13},{13,9},{2,6},{6,2},{1... | collective-permute-start | bytes 393224 | tf_op jit(solution)/shard_map/ppermute | solution.py:314
  11.5 0.9 %collective-permute-start.3 = (bf16[256,256]{1,0:T(8,128)(2,1)S(1)}, bf16[256,256]{1,0:T(8,128)(2,1)S(1)}, u32[]{:S(2)}, u32[]{:S(2)}) collective-permute-start(bf16[256,256]{1,0:T(8,128)(2,1)S(1)} %get-tuple-element.74), channel_id=1, source_target_pairs={{0,12},{4,8},{8,4},{12,0},{1,13},{5,9},{9,5},{13,1},{2,14},{6,10},... | collective-permute-start | bytes 393224 | tf_op jit(solution)/shard_map/ppermute | solution.py:314
  12.4 0.0 collective-permute-done.refs_3_
  12.4 2.2 %collective-permute-done.1.refs_4_ = bf16[256,256]{1,0:T(8,128)(2,1)S(1)} collective-permute-done((bf16[256,256]{1,0:T(8,128)(2,1)S(1)}, bf16[256,256]{1,0:T(8,128)(2,1)S(1)}, u32[]{:S(2)}, u32[]{:S(2)}) %collective-permute-start.1) | collective-permute-done | bytes 131104 | tf_op jit(solution)/shard_map/ppermute | solution.py:314
  14.6 0.0 copy-done.2
  14.6 0.0 copy-done.4
  14.7 0.0 copy-done.5
  14.7 2.9 %shard_map.155 = (bf16[256,1536]{1,0:T(8,128)(2,1)S(1)}, bf16[256,1536]{1,0:T(8,128)(2,1)S(1)}, bf16[256,1536]{1,0:T(8,128)(2,1)S(1)}, bf16[256,1536]{1,0:T(8,12...) custom-call(s32[1]{0:T(128)} %bitcast.1.region_ref.refs_0_, ...), custom_call_target="tpu_custom_call" | custom-call | flops 905969664 | bytes 8388608 | tf_op jit(solution)/shard_map/pallas_call | solution.py:357
  17.5 0.0 copy-start.3
  17.6 1.5 %collective-permute-start.7 = (bf16[128,1536]{1,0:T(8,128)(2,1)S(1)}, bf16[128,1536]{1,0:T(8,128)(2,1)S(1)}, u32[]{:S(2)}, u32[]{:S(2)}) collective-permute-start(bf16[128,1536]{1,0:T(8,128)(2,1)S(1)} %get-tuple-element.72.refs_2_), channel_id=1, source_target_pairs={{0,2},{1,3},{2,0},{3,1},{4,6},{5,7},{6,4},{7,5},{8,10},{9,11},{10,... | collective-permute-start | bytes 1179656 | tf_op jit(solution)/shard_map/ppermute | solution.py:318
  19.1 0.0 collective-permute-start.5
  19.1 0.0 collective-permute-done.2.refs_3_
  19.1 0.2 collective-permute-done.3.refs_4_
  19.3 3.7 %shard_map.156 = (bf16[256,1536]{1,0:T(8,128)(2,1)S(1)}, bf16[256,1536]{1,0:T(8,128)(2,1)S(1)}, bf16[256,1536]{1,0:T(8,128)(2,1)S(1)}, bf16[256,1536]{1,0:T(8,12...) custom-call(s32[1]{0:T(128)} %bitcast.1.region_ref.refs_0_, ...), custom_call_target="tpu_custom_call" | custom-call | flops 1711276032 | bytes 8388608 | tf_op jit(solution)/shard_map/pallas_call | solution.py:357
  23.0 0.4 collective-permute-start.6
  23.4 1.3 %collective-permute-start.4 = (bf16[128,1536]{1,0:T(8,128)(2,1)S(1)}, bf16[128,1536]{1,0:T(8,128)(2,1)S(1)}, u32[]{:S(2)}, u32[]{:S(2)}) collective-permute-start(bf16[128,1536]{1,0:T(8,128)(2,1)S(1)} %get-tuple-element.75.refs_3_), channel_id=1, source_target_pairs={{0,2},{1,3},{2,0},{3,1},{4,6},{5,7},{6,4},{7,5},{8,10},{9,11},{10,... | collective-permute-start | bytes 1179656 | tf_op jit(solution)/shard_map/ppermute | solution.py:318
  24.7 2.2 %collective-permute-done.7.refs_6_ = bf16[128,1536]{1,0:T(8,128)(2,1)S(1)} collective-permute-done((bf16[128,1536]{1,0:T(8,128)(2,1)S(1)}, bf16[128,1536]{1,0:T(8,128)(2,1)S(1)}, u32[]{:S(2)}, u32[]{:S(2)}) %collective-permute-start.7) | collective-permute-done | bytes 393248 | tf_op jit(solution)/shard_map/ppermute | solution.py:318
  26.9 0.0 collective-permute-done.5.refs_4_
  26.9 0.0 collective-permute-done.6.refs_5_
  26.9 0.0 copy-done.3
  26.9 2.7 %shard_map.157 = (f32[128,1536]{1,0:T(8,128)S(1)}, f32[128,1536]{1,0:T(8,128)S(1)}, f32[1,128]{1,0:T(1,128)S(1)}) custom-call(s32[1]{0:T(128)} %bitcast.1.region_ref.refs_0_, s32[4]{0:T(128)S(1)} %copy-done.6, bf16[128,1536]{1,0:T(8,128)(2,1)S(1)} %get-tuple-element.72.refs_2_, bf16[128,1536]{1,0:T(8,128)(2,1)S(1)} %get-tuple-element.75.refs_3_, ...), custom_call_target="tpu_custom_call" | custom-call | flops 4194304 | bytes 2097152 | tf_op jit(solution)/shard_map/pallas_call | solution.py:376
  29.6 5.4 %collective-permute-done.4.refs_4_ = bf16[128,1536]{1,0:T(8,128)(2,1)S(1)} collective-permute-done((bf16[128,1536]{1,0:T(8,128)(2,1)S(1)}, bf16[128,1536]{1,0:T(8,128)(2,1)S(1)}, u32[]{:S(2)}, u32[]{:S(2)}) %collective-permute-start.4) | collective-permute-done | bytes 393248 | tf_op jit(solution)/shard_map/ppermute | solution.py:318
  35.0 0.0 collective-permute-start.8
  35.0 0.5 collective-permute-start.9
  35.5 1.2 %collective-permute-done.8.refs_5_ = bf16[128,1536]{1,0:T(8,128)(2,1)S(1)} collective-permute-done((bf16[128,1536]{1,0:T(8,128)(2,1)S(1)}, bf16[128,1536]{1,0:T(8,128)(2,1)S(1)}, u32[]{:S(2)}, u32[]{:S(2)}) %collective-permute-start.8) | collective-permute-done | bytes 393248 | tf_op jit(solution)/shard_map/ppermute | solution.py:318
  36.7 0.6 collective-permute-done.9.refs_6_
  37.3 2.1 %shard_map.158 = (bf16[128,1536]{1,0:T(8,128)(2,1)S(1)}, bf16[128,1536]{1,0:T(8,128)(2,1)S(1)}, f32[1,128]{1,0:T(1,128)S(1)}) custom-call(s32[1]{0:T(128)} %bitcast.1.region_ref.refs_0_, s32[4]{0:T(128)S(1)} %copy-done.6, bf16[128,1536]{1,0:T(8,128)(2,1)S(1)} %get-tuple-element.72.refs_2_, bf16[128,1536]{1,0:T(8,128)(2,1)S(1)} %get-tuple-element.75.refs_3_, ...), custom_call_target="tpu_custom_call" | custom-call | flops 4194304 | bytes 2097152 | tf_op jit(solution)/shard_map/pallas_call | solution.py:376
  39.4 2.8 %shard_map.159 = (bf16[256,1536]{1,0:T(8,128)(2,1)S(1)}, bf16[256,1536]{1,0:T(8,128)(2,1)S(1)}, bf16[176,256]{1,0:T(8,128)(2,1)S(1)}, bf16[176,256]{1,0:T(8,128)...) custom-call(s32[1]{0:T(128)} %bitcast.1.region_ref.refs_0_, s32[1]{0:T(128)} %bitcast.rank_ref.refs_1_.refs_0_, ...), custom_call_target="tpu_custom_call" | custom-call | flops 2013265920 | bytes 10485760 | tf_op jit(solution)/shard_map/pallas_call | solution.py:395
  42.2 0.2 collective-permute-start.10
  42.4 0.4 collective-permute-start.11
  42.8 1.4 %shard_map.160 = (bf16[256,1536]{1,0:T(8,128)(2,1)S(1)}, bf16[256,1536]{1,0:T(8,128)(2,1)S(1)}, bf16[2,256,256]{2,1,0:T(8,128)(2,1)S(1)}, bf16[2,256,256]{2,1,0:T(8,128)(2,1)S(1)}) custom-call(s32[1]{0:T(128)} %bitcast.1.region_ref.refs_0_, bf16[1536,1536]{1,0:T(8,128)(2,1)S(1)} %get-tuple-element.69.refs_2_.refs_1_.table_ref, ...), custom_call_target="tpu_custom_call" | custom-call | flops 1207959552 | bytes 6291456 | tf_op jit(solution)/shard_map/pallas_call | solution.py:411
  44.2 0.0 collective-permute-done.10.refs_2_
  44.2 0.0 collective-permute-done.11.refs_3_
  44.2 1.8 %collective-permute-start.14 = (bf16[2,256,256]{2,1,0:T(8,128)(2,1)S(1)}, bf16[2,256,256]{2,1,0:T(8,128)(2,1)S(1)}, u32[]{:S(2)}, u32[]{:S(2)}) collective-permute-start(bf16[2,256,256]{2,1,0:T(8,128)(2,1)S(1)} %get-tuple-element.108), channel_id=1, source_target_pairs={{0,12},{4,8},{8,4},{12,0},{1,13},{5,9},{9,5},{13,1},{2,14},{6,10},... | collective-permute-start | bytes 786440 | tf_op jit(solution)/shard_map/ppermute | solution.py:314
  46.0 1.6 %collective-permute-start.12 = (bf16[176,256]{1,0:T(8,128)(2,1)S(1)}, bf16[176,256]{1,0:T(8,128)(2,1)S(1)}, u32[]{:S(2)}, u32[]{:S(2)}) collective-permute-start(bf16[176,256]{1,0:T(8,128)(2,1)S(1)} %get-tuple-element.107), channel_id=1, source_target_pairs={{0,2},{1,3},{2,0},{3,1},{4,6},{5,7},{6,4},{7,5},{8,10},{9,11},{10,... | collective-permute-start | bytes 270344 | tf_op jit(solution)/shard_map/ppermute | solution.py:318
  47.6 3.0 %collective-permute-done.12.refs_1_ = bf16[176,256]{1,0:T(8,128)(2,1)S(1)} collective-permute-done((bf16[176,256]{1,0:T(8,128)(2,1)S(1)}, bf16[176,256]{1,0:T(8,128)(2,1)S(1)}, u32[]{:S(2)}, u32[]{:S(2)}) %collective-permute-start.12) | collective-permute-done | bytes 90144 | tf_op jit(solution)/shard_map/ppermute | solution.py:318
  50.6 1.7 %collective-permute-start.13 = (bf16[176,256]{1,0:T(8,128)(2,1)S(1)}, bf16[176,256]{1,0:T(8,128)(2,1)S(1)}, u32[]{:S(2)}, u32[]{:S(2)}) collective-permute-start(bf16[176,256]{1,0:T(8,128)(2,1)S(1)} %shard_map.162.refs_0_), channel_id=1, source_target_pairs={{0,4},{4,0},{8,12},{12,8},{1,5},{5,1},{9,13},{13,9},{2,6},{6,2},{1... | collective-permute-start | bytes 270344 | tf_op jit(solution)/shard_map/ppermute | solution.py:318
  52.4 1.8 %shard_map.164.own_ref = f32[2,1024,256]{2,1,0:T(8,128)S(1)} custom-call(bf16[1536,1536]{1,0:T(8,128)(2,1)S(1)} %get-tuple-element.69.refs_2_.refs_1_.table_ref, bf16[256,1536]{1,0:T(8,128)(2,1)S(1)} %get-tuple-element.109.refs_0_, bf16[256,1536]{1,0:T(8,128)(2,1)S(1)} %get-tuple-element.110.refs_1_), custom_call_target="tpu_custom_call" | custom-call | flops 1610612736 | bytes 6291456 | tf_op jit(solution)/shard_map/pallas_call | solution.py:428
  54.2 2.3 %collective-permute-done.13.refs_1_ = bf16[176,256]{1,0:T(8,128)(2,1)S(1)} collective-permute-done((bf16[176,256]{1,0:T(8,128)(2,1)S(1)}, bf16[176,256]{1,0:T(8,128)(2,1)S(1)}, u32[]{:S(2)}, u32[]{:S(2)}) %collective-permute-start.13) | collective-permute-done | bytes 90144 | tf_op jit(solution)/shard_map/ppermute | solution.py:318
  56.5 0.0 collective-permute-done.14.other_ref
  56.5 4.3 %collective-permute-start.15 = (bf16[176,256]{1,0:T(8,128)(2,1)S(1)}, bf16[176,256]{1,0:T(8,128)(2,1)S(1)}, u32[]{:S(2)}, u32[]{:S(2)}) collective-permute-start(bf16[176,256]{1,0:T(8,128)(2,1)S(1)} %shard_map.163.refs_0_), channel_id=1, source_target_pairs={{0,8},{4,12},{8,0},{12,4},{1,9},{5,13},{9,1},{13,5},{2,10},{6,14},... | collective-permute-start | bytes 270344 | tf_op jit(solution)/shard_map/ppermute | solution.py:318
  60.8 0.0 collective-permute-start.19
  60.8 4.6 %collective-permute-done.15.refs_1_ = bf16[176,256]{1,0:T(8,128)(2,1)S(1)} collective-permute-done((bf16[176,256]{1,0:T(8,128)(2,1)S(1)}, bf16[176,256]{1,0:T(8,128)(2,1)S(1)}, u32[]{:S(2)}, u32[]{:S(2)}) %collective-permute-start.15) | collective-permute-done | bytes 90144 | tf_op jit(solution)/shard_map/ppermute | solution.py:318
  65.5 0.3 collective-permute-start.17
  65.8 0.0 collective-permute-start.16
  65.8 4.3 %collective-permute-done.17.refs_3_ = bf16[176,256]{1,0:T(8,128)(2,1)S(1)} collective-permute-done((bf16[176,256]{1,0:T(8,128)(2,1)S(1)}, bf16[176,256]{1,0:T(8,128)(2,1)S(1)}, u32[]{:S(2)}, u32[]{:S(2)}) %collective-permute-start.17) | collective-permute-done | bytes 90144 | tf_op jit(solution)/shard_map/ppermute | solution.py:318
  70.1 0.0 collective-permute-start.18
  70.1 0.0 collective-permute-done.19.one_ref
  70.1 1.1 %shard_map.166 = bf16[2,1024,256]{2,1,0:T(8,128)(2,1)} custom-call(s32[1]{0:T(128)} %bitcast.1.region_ref.refs_0_, f32[2,1024,256]{2,1,0:T(8,128)S(1)} %shard_map.164.own_ref, bf16[2,256,256]{2,1,0:T(8,128)(2,1)S(1)} %collective-permute-done.19.one_ref, bf16[2,256,256]{2,1,0:T(8,128)(2,1)S(1)} %collective-permute-done.14.other_ref), custom_call_target="tpu_custom_call" | custom-call | flops 1048576 | bytes 3145728 | tf_op jit(solution)/shard_map/pallas_call | solution.py:450
  71.2 0.0 collective-permute-done.16.refs_2_
  71.2 0.1 collective-permute-done.18.refs_4_
  71.3 0.9 %shard_map.167 = (f32[256,256]{1,0:T(8,128)}, f32[1,256]{1,0:T(1,128)}, f32[256,256]{1,0:T(8,128)}, f32[1,256]{1,0:T(1,128)}, f32[256,128]{1,0:T(8,128)}, /*index=5*/f32[1,4]{1,0:T(1,128)}) custom-call(s32[1]{0:T(128)} %bitcast.rank_ref.refs_1_.refs_0_, bf16[176,256]{1,0:T(8,128)(2,1)S(1)} %shard_map.165.refs_1_, ...), custom_call_target="tpu_custom_call" | custom-call | flops 1048576 | bytes 2097152 | tf_op jit(solution)/shard_map/pallas_call | solution.py:461
  (11 shorter events, 0.1 us)
Async XLA Ops:
  0.6 1.2 %copy-start.7 = (bf16[2,1024,256]{2,1,0:T(8,128)(2,1)S(1)}, bf16[2,1024,256]{2,1,0:T(8,128)(2,1)}, u32[]{:S(2)}) copy-start(bf16[2,1024,256]{2,1,0:T(8,128)(2,1)} %latent_ref.1) | copy-start | bytes 3145732
  1.9 5.7 %copy-start.6 = (s32[4]{0:T(128)S(1)}, s32[4]{0:T(128)}, u32[]{:S(2)}) copy-start(s32[4]{0:T(128)} %refs_1_.3) | copy-start | bytes 52
  1.9 5.7 %copy-start.8 = (s32[4,1536]{1,0:T(4,128)S(1)}, s32[4,1536]{1,0:T(4,128)}, u32[]{:S(2)}) copy-start(s32[4,1536]{1,0:T(4,128)} %nbr_ref.1) | copy-start | bytes 73732
  1.9 5.7 %copy-start.9 = (f32[4,1536]{1,0:T(4,128)S(1)}, f32[4,1536]{1,0:T(4,128)}, u32[]{:S(2)}) copy-start(f32[4,1536]{1,0:T(4,128)} %weight_ref.1) | copy-start | bytes 73732
  2.0 12.7 %copy-start = (bf16[256,256]{1,0:T(8,128)(2,1)S(1)}, bf16[256,256]{1,0:T(8,128)(2,1)}, u32[]{:S(2)}) copy-start(bf16[256,256]{1,0:T(8,128)(2,1)} %refs_2_.2) | copy-start | bytes 393220
  2.0 12.7 %copy-start.1 = (bf16[256,256]{1,0:T(8,128)(2,1)S(1)}, bf16[256,256]{1,0:T(8,128)(2,1)}, u32[]{:S(2)}) copy-start(bf16[256,256]{1,0:T(8,128)(2,1)} %refs_2_.3) | copy-start | bytes 393220
  2.0 12.7 %copy-start.2 = (bf16[256,128]{1,0:T(8,128)(2,1)S(1)}, bf16[256,128]{1,0:T(8,128)(2,1)}, u32[]{:S(2)}) copy-start(bf16[256,128]{1,0:T(8,128)(2,1)} %refs_3_.1) | copy-start | bytes 196612
  2.0 12.6 %copy-start.4 = (f32[256]{0:T(256)S(1)}, f32[256]{0:T(256)}, u32[]{:S(2)}) copy-start(f32[256]{0:T(256)} %param.16) | copy-start | bytes 3076
  2.0 12.6 %copy-start.5 = (f32[256]{0:T(256)S(1)}, f32[256]{0:T(256)}, u32[]{:S(2)}) copy-start(f32[256]{0:T(256)} %param.18) | copy-start | bytes 3076
  2.0 10.4 %collective-permute-start = (bf16[256,256]{1,0:T(8,128)(2,1)S(1)}, bf16[256,256]{1,0:T(8,128)(2,1)S(1)}, u32[]{:S(2)}, u32[]{:S(2)}) collective-permute-start(bf16[256,256]{1,0:T(8,128)(2,1)S(1)} %get-tuple-element.70), channel_id=1, source_target_pairs={{0,4},{4,0},{8,12},{12,8},{1,5},{5,1},{9,13},{13,9},{2,6},{6,2},{1... | collective-permute-start | bytes 393224 | tf_op jit(solution)/shard_map/ppermute | solution.py:314
  5.1 9.5 %collective-permute-start.1 = (bf16[256,256]{1,0:T(8,128)(2,1)S(1)}, bf16[256,256]{1,0:T(8,128)(2,1)S(1)}, u32[]{:S(2)}, u32[]{:S(2)}) collective-permute-start(bf16[256,256]{1,0:T(8,128)(2,1)S(1)} %get-tuple-element.71), channel_id=1, source_target_pairs={{0,12},{4,8},{8,4},{12,0},{1,13},{5,9},{9,5},{13,1},{2,14},{6,10},... | collective-permute-start | bytes 393224 | tf_op jit(solution)/shard_map/ppermute | solution.py:314
  10.7 8.4 %collective-permute-start.2 = (bf16[256,256]{1,0:T(8,128)(2,1)S(1)}, bf16[256,256]{1,0:T(8,128)(2,1)S(1)}, u32[]{:S(2)}, u32[]{:S(2)}) collective-permute-start(bf16[256,256]{1,0:T(8,128)(2,1)S(1)} %get-tuple-element.73), channel_id=1, source_target_pairs={{0,4},{4,0},{8,12},{12,8},{1,5},{5,1},{9,13},{13,9},{2,6},{6,2},{1... | collective-permute-start | bytes 393224 | tf_op jit(solution)/shard_map/ppermute | solution.py:314
  11.5 7.8 %collective-permute-start.3 = (bf16[256,256]{1,0:T(8,128)(2,1)S(1)}, bf16[256,256]{1,0:T(8,128)(2,1)S(1)}, u32[]{:S(2)}, u32[]{:S(2)}) collective-permute-start(bf16[256,256]{1,0:T(8,128)(2,1)S(1)} %get-tuple-element.74), channel_id=1, source_target_pairs={{0,12},{4,8},{8,4},{12,0},{1,13},{5,9},{9,5},{13,1},{2,14},{6,10},... | collective-permute-start | bytes 393224 | tf_op jit(solution)/shard_map/ppermute | solution.py:314
  17.5 9.4 %copy-start.3 = (bf16[1536,128]{1,0:T(8,128)(2,1)S(1)}, bf16[1536,128]{1,0:T(8,128)(2,1)}, u32[]{:S(2)}) copy-start(bf16[1536,128]{1,0:T(8,128)(2,1)} %refs_7_.5) | copy-start | bytes 1179652
  17.6 9.3 %collective-permute-start.7 = (bf16[128,1536]{1,0:T(8,128)(2,1)S(1)}, bf16[128,1536]{1,0:T(8,128)(2,1)S(1)}, u32[]{:S(2)}, u32[]{:S(2)}) collective-permute-start(bf16[128,1536]{1,0:T(8,128)(2,1)S(1)} %get-tuple-element.72.refs_2_), channel_id=1, source_target_pairs={{0,2},{1,3},{2,0},{3,1},{4,6},{5,7},{6,4},{7,5},{8,10},{9,11},{10,... | collective-permute-start | bytes 1179656 | tf_op jit(solution)/shard_map/ppermute | solution.py:318
  19.1 7.8 %collective-permute-start.5 = (bf16[128,1536]{1,0:T(8,128)(2,1)S(1)}, bf16[128,1536]{1,0:T(8,128)(2,1)S(1)}, u32[]{:S(2)}, u32[]{:S(2)}) collective-permute-start(bf16[128,1536]{1,0:T(8,128)(2,1)S(1)} %get-tuple-element.72.refs_2_), channel_id=1, source_target_pairs={{0,1},{1,0},{2,3},{3,2},{4,5},{5,4},{6,7},{7,6},{8,9},{9,8},{10,11... | collective-permute-start | bytes 1179656 | tf_op jit(solution)/shard_map/ppermute | solution.py:318
  23.0 3.9 %collective-permute-start.6 = (bf16[128,1536]{1,0:T(8,128)(2,1)S(1)}, bf16[128,1536]{1,0:T(8,128)(2,1)S(1)}, u32[]{:S(2)}, u32[]{:S(2)}) collective-permute-start(bf16[128,1536]{1,0:T(8,128)(2,1)S(1)} %get-tuple-element.75.refs_3_), channel_id=1, source_target_pairs={{0,1},{1,0},{2,3},{3,2},{4,5},{5,4},{6,7},{7,6},{8,9},{9,8},{10,11... | collective-permute-start | bytes 1179656 | tf_op jit(solution)/shard_map/ppermute | solution.py:318
  23.4 11.6 %collective-permute-start.4 = (bf16[128,1536]{1,0:T(8,128)(2,1)S(1)}, bf16[128,1536]{1,0:T(8,128)(2,1)S(1)}, u32[]{:S(2)}, u32[]{:S(2)}) collective-permute-start(bf16[128,1536]{1,0:T(8,128)(2,1)S(1)} %get-tuple-element.75.refs_3_), channel_id=1, source_target_pairs={{0,2},{1,3},{2,0},{3,1},{4,6},{5,7},{6,4},{7,5},{8,10},{9,11},{10,... | collective-permute-start | bytes 1179656 | tf_op jit(solution)/shard_map/ppermute | solution.py:318
  35.0 1.7 %collective-permute-start.8 = (bf16[128,1536]{1,0:T(8,128)(2,1)S(1)}, bf16[128,1536]{1,0:T(8,128)(2,1)S(1)}, u32[]{:S(2)}, u32[]{:S(2)}) collective-permute-start(bf16[128,1536]{1,0:T(8,128)(2,1)S(1)} %collective-permute-done.7.refs_6_), channel_id=1, source_target_pairs={{0,1},{1,0},{2,3},{3,2},{4,5},{5,4},{6,7},{7,6},{8,9},{9,8},{10,11... | collective-permute-start | bytes 1179656 | tf_op jit(solution)/shard_map/ppermute | solution.py:318
  35.0 2.3 %collective-permute-start.9 = (bf16[128,1536]{1,0:T(8,128)(2,1)S(1)}, bf16[128,1536]{1,0:T(8,128)(2,1)S(1)}, u32[]{:S(2)}, u32[]{:S(2)}) collective-permute-start(bf16[128,1536]{1,0:T(8,128)(2,1)S(1)} %collective-permute-done.4.refs_4_), channel_id=1, source_target_pairs={{0,1},{1,0},{2,3},{3,2},{4,5},{5,4},{6,7},{7,6},{8,9},{9,8},{10,11... | collective-permute-start | bytes 1179656 | tf_op jit(solution)/shard_map/ppermute | solution.py:318
  42.2 2.0 %collective-permute-start.10 = (bf16[176,256]{1,0:T(8,128)(2,1)S(1)}, bf16[176,256]{1,0:T(8,128)(2,1)S(1)}, u32[]{:S(2)}, u32[]{:S(2)}) collective-permute-start(bf16[176,256]{1,0:T(8,128)(2,1)S(1)} %get-tuple-element.98), channel_id=1, source_target_pairs={{0,1},{1,0},{2,3},{3,2},{4,5},{5,4},{6,7},{7,6},{8,9},{9,8},{10,11... | collective-permute-start | bytes 270344 | tf_op jit(solution)/shard_map/ppermute | solution.py:318
  42.4 1.8 %collective-permute-start.11 = (bf16[176,256]{1,0:T(8,128)(2,1)S(1)}, bf16[176,256]{1,0:T(8,128)(2,1)S(1)}, u32[]{:S(2)}, u32[]{:S(2)}) collective-permute-start(bf16[176,256]{1,0:T(8,128)(2,1)S(1)} %get-tuple-element.99), channel_id=1, source_target_pairs={{0,1},{1,0},{2,3},{3,2},{4,5},{5,4},{6,7},{7,6},{8,9},{9,8},{10,11... | collective-permute-start | bytes 270344 | tf_op jit(solution)/shard_map/ppermute | solution.py:318
  44.2 12.3 %collective-permute-start.14 = (bf16[2,256,256]{2,1,0:T(8,128)(2,1)S(1)}, bf16[2,256,256]{2,1,0:T(8,128)(2,1)S(1)}, u32[]{:S(2)}, u32[]{:S(2)}) collective-permute-start(bf16[2,256,256]{2,1,0:T(8,128)(2,1)S(1)} %get-tuple-element.108), channel_id=1, source_target_pairs={{0,12},{4,8},{8,4},{12,0},{1,13},{5,9},{9,5},{13,1},{2,14},{6,10},... | collective-permute-start | bytes 786440 | tf_op jit(solution)/shard_map/ppermute | solution.py:314
  46.0 4.6 %collective-permute-start.12 = (bf16[176,256]{1,0:T(8,128)(2,1)S(1)}, bf16[176,256]{1,0:T(8,128)(2,1)S(1)}, u32[]{:S(2)}, u32[]{:S(2)}) collective-permute-start(bf16[176,256]{1,0:T(8,128)(2,1)S(1)} %get-tuple-element.107), channel_id=1, source_target_pairs={{0,2},{1,3},{2,0},{3,1},{4,6},{5,7},{6,4},{7,5},{8,10},{9,11},{10,... | collective-permute-start | bytes 270344 | tf_op jit(solution)/shard_map/ppermute | solution.py:318
  50.6 5.8 %collective-permute-start.13 = (bf16[176,256]{1,0:T(8,128)(2,1)S(1)}, bf16[176,256]{1,0:T(8,128)(2,1)S(1)}, u32[]{:S(2)}, u32[]{:S(2)}) collective-permute-start(bf16[176,256]{1,0:T(8,128)(2,1)S(1)} %shard_map.162.refs_0_), channel_id=1, source_target_pairs={{0,4},{4,0},{8,12},{12,8},{1,5},{5,1},{9,13},{13,9},{2,6},{6,2},{1... | collective-permute-start | bytes 270344 | tf_op jit(solution)/shard_map/ppermute | solution.py:318
  56.5 8.9 %collective-permute-start.15 = (bf16[176,256]{1,0:T(8,128)(2,1)S(1)}, bf16[176,256]{1,0:T(8,128)(2,1)S(1)}, u32[]{:S(2)}, u32[]{:S(2)}) collective-permute-start(bf16[176,256]{1,0:T(8,128)(2,1)S(1)} %shard_map.163.refs_0_), channel_id=1, source_target_pairs={{0,8},{4,12},{8,0},{12,4},{1,9},{5,13},{9,1},{13,5},{2,10},{6,14},... | collective-permute-start | bytes 270344 | tf_op jit(solution)/shard_map/ppermute | solution.py:318
  60.8 9.2 %collective-permute-start.19 = (bf16[2,256,256]{2,1,0:T(8,128)(2,1)S(1)}, bf16[2,256,256]{2,1,0:T(8,128)(2,1)S(1)}, u32[]{:S(2)}, u32[]{:S(2)}) collective-permute-start(bf16[2,256,256]{2,1,0:T(8,128)(2,1)S(1)} %get-tuple-element.114), channel_id=1, source_target_pairs={{0,4},{4,0},{8,12},{12,8},{1,5},{5,1},{9,13},{13,9},{2,6},{6,2},{1... | collective-permute-start | bytes 786440 | tf_op jit(solution)/shard_map/ppermute | solution.py:314
  65.5 4.6 %collective-permute-start.17 = (bf16[176,256]{1,0:T(8,128)(2,1)S(1)}, bf16[176,256]{1,0:T(8,128)(2,1)S(1)}, u32[]{:S(2)}, u32[]{:S(2)}) collective-permute-start(bf16[176,256]{1,0:T(8,128)(2,1)S(1)} %shard_map.165.refs_1_), channel_id=1, source_target_pairs={{0,2},{1,3},{2,0},{3,1},{4,6},{5,7},{6,4},{7,5},{8,10},{9,11},{10,... | collective-permute-start | bytes 270344 | tf_op jit(solution)/shard_map/ppermute | solution.py:318
  65.8 5.4 %collective-permute-start.16 = (bf16[176,256]{1,0:T(8,128)(2,1)S(1)}, bf16[176,256]{1,0:T(8,128)(2,1)S(1)}, u32[]{:S(2)}, u32[]{:S(2)}) collective-permute-start(bf16[176,256]{1,0:T(8,128)(2,1)S(1)} %shard_map.165.refs_1_), channel_id=1, source_target_pairs={{0,1},{1,0},{2,3},{3,2},{4,5},{5,4},{6,7},{7,6},{8,9},{9,8},{10,11... | collective-permute-start | bytes 270344 | tf_op jit(solution)/shard_map/ppermute | solution.py:318
  70.1 1.3 %collective-permute-start.18 = (bf16[176,256]{1,0:T(8,128)(2,1)S(1)}, bf16[176,256]{1,0:T(8,128)(2,1)S(1)}, u32[]{:S(2)}, u32[]{:S(2)}) collective-permute-start(bf16[176,256]{1,0:T(8,128)(2,1)S(1)} %collective-permute-done.17.refs_3_), channel_id=1, source_target_pairs={{0,1},{1,0},{2,3},{3,2},{4,5},{5,4},{6,7},{7,6},{8,9},{9,8},{10,11... | collective-permute-start | bytes 270344 | tf_op jit(solution)/shard_map/ppermute | solution.py:318

commit v14 on v13

--- a/solution.py
+++ b/solution.py
@@ -436,10 +436,13 @@
     (total,) = pieces
     step = 1
     while step < regions:
-        (total,) = summed([total], [swapped(total, "space", step)])
+        received = swapped(total, "space", step)
         step = 2 * step
+        if step == regions:
+            received, other = lax.optimization_barrier((received, other))
+        (total,) = summed([total], [received])
         if 2 * step == regions:
-            total, other, own, rims = lax.optimization_barrier((total, other, own, rims))
+            total, own, rims = lax.optimization_barrier((total, own, rims))
             one = exchanged(rims[0], False)
     totals = {0: total}
     bit = 2

time: 72.4 us -> 71.2 us (0.983)
  starting transfers between devices: 21.2 us -> 18.6 us
  waiting for transfers between devices: 26.2 us -> 27.6 us
    ppermute x14, starting transfers between devices: 12.2 us -> 8.04 us  [swapped(): lax.ppermute(block, axis, [(i, i ^ by) for i in range(lax.axis_size(axis))])]
    ppermute x6, starting transfers between devices: 8.98 us -> 10.6 us  [exchanged(): return lax.ppermute(block, 'space', pairs)]
    ppermute x14, waiting for transfers between devices: 23.7 us -> 25.1 us  [swapped(): lax.ppermute(block, axis, [(i, i ^ by) for i in range(lax.axis_size(axis))])]
  transfers between devices with their start and end apart: 20 -> 20, of which waited for: 11 -> 11; matrix products, arithmetic and copies ran while one was open for 0% -> 0% of each run, Pallas kernels for 23% -> 24%
where the time goes in v14:
time: 71.2 us; the launch traced here: 71.1 us
  waiting for transfers between devices  27.6 us (39%)
  Pallas kernels  22.8 us (32%)
  starting transfers between devices  18.6 us (26%)
  local copies, waits for them, and re-layouts  1.27 us (2%)
  between operations  0.83 us (1%)
    ppermute x14, waiting for transfers between devices, swapped(): lax.ppermute(block, axis, [(i, i ^ by) for i in range(lax.axis_size(axis))])  25.1 us
    ppermute x6, starting transfers between devices, exchanged(): return lax.ppermute(block, 'space', pairs)  10.6 us
    ppermute x14, starting transfers between devices, swapped(): lax.ppermute(block, axis, [(i, i ^ by) for i in range(lax.axis_size(axis))])  8.04 us
    pallas_call x2, Pallas kernels, per_device(): kernel_call(lambda *refs: forward_kernel(m, *refs), (mixed_shape,) + (sav...  6.57 us
    pallas_call x2, Pallas kernels, scored(): kernel_call(lambda *refs: score_kernel(members, len(others), members * ra...  4.77 us
    pallas_call x1, Pallas kernels, per_device(): kernel_call(table_kernel, (shape((ext, slots), bf16), shape((width, slots...  3.13 us
    pallas_call x1, Pallas kernels, per_device(): kernel_call(lambda *refs: backward_kernel(members, ranks, *refs), (saved_...  2.84 us
    ppermute x6, waiting for transfers between devices, exchanged(): return lax.ppermute(block, 'space', pairs)  2.46 us
  transfers between devices with their start and end apart: 20, of which 11 were waited for; matrix products, arithmetic and copies ran while one was open for 0% of the time, Pallas kernels for 24%

profile of v14, /device:TPU:0, one launch (start us, length us, event | category | flops | bytes accessed | tf_op | source)
XLA Modules:
  0.0 71.1 jit_solution(13357133283944154659)
XLA Ops:
  0.6 0.0 copy-start.7
  0.6 1.2 %copy-done.7 = bf16[2,1024,256]{2,1,0:T(8,128)(2,1)S(1)} copy-done((bf16[2,1024,256]{2,1,0:T(8,128)(2,1)S(1)}, bf16[2,1024,256]{2,1,0:T(8,128)(2,1)}, u32[]{:S(2)}) %copy-start.7) | copy-done | bytes 1048600
  1.9 0.1 shard_map.153
  2.0 0.0 copy-start
  2.0 0.0 copy-start.1
  2.0 0.0 copy-start.2
  2.0 0.0 copy-start.4
  2.0 0.0 copy-start.5
  2.0 3.1 %collective-permute-start = (bf16[256,256]{1,0:T(8,128)(2,1)S(1)}, bf16[256,256]{1,0:T(8,128)(2,1)S(1)}, u32[]{:S(2)}, u32[]{:S(2)}) collective-permute-start(bf16[256,256]{1,0:T(8,128)(2,1)S(1)} %get-tuple-element.71), channel_id=1, source_target_pairs={{0,4},{4,0},{8,12},{12,8},{1,5},{5,1},{9,13},{13,9},{2,6},{6,2},{1... | collective-permute-start | bytes 393224 | tf_op jit(solution)/shard_map/ppermute | solution.py:314
  5.1 2.5 %collective-permute-start.1 = (bf16[256,256]{1,0:T(8,128)(2,1)S(1)}, bf16[256,256]{1,0:T(8,128)(2,1)S(1)}, u32[]{:S(2)}, u32[]{:S(2)}) collective-permute-start(bf16[256,256]{1,0:T(8,128)(2,1)S(1)} %get-tuple-element.72), channel_id=1, source_target_pairs={{0,12},{4,8},{8,4},{12,0},{1,13},{5,9},{9,5},{13,1},{2,14},{6,10},... | collective-permute-start | bytes 393224 | tf_op jit(solution)/shard_map/ppermute | solution.py:314
  7.6 0.0 copy-done.6
  7.6 0.0 copy-done.8
  7.6 0.0 copy-done.9
  7.6 3.1 %shard_map.154 = (bf16[1536,1536]{1,0:T(8,128)(2,1)S(1)}, f32[256,1536]{1,0:T(8,128)S(1)}, bf16[256,256]{1,0:T(8,128)(2,1)S(1)}, bf16[256,256]{1,0:T(8,128)(2,1)S(1)}) custom-call(s32[1]{0:T(128)} %bitcast.1.region_ref.refs_0_, s32[1]{0:T(128)} %bitcast.rank_ref.refs_1_.refs_0_, s32[4]{0:T(128)S(1)} %copy-done.6, s32[4,1536]{1,0:T(4,128)S(1)} %copy-done.8, ...), custom_call_target="tpu_custom_call" | custom-call | flops 805306368 | bytes 12582912 | tf_op jit(solution)/shard_map/pallas_call | solution.py:341
  10.7 0.7 %collective-permute-start.2 = (bf16[256,256]{1,0:T(8,128)(2,1)S(1)}, bf16[256,256]{1,0:T(8,128)(2,1)S(1)}, u32[]{:S(2)}, u32[]{:S(2)}) collective-permute-start(bf16[256,256]{1,0:T(8,128)(2,1)S(1)} %get-tuple-element.74), channel_id=1, source_target_pairs={{0,4},{4,0},{8,12},{12,8},{1,5},{5,1},{9,13},{13,9},{2,6},{6,2},{1... | collective-permute-start | bytes 393224 | tf_op jit(solution)/shard_map/ppermute | solution.py:314
  11.5 0.9 %collective-permute-start.3 = (bf16[256,256]{1,0:T(8,128)(2,1)S(1)}, bf16[256,256]{1,0:T(8,128)(2,1)S(1)}, u32[]{:S(2)}, u32[]{:S(2)}) collective-permute-start(bf16[256,256]{1,0:T(8,128)(2,1)S(1)} %get-tuple-element.75), channel_id=1, source_target_pairs={{0,12},{4,8},{8,4},{12,0},{1,13},{5,9},{9,5},{13,1},{2,14},{6,10},... | collective-permute-start | bytes 393224 | tf_op jit(solution)/shard_map/ppermute | solution.py:314
  12.4 0.0 collective-permute-done.refs_3_
  12.4 2.2 %collective-permute-done.1.refs_4_ = bf16[256,256]{1,0:T(8,128)(2,1)S(1)} collective-permute-done((bf16[256,256]{1,0:T(8,128)(2,1)S(1)}, bf16[256,256]{1,0:T(8,128)(2,1)S(1)}, u32[]{:S(2)}, u32[]{:S(2)}) %collective-permute-start.1) | collective-permute-done | bytes 131104 | tf_op jit(solution)/shard_map/ppermute | solution.py:314
  14.6 0.0 copy-done
  14.6 0.0 copy-done.2
  14.7 2.9 %shard_map.155 = (bf16[256,1536]{1,0:T(8,128)(2,1)S(1)}, bf16[256,1536]{1,0:T(8,128)(2,1)S(1)}, bf16[256,1536]{1,0:T(8,128)(2,1)S(1)}, bf16[256,1536]{1,0:T(8,12...) custom-call(s32[1]{0:T(128)} %bitcast.1.region_ref.refs_0_, ...), custom_call_target="tpu_custom_call" | custom-call | flops 905969664 | bytes 8388608 | tf_op jit(solution)/shard_map/pallas_call | solution.py:357
  17.5 0.0 copy-start.3
  17.6 1.5 %collective-permute-start.7 = (bf16[128,1536]{1,0:T(8,128)(2,1)S(1)}, bf16[128,1536]{1,0:T(8,128)(2,1)S(1)}, u32[]{:S(2)}, u32[]{:S(2)}) collective-permute-start(bf16[128,1536]{1,0:T(8,128)(2,1)S(1)} %get-tuple-element.73.refs_2_), channel_id=1, source_target_pairs={{0,2},{1,3},{2,0},{3,1},{4,6},{5,7},{6,4},{7,5},{8,10},{9,11},{10,... | collective-permute-start | bytes 1179656 | tf_op jit(solution)/shard_map/ppermute | solution.py:318
  19.1 0.0 collective-permute-start.5
  19.1 0.0 collective-permute-done.2.refs_3_
  19.1 0.2 collective-permute-done.3.refs_4_
  19.3 3.7 %shard_map.156 = (bf16[256,1536]{1,0:T(8,128)(2,1)S(1)}, bf16[256,1536]{1,0:T(8,128)(2,1)S(1)}, bf16[256,1536]{1,0:T(8,128)(2,1)S(1)}, bf16[256,1536]{1,0:T(8,12...) custom-call(s32[1]{0:T(128)} %bitcast.1.region_ref.refs_0_, ...), custom_call_target="tpu_custom_call" | custom-call | flops 1711276032 | bytes 8388608 | tf_op jit(solution)/shard_map/pallas_call | solution.py:357
  23.0 0.4 collective-permute-start.6
  23.4 1.3 %collective-permute-start.4 = (bf16[128,1536]{1,0:T(8,128)(2,1)S(1)}, bf16[128,1536]{1,0:T(8,128)(2,1)S(1)}, u32[]{:S(2)}, u32[]{:S(2)}) collective-permute-start(bf16[128,1536]{1,0:T(8,128)(2,1)S(1)} %get-tuple-element.76.refs_3_), channel_id=1, source_target_pairs={{0,2},{1,3},{2,0},{3,1},{4,6},{5,7},{6,4},{7,5},{8,10},{9,11},{10,... | collective-permute-start | bytes 1179656 | tf_op jit(solution)/shard_map/ppermute | solution.py:318
  24.7 2.2 %collective-permute-done.7.refs_6_ = bf16[128,1536]{1,0:T(8,128)(2,1)S(1)} collective-permute-done((bf16[128,1536]{1,0:T(8,128)(2,1)S(1)}, bf16[128,1536]{1,0:T(8,128)(2,1)S(1)}, u32[]{:S(2)}, u32[]{:S(2)}) %collective-permute-start.7) | collective-permute-done | bytes 393248 | tf_op jit(solution)/shard_map/ppermute | solution.py:318
  26.9 0.0 collective-permute-done.5.refs_4_
  26.9 0.0 collective-permute-done.6.refs_5_
  26.9 2.7 %shard_map.157 = (f32[128,1536]{1,0:T(8,128)S(1)}, f32[128,1536]{1,0:T(8,128)S(1)}, f32[1,128]{1,0:T(1,128)S(1)}) custom-call(s32[1]{0:T(128)} %bitcast.1.region_ref.refs_0_, s32[4]{0:T(128)S(1)} %copy-done.6, bf16[128,1536]{1,0:T(8,128)(2,1)S(1)} %get-tuple-element.73.refs_2_, bf16[128,1536]{1,0:T(8,128)(2,1)S(1)} %get-tuple-element.76.refs_3_, ...), custom_call_target="tpu_custom_call" | custom-call | flops 4194304 | bytes 2097152 | tf_op jit(solution)/shard_map/pallas_call | solution.py:376
  29.6 5.4 %collective-permute-done.4.refs_4_ = bf16[128,1536]{1,0:T(8,128)(2,1)S(1)} collective-permute-done((bf16[128,1536]{1,0:T(8,128)(2,1)S(1)}, bf16[128,1536]{1,0:T(8,128)(2,1)S(1)}, u32[]{:S(2)}, u32[]{:S(2)}) %collective-permute-start.4) | collective-permute-done | bytes 393248 | tf_op jit(solution)/shard_map/ppermute | solution.py:318
  35.0 0.0 collective-permute-start.8
  35.0 0.5 collective-permute-start.9
  35.5 1.2 %collective-permute-done.8.refs_5_ = bf16[128,1536]{1,0:T(8,128)(2,1)S(1)} collective-permute-done((bf16[128,1536]{1,0:T(8,128)(2,1)S(1)}, bf16[128,1536]{1,0:T(8,128)(2,1)S(1)}, u32[]{:S(2)}, u32[]{:S(2)}) %collective-permute-start.8) | collective-permute-done | bytes 393248 | tf_op jit(solution)/shard_map/ppermute | solution.py:318
  36.7 0.6 collective-permute-done.9.refs_6_
  37.3 2.1 %shard_map.158 = (bf16[128,1536]{1,0:T(8,128)(2,1)S(1)}, bf16[128,1536]{1,0:T(8,128)(2,1)S(1)}, f32[1,128]{1,0:T(1,128)S(1)}) custom-call(s32[1]{0:T(128)} %bitcast.1.region_ref.refs_0_, s32[4]{0:T(128)S(1)} %copy-done.6, bf16[128,1536]{1,0:T(8,128)(2,1)S(1)} %get-tuple-element.73.refs_2_, bf16[128,1536]{1,0:T(8,128)(2,1)S(1)} %get-tuple-element.76.refs_3_, ...), custom_call_target="tpu_custom_call" | custom-call | flops 4194304 | bytes 2097152 | tf_op jit(solution)/shard_map/pallas_call | solution.py:376
  39.4 2.8 %shard_map.159 = (bf16[256,1536]{1,0:T(8,128)(2,1)S(1)}, bf16[256,1536]{1,0:T(8,128)(2,1)S(1)}, bf16[176,256]{1,0:T(8,128)(2,1)S(1)}, bf16[176,256]{1,0:T(8,128)...) custom-call(s32[1]{0:T(128)} %bitcast.1.region_ref.refs_0_, s32[1]{0:T(128)} %bitcast.rank_ref.refs_1_.refs_0_, ...), custom_call_target="tpu_custom_call" | custom-call | flops 2013265920 | bytes 10485760 | tf_op jit(solution)/shard_map/pallas_call | solution.py:395
  42.2 0.2 collective-permute-start.10
  42.4 0.4 collective-permute-start.11
  42.8 1.4 %shard_map.160 = (bf16[256,1536]{1,0:T(8,128)(2,1)S(1)}, bf16[256,1536]{1,0:T(8,128)(2,1)S(1)}, bf16[2,256,256]{2,1,0:T(8,128)(2,1)S(1)}, bf16[2,256,256]{2,1,0:T(8,128)(2,1)S(1)}) custom-call(s32[1]{0:T(128)} %bitcast.1.region_ref.refs_0_, bf16[1536,1536]{1,0:T(8,128)(2,1)S(1)} %get-tuple-element.70.refs_2_.refs_1_.table_ref, ...), custom_call_target="tpu_custom_call" | custom-call | flops 1207959552 | bytes 6291456 | tf_op jit(solution)/shard_map/pallas_call | solution.py:411
  44.2 0.0 collective-permute-done.10.refs_2_
  44.2 0.0 collective-permute-done.11.refs_3_
  44.3 1.6 %collective-permute-start.12 = (bf16[176,256]{1,0:T(8,128)(2,1)S(1)}, bf16[176,256]{1,0:T(8,128)(2,1)S(1)}, u32[]{:S(2)}, u32[]{:S(2)}) collective-permute-start(bf16[176,256]{1,0:T(8,128)(2,1)S(1)} %get-tuple-element.108), channel_id=1, source_target_pairs={{0,2},{1,3},{2,0},{3,1},{4,6},{5,7},{6,4},{7,5},{8,10},{9,11},{10,... | collective-permute-start | bytes 270344 | tf_op jit(solution)/shard_map/ppermute | solution.py:318
  45.8 1.7 %collective-permute-start.15 = (bf16[2,256,256]{2,1,0:T(8,128)(2,1)S(1)}, bf16[2,256,256]{2,1,0:T(8,128)(2,1)S(1)}, u32[]{:S(2)}, u32[]{:S(2)}) collective-permute-start(bf16[2,256,256]{2,1,0:T(8,128)(2,1)S(1)} %get-tuple-element.112), channel_id=1, source_target_pairs={{0,12},{4,8},{8,4},{12,0},{1,13},{5,9},{9,5},{13,1},{2,14},{6,10},... | collective-permute-start | bytes 786440 | tf_op jit(solution)/shard_map/ppermute | solution.py:314
  47.5 1.5 %collective-permute-done.12.refs_1_ = bf16[176,256]{1,0:T(8,128)(2,1)S(1)} collective-permute-done((bf16[176,256]{1,0:T(8,128)(2,1)S(1)}, bf16[176,256]{1,0:T(8,128)(2,1)S(1)}, u32[]{:S(2)}, u32[]{:S(2)}) %collective-permute-start.12) | collective-permute-done | bytes 90144 | tf_op jit(solution)/shard_map/ppermute | solution.py:318
  49.0 0.8 %collective-permute-start.13 = (bf16[176,256]{1,0:T(8,128)(2,1)S(1)}, bf16[176,256]{1,0:T(8,128)(2,1)S(1)}, u32[]{:S(2)}, u32[]{:S(2)}) collective-permute-start(bf16[176,256]{1,0:T(8,128)(2,1)S(1)} %shard_map.162.refs_0_), channel_id=1, source_target_pairs={{0,4},{4,0},{8,12},{12,8},{1,5},{5,1},{9,13},{13,9},{2,6},{6,2},{1... | collective-permute-start | bytes 270344 | tf_op jit(solution)/shard_map/ppermute | solution.py:318
  49.8 1.8 %shard_map.164.own_ref = f32[2,1024,256]{2,1,0:T(8,128)S(1)} custom-call(bf16[1536,1536]{1,0:T(8,128)(2,1)S(1)} %get-tuple-element.70.refs_2_.refs_1_.table_ref, bf16[256,1536]{1,0:T(8,128)(2,1)S(1)} %get-tuple-element.109.refs_0_, bf16[256,1536]{1,0:T(8,128)(2,1)S(1)} %get-tuple-element.110.refs_1_), custom_call_target="tpu_custom_call" | custom-call | flops 1610612736 | bytes 6291456 | tf_op jit(solution)/shard_map/pallas_call | solution.py:428
  51.6 6.1 %collective-permute-done.13.refs_1_ = bf16[176,256]{1,0:T(8,128)(2,1)S(1)} collective-permute-done((bf16[176,256]{1,0:T(8,128)(2,1)S(1)}, bf16[176,256]{1,0:T(8,128)(2,1)S(1)}, u32[]{:S(2)}, u32[]{:S(2)}) %collective-permute-start.13) | collective-permute-done | bytes 90144 | tf_op jit(solution)/shard_map/ppermute | solution.py:318
  57.8 0.6 collective-permute-start.14
  58.4 1.7 %collective-permute-start.19 = (bf16[2,256,256]{2,1,0:T(8,128)(2,1)S(1)}, bf16[2,256,256]{2,1,0:T(8,128)(2,1)S(1)}, u32[]{:S(2)}, u32[]{:S(2)}) collective-permute-start(bf16[2,256,256]{2,1,0:T(8,128)(2,1)S(1)} %get-tuple-element.116), channel_id=1, source_target_pairs={{0,4},{4,0},{8,12},{12,8},{1,5},{5,1},{9,13},{13,9},{2,6},{6,2},{1... | collective-permute-start | bytes 786440 | tf_op jit(solution)/shard_map/ppermute | solution.py:314
  60.1 0.0 collective-permute-done.15.other_ref
  60.1 4.2 %collective-permute-done.14.refs_1_ = bf16[176,256]{1,0:T(8,128)(2,1)S(1)} collective-permute-done((bf16[176,256]{1,0:T(8,128)(2,1)S(1)}, bf16[176,256]{1,0:T(8,128)(2,1)S(1)}, u32[]{:S(2)}, u32[]{:S(2)}) %collective-permute-start.14) | collective-permute-done | bytes 90144 | tf_op jit(solution)/shard_map/ppermute | solution.py:318
  64.3 0.8 %collective-permute-start.17 = (bf16[176,256]{1,0:T(8,128)(2,1)S(1)}, bf16[176,256]{1,0:T(8,128)(2,1)S(1)}, u32[]{:S(2)}, u32[]{:S(2)}) collective-permute-start(bf16[176,256]{1,0:T(8,128)(2,1)S(1)} %shard_map.165.refs_1_), channel_id=1, source_target_pairs={{0,2},{1,3},{2,0},{3,1},{4,6},{5,7},{6,4},{7,5},{8,10},{9,11},{10,... | collective-permute-start | bytes 270344 | tf_op jit(solution)/shard_map/ppermute | solution.py:318
  65.1 0.0 collective-permute-start.16
  65.1 3.8 %collective-permute-done.17.refs_3_ = bf16[176,256]{1,0:T(8,128)(2,1)S(1)} collective-permute-done((bf16[176,256]{1,0:T(8,128)(2,1)S(1)}, bf16[176,256]{1,0:T(8,128)(2,1)S(1)}, u32[]{:S(2)}, u32[]{:S(2)}) %collective-permute-start.17) | collective-permute-done | bytes 90144 | tf_op jit(solution)/shard_map/ppermute | solution.py:318
  68.9 0.0 collective-permute-start.18
  68.9 0.0 collective-permute-done.19.one_ref
  68.9 1.1 %shard_map.166 = bf16[2,1024,256]{2,1,0:T(8,128)(2,1)} custom-call(s32[1]{0:T(128)} %bitcast.1.region_ref.refs_0_, f32[2,1024,256]{2,1,0:T(8,128)S(1)} %shard_map.164.own_ref, bf16[2,256,256]{2,1,0:T(8,128)(2,1)S(1)} %collective-permute-done.19.one_ref, bf16[2,256,256]{2,1,0:T(8,128)(2,1)S(1)} %collective-permute-done.15.other_ref), custom_call_target="tpu_custom_call" | custom-call | flops 1048576 | bytes 3145728 | tf_op jit(solution)/shard_map/pallas_call | solution.py:453
  70.1 0.0 collective-permute-done.16.refs_2_
  70.1 0.1 collective-permute-done.18.refs_4_
  70.2 0.9 %shard_map.167 = (f32[256,256]{1,0:T(8,128)}, f32[1,256]{1,0:T(1,128)}, f32[256,256]{1,0:T(8,128)}, f32[1,256]{1,0:T(1,128)}, f32[256,128]{1,0:T(8,128)}, /*index=5*/f32[1,4]{1,0:T(1,128)}) custom-call(s32[1]{0:T(128)} %bitcast.rank_ref.refs_1_.refs_0_, bf16[176,256]{1,0:T(8,128)(2,1)S(1)} %shard_map.165.refs_1_, ...), custom_call_target="tpu_custom_call" | custom-call | flops 1048576 | bytes 2097152 | tf_op jit(solution)/shard_map/pallas_call | solution.py:464
  (11 shorter events, 0.1 us)
Async XLA Ops:
  0.6 1.2 %copy-start.7 = (bf16[2,1024,256]{2,1,0:T(8,128)(2,1)S(1)}, bf16[2,1024,256]{2,1,0:T(8,128)(2,1)}, u32[]{:S(2)}) copy-start(bf16[2,1024,256]{2,1,0:T(8,128)(2,1)} %latent_ref.1) | copy-start | bytes 3145732
  1.9 5.7 %copy-start.6 = (s32[4]{0:T(128)S(1)}, s32[4]{0:T(128)}, u32[]{:S(2)}) copy-start(s32[4]{0:T(128)} %refs_1_.3) | copy-start | bytes 52
  1.9 5.7 %copy-start.8 = (s32[4,1536]{1,0:T(4,128)S(1)}, s32[4,1536]{1,0:T(4,128)}, u32[]{:S(2)}) copy-start(s32[4,1536]{1,0:T(4,128)} %nbr_ref.1) | copy-start | bytes 73732
  1.9 5.7 %copy-start.9 = (f32[4,1536]{1,0:T(4,128)S(1)}, f32[4,1536]{1,0:T(4,128)}, u32[]{:S(2)}) copy-start(f32[4,1536]{1,0:T(4,128)} %weight_ref.1) | copy-start | bytes 73732
  2.0 12.7 %copy-start = (bf16[256,256]{1,0:T(8,128)(2,1)S(1)}, bf16[256,256]{1,0:T(8,128)(2,1)}, u32[]{:S(2)}) copy-start(bf16[256,256]{1,0:T(8,128)(2,1)} %refs_2_.2) | copy-start | bytes 393220
  2.0 12.7 %copy-start.1 = (bf16[256,256]{1,0:T(8,128)(2,1)S(1)}, bf16[256,256]{1,0:T(8,128)(2,1)}, u32[]{:S(2)}) copy-start(bf16[256,256]{1,0:T(8,128)(2,1)} %refs_2_.3) | copy-start | bytes 393220
  2.0 12.7 %copy-start.2 = (bf16[256,128]{1,0:T(8,128)(2,1)S(1)}, bf16[256,128]{1,0:T(8,128)(2,1)}, u32[]{:S(2)}) copy-start(bf16[256,128]{1,0:T(8,128)(2,1)} %refs_3_.1) | copy-start | bytes 196612
  2.0 12.6 %copy-start.4 = (f32[256]{0:T(256)S(1)}, f32[256]{0:T(256)}, u32[]{:S(2)}) copy-start(f32[256]{0:T(256)} %param.16) | copy-start | bytes 3076
  2.0 12.6 %copy-start.5 = (f32[256]{0:T(256)S(1)}, f32[256]{0:T(256)}, u32[]{:S(2)}) copy-start(f32[256]{0:T(256)} %param.18) | copy-start | bytes 3076
  2.0 10.4 %collective-permute-start = (bf16[256,256]{1,0:T(8,128)(2,1)S(1)}, bf16[256,256]{1,0:T(8,128)(2,1)S(1)}, u32[]{:S(2)}, u32[]{:S(2)}) collective-permute-start(bf16[256,256]{1,0:T(8,128)(2,1)S(1)} %get-tuple-element.71), channel_id=1, source_target_pairs={{0,4},{4,0},{8,12},{12,8},{1,5},{5,1},{9,13},{13,9},{2,6},{6,2},{1... | collective-permute-start | bytes 393224 | tf_op jit(solution)/shard_map/ppermute | solution.py:314
  5.1 9.5 %collective-permute-start.1 = (bf16[256,256]{1,0:T(8,128)(2,1)S(1)}, bf16[256,256]{1,0:T(8,128)(2,1)S(1)}, u32[]{:S(2)}, u32[]{:S(2)}) collective-permute-start(bf16[256,256]{1,0:T(8,128)(2,1)S(1)} %get-tuple-element.72), channel_id=1, source_target_pairs={{0,12},{4,8},{8,4},{12,0},{1,13},{5,9},{9,5},{13,1},{2,14},{6,10},... | collective-permute-start | bytes 393224 | tf_op jit(solution)/shard_map/ppermute | solution.py:314
  10.7 8.4 %collective-permute-start.2 = (bf16[256,256]{1,0:T(8,128)(2,1)S(1)}, bf16[256,256]{1,0:T(8,128)(2,1)S(1)}, u32[]{:S(2)}, u32[]{:S(2)}) collective-permute-start(bf16[256,256]{1,0:T(8,128)(2,1)S(1)} %get-tuple-element.74), channel_id=1, source_target_pairs={{0,4},{4,0},{8,12},{12,8},{1,5},{5,1},{9,13},{13,9},{2,6},{6,2},{1... | collective-permute-start | bytes 393224 | tf_op jit(solution)/shard_map/ppermute | solution.py:314
  11.5 7.8 %collective-permute-start.3 = (bf16[256,256]{1,0:T(8,128)(2,1)S(1)}, bf16[256,256]{1,0:T(8,128)(2,1)S(1)}, u32[]{:S(2)}, u32[]{:S(2)}) collective-permute-start(bf16[256,256]{1,0:T(8,128)(2,1)S(1)} %get-tuple-element.75), channel_id=1, source_target_pairs={{0,12},{4,8},{8,4},{12,0},{1,13},{5,9},{9,5},{13,1},{2,14},{6,10},... | collective-permute-start | bytes 393224 | tf_op jit(solution)/shard_map/ppermute | solution.py:314
  17.5 9.4 %copy-start.3 = (bf16[1536,128]{1,0:T(8,128)(2,1)S(1)}, bf16[1536,128]{1,0:T(8,128)(2,1)}, u32[]{:S(2)}) copy-start(bf16[1536,128]{1,0:T(8,128)(2,1)} %refs_7_.5) | copy-start | bytes 1179652
  17.6 9.3 %collective-permute-start.7 = (bf16[128,1536]{1,0:T(8,128)(2,1)S(1)}, bf16[128,1536]{1,0:T(8,128)(2,1)S(1)}, u32[]{:S(2)}, u32[]{:S(2)}) collective-permute-start(bf16[128,1536]{1,0:T(8,128)(2,1)S(1)} %get-tuple-element.73.refs_2_), channel_id=1, source_target_pairs={{0,2},{1,3},{2,0},{3,1},{4,6},{5,7},{6,4},{7,5},{8,10},{9,11},{10,... | collective-permute-start | bytes 1179656 | tf_op jit(solution)/shard_map/ppermute | solution.py:318
  19.1 7.8 %collective-permute-start.5 = (bf16[128,1536]{1,0:T(8,128)(2,1)S(1)}, bf16[128,1536]{1,0:T(8,128)(2,1)S(1)}, u32[]{:S(2)}, u32[]{:S(2)}) collective-permute-start(bf16[128,1536]{1,0:T(8,128)(2,1)S(1)} %get-tuple-element.73.refs_2_), channel_id=1, source_target_pairs={{0,1},{1,0},{2,3},{3,2},{4,5},{5,4},{6,7},{7,6},{8,9},{9,8},{10,11... | collective-permute-start | bytes 1179656 | tf_op jit(solution)/shard_map/ppermute | solution.py:318
  23.0 3.9 %collective-permute-start.6 = (bf16[128,1536]{1,0:T(8,128)(2,1)S(1)}, bf16[128,1536]{1,0:T(8,128)(2,1)S(1)}, u32[]{:S(2)}, u32[]{:S(2)}) collective-permute-start(bf16[128,1536]{1,0:T(8,128)(2,1)S(1)} %get-tuple-element.76.refs_3_), channel_id=1, source_target_pairs={{0,1},{1,0},{2,3},{3,2},{4,5},{5,4},{6,7},{7,6},{8,9},{9,8},{10,11... | collective-permute-start | bytes 1179656 | tf_op jit(solution)/shard_map/ppermute | solution.py:318
  23.4 11.6 %collective-permute-start.4 = (bf16[128,1536]{1,0:T(8,128)(2,1)S(1)}, bf16[128,1536]{1,0:T(8,128)(2,1)S(1)}, u32[]{:S(2)}, u32[]{:S(2)}) collective-permute-start(bf16[128,1536]{1,0:T(8,128)(2,1)S(1)} %get-tuple-element.76.refs_3_), channel_id=1, source_target_pairs={{0,2},{1,3},{2,0},{3,1},{4,6},{5,7},{6,4},{7,5},{8,10},{9,11},{10,... | collective-permute-start | bytes 1179656 | tf_op jit(solution)/shard_map/ppermute | solution.py:318
  35.0 1.7 %collective-permute-start.8 = (bf16[128,1536]{1,0:T(8,128)(2,1)S(1)}, bf16[128,1536]{1,0:T(8,128)(2,1)S(1)}, u32[]{:S(2)}, u32[]{:S(2)}) collective-permute-start(bf16[128,1536]{1,0:T(8,128)(2,1)S(1)} %collective-permute-done.7.refs_6_), channel_id=1, source_target_pairs={{0,1},{1,0},{2,3},{3,2},{4,5},{5,4},{6,7},{7,6},{8,9},{9,8},{10,11... | collective-permute-start | bytes 1179656 | tf_op jit(solution)/shard_map/ppermute | solution.py:318
  35.0 2.3 %collective-permute-start.9 = (bf16[128,1536]{1,0:T(8,128)(2,1)S(1)}, bf16[128,1536]{1,0:T(8,128)(2,1)S(1)}, u32[]{:S(2)}, u32[]{:S(2)}) collective-permute-start(bf16[128,1536]{1,0:T(8,128)(2,1)S(1)} %collective-permute-done.4.refs_4_), channel_id=1, source_target_pairs={{0,1},{1,0},{2,3},{3,2},{4,5},{5,4},{6,7},{7,6},{8,9},{9,8},{10,11... | collective-permute-start | bytes 1179656 | tf_op jit(solution)/shard_map/ppermute | solution.py:318
  42.2 2.0 %collective-permute-start.10 = (bf16[176,256]{1,0:T(8,128)(2,1)S(1)}, bf16[176,256]{1,0:T(8,128)(2,1)S(1)}, u32[]{:S(2)}, u32[]{:S(2)}) collective-permute-start(bf16[176,256]{1,0:T(8,128)(2,1)S(1)} %get-tuple-element.99), channel_id=1, source_target_pairs={{0,1},{1,0},{2,3},{3,2},{4,5},{5,4},{6,7},{7,6},{8,9},{9,8},{10,11... | collective-permute-start | bytes 270344 | tf_op jit(solution)/shard_map/ppermute | solution.py:318
  42.4 1.8 %collective-permute-start.11 = (bf16[176,256]{1,0:T(8,128)(2,1)S(1)}, bf16[176,256]{1,0:T(8,128)(2,1)S(1)}, u32[]{:S(2)}, u32[]{:S(2)}) collective-permute-start(bf16[176,256]{1,0:T(8,128)(2,1)S(1)} %get-tuple-element.100), channel_id=1, source_target_pairs={{0,1},{1,0},{2,3},{3,2},{4,5},{5,4},{6,7},{7,6},{8,9},{9,8},{10,11... | collective-permute-start | bytes 270344 | tf_op jit(solution)/shard_map/ppermute | solution.py:318
  44.3 4.7 %collective-permute-start.12 = (bf16[176,256]{1,0:T(8,128)(2,1)S(1)}, bf16[176,256]{1,0:T(8,128)(2,1)S(1)}, u32[]{:S(2)}, u32[]{:S(2)}) collective-permute-start(bf16[176,256]{1,0:T(8,128)(2,1)S(1)} %get-tuple-element.108), channel_id=1, source_target_pairs={{0,2},{1,3},{2,0},{3,1},{4,6},{5,7},{6,4},{7,5},{8,10},{9,11},{10,... | collective-permute-start | bytes 270344 | tf_op jit(solution)/shard_map/ppermute | solution.py:318
  45.8 14.3 %collective-permute-start.15 = (bf16[2,256,256]{2,1,0:T(8,128)(2,1)S(1)}, bf16[2,256,256]{2,1,0:T(8,128)(2,1)S(1)}, u32[]{:S(2)}, u32[]{:S(2)}) collective-permute-start(bf16[2,256,256]{2,1,0:T(8,128)(2,1)S(1)} %get-tuple-element.112), channel_id=1, source_target_pairs={{0,12},{4,8},{8,4},{12,0},{1,13},{5,9},{9,5},{13,1},{2,14},{6,10},... | collective-permute-start | bytes 786440 | tf_op jit(solution)/shard_map/ppermute | solution.py:314
  49.0 8.7 %collective-permute-start.13 = (bf16[176,256]{1,0:T(8,128)(2,1)S(1)}, bf16[176,256]{1,0:T(8,128)(2,1)S(1)}, u32[]{:S(2)}, u32[]{:S(2)}) collective-permute-start(bf16[176,256]{1,0:T(8,128)(2,1)S(1)} %shard_map.162.refs_0_), channel_id=1, source_target_pairs={{0,4},{4,0},{8,12},{12,8},{1,5},{5,1},{9,13},{13,9},{2,6},{6,2},{1... | collective-permute-start | bytes 270344 | tf_op jit(solution)/shard_map/ppermute | solution.py:318
  57.8 6.5 %collective-permute-start.14 = (bf16[176,256]{1,0:T(8,128)(2,1)S(1)}, bf16[176,256]{1,0:T(8,128)(2,1)S(1)}, u32[]{:S(2)}, u32[]{:S(2)}) collective-permute-start(bf16[176,256]{1,0:T(8,128)(2,1)S(1)} %shard_map.163.refs_0_), channel_id=1, source_target_pairs={{0,8},{4,12},{8,0},{12,4},{1,9},{5,13},{9,1},{13,5},{2,10},{6,14},... | collective-permute-start | bytes 270344 | tf_op jit(solution)/shard_map/ppermute | solution.py:318
  58.4 10.6 %collective-permute-start.19 = (bf16[2,256,256]{2,1,0:T(8,128)(2,1)S(1)}, bf16[2,256,256]{2,1,0:T(8,128)(2,1)S(1)}, u32[]{:S(2)}, u32[]{:S(2)}) collective-permute-start(bf16[2,256,256]{2,1,0:T(8,128)(2,1)S(1)} %get-tuple-element.116), channel_id=1, source_target_pairs={{0,4},{4,0},{8,12},{12,8},{1,5},{5,1},{9,13},{13,9},{2,6},{6,2},{1... | collective-permute-start | bytes 786440 | tf_op jit(solution)/shard_map/ppermute | solution.py:314
  64.3 4.6 %collective-permute-start.17 = (bf16[176,256]{1,0:T(8,128)(2,1)S(1)}, bf16[176,256]{1,0:T(8,128)(2,1)S(1)}, u32[]{:S(2)}, u32[]{:S(2)}) collective-permute-start(bf16[176,256]{1,0:T(8,128)(2,1)S(1)} %shard_map.165.refs_1_), channel_id=1, source_target_pairs={{0,2},{1,3},{2,0},{3,1},{4,6},{5,7},{6,4},{7,5},{8,10},{9,11},{10,... | collective-permute-start | bytes 270344 | tf_op jit(solution)/shard_map/ppermute | solution.py:318
  65.1 4.9 %collective-permute-start.16 = (bf16[176,256]{1,0:T(8,128)(2,1)S(1)}, bf16[176,256]{1,0:T(8,128)(2,1)S(1)}, u32[]{:S(2)}, u32[]{:S(2)}) collective-permute-start(bf16[176,256]{1,0:T(8,128)(2,1)S(1)} %shard_map.165.refs_1_), channel_id=1, source_target_pairs={{0,1},{1,0},{2,3},{3,2},{4,5},{5,4},{6,7},{7,6},{8,9},{9,8},{10,11... | collective-permute-start | bytes 270344 | tf_op jit(solution)/shard_map/ppermute | solution.py:318
  68.9 1.3 %collective-permute-start.18 = (bf16[176,256]{1,0:T(8,128)(2,1)S(1)}, bf16[176,256]{1,0:T(8,128)(2,1)S(1)}, u32[]{:S(2)}, u32[]{:S(2)}) collective-permute-start(bf16[176,256]{1,0:T(8,128)(2,1)S(1)} %collective-permute-done.17.refs_3_), channel_id=1, source_target_pairs={{0,1},{1,0},{2,3},{3,2},{4,5},{5,4},{6,7},{7,6},{8,9},{9,8},{10,11... | collective-permute-start | bytes 270344 | tf_op jit(solution)/shard_map/ppermute | solution.py:318

commit v15 on v14

--- a/solution.py
+++ b/solution.py
@@ -11,7 +11,7 @@
 EPSILON = 1e-05
 BLOCK = 256
 LANE = 128
-CHUNK = 512
+CHUNK = 256
 MIB = 1 << 20
 
 

time: 71.2 us -> 73.7 us (1.035)
  Pallas kernels: 22.8 us -> 25.9 us
    pallas_call x2, Pallas kernels: 6.57 us -> 9.56 us  [per_device(): kernel_call(lambda *refs: forward_kernel(m, *refs), (mixed_shape,) + (sav...]
  transfers between devices with their start and end apart: 20 -> 20, of which waited for: 11 -> 11; matrix products, arithmetic and copies ran while one was open for 0% -> 0% of each run, Pallas kernels for 24% -> 27%
where the time goes in v15:
time: 73.7 us; the launch traced here: 73.5 us
  waiting for transfers between devices  27.3 us (37%)
  Pallas kernels  25.9 us (35%)
  starting transfers between devices  18.2 us (25%)
  local copies, waits for them, and re-layouts  1.27 us (2%)
  between operations  0.83 us (1%)
    ppermute x14, waiting for transfers between devices, swapped(): lax.ppermute(block, axis, [(i, i ^ by) for i in range(lax.axis_size(axis))])  25.1 us
    ppermute x6, starting transfers between devices, exchanged(): return lax.ppermute(block, 'space', pairs)  10.2 us
    pallas_call x2, Pallas kernels, per_device(): kernel_call(lambda *refs: forward_kernel(m, *refs), (mixed_shape,) + (sav...  9.56 us
    ppermute x14, starting transfers between devices, swapped(): lax.ppermute(block, axis, [(i, i ^ by) for i in range(lax.axis_size(axis))])  7.94 us
    pallas_call x2, Pallas kernels, scored(): kernel_call(lambda *refs: score_kernel(members, len(others), members * ra...  4.76 us
    pallas_call x1, Pallas kernels, per_device(): kernel_call(table_kernel, (shape((ext, slots), bf16), shape((width, slots...  3.13 us
    pallas_call x1, Pallas kernels, per_device(): kernel_call(lambda *refs: backward_kernel(members, ranks, *refs), (saved_...  3.04 us
    ppermute x6, waiting for transfers between devices, exchanged(): return lax.ppermute(block, 'space', pairs)  2.25 us
  transfers between devices with their start and end apart: 20, of which 11 were waited for; matrix products, arithmetic and copies ran while one was open for 0% of the time, Pallas kernels for 27%

profile of v15, /device:TPU:0, one launch (start us, length us, event | category | flops | bytes accessed | tf_op | source)
XLA Modules:
  0.0 73.5 jit_solution(16118641181295649177)
XLA Ops:
  0.6 0.0 copy-start.7
  0.6 1.2 %copy-done.7 = bf16[2,1024,256]{2,1,0:T(8,128)(2,1)S(1)} copy-done((bf16[2,1024,256]{2,1,0:T(8,128)(2,1)S(1)}, bf16[2,1024,256]{2,1,0:T(8,128)(2,1)}, u32[]{:S(2)}) %copy-start.7) | copy-done | bytes 1048600
  1.9 0.1 shard_map.153
  2.0 0.0 copy-start
  2.0 0.0 copy-start.1
  2.0 0.0 copy-start.2
  2.0 0.0 copy-start.4
  2.0 0.0 copy-start.5
  2.0 3.1 %collective-permute-start = (bf16[256,256]{1,0:T(8,128)(2,1)S(1)}, bf16[256,256]{1,0:T(8,128)(2,1)S(1)}, u32[]{:S(2)}, u32[]{:S(2)}) collective-permute-start(bf16[256,256]{1,0:T(8,128)(2,1)S(1)} %get-tuple-element.71), channel_id=1, source_target_pairs={{0,4},{4,0},{8,12},{12,8},{1,5},{5,1},{9,13},{13,9},{2,6},{6,2},{1... | collective-permute-start | bytes 393224 | tf_op jit(solution)/shard_map/ppermute | solution.py:314
  5.1 2.5 %collective-permute-start.1 = (bf16[256,256]{1,0:T(8,128)(2,1)S(1)}, bf16[256,256]{1,0:T(8,128)(2,1)S(1)}, u32[]{:S(2)}, u32[]{:S(2)}) collective-permute-start(bf16[256,256]{1,0:T(8,128)(2,1)S(1)} %get-tuple-element.72), channel_id=1, source_target_pairs={{0,12},{4,8},{8,4},{12,0},{1,13},{5,9},{9,5},{13,1},{2,14},{6,10},... | collective-permute-start | bytes 393224 | tf_op jit(solution)/shard_map/ppermute | solution.py:314
  7.6 0.0 copy-done.6
  7.6 0.0 copy-done.8
  7.6 0.0 copy-done.9
  7.6 3.1 %shard_map.154 = (bf16[1536,1536]{1,0:T(8,128)(2,1)S(1)}, f32[256,1536]{1,0:T(8,128)S(1)}, bf16[256,256]{1,0:T(8,128)(2,1)S(1)}, bf16[256,256]{1,0:T(8,128)(2,1)S(1)}) custom-call(s32[1]{0:T(128)} %bitcast.1.region_ref.refs_0_, s32[1]{0:T(128)} %bitcast.rank_ref.refs_1_.refs_0_, s32[4]{0:T(128)S(1)} %copy-done.6, s32[4,1536]{1,0:T(4,128)S(1)} %copy-done.8, ...), custom_call_target="tpu_custom_call" | custom-call | flops 805306368 | bytes 12582912 | tf_op jit(solution)/shard_map/pallas_call | solution.py:341
  10.7 0.7 %collective-permute-start.2 = (bf16[256,256]{1,0:T(8,128)(2,1)S(1)}, bf16[256,256]{1,0:T(8,128)(2,1)S(1)}, u32[]{:S(2)}, u32[]{:S(2)}) collective-permute-start(bf16[256,256]{1,0:T(8,128)(2,1)S(1)} %get-tuple-element.74), channel_id=1, source_target_pairs={{0,4},{4,0},{8,12},{12,8},{1,5},{5,1},{9,13},{13,9},{2,6},{6,2},{1... | collective-permute-start | bytes 393224 | tf_op jit(solution)/shard_map/ppermute | solution.py:314
  11.5 0.9 %collective-permute-start.3 = (bf16[256,256]{1,0:T(8,128)(2,1)S(1)}, bf16[256,256]{1,0:T(8,128)(2,1)S(1)}, u32[]{:S(2)}, u32[]{:S(2)}) collective-permute-start(bf16[256,256]{1,0:T(8,128)(2,1)S(1)} %get-tuple-element.75), channel_id=1, source_target_pairs={{0,12},{4,8},{8,4},{12,0},{1,13},{5,9},{9,5},{13,1},{2,14},{6,10},... | collective-permute-start | bytes 393224 | tf_op jit(solution)/shard_map/ppermute | solution.py:314
  12.4 0.0 collective-permute-done.refs_3_
  12.4 2.2 %collective-permute-done.1.refs_4_ = bf16[256,256]{1,0:T(8,128)(2,1)S(1)} collective-permute-done((bf16[256,256]{1,0:T(8,128)(2,1)S(1)}, bf16[256,256]{1,0:T(8,128)(2,1)S(1)}, u32[]{:S(2)}, u32[]{:S(2)}) %collective-permute-start.1) | collective-permute-done | bytes 131104 | tf_op jit(solution)/shard_map/ppermute | solution.py:314
  14.6 0.0 copy-done
  14.6 0.0 copy-done.1
  14.7 3.6 %shard_map.155 = (bf16[256,1536]{1,0:T(8,128)(2,1)S(1)}, bf16[256,1536]{1,0:T(8,128)(2,1)S(1)}, bf16[256,1536]{1,0:T(8,128)(2,1)S(1)}, bf16[256,1536]{1,0:T(8,12...) custom-call(s32[1]{0:T(128)} %bitcast.1.region_ref.refs_0_, ...), custom_call_target="tpu_custom_call" | custom-call | flops 905969664 | bytes 8388608 | tf_op jit(solution)/shard_map/pallas_call | solution.py:357
  18.2 0.0 copy-start.3
  18.2 1.6 %collective-permute-start.7 = (bf16[128,1536]{1,0:T(8,128)(2,1)S(1)}, bf16[128,1536]{1,0:T(8,128)(2,1)S(1)}, u32[]{:S(2)}, u32[]{:S(2)}) collective-permute-start(bf16[128,1536]{1,0:T(8,128)(2,1)S(1)} %get-tuple-element.73.refs_2_), channel_id=1, source_target_pairs={{0,2},{1,3},{2,0},{3,1},{4,6},{5,7},{6,4},{7,5},{8,10},{9,11},{10,... | collective-permute-start | bytes 1179656 | tf_op jit(solution)/shard_map/ppermute | solution.py:318
  19.8 0.0 collective-permute-start.5
  19.8 0.0 collective-permute-done.2.refs_3_
  19.8 0.0 collective-permute-done.3.refs_4_
  19.8 6.0 %shard_map.156 = (bf16[256,1536]{1,0:T(8,128)(2,1)S(1)}, bf16[256,1536]{1,0:T(8,128)(2,1)S(1)}, bf16[256,1536]{1,0:T(8,128)(2,1)S(1)}, bf16[256,1536]{1,0:T(8,12...) custom-call(s32[1]{0:T(128)} %bitcast.1.region_ref.refs_0_, ...), custom_call_target="tpu_custom_call" | custom-call | flops 1711276032 | bytes 8388608 | tf_op jit(solution)/shard_map/pallas_call | solution.py:357
  25.8 0.6 collective-permute-start.6
  26.4 0.6 collective-permute-start.4
  27.0 0.3 collective-permute-done.7.refs_6_
  27.3 0.0 collective-permute-done.5.refs_4_
  27.3 0.5 collective-permute-done.6.refs_5_
  27.7 2.7 %shard_map.157 = (f32[128,1536]{1,0:T(8,128)S(1)}, f32[128,1536]{1,0:T(8,128)S(1)}, f32[1,128]{1,0:T(1,128)S(1)}) custom-call(s32[1]{0:T(128)} %bitcast.1.region_ref.refs_0_, s32[4]{0:T(128)S(1)} %copy-done.6, bf16[128,1536]{1,0:T(8,128)(2,1)S(1)} %get-tuple-element.73.refs_2_, bf16[128,1536]{1,0:T(8,128)(2,1)S(1)} %get-tuple-element.76.refs_3_, ...), custom_call_target="tpu_custom_call" | custom-call | flops 4194304 | bytes 2097152 | tf_op jit(solution)/shard_map/pallas_call | solution.py:376
  30.4 7.0 %collective-permute-done.4.refs_4_ = bf16[128,1536]{1,0:T(8,128)(2,1)S(1)} collective-permute-done((bf16[128,1536]{1,0:T(8,128)(2,1)S(1)}, bf16[128,1536]{1,0:T(8,128)(2,1)S(1)}, u32[]{:S(2)}, u32[]{:S(2)}) %collective-permute-start.4) | collective-permute-done | bytes 393248 | tf_op jit(solution)/shard_map/ppermute | solution.py:318
  37.5 0.0 collective-permute-start.8
  37.5 0.5 collective-permute-start.9
  38.0 1.2 %collective-permute-done.8.refs_5_ = bf16[128,1536]{1,0:T(8,128)(2,1)S(1)} collective-permute-done((bf16[128,1536]{1,0:T(8,128)(2,1)S(1)}, bf16[128,1536]{1,0:T(8,128)(2,1)S(1)}, u32[]{:S(2)}, u32[]{:S(2)}) %collective-permute-start.8) | collective-permute-done | bytes 393248 | tf_op jit(solution)/shard_map/ppermute | solution.py:318
  39.2 0.6 collective-permute-done.9.refs_6_
  39.8 2.1 %shard_map.158 = (bf16[128,1536]{1,0:T(8,128)(2,1)S(1)}, bf16[128,1536]{1,0:T(8,128)(2,1)S(1)}, f32[1,128]{1,0:T(1,128)S(1)}) custom-call(s32[1]{0:T(128)} %bitcast.1.region_ref.refs_0_, s32[4]{0:T(128)S(1)} %copy-done.6, bf16[128,1536]{1,0:T(8,128)(2,1)S(1)} %get-tuple-element.73.refs_2_, bf16[128,1536]{1,0:T(8,128)(2,1)S(1)} %get-tuple-element.76.refs_3_, ...), custom_call_target="tpu_custom_call" | custom-call | flops 4194304 | bytes 2097152 | tf_op jit(solution)/shard_map/pallas_call | solution.py:376
  41.8 3.0 %shard_map.159 = (bf16[256,1536]{1,0:T(8,128)(2,1)S(1)}, bf16[256,1536]{1,0:T(8,128)(2,1)S(1)}, bf16[176,256]{1,0:T(8,128)(2,1)S(1)}, bf16[176,256]{1,0:T(8,128)...) custom-call(s32[1]{0:T(128)} %bitcast.1.region_ref.refs_0_, s32[1]{0:T(128)} %bitcast.rank_ref.refs_1_.refs_0_, ...), custom_call_target="tpu_custom_call" | custom-call | flops 2013265920 | bytes 10485760 | tf_op jit(solution)/shard_map/pallas_call | solution.py:395
  44.9 0.2 collective-permute-start.10
  45.1 0.4 collective-permute-start.11
  45.4 1.4 %shard_map.160 = (bf16[256,1536]{1,0:T(8,128)(2,1)S(1)}, bf16[256,1536]{1,0:T(8,128)(2,1)S(1)}, bf16[2,256,256]{2,1,0:T(8,128)(2,1)S(1)}, bf16[2,256,256]{2,1,0:T(8,128)(2,1)S(1)}) custom-call(s32[1]{0:T(128)} %bitcast.1.region_ref.refs_0_, bf16[1536,1536]{1,0:T(8,128)(2,1)S(1)} %get-tuple-element.70.refs_2_.refs_1_.table_ref, ...), custom_call_target="tpu_custom_call" | custom-call | flops 1207959552 | bytes 6291456 | tf_op jit(solution)/shard_map/pallas_call | solution.py:411
  46.9 0.0 collective-permute-done.10.refs_2_
  46.9 0.0 collective-permute-done.11.refs_3_
  46.9 1.0 %collective-permute-start.12 = (bf16[176,256]{1,0:T(8,128)(2,1)S(1)}, bf16[176,256]{1,0:T(8,128)(2,1)S(1)}, u32[]{:S(2)}, u32[]{:S(2)}) collective-permute-start(bf16[176,256]{1,0:T(8,128)(2,1)S(1)} %get-tuple-element.108), channel_id=1, source_target_pairs={{0,2},{1,3},{2,0},{3,1},{4,6},{5,7},{6,4},{7,5},{8,10},{9,11},{10,... | collective-permute-start | bytes 270344 | tf_op jit(solution)/shard_map/ppermute | solution.py:318
  47.9 1.5 %collective-permute-start.15 = (bf16[2,256,256]{2,1,0:T(8,128)(2,1)S(1)}, bf16[2,256,256]{2,1,0:T(8,128)(2,1)S(1)}, u32[]{:S(2)}, u32[]{:S(2)}) collective-permute-start(bf16[2,256,256]{2,1,0:T(8,128)(2,1)S(1)} %get-tuple-element.112), channel_id=1, source_target_pairs={{0,12},{4,8},{8,4},{12,0},{1,13},{5,9},{9,5},{13,1},{2,14},{6,10},... | collective-permute-start | bytes 786440 | tf_op jit(solution)/shard_map/ppermute | solution.py:314
  49.4 2.2 %collective-permute-done.12.refs_1_ = bf16[176,256]{1,0:T(8,128)(2,1)S(1)} collective-permute-done((bf16[176,256]{1,0:T(8,128)(2,1)S(1)}, bf16[176,256]{1,0:T(8,128)(2,1)S(1)}, u32[]{:S(2)}, u32[]{:S(2)}) %collective-permute-start.12) | collective-permute-done | bytes 90144 | tf_op jit(solution)/shard_map/ppermute | solution.py:318
  51.7 1.0 %collective-permute-start.13 = (bf16[176,256]{1,0:T(8,128)(2,1)S(1)}, bf16[176,256]{1,0:T(8,128)(2,1)S(1)}, u32[]{:S(2)}, u32[]{:S(2)}) collective-permute-start(bf16[176,256]{1,0:T(8,128)(2,1)S(1)} %shard_map.162.refs_0_), channel_id=1, source_target_pairs={{0,4},{4,0},{8,12},{12,8},{1,5},{5,1},{9,13},{13,9},{2,6},{6,2},{1... | collective-permute-start | bytes 270344 | tf_op jit(solution)/shard_map/ppermute | solution.py:318
  52.6 1.8 %shard_map.164.own_ref = f32[2,1024,256]{2,1,0:T(8,128)S(1)} custom-call(bf16[1536,1536]{1,0:T(8,128)(2,1)S(1)} %get-tuple-element.70.refs_2_.refs_1_.table_ref, bf16[256,1536]{1,0:T(8,128)(2,1)S(1)} %get-tuple-element.109.refs_0_, bf16[256,1536]{1,0:T(8,128)(2,1)S(1)} %get-tuple-element.110.refs_1_), custom_call_target="tpu_custom_call" | custom-call | flops 1610612736 | bytes 6291456 | tf_op jit(solution)/shard_map/pallas_call | solution.py:428
  54.4 5.4 %collective-permute-done.13.refs_1_ = bf16[176,256]{1,0:T(8,128)(2,1)S(1)} collective-permute-done((bf16[176,256]{1,0:T(8,128)(2,1)S(1)}, bf16[176,256]{1,0:T(8,128)(2,1)S(1)}, u32[]{:S(2)}, u32[]{:S(2)}) %collective-permute-start.13) | collective-permute-done | bytes 90144 | tf_op jit(solution)/shard_map/ppermute | solution.py:318
  59.9 0.6 collective-permute-start.14
  60.5 1.5 %collective-permute-start.19 = (bf16[2,256,256]{2,1,0:T(8,128)(2,1)S(1)}, bf16[2,256,256]{2,1,0:T(8,128)(2,1)S(1)}, u32[]{:S(2)}, u32[]{:S(2)}) collective-permute-start(bf16[2,256,256]{2,1,0:T(8,128)(2,1)S(1)} %get-tuple-element.116), channel_id=1, source_target_pairs={{0,4},{4,0},{8,12},{12,8},{1,5},{5,1},{9,13},{13,9},{2,6},{6,2},{1... | collective-permute-start | bytes 786440 | tf_op jit(solution)/shard_map/ppermute | solution.py:314
  62.0 0.0 collective-permute-done.15.other_ref
  62.0 4.7 %collective-permute-done.14.refs_1_ = bf16[176,256]{1,0:T(8,128)(2,1)S(1)} collective-permute-done((bf16[176,256]{1,0:T(8,128)(2,1)S(1)}, bf16[176,256]{1,0:T(8,128)(2,1)S(1)}, u32[]{:S(2)}, u32[]{:S(2)}) %collective-permute-start.14) | collective-permute-done | bytes 90144 | tf_op jit(solution)/shard_map/ppermute | solution.py:318
  66.8 1.6 %collective-permute-start.17 = (bf16[176,256]{1,0:T(8,128)(2,1)S(1)}, bf16[176,256]{1,0:T(8,128)(2,1)S(1)}, u32[]{:S(2)}, u32[]{:S(2)}) collective-permute-start(bf16[176,256]{1,0:T(8,128)(2,1)S(1)} %shard_map.165.refs_1_), channel_id=1, source_target_pairs={{0,2},{1,3},{2,0},{3,1},{4,6},{5,7},{6,4},{7,5},{8,10},{9,11},{10,... | collective-permute-start | bytes 270344 | tf_op jit(solution)/shard_map/ppermute | solution.py:318
  68.3 0.0 collective-permute-start.16
  68.3 3.0 %collective-permute-done.17.refs_3_ = bf16[176,256]{1,0:T(8,128)(2,1)S(1)} collective-permute-done((bf16[176,256]{1,0:T(8,128)(2,1)S(1)}, bf16[176,256]{1,0:T(8,128)(2,1)S(1)}, u32[]{:S(2)}, u32[]{:S(2)}) %collective-permute-start.17) | collective-permute-done | bytes 90144 | tf_op jit(solution)/shard_map/ppermute | solution.py:318
  71.4 0.0 collective-permute-start.18
  71.4 0.0 collective-permute-done.19.one_ref
  71.4 1.1 %shard_map.166 = bf16[2,1024,256]{2,1,0:T(8,128)(2,1)} custom-call(s32[1]{0:T(128)} %bitcast.1.region_ref.refs_0_, f32[2,1024,256]{2,1,0:T(8,128)S(1)} %shard_map.164.own_ref, bf16[2,256,256]{2,1,0:T(8,128)(2,1)S(1)} %collective-permute-done.19.one_ref, bf16[2,256,256]{2,1,0:T(8,128)(2,1)S(1)} %collective-permute-done.15.other_ref), custom_call_target="tpu_custom_call" | custom-call | flops 1048576 | bytes 3145728 | tf_op jit(solution)/shard_map/pallas_call | solution.py:453
  72.5 0.0 collective-permute-done.16.refs_2_
  72.5 0.1 collective-permute-done.18.refs_4_
  72.7 0.9 %shard_map.167 = (f32[256,256]{1,0:T(8,128)}, f32[1,256]{1,0:T(1,128)}, f32[256,256]{1,0:T(8,128)}, f32[1,256]{1,0:T(1,128)}, f32[256,128]{1,0:T(8,128)}, /*index=5*/f32[1,4]{1,0:T(1,128)}) custom-call(s32[1]{0:T(128)} %bitcast.rank_ref.refs_1_.refs_0_, bf16[176,256]{1,0:T(8,128)(2,1)S(1)} %shard_map.165.refs_1_, ...), custom_call_target="tpu_custom_call" | custom-call | flops 1048576 | bytes 2097152 | tf_op jit(solution)/shard_map/pallas_call | solution.py:464
  (11 shorter events, 0.1 us)
Async XLA Ops:
  0.6 1.2 %copy-start.7 = (bf16[2,1024,256]{2,1,0:T(8,128)(2,1)S(1)}, bf16[2,1024,256]{2,1,0:T(8,128)(2,1)}, u32[]{:S(2)}) copy-start(bf16[2,1024,256]{2,1,0:T(8,128)(2,1)} %latent_ref.1) | copy-start | bytes 3145732
  1.9 5.7 %copy-start.6 = (s32[4]{0:T(128)S(1)}, s32[4]{0:T(128)}, u32[]{:S(2)}) copy-start(s32[4]{0:T(128)} %refs_1_.3) | copy-start | bytes 52
  1.9 5.7 %copy-start.8 = (s32[4,1536]{1,0:T(4,128)S(1)}, s32[4,1536]{1,0:T(4,128)}, u32[]{:S(2)}) copy-start(s32[4,1536]{1,0:T(4,128)} %nbr_ref.1) | copy-start | bytes 73732
  1.9 5.7 %copy-start.9 = (f32[4,1536]{1,0:T(4,128)S(1)}, f32[4,1536]{1,0:T(4,128)}, u32[]{:S(2)}) copy-start(f32[4,1536]{1,0:T(4,128)} %weight_ref.1) | copy-start | bytes 73732
  2.0 12.7 %copy-start = (bf16[256,256]{1,0:T(8,128)(2,1)S(1)}, bf16[256,256]{1,0:T(8,128)(2,1)}, u32[]{:S(2)}) copy-start(bf16[256,256]{1,0:T(8,128)(2,1)} %refs_2_.2) | copy-start | bytes 393220
  2.0 12.7 %copy-start.1 = (bf16[256,256]{1,0:T(8,128)(2,1)S(1)}, bf16[256,256]{1,0:T(8,128)(2,1)}, u32[]{:S(2)}) copy-start(bf16[256,256]{1,0:T(8,128)(2,1)} %refs_2_.3) | copy-start | bytes 393220
  2.0 12.7 %copy-start.2 = (bf16[256,128]{1,0:T(8,128)(2,1)S(1)}, bf16[256,128]{1,0:T(8,128)(2,1)}, u32[]{:S(2)}) copy-start(bf16[256,128]{1,0:T(8,128)(2,1)} %refs_3_.1) | copy-start | bytes 196612
  2.0 12.6 %copy-start.4 = (f32[256]{0:T(256)S(1)}, f32[256]{0:T(256)}, u32[]{:S(2)}) copy-start(f32[256]{0:T(256)} %param.16) | copy-start | bytes 3076
  2.0 12.6 %copy-start.5 = (f32[256]{0:T(256)S(1)}, f32[256]{0:T(256)}, u32[]{:S(2)}) copy-start(f32[256]{0:T(256)} %param.18) | copy-start | bytes 3076
  2.0 10.4 %collective-permute-start = (bf16[256,256]{1,0:T(8,128)(2,1)S(1)}, bf16[256,256]{1,0:T(8,128)(2,1)S(1)}, u32[]{:S(2)}, u32[]{:S(2)}) collective-permute-start(bf16[256,256]{1,0:T(8,128)(2,1)S(1)} %get-tuple-element.71), channel_id=1, source_target_pairs={{0,4},{4,0},{8,12},{12,8},{1,5},{5,1},{9,13},{13,9},{2,6},{6,2},{1... | collective-permute-start | bytes 393224 | tf_op jit(solution)/shard_map/ppermute | solution.py:314
  5.1 9.5 %collective-permute-start.1 = (bf16[256,256]{1,0:T(8,128)(2,1)S(1)}, bf16[256,256]{1,0:T(8,128)(2,1)S(1)}, u32[]{:S(2)}, u32[]{:S(2)}) collective-permute-start(bf16[256,256]{1,0:T(8,128)(2,1)S(1)} %get-tuple-element.72), channel_id=1, source_target_pairs={{0,12},{4,8},{8,4},{12,0},{1,13},{5,9},{9,5},{13,1},{2,14},{6,10},... | collective-permute-start | bytes 393224 | tf_op jit(solution)/shard_map/ppermute | solution.py:314
  10.7 9.1 %collective-permute-start.2 = (bf16[256,256]{1,0:T(8,128)(2,1)S(1)}, bf16[256,256]{1,0:T(8,128)(2,1)S(1)}, u32[]{:S(2)}, u32[]{:S(2)}) collective-permute-start(bf16[256,256]{1,0:T(8,128)(2,1)S(1)} %get-tuple-element.74), channel_id=1, source_target_pairs={{0,4},{4,0},{8,12},{12,8},{1,5},{5,1},{9,13},{13,9},{2,6},{6,2},{1... | collective-permute-start | bytes 393224 | tf_op jit(solution)/shard_map/ppermute | solution.py:314
  11.5 8.3 %collective-permute-start.3 = (bf16[256,256]{1,0:T(8,128)(2,1)S(1)}, bf16[256,256]{1,0:T(8,128)(2,1)S(1)}, u32[]{:S(2)}, u32[]{:S(2)}) collective-permute-start(bf16[256,256]{1,0:T(8,128)(2,1)S(1)} %get-tuple-element.75), channel_id=1, source_target_pairs={{0,12},{4,8},{8,4},{12,0},{1,13},{5,9},{9,5},{13,1},{2,14},{6,10},... | collective-permute-start | bytes 393224 | tf_op jit(solution)/shard_map/ppermute | solution.py:314
  18.2 9.5 %copy-start.3 = (bf16[1536,128]{1,0:T(8,128)(2,1)S(1)}, bf16[1536,128]{1,0:T(8,128)(2,1)}, u32[]{:S(2)}) copy-start(bf16[1536,128]{1,0:T(8,128)(2,1)} %refs_7_.5) | copy-start | bytes 1179652
  18.2 9.0 %collective-permute-start.7 = (bf16[128,1536]{1,0:T(8,128)(2,1)S(1)}, bf16[128,1536]{1,0:T(8,128)(2,1)S(1)}, u32[]{:S(2)}, u32[]{:S(2)}) collective-permute-start(bf16[128,1536]{1,0:T(8,128)(2,1)S(1)} %get-tuple-element.73.refs_2_), channel_id=1, source_target_pairs={{0,2},{1,3},{2,0},{3,1},{4,6},{5,7},{6,4},{7,5},{8,10},{9,11},{10,... | collective-permute-start | bytes 1179656 | tf_op jit(solution)/shard_map/ppermute | solution.py:318
  19.8 7.5 %collective-permute-start.5 = (bf16[128,1536]{1,0:T(8,128)(2,1)S(1)}, bf16[128,1536]{1,0:T(8,128)(2,1)S(1)}, u32[]{:S(2)}, u32[]{:S(2)}) collective-permute-start(bf16[128,1536]{1,0:T(8,128)(2,1)S(1)} %get-tuple-element.73.refs_2_), channel_id=1, source_target_pairs={{0,1},{1,0},{2,3},{3,2},{4,5},{5,4},{6,7},{7,6},{8,9},{9,8},{10,11... | collective-permute-start | bytes 1179656 | tf_op jit(solution)/shard_map/ppermute | solution.py:318
  25.8 1.9 %collective-permute-start.6 = (bf16[128,1536]{1,0:T(8,128)(2,1)S(1)}, bf16[128,1536]{1,0:T(8,128)(2,1)S(1)}, u32[]{:S(2)}, u32[]{:S(2)}) collective-permute-start(bf16[128,1536]{1,0:T(8,128)(2,1)S(1)} %get-tuple-element.76.refs_3_), channel_id=1, source_target_pairs={{0,1},{1,0},{2,3},{3,2},{4,5},{5,4},{6,7},{7,6},{8,9},{9,8},{10,11... | collective-permute-start | bytes 1179656 | tf_op jit(solution)/shard_map/ppermute | solution.py:318
  26.4 11.1 %collective-permute-start.4 = (bf16[128,1536]{1,0:T(8,128)(2,1)S(1)}, bf16[128,1536]{1,0:T(8,128)(2,1)S(1)}, u32[]{:S(2)}, u32[]{:S(2)}) collective-permute-start(bf16[128,1536]{1,0:T(8,128)(2,1)S(1)} %get-tuple-element.76.refs_3_), channel_id=1, source_target_pairs={{0,2},{1,3},{2,0},{3,1},{4,6},{5,7},{6,4},{7,5},{8,10},{9,11},{10,... | collective-permute-start | bytes 1179656 | tf_op jit(solution)/shard_map/ppermute | solution.py:318
  37.5 1.7 %collective-permute-start.8 = (bf16[128,1536]{1,0:T(8,128)(2,1)S(1)}, bf16[128,1536]{1,0:T(8,128)(2,1)S(1)}, u32[]{:S(2)}, u32[]{:S(2)}) collective-permute-start(bf16[128,1536]{1,0:T(8,128)(2,1)S(1)} %collective-permute-done.7.refs_6_), channel_id=1, source_target_pairs={{0,1},{1,0},{2,3},{3,2},{4,5},{5,4},{6,7},{7,6},{8,9},{9,8},{10,11... | collective-permute-start | bytes 1179656 | tf_op jit(solution)/shard_map/ppermute | solution.py:318
  37.5 2.3 %collective-permute-start.9 = (bf16[128,1536]{1,0:T(8,128)(2,1)S(1)}, bf16[128,1536]{1,0:T(8,128)(2,1)S(1)}, u32[]{:S(2)}, u32[]{:S(2)}) collective-permute-start(bf16[128,1536]{1,0:T(8,128)(2,1)S(1)} %collective-permute-done.4.refs_4_), channel_id=1, source_target_pairs={{0,1},{1,0},{2,3},{3,2},{4,5},{5,4},{6,7},{7,6},{8,9},{9,8},{10,11... | collective-permute-start | bytes 1179656 | tf_op jit(solution)/shard_map/ppermute | solution.py:318
  44.9 2.0 %collective-permute-start.10 = (bf16[176,256]{1,0:T(8,128)(2,1)S(1)}, bf16[176,256]{1,0:T(8,128)(2,1)S(1)}, u32[]{:S(2)}, u32[]{:S(2)}) collective-permute-start(bf16[176,256]{1,0:T(8,128)(2,1)S(1)} %get-tuple-element.99), channel_id=1, source_target_pairs={{0,1},{1,0},{2,3},{3,2},{4,5},{5,4},{6,7},{7,6},{8,9},{9,8},{10,11... | collective-permute-start | bytes 270344 | tf_op jit(solution)/shard_map/ppermute | solution.py:318
  45.1 1.8 %collective-permute-start.11 = (bf16[176,256]{1,0:T(8,128)(2,1)S(1)}, bf16[176,256]{1,0:T(8,128)(2,1)S(1)}, u32[]{:S(2)}, u32[]{:S(2)}) collective-permute-start(bf16[176,256]{1,0:T(8,128)(2,1)S(1)} %get-tuple-element.100), channel_id=1, source_target_pairs={{0,1},{1,0},{2,3},{3,2},{4,5},{5,4},{6,7},{7,6},{8,9},{9,8},{10,11... | collective-permute-start | bytes 270344 | tf_op jit(solution)/shard_map/ppermute | solution.py:318
  46.9 4.7 %collective-permute-start.12 = (bf16[176,256]{1,0:T(8,128)(2,1)S(1)}, bf16[176,256]{1,0:T(8,128)(2,1)S(1)}, u32[]{:S(2)}, u32[]{:S(2)}) collective-permute-start(bf16[176,256]{1,0:T(8,128)(2,1)S(1)} %get-tuple-element.108), channel_id=1, source_target_pairs={{0,2},{1,3},{2,0},{3,1},{4,6},{5,7},{6,4},{7,5},{8,10},{9,11},{10,... | collective-permute-start | bytes 270344 | tf_op jit(solution)/shard_map/ppermute | solution.py:318
  47.9 14.1 %collective-permute-start.15 = (bf16[2,256,256]{2,1,0:T(8,128)(2,1)S(1)}, bf16[2,256,256]{2,1,0:T(8,128)(2,1)S(1)}, u32[]{:S(2)}, u32[]{:S(2)}) collective-permute-start(bf16[2,256,256]{2,1,0:T(8,128)(2,1)S(1)} %get-tuple-element.112), channel_id=1, source_target_pairs={{0,12},{4,8},{8,4},{12,0},{1,13},{5,9},{9,5},{13,1},{2,14},{6,10},... | collective-permute-start | bytes 786440 | tf_op jit(solution)/shard_map/ppermute | solution.py:314
  51.7 8.2 %collective-permute-start.13 = (bf16[176,256]{1,0:T(8,128)(2,1)S(1)}, bf16[176,256]{1,0:T(8,128)(2,1)S(1)}, u32[]{:S(2)}, u32[]{:S(2)}) collective-permute-start(bf16[176,256]{1,0:T(8,128)(2,1)S(1)} %shard_map.162.refs_0_), channel_id=1, source_target_pairs={{0,4},{4,0},{8,12},{12,8},{1,5},{5,1},{9,13},{13,9},{2,6},{6,2},{1... | collective-permute-start | bytes 270344 | tf_op jit(solution)/shard_map/ppermute | solution.py:318
  59.9 6.9 %collective-permute-start.14 = (bf16[176,256]{1,0:T(8,128)(2,1)S(1)}, bf16[176,256]{1,0:T(8,128)(2,1)S(1)}, u32[]{:S(2)}, u32[]{:S(2)}) collective-permute-start(bf16[176,256]{1,0:T(8,128)(2,1)S(1)} %shard_map.163.refs_0_), channel_id=1, source_target_pairs={{0,8},{4,12},{8,0},{12,4},{1,9},{5,13},{9,1},{13,5},{2,10},{6,14},... | collective-permute-start | bytes 270344 | tf_op jit(solution)/shard_map/ppermute | solution.py:318
  60.5 10.9 %collective-permute-start.19 = (bf16[2,256,256]{2,1,0:T(8,128)(2,1)S(1)}, bf16[2,256,256]{2,1,0:T(8,128)(2,1)S(1)}, u32[]{:S(2)}, u32[]{:S(2)}) collective-permute-start(bf16[2,256,256]{2,1,0:T(8,128)(2,1)S(1)} %get-tuple-element.116), channel_id=1, source_target_pairs={{0,4},{4,0},{8,12},{12,8},{1,5},{5,1},{9,13},{13,9},{2,6},{6,2},{1... | collective-permute-start | bytes 786440 | tf_op jit(solution)/shard_map/ppermute | solution.py:314
  66.8 4.6 %collective-permute-start.17 = (bf16[176,256]{1,0:T(8,128)(2,1)S(1)}, bf16[176,256]{1,0:T(8,128)(2,1)S(1)}, u32[]{:S(2)}, u32[]{:S(2)}) collective-permute-start(bf16[176,256]{1,0:T(8,128)(2,1)S(1)} %shard_map.165.refs_1_), channel_id=1, source_target_pairs={{0,2},{1,3},{2,0},{3,1},{4,6},{5,7},{6,4},{7,5},{8,10},{9,11},{10,... | collective-permute-start | bytes 270344 | tf_op jit(solution)/shard_map/ppermute | solution.py:318
  68.3 4.2 %collective-permute-start.16 = (bf16[176,256]{1,0:T(8,128)(2,1)S(1)}, bf16[176,256]{1,0:T(8,128)(2,1)S(1)}, u32[]{:S(2)}, u32[]{:S(2)}) collective-permute-start(bf16[176,256]{1,0:T(8,128)(2,1)S(1)} %shard_map.165.refs_1_), channel_id=1, source_target_pairs={{0,1},{1,0},{2,3},{3,2},{4,5},{5,4},{6,7},{7,6},{8,9},{9,8},{10,11... | collective-permute-start | bytes 270344 | tf_op jit(solution)/shard_map/ppermute | solution.py:318
  71.4 1.3 %collective-permute-start.18 = (bf16[176,256]{1,0:T(8,128)(2,1)S(1)}, bf16[176,256]{1,0:T(8,128)(2,1)S(1)}, u32[]{:S(2)}, u32[]{:S(2)}) collective-permute-start(bf16[176,256]{1,0:T(8,128)(2,1)S(1)} %collective-permute-done.17.refs_3_), channel_id=1, source_target_pairs={{0,1},{1,0},{2,3},{3,2},{4,5},{5,4},{6,7},{7,6},{8,9},{9,8},{10,11... | collective-permute-start | bytes 270344 | tf_op jit(solution)/shard_map/ppermute | solution.py:318

commit v16 on v15

--- a/solution.py
+++ b/solution.py
@@ -11,7 +11,7 @@
 EPSILON = 1e-05
 BLOCK = 256
 LANE = 128
-CHUNK = 256
+CHUNK = 768
 MIB = 1 << 20
 
 
@@ -257,7 +257,7 @@
 
 
 def edges_kernel(members, region_ref, table_ref, w_one_ref, *refs):
-    d_one_refs, d_mixed_refs, (one_ref, other_ref) = refs[:members], refs[members : 2 * members], refs[2 * members :]
+    d_one_refs, d_mixed_refs, (one_ref, *other_refs) = refs[:members], refs[members : 2 * members], refs[2 * members :]
     ext = table_ref.shape[0]
     rows = jnp.concatenate([table_ref[rows, :] for rows in rim_starts(region_ref, ext)], axis=0)
     for m in range(members):
@@ -265,7 +265,7 @@
         d_mixed_refs[m][...] = d_mixed
         grads = nt_dot(rows, d_mixed).astype(jnp.bfloat16)
         one_ref[m] = grads[:HALO]
-        other_ref[m] = grads[HALO:]
+        other_refs[m][...] = grads[HALO:]
 
 
 def sum_kernel(count, *refs):
@@ -301,11 +301,15 @@
         own_ref[m] = nt_dot(table_ref[HALO : HALO + nodes, :], d_mixed_refs[m][...])
 
 
-def finish_kernel(region_ref, own_ref, one_ref, other_ref, out_ref):
-    nodes = own_ref.shape[1]
+def finish_kernel(region_ref, own_ref, one_ref, *refs):
+    *other_refs, out_ref = refs
+    members, nodes, _ = own_ref.shape
     out_ref[:, HALO : nodes - HALO] = own_ref[:, HALO : nodes - HALO].astype(jnp.bfloat16)
-    for ref, rows in zip((one_ref, other_ref), rim_starts(region_ref, nodes)):
-        out_ref[:, rows] = (own_ref[:, rows] + ref[...].astype(jnp.float32)).astype(jnp.bfloat16)
+    one_rows, other_rows = rim_starts(region_ref, nodes)
+    out_ref[:, one_rows] = (own_ref[:, one_rows] + one_ref[...].astype(jnp.float32)).astype(jnp.bfloat16)
+    for m in range(members):
+        rows = own_ref[m, other_rows] + other_refs[m][...].astype(jnp.float32)
+        out_ref[m, other_rows] = rows.astype(jnp.bfloat16)
 
 
 def exchanged(block, second):
@@ -410,7 +414,7 @@
 
     out = kernel_call(
         lambda *refs: edges_kernel(members, *refs),
-        (mixed_shape,) * members + (shape((members, HALO, width), bf16),) * 2,
+        (mixed_shape,) * members + (shape((members, HALO, width), bf16),) + (edge,) * members,
         flops=2 * members * slots * width * (hidden + 2 * HALO),
         moved=6 * MIB,
         smem=1,
@@ -432,17 +436,17 @@
         moved=6 * MIB,
         operands=1 + members,
     )(table, *d_mixed)
-    other = exchanged(rims[1], True)
+    other = [exchanged(block, True) for block in rims[1:]]
     (total,) = pieces
     step = 1
     while step < regions:
         received = swapped(total, "space", step)
         step = 2 * step
         if step == regions:
-            received, other = lax.optimization_barrier((received, other))
+            received, other, own = lax.optimization_barrier((received, other, own))
         (total,) = summed([total], [received])
         if 2 * step == regions:
-            total, own, rims = lax.optimization_barrier((total, own, rims))
+            total, rims = lax.optimization_barrier((total, rims))
             one = exchanged(rims[0], False)
     totals = {0: total}
     bit = 2
@@ -456,8 +460,8 @@
         flops=MIB,
         moved=3 * MIB,
         smem=1,
-        operands=4,
-    )(region_at, own, one, other)
+        operands=3 + members,
+    )(region_at, own, one, *other)
     totals = [totals[i] for i in range(ranks)]
     totals, latent_grad = lax.optimization_barrier((totals, latent_grad))
     row = shape((1, hidden), f32)

time: 73.7 us -> 73.7 us (level)
  starting transfers between devices: 18.2 us -> 22.7 us
  Pallas kernels: 25.9 us -> 21.5 us
    pallas_call x2, Pallas kernels: 9.56 us -> 4.98 us  [per_device(): kernel_call(lambda *refs: forward_kernel(m, *refs), (mixed_shape,) + (sav...]
    ppermute x14, waiting for transfers between devices: 25.1 us -> 21.4 us  [swapped(): lax.ppermute(block, axis, [(i, i ^ by) for i in range(lax.axis_size(axis))])]
    ppermute x6 -> x7, waiting for transfers between devices: 2.25 us -> 5.89 us  [exchanged(): return lax.ppermute(block, 'space', pairs)]
    ppermute x14, starting transfers between devices: 7.94 us -> 11 us  [swapped(): lax.ppermute(block, axis, [(i, i ^ by) for i in range(lax.axis_size(axis))])]
    ppermute x6 -> x7, starting transfers between devices: 10.2 us -> 11.7 us  [exchanged(): return lax.ppermute(block, 'space', pairs)]
  transfers between devices with their start and end apart: 20 -> 21, of which waited for: 11 -> 11; matrix products, arithmetic and copies ran while one was open for 0% -> 0% of each run, Pallas kernels for 27% -> 21%
where the time goes in v16:
time: 73.7 us; the launch traced here: 73.6 us
  waiting for transfers between devices  27.3 us (37%)
  starting transfers between devices  22.7 us (31%)
  Pallas kernels  21.5 us (29%)
  local copies, waits for them, and re-layouts  1.27 us (2%)
  between operations  0.85 us (1%)
    ppermute x14, waiting for transfers between devices, swapped(): lax.ppermute(block, axis, [(i, i ^ by) for i in range(lax.axis_size(axis))])  21.4 us
    ppermute x7, starting transfers between devices, exchanged(): return lax.ppermute(block, 'space', pairs)  11.7 us
    ppermute x14, starting transfers between devices, swapped(): lax.ppermute(block, axis, [(i, i ^ by) for i in range(lax.axis_size(axis))])  11 us
    ppermute x7, waiting for transfers between devices, exchanged(): return lax.ppermute(block, 'space', pairs)  5.89 us
    pallas_call x2, Pallas kernels, per_device(): kernel_call(lambda *refs: forward_kernel(m, *refs), (mixed_shape,) + (sav...  4.98 us
    pallas_call x2, Pallas kernels, scored(): kernel_call(lambda *refs: score_kernel(members, len(others), members * ra...  4.77 us
    pallas_call x1, Pallas kernels, per_device(): kernel_call(lambda *refs: backward_kernel(members, ranks, *refs), (saved_...  3.15 us
    pallas_call x1, Pallas kernels, per_device(): kernel_call(table_kernel, (shape((ext, slots), bf16), shape((width, slots...  3.13 us
  transfers between devices with their start and end apart: 21, of which 11 were waited for; matrix products, arithmetic and copies ran while one was open for 0% of the time, Pallas kernels for 21%

profile of v16, /device:TPU:0, one launch (start us, length us, event | category | flops | bytes accessed | tf_op | source)
XLA Modules:
  0.0 73.6 jit_solution(10922965769451529149)
XLA Ops:
  0.6 0.0 copy-start.7
  0.6 1.2 %copy-done.7 = bf16[2,1024,256]{2,1,0:T(8,128)(2,1)S(1)} copy-done((bf16[2,1024,256]{2,1,0:T(8,128)(2,1)S(1)}, bf16[2,1024,256]{2,1,0:T(8,128)(2,1)}, u32[]{:S(2)}) %copy-start.7) | copy-done | bytes 1048600
  1.9 0.1 shard_map.153
  2.0 0.0 copy-start
  2.0 0.0 copy-start.1
  2.0 0.0 copy-start.2
  2.0 0.0 copy-start.4
  2.0 0.0 copy-start.5
  2.0 3.1 %collective-permute-start = (bf16[256,256]{1,0:T(8,128)(2,1)S(1)}, bf16[256,256]{1,0:T(8,128)(2,1)S(1)}, u32[]{:S(2)}, u32[]{:S(2)}) collective-permute-start(bf16[256,256]{1,0:T(8,128)(2,1)S(1)} %get-tuple-element.74), channel_id=1, source_target_pairs={{0,4},{4,0},{8,12},{12,8},{1,5},{5,1},{9,13},{13,9},{2,6},{6,2},{1... | collective-permute-start | bytes 393224 | tf_op jit(solution)/shard_map/ppermute | solution.py:318
  5.1 2.5 %collective-permute-start.1 = (bf16[256,256]{1,0:T(8,128)(2,1)S(1)}, bf16[256,256]{1,0:T(8,128)(2,1)S(1)}, u32[]{:S(2)}, u32[]{:S(2)}) collective-permute-start(bf16[256,256]{1,0:T(8,128)(2,1)S(1)} %get-tuple-element.75), channel_id=1, source_target_pairs={{0,12},{4,8},{8,4},{12,0},{1,13},{5,9},{9,5},{13,1},{2,14},{6,10},... | collective-permute-start | bytes 393224 | tf_op jit(solution)/shard_map/ppermute | solution.py:318
  7.6 0.0 copy-done.6
  7.6 0.0 copy-done.9
  7.6 3.1 %shard_map.154 = (bf16[1536,1536]{1,0:T(8,128)(2,1)S(1)}, f32[256,1536]{1,0:T(8,128)S(1)}, bf16[256,256]{1,0:T(8,128)(2,1)S(1)}, bf16[256,256]{1,0:T(8,128)(2,1)S(1)}) custom-call(s32[1]{0:T(128)} %bitcast.1.region_ref.refs_0_, s32[1]{0:T(128)} %bitcast.rank_ref.refs_1_.refs_0_, s32[4]{0:T(128)S(1)} %copy-done.6, s32[4,1536]{1,0:T(4,128)S(1)} %copy-done.8, ...), custom_call_target="tpu_custom_call" | custom-call | flops 805306368 | bytes 12582912 | tf_op jit(solution)/shard_map/pallas_call | solution.py:345
  10.7 0.7 %collective-permute-start.2 = (bf16[256,256]{1,0:T(8,128)(2,1)S(1)}, bf16[256,256]{1,0:T(8,128)(2,1)S(1)}, u32[]{:S(2)}, u32[]{:S(2)}) collective-permute-start(bf16[256,256]{1,0:T(8,128)(2,1)S(1)} %get-tuple-element.77), channel_id=1, source_target_pairs={{0,4},{4,0},{8,12},{12,8},{1,5},{5,1},{9,13},{13,9},{2,6},{6,2},{1... | collective-permute-start | bytes 393224 | tf_op jit(solution)/shard_map/ppermute | solution.py:318
  11.5 0.9 %collective-permute-start.3 = (bf16[256,256]{1,0:T(8,128)(2,1)S(1)}, bf16[256,256]{1,0:T(8,128)(2,1)S(1)}, u32[]{:S(2)}, u32[]{:S(2)}) collective-permute-start(bf16[256,256]{1,0:T(8,128)(2,1)S(1)} %get-tuple-element.78), channel_id=1, source_target_pairs={{0,12},{4,8},{8,4},{12,0},{1,13},{5,9},{9,5},{13,1},{2,14},{6,10},... | collective-permute-start | bytes 393224 | tf_op jit(solution)/shard_map/ppermute | solution.py:318
  12.4 0.0 collective-permute-done.refs_3_
  12.4 2.2 %collective-permute-done.1.refs_4_ = bf16[256,256]{1,0:T(8,128)(2,1)S(1)} collective-permute-done((bf16[256,256]{1,0:T(8,128)(2,1)S(1)}, bf16[256,256]{1,0:T(8,128)(2,1)S(1)}, u32[]{:S(2)}, u32[]{:S(2)}) %collective-permute-start.1) | collective-permute-done | bytes 131104 | tf_op jit(solution)/shard_map/ppermute | solution.py:318
  14.6 0.0 copy-done.1
  14.7 2.0 %shard_map.155 = (bf16[256,1536]{1,0:T(8,128)(2,1)S(1)}, bf16[256,1536]{1,0:T(8,128)(2,1)S(1)}, bf16[256,1536]{1,0:T(8,128)(2,1)S(1)}, bf16[256,1536]{1,0:T(8,12...) custom-call(s32[1]{0:T(128)} %bitcast.1.region_ref.refs_0_, ...), custom_call_target="tpu_custom_call" | custom-call | flops 905969664 | bytes 8388608 | tf_op jit(solution)/shard_map/pallas_call | solution.py:361
  16.6 0.0 copy-start.3
  16.6 1.6 %collective-permute-start.7 = (bf16[128,1536]{1,0:T(8,128)(2,1)S(1)}, bf16[128,1536]{1,0:T(8,128)(2,1)S(1)}, u32[]{:S(2)}, u32[]{:S(2)}) collective-permute-start(bf16[128,1536]{1,0:T(8,128)(2,1)S(1)} %get-tuple-element.76.refs_2_), channel_id=1, source_target_pairs={{0,2},{1,3},{2,0},{3,1},{4,6},{5,7},{6,4},{7,5},{8,10},{9,11},{10,... | collective-permute-start | bytes 1179656 | tf_op jit(solution)/shard_map/ppermute | solution.py:322
  18.2 0.0 collective-permute-start.5
  18.2 0.0 collective-permute-done.2.refs_3_
  18.2 1.1 %collective-permute-done.3.refs_4_ = bf16[256,256]{1,0:T(8,128)(2,1)S(1)} collective-permute-done((bf16[256,256]{1,0:T(8,128)(2,1)S(1)}, bf16[256,256]{1,0:T(8,128)(2,1)S(1)}, u32[]{:S(2)}, u32[]{:S(2)}) %collective-permute-start.3) | collective-permute-done | bytes 131104 | tf_op jit(solution)/shard_map/ppermute | solution.py:318
  19.3 3.0 %shard_map.156 = (bf16[256,1536]{1,0:T(8,128)(2,1)S(1)}, bf16[256,1536]{1,0:T(8,128)(2,1)S(1)}, bf16[256,1536]{1,0:T(8,128)(2,1)S(1)}, bf16[256,1536]{1,0:T(8,12...) custom-call(s32[1]{0:T(128)} %bitcast.1.region_ref.refs_0_, ...), custom_call_target="tpu_custom_call" | custom-call | flops 1711276032 | bytes 8388608 | tf_op jit(solution)/shard_map/pallas_call | solution.py:361
  22.4 0.1 collective-permute-start.6
  22.4 1.5 %collective-permute-start.4 = (bf16[128,1536]{1,0:T(8,128)(2,1)S(1)}, bf16[128,1536]{1,0:T(8,128)(2,1)S(1)}, u32[]{:S(2)}, u32[]{:S(2)}) collective-permute-start(bf16[128,1536]{1,0:T(8,128)(2,1)S(1)} %get-tuple-element.79.refs_3_), channel_id=1, source_target_pairs={{0,2},{1,3},{2,0},{3,1},{4,6},{5,7},{6,4},{7,5},{8,10},{9,11},{10,... | collective-permute-start | bytes 1179656 | tf_op jit(solution)/shard_map/ppermute | solution.py:322
  24.0 1.7 %collective-permute-done.7.refs_6_ = bf16[128,1536]{1,0:T(8,128)(2,1)S(1)} collective-permute-done((bf16[128,1536]{1,0:T(8,128)(2,1)S(1)}, bf16[128,1536]{1,0:T(8,128)(2,1)S(1)}, u32[]{:S(2)}, u32[]{:S(2)}) %collective-permute-start.7) | collective-permute-done | bytes 393248 | tf_op jit(solution)/shard_map/ppermute | solution.py:322
  25.7 0.0 collective-permute-done.5.refs_4_
  25.7 0.0 collective-permute-done.6.refs_5_
  25.7 2.7 %shard_map.157 = (f32[128,1536]{1,0:T(8,128)S(1)}, f32[128,1536]{1,0:T(8,128)S(1)}, f32[1,128]{1,0:T(1,128)S(1)}) custom-call(s32[1]{0:T(128)} %bitcast.1.region_ref.refs_0_, s32[4]{0:T(128)S(1)} %copy-done.6, bf16[128,1536]{1,0:T(8,128)(2,1)S(1)} %get-tuple-element.76.refs_2_, bf16[128,1536]{1,0:T(8,128)(2,1)S(1)} %get-tuple-element.79.refs_3_, ...), custom_call_target="tpu_custom_call" | custom-call | flops 4194304 | bytes 2097152 | tf_op jit(solution)/shard_map/pallas_call | solution.py:380
  28.4 5.7 %collective-permute-done.4.refs_4_ = bf16[128,1536]{1,0:T(8,128)(2,1)S(1)} collective-permute-done((bf16[128,1536]{1,0:T(8,128)(2,1)S(1)}, bf16[128,1536]{1,0:T(8,128)(2,1)S(1)}, u32[]{:S(2)}, u32[]{:S(2)}) %collective-permute-start.4) | collective-permute-done | bytes 393248 | tf_op jit(solution)/shard_map/ppermute | solution.py:322
  34.1 0.0 collective-permute-start.8
  34.1 0.5 collective-permute-start.9
  34.6 1.2 %collective-permute-done.8.refs_5_ = bf16[128,1536]{1,0:T(8,128)(2,1)S(1)} collective-permute-done((bf16[128,1536]{1,0:T(8,128)(2,1)S(1)}, bf16[128,1536]{1,0:T(8,128)(2,1)S(1)}, u32[]{:S(2)}, u32[]{:S(2)}) %collective-permute-start.8) | collective-permute-done | bytes 393248 | tf_op jit(solution)/shard_map/ppermute | solution.py:322
  35.8 0.6 collective-permute-done.9.refs_6_
  36.4 2.1 %shard_map.158 = (bf16[128,1536]{1,0:T(8,128)(2,1)S(1)}, bf16[128,1536]{1,0:T(8,128)(2,1)S(1)}, f32[1,128]{1,0:T(1,128)S(1)}) custom-call(s32[1]{0:T(128)} %bitcast.1.region_ref.refs_0_, s32[4]{0:T(128)S(1)} %copy-done.6, bf16[128,1536]{1,0:T(8,128)(2,1)S(1)} %get-tuple-element.76.refs_2_, bf16[128,1536]{1,0:T(8,128)(2,1)S(1)} %get-tuple-element.79.refs_3_, ...), custom_call_target="tpu_custom_call" | custom-call | flops 4194304 | bytes 2097152 | tf_op jit(solution)/shard_map/pallas_call | solution.py:380
  38.4 3.2 %shard_map.159 = (bf16[256,1536]{1,0:T(8,128)(2,1)S(1)}, bf16[256,1536]{1,0:T(8,128)(2,1)S(1)}, bf16[176,256]{1,0:T(8,128)(2,1)S(1)}, bf16[176,256]{1,0:T(8,128)...) custom-call(s32[1]{0:T(128)} %bitcast.1.region_ref.refs_0_, s32[1]{0:T(128)} %bitcast.rank_ref.refs_1_.refs_0_, ...), custom_call_target="tpu_custom_call" | custom-call | flops 2013265920 | bytes 10485760 | tf_op jit(solution)/shard_map/pallas_call | solution.py:399
  41.6 0.2 collective-permute-start.10
  41.8 0.4 collective-permute-start.11
  42.2 1.4 %shard_map.160 = (bf16[256,1536]{1,0:T(8,128)(2,1)S(1)}, bf16[256,1536]{1,0:T(8,128)(2,1)S(1)}, bf16[2,256,256]{2,1,0:T(8,128)(2,1)S(1)}, bf16[256,256]{1,0:T(8,128)(2,1)S(1)}, bf16[256,256]{1,0:T(8,128)(2,1)S(1)}) custom-call(s32[1]{0:T(128)} %bitcast.1.region_ref.refs_0_, bf16[1536,1536]{1,0:T(8,128)(2,1)S(1)} %get-tuple-element.73.refs_2_.refs_1_.table_ref, ...), custom_call_target="tpu_custom_call" | custom-call | flops 1207959552 | bytes 6291456 | tf_op jit(solution)/shard_map/pallas_call | solution.py:415
  43.6 0.0 collective-permute-done.10.refs_2_
  43.6 0.0 collective-permute-done.11.refs_3_
  43.7 1.6 %collective-permute-start.12 = (bf16[176,256]{1,0:T(8,128)(2,1)S(1)}, bf16[176,256]{1,0:T(8,128)(2,1)S(1)}, u32[]{:S(2)}, u32[]{:S(2)}) collective-permute-start(bf16[176,256]{1,0:T(8,128)(2,1)S(1)} %get-tuple-element.112), channel_id=1, source_target_pairs={{0,2},{1,3},{2,0},{3,1},{4,6},{5,7},{6,4},{7,5},{8,10},{9,11},{10,... | collective-permute-start | bytes 270344 | tf_op jit(solution)/shard_map/ppermute | solution.py:322
  45.2 3.2 %collective-permute-done.12.refs_1_ = bf16[176,256]{1,0:T(8,128)(2,1)S(1)} collective-permute-done((bf16[176,256]{1,0:T(8,128)(2,1)S(1)}, bf16[176,256]{1,0:T(8,128)(2,1)S(1)}, u32[]{:S(2)}, u32[]{:S(2)}) %collective-permute-start.12) | collective-permute-done | bytes 90144 | tf_op jit(solution)/shard_map/ppermute | solution.py:322
  48.4 1.0 %collective-permute-start.13 = (bf16[176,256]{1,0:T(8,128)(2,1)S(1)}, bf16[176,256]{1,0:T(8,128)(2,1)S(1)}, u32[]{:S(2)}, u32[]{:S(2)}) collective-permute-start(bf16[176,256]{1,0:T(8,128)(2,1)S(1)} %shard_map.162.refs_0_), channel_id=1, source_target_pairs={{0,4},{4,0},{8,12},{12,8},{1,5},{5,1},{9,13},{13,9},{2,6},{6,2},{1... | collective-permute-start | bytes 270344 | tf_op jit(solution)/shard_map/ppermute | solution.py:322
  49.4 2.6 %collective-permute-start.15 = (bf16[256,256]{1,0:T(8,128)(2,1)S(1)}, bf16[256,256]{1,0:T(8,128)(2,1)S(1)}, u32[]{:S(2)}, u32[]{:S(2)}) collective-permute-start(bf16[256,256]{1,0:T(8,128)(2,1)S(1)} %get-tuple-element.114), channel_id=1, source_target_pairs={{0,12},{4,8},{8,4},{12,0},{1,13},{5,9},{9,5},{13,1},{2,14},{6,10},... | collective-permute-start | bytes 393224 | tf_op jit(solution)/shard_map/ppermute | solution.py:318
  52.1 1.2 %collective-permute-start.16 = (bf16[256,256]{1,0:T(8,128)(2,1)S(1)}, bf16[256,256]{1,0:T(8,128)(2,1)S(1)}, u32[]{:S(2)}, u32[]{:S(2)}) collective-permute-start(bf16[256,256]{1,0:T(8,128)(2,1)S(1)} %get-tuple-element.115), channel_id=1, source_target_pairs={{0,12},{4,8},{8,4},{12,0},{1,13},{5,9},{9,5},{13,1},{2,14},{6,10},... | collective-permute-start | bytes 393224 | tf_op jit(solution)/shard_map/ppermute | solution.py:318
  53.3 0.0 collective-permute-done.13.refs_1_
  53.3 2.6 %collective-permute-start.14 = (bf16[176,256]{1,0:T(8,128)(2,1)S(1)}, bf16[176,256]{1,0:T(8,128)(2,1)S(1)}, u32[]{:S(2)}, u32[]{:S(2)}) collective-permute-start(bf16[176,256]{1,0:T(8,128)(2,1)S(1)} %shard_map.163.refs_0_), channel_id=1, source_target_pairs={{0,8},{4,12},{8,0},{12,4},{1,9},{5,13},{9,1},{13,5},{2,10},{6,14},... | collective-permute-start | bytes 270344 | tf_op jit(solution)/shard_map/ppermute | solution.py:322
  55.9 0.6 collective-permute-start.20
  56.6 1.8 %shard_map.164.own_ref = f32[2,1024,256]{2,1,0:T(8,128)S(1)} custom-call(bf16[1536,1536]{1,0:T(8,128)(2,1)S(1)} %get-tuple-element.73.refs_2_.refs_1_.table_ref, bf16[256,1536]{1,0:T(8,128)(2,1)S(1)} %get-tuple-element.117.refs_0_, bf16[256,1536]{1,0:T(8,128)(2,1)S(1)} %get-tuple-element.118.refs_1_), custom_call_target="tpu_custom_call" | custom-call | flops 1610612736 | bytes 6291456 | tf_op jit(solution)/shard_map/pallas_call | solution.py:432
  58.4 0.0 collective-permute-done.15.refs_0_
  58.4 2.5 %collective-permute-done.16.refs_1_ = bf16[256,256]{1,0:T(8,128)(2,1)S(1)} collective-permute-done((bf16[256,256]{1,0:T(8,128)(2,1)S(1)}, bf16[256,256]{1,0:T(8,128)(2,1)S(1)}, u32[]{:S(2)}, u32[]{:S(2)}) %collective-permute-start.16) | collective-permute-done | bytes 131104 | tf_op jit(solution)/shard_map/ppermute | solution.py:318
  60.9 5.9 %collective-permute-done.14.refs_1_ = bf16[176,256]{1,0:T(8,128)(2,1)S(1)} collective-permute-done((bf16[176,256]{1,0:T(8,128)(2,1)S(1)}, bf16[176,256]{1,0:T(8,128)(2,1)S(1)}, u32[]{:S(2)}, u32[]{:S(2)}) %collective-permute-start.14) | collective-permute-done | bytes 90144 | tf_op jit(solution)/shard_map/ppermute | solution.py:322
  66.8 1.6 %collective-permute-start.18 = (bf16[176,256]{1,0:T(8,128)(2,1)S(1)}, bf16[176,256]{1,0:T(8,128)(2,1)S(1)}, u32[]{:S(2)}, u32[]{:S(2)}) collective-permute-start(bf16[176,256]{1,0:T(8,128)(2,1)S(1)} %shard_map.165.refs_1_), channel_id=1, source_target_pairs={{0,2},{1,3},{2,0},{3,1},{4,6},{5,7},{6,4},{7,5},{8,10},{9,11},{10,... | collective-permute-start | bytes 270344 | tf_op jit(solution)/shard_map/ppermute | solution.py:322
  68.3 0.0 collective-permute-start.17
  68.4 3.0 %collective-permute-done.18.refs_3_ = bf16[176,256]{1,0:T(8,128)(2,1)S(1)} collective-permute-done((bf16[176,256]{1,0:T(8,128)(2,1)S(1)}, bf16[176,256]{1,0:T(8,128)(2,1)S(1)}, u32[]{:S(2)}, u32[]{:S(2)}) %collective-permute-start.18) | collective-permute-done | bytes 90144 | tf_op jit(solution)/shard_map/ppermute | solution.py:322
  71.4 0.0 collective-permute-start.19
  71.4 0.0 collective-permute-done.20.one_ref
  71.4 1.1 %shard_map.166 = bf16[2,1024,256]{2,1,0:T(8,128)(2,1)} custom-call(s32[1]{0:T(128)} %bitcast.1.region_ref.refs_0_, f32[2,1024,256]{2,1,0:T(8,128)S(1)} %shard_map.164.own_ref, bf16[2,256,256]{2,1,0:T(8,128)(2,1)S(1)} %collective-permute-done.20.one_ref, bf16[256,256]{1,0:T(8,128)(2,1)S(1)} %collective-permute-done.15.refs_0_, ...), custom_call_target="tpu_custom_call" | custom-call | flops 1048576 | bytes 3145728 | tf_op jit(solution)/shard_map/pallas_call | solution.py:457
  72.5 0.0 collective-permute-done.17.refs_2_
  72.6 0.1 collective-permute-done.19.refs_4_
  72.7 0.9 %shard_map.167 = (f32[256,256]{1,0:T(8,128)}, f32[1,256]{1,0:T(1,128)}, f32[256,256]{1,0:T(8,128)}, f32[1,256]{1,0:T(1,128)}, f32[256,128]{1,0:T(8,128)}, /*index=5*/f32[1,4]{1,0:T(1,128)}) custom-call(s32[1]{0:T(128)} %bitcast.rank_ref.refs_1_.refs_0_, bf16[176,256]{1,0:T(8,128)(2,1)S(1)} %shard_map.165.refs_1_, ...), custom_call_target="tpu_custom_call" | custom-call | flops 1048576 | bytes 2097152 | tf_op jit(solution)/shard_map/pallas_call | solution.py:468
  (13 shorter events, 0.1 us)
Async XLA Ops:
  0.6 1.2 %copy-start.7 = (bf16[2,1024,256]{2,1,0:T(8,128)(2,1)S(1)}, bf16[2,1024,256]{2,1,0:T(8,128)(2,1)}, u32[]{:S(2)}) copy-start(bf16[2,1024,256]{2,1,0:T(8,128)(2,1)} %latent_ref.1) | copy-start | bytes 3145732
  1.9 5.7 %copy-start.6 = (s32[4]{0:T(128)S(1)}, s32[4]{0:T(128)}, u32[]{:S(2)}) copy-start(s32[4]{0:T(128)} %refs_1_.3) | copy-start | bytes 52
  1.9 5.7 %copy-start.8 = (s32[4,1536]{1,0:T(4,128)S(1)}, s32[4,1536]{1,0:T(4,128)}, u32[]{:S(2)}) copy-start(s32[4,1536]{1,0:T(4,128)} %nbr_ref.1) | copy-start | bytes 73732
  1.9 5.7 %copy-start.9 = (f32[4,1536]{1,0:T(4,128)S(1)}, f32[4,1536]{1,0:T(4,128)}, u32[]{:S(2)}) copy-start(f32[4,1536]{1,0:T(4,128)} %weight_ref.1) | copy-start | bytes 73732
  2.0 12.7 %copy-start = (bf16[256,256]{1,0:T(8,128)(2,1)S(1)}, bf16[256,256]{1,0:T(8,128)(2,1)}, u32[]{:S(2)}) copy-start(bf16[256,256]{1,0:T(8,128)(2,1)} %refs_2_.2) | copy-start | bytes 393220
  2.0 12.7 %copy-start.1 = (bf16[256,256]{1,0:T(8,128)(2,1)S(1)}, bf16[256,256]{1,0:T(8,128)(2,1)}, u32[]{:S(2)}) copy-start(bf16[256,256]{1,0:T(8,128)(2,1)} %refs_2_.3) | copy-start | bytes 393220
  2.0 12.7 %copy-start.2 = (bf16[256,128]{1,0:T(8,128)(2,1)S(1)}, bf16[256,128]{1,0:T(8,128)(2,1)}, u32[]{:S(2)}) copy-start(bf16[256,128]{1,0:T(8,128)(2,1)} %refs_3_.1) | copy-start | bytes 196612
  2.0 12.6 %copy-start.4 = (f32[256]{0:T(256)S(1)}, f32[256]{0:T(256)}, u32[]{:S(2)}) copy-start(f32[256]{0:T(256)} %param.16) | copy-start | bytes 3076
  2.0 12.6 %copy-start.5 = (f32[256]{0:T(256)S(1)}, f32[256]{0:T(256)}, u32[]{:S(2)}) copy-start(f32[256]{0:T(256)} %param.18) | copy-start | bytes 3076
  2.0 10.4 %collective-permute-start = (bf16[256,256]{1,0:T(8,128)(2,1)S(1)}, bf16[256,256]{1,0:T(8,128)(2,1)S(1)}, u32[]{:S(2)}, u32[]{:S(2)}) collective-permute-start(bf16[256,256]{1,0:T(8,128)(2,1)S(1)} %get-tuple-element.74), channel_id=1, source_target_pairs={{0,4},{4,0},{8,12},{12,8},{1,5},{5,1},{9,13},{13,9},{2,6},{6,2},{1... | collective-permute-start | bytes 393224 | tf_op jit(solution)/shard_map/ppermute | solution.py:318
  5.1 9.5 %collective-permute-start.1 = (bf16[256,256]{1,0:T(8,128)(2,1)S(1)}, bf16[256,256]{1,0:T(8,128)(2,1)S(1)}, u32[]{:S(2)}, u32[]{:S(2)}) collective-permute-start(bf16[256,256]{1,0:T(8,128)(2,1)S(1)} %get-tuple-element.75), channel_id=1, source_target_pairs={{0,12},{4,8},{8,4},{12,0},{1,13},{5,9},{9,5},{13,1},{2,14},{6,10},... | collective-permute-start | bytes 393224 | tf_op jit(solution)/shard_map/ppermute | solution.py:318
  10.7 7.5 %collective-permute-start.2 = (bf16[256,256]{1,0:T(8,128)(2,1)S(1)}, bf16[256,256]{1,0:T(8,128)(2,1)S(1)}, u32[]{:S(2)}, u32[]{:S(2)}) collective-permute-start(bf16[256,256]{1,0:T(8,128)(2,1)S(1)} %get-tuple-element.77), channel_id=1, source_target_pairs={{0,4},{4,0},{8,12},{12,8},{1,5},{5,1},{9,13},{13,9},{2,6},{6,2},{1... | collective-permute-start | bytes 393224 | tf_op jit(solution)/shard_map/ppermute | solution.py:318
  11.5 7.8 %collective-permute-start.3 = (bf16[256,256]{1,0:T(8,128)(2,1)S(1)}, bf16[256,256]{1,0:T(8,128)(2,1)S(1)}, u32[]{:S(2)}, u32[]{:S(2)}) collective-permute-start(bf16[256,256]{1,0:T(8,128)(2,1)S(1)} %get-tuple-element.78), channel_id=1, source_target_pairs={{0,12},{4,8},{8,4},{12,0},{1,13},{5,9},{9,5},{13,1},{2,14},{6,10},... | collective-permute-start | bytes 393224 | tf_op jit(solution)/shard_map/ppermute | solution.py:318
  16.6 9.1 %copy-start.3 = (bf16[1536,128]{1,0:T(8,128)(2,1)S(1)}, bf16[1536,128]{1,0:T(8,128)(2,1)}, u32[]{:S(2)}) copy-start(bf16[1536,128]{1,0:T(8,128)(2,1)} %refs_7_.5) | copy-start | bytes 1179652
  16.6 9.1 %collective-permute-start.7 = (bf16[128,1536]{1,0:T(8,128)(2,1)S(1)}, bf16[128,1536]{1,0:T(8,128)(2,1)S(1)}, u32[]{:S(2)}, u32[]{:S(2)}) collective-permute-start(bf16[128,1536]{1,0:T(8,128)(2,1)S(1)} %get-tuple-element.76.refs_2_), channel_id=1, source_target_pairs={{0,2},{1,3},{2,0},{3,1},{4,6},{5,7},{6,4},{7,5},{8,10},{9,11},{10,... | collective-permute-start | bytes 1179656 | tf_op jit(solution)/shard_map/ppermute | solution.py:322
  18.2 7.5 %collective-permute-start.5 = (bf16[128,1536]{1,0:T(8,128)(2,1)S(1)}, bf16[128,1536]{1,0:T(8,128)(2,1)S(1)}, u32[]{:S(2)}, u32[]{:S(2)}) collective-permute-start(bf16[128,1536]{1,0:T(8,128)(2,1)S(1)} %get-tuple-element.76.refs_2_), channel_id=1, source_target_pairs={{0,1},{1,0},{2,3},{3,2},{4,5},{5,4},{6,7},{7,6},{8,9},{9,8},{10,11... | collective-permute-start | bytes 1179656 | tf_op jit(solution)/shard_map/ppermute | solution.py:322
  22.4 3.4 %collective-permute-start.6 = (bf16[128,1536]{1,0:T(8,128)(2,1)S(1)}, bf16[128,1536]{1,0:T(8,128)(2,1)S(1)}, u32[]{:S(2)}, u32[]{:S(2)}) collective-permute-start(bf16[128,1536]{1,0:T(8,128)(2,1)S(1)} %get-tuple-element.79.refs_3_), channel_id=1, source_target_pairs={{0,1},{1,0},{2,3},{3,2},{4,5},{5,4},{6,7},{7,6},{8,9},{9,8},{10,11... | collective-permute-start | bytes 1179656 | tf_op jit(solution)/shard_map/ppermute | solution.py:322
  22.4 11.6 %collective-permute-start.4 = (bf16[128,1536]{1,0:T(8,128)(2,1)S(1)}, bf16[128,1536]{1,0:T(8,128)(2,1)S(1)}, u32[]{:S(2)}, u32[]{:S(2)}) collective-permute-start(bf16[128,1536]{1,0:T(8,128)(2,1)S(1)} %get-tuple-element.79.refs_3_), channel_id=1, source_target_pairs={{0,2},{1,3},{2,0},{3,1},{4,6},{5,7},{6,4},{7,5},{8,10},{9,11},{10,... | collective-permute-start | bytes 1179656 | tf_op jit(solution)/shard_map/ppermute | solution.py:322
  34.1 1.7 %collective-permute-start.8 = (bf16[128,1536]{1,0:T(8,128)(2,1)S(1)}, bf16[128,1536]{1,0:T(8,128)(2,1)S(1)}, u32[]{:S(2)}, u32[]{:S(2)}) collective-permute-start(bf16[128,1536]{1,0:T(8,128)(2,1)S(1)} %collective-permute-done.7.refs_6_), channel_id=1, source_target_pairs={{0,1},{1,0},{2,3},{3,2},{4,5},{5,4},{6,7},{7,6},{8,9},{9,8},{10,11... | collective-permute-start | bytes 1179656 | tf_op jit(solution)/shard_map/ppermute | solution.py:322
  34.1 2.3 %collective-permute-start.9 = (bf16[128,1536]{1,0:T(8,128)(2,1)S(1)}, bf16[128,1536]{1,0:T(8,128)(2,1)S(1)}, u32[]{:S(2)}, u32[]{:S(2)}) collective-permute-start(bf16[128,1536]{1,0:T(8,128)(2,1)S(1)} %collective-permute-done.4.refs_4_), channel_id=1, source_target_pairs={{0,1},{1,0},{2,3},{3,2},{4,5},{5,4},{6,7},{7,6},{8,9},{9,8},{10,11... | collective-permute-start | bytes 1179656 | tf_op jit(solution)/shard_map/ppermute | solution.py:322
  41.6 2.0 %collective-permute-start.10 = (bf16[176,256]{1,0:T(8,128)(2,1)S(1)}, bf16[176,256]{1,0:T(8,128)(2,1)S(1)}, u32[]{:S(2)}, u32[]{:S(2)}) collective-permute-start(bf16[176,256]{1,0:T(8,128)(2,1)S(1)} %get-tuple-element.102), channel_id=1, source_target_pairs={{0,1},{1,0},{2,3},{3,2},{4,5},{5,4},{6,7},{7,6},{8,9},{9,8},{10,11... | collective-permute-start | bytes 270344 | tf_op jit(solution)/shard_map/ppermute | solution.py:322
  41.8 1.8 %collective-permute-start.11 = (bf16[176,256]{1,0:T(8,128)(2,1)S(1)}, bf16[176,256]{1,0:T(8,128)(2,1)S(1)}, u32[]{:S(2)}, u32[]{:S(2)}) collective-permute-start(bf16[176,256]{1,0:T(8,128)(2,1)S(1)} %get-tuple-element.103), channel_id=1, source_target_pairs={{0,1},{1,0},{2,3},{3,2},{4,5},{5,4},{6,7},{7,6},{8,9},{9,8},{10,11... | collective-permute-start | bytes 270344 | tf_op jit(solution)/shard_map/ppermute | solution.py:322
  43.7 4.7 %collective-permute-start.12 = (bf16[176,256]{1,0:T(8,128)(2,1)S(1)}, bf16[176,256]{1,0:T(8,128)(2,1)S(1)}, u32[]{:S(2)}, u32[]{:S(2)}) collective-permute-start(bf16[176,256]{1,0:T(8,128)(2,1)S(1)} %get-tuple-element.112), channel_id=1, source_target_pairs={{0,2},{1,3},{2,0},{3,1},{4,6},{5,7},{6,4},{7,5},{8,10},{9,11},{10,... | collective-permute-start | bytes 270344 | tf_op jit(solution)/shard_map/ppermute | solution.py:322
  48.4 4.9 %collective-permute-start.13 = (bf16[176,256]{1,0:T(8,128)(2,1)S(1)}, bf16[176,256]{1,0:T(8,128)(2,1)S(1)}, u32[]{:S(2)}, u32[]{:S(2)}) collective-permute-start(bf16[176,256]{1,0:T(8,128)(2,1)S(1)} %shard_map.162.refs_0_), channel_id=1, source_target_pairs={{0,4},{4,0},{8,12},{12,8},{1,5},{5,1},{9,13},{13,9},{2,6},{6,2},{1... | collective-permute-start | bytes 270344 | tf_op jit(solution)/shard_map/ppermute | solution.py:322
  49.4 8.9 %collective-permute-start.15 = (bf16[256,256]{1,0:T(8,128)(2,1)S(1)}, bf16[256,256]{1,0:T(8,128)(2,1)S(1)}, u32[]{:S(2)}, u32[]{:S(2)}) collective-permute-start(bf16[256,256]{1,0:T(8,128)(2,1)S(1)} %get-tuple-element.114), channel_id=1, source_target_pairs={{0,12},{4,8},{8,4},{12,0},{1,13},{5,9},{9,5},{13,1},{2,14},{6,10},... | collective-permute-start | bytes 393224 | tf_op jit(solution)/shard_map/ppermute | solution.py:318
  52.1 8.8 %collective-permute-start.16 = (bf16[256,256]{1,0:T(8,128)(2,1)S(1)}, bf16[256,256]{1,0:T(8,128)(2,1)S(1)}, u32[]{:S(2)}, u32[]{:S(2)}) collective-permute-start(bf16[256,256]{1,0:T(8,128)(2,1)S(1)} %get-tuple-element.115), channel_id=1, source_target_pairs={{0,12},{4,8},{8,4},{12,0},{1,13},{5,9},{9,5},{13,1},{2,14},{6,10},... | collective-permute-start | bytes 393224 | tf_op jit(solution)/shard_map/ppermute | solution.py:318
  53.3 13.5 %collective-permute-start.14 = (bf16[176,256]{1,0:T(8,128)(2,1)S(1)}, bf16[176,256]{1,0:T(8,128)(2,1)S(1)}, u32[]{:S(2)}, u32[]{:S(2)}) collective-permute-start(bf16[176,256]{1,0:T(8,128)(2,1)S(1)} %shard_map.163.refs_0_), channel_id=1, source_target_pairs={{0,8},{4,12},{8,0},{12,4},{1,9},{5,13},{9,1},{13,5},{2,10},{6,14},... | collective-permute-start | bytes 270344 | tf_op jit(solution)/shard_map/ppermute | solution.py:322
  55.9 15.5 %collective-permute-start.20 = (bf16[2,256,256]{2,1,0:T(8,128)(2,1)S(1)}, bf16[2,256,256]{2,1,0:T(8,128)(2,1)S(1)}, u32[]{:S(2)}, u32[]{:S(2)}) collective-permute-start(bf16[2,256,256]{2,1,0:T(8,128)(2,1)S(1)} %get-tuple-element.121), channel_id=1, source_target_pairs={{0,4},{4,0},{8,12},{12,8},{1,5},{5,1},{9,13},{13,9},{2,6},{6,2},{1... | collective-permute-start | bytes 786440 | tf_op jit(solution)/shard_map/ppermute | solution.py:318
  66.8 4.6 %collective-permute-start.18 = (bf16[176,256]{1,0:T(8,128)(2,1)S(1)}, bf16[176,256]{1,0:T(8,128)(2,1)S(1)}, u32[]{:S(2)}, u32[]{:S(2)}) collective-permute-start(bf16[176,256]{1,0:T(8,128)(2,1)S(1)} %shard_map.165.refs_1_), channel_id=1, source_target_pairs={{0,2},{1,3},{2,0},{3,1},{4,6},{5,7},{6,4},{7,5},{8,10},{9,11},{10,... | collective-permute-start | bytes 270344 | tf_op jit(solution)/shard_map/ppermute | solution.py:322
  68.3 4.2 %collective-permute-start.17 = (bf16[176,256]{1,0:T(8,128)(2,1)S(1)}, bf16[176,256]{1,0:T(8,128)(2,1)S(1)}, u32[]{:S(2)}, u32[]{:S(2)}) collective-permute-start(bf16[176,256]{1,0:T(8,128)(2,1)S(1)} %shard_map.165.refs_1_), channel_id=1, source_target_pairs={{0,1},{1,0},{2,3},{3,2},{4,5},{5,4},{6,7},{7,6},{8,9},{9,8},{10,11... | collective-permute-start | bytes 270344 | tf_op jit(solution)/shard_map/ppermute | solution.py:322
  71.4 1.3 %collective-permute-start.19 = (bf16[176,256]{1,0:T(8,128)(2,1)S(1)}, bf16[176,256]{1,0:T(8,128)(2,1)S(1)}, u32[]{:S(2)}, u32[]{:S(2)}) collective-permute-start(bf16[176,256]{1,0:T(8,128)(2,1)S(1)} %collective-permute-done.18.refs_3_), channel_id=1, source_target_pairs={{0,1},{1,0},{2,3},{3,2},{4,5},{5,4},{6,7},{7,6},{8,9},{9,8},{10,11... | collective-permute-start | bytes 270344 | tf_op jit(solution)/shard_map/ppermute | solution.py:322

commit v17 on v15

--- a/solution.py
+++ b/solution.py
@@ -11,7 +11,8 @@
 EPSILON = 1e-05
 BLOCK = 256
 LANE = 128
-CHUNK = 256
+CHUNK = 768
+BACK_CHUNK = 512
 MIB = 1 << 20
 
 
@@ -224,7 +225,7 @@
 
     for m in range(members):
         mixed_ref, act_one_ref, slope_one_ref, act_two_ref, slope_two_ref, d_dec_ref = saved[m]
-        for lo, size in split(slots, CHUNK):
+        for lo, size in split(slots, BACK_CHUNK):
             lanes = slice(lo, lo + size)
             back = nn_dot(w_three, d_dec_ref[:, lanes]) * slope_two_ref[:, lanes].astype(jnp.float32)
             bias_two = bias_two + lane_sum(back)

time: 73.7 us -> 70.3 us (0.954)
  Pallas kernels: 25.9 us -> 21.2 us
  waiting for transfers between devices: 27.3 us -> 28.1 us
    pallas_call x2, Pallas kernels: 9.56 us -> 4.98 us  [per_device(): kernel_call(lambda *refs: forward_kernel(m, *refs), (mixed_shape,) + (sav...]
    ppermute x6, waiting for transfers between devices: 2.25 us -> 3.37 us  [exchanged(): return lax.ppermute(block, 'space', pairs)]
  transfers between devices with their start and end apart: 20 -> 20, of which waited for: 11 -> 11; matrix products, arithmetic and copies ran while one was open for 0% -> 0% of each run, Pallas kernels for 27% -> 22%
where the time goes in v17:
time: 70.3 us; the launch traced here: 70.2 us
  waiting for transfers between devices  28.1 us (40%)
  Pallas kernels  21.2 us (30%)
  starting transfers between devices  18.7 us (27%)
  local copies, waits for them, and re-layouts  1.27 us (2%)
  between operations  0.84 us (1%)
    ppermute x14, waiting for transfers between devices, swapped(): lax.ppermute(block, axis, [(i, i ^ by) for i in range(lax.axis_size(axis))])  24.8 us
    ppermute x6, starting transfers between devices, exchanged(): return lax.ppermute(block, 'space', pairs)  10.6 us
    ppermute x14, starting transfers between devices, swapped(): lax.ppermute(block, axis, [(i, i ^ by) for i in range(lax.axis_size(axis))])  8.13 us
    pallas_call x2, Pallas kernels, per_device(): kernel_call(lambda *refs: forward_kernel(m, *refs), (mixed_shape,) + (sav...  4.98 us
    pallas_call x2, Pallas kernels, scored(): kernel_call(lambda *refs: score_kernel(members, len(others), members * ra...  4.77 us
    ppermute x6, waiting for transfers between devices, exchanged(): return lax.ppermute(block, 'space', pairs)  3.37 us
    pallas_call x1, Pallas kernels, per_device(): kernel_call(table_kernel, (shape((ext, slots), bf16), shape((width, slots...  3.13 us
    pallas_call x1, Pallas kernels, per_device(): kernel_call(lambda *refs: backward_kernel(members, ranks, *refs), (saved_...  2.84 us
  transfers between devices with their start and end apart: 20, of which 11 were waited for; matrix products, arithmetic and copies ran while one was open for 0% of the time, Pallas kernels for 22%

profile of v17, /device:TPU:0, one launch (start us, length us, event | category | flops | bytes accessed | tf_op | source)
XLA Modules:
  0.0 70.2 jit_solution(687990580679847336)
XLA Ops:
  0.6 0.0 copy-start.7
  0.6 1.2 %copy-done.7 = bf16[2,1024,256]{2,1,0:T(8,128)(2,1)S(1)} copy-done((bf16[2,1024,256]{2,1,0:T(8,128)(2,1)S(1)}, bf16[2,1024,256]{2,1,0:T(8,128)(2,1)}, u32[]{:S(2)}) %copy-start.7) | copy-done | bytes 1048600
  1.9 0.1 shard_map.153
  2.0 0.0 copy-start
  2.0 0.0 copy-start.1
  2.0 0.0 copy-start.2
  2.0 0.0 copy-start.4
  2.0 0.0 copy-start.5
  2.0 3.1 %collective-permute-start = (bf16[256,256]{1,0:T(8,128)(2,1)S(1)}, bf16[256,256]{1,0:T(8,128)(2,1)S(1)}, u32[]{:S(2)}, u32[]{:S(2)}) collective-permute-start(bf16[256,256]{1,0:T(8,128)(2,1)S(1)} %get-tuple-element.71), channel_id=1, source_target_pairs={{0,4},{4,0},{8,12},{12,8},{1,5},{5,1},{9,13},{13,9},{2,6},{6,2},{1... | collective-permute-start | bytes 393224 | tf_op jit(solution)/shard_map/ppermute | solution.py:315
  5.1 2.5 %collective-permute-start.1 = (bf16[256,256]{1,0:T(8,128)(2,1)S(1)}, bf16[256,256]{1,0:T(8,128)(2,1)S(1)}, u32[]{:S(2)}, u32[]{:S(2)}) collective-permute-start(bf16[256,256]{1,0:T(8,128)(2,1)S(1)} %get-tuple-element.72), channel_id=1, source_target_pairs={{0,12},{4,8},{8,4},{12,0},{1,13},{5,9},{9,5},{13,1},{2,14},{6,10},... | collective-permute-start | bytes 393224 | tf_op jit(solution)/shard_map/ppermute | solution.py:315
  7.6 0.0 copy-done.6
  7.6 0.0 copy-done.8
  7.6 0.0 copy-done.9
  7.6 3.1 %shard_map.154 = (bf16[1536,1536]{1,0:T(8,128)(2,1)S(1)}, f32[256,1536]{1,0:T(8,128)S(1)}, bf16[256,256]{1,0:T(8,128)(2,1)S(1)}, bf16[256,256]{1,0:T(8,128)(2,1)S(1)}) custom-call(s32[1]{0:T(128)} %bitcast.1.region_ref.refs_0_, s32[1]{0:T(128)} %bitcast.rank_ref.refs_1_.refs_0_, s32[4]{0:T(128)S(1)} %copy-done.6, s32[4,1536]{1,0:T(4,128)S(1)} %copy-done.8, ...), custom_call_target="tpu_custom_call" | custom-call | flops 805306368 | bytes 12582912 | tf_op jit(solution)/shard_map/pallas_call | solution.py:342
  10.7 0.7 %collective-permute-start.2 = (bf16[256,256]{1,0:T(8,128)(2,1)S(1)}, bf16[256,256]{1,0:T(8,128)(2,1)S(1)}, u32[]{:S(2)}, u32[]{:S(2)}) collective-permute-start(bf16[256,256]{1,0:T(8,128)(2,1)S(1)} %get-tuple-element.74), channel_id=1, source_target_pairs={{0,4},{4,0},{8,12},{12,8},{1,5},{5,1},{9,13},{13,9},{2,6},{6,2},{1... | collective-permute-start | bytes 393224 | tf_op jit(solution)/shard_map/ppermute | solution.py:315
  11.5 0.9 %collective-permute-start.3 = (bf16[256,256]{1,0:T(8,128)(2,1)S(1)}, bf16[256,256]{1,0:T(8,128)(2,1)S(1)}, u32[]{:S(2)}, u32[]{:S(2)}) collective-permute-start(bf16[256,256]{1,0:T(8,128)(2,1)S(1)} %get-tuple-element.75), channel_id=1, source_target_pairs={{0,12},{4,8},{8,4},{12,0},{1,13},{5,9},{9,5},{13,1},{2,14},{6,10},... | collective-permute-start | bytes 393224 | tf_op jit(solution)/shard_map/ppermute | solution.py:315
  12.4 0.0 collective-permute-done.refs_3_
  12.4 2.2 %collective-permute-done.1.refs_4_ = bf16[256,256]{1,0:T(8,128)(2,1)S(1)} collective-permute-done((bf16[256,256]{1,0:T(8,128)(2,1)S(1)}, bf16[256,256]{1,0:T(8,128)(2,1)S(1)}, u32[]{:S(2)}, u32[]{:S(2)}) %collective-permute-start.1) | collective-permute-done | bytes 131104 | tf_op jit(solution)/shard_map/ppermute | solution.py:315
  14.6 0.0 copy-done
  14.6 0.0 copy-done.1
  14.7 2.0 %shard_map.155 = (bf16[256,1536]{1,0:T(8,128)(2,1)S(1)}, bf16[256,1536]{1,0:T(8,128)(2,1)S(1)}, bf16[256,1536]{1,0:T(8,128)(2,1)S(1)}, bf16[256,1536]{1,0:T(8,12...) custom-call(s32[1]{0:T(128)} %bitcast.1.region_ref.refs_0_, ...), custom_call_target="tpu_custom_call" | custom-call | flops 905969664 | bytes 8388608 | tf_op jit(solution)/shard_map/pallas_call | solution.py:358
  16.6 0.0 copy-start.3
  16.6 1.6 %collective-permute-start.7 = (bf16[128,1536]{1,0:T(8,128)(2,1)S(1)}, bf16[128,1536]{1,0:T(8,128)(2,1)S(1)}, u32[]{:S(2)}, u32[]{:S(2)}) collective-permute-start(bf16[128,1536]{1,0:T(8,128)(2,1)S(1)} %get-tuple-element.73.refs_2_), channel_id=1, source_target_pairs={{0,2},{1,3},{2,0},{3,1},{4,6},{5,7},{6,4},{7,5},{8,10},{9,11},{10,... | collective-permute-start | bytes 1179656 | tf_op jit(solution)/shard_map/ppermute | solution.py:319
  18.2 0.0 collective-permute-start.5
  18.2 0.0 collective-permute-done.2.refs_3_
  18.2 1.1 %collective-permute-done.3.refs_4_ = bf16[256,256]{1,0:T(8,128)(2,1)S(1)} collective-permute-done((bf16[256,256]{1,0:T(8,128)(2,1)S(1)}, bf16[256,256]{1,0:T(8,128)(2,1)S(1)}, u32[]{:S(2)}, u32[]{:S(2)}) %collective-permute-start.3) | collective-permute-done | bytes 131104 | tf_op jit(solution)/shard_map/ppermute | solution.py:315
  19.3 3.0 %shard_map.156 = (bf16[256,1536]{1,0:T(8,128)(2,1)S(1)}, bf16[256,1536]{1,0:T(8,128)(2,1)S(1)}, bf16[256,1536]{1,0:T(8,128)(2,1)S(1)}, bf16[256,1536]{1,0:T(8,12...) custom-call(s32[1]{0:T(128)} %bitcast.1.region_ref.refs_0_, ...), custom_call_target="tpu_custom_call" | custom-call | flops 1711276032 | bytes 8388608 | tf_op jit(solution)/shard_map/pallas_call | solution.py:358
  22.4 0.1 collective-permute-start.6
  22.4 1.5 %collective-permute-start.4 = (bf16[128,1536]{1,0:T(8,128)(2,1)S(1)}, bf16[128,1536]{1,0:T(8,128)(2,1)S(1)}, u32[]{:S(2)}, u32[]{:S(2)}) collective-permute-start(bf16[128,1536]{1,0:T(8,128)(2,1)S(1)} %get-tuple-element.76.refs_3_), channel_id=1, source_target_pairs={{0,2},{1,3},{2,0},{3,1},{4,6},{5,7},{6,4},{7,5},{8,10},{9,11},{10,... | collective-permute-start | bytes 1179656 | tf_op jit(solution)/shard_map/ppermute | solution.py:319
  24.0 1.7 %collective-permute-done.7.refs_6_ = bf16[128,1536]{1,0:T(8,128)(2,1)S(1)} collective-permute-done((bf16[128,1536]{1,0:T(8,128)(2,1)S(1)}, bf16[128,1536]{1,0:T(8,128)(2,1)S(1)}, u32[]{:S(2)}, u32[]{:S(2)}) %collective-permute-start.7) | collective-permute-done | bytes 393248 | tf_op jit(solution)/shard_map/ppermute | solution.py:319
  25.7 0.0 collective-permute-done.5.refs_4_
  25.7 0.0 collective-permute-done.6.refs_5_
  25.7 2.7 %shard_map.157 = (f32[128,1536]{1,0:T(8,128)S(1)}, f32[128,1536]{1,0:T(8,128)S(1)}, f32[1,128]{1,0:T(1,128)S(1)}) custom-call(s32[1]{0:T(128)} %bitcast.1.region_ref.refs_0_, s32[4]{0:T(128)S(1)} %copy-done.6, bf16[128,1536]{1,0:T(8,128)(2,1)S(1)} %get-tuple-element.73.refs_2_, bf16[128,1536]{1,0:T(8,128)(2,1)S(1)} %get-tuple-element.76.refs_3_, ...), custom_call_target="tpu_custom_call" | custom-call | flops 4194304 | bytes 2097152 | tf_op jit(solution)/shard_map/pallas_call | solution.py:377
  28.4 5.7 %collective-permute-done.4.refs_4_ = bf16[128,1536]{1,0:T(8,128)(2,1)S(1)} collective-permute-done((bf16[128,1536]{1,0:T(8,128)(2,1)S(1)}, bf16[128,1536]{1,0:T(8,128)(2,1)S(1)}, u32[]{:S(2)}, u32[]{:S(2)}) %collective-permute-start.4) | collective-permute-done | bytes 393248 | tf_op jit(solution)/shard_map/ppermute | solution.py:319
  34.1 0.0 collective-permute-start.8
  34.1 0.5 collective-permute-start.9
  34.6 1.2 %collective-permute-done.8.refs_5_ = bf16[128,1536]{1,0:T(8,128)(2,1)S(1)} collective-permute-done((bf16[128,1536]{1,0:T(8,128)(2,1)S(1)}, bf16[128,1536]{1,0:T(8,128)(2,1)S(1)}, u32[]{:S(2)}, u32[]{:S(2)}) %collective-permute-start.8) | collective-permute-done | bytes 393248 | tf_op jit(solution)/shard_map/ppermute | solution.py:319
  35.8 0.6 collective-permute-done.9.refs_6_
  36.4 2.1 %shard_map.158 = (bf16[128,1536]{1,0:T(8,128)(2,1)S(1)}, bf16[128,1536]{1,0:T(8,128)(2,1)S(1)}, f32[1,128]{1,0:T(1,128)S(1)}) custom-call(s32[1]{0:T(128)} %bitcast.1.region_ref.refs_0_, s32[4]{0:T(128)S(1)} %copy-done.6, bf16[128,1536]{1,0:T(8,128)(2,1)S(1)} %get-tuple-element.73.refs_2_, bf16[128,1536]{1,0:T(8,128)(2,1)S(1)} %get-tuple-element.76.refs_3_, ...), custom_call_target="tpu_custom_call" | custom-call | flops 4194304 | bytes 2097152 | tf_op jit(solution)/shard_map/pallas_call | solution.py:377
  38.4 2.8 %shard_map.159 = (bf16[256,1536]{1,0:T(8,128)(2,1)S(1)}, bf16[256,1536]{1,0:T(8,128)(2,1)S(1)}, bf16[176,256]{1,0:T(8,128)(2,1)S(1)}, bf16[176,256]{1,0:T(8,128)...) custom-call(s32[1]{0:T(128)} %bitcast.1.region_ref.refs_0_, s32[1]{0:T(128)} %bitcast.rank_ref.refs_1_.refs_0_, ...), custom_call_target="tpu_custom_call" | custom-call | flops 2013265920 | bytes 10485760 | tf_op jit(solution)/shard_map/pallas_call | solution.py:396
  41.3 0.2 collective-permute-start.10
  41.5 0.4 collective-permute-start.11
  41.9 1.4 %shard_map.160 = (bf16[256,1536]{1,0:T(8,128)(2,1)S(1)}, bf16[256,1536]{1,0:T(8,128)(2,1)S(1)}, bf16[2,256,256]{2,1,0:T(8,128)(2,1)S(1)}, bf16[2,256,256]{2,1,0:T(8,128)(2,1)S(1)}) custom-call(s32[1]{0:T(128)} %bitcast.1.region_ref.refs_0_, bf16[1536,1536]{1,0:T(8,128)(2,1)S(1)} %get-tuple-element.70.refs_2_.refs_1_.table_ref, ...), custom_call_target="tpu_custom_call" | custom-call | flops 1207959552 | bytes 6291456 | tf_op jit(solution)/shard_map/pallas_call | solution.py:412
  43.3 0.0 collective-permute-done.10.refs_2_
  43.3 0.0 collective-permute-done.11.refs_3_
  43.3 1.6 %collective-permute-start.12 = (bf16[176,256]{1,0:T(8,128)(2,1)S(1)}, bf16[176,256]{1,0:T(8,128)(2,1)S(1)}, u32[]{:S(2)}, u32[]{:S(2)}) collective-permute-start(bf16[176,256]{1,0:T(8,128)(2,1)S(1)} %get-tuple-element.108), channel_id=1, source_target_pairs={{0,2},{1,3},{2,0},{3,1},{4,6},{5,7},{6,4},{7,5},{8,10},{9,11},{10,... | collective-permute-start | bytes 270344 | tf_op jit(solution)/shard_map/ppermute | solution.py:319
  44.9 1.7 %collective-permute-start.15 = (bf16[2,256,256]{2,1,0:T(8,128)(2,1)S(1)}, bf16[2,256,256]{2,1,0:T(8,128)(2,1)S(1)}, u32[]{:S(2)}, u32[]{:S(2)}) collective-permute-start(bf16[2,256,256]{2,1,0:T(8,128)(2,1)S(1)} %get-tuple-element.112), channel_id=1, source_target_pairs={{0,12},{4,8},{8,4},{12,0},{1,13},{5,9},{9,5},{13,1},{2,14},{6,10},... | collective-permute-start | bytes 786440 | tf_op jit(solution)/shard_map/ppermute | solution.py:315
  46.6 1.5 %collective-permute-done.12.refs_1_ = bf16[176,256]{1,0:T(8,128)(2,1)S(1)} collective-permute-done((bf16[176,256]{1,0:T(8,128)(2,1)S(1)}, bf16[176,256]{1,0:T(8,128)(2,1)S(1)}, u32[]{:S(2)}, u32[]{:S(2)}) %collective-permute-start.12) | collective-permute-done | bytes 90144 | tf_op jit(solution)/shard_map/ppermute | solution.py:319
  48.1 1.0 %collective-permute-start.13 = (bf16[176,256]{1,0:T(8,128)(2,1)S(1)}, bf16[176,256]{1,0:T(8,128)(2,1)S(1)}, u32[]{:S(2)}, u32[]{:S(2)}) collective-permute-start(bf16[176,256]{1,0:T(8,128)(2,1)S(1)} %shard_map.162.refs_0_), channel_id=1, source_target_pairs={{0,4},{4,0},{8,12},{12,8},{1,5},{5,1},{9,13},{13,9},{2,6},{6,2},{1... | collective-permute-start | bytes 270344 | tf_op jit(solution)/shard_map/ppermute | solution.py:319
  49.1 1.8 %shard_map.164.own_ref = f32[2,1024,256]{2,1,0:T(8,128)S(1)} custom-call(bf16[1536,1536]{1,0:T(8,128)(2,1)S(1)} %get-tuple-element.70.refs_2_.refs_1_.table_ref, bf16[256,1536]{1,0:T(8,128)(2,1)S(1)} %get-tuple-element.109.refs_0_, bf16[256,1536]{1,0:T(8,128)(2,1)S(1)} %get-tuple-element.110.refs_1_), custom_call_target="tpu_custom_call" | custom-call | flops 1610612736 | bytes 6291456 | tf_op jit(solution)/shard_map/pallas_call | solution.py:429
  51.0 5.8 %collective-permute-done.13.refs_1_ = bf16[176,256]{1,0:T(8,128)(2,1)S(1)} collective-permute-done((bf16[176,256]{1,0:T(8,128)(2,1)S(1)}, bf16[176,256]{1,0:T(8,128)(2,1)S(1)}, u32[]{:S(2)}, u32[]{:S(2)}) %collective-permute-start.13) | collective-permute-done | bytes 90144 | tf_op jit(solution)/shard_map/ppermute | solution.py:319
  56.8 0.6 collective-permute-start.14
  57.4 1.7 %collective-permute-start.19 = (bf16[2,256,256]{2,1,0:T(8,128)(2,1)S(1)}, bf16[2,256,256]{2,1,0:T(8,128)(2,1)S(1)}, u32[]{:S(2)}, u32[]{:S(2)}) collective-permute-start(bf16[2,256,256]{2,1,0:T(8,128)(2,1)S(1)} %get-tuple-element.116), channel_id=1, source_target_pairs={{0,4},{4,0},{8,12},{12,8},{1,5},{5,1},{9,13},{13,9},{2,6},{6,2},{1... | collective-permute-start | bytes 786440 | tf_op jit(solution)/shard_map/ppermute | solution.py:315
  59.1 0.0 collective-permute-done.15.other_ref
  59.2 4.2 %collective-permute-done.14.refs_1_ = bf16[176,256]{1,0:T(8,128)(2,1)S(1)} collective-permute-done((bf16[176,256]{1,0:T(8,128)(2,1)S(1)}, bf16[176,256]{1,0:T(8,128)(2,1)S(1)}, u32[]{:S(2)}, u32[]{:S(2)}) %collective-permute-start.14) | collective-permute-done | bytes 90144 | tf_op jit(solution)/shard_map/ppermute | solution.py:319
  63.4 0.7 collective-permute-start.17
  64.1 0.0 collective-permute-start.16
  64.1 3.9 %collective-permute-done.17.refs_3_ = bf16[176,256]{1,0:T(8,128)(2,1)S(1)} collective-permute-done((bf16[176,256]{1,0:T(8,128)(2,1)S(1)}, bf16[176,256]{1,0:T(8,128)(2,1)S(1)}, u32[]{:S(2)}, u32[]{:S(2)}) %collective-permute-start.17) | collective-permute-done | bytes 90144 | tf_op jit(solution)/shard_map/ppermute | solution.py:319
  68.0 0.0 collective-permute-start.18
  68.0 0.0 collective-permute-done.19.one_ref
  68.0 1.1 %shard_map.166 = bf16[2,1024,256]{2,1,0:T(8,128)(2,1)} custom-call(s32[1]{0:T(128)} %bitcast.1.region_ref.refs_0_, f32[2,1024,256]{2,1,0:T(8,128)S(1)} %shard_map.164.own_ref, bf16[2,256,256]{2,1,0:T(8,128)(2,1)S(1)} %collective-permute-done.19.one_ref, bf16[2,256,256]{2,1,0:T(8,128)(2,1)S(1)} %collective-permute-done.15.other_ref), custom_call_target="tpu_custom_call" | custom-call | flops 1048576 | bytes 3145728 | tf_op jit(solution)/shard_map/pallas_call | solution.py:454
  69.1 0.0 collective-permute-done.16.refs_2_
  69.2 0.1 collective-permute-done.18.refs_4_
  69.3 0.9 %shard_map.167 = (f32[256,256]{1,0:T(8,128)}, f32[1,256]{1,0:T(1,128)}, f32[256,256]{1,0:T(8,128)}, f32[1,256]{1,0:T(1,128)}, f32[256,128]{1,0:T(8,128)}, /*index=5*/f32[1,4]{1,0:T(1,128)}) custom-call(s32[1]{0:T(128)} %bitcast.rank_ref.refs_1_.refs_0_, bf16[176,256]{1,0:T(8,128)(2,1)S(1)} %shard_map.165.refs_1_, ...), custom_call_target="tpu_custom_call" | custom-call | flops 1048576 | bytes 2097152 | tf_op jit(solution)/shard_map/pallas_call | solution.py:465
  (11 shorter events, 0.1 us)
Async XLA Ops:
  0.6 1.2 %copy-start.7 = (bf16[2,1024,256]{2,1,0:T(8,128)(2,1)S(1)}, bf16[2,1024,256]{2,1,0:T(8,128)(2,1)}, u32[]{:S(2)}) copy-start(bf16[2,1024,256]{2,1,0:T(8,128)(2,1)} %latent_ref.1) | copy-start | bytes 3145732
  1.9 5.7 %copy-start.6 = (s32[4]{0:T(128)S(1)}, s32[4]{0:T(128)}, u32[]{:S(2)}) copy-start(s32[4]{0:T(128)} %refs_1_.3) | copy-start | bytes 52
  1.9 5.7 %copy-start.8 = (s32[4,1536]{1,0:T(4,128)S(1)}, s32[4,1536]{1,0:T(4,128)}, u32[]{:S(2)}) copy-start(s32[4,1536]{1,0:T(4,128)} %nbr_ref.1) | copy-start | bytes 73732
  1.9 5.7 %copy-start.9 = (f32[4,1536]{1,0:T(4,128)S(1)}, f32[4,1536]{1,0:T(4,128)}, u32[]{:S(2)}) copy-start(f32[4,1536]{1,0:T(4,128)} %weight_ref.1) | copy-start | bytes 73732
  2.0 12.7 %copy-start = (bf16[256,256]{1,0:T(8,128)(2,1)S(1)}, bf16[256,256]{1,0:T(8,128)(2,1)}, u32[]{:S(2)}) copy-start(bf16[256,256]{1,0:T(8,128)(2,1)} %refs_2_.2) | copy-start | bytes 393220
  2.0 12.7 %copy-start.1 = (bf16[256,256]{1,0:T(8,128)(2,1)S(1)}, bf16[256,256]{1,0:T(8,128)(2,1)}, u32[]{:S(2)}) copy-start(bf16[256,256]{1,0:T(8,128)(2,1)} %refs_2_.3) | copy-start | bytes 393220
  2.0 12.7 %copy-start.2 = (bf16[256,128]{1,0:T(8,128)(2,1)S(1)}, bf16[256,128]{1,0:T(8,128)(2,1)}, u32[]{:S(2)}) copy-start(bf16[256,128]{1,0:T(8,128)(2,1)} %refs_3_.1) | copy-start | bytes 196612
  2.0 12.6 %copy-start.4 = (f32[256]{0:T(256)S(1)}, f32[256]{0:T(256)}, u32[]{:S(2)}) copy-start(f32[256]{0:T(256)} %param.16) | copy-start | bytes 3076
  2.0 12.6 %copy-start.5 = (f32[256]{0:T(256)S(1)}, f32[256]{0:T(256)}, u32[]{:S(2)}) copy-start(f32[256]{0:T(256)} %param.18) | copy-start | bytes 3076
  2.0 10.4 %collective-permute-start = (bf16[256,256]{1,0:T(8,128)(2,1)S(1)}, bf16[256,256]{1,0:T(8,128)(2,1)S(1)}, u32[]{:S(2)}, u32[]{:S(2)}) collective-permute-start(bf16[256,256]{1,0:T(8,128)(2,1)S(1)} %get-tuple-element.71), channel_id=1, source_target_pairs={{0,4},{4,0},{8,12},{12,8},{1,5},{5,1},{9,13},{13,9},{2,6},{6,2},{1... | collective-permute-start | bytes 393224 | tf_op jit(solution)/shard_map/ppermute | solution.py:315
  5.1 9.5 %collective-permute-start.1 = (bf16[256,256]{1,0:T(8,128)(2,1)S(1)}, bf16[256,256]{1,0:T(8,128)(2,1)S(1)}, u32[]{:S(2)}, u32[]{:S(2)}) collective-permute-start(bf16[256,256]{1,0:T(8,128)(2,1)S(1)} %get-tuple-element.72), channel_id=1, source_target_pairs={{0,12},{4,8},{8,4},{12,0},{1,13},{5,9},{9,5},{13,1},{2,14},{6,10},... | collective-permute-start | bytes 393224 | tf_op jit(solution)/shard_map/ppermute | solution.py:315
  10.7 7.5 %collective-permute-start.2 = (bf16[256,256]{1,0:T(8,128)(2,1)S(1)}, bf16[256,256]{1,0:T(8,128)(2,1)S(1)}, u32[]{:S(2)}, u32[]{:S(2)}) collective-permute-start(bf16[256,256]{1,0:T(8,128)(2,1)S(1)} %get-tuple-element.74), channel_id=1, source_target_pairs={{0,4},{4,0},{8,12},{12,8},{1,5},{5,1},{9,13},{13,9},{2,6},{6,2},{1... | collective-permute-start | bytes 393224 | tf_op jit(solution)/shard_map/ppermute | solution.py:315
  11.5 7.8 %collective-permute-start.3 = (bf16[256,256]{1,0:T(8,128)(2,1)S(1)}, bf16[256,256]{1,0:T(8,128)(2,1)S(1)}, u32[]{:S(2)}, u32[]{:S(2)}) collective-permute-start(bf16[256,256]{1,0:T(8,128)(2,1)S(1)} %get-tuple-element.75), channel_id=1, source_target_pairs={{0,12},{4,8},{8,4},{12,0},{1,13},{5,9},{9,5},{13,1},{2,14},{6,10},... | collective-permute-start | bytes 393224 | tf_op jit(solution)/shard_map/ppermute | solution.py:315
  16.6 9.1 %copy-start.3 = (bf16[1536,128]{1,0:T(8,128)(2,1)S(1)}, bf16[1536,128]{1,0:T(8,128)(2,1)}, u32[]{:S(2)}) copy-start(bf16[1536,128]{1,0:T(8,128)(2,1)} %refs_7_.5) | copy-start | bytes 1179652
  16.6 9.1 %collective-permute-start.7 = (bf16[128,1536]{1,0:T(8,128)(2,1)S(1)}, bf16[128,1536]{1,0:T(8,128)(2,1)S(1)}, u32[]{:S(2)}, u32[]{:S(2)}) collective-permute-start(bf16[128,1536]{1,0:T(8,128)(2,1)S(1)} %get-tuple-element.73.refs_2_), channel_id=1, source_target_pairs={{0,2},{1,3},{2,0},{3,1},{4,6},{5,7},{6,4},{7,5},{8,10},{9,11},{10,... | collective-permute-start | bytes 1179656 | tf_op jit(solution)/shard_map/ppermute | solution.py:319
  18.2 7.5 %collective-permute-start.5 = (bf16[128,1536]{1,0:T(8,128)(2,1)S(1)}, bf16[128,1536]{1,0:T(8,128)(2,1)S(1)}, u32[]{:S(2)}, u32[]{:S(2)}) collective-permute-start(bf16[128,1536]{1,0:T(8,128)(2,1)S(1)} %get-tuple-element.73.refs_2_), channel_id=1, source_target_pairs={{0,1},{1,0},{2,3},{3,2},{4,5},{5,4},{6,7},{7,6},{8,9},{9,8},{10,11... | collective-permute-start | bytes 1179656 | tf_op jit(solution)/shard_map/ppermute | solution.py:319
  22.4 3.4 %collective-permute-start.6 = (bf16[128,1536]{1,0:T(8,128)(2,1)S(1)}, bf16[128,1536]{1,0:T(8,128)(2,1)S(1)}, u32[]{:S(2)}, u32[]{:S(2)}) collective-permute-start(bf16[128,1536]{1,0:T(8,128)(2,1)S(1)} %get-tuple-element.76.refs_3_), channel_id=1, source_target_pairs={{0,1},{1,0},{2,3},{3,2},{4,5},{5,4},{6,7},{7,6},{8,9},{9,8},{10,11... | collective-permute-start | bytes 1179656 | tf_op jit(solution)/shard_map/ppermute | solution.py:319
  22.4 11.6 %collective-permute-start.4 = (bf16[128,1536]{1,0:T(8,128)(2,1)S(1)}, bf16[128,1536]{1,0:T(8,128)(2,1)S(1)}, u32[]{:S(2)}, u32[]{:S(2)}) collective-permute-start(bf16[128,1536]{1,0:T(8,128)(2,1)S(1)} %get-tuple-element.76.refs_3_), channel_id=1, source_target_pairs={{0,2},{1,3},{2,0},{3,1},{4,6},{5,7},{6,4},{7,5},{8,10},{9,11},{10,... | collective-permute-start | bytes 1179656 | tf_op jit(solution)/shard_map/ppermute | solution.py:319
  34.1 1.7 %collective-permute-start.8 = (bf16[128,1536]{1,0:T(8,128)(2,1)S(1)}, bf16[128,1536]{1,0:T(8,128)(2,1)S(1)}, u32[]{:S(2)}, u32[]{:S(2)}) collective-permute-start(bf16[128,1536]{1,0:T(8,128)(2,1)S(1)} %collective-permute-done.7.refs_6_), channel_id=1, source_target_pairs={{0,1},{1,0},{2,3},{3,2},{4,5},{5,4},{6,7},{7,6},{8,9},{9,8},{10,11... | collective-permute-start | bytes 1179656 | tf_op jit(solution)/shard_map/ppermute | solution.py:319
  34.1 2.3 %collective-permute-start.9 = (bf16[128,1536]{1,0:T(8,128)(2,1)S(1)}, bf16[128,1536]{1,0:T(8,128)(2,1)S(1)}, u32[]{:S(2)}, u32[]{:S(2)}) collective-permute-start(bf16[128,1536]{1,0:T(8,128)(2,1)S(1)} %collective-permute-done.4.refs_4_), channel_id=1, source_target_pairs={{0,1},{1,0},{2,3},{3,2},{4,5},{5,4},{6,7},{7,6},{8,9},{9,8},{10,11... | collective-permute-start | bytes 1179656 | tf_op jit(solution)/shard_map/ppermute | solution.py:319
  41.3 2.0 %collective-permute-start.10 = (bf16[176,256]{1,0:T(8,128)(2,1)S(1)}, bf16[176,256]{1,0:T(8,128)(2,1)S(1)}, u32[]{:S(2)}, u32[]{:S(2)}) collective-permute-start(bf16[176,256]{1,0:T(8,128)(2,1)S(1)} %get-tuple-element.99), channel_id=1, source_target_pairs={{0,1},{1,0},{2,3},{3,2},{4,5},{5,4},{6,7},{7,6},{8,9},{9,8},{10,11... | collective-permute-start | bytes 270344 | tf_op jit(solution)/shard_map/ppermute | solution.py:319
  41.5 1.8 %collective-permute-start.11 = (bf16[176,256]{1,0:T(8,128)(2,1)S(1)}, bf16[176,256]{1,0:T(8,128)(2,1)S(1)}, u32[]{:S(2)}, u32[]{:S(2)}) collective-permute-start(bf16[176,256]{1,0:T(8,128)(2,1)S(1)} %get-tuple-element.100), channel_id=1, source_target_pairs={{0,1},{1,0},{2,3},{3,2},{4,5},{5,4},{6,7},{7,6},{8,9},{9,8},{10,11... | collective-permute-start | bytes 270344 | tf_op jit(solution)/shard_map/ppermute | solution.py:319
  43.3 4.7 %collective-permute-start.12 = (bf16[176,256]{1,0:T(8,128)(2,1)S(1)}, bf16[176,256]{1,0:T(8,128)(2,1)S(1)}, u32[]{:S(2)}, u32[]{:S(2)}) collective-permute-start(bf16[176,256]{1,0:T(8,128)(2,1)S(1)} %get-tuple-element.108), channel_id=1, source_target_pairs={{0,2},{1,3},{2,0},{3,1},{4,6},{5,7},{6,4},{7,5},{8,10},{9,11},{10,... | collective-permute-start | bytes 270344 | tf_op jit(solution)/shard_map/ppermute | solution.py:319
  44.9 14.2 %collective-permute-start.15 = (bf16[2,256,256]{2,1,0:T(8,128)(2,1)S(1)}, bf16[2,256,256]{2,1,0:T(8,128)(2,1)S(1)}, u32[]{:S(2)}, u32[]{:S(2)}) collective-permute-start(bf16[2,256,256]{2,1,0:T(8,128)(2,1)S(1)} %get-tuple-element.112), channel_id=1, source_target_pairs={{0,12},{4,8},{8,4},{12,0},{1,13},{5,9},{9,5},{13,1},{2,14},{6,10},... | collective-permute-start | bytes 786440 | tf_op jit(solution)/shard_map/ppermute | solution.py:315
  48.1 8.7 %collective-permute-start.13 = (bf16[176,256]{1,0:T(8,128)(2,1)S(1)}, bf16[176,256]{1,0:T(8,128)(2,1)S(1)}, u32[]{:S(2)}, u32[]{:S(2)}) collective-permute-start(bf16[176,256]{1,0:T(8,128)(2,1)S(1)} %shard_map.162.refs_0_), channel_id=1, source_target_pairs={{0,4},{4,0},{8,12},{12,8},{1,5},{5,1},{9,13},{13,9},{2,6},{6,2},{1... | collective-permute-start | bytes 270344 | tf_op jit(solution)/shard_map/ppermute | solution.py:319
  56.8 6.5 %collective-permute-start.14 = (bf16[176,256]{1,0:T(8,128)(2,1)S(1)}, bf16[176,256]{1,0:T(8,128)(2,1)S(1)}, u32[]{:S(2)}, u32[]{:S(2)}) collective-permute-start(bf16[176,256]{1,0:T(8,128)(2,1)S(1)} %shard_map.163.refs_0_), channel_id=1, source_target_pairs={{0,8},{4,12},{8,0},{12,4},{1,9},{5,13},{9,1},{13,5},{2,10},{6,14},... | collective-permute-start | bytes 270344 | tf_op jit(solution)/shard_map/ppermute | solution.py:319
  57.4 10.6 %collective-permute-start.19 = (bf16[2,256,256]{2,1,0:T(8,128)(2,1)S(1)}, bf16[2,256,256]{2,1,0:T(8,128)(2,1)S(1)}, u32[]{:S(2)}, u32[]{:S(2)}) collective-permute-start(bf16[2,256,256]{2,1,0:T(8,128)(2,1)S(1)} %get-tuple-element.116), channel_id=1, source_target_pairs={{0,4},{4,0},{8,12},{12,8},{1,5},{5,1},{9,13},{13,9},{2,6},{6,2},{1... | collective-permute-start | bytes 786440 | tf_op jit(solution)/shard_map/ppermute | solution.py:315
  63.4 4.6 %collective-permute-start.17 = (bf16[176,256]{1,0:T(8,128)(2,1)S(1)}, bf16[176,256]{1,0:T(8,128)(2,1)S(1)}, u32[]{:S(2)}, u32[]{:S(2)}) collective-permute-start(bf16[176,256]{1,0:T(8,128)(2,1)S(1)} %shard_map.165.refs_1_), channel_id=1, source_target_pairs={{0,2},{1,3},{2,0},{3,1},{4,6},{5,7},{6,4},{7,5},{8,10},{9,11},{10,... | collective-permute-start | bytes 270344 | tf_op jit(solution)/shard_map/ppermute | solution.py:319
  64.1 5.1 %collective-permute-start.16 = (bf16[176,256]{1,0:T(8,128)(2,1)S(1)}, bf16[176,256]{1,0:T(8,128)(2,1)S(1)}, u32[]{:S(2)}, u32[]{:S(2)}) collective-permute-start(bf16[176,256]{1,0:T(8,128)(2,1)S(1)} %shard_map.165.refs_1_), channel_id=1, source_target_pairs={{0,1},{1,0},{2,3},{3,2},{4,5},{5,4},{6,7},{7,6},{8,9},{9,8},{10,11... | collective-permute-start | bytes 270344 | tf_op jit(solution)/shard_map/ppermute | solution.py:319
  68.0 1.3 %collective-permute-start.18 = (bf16[176,256]{1,0:T(8,128)(2,1)S(1)}, bf16[176,256]{1,0:T(8,128)(2,1)S(1)}, u32[]{:S(2)}, u32[]{:S(2)}) collective-permute-start(bf16[176,256]{1,0:T(8,128)(2,1)S(1)} %collective-permute-done.17.refs_3_), channel_id=1, source_target_pairs={{0,1},{1,0},{2,3},{3,2},{4,5},{5,4},{6,7},{7,6},{8,9},{9,8},{10,11... | collective-permute-start | bytes 270344 | tf_op jit(solution)/shard_map/ppermute | solution.py:319

commit v18 on v17

--- a/solution.py
+++ b/solution.py
@@ -13,6 +13,7 @@
 LANE = 128
 CHUNK = 768
 BACK_CHUNK = 512
+FORWARD_CHUNK = 1536
 MIB = 1 << 20
 
 
@@ -117,7 +118,7 @@
 
     edges = jnp.concatenate([one_ref[...].T, other_ref[...].T], axis=1)
     own = own_ref[member].T if member else None
-    for lo, size in split(slots, CHUNK):
+    for lo, size in split(slots, FORWARD_CHUNK):
         lanes = slice(lo, lo + size)
         rims = jnp.concatenate([table_ref[rows, lanes] for rows in rim_starts(region_ref, ext)], axis=0)
         share = nn_dot(own, table_ref[HALO : ext - HALO, lanes]) if member else own_ref[:, lanes]

time: 70.3 us -> 70.2 us (level)
  waiting for transfers between devices: 28.1 us -> 28.9 us
  transfers between devices with their start and end apart: 20 -> 20, of which waited for: 11 -> 11; matrix products, arithmetic and copies ran while one was open for 0% -> 0% of each run, Pallas kernels for 22% -> 21%
where the time goes in v18:
time: 70.2 us; the launch traced here: 70.1 us
  waiting for transfers between devices  28.9 us (41%)
  Pallas kernels  20.6 us (29%)
  starting transfers between devices  18.4 us (26%)
  local copies, waits for them, and re-layouts  1.27 us (2%)
  between operations  0.84 us (1%)
    ppermute x14, waiting for transfers between devices, swapped(): lax.ppermute(block, axis, [(i, i ^ by) for i in range(lax.axis_size(axis))])  25.4 us
    ppermute x6, starting transfers between devices, exchanged(): return lax.ppermute(block, 'space', pairs)  10.6 us
    ppermute x14, starting transfers between devices, swapped(): lax.ppermute(block, axis, [(i, i ^ by) for i in range(lax.axis_size(axis))])  7.8 us
    pallas_call x2, Pallas kernels, scored(): kernel_call(lambda *refs: score_kernel(members, len(others), members * ra...  4.77 us
    pallas_call x2, Pallas kernels, per_device(): kernel_call(lambda *refs: forward_kernel(m, *refs), (mixed_shape,) + (sav...  4.42 us
    ppermute x6, waiting for transfers between devices, exchanged(): return lax.ppermute(block, 'space', pairs)  3.52 us
    pallas_call x1, Pallas kernels, per_device(): kernel_call(table_kernel, (shape((ext, slots), bf16), shape((width, slots...  3.13 us
    pallas_call x1, Pallas kernels, per_device(): kernel_call(lambda *refs: backward_kernel(members, ranks, *refs), (saved_...  2.85 us
  transfers between devices with their start and end apart: 20, of which 11 were waited for; matrix products, arithmetic and copies ran while one was open for 0% of the time, Pallas kernels for 21%

profile of v18, /device:TPU:0, one launch (start us, length us, event | category | flops | bytes accessed | tf_op | source)
XLA Modules:
  0.0 70.1 jit_solution(6522947145312999158)
XLA Ops:
  0.6 0.0 copy-start.7
  0.6 1.2 %copy-done.7 = bf16[2,1024,256]{2,1,0:T(8,128)(2,1)S(1)} copy-done((bf16[2,1024,256]{2,1,0:T(8,128)(2,1)S(1)}, bf16[2,1024,256]{2,1,0:T(8,128)(2,1)}, u32[]{:S(2)}) %copy-start.7) | copy-done | bytes 1048600
  1.9 0.1 shard_map.153
  2.0 0.0 copy-start
  2.0 0.0 copy-start.1
  2.0 0.0 copy-start.2
  2.0 0.0 copy-start.4
  2.0 0.0 copy-start.5
  2.0 3.1 %collective-permute-start = (bf16[256,256]{1,0:T(8,128)(2,1)S(1)}, bf16[256,256]{1,0:T(8,128)(2,1)S(1)}, u32[]{:S(2)}, u32[]{:S(2)}) collective-permute-start(bf16[256,256]{1,0:T(8,128)(2,1)S(1)} %get-tuple-element.71), channel_id=1, source_target_pairs={{0,4},{4,0},{8,12},{12,8},{1,5},{5,1},{9,13},{13,9},{2,6},{6,2},{1... | collective-permute-start | bytes 393224 | tf_op jit(solution)/shard_map/ppermute | solution.py:316
  5.1 2.5 %collective-permute-start.1 = (bf16[256,256]{1,0:T(8,128)(2,1)S(1)}, bf16[256,256]{1,0:T(8,128)(2,1)S(1)}, u32[]{:S(2)}, u32[]{:S(2)}) collective-permute-start(bf16[256,256]{1,0:T(8,128)(2,1)S(1)} %get-tuple-element.72), channel_id=1, source_target_pairs={{0,12},{4,8},{8,4},{12,0},{1,13},{5,9},{9,5},{13,1},{2,14},{6,10},... | collective-permute-start | bytes 393224 | tf_op jit(solution)/shard_map/ppermute | solution.py:316
  7.6 0.0 copy-done.6
  7.6 0.0 copy-done.8
  7.6 0.0 copy-done.9
  7.6 3.1 %shard_map.154 = (bf16[1536,1536]{1,0:T(8,128)(2,1)S(1)}, f32[256,1536]{1,0:T(8,128)S(1)}, bf16[256,256]{1,0:T(8,128)(2,1)S(1)}, bf16[256,256]{1,0:T(8,128)(2,1)S(1)}) custom-call(s32[1]{0:T(128)} %bitcast.1.region_ref.refs_0_, s32[1]{0:T(128)} %bitcast.rank_ref.refs_1_.refs_0_, s32[4]{0:T(128)S(1)} %copy-done.6, s32[4,1536]{1,0:T(4,128)S(1)} %copy-done.8, ...), custom_call_target="tpu_custom_call" | custom-call | flops 805306368 | bytes 12582912 | tf_op jit(solution)/shard_map/pallas_call | solution.py:343
  10.7 0.7 %collective-permute-start.2 = (bf16[256,256]{1,0:T(8,128)(2,1)S(1)}, bf16[256,256]{1,0:T(8,128)(2,1)S(1)}, u32[]{:S(2)}, u32[]{:S(2)}) collective-permute-start(bf16[256,256]{1,0:T(8,128)(2,1)S(1)} %get-tuple-element.74), channel_id=1, source_target_pairs={{0,4},{4,0},{8,12},{12,8},{1,5},{5,1},{9,13},{13,9},{2,6},{6,2},{1... | collective-permute-start | bytes 393224 | tf_op jit(solution)/shard_map/ppermute | solution.py:316
  11.5 0.9 %collective-permute-start.3 = (bf16[256,256]{1,0:T(8,128)(2,1)S(1)}, bf16[256,256]{1,0:T(8,128)(2,1)S(1)}, u32[]{:S(2)}, u32[]{:S(2)}) collective-permute-start(bf16[256,256]{1,0:T(8,128)(2,1)S(1)} %get-tuple-element.75), channel_id=1, source_target_pairs={{0,12},{4,8},{8,4},{12,0},{1,13},{5,9},{9,5},{13,1},{2,14},{6,10},... | collective-permute-start | bytes 393224 | tf_op jit(solution)/shard_map/ppermute | solution.py:316
  12.4 0.0 collective-permute-done.refs_3_
  12.4 2.2 %collective-permute-done.1.refs_4_ = bf16[256,256]{1,0:T(8,128)(2,1)S(1)} collective-permute-done((bf16[256,256]{1,0:T(8,128)(2,1)S(1)}, bf16[256,256]{1,0:T(8,128)(2,1)S(1)}, u32[]{:S(2)}, u32[]{:S(2)}) %collective-permute-start.1) | collective-permute-done | bytes 131104 | tf_op jit(solution)/shard_map/ppermute | solution.py:316
  14.6 0.0 copy-done
  14.6 0.0 copy-done.1
  14.7 1.8 %shard_map.155 = (bf16[256,1536]{1,0:T(8,128)(2,1)S(1)}, bf16[256,1536]{1,0:T(8,128)(2,1)S(1)}, bf16[256,1536]{1,0:T(8,128)(2,1)S(1)}, bf16[256,1536]{1,0:T(8,12...) custom-call(s32[1]{0:T(128)} %bitcast.1.region_ref.refs_0_, ...), custom_call_target="tpu_custom_call" | custom-call | flops 905969664 | bytes 8388608 | tf_op jit(solution)/shard_map/pallas_call | solution.py:359
  16.5 0.0 copy-start.3
  16.5 1.6 %collective-permute-start.7 = (bf16[128,1536]{1,0:T(8,128)(2,1)S(1)}, bf16[128,1536]{1,0:T(8,128)(2,1)S(1)}, u32[]{:S(2)}, u32[]{:S(2)}) collective-permute-start(bf16[128,1536]{1,0:T(8,128)(2,1)S(1)} %get-tuple-element.73.refs_2_), channel_id=1, source_target_pairs={{0,2},{1,3},{2,0},{3,1},{4,6},{5,7},{6,4},{7,5},{8,10},{9,11},{10,... | collective-permute-start | bytes 1179656 | tf_op jit(solution)/shard_map/ppermute | solution.py:320
  18.0 0.0 collective-permute-start.5
  18.1 0.0 collective-permute-done.2.refs_3_
  18.1 1.3 %collective-permute-done.3.refs_4_ = bf16[256,256]{1,0:T(8,128)(2,1)S(1)} collective-permute-done((bf16[256,256]{1,0:T(8,128)(2,1)S(1)}, bf16[256,256]{1,0:T(8,128)(2,1)S(1)}, u32[]{:S(2)}, u32[]{:S(2)}) %collective-permute-start.3) | collective-permute-done | bytes 131104 | tf_op jit(solution)/shard_map/ppermute | solution.py:316
  19.3 2.6 %shard_map.156 = (bf16[256,1536]{1,0:T(8,128)(2,1)S(1)}, bf16[256,1536]{1,0:T(8,128)(2,1)S(1)}, bf16[256,1536]{1,0:T(8,128)(2,1)S(1)}, bf16[256,1536]{1,0:T(8,12...) custom-call(s32[1]{0:T(128)} %bitcast.1.region_ref.refs_0_, ...), custom_call_target="tpu_custom_call" | custom-call | flops 1711276032 | bytes 8388608 | tf_op jit(solution)/shard_map/pallas_call | solution.py:359
  21.9 0.1 collective-permute-start.6
  22.0 1.6 %collective-permute-start.4 = (bf16[128,1536]{1,0:T(8,128)(2,1)S(1)}, bf16[128,1536]{1,0:T(8,128)(2,1)S(1)}, u32[]{:S(2)}, u32[]{:S(2)}) collective-permute-start(bf16[128,1536]{1,0:T(8,128)(2,1)S(1)} %get-tuple-element.76.refs_3_), channel_id=1, source_target_pairs={{0,2},{1,3},{2,0},{3,1},{4,6},{5,7},{6,4},{7,5},{8,10},{9,11},{10,... | collective-permute-start | bytes 1179656 | tf_op jit(solution)/shard_map/ppermute | solution.py:320
  23.6 2.3 %collective-permute-done.7.refs_6_ = bf16[128,1536]{1,0:T(8,128)(2,1)S(1)} collective-permute-done((bf16[128,1536]{1,0:T(8,128)(2,1)S(1)}, bf16[128,1536]{1,0:T(8,128)(2,1)S(1)}, u32[]{:S(2)}, u32[]{:S(2)}) %collective-permute-start.7) | collective-permute-done | bytes 393248 | tf_op jit(solution)/shard_map/ppermute | solution.py:320
  25.8 0.0 collective-permute-done.5.refs_4_
  25.8 0.0 collective-permute-done.6.refs_5_
  25.8 2.7 %shard_map.157 = (f32[128,1536]{1,0:T(8,128)S(1)}, f32[128,1536]{1,0:T(8,128)S(1)}, f32[1,128]{1,0:T(1,128)S(1)}) custom-call(s32[1]{0:T(128)} %bitcast.1.region_ref.refs_0_, s32[4]{0:T(128)S(1)} %copy-done.6, bf16[128,1536]{1,0:T(8,128)(2,1)S(1)} %get-tuple-element.73.refs_2_, bf16[128,1536]{1,0:T(8,128)(2,1)S(1)} %get-tuple-element.76.refs_3_, ...), custom_call_target="tpu_custom_call" | custom-call | flops 4194304 | bytes 2097152 | tf_op jit(solution)/shard_map/pallas_call | solution.py:378
  28.6 5.4 %collective-permute-done.4.refs_4_ = bf16[128,1536]{1,0:T(8,128)(2,1)S(1)} collective-permute-done((bf16[128,1536]{1,0:T(8,128)(2,1)S(1)}, bf16[128,1536]{1,0:T(8,128)(2,1)S(1)}, u32[]{:S(2)}, u32[]{:S(2)}) %collective-permute-start.4) | collective-permute-done | bytes 393248 | tf_op jit(solution)/shard_map/ppermute | solution.py:320
  33.9 0.0 collective-permute-start.8
  33.9 0.5 collective-permute-start.9
  34.5 1.2 %collective-permute-done.8.refs_5_ = bf16[128,1536]{1,0:T(8,128)(2,1)S(1)} collective-permute-done((bf16[128,1536]{1,0:T(8,128)(2,1)S(1)}, bf16[128,1536]{1,0:T(8,128)(2,1)S(1)}, u32[]{:S(2)}, u32[]{:S(2)}) %collective-permute-start.8) | collective-permute-done | bytes 393248 | tf_op jit(solution)/shard_map/ppermute | solution.py:320
  35.7 0.6 collective-permute-done.9.refs_6_
  36.2 2.1 %shard_map.158 = (bf16[128,1536]{1,0:T(8,128)(2,1)S(1)}, bf16[128,1536]{1,0:T(8,128)(2,1)S(1)}, f32[1,128]{1,0:T(1,128)S(1)}) custom-call(s32[1]{0:T(128)} %bitcast.1.region_ref.refs_0_, s32[4]{0:T(128)S(1)} %copy-done.6, bf16[128,1536]{1,0:T(8,128)(2,1)S(1)} %get-tuple-element.73.refs_2_, bf16[128,1536]{1,0:T(8,128)(2,1)S(1)} %get-tuple-element.76.refs_3_, ...), custom_call_target="tpu_custom_call" | custom-call | flops 4194304 | bytes 2097152 | tf_op jit(solution)/shard_map/pallas_call | solution.py:378
  38.3 2.8 %shard_map.159 = (bf16[256,1536]{1,0:T(8,128)(2,1)S(1)}, bf16[256,1536]{1,0:T(8,128)(2,1)S(1)}, bf16[176,256]{1,0:T(8,128)(2,1)S(1)}, bf16[176,256]{1,0:T(8,128)...) custom-call(s32[1]{0:T(128)} %bitcast.1.region_ref.refs_0_, s32[1]{0:T(128)} %bitcast.rank_ref.refs_1_.refs_0_, ...), custom_call_target="tpu_custom_call" | custom-call | flops 2013265920 | bytes 10485760 | tf_op jit(solution)/shard_map/pallas_call | solution.py:397
  41.1 0.2 collective-permute-start.10
  41.4 0.4 collective-permute-start.11
  41.7 1.4 %shard_map.160 = (bf16[256,1536]{1,0:T(8,128)(2,1)S(1)}, bf16[256,1536]{1,0:T(8,128)(2,1)S(1)}, bf16[2,256,256]{2,1,0:T(8,128)(2,1)S(1)}, bf16[2,256,256]{2,1,0:T(8,128)(2,1)S(1)}) custom-call(s32[1]{0:T(128)} %bitcast.1.region_ref.refs_0_, bf16[1536,1536]{1,0:T(8,128)(2,1)S(1)} %get-tuple-element.70.refs_2_.refs_1_.table_ref, ...), custom_call_target="tpu_custom_call" | custom-call | flops 1207959552 | bytes 6291456 | tf_op jit(solution)/shard_map/pallas_call | solution.py:413
  43.1 0.0 collective-permute-done.10.refs_2_
  43.1 0.0 collective-permute-done.11.refs_3_
  43.2 1.5 %collective-permute-start.12 = (bf16[176,256]{1,0:T(8,128)(2,1)S(1)}, bf16[176,256]{1,0:T(8,128)(2,1)S(1)}, u32[]{:S(2)}, u32[]{:S(2)}) collective-permute-start(bf16[176,256]{1,0:T(8,128)(2,1)S(1)} %get-tuple-element.108), channel_id=1, source_target_pairs={{0,2},{1,3},{2,0},{3,1},{4,6},{5,7},{6,4},{7,5},{8,10},{9,11},{10,... | collective-permute-start | bytes 270344 | tf_op jit(solution)/shard_map/ppermute | solution.py:320
  44.8 1.7 %collective-permute-start.15 = (bf16[2,256,256]{2,1,0:T(8,128)(2,1)S(1)}, bf16[2,256,256]{2,1,0:T(8,128)(2,1)S(1)}, u32[]{:S(2)}, u32[]{:S(2)}) collective-permute-start(bf16[2,256,256]{2,1,0:T(8,128)(2,1)S(1)} %get-tuple-element.112), channel_id=1, source_target_pairs={{0,12},{4,8},{8,4},{12,0},{1,13},{5,9},{9,5},{13,1},{2,14},{6,10},... | collective-permute-start | bytes 786440 | tf_op jit(solution)/shard_map/ppermute | solution.py:316
  46.5 1.5 %collective-permute-done.12.refs_1_ = bf16[176,256]{1,0:T(8,128)(2,1)S(1)} collective-permute-done((bf16[176,256]{1,0:T(8,128)(2,1)S(1)}, bf16[176,256]{1,0:T(8,128)(2,1)S(1)}, u32[]{:S(2)}, u32[]{:S(2)}) %collective-permute-start.12) | collective-permute-done | bytes 90144 | tf_op jit(solution)/shard_map/ppermute | solution.py:320
  48.0 0.8 %collective-permute-start.13 = (bf16[176,256]{1,0:T(8,128)(2,1)S(1)}, bf16[176,256]{1,0:T(8,128)(2,1)S(1)}, u32[]{:S(2)}, u32[]{:S(2)}) collective-permute-start(bf16[176,256]{1,0:T(8,128)(2,1)S(1)} %shard_map.162.refs_0_), channel_id=1, source_target_pairs={{0,4},{4,0},{8,12},{12,8},{1,5},{5,1},{9,13},{13,9},{2,6},{6,2},{1... | collective-permute-start | bytes 270344 | tf_op jit(solution)/shard_map/ppermute | solution.py:320
  48.7 1.8 %shard_map.164.own_ref = f32[2,1024,256]{2,1,0:T(8,128)S(1)} custom-call(bf16[1536,1536]{1,0:T(8,128)(2,1)S(1)} %get-tuple-element.70.refs_2_.refs_1_.table_ref, bf16[256,1536]{1,0:T(8,128)(2,1)S(1)} %get-tuple-element.109.refs_0_, bf16[256,1536]{1,0:T(8,128)(2,1)S(1)} %get-tuple-element.110.refs_1_), custom_call_target="tpu_custom_call" | custom-call | flops 1610612736 | bytes 6291456 | tf_op jit(solution)/shard_map/pallas_call | solution.py:430
  50.5 6.1 %collective-permute-done.13.refs_1_ = bf16[176,256]{1,0:T(8,128)(2,1)S(1)} collective-permute-done((bf16[176,256]{1,0:T(8,128)(2,1)S(1)}, bf16[176,256]{1,0:T(8,128)(2,1)S(1)}, u32[]{:S(2)}, u32[]{:S(2)}) %collective-permute-start.13) | collective-permute-done | bytes 90144 | tf_op jit(solution)/shard_map/ppermute | solution.py:320
  56.7 0.6 collective-permute-start.14
  57.3 1.7 %collective-permute-start.19 = (bf16[2,256,256]{2,1,0:T(8,128)(2,1)S(1)}, bf16[2,256,256]{2,1,0:T(8,128)(2,1)S(1)}, u32[]{:S(2)}, u32[]{:S(2)}) collective-permute-start(bf16[2,256,256]{2,1,0:T(8,128)(2,1)S(1)} %get-tuple-element.116), channel_id=1, source_target_pairs={{0,4},{4,0},{8,12},{12,8},{1,5},{5,1},{9,13},{13,9},{2,6},{6,2},{1... | collective-permute-start | bytes 786440 | tf_op jit(solution)/shard_map/ppermute | solution.py:316
  59.0 0.0 collective-permute-done.15.other_ref
  59.0 4.3 %collective-permute-done.14.refs_1_ = bf16[176,256]{1,0:T(8,128)(2,1)S(1)} collective-permute-done((bf16[176,256]{1,0:T(8,128)(2,1)S(1)}, bf16[176,256]{1,0:T(8,128)(2,1)S(1)}, u32[]{:S(2)}, u32[]{:S(2)}) %collective-permute-start.14) | collective-permute-done | bytes 90144 | tf_op jit(solution)/shard_map/ppermute | solution.py:320
  63.3 0.6 collective-permute-start.17
  63.9 0.0 collective-permute-start.16
  63.9 4.0 %collective-permute-done.17.refs_3_ = bf16[176,256]{1,0:T(8,128)(2,1)S(1)} collective-permute-done((bf16[176,256]{1,0:T(8,128)(2,1)S(1)}, bf16[176,256]{1,0:T(8,128)(2,1)S(1)}, u32[]{:S(2)}, u32[]{:S(2)}) %collective-permute-start.17) | collective-permute-done | bytes 90144 | tf_op jit(solution)/shard_map/ppermute | solution.py:320
  67.9 0.0 collective-permute-start.18
  67.9 0.0 collective-permute-done.19.one_ref
  67.9 1.1 %shard_map.166 = bf16[2,1024,256]{2,1,0:T(8,128)(2,1)} custom-call(s32[1]{0:T(128)} %bitcast.1.region_ref.refs_0_, f32[2,1024,256]{2,1,0:T(8,128)S(1)} %shard_map.164.own_ref, bf16[2,256,256]{2,1,0:T(8,128)(2,1)S(1)} %collective-permute-done.19.one_ref, bf16[2,256,256]{2,1,0:T(8,128)(2,1)S(1)} %collective-permute-done.15.other_ref), custom_call_target="tpu_custom_call" | custom-call | flops 1048576 | bytes 3145728 | tf_op jit(solution)/shard_map/pallas_call | solution.py:455
  69.1 0.0 collective-permute-done.16.refs_2_
  69.1 0.1 collective-permute-done.18.refs_4_
  69.2 0.9 %shard_map.167 = (f32[256,256]{1,0:T(8,128)}, f32[1,256]{1,0:T(1,128)}, f32[256,256]{1,0:T(8,128)}, f32[1,256]{1,0:T(1,128)}, f32[256,128]{1,0:T(8,128)}, /*index=5*/f32[1,4]{1,0:T(1,128)}) custom-call(s32[1]{0:T(128)} %bitcast.rank_ref.refs_1_.refs_0_, bf16[176,256]{1,0:T(8,128)(2,1)S(1)} %shard_map.165.refs_1_, ...), custom_call_target="tpu_custom_call" | custom-call | flops 1048576 | bytes 2097152 | tf_op jit(solution)/shard_map/pallas_call | solution.py:466
  (11 shorter events, 0.1 us)
Async XLA Ops:
  0.6 1.2 %copy-start.7 = (bf16[2,1024,256]{2,1,0:T(8,128)(2,1)S(1)}, bf16[2,1024,256]{2,1,0:T(8,128)(2,1)}, u32[]{:S(2)}) copy-start(bf16[2,1024,256]{2,1,0:T(8,128)(2,1)} %latent_ref.1) | copy-start | bytes 3145732
  1.9 5.7 %copy-start.6 = (s32[4]{0:T(128)S(1)}, s32[4]{0:T(128)}, u32[]{:S(2)}) copy-start(s32[4]{0:T(128)} %refs_1_.3) | copy-start | bytes 52
  1.9 5.7 %copy-start.8 = (s32[4,1536]{1,0:T(4,128)S(1)}, s32[4,1536]{1,0:T(4,128)}, u32[]{:S(2)}) copy-start(s32[4,1536]{1,0:T(4,128)} %nbr_ref.1) | copy-start | bytes 73732
  1.9 5.7 %copy-start.9 = (f32[4,1536]{1,0:T(4,128)S(1)}, f32[4,1536]{1,0:T(4,128)}, u32[]{:S(2)}) copy-start(f32[4,1536]{1,0:T(4,128)} %weight_ref.1) | copy-start | bytes 73732
  2.0 12.7 %copy-start = (bf16[256,256]{1,0:T(8,128)(2,1)S(1)}, bf16[256,256]{1,0:T(8,128)(2,1)}, u32[]{:S(2)}) copy-start(bf16[256,256]{1,0:T(8,128)(2,1)} %refs_2_.2) | copy-start | bytes 393220
  2.0 12.7 %copy-start.1 = (bf16[256,256]{1,0:T(8,128)(2,1)S(1)}, bf16[256,256]{1,0:T(8,128)(2,1)}, u32[]{:S(2)}) copy-start(bf16[256,256]{1,0:T(8,128)(2,1)} %refs_2_.3) | copy-start | bytes 393220
  2.0 12.7 %copy-start.2 = (bf16[256,128]{1,0:T(8,128)(2,1)S(1)}, bf16[256,128]{1,0:T(8,128)(2,1)}, u32[]{:S(2)}) copy-start(bf16[256,128]{1,0:T(8,128)(2,1)} %refs_3_.1) | copy-start | bytes 196612
  2.0 12.6 %copy-start.4 = (f32[256]{0:T(256)S(1)}, f32[256]{0:T(256)}, u32[]{:S(2)}) copy-start(f32[256]{0:T(256)} %param.16) | copy-start | bytes 3076
  2.0 12.6 %copy-start.5 = (f32[256]{0:T(256)S(1)}, f32[256]{0:T(256)}, u32[]{:S(2)}) copy-start(f32[256]{0:T(256)} %param.18) | copy-start | bytes 3076
  2.0 10.4 %collective-permute-start = (bf16[256,256]{1,0:T(8,128)(2,1)S(1)}, bf16[256,256]{1,0:T(8,128)(2,1)S(1)}, u32[]{:S(2)}, u32[]{:S(2)}) collective-permute-start(bf16[256,256]{1,0:T(8,128)(2,1)S(1)} %get-tuple-element.71), channel_id=1, source_target_pairs={{0,4},{4,0},{8,12},{12,8},{1,5},{5,1},{9,13},{13,9},{2,6},{6,2},{1... | collective-permute-start | bytes 393224 | tf_op jit(solution)/shard_map/ppermute | solution.py:316
  5.1 9.5 %collective-permute-start.1 = (bf16[256,256]{1,0:T(8,128)(2,1)S(1)}, bf16[256,256]{1,0:T(8,128)(2,1)S(1)}, u32[]{:S(2)}, u32[]{:S(2)}) collective-permute-start(bf16[256,256]{1,0:T(8,128)(2,1)S(1)} %get-tuple-element.72), channel_id=1, source_target_pairs={{0,12},{4,8},{8,4},{12,0},{1,13},{5,9},{9,5},{13,1},{2,14},{6,10},... | collective-permute-start | bytes 393224 | tf_op jit(solution)/shard_map/ppermute | solution.py:316
  10.7 7.3 %collective-permute-start.2 = (bf16[256,256]{1,0:T(8,128)(2,1)S(1)}, bf16[256,256]{1,0:T(8,128)(2,1)S(1)}, u32[]{:S(2)}, u32[]{:S(2)}) collective-permute-start(bf16[256,256]{1,0:T(8,128)(2,1)S(1)} %get-tuple-element.74), channel_id=1, source_target_pairs={{0,4},{4,0},{8,12},{12,8},{1,5},{5,1},{9,13},{13,9},{2,6},{6,2},{1... | collective-permute-start | bytes 393224 | tf_op jit(solution)/shard_map/ppermute | solution.py:316
  11.5 7.8 %collective-permute-start.3 = (bf16[256,256]{1,0:T(8,128)(2,1)S(1)}, bf16[256,256]{1,0:T(8,128)(2,1)S(1)}, u32[]{:S(2)}, u32[]{:S(2)}) collective-permute-start(bf16[256,256]{1,0:T(8,128)(2,1)S(1)} %get-tuple-element.75), channel_id=1, source_target_pairs={{0,12},{4,8},{8,4},{12,0},{1,13},{5,9},{9,5},{13,1},{2,14},{6,10},... | collective-permute-start | bytes 393224 | tf_op jit(solution)/shard_map/ppermute | solution.py:316
  16.5 9.4 %copy-start.3 = (bf16[1536,128]{1,0:T(8,128)(2,1)S(1)}, bf16[1536,128]{1,0:T(8,128)(2,1)}, u32[]{:S(2)}) copy-start(bf16[1536,128]{1,0:T(8,128)(2,1)} %refs_7_.5) | copy-start | bytes 1179652
  16.5 9.3 %collective-permute-start.7 = (bf16[128,1536]{1,0:T(8,128)(2,1)S(1)}, bf16[128,1536]{1,0:T(8,128)(2,1)S(1)}, u32[]{:S(2)}, u32[]{:S(2)}) collective-permute-start(bf16[128,1536]{1,0:T(8,128)(2,1)S(1)} %get-tuple-element.73.refs_2_), channel_id=1, source_target_pairs={{0,2},{1,3},{2,0},{3,1},{4,6},{5,7},{6,4},{7,5},{8,10},{9,11},{10,... | collective-permute-start | bytes 1179656 | tf_op jit(solution)/shard_map/ppermute | solution.py:320
  18.0 7.8 %collective-permute-start.5 = (bf16[128,1536]{1,0:T(8,128)(2,1)S(1)}, bf16[128,1536]{1,0:T(8,128)(2,1)S(1)}, u32[]{:S(2)}, u32[]{:S(2)}) collective-permute-start(bf16[128,1536]{1,0:T(8,128)(2,1)S(1)} %get-tuple-element.73.refs_2_), channel_id=1, source_target_pairs={{0,1},{1,0},{2,3},{3,2},{4,5},{5,4},{6,7},{7,6},{8,9},{9,8},{10,11... | collective-permute-start | bytes 1179656 | tf_op jit(solution)/shard_map/ppermute | solution.py:320
  21.9 3.9 %collective-permute-start.6 = (bf16[128,1536]{1,0:T(8,128)(2,1)S(1)}, bf16[128,1536]{1,0:T(8,128)(2,1)S(1)}, u32[]{:S(2)}, u32[]{:S(2)}) collective-permute-start(bf16[128,1536]{1,0:T(8,128)(2,1)S(1)} %get-tuple-element.76.refs_3_), channel_id=1, source_target_pairs={{0,1},{1,0},{2,3},{3,2},{4,5},{5,4},{6,7},{7,6},{8,9},{9,8},{10,11... | collective-permute-start | bytes 1179656 | tf_op jit(solution)/shard_map/ppermute | solution.py:320
  22.0 11.9 %collective-permute-start.4 = (bf16[128,1536]{1,0:T(8,128)(2,1)S(1)}, bf16[128,1536]{1,0:T(8,128)(2,1)S(1)}, u32[]{:S(2)}, u32[]{:S(2)}) collective-permute-start(bf16[128,1536]{1,0:T(8,128)(2,1)S(1)} %get-tuple-element.76.refs_3_), channel_id=1, source_target_pairs={{0,2},{1,3},{2,0},{3,1},{4,6},{5,7},{6,4},{7,5},{8,10},{9,11},{10,... | collective-permute-start | bytes 1179656 | tf_op jit(solution)/shard_map/ppermute | solution.py:320
  33.9 1.7 %collective-permute-start.8 = (bf16[128,1536]{1,0:T(8,128)(2,1)S(1)}, bf16[128,1536]{1,0:T(8,128)(2,1)S(1)}, u32[]{:S(2)}, u32[]{:S(2)}) collective-permute-start(bf16[128,1536]{1,0:T(8,128)(2,1)S(1)} %collective-permute-done.7.refs_6_), channel_id=1, source_target_pairs={{0,1},{1,0},{2,3},{3,2},{4,5},{5,4},{6,7},{7,6},{8,9},{9,8},{10,11... | collective-permute-start | bytes 1179656 | tf_op jit(solution)/shard_map/ppermute | solution.py:320
  33.9 2.3 %collective-permute-start.9 = (bf16[128,1536]{1,0:T(8,128)(2,1)S(1)}, bf16[128,1536]{1,0:T(8,128)(2,1)S(1)}, u32[]{:S(2)}, u32[]{:S(2)}) collective-permute-start(bf16[128,1536]{1,0:T(8,128)(2,1)S(1)} %collective-permute-done.4.refs_4_), channel_id=1, source_target_pairs={{0,1},{1,0},{2,3},{3,2},{4,5},{5,4},{6,7},{7,6},{8,9},{9,8},{10,11... | collective-permute-start | bytes 1179656 | tf_op jit(solution)/shard_map/ppermute | solution.py:320
  41.1 2.0 %collective-permute-start.10 = (bf16[176,256]{1,0:T(8,128)(2,1)S(1)}, bf16[176,256]{1,0:T(8,128)(2,1)S(1)}, u32[]{:S(2)}, u32[]{:S(2)}) collective-permute-start(bf16[176,256]{1,0:T(8,128)(2,1)S(1)} %get-tuple-element.99), channel_id=1, source_target_pairs={{0,1},{1,0},{2,3},{3,2},{4,5},{5,4},{6,7},{7,6},{8,9},{9,8},{10,11... | collective-permute-start | bytes 270344 | tf_op jit(solution)/shard_map/ppermute | solution.py:320
  41.4 1.8 %collective-permute-start.11 = (bf16[176,256]{1,0:T(8,128)(2,1)S(1)}, bf16[176,256]{1,0:T(8,128)(2,1)S(1)}, u32[]{:S(2)}, u32[]{:S(2)}) collective-permute-start(bf16[176,256]{1,0:T(8,128)(2,1)S(1)} %get-tuple-element.100), channel_id=1, source_target_pairs={{0,1},{1,0},{2,3},{3,2},{4,5},{5,4},{6,7},{7,6},{8,9},{9,8},{10,11... | collective-permute-start | bytes 270344 | tf_op jit(solution)/shard_map/ppermute | solution.py:320
  43.2 4.7 %collective-permute-start.12 = (bf16[176,256]{1,0:T(8,128)(2,1)S(1)}, bf16[176,256]{1,0:T(8,128)(2,1)S(1)}, u32[]{:S(2)}, u32[]{:S(2)}) collective-permute-start(bf16[176,256]{1,0:T(8,128)(2,1)S(1)} %get-tuple-element.108), channel_id=1, source_target_pairs={{0,2},{1,3},{2,0},{3,1},{4,6},{5,7},{6,4},{7,5},{8,10},{9,11},{10,... | collective-permute-start | bytes 270344 | tf_op jit(solution)/shard_map/ppermute | solution.py:320
  44.8 14.2 %collective-permute-start.15 = (bf16[2,256,256]{2,1,0:T(8,128)(2,1)S(1)}, bf16[2,256,256]{2,1,0:T(8,128)(2,1)S(1)}, u32[]{:S(2)}, u32[]{:S(2)}) collective-permute-start(bf16[2,256,256]{2,1,0:T(8,128)(2,1)S(1)} %get-tuple-element.112), channel_id=1, source_target_pairs={{0,12},{4,8},{8,4},{12,0},{1,13},{5,9},{9,5},{13,1},{2,14},{6,10},... | collective-permute-start | bytes 786440 | tf_op jit(solution)/shard_map/ppermute | solution.py:316
  48.0 8.7 %collective-permute-start.13 = (bf16[176,256]{1,0:T(8,128)(2,1)S(1)}, bf16[176,256]{1,0:T(8,128)(2,1)S(1)}, u32[]{:S(2)}, u32[]{:S(2)}) collective-permute-start(bf16[176,256]{1,0:T(8,128)(2,1)S(1)} %shard_map.162.refs_0_), channel_id=1, source_target_pairs={{0,4},{4,0},{8,12},{12,8},{1,5},{5,1},{9,13},{13,9},{2,6},{6,2},{1... | collective-permute-start | bytes 270344 | tf_op jit(solution)/shard_map/ppermute | solution.py:320
  56.7 6.6 %collective-permute-start.14 = (bf16[176,256]{1,0:T(8,128)(2,1)S(1)}, bf16[176,256]{1,0:T(8,128)(2,1)S(1)}, u32[]{:S(2)}, u32[]{:S(2)}) collective-permute-start(bf16[176,256]{1,0:T(8,128)(2,1)S(1)} %shard_map.163.refs_0_), channel_id=1, source_target_pairs={{0,8},{4,12},{8,0},{12,4},{1,9},{5,13},{9,1},{13,5},{2,10},{6,14},... | collective-permute-start | bytes 270344 | tf_op jit(solution)/shard_map/ppermute | solution.py:320
  57.3 10.6 %collective-permute-start.19 = (bf16[2,256,256]{2,1,0:T(8,128)(2,1)S(1)}, bf16[2,256,256]{2,1,0:T(8,128)(2,1)S(1)}, u32[]{:S(2)}, u32[]{:S(2)}) collective-permute-start(bf16[2,256,256]{2,1,0:T(8,128)(2,1)S(1)} %get-tuple-element.116), channel_id=1, source_target_pairs={{0,4},{4,0},{8,12},{12,8},{1,5},{5,1},{9,13},{13,9},{2,6},{6,2},{1... | collective-permute-start | bytes 786440 | tf_op jit(solution)/shard_map/ppermute | solution.py:316
  63.3 4.6 %collective-permute-start.17 = (bf16[176,256]{1,0:T(8,128)(2,1)S(1)}, bf16[176,256]{1,0:T(8,128)(2,1)S(1)}, u32[]{:S(2)}, u32[]{:S(2)}) collective-permute-start(bf16[176,256]{1,0:T(8,128)(2,1)S(1)} %shard_map.165.refs_1_), channel_id=1, source_target_pairs={{0,2},{1,3},{2,0},{3,1},{4,6},{5,7},{6,4},{7,5},{8,10},{9,11},{10,... | collective-permute-start | bytes 270344 | tf_op jit(solution)/shard_map/ppermute | solution.py:320
  63.9 5.2 %collective-permute-start.16 = (bf16[176,256]{1,0:T(8,128)(2,1)S(1)}, bf16[176,256]{1,0:T(8,128)(2,1)S(1)}, u32[]{:S(2)}, u32[]{:S(2)}) collective-permute-start(bf16[176,256]{1,0:T(8,128)(2,1)S(1)} %shard_map.165.refs_1_), channel_id=1, source_target_pairs={{0,1},{1,0},{2,3},{3,2},{4,5},{5,4},{6,7},{7,6},{8,9},{9,8},{10,11... | collective-permute-start | bytes 270344 | tf_op jit(solution)/shard_map/ppermute | solution.py:320
  67.9 1.3 %collective-permute-start.18 = (bf16[176,256]{1,0:T(8,128)(2,1)S(1)}, bf16[176,256]{1,0:T(8,128)(2,1)S(1)}, u32[]{:S(2)}, u32[]{:S(2)}) collective-permute-start(bf16[176,256]{1,0:T(8,128)(2,1)S(1)} %collective-permute-done.17.refs_3_), channel_id=1, source_target_pairs={{0,1},{1,0},{2,3},{3,2},{4,5},{5,4},{6,7},{7,6},{8,9},{9,8},{10,11... | collective-permute-start | bytes 270344 | tf_op jit(solution)/shard_map/ppermute | solution.py:320

commit v19 on v18

--- a/solution.py
+++ b/solution.py
@@ -263,11 +263,12 @@
     ext = table_ref.shape[0]
     rows = jnp.concatenate([table_ref[rows, :] for rows in rim_starts(region_ref, ext)], axis=0)
     for m in range(members):
-        d_mixed = nn_dot(w_one_ref[...], d_one_refs[m][...]).astype(jnp.bfloat16)
-        d_mixed_refs[m][...] = d_mixed
-        grads = nt_dot(rows, d_mixed).astype(jnp.bfloat16)
-        one_ref[m] = grads[:HALO]
-        other_ref[m] = grads[HALO:]
+        d_mixed_refs[m][...] = nn_dot(w_one_ref[...], d_one_refs[m][...]).astype(jnp.bfloat16)
+    width = one_ref.shape[2]
+    grads = nt_dot(rows, jnp.concatenate([ref[...] for ref in d_mixed_refs], axis=0)).astype(jnp.bfloat16)
+    for m in range(members):
+        one_ref[m] = grads[:HALO, m * width : (m + 1) * width]
+        other_ref[m] = grads[HALO:, m * width : (m + 1) * width]
 
 
 def sum_kernel(count, *refs):

time: 70.2 us -> 70.2 us (level)
  no operation moved by 1% of the time
where the time goes in v19:
time: 70.2 us; the launch traced here: 70 us
  waiting for transfers between devices  28.9 us (41%)
  Pallas kernels  20.6 us (29%)
  starting transfers between devices  18.4 us (26%)
  local copies, waits for them, and re-layouts  1.27 us (2%)
  between operations  0.84 us (1%)
    ppermute x14, waiting for transfers between devices, swapped(): lax.ppermute(block, axis, [(i, i ^ by) for i in range(lax.axis_size(axis))])  25.4 us
    ppermute x6, starting transfers between devices, exchanged(): return lax.ppermute(block, 'space', pairs)  10.6 us
    ppermute x14, starting transfers between devices, swapped(): lax.ppermute(block, axis, [(i, i ^ by) for i in range(lax.axis_size(axis))])  7.8 us
    pallas_call x2, Pallas kernels, scored(): kernel_call(lambda *refs: score_kernel(members, len(others), members * ra...  4.77 us
    pallas_call x2, Pallas kernels, per_device(): kernel_call(lambda *refs: forward_kernel(m, *refs), (mixed_shape,) + (sav...  4.42 us
    ppermute x6, waiting for transfers between devices, exchanged(): return lax.ppermute(block, 'space', pairs)  3.52 us
    pallas_call x1, Pallas kernels, per_device(): kernel_call(table_kernel, (shape((ext, slots), bf16), shape((width, slots...  3.13 us
    pallas_call x1, Pallas kernels, per_device(): kernel_call(lambda *refs: backward_kernel(members, ranks, *refs), (saved_...  2.85 us
  transfers between devices with their start and end apart: 20, of which 11 were waited for; matrix products, arithmetic and copies ran while one was open for 0% of the time, Pallas kernels for 21%

profile of v19, /device:TPU:0, one launch (start us, length us, event | category | flops | bytes accessed | tf_op | source)
XLA Modules:
  0.0 70.0 jit_solution(14363924752908479508)
XLA Ops:
  0.6 0.0 copy-start.7
  0.6 1.2 %copy-done.7 = bf16[2,1024,256]{2,1,0:T(8,128)(2,1)S(1)} copy-done((bf16[2,1024,256]{2,1,0:T(8,128)(2,1)S(1)}, bf16[2,1024,256]{2,1,0:T(8,128)(2,1)}, u32[]{:S(2)}) %copy-start.7) | copy-done | bytes 1048600
  1.9 0.1 shard_map.153
  2.0 0.0 copy-start
  2.0 0.0 copy-start.1
  2.0 0.0 copy-start.2
  2.0 0.0 copy-start.4
  2.0 0.0 copy-start.5
  2.0 3.1 %collective-permute-start = (bf16[256,256]{1,0:T(8,128)(2,1)S(1)}, bf16[256,256]{1,0:T(8,128)(2,1)S(1)}, u32[]{:S(2)}, u32[]{:S(2)}) collective-permute-start(bf16[256,256]{1,0:T(8,128)(2,1)S(1)} %get-tuple-element.71), channel_id=1, source_target_pairs={{0,4},{4,0},{8,12},{12,8},{1,5},{5,1},{9,13},{13,9},{2,6},{6,2},{1... | collective-permute-start | bytes 393224 | tf_op jit(solution)/shard_map/ppermute | solution.py:317
  5.1 2.5 %collective-permute-start.1 = (bf16[256,256]{1,0:T(8,128)(2,1)S(1)}, bf16[256,256]{1,0:T(8,128)(2,1)S(1)}, u32[]{:S(2)}, u32[]{:S(2)}) collective-permute-start(bf16[256,256]{1,0:T(8,128)(2,1)S(1)} %get-tuple-element.72), channel_id=1, source_target_pairs={{0,12},{4,8},{8,4},{12,0},{1,13},{5,9},{9,5},{13,1},{2,14},{6,10},... | collective-permute-start | bytes 393224 | tf_op jit(solution)/shard_map/ppermute | solution.py:317
  7.6 0.0 copy-done.6
  7.6 0.0 copy-done.8
  7.6 0.0 copy-done.9
  7.6 3.1 %shard_map.154 = (bf16[1536,1536]{1,0:T(8,128)(2,1)S(1)}, f32[256,1536]{1,0:T(8,128)S(1)}, bf16[256,256]{1,0:T(8,128)(2,1)S(1)}, bf16[256,256]{1,0:T(8,128)(2,1)S(1)}) custom-call(s32[1]{0:T(128)} %bitcast.1.region_ref.refs_0_, s32[1]{0:T(128)} %bitcast.rank_ref.refs_1_.refs_0_, s32[4]{0:T(128)S(1)} %copy-done.6, s32[4,1536]{1,0:T(4,128)S(1)} %copy-done.8, ...), custom_call_target="tpu_custom_call" | custom-call | flops 805306368 | bytes 12582912 | tf_op jit(solution)/shard_map/pallas_call | solution.py:344
  10.7 0.7 %collective-permute-start.2 = (bf16[256,256]{1,0:T(8,128)(2,1)S(1)}, bf16[256,256]{1,0:T(8,128)(2,1)S(1)}, u32[]{:S(2)}, u32[]{:S(2)}) collective-permute-start(bf16[256,256]{1,0:T(8,128)(2,1)S(1)} %get-tuple-element.74), channel_id=1, source_target_pairs={{0,4},{4,0},{8,12},{12,8},{1,5},{5,1},{9,13},{13,9},{2,6},{6,2},{1... | collective-permute-start | bytes 393224 | tf_op jit(solution)/shard_map/ppermute | solution.py:317
  11.5 0.9 %collective-permute-start.3 = (bf16[256,256]{1,0:T(8,128)(2,1)S(1)}, bf16[256,256]{1,0:T(8,128)(2,1)S(1)}, u32[]{:S(2)}, u32[]{:S(2)}) collective-permute-start(bf16[256,256]{1,0:T(8,128)(2,1)S(1)} %get-tuple-element.75), channel_id=1, source_target_pairs={{0,12},{4,8},{8,4},{12,0},{1,13},{5,9},{9,5},{13,1},{2,14},{6,10},... | collective-permute-start | bytes 393224 | tf_op jit(solution)/shard_map/ppermute | solution.py:317
  12.4 0.0 collective-permute-done.refs_3_
  12.4 2.2 %collective-permute-done.1.refs_4_ = bf16[256,256]{1,0:T(8,128)(2,1)S(1)} collective-permute-done((bf16[256,256]{1,0:T(8,128)(2,1)S(1)}, bf16[256,256]{1,0:T(8,128)(2,1)S(1)}, u32[]{:S(2)}, u32[]{:S(2)}) %collective-permute-start.1) | collective-permute-done | bytes 131104 | tf_op jit(solution)/shard_map/ppermute | solution.py:317
  14.6 0.0 copy-done
  14.6 0.0 copy-done.1
  14.7 1.8 %shard_map.155 = (bf16[256,1536]{1,0:T(8,128)(2,1)S(1)}, bf16[256,1536]{1,0:T(8,128)(2,1)S(1)}, bf16[256,1536]{1,0:T(8,128)(2,1)S(1)}, bf16[256,1536]{1,0:T(8,12...) custom-call(s32[1]{0:T(128)} %bitcast.1.region_ref.refs_0_, ...), custom_call_target="tpu_custom_call" | custom-call | flops 905969664 | bytes 8388608 | tf_op jit(solution)/shard_map/pallas_call | solution.py:360
  16.5 0.0 copy-start.3
  16.5 1.6 %collective-permute-start.7 = (bf16[128,1536]{1,0:T(8,128)(2,1)S(1)}, bf16[128,1536]{1,0:T(8,128)(2,1)S(1)}, u32[]{:S(2)}, u32[]{:S(2)}) collective-permute-start(bf16[128,1536]{1,0:T(8,128)(2,1)S(1)} %get-tuple-element.73.refs_2_), channel_id=1, source_target_pairs={{0,2},{1,3},{2,0},{3,1},{4,6},{5,7},{6,4},{7,5},{8,10},{9,11},{10,... | collective-permute-start | bytes 1179656 | tf_op jit(solution)/shard_map/ppermute | solution.py:321
  18.0 0.0 collective-permute-start.5
  18.1 0.0 collective-permute-done.2.refs_3_
  18.1 1.3 %collective-permute-done.3.refs_4_ = bf16[256,256]{1,0:T(8,128)(2,1)S(1)} collective-permute-done((bf16[256,256]{1,0:T(8,128)(2,1)S(1)}, bf16[256,256]{1,0:T(8,128)(2,1)S(1)}, u32[]{:S(2)}, u32[]{:S(2)}) %collective-permute-start.3) | collective-permute-done | bytes 131104 | tf_op jit(solution)/shard_map/ppermute | solution.py:317
  19.3 2.6 %shard_map.156 = (bf16[256,1536]{1,0:T(8,128)(2,1)S(1)}, bf16[256,1536]{1,0:T(8,128)(2,1)S(1)}, bf16[256,1536]{1,0:T(8,128)(2,1)S(1)}, bf16[256,1536]{1,0:T(8,12...) custom-call(s32[1]{0:T(128)} %bitcast.1.region_ref.refs_0_, ...), custom_call_target="tpu_custom_call" | custom-call | flops 1711276032 | bytes 8388608 | tf_op jit(solution)/shard_map/pallas_call | solution.py:360
  21.9 0.1 collective-permute-start.6
  22.0 1.6 %collective-permute-start.4 = (bf16[128,1536]{1,0:T(8,128)(2,1)S(1)}, bf16[128,1536]{1,0:T(8,128)(2,1)S(1)}, u32[]{:S(2)}, u32[]{:S(2)}) collective-permute-start(bf16[128,1536]{1,0:T(8,128)(2,1)S(1)} %get-tuple-element.76.refs_3_), channel_id=1, source_target_pairs={{0,2},{1,3},{2,0},{3,1},{4,6},{5,7},{6,4},{7,5},{8,10},{9,11},{10,... | collective-permute-start | bytes 1179656 | tf_op jit(solution)/shard_map/ppermute | solution.py:321
  23.6 2.3 %collective-permute-done.7.refs_6_ = bf16[128,1536]{1,0:T(8,128)(2,1)S(1)} collective-permute-done((bf16[128,1536]{1,0:T(8,128)(2,1)S(1)}, bf16[128,1536]{1,0:T(8,128)(2,1)S(1)}, u32[]{:S(2)}, u32[]{:S(2)}) %collective-permute-start.7) | collective-permute-done | bytes 393248 | tf_op jit(solution)/shard_map/ppermute | solution.py:321
  25.8 0.0 collective-permute-done.5.refs_4_
  25.8 0.0 collective-permute-done.6.refs_5_
  25.8 2.7 %shard_map.157 = (f32[128,1536]{1,0:T(8,128)S(1)}, f32[128,1536]{1,0:T(8,128)S(1)}, f32[1,128]{1,0:T(1,128)S(1)}) custom-call(s32[1]{0:T(128)} %bitcast.1.region_ref.refs_0_, s32[4]{0:T(128)S(1)} %copy-done.6, bf16[128,1536]{1,0:T(8,128)(2,1)S(1)} %get-tuple-element.73.refs_2_, bf16[128,1536]{1,0:T(8,128)(2,1)S(1)} %get-tuple-element.76.refs_3_, ...), custom_call_target="tpu_custom_call" | custom-call | flops 4194304 | bytes 2097152 | tf_op jit(solution)/shard_map/pallas_call | solution.py:379
  28.6 5.4 %collective-permute-done.4.refs_4_ = bf16[128,1536]{1,0:T(8,128)(2,1)S(1)} collective-permute-done((bf16[128,1536]{1,0:T(8,128)(2,1)S(1)}, bf16[128,1536]{1,0:T(8,128)(2,1)S(1)}, u32[]{:S(2)}, u32[]{:S(2)}) %collective-permute-start.4) | collective-permute-done | bytes 393248 | tf_op jit(solution)/shard_map/ppermute | solution.py:321
  33.9 0.0 collective-permute-start.8
  33.9 0.5 collective-permute-start.9
  34.5 1.2 %collective-permute-done.8.refs_5_ = bf16[128,1536]{1,0:T(8,128)(2,1)S(1)} collective-permute-done((bf16[128,1536]{1,0:T(8,128)(2,1)S(1)}, bf16[128,1536]{1,0:T(8,128)(2,1)S(1)}, u32[]{:S(2)}, u32[]{:S(2)}) %collective-permute-start.8) | collective-permute-done | bytes 393248 | tf_op jit(solution)/shard_map/ppermute | solution.py:321
  35.7 0.6 collective-permute-done.9.refs_6_
  36.2 2.1 %shard_map.158 = (bf16[128,1536]{1,0:T(8,128)(2,1)S(1)}, bf16[128,1536]{1,0:T(8,128)(2,1)S(1)}, f32[1,128]{1,0:T(1,128)S(1)}) custom-call(s32[1]{0:T(128)} %bitcast.1.region_ref.refs_0_, s32[4]{0:T(128)S(1)} %copy-done.6, bf16[128,1536]{1,0:T(8,128)(2,1)S(1)} %get-tuple-element.73.refs_2_, bf16[128,1536]{1,0:T(8,128)(2,1)S(1)} %get-tuple-element.76.refs_3_, ...), custom_call_target="tpu_custom_call" | custom-call | flops 4194304 | bytes 2097152 | tf_op jit(solution)/shard_map/pallas_call | solution.py:379
  38.3 2.8 %shard_map.159 = (bf16[256,1536]{1,0:T(8,128)(2,1)S(1)}, bf16[256,1536]{1,0:T(8,128)(2,1)S(1)}, bf16[176,256]{1,0:T(8,128)(2,1)S(1)}, bf16[176,256]{1,0:T(8,128)...) custom-call(s32[1]{0:T(128)} %bitcast.1.region_ref.refs_0_, s32[1]{0:T(128)} %bitcast.rank_ref.refs_1_.refs_0_, ...), custom_call_target="tpu_custom_call" | custom-call | flops 2013265920 | bytes 10485760 | tf_op jit(solution)/shard_map/pallas_call | solution.py:398
  41.1 0.2 collective-permute-start.10
  41.4 0.4 collective-permute-start.11
  41.7 1.4 %shard_map.160 = (bf16[256,1536]{1,0:T(8,128)(2,1)S(1)}, bf16[256,1536]{1,0:T(8,128)(2,1)S(1)}, bf16[2,256,256]{2,1,0:T(8,128)(2,1)S(1)}, bf16[2,256,256]{2,1,0:T(8,128)(2,1)S(1)}) custom-call(s32[1]{0:T(128)} %bitcast.1.region_ref.refs_0_, bf16[1536,1536]{1,0:T(8,128)(2,1)S(1)} %get-tuple-element.70.refs_2_.refs_1_.table_ref, ...), custom_call_target="tpu_custom_call" | custom-call | flops 1207959552 | bytes 6291456 | tf_op jit(solution)/shard_map/pallas_call | solution.py:414
  43.1 0.0 collective-permute-done.10.refs_2_
  43.1 0.0 collective-permute-done.11.refs_3_
  43.2 1.5 %collective-permute-start.12 = (bf16[176,256]{1,0:T(8,128)(2,1)S(1)}, bf16[176,256]{1,0:T(8,128)(2,1)S(1)}, u32[]{:S(2)}, u32[]{:S(2)}) collective-permute-start(bf16[176,256]{1,0:T(8,128)(2,1)S(1)} %get-tuple-element.108), channel_id=1, source_target_pairs={{0,2},{1,3},{2,0},{3,1},{4,6},{5,7},{6,4},{7,5},{8,10},{9,11},{10,... | collective-permute-start | bytes 270344 | tf_op jit(solution)/shard_map/ppermute | solution.py:321
  44.7 1.7 %collective-permute-start.15 = (bf16[2,256,256]{2,1,0:T(8,128)(2,1)S(1)}, bf16[2,256,256]{2,1,0:T(8,128)(2,1)S(1)}, u32[]{:S(2)}, u32[]{:S(2)}) collective-permute-start(bf16[2,256,256]{2,1,0:T(8,128)(2,1)S(1)} %get-tuple-element.112), channel_id=1, source_target_pairs={{0,12},{4,8},{8,4},{12,0},{1,13},{5,9},{9,5},{13,1},{2,14},{6,10},... | collective-permute-start | bytes 786440 | tf_op jit(solution)/shard_map/ppermute | solution.py:317
  46.4 1.5 %collective-permute-done.12.refs_1_ = bf16[176,256]{1,0:T(8,128)(2,1)S(1)} collective-permute-done((bf16[176,256]{1,0:T(8,128)(2,1)S(1)}, bf16[176,256]{1,0:T(8,128)(2,1)S(1)}, u32[]{:S(2)}, u32[]{:S(2)}) %collective-permute-start.12) | collective-permute-done | bytes 90144 | tf_op jit(solution)/shard_map/ppermute | solution.py:321
  47.9 0.8 %collective-permute-start.13 = (bf16[176,256]{1,0:T(8,128)(2,1)S(1)}, bf16[176,256]{1,0:T(8,128)(2,1)S(1)}, u32[]{:S(2)}, u32[]{:S(2)}) collective-permute-start(bf16[176,256]{1,0:T(8,128)(2,1)S(1)} %shard_map.162.refs_0_), channel_id=1, source_target_pairs={{0,4},{4,0},{8,12},{12,8},{1,5},{5,1},{9,13},{13,9},{2,6},{6,2},{1... | collective-permute-start | bytes 270344 | tf_op jit(solution)/shard_map/ppermute | solution.py:321
  48.7 1.8 %shard_map.164.own_ref = f32[2,1024,256]{2,1,0:T(8,128)S(1)} custom-call(bf16[1536,1536]{1,0:T(8,128)(2,1)S(1)} %get-tuple-element.70.refs_2_.refs_1_.table_ref, bf16[256,1536]{1,0:T(8,128)(2,1)S(1)} %get-tuple-element.109.refs_0_, bf16[256,1536]{1,0:T(8,128)(2,1)S(1)} %get-tuple-element.110.refs_1_), custom_call_target="tpu_custom_call" | custom-call | flops 1610612736 | bytes 6291456 | tf_op jit(solution)/shard_map/pallas_call | solution.py:431
  50.5 6.1 %collective-permute-done.13.refs_1_ = bf16[176,256]{1,0:T(8,128)(2,1)S(1)} collective-permute-done((bf16[176,256]{1,0:T(8,128)(2,1)S(1)}, bf16[176,256]{1,0:T(8,128)(2,1)S(1)}, u32[]{:S(2)}, u32[]{:S(2)}) %collective-permute-start.13) | collective-permute-done | bytes 90144 | tf_op jit(solution)/shard_map/ppermute | solution.py:321
  56.7 0.6 collective-permute-start.14
  57.3 1.7 %collective-permute-start.19 = (bf16[2,256,256]{2,1,0:T(8,128)(2,1)S(1)}, bf16[2,256,256]{2,1,0:T(8,128)(2,1)S(1)}, u32[]{:S(2)}, u32[]{:S(2)}) collective-permute-start(bf16[2,256,256]{2,1,0:T(8,128)(2,1)S(1)} %get-tuple-element.116), channel_id=1, source_target_pairs={{0,4},{4,0},{8,12},{12,8},{1,5},{5,1},{9,13},{13,9},{2,6},{6,2},{1... | collective-permute-start | bytes 786440 | tf_op jit(solution)/shard_map/ppermute | solution.py:317
  59.0 0.0 collective-permute-done.15.other_ref
  59.0 4.3 %collective-permute-done.14.refs_1_ = bf16[176,256]{1,0:T(8,128)(2,1)S(1)} collective-permute-done((bf16[176,256]{1,0:T(8,128)(2,1)S(1)}, bf16[176,256]{1,0:T(8,128)(2,1)S(1)}, u32[]{:S(2)}, u32[]{:S(2)}) %collective-permute-start.14) | collective-permute-done | bytes 90144 | tf_op jit(solution)/shard_map/ppermute | solution.py:321
  63.3 0.6 collective-permute-start.17
  63.9 0.0 collective-permute-start.16
  63.9 4.0 %collective-permute-done.17.refs_3_ = bf16[176,256]{1,0:T(8,128)(2,1)S(1)} collective-permute-done((bf16[176,256]{1,0:T(8,128)(2,1)S(1)}, bf16[176,256]{1,0:T(8,128)(2,1)S(1)}, u32[]{:S(2)}, u32[]{:S(2)}) %collective-permute-start.17) | collective-permute-done | bytes 90144 | tf_op jit(solution)/shard_map/ppermute | solution.py:321
  67.9 0.0 collective-permute-start.18
  67.9 0.0 collective-permute-done.19.one_ref
  67.9 1.1 %shard_map.166 = bf16[2,1024,256]{2,1,0:T(8,128)(2,1)} custom-call(s32[1]{0:T(128)} %bitcast.1.region_ref.refs_0_, f32[2,1024,256]{2,1,0:T(8,128)S(1)} %shard_map.164.own_ref, bf16[2,256,256]{2,1,0:T(8,128)(2,1)S(1)} %collective-permute-done.19.one_ref, bf16[2,256,256]{2,1,0:T(8,128)(2,1)S(1)} %collective-permute-done.15.other_ref), custom_call_target="tpu_custom_call" | custom-call | flops 1048576 | bytes 3145728 | tf_op jit(solution)/shard_map/pallas_call | solution.py:456
  69.0 0.0 collective-permute-done.16.refs_2_
  69.0 0.1 collective-permute-done.18.refs_4_
  69.2 0.9 %shard_map.167 = (f32[256,256]{1,0:T(8,128)}, f32[1,256]{1,0:T(1,128)}, f32[256,256]{1,0:T(8,128)}, f32[1,256]{1,0:T(1,128)}, f32[256,128]{1,0:T(8,128)}, /*index=5*/f32[1,4]{1,0:T(1,128)}) custom-call(s32[1]{0:T(128)} %bitcast.rank_ref.refs_1_.refs_0_, bf16[176,256]{1,0:T(8,128)(2,1)S(1)} %shard_map.165.refs_1_, ...), custom_call_target="tpu_custom_call" | custom-call | flops 1048576 | bytes 2097152 | tf_op jit(solution)/shard_map/pallas_call | solution.py:467
  (11 shorter events, 0.1 us)
Async XLA Ops:
  0.6 1.2 %copy-start.7 = (bf16[2,1024,256]{2,1,0:T(8,128)(2,1)S(1)}, bf16[2,1024,256]{2,1,0:T(8,128)(2,1)}, u32[]{:S(2)}) copy-start(bf16[2,1024,256]{2,1,0:T(8,128)(2,1)} %latent_ref.1) | copy-start | bytes 3145732
  1.9 5.7 %copy-start.6 = (s32[4]{0:T(128)S(1)}, s32[4]{0:T(128)}, u32[]{:S(2)}) copy-start(s32[4]{0:T(128)} %refs_1_.3) | copy-start | bytes 52
  1.9 5.7 %copy-start.8 = (s32[4,1536]{1,0:T(4,128)S(1)}, s32[4,1536]{1,0:T(4,128)}, u32[]{:S(2)}) copy-start(s32[4,1536]{1,0:T(4,128)} %nbr_ref.1) | copy-start | bytes 73732
  1.9 5.7 %copy-start.9 = (f32[4,1536]{1,0:T(4,128)S(1)}, f32[4,1536]{1,0:T(4,128)}, u32[]{:S(2)}) copy-start(f32[4,1536]{1,0:T(4,128)} %weight_ref.1) | copy-start | bytes 73732
  2.0 12.7 %copy-start = (bf16[256,256]{1,0:T(8,128)(2,1)S(1)}, bf16[256,256]{1,0:T(8,128)(2,1)}, u32[]{:S(2)}) copy-start(bf16[256,256]{1,0:T(8,128)(2,1)} %refs_2_.2) | copy-start | bytes 393220
  2.0 12.7 %copy-start.1 = (bf16[256,256]{1,0:T(8,128)(2,1)S(1)}, bf16[256,256]{1,0:T(8,128)(2,1)}, u32[]{:S(2)}) copy-start(bf16[256,256]{1,0:T(8,128)(2,1)} %refs_2_.3) | copy-start | bytes 393220
  2.0 12.7 %copy-start.2 = (bf16[256,128]{1,0:T(8,128)(2,1)S(1)}, bf16[256,128]{1,0:T(8,128)(2,1)}, u32[]{:S(2)}) copy-start(bf16[256,128]{1,0:T(8,128)(2,1)} %refs_3_.1) | copy-start | bytes 196612
  2.0 12.6 %copy-start.4 = (f32[256]{0:T(256)S(1)}, f32[256]{0:T(256)}, u32[]{:S(2)}) copy-start(f32[256]{0:T(256)} %param.16) | copy-start | bytes 3076
  2.0 12.6 %copy-start.5 = (f32[256]{0:T(256)S(1)}, f32[256]{0:T(256)}, u32[]{:S(2)}) copy-start(f32[256]{0:T(256)} %param.18) | copy-start | bytes 3076
  2.0 10.4 %collective-permute-start = (bf16[256,256]{1,0:T(8,128)(2,1)S(1)}, bf16[256,256]{1,0:T(8,128)(2,1)S(1)}, u32[]{:S(2)}, u32[]{:S(2)}) collective-permute-start(bf16[256,256]{1,0:T(8,128)(2,1)S(1)} %get-tuple-element.71), channel_id=1, source_target_pairs={{0,4},{4,0},{8,12},{12,8},{1,5},{5,1},{9,13},{13,9},{2,6},{6,2},{1... | collective-permute-start | bytes 393224 | tf_op jit(solution)/shard_map/ppermute | solution.py:317
  5.1 9.5 %collective-permute-start.1 = (bf16[256,256]{1,0:T(8,128)(2,1)S(1)}, bf16[256,256]{1,0:T(8,128)(2,1)S(1)}, u32[]{:S(2)}, u32[]{:S(2)}) collective-permute-start(bf16[256,256]{1,0:T(8,128)(2,1)S(1)} %get-tuple-element.72), channel_id=1, source_target_pairs={{0,12},{4,8},{8,4},{12,0},{1,13},{5,9},{9,5},{13,1},{2,14},{6,10},... | collective-permute-start | bytes 393224 | tf_op jit(solution)/shard_map/ppermute | solution.py:317
  10.7 7.3 %collective-permute-start.2 = (bf16[256,256]{1,0:T(8,128)(2,1)S(1)}, bf16[256,256]{1,0:T(8,128)(2,1)S(1)}, u32[]{:S(2)}, u32[]{:S(2)}) collective-permute-start(bf16[256,256]{1,0:T(8,128)(2,1)S(1)} %get-tuple-element.74), channel_id=1, source_target_pairs={{0,4},{4,0},{8,12},{12,8},{1,5},{5,1},{9,13},{13,9},{2,6},{6,2},{1... | collective-permute-start | bytes 393224 | tf_op jit(solution)/shard_map/ppermute | solution.py:317
  11.5 7.8 %collective-permute-start.3 = (bf16[256,256]{1,0:T(8,128)(2,1)S(1)}, bf16[256,256]{1,0:T(8,128)(2,1)S(1)}, u32[]{:S(2)}, u32[]{:S(2)}) collective-permute-start(bf16[256,256]{1,0:T(8,128)(2,1)S(1)} %get-tuple-element.75), channel_id=1, source_target_pairs={{0,12},{4,8},{8,4},{12,0},{1,13},{5,9},{9,5},{13,1},{2,14},{6,10},... | collective-permute-start | bytes 393224 | tf_op jit(solution)/shard_map/ppermute | solution.py:317
  16.5 9.4 %copy-start.3 = (bf16[1536,128]{1,0:T(8,128)(2,1)S(1)}, bf16[1536,128]{1,0:T(8,128)(2,1)}, u32[]{:S(2)}) copy-start(bf16[1536,128]{1,0:T(8,128)(2,1)} %refs_7_.5) | copy-start | bytes 1179652
  16.5 9.3 %collective-permute-start.7 = (bf16[128,1536]{1,0:T(8,128)(2,1)S(1)}, bf16[128,1536]{1,0:T(8,128)(2,1)S(1)}, u32[]{:S(2)}, u32[]{:S(2)}) collective-permute-start(bf16[128,1536]{1,0:T(8,128)(2,1)S(1)} %get-tuple-element.73.refs_2_), channel_id=1, source_target_pairs={{0,2},{1,3},{2,0},{3,1},{4,6},{5,7},{6,4},{7,5},{8,10},{9,11},{10,... | collective-permute-start | bytes 1179656 | tf_op jit(solution)/shard_map/ppermute | solution.py:321
  18.0 7.8 %collective-permute-start.5 = (bf16[128,1536]{1,0:T(8,128)(2,1)S(1)}, bf16[128,1536]{1,0:T(8,128)(2,1)S(1)}, u32[]{:S(2)}, u32[]{:S(2)}) collective-permute-start(bf16[128,1536]{1,0:T(8,128)(2,1)S(1)} %get-tuple-element.73.refs_2_), channel_id=1, source_target_pairs={{0,1},{1,0},{2,3},{3,2},{4,5},{5,4},{6,7},{7,6},{8,9},{9,8},{10,11... | collective-permute-start | bytes 1179656 | tf_op jit(solution)/shard_map/ppermute | solution.py:321
  21.9 3.9 %collective-permute-start.6 = (bf16[128,1536]{1,0:T(8,128)(2,1)S(1)}, bf16[128,1536]{1,0:T(8,128)(2,1)S(1)}, u32[]{:S(2)}, u32[]{:S(2)}) collective-permute-start(bf16[128,1536]{1,0:T(8,128)(2,1)S(1)} %get-tuple-element.76.refs_3_), channel_id=1, source_target_pairs={{0,1},{1,0},{2,3},{3,2},{4,5},{5,4},{6,7},{7,6},{8,9},{9,8},{10,11... | collective-permute-start | bytes 1179656 | tf_op jit(solution)/shard_map/ppermute | solution.py:321
  22.0 11.9 %collective-permute-start.4 = (bf16[128,1536]{1,0:T(8,128)(2,1)S(1)}, bf16[128,1536]{1,0:T(8,128)(2,1)S(1)}, u32[]{:S(2)}, u32[]{:S(2)}) collective-permute-start(bf16[128,1536]{1,0:T(8,128)(2,1)S(1)} %get-tuple-element.76.refs_3_), channel_id=1, source_target_pairs={{0,2},{1,3},{2,0},{3,1},{4,6},{5,7},{6,4},{7,5},{8,10},{9,11},{10,... | collective-permute-start | bytes 1179656 | tf_op jit(solution)/shard_map/ppermute | solution.py:321
  33.9 1.7 %collective-permute-start.8 = (bf16[128,1536]{1,0:T(8,128)(2,1)S(1)}, bf16[128,1536]{1,0:T(8,128)(2,1)S(1)}, u32[]{:S(2)}, u32[]{:S(2)}) collective-permute-start(bf16[128,1536]{1,0:T(8,128)(2,1)S(1)} %collective-permute-done.7.refs_6_), channel_id=1, source_target_pairs={{0,1},{1,0},{2,3},{3,2},{4,5},{5,4},{6,7},{7,6},{8,9},{9,8},{10,11... | collective-permute-start | bytes 1179656 | tf_op jit(solution)/shard_map/ppermute | solution.py:321
  33.9 2.3 %collective-permute-start.9 = (bf16[128,1536]{1,0:T(8,128)(2,1)S(1)}, bf16[128,1536]{1,0:T(8,128)(2,1)S(1)}, u32[]{:S(2)}, u32[]{:S(2)}) collective-permute-start(bf16[128,1536]{1,0:T(8,128)(2,1)S(1)} %collective-permute-done.4.refs_4_), channel_id=1, source_target_pairs={{0,1},{1,0},{2,3},{3,2},{4,5},{5,4},{6,7},{7,6},{8,9},{9,8},{10,11... | collective-permute-start | bytes 1179656 | tf_op jit(solution)/shard_map/ppermute | solution.py:321
  41.1 2.0 %collective-permute-start.10 = (bf16[176,256]{1,0:T(8,128)(2,1)S(1)}, bf16[176,256]{1,0:T(8,128)(2,1)S(1)}, u32[]{:S(2)}, u32[]{:S(2)}) collective-permute-start(bf16[176,256]{1,0:T(8,128)(2,1)S(1)} %get-tuple-element.99), channel_id=1, source_target_pairs={{0,1},{1,0},{2,3},{3,2},{4,5},{5,4},{6,7},{7,6},{8,9},{9,8},{10,11... | collective-permute-start | bytes 270344 | tf_op jit(solution)/shard_map/ppermute | solution.py:321
  41.4 1.8 %collective-permute-start.11 = (bf16[176,256]{1,0:T(8,128)(2,1)S(1)}, bf16[176,256]{1,0:T(8,128)(2,1)S(1)}, u32[]{:S(2)}, u32[]{:S(2)}) collective-permute-start(bf16[176,256]{1,0:T(8,128)(2,1)S(1)} %get-tuple-element.100), channel_id=1, source_target_pairs={{0,1},{1,0},{2,3},{3,2},{4,5},{5,4},{6,7},{7,6},{8,9},{9,8},{10,11... | collective-permute-start | bytes 270344 | tf_op jit(solution)/shard_map/ppermute | solution.py:321
  43.2 4.7 %collective-permute-start.12 = (bf16[176,256]{1,0:T(8,128)(2,1)S(1)}, bf16[176,256]{1,0:T(8,128)(2,1)S(1)}, u32[]{:S(2)}, u32[]{:S(2)}) collective-permute-start(bf16[176,256]{1,0:T(8,128)(2,1)S(1)} %get-tuple-element.108), channel_id=1, source_target_pairs={{0,2},{1,3},{2,0},{3,1},{4,6},{5,7},{6,4},{7,5},{8,10},{9,11},{10,... | collective-permute-start | bytes 270344 | tf_op jit(solution)/shard_map/ppermute | solution.py:321
  44.7 14.2 %collective-permute-start.15 = (bf16[2,256,256]{2,1,0:T(8,128)(2,1)S(1)}, bf16[2,256,256]{2,1,0:T(8,128)(2,1)S(1)}, u32[]{:S(2)}, u32[]{:S(2)}) collective-permute-start(bf16[2,256,256]{2,1,0:T(8,128)(2,1)S(1)} %get-tuple-element.112), channel_id=1, source_target_pairs={{0,12},{4,8},{8,4},{12,0},{1,13},{5,9},{9,5},{13,1},{2,14},{6,10},... | collective-permute-start | bytes 786440 | tf_op jit(solution)/shard_map/ppermute | solution.py:317
  47.9 8.7 %collective-permute-start.13 = (bf16[176,256]{1,0:T(8,128)(2,1)S(1)}, bf16[176,256]{1,0:T(8,128)(2,1)S(1)}, u32[]{:S(2)}, u32[]{:S(2)}) collective-permute-start(bf16[176,256]{1,0:T(8,128)(2,1)S(1)} %shard_map.162.refs_0_), channel_id=1, source_target_pairs={{0,4},{4,0},{8,12},{12,8},{1,5},{5,1},{9,13},{13,9},{2,6},{6,2},{1... | collective-permute-start | bytes 270344 | tf_op jit(solution)/shard_map/ppermute | solution.py:321
  56.7 6.6 %collective-permute-start.14 = (bf16[176,256]{1,0:T(8,128)(2,1)S(1)}, bf16[176,256]{1,0:T(8,128)(2,1)S(1)}, u32[]{:S(2)}, u32[]{:S(2)}) collective-permute-start(bf16[176,256]{1,0:T(8,128)(2,1)S(1)} %shard_map.163.refs_0_), channel_id=1, source_target_pairs={{0,8},{4,12},{8,0},{12,4},{1,9},{5,13},{9,1},{13,5},{2,10},{6,14},... | collective-permute-start | bytes 270344 | tf_op jit(solution)/shard_map/ppermute | solution.py:321
  57.3 10.6 %collective-permute-start.19 = (bf16[2,256,256]{2,1,0:T(8,128)(2,1)S(1)}, bf16[2,256,256]{2,1,0:T(8,128)(2,1)S(1)}, u32[]{:S(2)}, u32[]{:S(2)}) collective-permute-start(bf16[2,256,256]{2,1,0:T(8,128)(2,1)S(1)} %get-tuple-element.116), channel_id=1, source_target_pairs={{0,4},{4,0},{8,12},{12,8},{1,5},{5,1},{9,13},{13,9},{2,6},{6,2},{1... | collective-permute-start | bytes 786440 | tf_op jit(solution)/shard_map/ppermute | solution.py:317
  63.3 4.6 %collective-permute-start.17 = (bf16[176,256]{1,0:T(8,128)(2,1)S(1)}, bf16[176,256]{1,0:T(8,128)(2,1)S(1)}, u32[]{:S(2)}, u32[]{:S(2)}) collective-permute-start(bf16[176,256]{1,0:T(8,128)(2,1)S(1)} %shard_map.165.refs_1_), channel_id=1, source_target_pairs={{0,2},{1,3},{2,0},{3,1},{4,6},{5,7},{6,4},{7,5},{8,10},{9,11},{10,... | collective-permute-start | bytes 270344 | tf_op jit(solution)/shard_map/ppermute | solution.py:321
  63.9 5.2 %collective-permute-start.16 = (bf16[176,256]{1,0:T(8,128)(2,1)S(1)}, bf16[176,256]{1,0:T(8,128)(2,1)S(1)}, u32[]{:S(2)}, u32[]{:S(2)}) collective-permute-start(bf16[176,256]{1,0:T(8,128)(2,1)S(1)} %shard_map.165.refs_1_), channel_id=1, source_target_pairs={{0,1},{1,0},{2,3},{3,2},{4,5},{5,4},{6,7},{7,6},{8,9},{9,8},{10,11... | collective-permute-start | bytes 270344 | tf_op jit(solution)/shard_map/ppermute | solution.py:321
  67.9 1.3 %collective-permute-start.18 = (bf16[176,256]{1,0:T(8,128)(2,1)S(1)}, bf16[176,256]{1,0:T(8,128)(2,1)S(1)}, u32[]{:S(2)}, u32[]{:S(2)}) collective-permute-start(bf16[176,256]{1,0:T(8,128)(2,1)S(1)} %collective-permute-done.17.refs_3_), channel_id=1, source_target_pairs={{0,1},{1,0},{2,3},{3,2},{4,5},{5,4},{6,7},{7,6},{8,9},{9,8},{10,11... | collective-permute-start | bytes 270344 | tf_op jit(solution)/shard_map/ppermute | solution.py:321
